TPU v7x, 32 devices: a whole 2x2x4 slice. The times are simulated.
32 devices in a mesh: depth: 4 (over y, x), rows: 8 (over z, core).
Axes of the slice: x: 2, y: 2, z: 4, core: 2. Of those that a mesh axis runs over, the one named last changes fastest.
Arguments:
- incident: bfloat16 [3, 2, 256, 1024], P(None, None, 'rows'), may hold values from -6 to 6
- row_taps: bfloat16 [4, 3, 2, 33], P('depth'), may hold values from -0.75 to 0.75
- col_taps: bfloat16 [4, 3, 2, 127], P('depth'), may hold values from -0.375 to 0.375
- hogel_light: float32 [4, 3, 256, 1024], P('depth', None, 'rows'), may hold values from -6 to 6
- silhouette: int32 [4, 256, 64], P('depth', 'rows'), may hold values from 0 to 16
- fill_counts: int32 [4, 16], P('depth', 'rows'), may hold values from 1 to 64, 640 in all within a row
- hogel_index: int32 [4, 16, 64], P('depth', 'rows'), may hold values from 0 to 63, each once within a row
Outputs:
- layer_fields: bfloat16 [4, 3, 2, 256, 1024], P('depth', None, None, 'rows')
Inputs may be any that keep to these rules, and one draw needn't show every extreme that they name: Each entry is the count of one hogel row, at most 64; for each layer l, the sum of fill_counts[l, g] over all 16 hogel rows g is 640. `hogel_index`: each list names every position of its hogel row once.
All inputs are finite; a program needn't handle non-finite values. No bound on the sum of `fill_counts` on one device may be relied on, other than what follows from the above.
Results may differ from a plain program's by a relative error of at most 0.006.
Values may be sent and summed in bfloat16 or wider, within the bound.
No kernel may reach another device: no remote copies, remote signals or barrier semaphores. Data moves between devices by JAX's collectives and lax.ppermute only.
A program may use at most 64 MiB of HBM per device.

v0:
```python
import math

import jax
import jax.numpy as jnp
from jax import lax
from jax.sharding import PartitionSpec as P

HS = 16
KR = 16
KC = 63
COLORS = 3


def padded_2(block, sides, width):
    for axis, dim in sides:
        count = lax.axis_size(axis)
        forward = [(i, i + 1) for i in range(count - 1)]
        backward = [(target, source) for source, target in forward]
        low = lax.ppermute(
            lax.slice_in_dim(block, block.shape[dim] - width, None, axis=dim), axis, forward
        )
        high = lax.ppermute(lax.slice_in_dim(block, 0, width, axis=dim), axis, backward)
        block = jnp.concatenate([low, block, high], axis=dim)
    return block


def from_behind(value, axis, by):
    peers = lax.axis_size(axis)
    pairs = [(i, i + by) for i in range(peers) if 0 <= i + by < peers]
    return lax.ppermute(value, axis, pairs)


def dft_tables(size_now):
    counter = jnp.arange(size_now, dtype=jnp.int32)
    product = counter[:, None] * counter[None, :] % size_now
    angles = product.astype(jnp.float32) * (2.0 * math.pi / size_now)
    return (jnp.cos(angles) / math.sqrt(size_now), jnp.sin(angles) / math.sqrt(size_now))


def toeplitz_from(vector, row_count, col_count):
    tiled = jnp.tile(vector, (1, row_count))
    return tiled[:, : row_count * col_count].reshape(vector.shape[0], row_count, col_count)


def row_matrix(taps, height, reach):
    width_ext = height + 2 * reach
    tail = width_ext + 1 - (2 * reach + 1)
    vector = jnp.concatenate([taps, jnp.zeros((2, tail), taps.dtype)], axis=1)
    banded = toeplitz_from(vector, height, width_ext)
    upper = jnp.concatenate([banded[0], -banded[1]], axis=1)
    lower = jnp.concatenate([banded[1], banded[0]], axis=1)
    return jnp.concatenate([upper, lower], axis=0)


def column_matrix(taps, reach):
    front = jnp.zeros((2, 128 - reach), taps.dtype)
    back = jnp.zeros((2, 385 - 128 - reach - 1), taps.dtype)
    vector = jnp.concatenate([front, taps, back], axis=1)
    flipped = toeplitz_from(vector, 128, 384)
    blocks = flipped.transpose(0, 2, 1)
    real_rows = blocks[0]
    imag_rows = blocks[1]
    upper = jnp.concatenate([real_rows, imag_rows], axis=1)
    lower = jnp.concatenate([-imag_rows, real_rows], axis=1)
    return jnp.concatenate([upper, lower], axis=0)


def apply_columns(rowed, col_mats):
    colour_count, _, height, col_count = rowed.shape
    tile_count = col_count // 128
    padded = jnp.pad(rowed, ((0, 0), (0, 0), (0, 0), (128, 128)))
    pieces = [
        padded[..., tile_shift * 128 : tile_shift * 128 + col_count].reshape(
            colour_count, 2, height, tile_count, 128
        )
        for tile_shift in range(3)
    ]
    stacked = jnp.stack(pieces, axis=2)
    windows = stacked.transpose(0, 3, 4, 1, 2, 5).reshape(colour_count, height * tile_count, 768)
    mixed_cols = jnp.einsum("kna,kab->knb", windows, col_mats, preferred_element_type=jnp.float32)
    return (
        mixed_cols.reshape(colour_count, height, tile_count, 2, 128)
        .transpose(0, 3, 1, 2, 4)
        .reshape(colour_count, 2, height, col_count)
    )


def live_tiles(counts, index_list):
    positions = index_list.shape[1]
    slots = jnp.arange(positions, dtype=jnp.int32)
    named = (index_list[:, :, None] == slots[None, None, :]) & (
        slots[None, :, None] < counts[:, None, None]
    )
    return jnp.any(named, axis=1)


def transparency(edges, hogel_size):
    height, hogel_count = edges.shape
    within = jnp.arange(hogel_size, dtype=jnp.int32)
    clear = within[None, None, :] < edges[:, :, None]
    return clear.astype(jnp.float32).reshape(height, hogel_count * hogel_size)


def stereo_field(light, live, hogel_size):
    colour_count, height, col_count = light.shape
    hogel_rows, hogel_count = live.shape
    live_pix = jnp.broadcast_to(
        live[:, None, :, None], (hogel_rows, hogel_size, hogel_count, hogel_size)
    )
    live_pix = live_pix.reshape(hogel_rows * hogel_size, hogel_count * hogel_size).astype(
        jnp.float32
    )
    masked = light * live_pix[None]
    cos_tab, sin_tab = dft_tables(hogel_size)
    left_mat = jnp.concatenate([cos_tab, -sin_tab], axis=0)
    groups = height // hogel_size
    blocked = masked.reshape(colour_count, groups, hogel_size, col_count)
    left_out = jnp.einsum("ah,kghc->kgac", left_mat, blocked, precision=lax.Precision.HIGHEST)
    tile_count = col_count // 128
    arranged = (
        left_out.reshape(colour_count, groups, 2, hogel_size, tile_count, 128)
        .transpose(0, 1, 3, 4, 2, 5)
        .reshape(-1, 256)
    )
    per_block = 128 // hogel_size
    cos_big = jnp.kron(jnp.eye(per_block, dtype=jnp.float32), cos_tab)
    sin_big = jnp.kron(jnp.eye(per_block, dtype=jnp.float32), sin_tab)
    right_mat = jnp.concatenate(
        [jnp.concatenate([cos_big, -sin_big], axis=1), jnp.concatenate([sin_big, cos_big], axis=1)],
        axis=0,
    )
    result_tiles = jnp.dot(arranged, right_mat, precision=lax.Precision.HIGHEST)
    return (
        result_tiles.reshape(colour_count, groups, hogel_size, tile_count, 2, 128)
        .transpose(0, 4, 1, 2, 3, 5)
        .reshape(colour_count, 2, height, col_count)
    )


def propagate(field_in, row_mats, col_mats, clear, stereo):
    extended = padded_2(field_in, (("rows", 2),), KR)
    colour_count, _, ext_rows, col_count = extended.shape
    height = field_in.shape[2]
    flattened = extended.reshape(colour_count, 2 * ext_rows, col_count)
    rowed = jnp.einsum("kab,kbc->kac", row_mats, flattened, preferred_element_type=jnp.float32)
    rowed = rowed.astype(jnp.bfloat16).reshape(colour_count, 2, height, col_count)
    columned = apply_columns(rowed, col_mats)
    return (clear[None, None] * columned + stereo).astype(jnp.bfloat16)


def body(incident, row_taps, col_taps, hogel_light, silhouette, fill_counts, hogel_index):
    height = incident.shape[2]
    row_mats = jnp.stack([row_matrix(row_taps[0, colour], height, KR) for colour in range(COLORS)])
    col_mats = jnp.stack([column_matrix(col_taps[0, colour], KC) for colour in range(COLORS)])
    clear = transparency(silhouette[0], HS)
    live = live_tiles(fill_counts[0], hogel_index[0])
    stereo = stereo_field(hogel_light[0], live, HS)
    depth_here = lax.axis_index("depth")
    layer_total = lax.axis_size("depth")
    result = jnp.zeros_like(incident)
    field_in = incident
    for layer_step in range(layer_total):
        produced = propagate(field_in, row_mats, col_mats, clear, stereo)
        result = jnp.where(depth_here == layer_step, produced, result)
        if layer_step + 1 < layer_total:
            field_in = from_behind(produced, "depth", 1)
    return result[None]


def solution(mesh):
    placed = (
        P(None, None, "rows", None),
        P("depth", None, None, None),
        P("depth", None, None, None),
        P("depth", None, "rows", None),
        P("depth", "rows", None),
        P("depth", "rows"),
        P("depth", "rows", None),
    )
    return jax.shard_map(
        body,
        mesh=mesh,
        in_specs=placed,
        out_specs=P("depth", None, None, "rows", None),
        check_vma=False,
    )
```

profile of v0, /device:TPU:20, one launch (start us, length us, event | category | flops | bytes accessed | tf_op | source)
XLA Modules:
  0.0 120.9 jit_solution(1769865893774692498)
XLA Ops:
  0.0 1.8 %fusion.36 = (bf16[3,2,16,1024]{3,2,1,0:T(8,128)(2,1)}, bf16[3,2,16,1024]{3,2,1,0:T(8,128)(2,1)}) fusion(bf16[3,2,32,1024]{3,2,1,0:T(8,128)(2,1)} %param.7), kind=kLoop, calls=%fused_computation.113 | loop fusion | bytes 786432 | tf_op jit(solution)/shard_map/slice | solution.py:20
  1.8 1.9 %collective-permute-start = (bf16[3,2,16,1024]{3,2,1,0:T(8,128)(2,1)}, bf16[3,2,16,1024]{3,2,1,0:T(8,128)(2,1)}, u32[]{:S(2)}, u32[]{:S(2)}) collective-permute-start(bf16[3,2,16,1024]{3,2,1,0:T(8,128)(2,1)} %get-tuple-element.25), channel_id=1, source_target_pairs={{0,1},{1,2},{2,3},{3,4},{4,5},{5,6},{6,7},{8,9},{9,10},{10,11},{11... | collective-permute-start | bytes 589832 | tf_op jit(solution)/shard_map/ppermute | solution.py:19
  3.7 3.6 %collective-permute-start.1 = (bf16[3,2,16,1024]{3,2,1,0:T(8,128)(2,1)}, bf16[3,2,16,1024]{3,2,1,0:T(8,128)(2,1)}, u32[]{:S(2)}, u32[]{:S(2)}) collective-permute-start(bf16[3,2,16,1024]{3,2,1,0:T(8,128)(2,1)} %get-tuple-element.26), channel_id=1, source_target_pairs={{1,0},{2,1},{3,2},{4,3},{5,4},{6,5},{7,6},{9,8},{10,9},{11,10},{12... | collective-permute-start | bytes 589832 | tf_op jit(solution)/shard_map/ppermute | solution.py:22
  7.4 0.7 slice_bitcast_fusion.8
  8.3 0.7 tile.61
  9.3 0.7 slice_bitcast_fusion.4
  10.1 0.7 tile.63
  11.1 0.7 slice_bitcast_fusion.2
  11.9 0.7 tile.65
  15.3 0.9 fusion.14
  16.4 0.8 convolution_bitcast_fusion
  18.6 1.3 %maximum_bitcast_fusion.4 = (bf16[1,768,256]{2,1,0:T(8,128)(2,1)S(1)}, bf16[1,768,256]{2,1,0:T(8,128)(2,1)S(1)}) fusion(bf16[384,128]{1,0:T(8,128)(2,1)} %get-tuple-element.28, bf16[384,128]{1,0:T(8,128)(2,1)S(1)} %fusion.30, bf16[384,128]{1,0:T(8,128)(2,1)S(1)} %copy-done.17, bf16[384,128]{1,0:T(8,128)(2,1)} %get-tuple-element.30, ...), kind=kLoop, calls=%fused_computation.47 | loop fusion | flops 3145728 | bytes 1376256 | tf_op jit(solution)/shard_map/stack | solution.py:154
  19.9 1.3 %pad_maximum_fusion.1 = bf16[3,2,64,1024]{3,2,1,0:T(8,128)(2,1)S(1)} fusion(bf16[3,2,16,1024]{3,2,1,0:T(8,128)(2,1)} %collective-permute-done.1, bf16[3,2,32,1024]{3,2,1,0:T(8,128)(2,1)S(1)} %copy-done.2, bf16[3,2,16,1024]{3,2,1,0:T(8,128)(2,1)} %collective-permute-done), kind=kLoop, calls=%fused_computation.14 | loop fusion | flops 2359296 | bytes 1572864 | tf_op jit(solution)/shard_map/concatenate | solution.py:23
  23.6 3.4 %collective-permute-start.2 = (bf16[3,2,32,1024]{3,1,2,0:T(2,128)(2,1)S(1)}, bf16[3,2,32,1024]{3,1,2,0:T(2,128)(2,1)S(1)}, u32[]{:S(2)}, u32[]{:S(2)}) collective-permute-start(bf16[3,2,32,1024]{3,1,2,0:T(2,128)(2,1)S(1)} %add_convert_fusion.2), channel_id=1, source_target_pairs={{0,8},{8,16},{16,24},{1,9},{9,17},{17,25},{2,10},{10,18},{18,26},{... | collective-permute-start | bytes 1179656 | tf_op jit(solution)/shard_map/ppermute | solution.py:30
  27.0 10.4 %collective-permute-done.2 = bf16[3,2,32,1024]{3,1,2,0:T(2,128)(2,1)S(1)} collective-permute-done((bf16[3,2,32,1024]{3,1,2,0:T(2,128)(2,1)S(1)}, bf16[3,2,32,1024]{3,1,2,0:T(2,128)(2,1)S(1)}, u32[]{:S(2)}, u32[]{:S(2)}) %collective-permute-start.2) | collective-permute-done | bytes 393248 | tf_op jit(solution)/shard_map/ppermute | solution.py:30
  37.6 1.9 %collective-permute-start.3 = (bf16[3,2,16,1024]{3,1,2,0:T(2,128)(2,1)S(1)}, bf16[3,2,16,1024]{3,1,2,0:T(2,128)(2,1)S(1)}, u32[]{:S(2)}, u32[]{:S(2)}) collective-permute-start(bf16[3,2,16,1024]{3,1,2,0:T(2,128)(2,1)S(1)} %get-tuple-element.21), channel_id=1, source_target_pairs={{0,1},{1,2},{2,3},{3,4},{4,5},{5,6},{6,7},{8,9},{9,10},{10,11},{11... | collective-permute-start | bytes 589832 | tf_op jit(solution)/shard_map/ppermute | solution.py:19
  39.5 3.8 %collective-permute-start.4 = (bf16[3,2,16,1024]{3,1,2,0:T(2,128)(2,1)S(1)}, bf16[3,2,16,1024]{3,1,2,0:T(2,128)(2,1)S(1)}, u32[]{:S(2)}, u32[]{:S(2)}) collective-permute-start(bf16[3,2,16,1024]{3,1,2,0:T(2,128)(2,1)S(1)} %get-tuple-element.22), channel_id=1, source_target_pairs={{1,0},{2,1},{3,2},{4,3},{5,4},{6,5},{7,6},{9,8},{10,9},{11,10},{12... | collective-permute-start | bytes 589832 | tf_op jit(solution)/shard_map/ppermute | solution.py:22
  43.4 1.2 %collective-permute-done.3 = bf16[3,2,16,1024]{3,1,2,0:T(2,128)(2,1)S(1)} collective-permute-done((bf16[3,2,16,1024]{3,1,2,0:T(2,128)(2,1)S(1)}, bf16[3,2,16,1024]{3,1,2,0:T(2,128)(2,1)S(1)}, u32[]{:S(2)}, u32[]{:S(2)}) %collective-permute-start.3) | collective-permute-done | bytes 196640 | tf_op jit(solution)/shard_map/ppermute | solution.py:19
  44.6 1.8 %collective-permute-done.4 = bf16[3,2,16,1024]{3,1,2,0:T(2,128)(2,1)S(1)} collective-permute-done((bf16[3,2,16,1024]{3,1,2,0:T(2,128)(2,1)S(1)}, bf16[3,2,16,1024]{3,1,2,0:T(2,128)(2,1)S(1)}, u32[]{:S(2)}, u32[]{:S(2)}) %collective-permute-start.4) | collective-permute-done | bytes 196640 | tf_op jit(solution)/shard_map/ppermute | solution.py:22
  46.4 1.1 pad_maximum_fusion.2
  48.6 0.8 copy-done.6
  49.6 0.5 convolution_bitcast_fusion.3
  50.1 1.3 %reshape.364 = f32[3,2,32,1024]{3,1,2,0:T(2,128)} reshape(f32[3,2,32,8,128]{4,3,1,2,0:T(8,128)S(1)} %convolution_bitcast_fusion.3) | data formatting | bytes 1572864 | tf_op jit(solution)/shard_map/reshape | solution.py:84
  51.4 1.6 %add_convert_fusion.1 = bf16[3,2,32,1024]{3,1,2,0:T(2,128)(2,1)S(1)} fusion(f32[3,2,32,1024]{3,1,2,0:T(2,128)S(1)} %reshape.359, f32[3,2,32,1024]{3,1,2,0:T(2,128)} %reshape.364, f32[32,1024]{1,0:T(8,128)S(1)} %compare_convert_fusion), kind=kLoop, calls=%fused_computation.33 | loop fusion | flops 589824 | bytes 2097152 | tf_op jit(solution)/shard_map/convert_element_type | solution.py:148
  53.0 2.5 %collective-permute-start.5 = (bf16[3,2,32,1024]{3,1,2,0:T(2,128)(2,1)S(1)}, bf16[3,2,32,1024]{3,1,2,0:T(2,128)(2,1)S(1)}, u32[]{:S(2)}, u32[]{:S(2)}) collective-permute-start(bf16[3,2,32,1024]{3,1,2,0:T(2,128)(2,1)S(1)} %add_convert_fusion.1), channel_id=1, source_target_pairs={{0,8},{8,16},{16,24},{1,9},{9,17},{17,25},{2,10},{10,18},{18,26},{... | collective-permute-start | bytes 1179656 | tf_op jit(solution)/shard_map/ppermute | solution.py:30
  55.5 12.0 %collective-permute-done.5 = bf16[3,2,32,1024]{3,1,2,0:T(2,128)(2,1)S(1)} collective-permute-done((bf16[3,2,32,1024]{3,1,2,0:T(2,128)(2,1)S(1)}, bf16[3,2,32,1024]{3,1,2,0:T(2,128)(2,1)S(1)}, u32[]{:S(2)}, u32[]{:S(2)}) %collective-permute-start.5) | collective-permute-done | bytes 393248 | tf_op jit(solution)/shard_map/ppermute | solution.py:30
  67.8 2.0 %collective-permute-start.6 = (bf16[3,2,16,1024]{3,1,2,0:T(2,128)(2,1)S(1)}, bf16[3,2,16,1024]{3,1,2,0:T(2,128)(2,1)S(1)}, u32[]{:S(2)}, u32[]{:S(2)}) collective-permute-start(bf16[3,2,16,1024]{3,1,2,0:T(2,128)(2,1)S(1)} %get-tuple-element.17), channel_id=1, source_target_pairs={{0,1},{1,2},{2,3},{3,4},{4,5},{5,6},{6,7},{8,9},{9,10},{10,11},{11... | collective-permute-start | bytes 589832 | tf_op jit(solution)/shard_map/ppermute | solution.py:19
  69.8 3.5 %collective-permute-start.7 = (bf16[3,2,16,1024]{3,1,2,0:T(2,128)(2,1)S(1)}, bf16[3,2,16,1024]{3,1,2,0:T(2,128)(2,1)S(1)}, u32[]{:S(2)}, u32[]{:S(2)}) collective-permute-start(bf16[3,2,16,1024]{3,1,2,0:T(2,128)(2,1)S(1)} %get-tuple-element.18), channel_id=1, source_target_pairs={{1,0},{2,1},{3,2},{4,3},{5,4},{6,5},{7,6},{9,8},{10,9},{11,10},{12... | collective-permute-start | bytes 589832 | tf_op jit(solution)/shard_map/ppermute | solution.py:22
  73.4 1.4 %collective-permute-done.6 = bf16[3,2,16,1024]{3,1,2,0:T(2,128)(2,1)S(1)} collective-permute-done((bf16[3,2,16,1024]{3,1,2,0:T(2,128)(2,1)S(1)}, bf16[3,2,16,1024]{3,1,2,0:T(2,128)(2,1)S(1)}, u32[]{:S(2)}, u32[]{:S(2)}) %collective-permute-start.6) | collective-permute-done | bytes 196640 | tf_op jit(solution)/shard_map/ppermute | solution.py:19
  74.8 1.8 %collective-permute-done.7 = bf16[3,2,16,1024]{3,1,2,0:T(2,128)(2,1)S(1)} collective-permute-done((bf16[3,2,16,1024]{3,1,2,0:T(2,128)(2,1)S(1)}, bf16[3,2,16,1024]{3,1,2,0:T(2,128)(2,1)S(1)}, u32[]{:S(2)}, u32[]{:S(2)}) %collective-permute-start.7) | collective-permute-done | bytes 196640 | tf_op jit(solution)/shard_map/ppermute | solution.py:22
  76.5 1.1 pad_maximum_fusion.3
  78.8 0.8 copy-done.7
  79.8 1.4 %convolution_bitcast_fusion.2 = f32[3,2,32,8,128]{4,3,1,2,0:T(8,128)} fusion(bf16[3,256,768]{2,1,0:T(8,128)(2,1)S(1)} %bitcast.292, bf16[1,768,256]{2,1,0:T(8,128)(2,1)S(1)} %copy-done.7, bf16[1,768,256]{2,1,0:T(8,128)(2,1)S(1)} %copy-done.15, bf16[1,768,256]{2,1,0:T(8,128)(2,1)S(1)} %copy-done.11), kind=kOutput, calls=%fused_computation.2 | convolution fusion | flops 303169536 | bytes 3145728 | tf_op jit(solution)/shard_map/kna,kab->knb/dot_general | solution.py:80
  81.3 2.4 %reshape.369 = f32[3,2,32,1024]{3,1,2,0:T(2,128)} reshape(f32[3,2,32,8,128]{4,3,1,2,0:T(8,128)} %convolution_bitcast_fusion.2) | data formatting | bytes 1572864 | tf_op jit(solution)/shard_map/reshape | solution.py:84
  83.7 1.6 %add_convert_fusion = bf16[3,2,32,1024]{3,1,2,0:T(2,128)(2,1)S(1)} fusion(f32[3,2,32,1024]{3,1,2,0:T(2,128)S(1)} %reshape.359, f32[3,2,32,1024]{3,1,2,0:T(2,128)} %reshape.369, f32[32,1024]{1,0:T(8,128)S(1)} %compare_convert_fusion), kind=kLoop, calls=%fused_computation.32 | loop fusion | flops 589824 | bytes 2097152 | tf_op jit(solution)/shard_map/convert_element_type | solution.py:148
  85.3 1.9 %collective-permute-start.8 = (bf16[3,2,32,1024]{3,1,2,0:T(2,128)(2,1)S(1)}, bf16[3,2,32,1024]{3,1,2,0:T(2,128)(2,1)S(1)}, u32[]{:S(2)}, u32[]{:S(2)}) collective-permute-start(bf16[3,2,32,1024]{3,1,2,0:T(2,128)(2,1)S(1)} %add_convert_fusion), channel_id=1, source_target_pairs={{0,8},{8,16},{16,24},{1,9},{9,17},{17,25},{2,10},{10,18},{18,26},{... | collective-permute-start | bytes 1179656 | tf_op jit(solution)/shard_map/ppermute | solution.py:30
  87.2 12.2 %collective-permute-done.8 = bf16[3,2,32,1024]{3,1,2,0:T(2,128)(2,1)S(1)} collective-permute-done((bf16[3,2,32,1024]{3,1,2,0:T(2,128)(2,1)S(1)}, bf16[3,2,32,1024]{3,1,2,0:T(2,128)(2,1)S(1)}, u32[]{:S(2)}, u32[]{:S(2)}) %collective-permute-start.8) | collective-permute-done | bytes 393248 | tf_op jit(solution)/shard_map/ppermute | solution.py:30
  99.4 1.0 fusion.33
  100.4 1.9 %collective-permute-start.10 = (bf16[3,2,16,1024]{3,1,2,0:T(2,128)(2,1)}, bf16[3,2,16,1024]{3,1,2,0:T(2,128)(2,1)S(1)}, u32[]{:S(2)}, u32[]{:S(2)}) collective-permute-start(bf16[3,2,16,1024]{3,1,2,0:T(2,128)(2,1)} %get-tuple-element.14), channel_id=1, source_target_pairs={{1,0},{2,1},{3,2},{4,3},{5,4},{6,5},{7,6},{9,8},{10,9},{11,10},{12... | collective-permute-start | bytes 589832 | tf_op jit(solution)/shard_map/ppermute | solution.py:22
  102.3 2.6 %collective-permute-start.9 = (bf16[3,2,16,1024]{3,1,2,0:T(2,128)(2,1)}, bf16[3,2,16,1024]{3,1,2,0:T(2,128)(2,1)}, u32[]{:S(2)}, u32[]{:S(2)}) collective-permute-start(bf16[3,2,16,1024]{3,1,2,0:T(2,128)(2,1)} %get-tuple-element.13), channel_id=1, source_target_pairs={{0,1},{1,2},{2,3},{3,4},{4,5},{5,6},{6,7},{8,9},{9,10},{10,11},{11... | collective-permute-start | bytes 589832 | tf_op jit(solution)/shard_map/ppermute | solution.py:19
  105.4 1.3 %reshape.385 = f32[1,3,2,32,1024]{4,2,3,1,0:T(2,128)} reshape(f32[3,2,32,8,128]{4,3,1,2,0:T(8,128)S(1)} %convolution_bitcast_fusion.4) | data formatting | bytes 1572864 | tf_op jit(solution)/shard_map/reshape | solution.py:84
  107.1 0.7 copy-done
  108.2 1.4 %collective-permute-done.9 = bf16[3,2,16,1024]{3,1,2,0:T(2,128)(2,1)} collective-permute-done((bf16[3,2,16,1024]{3,1,2,0:T(2,128)(2,1)}, bf16[3,2,16,1024]{3,1,2,0:T(2,128)(2,1)}, u32[]{:S(2)}, u32[]{:S(2)}) %collective-permute-start.9) | collective-permute-done | bytes 196640 | tf_op jit(solution)/shard_map/ppermute | solution.py:19
  109.6 2.1 %pad_maximum_fusion.4 = bf16[3,2,64,1024]{3,1,2,0:T(2,128)(2,1)S(1)} fusion(bf16[3,2,16,1024]{3,1,2,0:T(2,128)(2,1)S(1)} %collective-permute-done.10, bf16[3,2,32,1024]{3,1,2,0:T(2,128)(2,1)} %copy-done.3, bf16[3,2,16,1024]{3,1,2,0:T(2,128)(2,1)} %collective-permute-done.9), kind=kLoop, calls=%fused_computation.17 | loop fusion | flops 786432 | bytes 1572864 | tf_op jit(solution)/shard_map/concatenate | solution.py:23
  112.9 0.8 copy-done.8
  113.9 1.4 %convolution_bitcast_fusion.1 = f32[3,2,32,8,128]{4,3,1,2,0:T(8,128)} fusion(bf16[3,256,768]{2,1,0:T(8,128)(2,1)S(1)} %bitcast.289, bf16[1,768,256]{2,1,0:T(8,128)(2,1)S(1)} %copy-done.8, bf16[1,768,256]{2,1,0:T(8,128)(2,1)S(1)} %copy-done.16, bf16[1,768,256]{2,1,0:T(8,128)(2,1)S(1)} %copy-done.12), kind=kOutput, calls=%fused_computation.1 | convolution fusion | flops 303169536 | bytes 3145728 | tf_op jit(solution)/shard_map/kna,kab->knb/dot_general | solution.py:80
  115.3 2.5 %reshape.382 = f32[1,3,2,32,1024]{4,2,3,1,0:T(2,128)} reshape(f32[3,2,32,8,128]{4,3,1,2,0:T(8,128)} %convolution_bitcast_fusion.1) | data formatting | bytes 1572864 | tf_op jit(solution)/shard_map/reshape | solution.py:84
  117.9 3.0 %fusion.10 = bf16[1,3,2,32,1024]{4,3,2,1,0:T(8,128)(2,1)} fusion(f32[1,3,2,32,1024]{4,2,3,1,0:T(2,128)S(1)} %reshape.375, f32[1,3,2,32,1024]{4,2,3,1,0:T(2,128)} %reshape.382, f32[1,3,2,32,1024]{4,2,3,1,0:T(2,128)S(1)} %reshape.383, f32[1,3,2,32,1024]{4,2,3,1,0:T(2,128)S(1)} %reshape.384, f32[1,3,2,32,1024]{4,2,3,1,0:T(2,128)S(1)} %copy-done.1, ...), kind=kLoop, calls=%fused_computation.43 | loop fusion | flops 3145728 | bytes 4456452 | tf_op jit(solution)/shard_map/jit(_where)/select_n | solution.py:164
  (149 shorter events, 12.9 us)
Async XLA Ops:
  1.8 18.1 %collective-permute-start = (bf16[3,2,16,1024]{3,2,1,0:T(8,128)(2,1)}, bf16[3,2,16,1024]{3,2,1,0:T(8,128)(2,1)}, u32[]{:S(2)}, u32[]{:S(2)}) collective-permute-start(bf16[3,2,16,1024]{3,2,1,0:T(8,128)(2,1)} %get-tuple-element.25), channel_id=1, source_target_pairs={{0,1},{1,2},{2,3},{3,4},{4,5},{5,6},{6,7},{8,9},{9,10},{10,11},{11... | collective-permute-start | bytes 589832 | tf_op jit(solution)/shard_map/ppermute | solution.py:19
  3.7 16.2 %collective-permute-start.1 = (bf16[3,2,16,1024]{3,2,1,0:T(8,128)(2,1)}, bf16[3,2,16,1024]{3,2,1,0:T(8,128)(2,1)}, u32[]{:S(2)}, u32[]{:S(2)}) collective-permute-start(bf16[3,2,16,1024]{3,2,1,0:T(8,128)(2,1)} %get-tuple-element.26), channel_id=1, source_target_pairs={{1,0},{2,1},{3,2},{4,3},{5,4},{6,5},{7,6},{9,8},{10,9},{11,10},{12... | collective-permute-start | bytes 589832 | tf_op jit(solution)/shard_map/ppermute | solution.py:22
  11.9 1.3 %copy-start.19 = (bf16[1,3,2,33]{3,2,1,0:T(2,128)(2,1)S(1)}, bf16[1,3,2,33]{3,2,1,0:T(2,128)(2,1)}, u32[]{:S(2)}) copy-start(bf16[1,3,2,33]{3,2,1,0:T(2,128)(2,1)} %param.8) | copy-start | bytes 1192
  14.3 0.7 copy-start.21
  14.3 0.7 copy-start.20
  14.3 1.0 copy-start.4
  17.2 0.7 copy-start.18
  17.7 0.9 copy-start.17
  18.4 1.5 %copy-start.2 = (bf16[3,2,32,1024]{3,2,1,0:T(8,128)(2,1)S(1)}, bf16[3,2,32,1024]{3,2,1,0:T(8,128)(2,1)}, u32[]{:S(2)}) copy-start(bf16[3,2,32,1024]{3,2,1,0:T(8,128)(2,1)} %param.7) | copy-start | bytes 1179652
  18.5 3.7 %copy-start.5 = (bf16[1,768,256]{2,1,0:T(8,128)(2,1)}, bf16[1,768,256]{2,1,0:T(8,128)(2,1)S(1)}, u32[]{:S(2)}) copy-start(bf16[1,768,256]{2,1,0:T(8,128)(2,1)S(1)} %maximum_bitcast_fusion.6) | copy-start | bytes 1179652
  19.9 2.3 %copy-start.9 = (bf16[1,768,256]{2,1,0:T(8,128)(2,1)}, bf16[1,768,256]{2,1,0:T(8,128)(2,1)S(1)}, u32[]{:S(2)}) copy-start(bf16[1,768,256]{2,1,0:T(8,128)(2,1)S(1)} %get-tuple-element.48) | copy-start | bytes 1179652
  19.9 2.3 %copy-start.13 = (bf16[1,768,256]{2,1,0:T(8,128)(2,1)}, bf16[1,768,256]{2,1,0:T(8,128)(2,1)S(1)}, u32[]{:S(2)}) copy-start(bf16[1,768,256]{2,1,0:T(8,128)(2,1)S(1)} %get-tuple-element.49) | copy-start | bytes 1179652
  23.6 13.8 %collective-permute-start.2 = (bf16[3,2,32,1024]{3,1,2,0:T(2,128)(2,1)S(1)}, bf16[3,2,32,1024]{3,1,2,0:T(2,128)(2,1)S(1)}, u32[]{:S(2)}, u32[]{:S(2)}) collective-permute-start(bf16[3,2,32,1024]{3,1,2,0:T(2,128)(2,1)S(1)} %add_convert_fusion.2), channel_id=1, source_target_pairs={{0,8},{8,16},{16,24},{1,9},{9,17},{17,25},{2,10},{10,18},{18,26},{... | collective-permute-start | bytes 1179656 | tf_op jit(solution)/shard_map/ppermute | solution.py:30
  37.6 7.0 %collective-permute-start.3 = (bf16[3,2,16,1024]{3,1,2,0:T(2,128)(2,1)S(1)}, bf16[3,2,16,1024]{3,1,2,0:T(2,128)(2,1)S(1)}, u32[]{:S(2)}, u32[]{:S(2)}) collective-permute-start(bf16[3,2,16,1024]{3,1,2,0:T(2,128)(2,1)S(1)} %get-tuple-element.21), channel_id=1, source_target_pairs={{0,1},{1,2},{2,3},{3,4},{4,5},{5,6},{6,7},{8,9},{9,10},{10,11},{11... | collective-permute-start | bytes 589832 | tf_op jit(solution)/shard_map/ppermute | solution.py:19
  39.5 6.8 %collective-permute-start.4 = (bf16[3,2,16,1024]{3,1,2,0:T(2,128)(2,1)S(1)}, bf16[3,2,16,1024]{3,1,2,0:T(2,128)(2,1)S(1)}, u32[]{:S(2)}, u32[]{:S(2)}) collective-permute-start(bf16[3,2,16,1024]{3,1,2,0:T(2,128)(2,1)S(1)} %get-tuple-element.22), channel_id=1, source_target_pairs={{1,0},{2,1},{3,2},{4,3},{5,4},{6,5},{7,6},{9,8},{10,9},{11,10},{12... | collective-permute-start | bytes 589832 | tf_op jit(solution)/shard_map/ppermute | solution.py:22
  48.4 1.0 copy-start.6
  48.4 1.1 copy-start.10
  48.4 1.2 %copy-start.14 = (bf16[1,768,256]{2,1,0:T(8,128)(2,1)S(1)}, bf16[1,768,256]{2,1,0:T(8,128)(2,1)}, u32[]{:S(2)}) copy-start(bf16[1,768,256]{2,1,0:T(8,128)(2,1)} %copy-done.13) | copy-start | bytes 1179652
  53.0 14.5 %collective-permute-start.5 = (bf16[3,2,32,1024]{3,1,2,0:T(2,128)(2,1)S(1)}, bf16[3,2,32,1024]{3,1,2,0:T(2,128)(2,1)S(1)}, u32[]{:S(2)}, u32[]{:S(2)}) collective-permute-start(bf16[3,2,32,1024]{3,1,2,0:T(2,128)(2,1)S(1)} %add_convert_fusion.1), channel_id=1, source_target_pairs={{0,8},{8,16},{16,24},{1,9},{9,17},{17,25},{2,10},{10,18},{18,26},{... | collective-permute-start | bytes 1179656 | tf_op jit(solution)/shard_map/ppermute | solution.py:30
  67.8 7.0 %collective-permute-start.6 = (bf16[3,2,16,1024]{3,1,2,0:T(2,128)(2,1)S(1)}, bf16[3,2,16,1024]{3,1,2,0:T(2,128)(2,1)S(1)}, u32[]{:S(2)}, u32[]{:S(2)}) collective-permute-start(bf16[3,2,16,1024]{3,1,2,0:T(2,128)(2,1)S(1)} %get-tuple-element.17), channel_id=1, source_target_pairs={{0,1},{1,2},{2,3},{3,4},{4,5},{5,6},{6,7},{8,9},{9,10},{10,11},{11... | collective-permute-start | bytes 589832 | tf_op jit(solution)/shard_map/ppermute | solution.py:19
  69.8 6.7 %collective-permute-start.7 = (bf16[3,2,16,1024]{3,1,2,0:T(2,128)(2,1)S(1)}, bf16[3,2,16,1024]{3,1,2,0:T(2,128)(2,1)S(1)}, u32[]{:S(2)}, u32[]{:S(2)}) collective-permute-start(bf16[3,2,16,1024]{3,1,2,0:T(2,128)(2,1)S(1)} %get-tuple-element.18), channel_id=1, source_target_pairs={{1,0},{2,1},{3,2},{4,3},{5,4},{6,5},{7,6},{9,8},{10,9},{11,10},{12... | collective-permute-start | bytes 589832 | tf_op jit(solution)/shard_map/ppermute | solution.py:22
  78.6 1.0 copy-start.7
  78.6 1.1 copy-start.11
  78.6 1.2 %copy-start.15 = (bf16[1,768,256]{2,1,0:T(8,128)(2,1)S(1)}, bf16[1,768,256]{2,1,0:T(8,128)(2,1)}, u32[]{:S(2)}) copy-start(bf16[1,768,256]{2,1,0:T(8,128)(2,1)} %copy-done.13) | copy-start | bytes 1179652
  85.3 14.1 %collective-permute-start.8 = (bf16[3,2,32,1024]{3,1,2,0:T(2,128)(2,1)S(1)}, bf16[3,2,32,1024]{3,1,2,0:T(2,128)(2,1)S(1)}, u32[]{:S(2)}, u32[]{:S(2)}) collective-permute-start(bf16[3,2,32,1024]{3,1,2,0:T(2,128)(2,1)S(1)} %add_convert_fusion), channel_id=1, source_target_pairs={{0,8},{8,16},{16,24},{1,9},{9,17},{17,25},{2,10},{10,18},{18,26},{... | collective-permute-start | bytes 1179656 | tf_op jit(solution)/shard_map/ppermute | solution.py:30
  99.4 2.9 %copy-start.3 = (bf16[3,2,32,1024]{3,1,2,0:T(2,128)(2,1)}, bf16[3,2,32,1024]{3,1,2,0:T(2,128)(2,1)S(1)}, u32[]{:S(2)}) copy-start(bf16[3,2,32,1024]{3,1,2,0:T(2,128)(2,1)S(1)} %collective-permute-done.8) | copy-start | bytes 1179652
  100.4 7.8 %collective-permute-start.10 = (bf16[3,2,16,1024]{3,1,2,0:T(2,128)(2,1)}, bf16[3,2,16,1024]{3,1,2,0:T(2,128)(2,1)S(1)}, u32[]{:S(2)}, u32[]{:S(2)}) collective-permute-start(bf16[3,2,16,1024]{3,1,2,0:T(2,128)(2,1)} %get-tuple-element.14), channel_id=1, source_target_pairs={{1,0},{2,1},{3,2},{4,3},{5,4},{6,5},{7,6},{9,8},{10,9},{11,10},{12... | collective-permute-start | bytes 589832 | tf_op jit(solution)/shard_map/ppermute | solution.py:22
  102.3 7.3 %collective-permute-start.9 = (bf16[3,2,16,1024]{3,1,2,0:T(2,128)(2,1)}, bf16[3,2,16,1024]{3,1,2,0:T(2,128)(2,1)}, u32[]{:S(2)}, u32[]{:S(2)}) collective-permute-start(bf16[3,2,16,1024]{3,1,2,0:T(2,128)(2,1)} %get-tuple-element.13), channel_id=1, source_target_pairs={{0,1},{1,2},{2,3},{3,4},{4,5},{5,6},{6,7},{8,9},{9,10},{10,11},{11... | collective-permute-start | bytes 589832 | tf_op jit(solution)/shard_map/ppermute | solution.py:19
  106.7 1.1 copy-start
  112.7 1.0 copy-start.8
  112.7 1.1 copy-start.12
  112.7 1.2 %copy-start.16 = (bf16[1,768,256]{2,1,0:T(8,128)(2,1)S(1)}, bf16[1,768,256]{2,1,0:T(8,128)(2,1)}, u32[]{:S(2)}) copy-start(bf16[1,768,256]{2,1,0:T(8,128)(2,1)} %copy-done.13) | copy-start | bytes 1179652
  115.3 2.5 %copy-start.1 = (f32[1,3,2,32,1024]{4,2,3,1,0:T(2,128)S(1)}, f32[1,3,2,32,1024]{4,2,3,1,0:T(2,128)}, u32[]{:S(2)}) copy-start(f32[1,3,2,32,1024]{4,2,3,1,0:T(2,128)} %reshape.385) | copy-start | bytes 2359300
where the time goes:
time: 122 us; the launch traced here: 121 us
  waiting for transfers between devices  42.1 us (35%)
  starting transfers between devices  29.2 us (24%)
  local copies, waits for them, and re-layouts  27 us (22%)
  other arithmetic  15 us (12%)
  matrix products  6.55 us (5%)
    ppermute x3, waiting for transfers between devices, from_behind(): return lax.ppermute(value, axis, pairs)  34.5 us
    ppermute x4, starting transfers between devices, padded_2(): lax.ppermute(lax.slice_in_dim(block, 0, width, axis=dim), axis, backward)  12.9 us
    reshape x7, local copies, waits for them, and re-layouts, apply_columns(): return mixed_cols.reshape(colour_count, height, tile_count, 2, 128).trans...  8.76 us
    ppermute x4, starting transfers between devices, padded_2(): lax.ppermute(lax.slice_in_dim(block, block.shape[dim] - width, None, axis...  8.48 us
    ppermute x3, starting transfers between devices, from_behind(): return lax.ppermute(value, axis, pairs)  7.84 us
    concatenate x4, other arithmetic, padded_2(): block = jnp.concatenate([low, block, high], axis=dim)  5.68 us
    unnamed x60, local copies, waits for them, and re-layouts  5.13 us
    ppermute x4, waiting for transfers between devices, padded_2(): lax.ppermute(lax.slice_in_dim(block, block.shape[dim] - width, None, axis...  4.04 us
  transfers between devices with their start and end apart: 11, of which 8 were waited for; matrix products, arithmetic and copies ran while one was open for 12% of the time, Pallas kernels for 0%

commit v1 on v0

v1 whole, which is shorter than its diff:
```python
import math

import jax
import jax.numpy as jnp
import numpy as np
from jax import lax
from jax.experimental import pallas as pl
from jax.experimental.pallas import tpu as pltpu
from jax.sharding import PartitionSpec as P

HS = 16
KR = 16
KC = 63
COLORS = 3
LAYERS = 4
BAND = 32
COLS = 1024
NH = COLS // HS
LANES = 128
TILES = COLS // LANES
HALO_W = COLS + LANES
FULL_W = COLS + 2 * LANES
NEAR = 2 * BAND + KR
FAR = KR
VMEM_LIMIT = 48 * 1024 * 1024


def split_table(table):
    high = table.astype(jnp.bfloat16)
    low = (table - high.astype(np.float64)).astype(jnp.bfloat16)
    return high, low


def dft_pair():
    counter = np.arange(HS)
    angles = (counter[:, None] * counter[None, :] % HS) * (2.0 * math.pi / HS)
    return np.cos(angles) / math.sqrt(HS), np.sin(angles) / math.sqrt(HS)


def left_table(height):
    cos_tab, sin_tab = dft_pair()
    eye = np.eye(height // HS)
    full = np.concatenate([np.kron(eye, cos_tab), np.kron(eye, -sin_tab)], axis=0)
    return np.concatenate(split_table(full), axis=1)


def right_table():
    cos_tab, sin_tab = dft_pair()
    eye = np.eye(LANES // HS)
    cos_big, sin_big = np.kron(eye, cos_tab), np.kron(eye, sin_tab)
    full = np.concatenate(
        [
            np.concatenate([cos_big, -sin_big], axis=1),
            np.concatenate([sin_big, cos_big], axis=1),
        ],
        axis=0,
    )
    return np.concatenate(split_table(full), axis=0)


def layer_height(layer):
    return BAND + 2 * KR * (LAYERS - 1 - layer)


def spread_matrix():
    tile = lax.broadcasted_iota(jnp.int32, (NH, COLS), 0)
    column = lax.broadcasted_iota(jnp.int32, (NH, COLS), 1)
    return jnp.where(column // HS == tile, 1.0, 0.0).astype(jnp.bfloat16)


def pack_kernel(light, edges, counts, listed, row_taps, col_taps, out, taps):
    slot = lax.broadcasted_iota(jnp.int32, (NH, NH), 0)
    place = lax.broadcasted_iota(jnp.int32, (NH, NH), 1)
    rows = []
    for group in range(BAND // HS):
        listing = jnp.broadcast_to(listed[0, group : group + 1, :], (NH, NH))
        column = jnp.sum(jnp.where(slot == place, listing, 0), axis=1, keepdims=True)
        named = (column == place) & (slot < counts[0, group])
        live = jnp.max(jnp.where(named, 1.0, 0.0), axis=0, keepdims=True)
        rows.append(jnp.broadcast_to(live, (HS, NH)))
    live_rows = jnp.concatenate(rows, axis=0).astype(jnp.bfloat16)
    live_pix = jnp.dot(live_rows, spread_matrix(), preferred_element_type=jnp.float32)
    edge_tile = jnp.concatenate(
        [edges[0].astype(jnp.float32), jnp.zeros((BAND, LANES - NH), jnp.float32)], axis=1
    ).astype(jnp.bfloat16)
    for colour in range(COLORS):
        out[colour, :, :COLS] = (light[0, colour] * live_pix).astype(jnp.bfloat16)
        out[colour, :, COLS:HALO_W] = edge_tile
        taps[...] = jnp.zeros_like(taps)
        taps[0:2, : 2 * KC + 1] = col_taps[0, colour].astype(jnp.float32)
        taps[2:4, : 2 * KR + 1] = row_taps[0, colour].astype(jnp.float32)
        out[colour, :, HALO_W:] = taps[...].astype(jnp.bfloat16)
    for spare in range(COLORS, LAYERS):
        out[spare] = jnp.zeros((BAND, FULL_W), jnp.bfloat16)


def halo_kernel(own, incident, up_near, down_near, up_far, down_far):
    for near in (up_near, down_near):
        near[0:BAND] = own[0, :, :HALO_W]
        near[BAND : 2 * BAND] = own[1, :, :HALO_W]
        near[NEAR : NEAR + BAND, :COLS] = incident[0]
        near[NEAR + BAND :, :COLS] = incident[1]
    up_near[2 * BAND : NEAR] = own[2, BAND - KR :, :HALO_W]
    down_near[2 * BAND : NEAR] = own[2, :KR, :HALO_W]
    up_far[0:FAR] = own[0, BAND - KR :, :HALO_W]
    down_far[0:FAR] = own[0, :KR, :HALO_W]
    for far in (up_far, down_far):
        far[FAR : FAR + BAND, :COLS] = incident[0]
        far[FAR + BAND :, :COLS] = incident[1]


def chain_kernel(
    own, incident, low_near, high_near, low_far, high_far, right_tab, *rest
):
    left_tabs, (out, field) = rest[:LAYERS], rest[LAYERS:]
    spread = spread_matrix()
    within = (lax.broadcasted_iota(jnp.int32, (1, COLS), 1) % HS).astype(jnp.float32)
    extended = []
    for part in range(2):
        near = slice(NEAR + part * BAND, NEAR + (part + 1) * BAND)
        far = slice(FAR + part * BAND, FAR + (part + 1) * BAND)
        pieces = [
            low_far[far, :COLS],
            low_near[near, :COLS],
            incident[part],
            high_near[near, :COLS],
            high_far[far, :COLS],
        ]
        extended.append(jnp.concatenate(pieces, axis=0))
    for layer in range(LAYERS):
        height = layer_height(layer)
        before = height + 2 * KR
        if layer == 0:
            pieces = [low_far[0:FAR], low_near[0:BAND], own[0, :, :HALO_W], high_near[0:BAND], high_far[0:FAR]]
        elif layer == 1:
            band = slice(BAND, 2 * BAND)
            pieces = [low_near[band], own[1, :, :HALO_W], high_near[band]]
        elif layer == 2:
            band = slice(2 * BAND, NEAR)
            pieces = [low_near[band], own[2, :, :HALO_W], high_near[band]]
        else:
            pieces = [own[3, :, :HALO_W]]
        packed = jnp.concatenate(pieces, axis=0) if len(pieces) > 1 else pieces[0]
        light = packed[:, :COLS]
        edge_pix = jnp.dot(packed[:, COLS : COLS + NH], spread, preferred_element_type=jnp.float32)
        clear = jnp.where(within < edge_pix, 1.0, 0.0)

        taps = own[layer, 0:16, HALO_W:].astype(jnp.float32)
        blank = jnp.zeros((1, LANES), jnp.float32)

        def banded(line, count, shift):
            base = jnp.concatenate([taps[line : line + 1], blank], axis=1)
            base = jnp.broadcast_to(base, (count, 2 * LANES))
            return pltpu.roll(base, shift, 1, stride=1, stride_axis=0)

        row_re = banded(2, height, 0)[:, :before]
        row_im = banded(3, height, 0)[:, :before]
        from_re = jnp.concatenate([row_re, row_im], axis=0).astype(jnp.bfloat16)
        from_im = jnp.concatenate([-row_im, row_re], axis=0).astype(jnp.bfloat16)
        col_re = banded(0, LANES, 1)
        col_im = banded(1, LANES, 1)
        col_mat = jnp.concatenate(
            [
                jnp.concatenate([col_re, -col_im], axis=1),
                jnp.concatenate([col_im, col_re], axis=1),
            ],
            axis=0,
        ).astype(jnp.bfloat16)

        if layer == 0:
            u_re, u_im = extended
        else:
            u_re, u_im = field[0, :before], field[1, :before]
        rowed = jnp.dot(from_re, u_re, preferred_element_type=jnp.float32)
        rowed = rowed + jnp.dot(from_im, u_im, preferred_element_type=jnp.float32)
        rowed = jnp.concatenate([rowed, jnp.zeros((2 * height, LANES), jnp.float32)], axis=1)
        rowed = pltpu.roll(rowed, LANES // 2, 1).astype(jnp.bfloat16)
        windows = jnp.concatenate(
            [
                jnp.concatenate(
                    [
                        rowed[:height, tile * LANES : (tile + 2) * LANES],
                        rowed[height:, tile * LANES : (tile + 2) * LANES],
                    ],
                    axis=1,
                )
                for tile in range(TILES)
            ],
            axis=0,
        )
        columned = lax.dot_general(
            windows, col_mat, (((1,), (1,)), ((), ())), preferred_element_type=jnp.float32
        )

        left = jnp.dot(
            left_tabs[layer][...],
            jnp.concatenate([light, light], axis=0),
            preferred_element_type=jnp.float32,
        ).astype(jnp.bfloat16)
        arranged = jnp.concatenate(
            [
                jnp.concatenate(
                    [
                        left[:height, tile * LANES : (tile + 1) * LANES],
                        left[height:, tile * LANES : (tile + 1) * LANES],
                    ],
                    axis=1,
                )
                for tile in range(TILES)
            ],
            axis=0,
        )
        stereo = jnp.dot(
            jnp.concatenate([arranged, arranged], axis=1),
            right_tab[...],
            preferred_element_type=jnp.float32,
        )
        for tile in range(TILES):
            span = slice(tile * height, (tile + 1) * height)
            lanes = slice(tile * LANES, (tile + 1) * LANES)
            for part in range(2):
                side = slice(part * LANES, (part + 1) * LANES)
                value = clear[:, lanes] * columned[span, side] + stereo[span, side]
                field[part, :height, lanes] = value.astype(jnp.bfloat16)
        start = (height - BAND) // 2
        for part in range(2):
            out[layer, part] = field[part, start : start + BAND]


def shifted(value, axis, by):
    count = lax.axis_size(axis)
    pairs = [(i, i + by) for i in range(count) if 0 <= i + by < count]
    return lax.ppermute(value, axis, pairs)


def params():
    return pltpu.CompilerParams(vmem_limit_bytes=VMEM_LIMIT)


def body(incident, row_taps, col_taps, hogel_light, silhouette, fill_counts, hogel_index):
    vmem = pl.BlockSpec(memory_space=pltpu.VMEM)
    smem = pl.BlockSpec(memory_space=pltpu.SMEM)
    bf16 = jnp.bfloat16
    payload = pl.pallas_call(
        pack_kernel,
        out_shape=jax.ShapeDtypeStruct((LAYERS, BAND, FULL_W), bf16),
        in_specs=[vmem, vmem, smem, vmem, vmem, vmem],
        out_specs=vmem,
        scratch_shapes=[pltpu.VMEM((BAND, LANES), jnp.float32)],
        compiler_params=params(),
        cost_estimate=pl.CostEstimate(flops=10**7, bytes_accessed=10**6, transcendentals=0),
    )(hogel_light, silhouette, fill_counts, hogel_index, row_taps, col_taps)
    own = lax.all_to_all(payload, "depth", 0, 0, tiled=True)
    colour = jnp.minimum(lax.axis_index("depth"), COLORS - 1)
    mine = lax.dynamic_index_in_dim(incident, colour, 0, keepdims=False)
    near = jax.ShapeDtypeStruct((NEAR + 2 * BAND, HALO_W), bf16)
    far = jax.ShapeDtypeStruct((FAR + 2 * BAND, HALO_W), bf16)
    up_near, down_near, up_far, down_far = pl.pallas_call(
        halo_kernel,
        out_shape=(near, near, far, far),
        in_specs=[vmem, vmem],
        out_specs=(vmem,) * 4,
        compiler_params=params(),
        cost_estimate=pl.CostEstimate(flops=0, bytes_accessed=2 * 10**6, transcendentals=0),
    )(own, mine)
    low_near = shifted(up_near, "rows", 1)
    high_near = shifted(down_near, "rows", -1)
    low_far = shifted(up_far, "rows", 2)
    high_far = shifted(down_far, "rows", -2)
    tables = [jnp.asarray(right_table())]
    tables += [jnp.asarray(left_table(layer_height(layer))) for layer in range(LAYERS)]
    result = pl.pallas_call(
        chain_kernel,
        out_shape=jax.ShapeDtypeStruct((LAYERS, 2, BAND, COLS), bf16),
        in_specs=[vmem] * (6 + len(tables)),
        out_specs=vmem,
        scratch_shapes=[pltpu.VMEM((2, layer_height(0), COLS), bf16)],
        compiler_params=params(),
        cost_estimate=pl.CostEstimate(flops=3 * 10**9, bytes_accessed=3 * 10**6, transcendentals=0),
    )(own, mine, low_near, high_near, low_far, high_far, *tables)
    gathered = lax.all_to_all(result, "depth", 0, 0, tiled=True)
    return gathered[None, :COLORS]


def solution(mesh):
    placed = (
        P(None, None, "rows", None),
        P("depth", None, None, None),
        P("depth", None, None, None),
        P("depth", None, "rows", None),
        P("depth", "rows", None),
        P("depth", "rows"),
        P("depth", "rows", None),
    )
    return jax.shard_map(
        body,
        mesh=mesh,
        in_specs=placed,
        out_specs=P("depth", None, None, "rows", None),
        check_vma=False,
    )
```

time: 122 us -> 49.7 us (0.41)
  the two profiles are of different devices: /device:TPU:20 before, /device:TPU:0 now
where the time goes in v1:
time: 49.7 us; the launch traced here: 49.3 us
  starting transfers between devices  15.5 us (31%)
  waiting for transfers between devices  12.6 us (25%)
  blocking collectives  10.1 us (20%)
  Pallas kernels  5.58 us (11%)
  local copies, waits for them, and re-layouts  5.28 us (11%)
    ppermute x4, starting transfers between devices, shifted(): return lax.ppermute(value, axis, pairs)  10.3 us
    all_to_all x1, blocking collectives, body(): gathered = lax.all_to_all(result, 'depth', 0, 0, tiled=True)  10.1 us
    ppermute x4, waiting for transfers between devices, shifted(): return lax.ppermute(value, axis, pairs)  6.82 us
    all_to_all x1, waiting for transfers between devices, body(): own = lax.all_to_all(payload, 'depth', 0, 0, tiled=True)  5.82 us
    all_to_all x1, starting transfers between devices, body(): own = lax.all_to_all(payload, 'depth', 0, 0, tiled=True)  5.16 us
    unnamed x24, local copies, waits for them, and re-layouts  4.49 us
    pallas_call x1, Pallas kernels, body(): pl.pallas_call(chain_kernel, out_shape=jax.ShapeDtypeStruct((LAYERS, 2, B...  4 us
    pallas_call x1, Pallas kernels, body(): pl.pallas_call(pack_kernel, out_shape=jax.ShapeDtypeStruct((LAYERS, BAND,...  1.52 us
  transfers between devices with their start and end apart: 5, of which 3 were waited for; matrix products, arithmetic and copies ran while one was open for 0% of the time, Pallas kernels for 0%

profile of v1, /device:TPU:0, one launch (start us, length us, event | category | flops | bytes accessed | tf_op | source)
XLA Modules:
  0.0 49.3 jit_solution(295607592705690710)
XLA Ops:
  0.0 0.0 copy-start
  0.0 0.0 copy-start.1
  0.0 1.0 %copy-done.1 = f32[1,3,32,1024]{3,2,1,0:T(8,128)S(1)} copy-done((f32[1,3,32,1024]{3,2,1,0:T(8,128)S(1)}, f32[1,3,32,1024]{3,2,1,0:T(8,128)}, u32[]{:S(2)}) %copy-start.1) | copy-done | bytes 393240
  1.1 0.0 copy-start.2
  1.1 0.7 %copy-done.2 = s32[1,32,64]{2,1,0:T(8,128)S(1)} copy-done((s32[1,32,64]{2,1,0:T(8,128)S(1)}, s32[1,32,64]{2,1,0:T(8,128)}, u32[]{:S(2)}) %copy-start.2) | copy-done | bytes 8216
  1.8 0.0 copy-start.3
  1.8 0.7 %copy-done.3 = bf16[1,3,2,33]{3,2,1,0:T(2,128)(2,1)S(1)} copy-done((bf16[1,3,2,33]{3,2,1,0:T(2,128)(2,1)S(1)}, bf16[1,3,2,33]{3,2,1,0:T(2,128)(2,1)}, u32[]{:S(2)}) %copy-start.3) | copy-done | bytes 420
  2.4 0.0 copy-start.4
  2.5 0.7 %copy-done.4 = bf16[1,3,2,127]{3,2,1,0:T(2,128)(2,1)S(1)} copy-done((bf16[1,3,2,127]{3,2,1,0:T(2,128)(2,1)S(1)}, bf16[1,3,2,127]{3,2,1,0:T(2,128)(2,1)}, u32[]{:S(2)}) %copy-start.4) | copy-done | bytes 1548
  3.1 0.0 copy-start.5
  3.1 0.7 %copy-done.5 = s32[1,2,64]{2,1,0:T(2,128)S(1)} copy-done((s32[1,2,64]{2,1,0:T(2,128)S(1)}, s32[1,2,64]{2,1,0:T(2,128)}, u32[]{:S(2)}) %copy-start.5) | copy-done | bytes 536
  3.8 0.0 copy-start.6
  3.8 0.7 %copy-done.6 = s32[1,2]{1,0:T(1,128)S(1)} copy-done((s32[1,2]{1,0:T(1,128)S(1)}, s32[1,2]{1,0:T(1,128)}, u32[]{:S(2)}) %copy-start.6) | copy-done | bytes 32
  4.5 1.5 %shard_map.118 = bf16[4,32,1280]{2,1,0:T(8,128)(2,1)} custom-call(f32[1,3,32,1024]{3,2,1,0:T(8,128)S(1)} %copy-done.1, s32[1,32,64]{2,1,0:T(8,128)S(1)} %copy-done.2, s32[1,2]{1,0:T(1,128)S(1)} %copy-done.6, s32[1,2,64]{2,1,0:T(2,128)S(1)} %copy-done.5, bf16[1,3,2,33]{3,2,1,0:T(2,128)(2,1)S(1)} %copy-done.3, bf16[1,3,2,127]{3,2,1,0:T(2,128)(2,1)S(1)} %copy-done.4), custom_call_target="tpu_custom_call" | custom-call | flops 10000000 | bytes 1000000 | tf_op jit(solution)/shard_map/pallas_call | solution.py:244
  6.0 5.2 %all-to-all-start = ((bf16[4,32,1280]{2,1,0:T(8,128)(2,1)}), bf16[4,32,1280]{2,1,0:T(8,128)(2,1)S(1)}, u32[]{:S(2)}, u32[]{:S(2)}) async-start(bf16[4,32,1280]{2,1,0:T(8,128)(2,1)} %shard_map.118), calls=%async_computation | async-start | bytes 655360 | tf_op jit(solution)/shard_map/all_to_all | solution.py:253
  11.2 0.0 copy-done
  11.2 0.0 copy-start.9
  11.2 0.0 copy-start.7
  11.2 0.0 copy-start.8
  11.2 0.0 copy-start.10
  11.2 0.0 copy-start.11
  11.2 5.8 %all-to-all-done.own = bf16[4,32,1280]{2,1,0:T(8,128)(2,1)S(1)} async-done(((bf16[4,32,1280]{2,1,0:T(8,128)(2,1)}), bf16[4,32,1280]{2,1,0:T(8,128)(2,1)S(1)}, u32[]{:S(2)}, u32[]{:S(2)}) %all-to-all-start) | async-done | bytes 327712 | tf_op jit(solution)/shard_map/all_to_all | solution.py:253
  17.0 0.1 shard_map.119
  17.1 1.3 %collective-permute-start = (bf16[144,1152]{1,0:T(8,128)(2,1)S(1)}, bf16[144,1152]{1,0:T(8,128)(2,1)S(1)}, u32[]{:S(2)}, u32[]{:S(2)}) collective-permute-start(bf16[144,1152]{1,0:T(8,128)(2,1)S(1)} %get-tuple-element.9), channel_id=1, source_target_pairs={{0,1},{1,2},{2,3},{3,4},{4,5},{5,6},{6,7},{8,9},{9,10},{10,11},{11... | collective-permute-start | bytes 995336 | tf_op jit(solution)/shard_map/ppermute | solution.py:233
  18.4 1.3 %collective-permute-start.1 = (bf16[144,1152]{1,0:T(8,128)(2,1)S(1)}, bf16[144,1152]{1,0:T(8,128)(2,1)S(1)}, u32[]{:S(2)}, u32[]{:S(2)}) collective-permute-start(bf16[144,1152]{1,0:T(8,128)(2,1)S(1)} %get-tuple-element.10), channel_id=1, source_target_pairs={{1,0},{2,1},{3,2},{4,3},{5,4},{6,5},{7,6},{9,8},{10,9},{11,10},{12... | collective-permute-start | bytes 995336 | tf_op jit(solution)/shard_map/ppermute | solution.py:233
  19.7 6.5 %collective-permute-start.2 = (bf16[80,1152]{1,0:T(8,128)(2,1)S(1)}, bf16[80,1152]{1,0:T(8,128)(2,1)S(1)}, u32[]{:S(2)}, u32[]{:S(2)}) collective-permute-start(bf16[80,1152]{1,0:T(8,128)(2,1)S(1)} %get-tuple-element.11), channel_id=1, source_target_pairs={{0,2},{1,3},{2,4},{3,5},{4,6},{5,7},{8,10},{9,11},{10,12},{11,13},... | collective-permute-start | bytes 552968 | tf_op jit(solution)/shard_map/ppermute | solution.py:233
  26.2 1.3 %collective-permute-start.3 = (bf16[80,1152]{1,0:T(8,128)(2,1)S(1)}, bf16[80,1152]{1,0:T(8,128)(2,1)S(1)}, u32[]{:S(2)}, u32[]{:S(2)}) collective-permute-start(bf16[80,1152]{1,0:T(8,128)(2,1)S(1)} %get-tuple-element.12), channel_id=1, source_target_pairs={{2,0},{3,1},{4,2},{5,3},{6,4},{7,5},{10,8},{11,9},{12,10},{13,11},... | collective-permute-start | bytes 552968 | tf_op jit(solution)/shard_map/ppermute | solution.py:233
  27.5 2.7 %collective-permute-done.2.low_far = bf16[80,1152]{1,0:T(8,128)(2,1)S(1)} collective-permute-done((bf16[80,1152]{1,0:T(8,128)(2,1)S(1)}, bf16[80,1152]{1,0:T(8,128)(2,1)S(1)}, u32[]{:S(2)}, u32[]{:S(2)}) %collective-permute-start.2) | collective-permute-done | bytes 184352 | tf_op jit(solution)/shard_map/ppermute | solution.py:233
  30.2 4.1 %collective-permute-done.3.high_far = bf16[80,1152]{1,0:T(8,128)(2,1)S(1)} collective-permute-done((bf16[80,1152]{1,0:T(8,128)(2,1)S(1)}, bf16[80,1152]{1,0:T(8,128)(2,1)S(1)}, u32[]{:S(2)}, u32[]{:S(2)}) %collective-permute-start.3) | collective-permute-done | bytes 184352 | tf_op jit(solution)/shard_map/ppermute | solution.py:233
  34.3 0.0 collective-permute-done.low_near
  34.3 0.0 collective-permute-done.1.high_near
  34.3 0.0 copy-done.9
  34.3 0.0 copy-done.7
  34.3 0.0 copy-done.8
  34.3 0.0 copy-done.10
  34.3 0.0 copy-done.11
  34.4 4.0 %shard_map.120 = bf16[4,2,32,1024]{3,2,1,0:T(8,128)(2,1)S(1)} custom-call(bf16[4,32,1280]{2,1,0:T(8,128)(2,1)S(1)} %all-to-all-done.own, bf16[2,32,1024]{2,1,0:T(8,128)(2,1)S(1)} %dynamic-slice_bitcast_fusion.incident, bf16[144,1152]{1,0:T(8,128)(2,1)S(1)} %collective-permute-done.low_near, bf16[144,1152]{1,0:T(8,128)(2,1)S(1)} %collective-permute-done.1.high_near, ...), custom_call_target="tpu_custom_call" | custom-call | flops 3000000000 | bytes 3000000 | tf_op jit(solution)/shard_map/pallas_call | solution.py:272
  38.4 10.1 %all_to_all.10 = bf16[4,2,32,1024]{3,2,1,0:T(8,128)(2,1)S(1)} all-to-all(bf16[4,2,32,1024]{3,2,1,0:T(8,128)(2,1)S(1)} %shard_map.120), channel_id=1, replica_groups=mesh['depth'=4,'rows'=8] {'depth'}, dimensions={0} | all-to-all | bytes 1048576 | tf_op jit(solution)/shard_map/all_to_all | solution.py:281
  48.5 0.8 %slice_bitcast_fusion = bf16[1,3,2,32,1024]{4,3,2,1,0:T(8,128)(2,1)} fusion(bf16[4,2,32,1024]{3,2,1,0:T(8,128)(2,1)S(1)} %all_to_all.10), kind=kLoop, calls=%fused_computation | loop fusion | bytes 786432 | tf_op jit(solution)/shard_map/broadcast_in_dim | solution.py:282
  (1 shorter events, 0.0 us)
Async XLA Ops:
  0.0 11.2 %copy-start = (bf16[3,2,32,1024]{3,2,1,0:T(8,128)(2,1)S(1)}, bf16[3,2,32,1024]{3,2,1,0:T(8,128)(2,1)}, u32[]{:S(2)}) copy-start(bf16[3,2,32,1024]{3,2,1,0:T(8,128)(2,1)} %param.12) | copy-start | bytes 1179652
  0.0 1.0 %copy-start.1 = (f32[1,3,32,1024]{3,2,1,0:T(8,128)S(1)}, f32[1,3,32,1024]{3,2,1,0:T(8,128)}, u32[]{:S(2)}) copy-start(f32[1,3,32,1024]{3,2,1,0:T(8,128)} %light.1) | copy-start | bytes 1179652
  1.1 0.7 %copy-start.2 = (s32[1,32,64]{2,1,0:T(8,128)S(1)}, s32[1,32,64]{2,1,0:T(8,128)}, u32[]{:S(2)}) copy-start(s32[1,32,64]{2,1,0:T(8,128)} %edges.1) | copy-start | bytes 24580
  1.8 0.7 %copy-start.3 = (bf16[1,3,2,33]{3,2,1,0:T(2,128)(2,1)S(1)}, bf16[1,3,2,33]{3,2,1,0:T(2,128)(2,1)}, u32[]{:S(2)}) copy-start(bf16[1,3,2,33]{3,2,1,0:T(2,128)(2,1)} %row_taps.1) | copy-start | bytes 1192
  2.4 0.7 %copy-start.4 = (bf16[1,3,2,127]{3,2,1,0:T(2,128)(2,1)S(1)}, bf16[1,3,2,127]{3,2,1,0:T(2,128)(2,1)}, u32[]{:S(2)}) copy-start(bf16[1,3,2,127]{3,2,1,0:T(2,128)(2,1)} %col_taps.1) | copy-start | bytes 4576
  3.1 0.7 %copy-start.5 = (s32[1,2,64]{2,1,0:T(2,128)S(1)}, s32[1,2,64]{2,1,0:T(2,128)}, u32[]{:S(2)}) copy-start(s32[1,2,64]{2,1,0:T(2,128)} %listed.1) | copy-start | bytes 1540
  3.8 0.7 %copy-start.6 = (s32[1,2]{1,0:T(1,128)S(1)}, s32[1,2]{1,0:T(1,128)}, u32[]{:S(2)}) copy-start(s32[1,2]{1,0:T(1,128)} %counts.1) | copy-start | bytes 28
  6.0 11.1 %all-to-all-start = ((bf16[4,32,1280]{2,1,0:T(8,128)(2,1)}), bf16[4,32,1280]{2,1,0:T(8,128)(2,1)S(1)}, u32[]{:S(2)}, u32[]{:S(2)}) async-start(bf16[4,32,1280]{2,1,0:T(8,128)(2,1)} %shard_map.118), calls=%async_computation | async-start | bytes 655360 | tf_op jit(solution)/shard_map/all_to_all | solution.py:253
  11.2 23.2 %copy-start.9 = (bf16[192,192]{1,0:T(8,128)(2,1)S(1)}, bf16[192,192]{1,0:T(8,128)(2,1)}, u32[]{:S(2)}) copy-start(bf16[192,192]{1,0:T(8,128)(2,1)} %constant.25.clone.rest_1_) | copy-start | bytes 221188
  11.2 23.1 %copy-start.7 = (bf16[512,256]{1,0:T(8,128)(2,1)S(1)}, bf16[512,256]{1,0:T(8,128)(2,1)}, u32[]{:S(2)}) copy-start(bf16[512,256]{1,0:T(8,128)(2,1)} %constant.23.clone.right_tab) | copy-start | bytes 786436
  11.2 23.1 %copy-start.8 = (bf16[256,256]{1,0:T(8,128)(2,1)S(1)}, bf16[256,256]{1,0:T(8,128)(2,1)}, u32[]{:S(2)}) copy-start(bf16[256,256]{1,0:T(8,128)(2,1)} %constant.24.clone.rest_0_) | copy-start | bytes 393220
  11.2 23.1 %copy-start.10 = (bf16[128,128]{1,0:T(8,128)(2,1)S(1)}, bf16[128,128]{1,0:T(8,128)(2,1)}, u32[]{:S(2)}) copy-start(bf16[128,128]{1,0:T(8,128)(2,1)} %constant.26.clone.rest_2_) | copy-start | bytes 98308
  11.2 23.1 %copy-start.11 = (bf16[64,64]{1,0:T(8,128)(2,1)S(1)}, bf16[64,64]{1,0:T(8,128)(2,1)}, u32[]{:S(2)}) copy-start(bf16[64,64]{1,0:T(8,128)(2,1)} %constant.27.clone.rest_3_) | copy-start | bytes 24580
  17.1 17.2 %collective-permute-start = (bf16[144,1152]{1,0:T(8,128)(2,1)S(1)}, bf16[144,1152]{1,0:T(8,128)(2,1)S(1)}, u32[]{:S(2)}, u32[]{:S(2)}) collective-permute-start(bf16[144,1152]{1,0:T(8,128)(2,1)S(1)} %get-tuple-element.9), channel_id=1, source_target_pairs={{0,1},{1,2},{2,3},{3,4},{4,5},{5,6},{6,7},{8,9},{9,10},{10,11},{11... | collective-permute-start | bytes 995336 | tf_op jit(solution)/shard_map/ppermute | solution.py:233
  18.4 15.9 %collective-permute-start.1 = (bf16[144,1152]{1,0:T(8,128)(2,1)S(1)}, bf16[144,1152]{1,0:T(8,128)(2,1)S(1)}, u32[]{:S(2)}, u32[]{:S(2)}) collective-permute-start(bf16[144,1152]{1,0:T(8,128)(2,1)S(1)} %get-tuple-element.10), channel_id=1, source_target_pairs={{1,0},{2,1},{3,2},{4,3},{5,4},{6,5},{7,6},{9,8},{10,9},{11,10},{12... | collective-permute-start | bytes 995336 | tf_op jit(solution)/shard_map/ppermute | solution.py:233
  19.7 10.4 %collective-permute-start.2 = (bf16[80,1152]{1,0:T(8,128)(2,1)S(1)}, bf16[80,1152]{1,0:T(8,128)(2,1)S(1)}, u32[]{:S(2)}, u32[]{:S(2)}) collective-permute-start(bf16[80,1152]{1,0:T(8,128)(2,1)S(1)} %get-tuple-element.11), channel_id=1, source_target_pairs={{0,2},{1,3},{2,4},{3,5},{4,6},{5,7},{8,10},{9,11},{10,12},{11,13},... | collective-permute-start | bytes 552968 | tf_op jit(solution)/shard_map/ppermute | solution.py:233
  26.2 8.1 %collective-permute-start.3 = (bf16[80,1152]{1,0:T(8,128)(2,1)S(1)}, bf16[80,1152]{1,0:T(8,128)(2,1)S(1)}, u32[]{:S(2)}, u32[]{:S(2)}) collective-permute-start(bf16[80,1152]{1,0:T(8,128)(2,1)S(1)} %get-tuple-element.12), channel_id=1, source_target_pairs={{2,0},{3,1},{4,2},{5,3},{6,4},{7,5},{10,8},{11,9},{12,10},{13,11},... | collective-permute-start | bytes 552968 | tf_op jit(solution)/shard_map/ppermute | solution.py:233

commit v2 on v1

v2 whole, which is shorter than its diff:
```python
import math

import jax
import jax.numpy as jnp
import numpy as np
from jax import lax
from jax.experimental import pallas as pl
from jax.experimental.pallas import tpu as pltpu
from jax.sharding import PartitionSpec as P

HS = 16
KR = 16
KC = 63
COLORS = 3
LAYERS = 4
BAND = 32
COLS = 1024
NH = COLS // HS
LANES = 128
TILES = COLS // LANES
HALO_W = COLS + LANES
HALF = LANES // 2
FULL_W = COLS + 2 * LANES
NEAR = 2 * BAND + KR
FAR = KR
VMEM_LIMIT = 48 * 1024 * 1024


def split_table(table):
    high = table.astype(jnp.bfloat16)
    low = (table - high.astype(np.float64)).astype(jnp.bfloat16)
    return high, low


def dft_pair():
    counter = np.arange(HS)
    angles = (counter[:, None] * counter[None, :] % HS) * (2.0 * math.pi / HS)
    return np.cos(angles) / math.sqrt(HS), np.sin(angles) / math.sqrt(HS)


def left_table():
    cos_tab, sin_tab = dft_pair()
    eye = np.eye(LANES // HS)
    full = np.concatenate([np.kron(eye, cos_tab), np.kron(eye, -sin_tab)], axis=0)
    return np.concatenate(split_table(full), axis=1)


def right_table():
    cos_tab, sin_tab = dft_pair()
    eye = np.eye(LANES // HS)
    cos_big, sin_big = np.kron(eye, cos_tab), np.kron(eye, sin_tab)
    full = np.concatenate(
        [
            np.concatenate([cos_big, -sin_big], axis=1),
            np.concatenate([sin_big, cos_big], axis=1),
        ],
        axis=0,
    )
    return np.concatenate(split_table(full), axis=0)


def layer_height(layer):
    return BAND + 2 * KR * (LAYERS - 1 - layer)


def block_height(layer):
    height = layer_height(layer)
    return height // 2 if 2 * (height + 2 * KR) > 2 * LANES else height


def spread_matrix():
    tile = lax.broadcasted_iota(jnp.int32, (NH, COLS), 0)
    column = lax.broadcasted_iota(jnp.int32, (NH, COLS), 1)
    return jnp.where(column // HS == tile, 1.0, 0.0).astype(jnp.bfloat16)


def pack_kernel(light, edges, counts, listed, row_taps, col_taps, out, *scratch):
    held, sems, taps = scratch[:6], scratch[6], scratch[7]
    sources = (listed, counts, edges, row_taps, col_taps, light)
    copies = [
        pltpu.make_async_copy(source, target, sems.at[place])
        for place, (source, target) in enumerate(zip(sources, held))
    ]
    for copy in reversed(copies):
        copy.start()
    listed, counts, edges, row_taps, col_taps, light = held
    spread = spread_matrix()
    slot = lax.broadcasted_iota(jnp.int32, (NH, NH), 0)
    place = lax.broadcasted_iota(jnp.int32, (NH, NH), 1)
    for copy in copies[:5]:
        copy.wait()
    rows = []
    for group in range(BAND // HS):
        listing = jnp.broadcast_to(listed[0, group : group + 1, :], (NH, NH))
        column = jnp.sum(jnp.where(slot == place, listing, 0), axis=1, keepdims=True)
        named = (column == place) & (slot < counts[0, group])
        live = jnp.max(jnp.where(named, 1.0, 0.0), axis=0, keepdims=True)
        rows.append(jnp.broadcast_to(live, (HS, NH)))
    live_rows = jnp.concatenate(rows, axis=0).astype(jnp.bfloat16)
    live_pix = jnp.dot(live_rows, spread, preferred_element_type=jnp.float32)
    edge_tile = jnp.concatenate(
        [edges[0].astype(jnp.float32), jnp.zeros((BAND, LANES - NH), jnp.float32)], axis=1
    ).astype(jnp.bfloat16)
    for colour in range(COLORS):
        out[colour, :, COLS:HALO_W] = edge_tile
        taps[...] = jnp.zeros_like(taps)
        taps[0:2, : 2 * KC + 1] = col_taps[0, colour].astype(jnp.float32)
        taps[2:4, : 2 * KR + 1] = row_taps[0, colour].astype(jnp.float32)
        out[colour, :, HALO_W:] = taps[...].astype(jnp.bfloat16)
    for spare in range(COLORS, LAYERS):
        out[spare] = jnp.zeros((BAND, FULL_W), jnp.bfloat16)
    copies[5].wait()
    for colour in range(COLORS):
        out[colour, :, :COLS] = (light[0, colour] * live_pix).astype(jnp.bfloat16)


def halo_kernel(own, incident, in_chip, cross, far_even, far_odd):
    band = lax.axis_index("rows")
    core = band % 2
    odd = (band // 2) % 2
    last = BAND - KR
    for near, start in ((in_chip, (1 - core) * last), (cross, core * last)):
        near[0:BAND] = own[0, :, :HALO_W]
        near[BAND : 2 * BAND] = own[1, :, :HALO_W]
        near[2 * BAND : NEAR] = own[2, pl.ds(pl.multiple_of(start, KR), KR), :HALO_W]
        near[NEAR : NEAR + BAND, :COLS] = incident[0]
        near[NEAR + BAND :, :COLS] = incident[1]
    for far, start in ((far_even, (1 - odd) * last), (far_odd, odd * last)):
        far[0:FAR] = own[0, pl.ds(pl.multiple_of(start, KR), KR), :HALO_W]
        far[FAR : FAR + BAND, :COLS] = incident[0]
        far[FAR + BAND :, :COLS] = incident[1]


def tiles_below(value, height):
    return jnp.concatenate(
        [
            jnp.concatenate(
                [
                    value[:height, tile * LANES : (tile + 1) * LANES],
                    value[height:, tile * LANES : (tile + 1) * LANES],
                ],
                axis=1,
            )
            for tile in range(TILES)
        ],
        axis=0,
    )


def stereo_tiles(light, left_tab, right_tab):
    height = light.shape[0]
    rows = jnp.concatenate([left_tab[:height], left_tab[LANES : LANES + height]], axis=0)
    left = jnp.dot(rows[:, :height], light, preferred_element_type=jnp.float32)
    low = rows[:, LANES : LANES + height]
    left = left + jnp.dot(low, light, preferred_element_type=jnp.float32)
    arranged = tiles_below(left.astype(jnp.bfloat16), height)
    out = jnp.dot(arranged, right_tab[: 2 * LANES], preferred_element_type=jnp.float32)
    return out + jnp.dot(arranged, right_tab[2 * LANES :], preferred_element_type=jnp.float32)


def banded(line, count, shift):
    base = jnp.concatenate([line, jnp.zeros((1, LANES), jnp.float32)], axis=1)
    base = jnp.broadcast_to(base, (count, 2 * LANES))
    return pltpu.roll(base, shift, 1, stride=1, stride_axis=0)


def prepare_kernel(own, left_tab, right_tab, col_mats, stereo, *row_mats):
    for layer in range(LAYERS):
        taps = own[layer, 0:16, HALO_W:].astype(jnp.float32)
        row_re, row_im = taps[2:3], taps[3:4]
        height = block_height(layer)
        before = height + 2 * KR
        upper = banded(row_re, height, 0) - banded(row_im, height, before)
        lower = banded(row_im, height, 0) + banded(row_re, height, before)
        row_mats[layer][...] = jnp.concatenate([upper, lower], axis=0).astype(jnp.bfloat16)
        col_re = banded(taps[0:1], LANES, 1)
        col_im = banded(taps[1:2], LANES, 1)
        upper = jnp.concatenate([col_re, -col_im], axis=1)
        lower = jnp.concatenate([col_im, col_re], axis=1)
        col_mats[layer] = jnp.concatenate([upper, lower], axis=0).astype(jnp.bfloat16)
    light = jnp.concatenate([own[layer, :, :COLS] for layer in range(LAYERS)], axis=0)
    tiles = stereo_tiles(light, left_tab, right_tab)
    for tile in range(TILES):
        for part in range(2):
            block = tiles[
                tile * LANES : (tile + 1) * LANES, part * LANES : (part + 1) * LANES
            ]
            stereo[part, :, tile * LANES : (tile + 1) * LANES] = block


def chain_kernel(
    own, incident, in_chip, cross, far_even, far_odd, left_tab, right_tab, col_mats, stereo, *rest
):
    row_mats, (out, field, low_near, high_near, low_far, high_far) = rest[:LAYERS], rest[LAYERS:]
    band = lax.axis_index("rows")
    even_core = band % 2 == 0
    even_chip = (band // 2) % 2 == 0
    low_near[...] = jnp.where(even_core, cross[...], in_chip[...])
    high_near[...] = jnp.where(even_core, in_chip[...], cross[...])
    low_far[...] = jnp.where(even_chip, far_odd[...], far_even[...])
    high_far[...] = jnp.where(even_chip, far_even[...], far_odd[...])

    pieces = [
        low_far[0:FAR],
        low_near[0:BAND],
        high_near[0:BAND],
        high_far[0:FAR],
        low_near[BAND : 2 * BAND],
        high_near[BAND : 2 * BAND],
        low_near[2 * BAND : NEAR],
        high_near[2 * BAND : NEAR],
    ]
    halo = jnp.concatenate(pieces, axis=0)
    count = halo.shape[0] // 2
    halves = [
        stereo_tiles(halo[half * count : (half + 1) * count, :COLS], left_tab, right_tab)
        for half in range(2)
    ]
    edges = jnp.concatenate(
        [halo[:, COLS : COLS + NH]]
        + [own[layer, :, COLS : COLS + NH] for layer in range(LAYERS)],
        axis=0,
    )
    edge_pix = jnp.dot(edges, spread_matrix(), preferred_element_type=jnp.float32)
    within = (lax.broadcasted_iota(jnp.int32, (1, COLS), 1) % HS).astype(jnp.float32)
    clear_all = jnp.where(within < edge_pix, 1.0, 0.0)

    extended = []
    for part in range(2):
        near = slice(NEAR + part * BAND, NEAR + (part + 1) * BAND)
        far = slice(FAR + part * BAND, FAR + (part + 1) * BAND)
        pieces = [
            low_far[far, :COLS],
            low_near[near, :COLS],
            incident[part],
            high_near[near, :COLS],
            high_far[far, :COLS],
        ]
        extended.append(jnp.concatenate(pieces, axis=0))
    below = (0, 2 * (BAND + FAR), 2 * (BAND + FAR) + 2 * BAND, 0)
    sides = (BAND + FAR, BAND, KR, 0)
    for layer in range(LAYERS):
        height = layer_height(layer)
        before = height + 2 * KR
        side = sides[layer]
        if layer == 0:
            u_re, u_im = extended
        else:
            u_re, u_im = field[0, :before], field[1, :before]
        block = block_height(layer)
        reach = block + 2 * KR
        parts = []
        for start in range(0, height, block):
            stacked = jnp.concatenate(
                [u_re[start : start + reach], u_im[start : start + reach]], axis=0
            )
            parts.append(
                jnp.dot(
                    row_mats[layer][:, : 2 * reach], stacked, preferred_element_type=jnp.float32
                )
            )
        rowed = jnp.concatenate(
            [part[:block] for part in parts] + [part[block:] for part in parts], axis=0
        )
        rowed = jnp.concatenate([rowed, jnp.zeros((2 * height, LANES), jnp.float32)], axis=1)
        rowed = pltpu.roll(rowed, HALF, 1).astype(jnp.bfloat16)
        windows = jnp.concatenate(
            [
                jnp.concatenate(
                    [
                        rowed[:height, tile * LANES : (tile + 2) * LANES],
                        rowed[height:, tile * LANES : (tile + 2) * LANES],
                    ],
                    axis=1,
                )
                for tile in range(TILES)
            ],
            axis=0,
        )
        columned = lax.dot_general(
            windows,
            col_mats[layer],
            (((1,), (1,)), ((), ())),
            preferred_element_type=jnp.float32,
        )

        def halo_rows(first, length, tile, part):
            half, inner = divmod(first, count)
            found = []
            while length > 0:
                take = min(length, count - inner)
                row = tile * count + inner
                found.append(
                    halves[half][row : row + take, part * LANES : (part + 1) * LANES]
                )
                half, inner, length = half + 1, 0, length - take
            return found

        own_clear = clear_all[2 * count + layer * BAND : 2 * count + (layer + 1) * BAND]
        low = below[layer]
        clear = jnp.concatenate(
            ([clear_all[low : low + side]] if side else [])
            + [own_clear]
            + ([clear_all[low + side : low + 2 * side]] if side else []),
            axis=0,
        )
        for tile in range(TILES):
            span = slice(tile * height, (tile + 1) * height)
            lanes = slice(tile * LANES, (tile + 1) * LANES)
            for part in range(2):
                pieces = [stereo[part, layer * BAND : (layer + 1) * BAND, lanes]]
                if side:
                    pieces = (
                        halo_rows(low, side, tile, part)
                        + pieces
                        + halo_rows(low + side, side, tile, part)
                    )
                added = jnp.concatenate(pieces, axis=0)
                value = columned[span, part * LANES : (part + 1) * LANES]
                value = clear[:, lanes] * value + added
                field[part, :height, lanes] = value.astype(jnp.bfloat16)
        for part in range(2):
            out[layer, part] = field[part, side : side + BAND]


def exchanged(value, axis, by, phase):
    count = lax.axis_size(axis)
    lower = [i for i in range(count - by) if (i // by) % 2 == phase]
    pairs = [(i, i + by) for i in lower] + [(i + by, i) for i in lower]
    return lax.ppermute(value, axis, pairs)


def call(kernel, out_shape, in_specs, scratch=(), flops=0, moved=10**6):
    vmem = pl.BlockSpec(memory_space=pltpu.VMEM)
    many = isinstance(out_shape, (tuple, list))
    return pl.pallas_call(
        kernel,
        out_shape=out_shape,
        in_specs=in_specs,
        out_specs=(vmem,) * len(out_shape) if many else vmem,
        scratch_shapes=scratch,
        compiler_params=pltpu.CompilerParams(vmem_limit_bytes=VMEM_LIMIT),
        cost_estimate=pl.CostEstimate(flops=flops, bytes_accessed=moved, transcendentals=0),
    )


def body(incident, row_taps, col_taps, hogel_light, silhouette, fill_counts, hogel_index):
    vmem = pl.BlockSpec(memory_space=pltpu.VMEM)
    hbm = pl.BlockSpec(memory_space=pltpu.HBM)
    bf16, f32 = jnp.bfloat16, jnp.float32
    shaped = jax.ShapeDtypeStruct
    held = [
        pltpu.VMEM(hogel_index.shape, jnp.int32),
        pltpu.SMEM(fill_counts.shape, jnp.int32),
        pltpu.VMEM(silhouette.shape, jnp.int32),
        pltpu.VMEM(row_taps.shape, bf16),
        pltpu.VMEM(col_taps.shape, bf16),
        pltpu.VMEM(hogel_light.shape, f32),
    ]
    payload = call(
        pack_kernel,
        shaped((LAYERS, BAND, FULL_W), bf16),
        [hbm] * 6,
        held + [pltpu.SemaphoreType.DMA((6,)), pltpu.VMEM((BAND, LANES), f32)],
        flops=10**7,
    )(hogel_light, silhouette, fill_counts, hogel_index, row_taps, col_taps)
    own = lax.all_to_all(payload, "depth", 0, 0, tiled=True)
    colour = jnp.minimum(lax.axis_index("depth"), COLORS - 1)
    mine = lax.dynamic_index_in_dim(incident, colour, 0, keepdims=False)
    near = shaped((NEAR + 2 * BAND, HALO_W), bf16)
    far = shaped((FAR + 2 * BAND, HALO_W), bf16)
    in_chip, cross, far_even, far_odd = call(halo_kernel, (near, near, far, far), [vmem] * 2)(
        own, mine
    )
    cross = exchanged(cross, "rows", 1, 1)
    far_even = exchanged(far_even, "rows", 2, 0)
    far_odd = exchanged(far_odd, "rows", 2, 1)
    in_chip = exchanged(in_chip, "rows", 1, 0)
    tables = [jnp.asarray(left_table()), jnp.asarray(right_table())]
    made = call(
        prepare_kernel,
        [shaped((LAYERS, 2 * LANES, 4 * LANES), bf16), shaped((2, LANES, COLS), f32)]
        + [shaped((2 * block_height(layer), 2 * LANES), bf16) for layer in range(LAYERS)],
        [vmem] * 3,
        flops=3 * 10**8,
        moved=3 * 10**6,
    )(own, *tables)
    result = call(
        chain_kernel,
        shaped((LAYERS, 2, BAND, COLS), bf16),
        [vmem] * (8 + len(made)),
        [pltpu.VMEM((2, layer_height(0), COLS), bf16)]
        + [pltpu.VMEM(near.shape, bf16)] * 2
        + [pltpu.VMEM(far.shape, bf16)] * 2,
        flops=3 * 10**9,
        moved=3 * 10**6,
    )(own, mine, in_chip, cross, far_even, far_odd, *tables, *made)
    gathered = lax.all_to_all(result, "depth", 0, 0, tiled=True)
    return gathered[None, :COLORS]


def solution(mesh):
    placed = (
        P(None, None, "rows", None),
        P("depth", None, None, None),
        P("depth", None, None, None),
        P("depth", None, "rows", None),
        P("depth", "rows", None),
        P("depth", "rows"),
        P("depth", "rows", None),
    )
    return jax.shard_map(
        body,
        mesh=mesh,
        in_specs=placed,
        out_specs=P("depth", None, None, "rows", None),
        check_vma=False,
    )
```

time: 49.7 us -> 45.4 us (0.913)
  starting transfers between devices: 15.5 us -> 10 us
  waiting for transfers between devices: 12.6 us -> 13.4 us
  Pallas kernels: 5.58 us -> 6.37 us
    ppermute x4, starting transfers between devices: 10.3 us -> 4.82 us  [exchanged(): return lax.ppermute(value, axis, pairs)]
    pallas_call x3 -> x4, Pallas kernels: 5.58 us -> 6.37 us  [the longest x1 3.76 us: body(): call(chain_kernel, shaped((LAYERS, 2, BAND, COLS), bf16), [vmem] * (8 + l...]
    ppermute x4, waiting for transfers between devices: 6.82 us -> 7.53 us  [exchanged(): return lax.ppermute(value, axis, pairs)]
    unnamed x24 -> x18, local copies, waits for them, and re-layouts: 4.49 us -> 4.47 us
  transfers between devices with their start and end apart: 5 -> 5, of which waited for: 3 -> 2; matrix products, arithmetic and copies ran while one was open for 0% -> 0% of each run, Pallas kernels for 0% -> 2%
where the time goes in v2:
time: 45.4 us; the launch traced here: 45 us
  waiting for transfers between devices  13.4 us (30%)
  starting transfers between devices  10 us (22%)
  blocking collectives  9.91 us (22%)
  Pallas kernels  6.37 us (14%)
  local copies, waits for them, and re-layouts  5.26 us (12%)
    all_to_all x1, blocking collectives, body(): gathered = lax.all_to_all(result, 'depth', 0, 0, tiled=True)  9.91 us
    ppermute x4, waiting for transfers between devices, exchanged(): return lax.ppermute(value, axis, pairs)  7.53 us
    all_to_all x1, waiting for transfers between devices, body(): own = lax.all_to_all(payload, 'depth', 0, 0, tiled=True)  5.85 us
    all_to_all x1, starting transfers between devices, body(): own = lax.all_to_all(payload, 'depth', 0, 0, tiled=True)  5.18 us
    ppermute x4, starting transfers between devices, exchanged(): return lax.ppermute(value, axis, pairs)  4.82 us
    unnamed x18, local copies, waits for them, and re-layouts  4.47 us
    pallas_call x1, Pallas kernels, body(): call(chain_kernel, shaped((LAYERS, 2, BAND, COLS), bf16), [vmem] * (8 + l...  3.76 us
    pallas_call x1, Pallas kernels, body(): call(pack_kernel, shaped((LAYERS, BAND, FULL_W), bf16), [hbm] * 6, held +...  1.81 us
  transfers between devices with their start and end apart: 5, of which 2 were waited for; matrix products, arithmetic and copies ran while one was open for 0% of the time, Pallas kernels for 2%

profile of v2, /device:TPU:0, one launch (start us, length us, event | category | flops | bytes accessed | tf_op | source)
XLA Modules:
  0.0 45.0 jit_solution(2488615369910307020)
XLA Ops:
  0.0 0.0 copy-start
  0.0 0.0 copy-start.1
  0.0 1.0 %copy-done.1 = f32[1,3,32,1024]{3,2,1,0:T(8,128)S(1)} copy-done((f32[1,3,32,1024]{3,2,1,0:T(8,128)S(1)}, f32[1,3,32,1024]{3,2,1,0:T(8,128)}, u32[]{:S(2)}) %copy-start.1) | copy-done | bytes 393240
  1.1 0.0 copy-start.2
  1.1 0.7 %copy-done.2 = s32[1,32,64]{2,1,0:T(8,128)S(1)} copy-done((s32[1,32,64]{2,1,0:T(8,128)S(1)}, s32[1,32,64]{2,1,0:T(8,128)}, u32[]{:S(2)}) %copy-start.2) | copy-done | bytes 8216
  1.8 0.0 copy-start.3
  1.8 0.7 %copy-done.3 = bf16[1,3,2,33]{3,2,1,0:T(2,128)(2,1)S(1)} copy-done((bf16[1,3,2,33]{3,2,1,0:T(2,128)(2,1)S(1)}, bf16[1,3,2,33]{3,2,1,0:T(2,128)(2,1)}, u32[]{:S(2)}) %copy-start.3) | copy-done | bytes 420
  2.4 0.0 copy-start.4
  2.5 0.7 %copy-done.4 = bf16[1,3,2,127]{3,2,1,0:T(2,128)(2,1)S(1)} copy-done((bf16[1,3,2,127]{3,2,1,0:T(2,128)(2,1)S(1)}, bf16[1,3,2,127]{3,2,1,0:T(2,128)(2,1)}, u32[]{:S(2)}) %copy-start.4) | copy-done | bytes 1548
  3.1 0.0 copy-start.5
  3.1 0.7 %copy-done.5 = s32[1,2,64]{2,1,0:T(2,128)S(1)} copy-done((s32[1,2,64]{2,1,0:T(2,128)S(1)}, s32[1,2,64]{2,1,0:T(2,128)}, u32[]{:S(2)}) %copy-start.5) | copy-done | bytes 536
  3.8 0.0 copy-start.6
  3.8 0.7 %copy-done.6 = s32[1,2]{1,0:T(1,128)S(1)} copy-done((s32[1,2]{1,0:T(1,128)S(1)}, s32[1,2]{1,0:T(1,128)}, u32[]{:S(2)}) %copy-start.6) | copy-done | bytes 32
  4.5 1.8 %shard_map.91 = bf16[4,32,1280]{2,1,0:T(8,128)(2,1)} custom-call(f32[1,3,32,1024]{3,2,1,0:T(8,128)S(1)} %copy-done.1, s32[1,32,64]{2,1,0:T(8,128)S(1)} %copy-done.2, s32[1,2]{1,0:T(1,128)S(1)} %copy-done.6, s32[1,2,64]{2,1,0:T(2,128)S(1)} %copy-done.5, bf16[1,3,2,33]{3,2,1,0:T(2,128)(2,1)S(1)} %copy-done.3, bf16[1,3,2,127]{3,2,1,0:T(2,128)(2,1)S(1)} %copy-done.4), custom_call_target="tpu_custom_call" | custom-call | flops 10000000 | bytes 1000000 | tf_op jit(solution)/shard_map/pallas_call | solution.py:360
  6.3 5.2 %all-to-all-start = ((bf16[4,32,1280]{2,1,0:T(8,128)(2,1)}), bf16[4,32,1280]{2,1,0:T(8,128)(2,1)S(1)}, u32[]{:S(2)}, u32[]{:S(2)}) async-start(bf16[4,32,1280]{2,1,0:T(8,128)(2,1)} %shard_map.91), calls=%async_computation | async-start | bytes 655360 | tf_op jit(solution)/shard_map/all_to_all | solution.py:367
  11.5 0.0 copy-done
  11.5 0.0 copy-start.7
  11.5 0.0 copy-start.8
  11.5 5.8 %all-to-all-done.own = bf16[4,32,1280]{2,1,0:T(8,128)(2,1)S(1)} async-done(((bf16[4,32,1280]{2,1,0:T(8,128)(2,1)}), bf16[4,32,1280]{2,1,0:T(8,128)(2,1)S(1)}, u32[]{:S(2)}, u32[]{:S(2)}) %all-to-all-start) | async-done | bytes 327712 | tf_op jit(solution)/shard_map/all_to_all | solution.py:367
  17.3 0.1 shard_map.92
  17.4 0.1 collective-permute-start
  17.5 0.7 %collective-permute-start.1 = (bf16[144,1152]{1,0:T(8,128)(2,1)S(1)}, bf16[144,1152]{1,0:T(8,128)(2,1)S(1)}, u32[]{:S(2)}, u32[]{:S(2)}) collective-permute-start(bf16[144,1152]{1,0:T(8,128)(2,1)S(1)} %get-tuple-element.16), channel_id=1, source_target_pairs={{1,2},{3,4},{5,6},{2,1},{4,3},{6,5},{9,10},{11,12},{13,14},{10,9},... | collective-permute-start | bytes 995336 | tf_op jit(solution)/shard_map/ppermute | solution.py:330
  18.2 3.4 %collective-permute-start.2 = (bf16[80,1152]{1,0:T(8,128)(2,1)S(1)}, bf16[80,1152]{1,0:T(8,128)(2,1)S(1)}, u32[]{:S(2)}, u32[]{:S(2)}) collective-permute-start(bf16[80,1152]{1,0:T(8,128)(2,1)S(1)} %get-tuple-element.17), channel_id=1, source_target_pairs={{0,2},{1,3},{4,6},{5,7},{2,0},{3,1},{6,4},{7,5},{8,10},{9,11},{12,... | collective-permute-start | bytes 552968 | tf_op jit(solution)/shard_map/ppermute | solution.py:330
  21.6 0.7 %collective-permute-start.3 = (bf16[80,1152]{1,0:T(8,128)(2,1)S(1)}, bf16[80,1152]{1,0:T(8,128)(2,1)S(1)}, u32[]{:S(2)}, u32[]{:S(2)}) collective-permute-start(bf16[80,1152]{1,0:T(8,128)(2,1)S(1)} %get-tuple-element.18), channel_id=1, source_target_pairs={{2,4},{3,5},{4,2},{5,3},{10,12},{11,13},{12,10},{13,11},{18,20},{1... | collective-permute-start | bytes 552968 | tf_op jit(solution)/shard_map/ppermute | solution.py:330
  22.3 0.0 copy-done.7
  22.3 0.0 copy-done.8
  22.3 0.7 %shard_map.93 = (bf16[4,256,512]{2,1,0:T(8,128)(2,1)S(1)}, f32[2,128,1024]{2,1,0:T(8,128)S(1)}, bf16[128,256]{1,0:T(8,128)(2,1)S(1)}, bf16[192,256]{1,0:T(8,128)...) custom-call(bf16[4,32,1280]{2,1,0:T(8,128)(2,1)S(1)} %all-to-all-done.own, ...), custom_call_target="tpu_custom_call" | custom-call | flops 300000000 | bytes 3000000 | tf_op jit(solution)/shard_map/pallas_call | solution.py:380
  23.0 7.5 %collective-permute-done.2.far_even = bf16[80,1152]{1,0:T(8,128)(2,1)S(1)} collective-permute-done((bf16[80,1152]{1,0:T(8,128)(2,1)S(1)}, bf16[80,1152]{1,0:T(8,128)(2,1)S(1)}, u32[]{:S(2)}, u32[]{:S(2)}) %collective-permute-start.2) | collective-permute-done | bytes 184352 | tf_op jit(solution)/shard_map/ppermute | solution.py:330
  30.5 0.0 collective-permute-done.3.far_odd
  30.5 0.0 collective-permute-done.in_chip
  30.6 0.0 collective-permute-done.1.cross
  30.6 3.8 %shard_map.94 = bf16[4,2,32,1024]{3,2,1,0:T(8,128)(2,1)S(1)} custom-call(bf16[4,32,1280]{2,1,0:T(8,128)(2,1)S(1)} %all-to-all-done.own, bf16[2,32,1024]{2,1,0:T(8,128)(2,1)S(1)} %dynamic-slice_bitcast_fusion.incident, bf16[144,1152]{1,0:T(8,128)(2,1)S(1)} %collective-permute-done.in_chip, bf16[144,1152]{1,0:T(8,128)(2,1)S(1)} %collective-permute-done.1.cross, ...), custom_call_target="tpu_custom_call" | custom-call | flops 3000000000 | bytes 3000000 | tf_op jit(solution)/shard_map/pallas_call | solution.py:388
  34.3 9.9 %all_to_all.10 = bf16[4,2,32,1024]{3,2,1,0:T(8,128)(2,1)S(1)} all-to-all(bf16[4,2,32,1024]{3,2,1,0:T(8,128)(2,1)S(1)} %shard_map.94), channel_id=1, replica_groups=mesh['depth'=4,'rows'=8] {'depth'}, dimensions={0} | all-to-all | bytes 1048576 | tf_op jit(solution)/shard_map/all_to_all | solution.py:398
  44.2 0.8 %slice_bitcast_fusion = bf16[1,3,2,32,1024]{4,3,2,1,0:T(8,128)(2,1)} fusion(bf16[4,2,32,1024]{3,2,1,0:T(8,128)(2,1)S(1)} %all_to_all.10), kind=kLoop, calls=%fused_computation | loop fusion | bytes 786432 | tf_op jit(solution)/shard_map/broadcast_in_dim | solution.py:399
  (1 shorter events, 0.0 us)
Async XLA Ops:
  0.0 11.5 %copy-start = (bf16[3,2,32,1024]{3,2,1,0:T(8,128)(2,1)S(1)}, bf16[3,2,32,1024]{3,2,1,0:T(8,128)(2,1)}, u32[]{:S(2)}) copy-start(bf16[3,2,32,1024]{3,2,1,0:T(8,128)(2,1)} %param.9) | copy-start | bytes 1179652
  0.0 1.0 %copy-start.1 = (f32[1,3,32,1024]{3,2,1,0:T(8,128)S(1)}, f32[1,3,32,1024]{3,2,1,0:T(8,128)}, u32[]{:S(2)}) copy-start(f32[1,3,32,1024]{3,2,1,0:T(8,128)} %light.1) | copy-start | bytes 1179652
  1.1 0.7 %copy-start.2 = (s32[1,32,64]{2,1,0:T(8,128)S(1)}, s32[1,32,64]{2,1,0:T(8,128)}, u32[]{:S(2)}) copy-start(s32[1,32,64]{2,1,0:T(8,128)} %edges.1) | copy-start | bytes 24580
  1.8 0.7 %copy-start.3 = (bf16[1,3,2,33]{3,2,1,0:T(2,128)(2,1)S(1)}, bf16[1,3,2,33]{3,2,1,0:T(2,128)(2,1)}, u32[]{:S(2)}) copy-start(bf16[1,3,2,33]{3,2,1,0:T(2,128)(2,1)} %row_taps.1) | copy-start | bytes 1192
  2.4 0.7 %copy-start.4 = (bf16[1,3,2,127]{3,2,1,0:T(2,128)(2,1)S(1)}, bf16[1,3,2,127]{3,2,1,0:T(2,128)(2,1)}, u32[]{:S(2)}) copy-start(bf16[1,3,2,127]{3,2,1,0:T(2,128)(2,1)} %col_taps.1) | copy-start | bytes 4576
  3.1 0.7 %copy-start.5 = (s32[1,2,64]{2,1,0:T(2,128)S(1)}, s32[1,2,64]{2,1,0:T(2,128)}, u32[]{:S(2)}) copy-start(s32[1,2,64]{2,1,0:T(2,128)} %listed.1) | copy-start | bytes 1540
  3.8 0.7 %copy-start.6 = (s32[1,2]{1,0:T(1,128)S(1)}, s32[1,2]{1,0:T(1,128)}, u32[]{:S(2)}) copy-start(s32[1,2]{1,0:T(1,128)} %counts.1) | copy-start | bytes 28
  6.3 11.1 %all-to-all-start = ((bf16[4,32,1280]{2,1,0:T(8,128)(2,1)}), bf16[4,32,1280]{2,1,0:T(8,128)(2,1)S(1)}, u32[]{:S(2)}, u32[]{:S(2)}) async-start(bf16[4,32,1280]{2,1,0:T(8,128)(2,1)} %shard_map.91), calls=%async_computation | async-start | bytes 655360 | tf_op jit(solution)/shard_map/all_to_all | solution.py:367
  11.5 10.8 %copy-start.7 = (bf16[512,256]{1,0:T(8,128)(2,1)S(1)}, bf16[512,256]{1,0:T(8,128)(2,1)}, u32[]{:S(2)}) copy-start(bf16[512,256]{1,0:T(8,128)(2,1)} %constant.18.clone.right_tab) | copy-start | bytes 786436
  11.5 10.8 %copy-start.8 = (bf16[256,256]{1,0:T(8,128)(2,1)S(1)}, bf16[256,256]{1,0:T(8,128)(2,1)}, u32[]{:S(2)}) copy-start(bf16[256,256]{1,0:T(8,128)(2,1)} %constant.17.clone.left_tab) | copy-start | bytes 393220
  17.4 13.1 %collective-permute-start = (bf16[144,1152]{1,0:T(8,128)(2,1)S(1)}, bf16[144,1152]{1,0:T(8,128)(2,1)S(1)}, u32[]{:S(2)}, u32[]{:S(2)}) collective-permute-start(bf16[144,1152]{1,0:T(8,128)(2,1)S(1)} %get-tuple-element.15), channel_id=1, source_target_pairs={{0,1},{2,3},{4,5},{6,7},{1,0},{3,2},{5,4},{7,6},{8,9},{10,11},{12,... | collective-permute-start | bytes 995336 | tf_op jit(solution)/shard_map/ppermute | solution.py:330
  17.5 13.1 %collective-permute-start.1 = (bf16[144,1152]{1,0:T(8,128)(2,1)S(1)}, bf16[144,1152]{1,0:T(8,128)(2,1)S(1)}, u32[]{:S(2)}, u32[]{:S(2)}) collective-permute-start(bf16[144,1152]{1,0:T(8,128)(2,1)S(1)} %get-tuple-element.16), channel_id=1, source_target_pairs={{1,2},{3,4},{5,6},{2,1},{4,3},{6,5},{9,10},{11,12},{13,14},{10,9},... | collective-permute-start | bytes 995336 | tf_op jit(solution)/shard_map/ppermute | solution.py:330
  18.2 12.4 %collective-permute-start.2 = (bf16[80,1152]{1,0:T(8,128)(2,1)S(1)}, bf16[80,1152]{1,0:T(8,128)(2,1)S(1)}, u32[]{:S(2)}, u32[]{:S(2)}) collective-permute-start(bf16[80,1152]{1,0:T(8,128)(2,1)S(1)} %get-tuple-element.17), channel_id=1, source_target_pairs={{0,2},{1,3},{4,6},{5,7},{2,0},{3,1},{6,4},{7,5},{8,10},{9,11},{12,... | collective-permute-start | bytes 552968 | tf_op jit(solution)/shard_map/ppermute | solution.py:330
  21.6 9.0 %collective-permute-start.3 = (bf16[80,1152]{1,0:T(8,128)(2,1)S(1)}, bf16[80,1152]{1,0:T(8,128)(2,1)S(1)}, u32[]{:S(2)}, u32[]{:S(2)}) collective-permute-start(bf16[80,1152]{1,0:T(8,128)(2,1)S(1)} %get-tuple-element.18), channel_id=1, source_target_pairs={{2,4},{3,5},{4,2},{5,3},{10,12},{11,13},{12,10},{13,11},{18,20},{1... | collective-permute-start | bytes 552968 | tf_op jit(solution)/shard_map/ppermute | solution.py:330

commit v3 on v2

v3 whole, which is shorter than its diff:
```python
import math

import jax
import jax.numpy as jnp
import numpy as np
from jax import lax
from jax.experimental import pallas as pl
from jax.experimental.pallas import tpu as pltpu
from jax.sharding import PartitionSpec as P

HS = 16
KR = 16
KC = 63
COLORS = 3
LAYERS = 4
BAND = 32
COLS = 1024
NH = COLS // HS
LANES = 128
TILES = COLS // LANES
HALO_W = COLS + LANES
HALF = LANES // 2
FULL_W = COLS + 2 * LANES
NEAR = 2 * BAND + KR
FAR = KR
VMEM_LIMIT = 48 * 1024 * 1024
PACK_LIMIT = 63 * 1024 * 1024


def split_table(table):
    high = table.astype(jnp.bfloat16)
    low = (table - high.astype(np.float64)).astype(jnp.bfloat16)
    return high, low


def dft_pair():
    counter = np.arange(HS)
    angles = (counter[:, None] * counter[None, :] % HS) * (2.0 * math.pi / HS)
    return np.cos(angles) / math.sqrt(HS), np.sin(angles) / math.sqrt(HS)


def left_table(height):
    cos_tab, sin_tab = dft_pair()
    eye = np.eye(height // HS)
    full = np.concatenate([np.kron(eye, cos_tab), np.kron(eye, -sin_tab)], axis=0)
    return np.concatenate(split_table(full), axis=1)


def right_table():
    cos_tab, sin_tab = dft_pair()
    eye = np.eye(LANES // HS)
    cos_big, sin_big = np.kron(eye, cos_tab), np.kron(eye, sin_tab)
    full = np.concatenate(
        [
            np.concatenate([cos_big, -sin_big], axis=1),
            np.concatenate([sin_big, cos_big], axis=1),
        ],
        axis=0,
    )
    return full.astype(jnp.bfloat16)


def layer_height(layer):
    return BAND + 2 * KR * (LAYERS - 1 - layer)


def block_height(layer):
    height = layer_height(layer)
    return height // 2 if 2 * (height + 2 * KR) > 2 * LANES else height


def spread_matrix():
    tile = lax.broadcasted_iota(jnp.int32, (NH, COLS), 0)
    column = lax.broadcasted_iota(jnp.int32, (NH, COLS), 1)
    return jnp.where(column // HS == tile, 1.0, 0.0).astype(jnp.bfloat16)


def pack_kernel(light, edges, counts, listed, row_taps, col_taps, out, *scratch):
    held, sems, taps = scratch[:6], scratch[6], scratch[7]
    sources = (listed, counts, edges, row_taps, col_taps, light)
    copies = [
        pltpu.make_async_copy(source, target, sems.at[place])
        for place, (source, target) in enumerate(zip(sources, held))
    ]
    for copy in reversed(copies):
        copy.start()
    listed, counts, edges, row_taps, col_taps, light = held
    spread = spread_matrix()
    slot = lax.broadcasted_iota(jnp.int32, (NH, NH), 0)
    place = lax.broadcasted_iota(jnp.int32, (NH, NH), 1)
    for copy in copies[:5]:
        copy.wait()
    rows = []
    for group in range(BAND // HS):
        listing = jnp.broadcast_to(listed[0, group : group + 1, :], (NH, NH))
        column = jnp.sum(jnp.where(slot == place, listing, 0), axis=1, keepdims=True)
        named = (column == place) & (slot < counts[0, group])
        live = jnp.max(jnp.where(named, 1.0, 0.0), axis=0, keepdims=True)
        rows.append(jnp.broadcast_to(live, (HS, NH)))
    live_rows = jnp.concatenate(rows, axis=0).astype(jnp.bfloat16)
    live_pix = jnp.dot(live_rows, spread, preferred_element_type=jnp.float32)
    edge_tile = jnp.concatenate(
        [edges[0].astype(jnp.float32), jnp.zeros((BAND, LANES - NH), jnp.float32)], axis=1
    ).astype(jnp.bfloat16)
    for colour in range(COLORS):
        out[colour, :, COLS:HALO_W] = edge_tile
        taps[...] = jnp.zeros_like(taps)
        taps[0:2, : 2 * KC + 1] = col_taps[0, colour].astype(jnp.float32)
        taps[2:4, : 2 * KR + 1] = row_taps[0, colour].astype(jnp.float32)
        out[colour, :, HALO_W:] = taps[...].astype(jnp.bfloat16)
    for spare in range(COLORS, LAYERS):
        out[spare] = jnp.zeros((BAND, FULL_W), jnp.bfloat16)
    copies[5].wait()
    for colour in range(COLORS):
        out[colour, :, :COLS] = (light[0, colour] * live_pix).astype(jnp.bfloat16)


def halo_kernel(own, in_chip, cross, far_even, far_odd):
    band = lax.axis_index("rows")
    core = band % 2
    odd = (band // 2) % 2
    last = BAND - KR
    for near, start in ((in_chip, (1 - core) * last), (cross, core * last)):
        near[0:BAND] = own[0, :, :HALO_W]
        near[BAND : 2 * BAND] = own[1, :, :HALO_W]
        near[2 * BAND : NEAR] = own[2, pl.ds(pl.multiple_of(start, KR), KR), :HALO_W]
    for far, start in ((far_even, (1 - odd) * last), (far_odd, odd * last)):
        far[...] = own[0, pl.ds(pl.multiple_of(start, KR), KR), :HALO_W]


def ordered(in_chip, cross, far_even, far_odd):
    band = lax.axis_index("rows")
    even_core = band % 2 == 0
    even_chip = (band // 2) % 2 == 0
    in_chip, cross = in_chip[...], cross[...]
    far_even, far_odd = far_even[...], far_odd[...]
    return (
        jnp.where(even_core, cross, in_chip),
        jnp.where(even_core, in_chip, cross),
        jnp.where(even_chip, far_odd, far_even),
        jnp.where(even_chip, far_even, far_odd),
    )


def tiles_below(value, height):
    return jnp.concatenate(
        [
            jnp.concatenate(
                [
                    value[:height, tile * LANES : (tile + 1) * LANES],
                    value[height:, tile * LANES : (tile + 1) * LANES],
                ],
                axis=1,
            )
            for tile in range(TILES)
        ],
        axis=0,
    )


def stereo_tiles(blocks, left_tab, right_tab):
    arranged = []
    for light in blocks:
        doubled = jnp.concatenate([light, light], axis=0)
        left = jnp.dot(left_tab[...], doubled, preferred_element_type=jnp.float32)
        arranged.append(tiles_below(left.astype(jnp.bfloat16), light.shape[0]))
    arranged = jnp.concatenate(arranged, axis=0) if len(arranged) > 1 else arranged[0]
    return jnp.dot(arranged, right_tab[...], preferred_element_type=jnp.float32)


def clear_pixels(edges):
    edge_pix = jnp.dot(edges, spread_matrix(), preferred_element_type=jnp.float32)
    within = (lax.broadcasted_iota(jnp.int32, (1, COLS), 1) % HS).astype(jnp.float32)
    return jnp.where(within < edge_pix, 1.0, 0.0)


def banded(line, count, shift):
    base = jnp.concatenate([line, jnp.zeros((1, LANES), jnp.float32)], axis=1)
    base = jnp.broadcast_to(base, (count, 2 * LANES))
    return pltpu.roll(base, shift, 1, stride=1, stride_axis=0)


def filters(taps, layer):
    row_re, row_im = taps[2:3], taps[3:4]
    height = block_height(layer)
    before = height + 2 * KR
    upper = banded(row_re, height, 0) - banded(row_im, height, before)
    lower = banded(row_im, height, 0) + banded(row_re, height, before)
    row_mat = jnp.concatenate([upper, lower], axis=0).astype(jnp.bfloat16)
    col_re = banded(taps[0:1], LANES, 1)
    col_im = banded(taps[1:2], LANES, 1)
    upper = jnp.concatenate([col_re, -col_im], axis=1)
    lower = jnp.concatenate([col_im, col_re], axis=1)
    col_mat = jnp.concatenate([upper, lower], axis=0).astype(jnp.bfloat16)
    return row_mat, col_mat


def propagated(u_re, u_im, row_mat, col_mat, layer):
    height = layer_height(layer)
    block = block_height(layer)
    reach = block + 2 * KR
    parts = []
    for start in range(0, height, block):
        stacked = jnp.concatenate(
            [u_re[start : start + reach], u_im[start : start + reach]], axis=0
        )
        parts.append(
            jnp.dot(row_mat[:, : 2 * reach], stacked, preferred_element_type=jnp.float32)
        )
    rowed = jnp.concatenate(
        [part[:block] for part in parts] + [part[block:] for part in parts], axis=0
    )
    rowed = jnp.concatenate([rowed, jnp.zeros((2 * height, LANES), jnp.float32)], axis=1)
    rowed = pltpu.roll(rowed, HALF, 1).astype(jnp.bfloat16)
    windows = jnp.concatenate(
        [
            jnp.concatenate(
                [
                    rowed[:height, tile * LANES : (tile + 2) * LANES],
                    rowed[height:, tile * LANES : (tile + 2) * LANES],
                ],
                axis=1,
            )
            for tile in range(TILES)
        ],
        axis=0,
    )
    return lax.dot_general(
        windows, col_mat, (((1,), (1,)), ((), ())), preferred_element_type=jnp.float32
    )


def prepare_kernel(
    own, incident, in_chip, cross, far_even, far_odd, left_tab, right_tab,
    first, stereo, clear, col_mats, *row_mats
):
    low_near, high_near, low_far, high_far = ordered(in_chip, cross, far_even, far_odd)
    extended = []
    for part in range(2):
        pieces = [low_far, low_near, incident[...], high_near, high_far]
        pieces = [piece[part * BAND : (part + 1) * BAND] for piece in pieces]
        extended.append(jnp.concatenate(pieces, axis=0))
    row_mat, col_mat = filters(own[0, 0:16, HALO_W:].astype(jnp.float32), 0)
    first[...] = propagated(extended[0], extended[1], row_mat, col_mat, 0)
    for layer in range(1, LAYERS):
        row_mat, col_mat = filters(own[layer, 0:16, HALO_W:].astype(jnp.float32), layer)
        row_mats[layer - 1][...] = row_mat
        col_mats[layer - 1] = col_mat
    packed = jnp.concatenate([own[layer, :, :HALO_W] for layer in range(LAYERS)], axis=0)
    clear[...] = clear_pixels(packed[:, COLS : COLS + NH])
    tiles = stereo_tiles([packed[:, :COLS]], left_tab, right_tab)
    for tile in range(TILES):
        for part in range(2):
            block = tiles[
                tile * LANES : (tile + 1) * LANES, part * LANES : (part + 1) * LANES
            ]
            stereo[part, :, tile * LANES : (tile + 1) * LANES] = block


def chain_kernel(
    in_chip, cross, far_even, far_odd, left_tab, right_tab, first, stereo, clear, col_mats, *rest
):
    row_mats, (out, field) = rest[: LAYERS - 1], rest[LAYERS - 1 :]
    low_near, high_near, low_far, high_far = ordered(in_chip, cross, far_even, far_odd)
    pieces = [
        low_far,
        low_near[0:BAND],
        high_near[0:BAND],
        high_far,
        low_near[BAND : 2 * BAND],
        high_near[BAND : 2 * BAND],
        low_near[2 * BAND : NEAR],
        high_near[2 * BAND : NEAR],
    ]
    halo = jnp.concatenate(pieces, axis=0)
    half = halo.shape[0] // 2
    halo_tiles = stereo_tiles(
        [halo[:half, :COLS], halo[half:, :COLS]], left_tab, right_tab
    )
    halo_clear = clear_pixels(halo[:, COLS : COLS + NH])
    begins = (0, half, half + 2 * BAND, 0)
    sides = (BAND + FAR, BAND, KR, 0)
    for layer in range(LAYERS):
        height = layer_height(layer)
        before = height + 2 * KR
        low, side = begins[layer], sides[layer]
        if layer == 0:
            columned = first
        else:
            columned = propagated(
                field[0, :before], field[1, :before], row_mats[layer - 1], col_mats[layer - 1], layer
            )
        band = slice(layer * BAND, (layer + 1) * BAND)
        pieces = [clear[band]]
        if side:
            pieces = [halo_clear[low : low + side], clear[band], halo_clear[low + side : low + 2 * side]]
        passing = jnp.concatenate(pieces, axis=0)
        for tile in range(TILES):
            span = slice(tile * height, (tile + 1) * height)
            lanes = slice(tile * LANES, (tile + 1) * LANES)
            row = (low // half * TILES + tile) * half + low % half
            for part in range(2):
                within = slice(part * LANES, (part + 1) * LANES)
                pieces = [stereo[part, band, lanes]]
                if side:
                    pieces = [
                        halo_tiles[row : row + side, within],
                        stereo[part, band, lanes],
                        halo_tiles[row + side : row + 2 * side, within],
                    ]
                added = jnp.concatenate(pieces, axis=0)
                value = passing[:, lanes] * columned[span, within] + added
                field[part, :height, lanes] = value.astype(jnp.bfloat16)
        for part in range(2):
            out[layer, part] = field[part, side : side + BAND]


def exchanged(value, axis, by, phase):
    count = lax.axis_size(axis)
    lower = [i for i in range(count - by) if (i // by) % 2 == phase]
    pairs = [(i, i + by) for i in lower] + [(i + by, i) for i in lower]
    return lax.ppermute(value, axis, pairs)


def neighbours(sent):
    in_chip, cross, far_even, far_odd = sent
    cross = exchanged(cross, "rows", 1, 1)
    far_even = exchanged(far_even, "rows", 2, 0)
    far_odd = exchanged(far_odd, "rows", 2, 1)
    in_chip = exchanged(in_chip, "rows", 1, 0)
    return in_chip, cross, far_even, far_odd


def call(kernel, out_shape, in_specs, scratch=(), flops=0, moved=10**6, limit=VMEM_LIMIT):
    vmem = pl.BlockSpec(memory_space=pltpu.VMEM)
    many = isinstance(out_shape, (tuple, list))
    return pl.pallas_call(
        kernel,
        out_shape=out_shape,
        in_specs=in_specs,
        out_specs=(vmem,) * len(out_shape) if many else vmem,
        scratch_shapes=scratch,
        compiler_params=pltpu.CompilerParams(vmem_limit_bytes=limit),
        cost_estimate=pl.CostEstimate(flops=flops, bytes_accessed=moved, transcendentals=0),
    )


def body(incident, row_taps, col_taps, hogel_light, silhouette, fill_counts, hogel_index):
    vmem = pl.BlockSpec(memory_space=pltpu.VMEM)
    hbm = pl.BlockSpec(memory_space=pltpu.HBM)
    bf16, f32 = jnp.bfloat16, jnp.float32
    shaped = jax.ShapeDtypeStruct
    held = [
        pltpu.VMEM(hogel_index.shape, jnp.int32),
        pltpu.SMEM(fill_counts.shape, jnp.int32),
        pltpu.VMEM(silhouette.shape, jnp.int32),
        pltpu.VMEM(row_taps.shape, bf16),
        pltpu.VMEM(col_taps.shape, bf16),
        pltpu.VMEM(hogel_light.shape, f32),
    ]
    payload = call(
        pack_kernel,
        shaped((LAYERS, BAND, FULL_W), bf16),
        [hbm] * 6,
        held + [pltpu.SemaphoreType.DMA((6,)), pltpu.VMEM((BAND, LANES), f32)],
        flops=10**7,
        limit=PACK_LIMIT,
    )(hogel_light, silhouette, fill_counts, hogel_index, row_taps, col_taps)
    colour = jnp.minimum(lax.axis_index("depth"), COLORS - 1)
    mine = lax.dynamic_index_in_dim(incident, colour, 0, keepdims=False)
    mine = mine.reshape(2 * BAND, COLS)
    payload, mine = lax.optimization_barrier((payload, mine))
    own = lax.all_to_all(payload, "depth", 0, 0, tiled=True)
    arrived = neighbours((mine,) * 4)
    near = shaped((NEAR, HALO_W), bf16)
    far = shaped((FAR, HALO_W), bf16)
    halos = neighbours(call(halo_kernel, (near, near, far, far), [vmem])(own))
    right_tab = jnp.asarray(right_table())
    made = call(
        prepare_kernel,
        [
            shaped((TILES * layer_height(0), 2 * LANES), f32),
            shaped((2, LANES, COLS), f32),
            shaped((LANES, COLS), f32),
            shaped((LAYERS - 1, 2 * LANES, 4 * LANES), bf16),
        ]
        + [shaped((2 * block_height(layer), 2 * LANES), bf16) for layer in range(1, LAYERS)],
        [vmem] * 8,
        flops=10**9,
        moved=3 * 10**6,
    )(own, mine, *arrived, jnp.asarray(left_table(LANES)), right_tab)
    halo_rows = NEAR + FAR
    result = call(
        chain_kernel,
        shaped((LAYERS, 2, BAND, COLS), bf16),
        [vmem] * (6 + len(made)),
        [pltpu.VMEM((2, layer_height(0), COLS), bf16)],
        flops=2 * 10**9,
        moved=3 * 10**6,
    )(*halos, jnp.asarray(left_table(halo_rows)), right_tab, *made)
    gathered = lax.all_to_all(result, "depth", 0, 0, tiled=True)
    return gathered[None, :COLORS]


def solution(mesh):
    placed = (
        P(None, None, "rows", None),
        P("depth", None, None, None),
        P("depth", None, None, None),
        P("depth", None, "rows", None),
        P("depth", "rows", None),
        P("depth", "rows"),
        P("depth", "rows", None),
    )
    return jax.shard_map(
        body,
        mesh=mesh,
        in_specs=placed,
        out_specs=P("depth", None, None, "rows", None),
        check_vma=False,
    )
```

time: 45.4 us -> 39.4 us (0.87)
  waiting for transfers between devices: 13.4 us -> 3.36 us
  starting transfers between devices: 10 us -> 16.1 us
  local copies, waits for them, and re-layouts: 5.26 us -> 1.79 us
  blocking collectives: 9.91 us -> 12.1 us
  Pallas kernels: 6.37 us -> 5.54 us
    ppermute x4 -> x8, starting transfers between devices: 4.82 us -> 10.9 us  [exchanged(): return lax.ppermute(value, axis, pairs)]
    ppermute x4 -> x8, waiting for transfers between devices: 7.53 us -> 2.25 us  [exchanged(): return lax.ppermute(value, axis, pairs)]
    all_to_all x1, waiting for transfers between devices: 5.85 us -> 1.11 us  [body(): own = lax.all_to_all(payload, 'depth', 0, 0, tiled=True)]
    unnamed x18 -> x8, local copies, waits for them, and re-layouts: 4.47 us -> 1.01 us
    all_to_all x1, blocking collectives: 9.91 us -> 12.1 us  [body(): gathered = lax.all_to_all(result, 'depth', 0, 0, tiled=True)]
    pallas_call x3, Pallas kernels: 4.56 us -> 3.61 us  [the longest x1 2.43 us: body(): call(chain_kernel, shaped((LAYERS, 2, BAND, COLS), bf16), [vmem] * (6 + l...]
  transfers between devices with their start and end apart: 5 -> 9, of which waited for: 2 -> 2; matrix products, arithmetic and copies ran while one was open for 0% -> 0% of each run, Pallas kernels for 2% -> 3%
where the time goes in v3:
time: 39.4 us; the launch traced here: 39 us
  starting transfers between devices  16.1 us (41%)
  blocking collectives  12.1 us (31%)
  Pallas kernels  5.54 us (14%)
  waiting for transfers between devices  3.36 us (9%)
  local copies, waits for them, and re-layouts  1.79 us (5%)
    all_to_all x1, blocking collectives, body(): gathered = lax.all_to_all(result, 'depth', 0, 0, tiled=True)  12.1 us
    ppermute x8, starting transfers between devices, exchanged(): return lax.ppermute(value, axis, pairs)  10.9 us
    all_to_all x1, starting transfers between devices, body(): own = lax.all_to_all(payload, 'depth', 0, 0, tiled=True)  5.18 us
    pallas_call x1, Pallas kernels, body(): call(chain_kernel, shaped((LAYERS, 2, BAND, COLS), bf16), [vmem] * (6 + l...  2.43 us
    ppermute x8, waiting for transfers between devices, exchanged(): return lax.ppermute(value, axis, pairs)  2.25 us
    pallas_call x1, Pallas kernels, body(): call(pack_kernel, shaped((LAYERS, BAND, FULL_W), bf16), [hbm] * 6, held +...  1.93 us
    pallas_call x1, Pallas kernels, body(): call(prepare_kernel, [shaped((TILES * layer_height(0), 2 * LANES), f32),...  1.14 us
    all_to_all x1, waiting for transfers between devices, body(): own = lax.all_to_all(payload, 'depth', 0, 0, tiled=True)  1.11 us
  transfers between devices with their start and end apart: 9, of which 2 were waited for; matrix products, arithmetic and copies ran while one was open for 0% of the time, Pallas kernels for 3%

profile of v3, /device:TPU:0, one launch (start us, length us, event | category | flops | bytes accessed | tf_op | source)
XLA Modules:
  0.0 39.0 jit_solution(10639776203999006014)
XLA Ops:
  0.0 0.0 copy-start
  0.0 1.0 %copy-done = bf16[3,2,32,1024]{3,2,1,0:T(8,128)(2,1)S(1)} copy-done((bf16[3,2,32,1024]{3,2,1,0:T(8,128)(2,1)S(1)}, bf16[3,2,32,1024]{3,2,1,0:T(8,128)(2,1)}, u32[]{:S(2)}) %copy-start) | copy-done | bytes 393240
  1.0 1.9 %shard_map.100 = bf16[4,32,1280]{2,1,0:T(8,128)(2,1)} custom-call(f32[1,3,32,1024]{3,2,1,0:T(8,128)} %light.1, s32[1,32,64]{2,1,0:T(8,128)} %edges.1, s32[1,2]{1,0:T(1,128)} %counts.1, s32[1,2,64]{2,1,0:T(2,128)} %listed.1, bf16[1,3,2,33]{3,2,1,0:T(2,128)(2,1)} %row_taps.1, bf16[1,3,2,127]{3,2,1,0:T(2,128)(2,1)} %col_taps.1), custom_call_target="tpu_custom_call" | custom-call | flops 10000000 | bytes 1000000 | tf_op jit(solution)/shard_map/pallas_call | solution.py:361
  3.0 5.2 %all-to-all-start = ((bf16[4,32,1280]{2,1,0:T(8,128)(2,1)}), bf16[4,32,1280]{2,1,0:T(8,128)(2,1)S(1)}, u32[]{:S(2)}, u32[]{:S(2)}) async-start(bf16[4,32,1280]{2,1,0:T(8,128)(2,1)} %shard_map.100), calls=%async_computation | async-start | bytes 655360 | tf_op jit(solution)/shard_map/all_to_all | solution.py:373
  8.1 0.0 copy-start.1
  8.1 0.0 copy-start.2
  8.1 0.0 collective-permute-start.4
  8.1 0.8 %collective-permute-start.5 = (bf16[64,1024]{1,0:T(8,128)(2,1)S(1)}, bf16[64,1024]{1,0:T(8,128)(2,1)S(1)}, u32[]{:S(2)}, u32[]{:S(2)}) collective-permute-start(bf16[64,1024]{1,0:T(8,128)(2,1)S(1)} %bitcast.4), channel_id=1, source_target_pairs={{1,2},{3,4},{5,6},{2,1},{4,3},{6,5},{9,10},{11,12},{13,14},{10,9},... | collective-permute-start | bytes 393224 | tf_op jit(solution)/shard_map/ppermute | solution.py:322
  8.9 3.3 %collective-permute-start.6 = (bf16[64,1024]{1,0:T(8,128)(2,1)S(1)}, bf16[64,1024]{1,0:T(8,128)(2,1)S(1)}, u32[]{:S(2)}, u32[]{:S(2)}) collective-permute-start(bf16[64,1024]{1,0:T(8,128)(2,1)S(1)} %bitcast.5), channel_id=1, source_target_pairs={{0,2},{1,3},{4,6},{5,7},{2,0},{3,1},{6,4},{7,5},{8,10},{9,11},{12,... | collective-permute-start | bytes 393224 | tf_op jit(solution)/shard_map/ppermute | solution.py:322
  12.2 0.7 %collective-permute-start.7 = (bf16[64,1024]{1,0:T(8,128)(2,1)S(1)}, bf16[64,1024]{1,0:T(8,128)(2,1)S(1)}, u32[]{:S(2)}, u32[]{:S(2)}) collective-permute-start(bf16[64,1024]{1,0:T(8,128)(2,1)S(1)} %bitcast.6), channel_id=1, source_target_pairs={{2,4},{3,5},{4,2},{5,3},{10,12},{11,13},{12,10},{13,11},{18,20},{1... | collective-permute-start | bytes 393224 | tf_op jit(solution)/shard_map/ppermute | solution.py:322
  12.9 1.1 %all-to-all-done.own = bf16[4,32,1280]{2,1,0:T(8,128)(2,1)S(1)} async-done(((bf16[4,32,1280]{2,1,0:T(8,128)(2,1)}), bf16[4,32,1280]{2,1,0:T(8,128)(2,1)S(1)}, u32[]{:S(2)}, u32[]{:S(2)}) %all-to-all-start) | async-done | bytes 327712 | tf_op jit(solution)/shard_map/all_to_all | solution.py:373
  14.1 0.1 collective-permute-start
  14.1 0.0 collective-permute-done.4.in_chip
  14.1 0.7 %collective-permute-start.1 = (bf16[80,1152]{1,0:T(8,128)(2,1)S(1)}, bf16[80,1152]{1,0:T(8,128)(2,1)S(1)}, u32[]{:S(2)}, u32[]{:S(2)}) collective-permute-start(bf16[80,1152]{1,0:T(8,128)(2,1)S(1)} %get-tuple-element.20), channel_id=1, source_target_pairs={{1,2},{3,4},{5,6},{2,1},{4,3},{6,5},{9,10},{11,12},{13,14},{10,9},... | collective-permute-start | bytes 552968 | tf_op jit(solution)/shard_map/ppermute | solution.py:322
  14.8 0.0 collective-permute-done.5.cross
  14.8 4.6 %collective-permute-start.2 = (bf16[16,1152]{1,0:T(8,128)(2,1)S(1)}, bf16[16,1152]{1,0:T(8,128)(2,1)S(1)}, u32[]{:S(2)}, u32[]{:S(2)}) collective-permute-start(bf16[16,1152]{1,0:T(8,128)(2,1)S(1)} %get-tuple-element.21), channel_id=1, source_target_pairs={{0,2},{1,3},{4,6},{5,7},{2,0},{3,1},{6,4},{7,5},{8,10},{9,11},{12,... | collective-permute-start | bytes 110600 | tf_op jit(solution)/shard_map/ppermute | solution.py:322
  19.4 0.0 collective-permute-done.6.far_even
  19.5 0.0 copy-start.3
  19.5 0.8 %collective-permute-start.3 = (bf16[16,1152]{1,0:T(8,128)(2,1)S(1)}, bf16[16,1152]{1,0:T(8,128)(2,1)S(1)}, u32[]{:S(2)}, u32[]{:S(2)}) collective-permute-start(bf16[16,1152]{1,0:T(8,128)(2,1)S(1)} %get-tuple-element.22), channel_id=1, source_target_pairs={{2,4},{3,5},{4,2},{5,3},{10,12},{11,13},{12,10},{13,11},{18,20},{1... | collective-permute-start | bytes 110600 | tf_op jit(solution)/shard_map/ppermute | solution.py:322
  20.2 0.0 collective-permute-done.7.far_odd
  20.3 0.0 copy-done.1
  20.3 0.0 copy-done.2
  20.3 1.1 %shard_map.102 = (f32[1024,256]{1,0:T(8,128)S(1)}, f32[2,128,1024]{2,1,0:T(8,128)S(1)}, f32[128,1024]{1,0:T(8,128)S(1)}, bf16[3,256,512]{2,1,0:T(8,128)(2,1)S(1)...) custom-call(bf16[4,32,1280]{2,1,0:T(8,128)(2,1)S(1)} %all-to-all-done.own, ...), custom_call_target="tpu_custom_call" | custom-call | flops 1000000000 | bytes 3000000 | tf_op jit(solution)/shard_map/pallas_call | solution.py:379
  21.4 2.2 %collective-permute-done.2.far_even = bf16[16,1152]{1,0:T(8,128)(2,1)S(1)} collective-permute-done((bf16[16,1152]{1,0:T(8,128)(2,1)S(1)}, bf16[16,1152]{1,0:T(8,128)(2,1)S(1)}, u32[]{:S(2)}, u32[]{:S(2)}) %collective-permute-start.2) | collective-permute-done | bytes 36896 | tf_op jit(solution)/shard_map/ppermute | solution.py:322
  23.7 0.0 collective-permute-done.3.far_odd
  23.7 0.0 collective-permute-done.in_chip
  23.7 0.0 collective-permute-done.1.cross
  23.7 0.0 copy-done.3
  23.7 2.4 %shard_map.103 = bf16[4,2,32,1024]{3,2,1,0:T(8,128)(2,1)S(1)} custom-call(bf16[80,1152]{1,0:T(8,128)(2,1)S(1)} %collective-permute-done.in_chip, bf16[80,1152]{1,0:T(8,128)(2,1)S(1)} %collective-permute-done.1.cross, bf16[16,1152]{1,0:T(8,128)(2,1)S(1)} %collective-permute-done.2.far_even, bf16[16,1152]{1,0:T(8,128)(2,1)S(1)} %collective-permute-done.3.far_odd, ...), custom_call_target="tpu_custom_call" | custom-call | flops 2000000000 | bytes 3000000 | tf_op jit(solution)/shard_map/pallas_call | solution.py:393
  26.1 12.1 %all_to_all.10 = bf16[4,2,32,1024]{3,2,1,0:T(8,128)(2,1)S(1)} all-to-all(bf16[4,2,32,1024]{3,2,1,0:T(8,128)(2,1)S(1)} %shard_map.103), channel_id=1, replica_groups=mesh['depth'=4,'rows'=8] {'depth'}, dimensions={0} | all-to-all | bytes 1048576 | tf_op jit(solution)/shard_map/all_to_all | solution.py:401
  38.2 0.8 %slice_bitcast_fusion = bf16[1,3,2,32,1024]{4,3,2,1,0:T(8,128)(2,1)} fusion(bf16[4,2,32,1024]{3,2,1,0:T(8,128)(2,1)S(1)} %all_to_all.10), kind=kLoop, calls=%fused_computation | loop fusion | bytes 786432 | tf_op jit(solution)/shard_map/broadcast_in_dim | solution.py:402
  (2 shorter events, 0.0 us)
Async XLA Ops:
  0.0 1.0 %copy-start = (bf16[3,2,32,1024]{3,2,1,0:T(8,128)(2,1)S(1)}, bf16[3,2,32,1024]{3,2,1,0:T(8,128)(2,1)}, u32[]{:S(2)}) copy-start(bf16[3,2,32,1024]{3,2,1,0:T(8,128)(2,1)} %param.10) | copy-start | bytes 1179652
  3.0 11.1 %all-to-all-start = ((bf16[4,32,1280]{2,1,0:T(8,128)(2,1)}), bf16[4,32,1280]{2,1,0:T(8,128)(2,1)S(1)}, u32[]{:S(2)}, u32[]{:S(2)}) async-start(bf16[4,32,1280]{2,1,0:T(8,128)(2,1)} %shard_map.100), calls=%async_computation | async-start | bytes 655360 | tf_op jit(solution)/shard_map/all_to_all | solution.py:373
  8.1 12.1 %copy-start.1 = (bf16[256,256]{1,0:T(8,128)(2,1)S(1)}, bf16[256,256]{1,0:T(8,128)(2,1)}, u32[]{:S(2)}) copy-start(bf16[256,256]{1,0:T(8,128)(2,1)} %constant.19.clone.right_tab) | copy-start | bytes 393220
  8.1 12.1 %copy-start.2 = (bf16[256,256]{1,0:T(8,128)(2,1)S(1)}, bf16[256,256]{1,0:T(8,128)(2,1)}, u32[]{:S(2)}) copy-start(bf16[256,256]{1,0:T(8,128)(2,1)} %constant.20.clone.left_tab) | copy-start | bytes 393220
  8.1 6.0 %collective-permute-start.4 = (bf16[64,1024]{1,0:T(8,128)(2,1)S(1)}, bf16[64,1024]{1,0:T(8,128)(2,1)S(1)}, u32[]{:S(2)}, u32[]{:S(2)}) collective-permute-start(bf16[64,1024]{1,0:T(8,128)(2,1)S(1)} %bitcast.3), channel_id=1, source_target_pairs={{0,1},{2,3},{4,5},{6,7},{1,0},{3,2},{5,4},{7,6},{8,9},{10,11},{12,... | collective-permute-start | bytes 393224 | tf_op jit(solution)/shard_map/ppermute | solution.py:322
  8.1 6.7 %collective-permute-start.5 = (bf16[64,1024]{1,0:T(8,128)(2,1)S(1)}, bf16[64,1024]{1,0:T(8,128)(2,1)S(1)}, u32[]{:S(2)}, u32[]{:S(2)}) collective-permute-start(bf16[64,1024]{1,0:T(8,128)(2,1)S(1)} %bitcast.4), channel_id=1, source_target_pairs={{1,2},{3,4},{5,6},{2,1},{4,3},{6,5},{9,10},{11,12},{13,14},{10,9},... | collective-permute-start | bytes 393224 | tf_op jit(solution)/shard_map/ppermute | solution.py:322
  8.9 10.5 %collective-permute-start.6 = (bf16[64,1024]{1,0:T(8,128)(2,1)S(1)}, bf16[64,1024]{1,0:T(8,128)(2,1)S(1)}, u32[]{:S(2)}, u32[]{:S(2)}) collective-permute-start(bf16[64,1024]{1,0:T(8,128)(2,1)S(1)} %bitcast.5), channel_id=1, source_target_pairs={{0,2},{1,3},{4,6},{5,7},{2,0},{3,1},{6,4},{7,5},{8,10},{9,11},{12,... | collective-permute-start | bytes 393224 | tf_op jit(solution)/shard_map/ppermute | solution.py:322
  12.2 8.0 %collective-permute-start.7 = (bf16[64,1024]{1,0:T(8,128)(2,1)S(1)}, bf16[64,1024]{1,0:T(8,128)(2,1)S(1)}, u32[]{:S(2)}, u32[]{:S(2)}) collective-permute-start(bf16[64,1024]{1,0:T(8,128)(2,1)S(1)} %bitcast.6), channel_id=1, source_target_pairs={{2,4},{3,5},{4,2},{5,3},{10,12},{11,13},{12,10},{13,11},{18,20},{1... | collective-permute-start | bytes 393224 | tf_op jit(solution)/shard_map/ppermute | solution.py:322
  14.1 9.6 %collective-permute-start = (bf16[80,1152]{1,0:T(8,128)(2,1)S(1)}, bf16[80,1152]{1,0:T(8,128)(2,1)S(1)}, u32[]{:S(2)}, u32[]{:S(2)}) collective-permute-start(bf16[80,1152]{1,0:T(8,128)(2,1)S(1)} %get-tuple-element.19), channel_id=1, source_target_pairs={{0,1},{2,3},{4,5},{6,7},{1,0},{3,2},{5,4},{7,6},{8,9},{10,11},{12,... | collective-permute-start | bytes 552968 | tf_op jit(solution)/shard_map/ppermute | solution.py:322
  14.1 9.5 %collective-permute-start.1 = (bf16[80,1152]{1,0:T(8,128)(2,1)S(1)}, bf16[80,1152]{1,0:T(8,128)(2,1)S(1)}, u32[]{:S(2)}, u32[]{:S(2)}) collective-permute-start(bf16[80,1152]{1,0:T(8,128)(2,1)S(1)} %get-tuple-element.20), channel_id=1, source_target_pairs={{1,2},{3,4},{5,6},{2,1},{4,3},{6,5},{9,10},{11,12},{13,14},{10,9},... | collective-permute-start | bytes 552968 | tf_op jit(solution)/shard_map/ppermute | solution.py:322
  14.8 8.8 %collective-permute-start.2 = (bf16[16,1152]{1,0:T(8,128)(2,1)S(1)}, bf16[16,1152]{1,0:T(8,128)(2,1)S(1)}, u32[]{:S(2)}, u32[]{:S(2)}) collective-permute-start(bf16[16,1152]{1,0:T(8,128)(2,1)S(1)} %get-tuple-element.21), channel_id=1, source_target_pairs={{0,2},{1,3},{4,6},{5,7},{2,0},{3,1},{6,4},{7,5},{8,10},{9,11},{12,... | collective-permute-start | bytes 110600 | tf_op jit(solution)/shard_map/ppermute | solution.py:322
  19.5 4.2 %copy-start.3 = (bf16[192,192]{1,0:T(8,128)(2,1)S(1)}, bf16[192,192]{1,0:T(8,128)(2,1)}, u32[]{:S(2)}) copy-start(bf16[192,192]{1,0:T(8,128)(2,1)} %constant.21.clone.left_tab) | copy-start | bytes 221188
  19.5 4.2 %collective-permute-start.3 = (bf16[16,1152]{1,0:T(8,128)(2,1)S(1)}, bf16[16,1152]{1,0:T(8,128)(2,1)S(1)}, u32[]{:S(2)}, u32[]{:S(2)}) collective-permute-start(bf16[16,1152]{1,0:T(8,128)(2,1)S(1)} %get-tuple-element.22), channel_id=1, source_target_pairs={{2,4},{3,5},{4,2},{5,3},{10,12},{11,13},{12,10},{13,11},{18,20},{1... | collective-permute-start | bytes 110600 | tf_op jit(solution)/shard_map/ppermute | solution.py:322

commit v4 on v3

--- a/solution.py
+++ b/solution.py
@@ -75,8 +75,13 @@
     return jnp.where(column // HS == tile, 1.0, 0.0).astype(jnp.bfloat16)
 
 
-def pack_kernel(light, edges, counts, listed, row_taps, col_taps, out, *scratch):
+def own_colour():
+    return jnp.maximum(lax.axis_index("depth") - (LAYERS - COLORS), 0)
+
+
+def pack_kernel(light, edges, counts, listed, row_taps, col_taps, incident, out, mine, *scratch):
     held, sems, taps = scratch[:6], scratch[6], scratch[7]
+    picked = pltpu.make_async_copy(incident.at[own_colour()], mine, sems.at[6])
     sources = (listed, counts, edges, row_taps, col_taps, light)
     copies = [
         pltpu.make_async_copy(source, target, sems.at[place])
@@ -84,6 +89,7 @@
     ]
     for copy in reversed(copies):
         copy.start()
+    picked.start()
     listed, counts, edges, row_taps, col_taps, light = held
     spread = spread_matrix()
     slot = lax.broadcasted_iota(jnp.int32, (NH, NH), 0)
@@ -103,19 +109,22 @@
         [edges[0].astype(jnp.float32), jnp.zeros((BAND, LANES - NH), jnp.float32)], axis=1
     ).astype(jnp.bfloat16)
     for colour in range(COLORS):
-        out[colour, :, COLS:HALO_W] = edge_tile
+        chunk = colour + LAYERS - COLORS
+        out[chunk, :, COLS:HALO_W] = edge_tile
         taps[...] = jnp.zeros_like(taps)
         taps[0:2, : 2 * KC + 1] = col_taps[0, colour].astype(jnp.float32)
         taps[2:4, : 2 * KR + 1] = row_taps[0, colour].astype(jnp.float32)
-        out[colour, :, HALO_W:] = taps[...].astype(jnp.bfloat16)
-    for spare in range(COLORS, LAYERS):
+        out[chunk, :, HALO_W:] = taps[...].astype(jnp.bfloat16)
+    for spare in range(LAYERS - COLORS):
         out[spare] = jnp.zeros((BAND, FULL_W), jnp.bfloat16)
     copies[5].wait()
     for colour in range(COLORS):
-        out[colour, :, :COLS] = (light[0, colour] * live_pix).astype(jnp.bfloat16)
-
-
-def halo_kernel(own, in_chip, cross, far_even, far_odd):
+        chunk = colour + LAYERS - COLORS
+        out[chunk, :, :COLS] = (light[0, colour] * live_pix).astype(jnp.bfloat16)
+    picked.wait()
+
+
+def halo_kernel(own, incident, beyond, in_chip, cross, far_even, far_odd):
     band = lax.axis_index("rows")
     core = band % 2
     odd = (band // 2) % 2
@@ -124,6 +133,9 @@
         near[0:BAND] = own[0, :, :HALO_W]
         near[BAND : 2 * BAND] = own[1, :, :HALO_W]
         near[2 * BAND : NEAR] = own[2, pl.ds(pl.multiple_of(start, KR), KR), :HALO_W]
+    in_chip[NEAR : NEAR + BAND, :COLS] = incident[0]
+    in_chip[NEAR + BAND : NEAR + 2 * BAND, :COLS] = incident[1]
+    in_chip[NEAR + 2 * BAND :, :COLS] = beyond[...]
     for far, start in ((far_even, (1 - odd) * last), (far_odd, odd * last)):
         far[...] = own[0, pl.ds(pl.multiple_of(start, KR), KR), :HALO_W]
 
@@ -132,7 +144,7 @@
     band = lax.axis_index("rows")
     even_core = band % 2 == 0
     even_chip = (band // 2) % 2 == 0
-    in_chip, cross = in_chip[...], cross[...]
+    in_chip, cross = in_chip[:NEAR], cross[...]
     far_even, far_odd = far_even[...], far_odd[...]
     return (
         jnp.where(even_core, cross, in_chip),
@@ -231,14 +243,25 @@
 
 
 def prepare_kernel(
-    own, incident, in_chip, cross, far_even, far_odd, left_tab, right_tab,
+    own, incident, in_chip, cross, far, left_tab, right_tab,
     first, stereo, clear, col_mats, *row_mats
 ):
-    low_near, high_near, low_far, high_far = ordered(in_chip, cross, far_even, far_odd)
+    even_core = lax.axis_index("rows") % 2 == 0
+    cross, far = cross[...], far[...]
+    partner = in_chip[NEAR : NEAR + 2 * BAND, :COLS]
+    beyond = in_chip[NEAR + 2 * BAND :, :COLS]
+    sides = (
+        jnp.where(even_core, far, beyond),
+        jnp.where(even_core, cross, partner),
+        jnp.where(even_core, partner, cross),
+        jnp.where(even_core, beyond, far),
+    )
     extended = []
     for part in range(2):
-        pieces = [low_far, low_near, incident[...], high_near, high_far]
-        pieces = [piece[part * BAND : (part + 1) * BAND] for piece in pieces]
+        low_far, low_near, high_near, high_far = (
+            side[part * BAND : (part + 1) * BAND] for side in sides
+        )
+        pieces = [low_far, low_near, incident[part], high_near, high_far]
         extended.append(jnp.concatenate(pieces, axis=0))
     row_mat, col_mat = filters(own[0, 0:16, HALO_W:].astype(jnp.float32), 0)
     first[...] = propagated(extended[0], extended[1], row_mat, col_mat, 0)
@@ -260,7 +283,8 @@
 def chain_kernel(
     in_chip, cross, far_even, far_odd, left_tab, right_tab, first, stereo, clear, col_mats, *rest
 ):
-    row_mats, (out, field) = rest[: LAYERS - 1], rest[LAYERS - 1 :]
+    row_mats, outs, field = rest[: LAYERS - 1], rest[LAYERS - 1 : -1], rest[-1]
+    depth = lax.axis_index("depth")
     low_near, high_near, low_far, high_far = ordered(in_chip, cross, far_even, far_odd)
     pieces = [
         low_far,
@@ -311,8 +335,27 @@
                 added = jnp.concatenate(pieces, axis=0)
                 value = passing[:, lanes] * columned[span, within] + added
                 field[part, :height, lanes] = value.astype(jnp.bfloat16)
-        for part in range(2):
-            out[layer, part] = field[part, side : side + BAND]
+        for hop, out in enumerate(outs):
+
+            @pl.when((depth + hop) % LAYERS == layer)
+            def keep(out=out, side=side):
+                for part in range(2):
+                    out[part] = field[part, side : side + BAND]
+
+
+def home_kernel(*refs):
+    arrived, out, sems = refs[:LAYERS], refs[LAYERS], refs[LAYERS + 1]
+    depth = lax.axis_index("depth")
+    for colour in range(COLORS):
+        source = colour + LAYERS - COLORS
+        for hop in range(LAYERS):
+
+            @pl.when((source + hop) % LAYERS == depth)
+            def begin(hop=hop, colour=colour):
+                pltpu.make_async_copy(arrived[hop], out.at[0, colour], sems.at[colour]).start()
+
+    for colour in range(COLORS):
+        pltpu.make_async_copy(arrived[0], out.at[0, colour], sems.at[colour]).wait()
 
 
 def exchanged(value, axis, by, phase):
@@ -322,17 +365,33 @@
     return lax.ppermute(value, axis, pairs)
 
 
+def far_incident(value):
+    count = lax.axis_size("rows")
+    pairs = [(i, i + 2) for i in range(0, count - 2, 2)]
+    pairs += [(i, i - 2) for i in range(3, count, 2)]
+    return lax.ppermute(value, "rows", pairs)
+
+
+def sent_home(value, hop):
+    first = LAYERS - COLORS
+    pairs = [(i, (i + hop) % LAYERS) for i in range(first, LAYERS)]
+    return lax.ppermute(value, "depth", pairs)
+
+
 def neighbours(sent):
     in_chip, cross, far_even, far_odd = sent
+    in_chip = exchanged(in_chip, "rows", 1, 0)
     cross = exchanged(cross, "rows", 1, 1)
     far_even = exchanged(far_even, "rows", 2, 0)
     far_odd = exchanged(far_odd, "rows", 2, 1)
-    in_chip = exchanged(in_chip, "rows", 1, 0)
     return in_chip, cross, far_even, far_odd
 
 
-def call(kernel, out_shape, in_specs, scratch=(), flops=0, moved=10**6, limit=VMEM_LIMIT):
-    vmem = pl.BlockSpec(memory_space=pltpu.VMEM)
+def call(
+    kernel, out_shape, in_specs, scratch=(), flops=0, moved=10**6, limit=VMEM_LIMIT,
+    out_space=pltpu.VMEM,
+):
+    vmem = pl.BlockSpec(memory_space=out_space)
     many = isinstance(out_shape, (tuple, list))
     return pl.pallas_call(
         kernel,
@@ -358,23 +417,22 @@
         pltpu.VMEM(col_taps.shape, bf16),
         pltpu.VMEM(hogel_light.shape, f32),
     ]
-    payload = call(
+    payload, mine = call(
         pack_kernel,
-        shaped((LAYERS, BAND, FULL_W), bf16),
-        [hbm] * 6,
-        held + [pltpu.SemaphoreType.DMA((6,)), pltpu.VMEM((BAND, LANES), f32)],
+        (shaped((LAYERS, BAND, FULL_W), bf16), shaped(incident.shape[1:], bf16)),
+        [hbm] * 7,
+        held + [pltpu.SemaphoreType.DMA((7,)), pltpu.VMEM((BAND, LANES), f32)],
         flops=10**7,
         limit=PACK_LIMIT,
-    )(hogel_light, silhouette, fill_counts, hogel_index, row_taps, col_taps)
-    colour = jnp.minimum(lax.axis_index("depth"), COLORS - 1)
-    mine = lax.dynamic_index_in_dim(incident, colour, 0, keepdims=False)
-    mine = mine.reshape(2 * BAND, COLS)
-    payload, mine = lax.optimization_barrier((payload, mine))
+    )(hogel_light, silhouette, fill_counts, hogel_index, row_taps, col_taps, incident)
+    flat = mine.reshape(2 * BAND, COLS)
     own = lax.all_to_all(payload, "depth", 0, 0, tiled=True)
-    arrived = neighbours((mine,) * 4)
+    cross_in = exchanged(flat, "rows", 1, 1)
+    far_in = far_incident(flat)
+    chip = shaped((NEAR + 4 * BAND, HALO_W), bf16)
     near = shaped((NEAR, HALO_W), bf16)
     far = shaped((FAR, HALO_W), bf16)
-    halos = neighbours(call(halo_kernel, (near, near, far, far), [vmem])(own))
+    halos = neighbours(call(halo_kernel, (chip, near, far, far), [vmem] * 3)(own, mine, cross_in))
     right_tab = jnp.asarray(right_table())
     made = call(
         prepare_kernel,
@@ -385,21 +443,28 @@
             shaped((LAYERS - 1, 2 * LANES, 4 * LANES), bf16),
         ]
         + [shaped((2 * block_height(layer), 2 * LANES), bf16) for layer in range(1, LAYERS)],
-        [vmem] * 8,
+        [vmem] * 7,
         flops=10**9,
         moved=3 * 10**6,
-    )(own, mine, *arrived, jnp.asarray(left_table(LANES)), right_tab)
+    )(own, mine, halos[0], cross_in, far_in, jnp.asarray(left_table(LANES)), right_tab)
     halo_rows = NEAR + FAR
-    result = call(
+    results = call(
         chain_kernel,
-        shaped((LAYERS, 2, BAND, COLS), bf16),
+        [shaped((2, BAND, COLS), bf16)] * LAYERS,
         [vmem] * (6 + len(made)),
         [pltpu.VMEM((2, layer_height(0), COLS), bf16)],
         flops=2 * 10**9,
         moved=3 * 10**6,
     )(*halos, jnp.asarray(left_table(halo_rows)), right_tab, *made)
-    gathered = lax.all_to_all(result, "depth", 0, 0, tiled=True)
-    return gathered[None, :COLORS]
+    arrived = [results[0]] + [sent_home(results[hop], hop) for hop in (2, 1, 3)]
+    arrived = [arrived[0], arrived[2], arrived[1], arrived[3]]
+    return call(
+        home_kernel,
+        shaped((1, COLORS, 2, BAND, COLS), bf16),
+        [vmem] * LAYERS,
+        [pltpu.SemaphoreType.DMA((COLORS,))],
+        out_space=pltpu.HBM,
+    )(*arrived)
 
 
 def solution(mesh):

time: 39.4 us -> 42.3 us (1.074)
  the two profiles are of different devices: /device:TPU:0 before, /device:TPU:10 now
where the time goes in v4:
time: 42.3 us; the launch traced here: 42 us
  starting transfers between devices  23.5 us (56%)
  waiting for transfers between devices  11.6 us (27%)
  Pallas kernels  6.69 us (16%)
    ppermute x5, starting transfers between devices, exchanged(): return lax.ppermute(value, axis, pairs)  8.41 us
    ppermute x3, starting transfers between devices, sent_home(): return lax.ppermute(value, 'depth', pairs)  7.22 us
    ppermute x3, waiting for transfers between devices, sent_home(): return lax.ppermute(value, 'depth', pairs)  6.5 us
    ppermute x5, waiting for transfers between devices, exchanged(): return lax.ppermute(value, axis, pairs)  5.1 us
    all_to_all x1, starting transfers between devices, body(): own = lax.all_to_all(payload, 'depth', 0, 0, tiled=True)  4.39 us
    ppermute x1, starting transfers between devices, far_incident(): return lax.ppermute(value, 'rows', pairs)  3.47 us
    pallas_call x1, Pallas kernels, body(): call(chain_kernel, [shaped((2, BAND, COLS), bf16)] * LAYERS, [vmem] * (6...  2.75 us
    pallas_call x1, Pallas kernels, body(): call(pack_kernel, (shaped((LAYERS, BAND, FULL_W), bf16), shaped(incident....  1.99 us
  transfers between devices with their start and end apart: 10, of which 4 were waited for; matrix products, arithmetic and copies ran while one was open for 0% of the time, Pallas kernels for 3%

profile of v4, /device:TPU:10, one launch (start us, length us, event | category | flops | bytes accessed | tf_op | source)
XLA Modules:
  0.0 42.0 jit_solution(16617880373059977435)
XLA Ops:
  0.0 2.0 %shard_map.100 = (bf16[4,32,1280]{2,1,0:T(8,128)(2,1)}, bf16[2,32,1024]{2,1,0:T(8,128)(2,1)}) custom-call(f32[1,3,32,1024]{3,2,1,0:T(8,128)} %light.1, s32[1,32,64]{2,1,0:T(8,128)} %edges.1, s32[1,2]{1,0:T(1,128)} %counts.1, s32[1,2,64]{2,1,0:T(2,128)} %listed.1, bf16[1,3,2,33]{3,2,1,0:T(2,128)(2,1)} %row_taps.1, bf16[1,3,2,127]{3,2,1,0:T(2,128)(2,1)} %col_taps.1, ...), custom_call_target="tpu_custom_call" | custom-call | flops 10000000 | bytes 1000000 | tf_op jit(solution)/shard_map/pallas_call | solution.py:420
  2.0 0.0 copy-start
  2.0 4.4 %all-to-all-start = ((bf16[4,32,1280]{2,1,0:T(8,128)(2,1)}), bf16[4,32,1280]{2,1,0:T(8,128)(2,1)S(1)}, u32[]{:S(2)}, u32[]{:S(2)}) async-start(bf16[4,32,1280]{2,1,0:T(8,128)(2,1)} %get-tuple-element.22), calls=%async_computation | async-start | bytes 655360 | tf_op jit(solution)/shard_map/all_to_all | solution.py:429
  6.4 0.0 copy-done
  6.4 0.0 copy-start.1
  6.4 0.0 copy-start.2
  6.4 2.0 %collective-permute-start = (bf16[64,1024]{1,0:T(8,128)(2,1)S(1)}, bf16[64,1024]{1,0:T(8,128)(2,1)S(1)}, u32[]{:S(2)}, u32[]{:S(2)}) collective-permute-start(bf16[64,1024]{1,0:T(8,128)(2,1)S(1)} %bitcast.1), channel_id=1, source_target_pairs={{1,2},{3,4},{5,6},{2,1},{4,3},{6,5},{9,10},{11,12},{13,14},{10,9},... | collective-permute-start | bytes 393224 | tf_op jit(solution)/shard_map/ppermute | solution.py:365
  8.5 4.4 %collective-permute-done.beyond.cross = bf16[64,1024]{1,0:T(8,128)(2,1)S(1)} collective-permute-done((bf16[64,1024]{1,0:T(8,128)(2,1)S(1)}, bf16[64,1024]{1,0:T(8,128)(2,1)S(1)}, u32[]{:S(2)}, u32[]{:S(2)}) %collective-permute-start) | collective-permute-done | bytes 131104 | tf_op jit(solution)/shard_map/ppermute | solution.py:365
  12.8 0.0 all-to-all-done.own
  12.9 0.2 collective-permute-start.1
  13.1 3.5 %collective-permute-start.5 = (bf16[64,1024]{1,0:T(8,128)(2,1)S(1)}, bf16[64,1024]{1,0:T(8,128)(2,1)S(1)}, u32[]{:S(2)}, u32[]{:S(2)}) collective-permute-start(bf16[64,1024]{1,0:T(8,128)(2,1)S(1)} %bitcast.2), channel_id=1, source_target_pairs={{0,2},{2,4},{4,6},{3,1},{5,3},{7,5},{8,10},{10,12},{12,14},{11,9},... | collective-permute-start | bytes 393224 | tf_op jit(solution)/shard_map/ppermute | solution.py:372
  16.5 1.9 %collective-permute-start.2 = (bf16[80,1152]{1,0:T(8,128)(2,1)S(1)}, bf16[80,1152]{1,0:T(8,128)(2,1)S(1)}, u32[]{:S(2)}, u32[]{:S(2)}) collective-permute-start(bf16[80,1152]{1,0:T(8,128)(2,1)S(1)} %get-tuple-element.25), channel_id=1, source_target_pairs={{1,2},{3,4},{5,6},{2,1},{4,3},{6,5},{9,10},{11,12},{13,14},{10,9},... | collective-permute-start | bytes 552968 | tf_op jit(solution)/shard_map/ppermute | solution.py:365
  18.5 0.1 collective-permute-start.3
  18.6 0.0 copy-start.3
  18.6 4.2 %collective-permute-start.4 = (bf16[16,1152]{1,0:T(8,128)(2,1)S(1)}, bf16[16,1152]{1,0:T(8,128)(2,1)S(1)}, u32[]{:S(2)}, u32[]{:S(2)}) collective-permute-start(bf16[16,1152]{1,0:T(8,128)(2,1)S(1)} %get-tuple-element.27), channel_id=1, source_target_pairs={{2,4},{3,5},{4,2},{5,3},{10,12},{11,13},{12,10},{13,11},{18,20},{1... | collective-permute-start | bytes 110600 | tf_op jit(solution)/shard_map/ppermute | solution.py:365
  22.8 0.0 collective-permute-done.5.far
  22.8 0.0 collective-permute-done.1.in_chip
  22.8 0.0 copy-done.1
  22.8 0.0 copy-done.2
  22.8 1.1 %shard_map.102 = (f32[1024,256]{1,0:T(8,128)S(1)}, f32[2,128,1024]{2,1,0:T(8,128)S(1)}, f32[128,1024]{1,0:T(8,128)S(1)}, bf16[3,256,512]{2,1,0:T(8,128)(2,1)S(1)...) custom-call(bf16[4,32,1280]{2,1,0:T(8,128)(2,1)S(1)} %all-to-all-done.own, ...), custom_call_target="tpu_custom_call" | custom-call | flops 1000000000 | bytes 3000000 | tf_op jit(solution)/shard_map/pallas_call | solution.py:437
  23.9 0.0 collective-permute-done.3.far_even
  23.9 0.7 %collective-permute-done.4.far_odd = bf16[16,1152]{1,0:T(8,128)(2,1)S(1)} collective-permute-done((bf16[16,1152]{1,0:T(8,128)(2,1)S(1)}, bf16[16,1152]{1,0:T(8,128)(2,1)S(1)}, u32[]{:S(2)}, u32[]{:S(2)}) %collective-permute-start.4) | collective-permute-done | bytes 36896 | tf_op jit(solution)/shard_map/ppermute | solution.py:365
  24.7 0.0 collective-permute-done.2.cross
  24.7 0.0 copy-done.3
  24.7 2.8 %shard_map.103 = (bf16[2,32,1024]{2,1,0:T(8,128)(2,1)S(1)}, bf16[2,32,1024]{2,1,0:T(8,128)(2,1)S(1)}, bf16[2,32,1024]{2,1,0:T(8,128)(2,1)S(1)}, bf16[2,32,1024]{2,1,0:T(8,128)(2,1)S(1)}) custom-call(bf16[208,1152]{1,0:T(8,128)(2,1)S(1)} %collective-permute-done.1.in_chip, bf16[80,1152]{1,0:T(8,128)(2,1)S(1)} %collective-permute-done.2.cross, ...), custom_call_target="tpu_custom_call" | custom-call | flops 2000000000 | bytes 3000000 | tf_op jit(solution)/shard_map/pallas_call | solution.py:451
  27.4 3.4 %collective-permute-start.6 = (bf16[2,32,1024]{2,1,0:T(8,128)(2,1)S(1)}, bf16[2,32,1024]{2,1,0:T(8,128)(2,1)S(1)}, u32[]{:S(2)}, u32[]{:S(2)}) collective-permute-start(bf16[2,32,1024]{2,1,0:T(8,128)(2,1)S(1)} %get-tuple-element.36), channel_id=1, source_target_pairs={{8,16},{16,24},{24,0},{9,17},{17,25},{25,1},{10,18},{18,26},{26,2}... | collective-permute-start | bytes 393224 | tf_op jit(solution)/shard_map/ppermute | solution.py:378
  30.8 1.9 %collective-permute-start.7 = (bf16[2,32,1024]{2,1,0:T(8,128)(2,1)S(1)}, bf16[2,32,1024]{2,1,0:T(8,128)(2,1)S(1)}, u32[]{:S(2)}, u32[]{:S(2)}) collective-permute-start(bf16[2,32,1024]{2,1,0:T(8,128)(2,1)S(1)} %get-tuple-element.37), channel_id=1, source_target_pairs={{8,24},{16,0},{24,8},{9,25},{17,1},{25,9},{10,26},{18,2},{26,10},{... | collective-permute-start | bytes 393224 | tf_op jit(solution)/shard_map/ppermute | solution.py:378
  32.8 1.9 %collective-permute-start.8 = (bf16[2,32,1024]{2,1,0:T(8,128)(2,1)S(1)}, bf16[2,32,1024]{2,1,0:T(8,128)(2,1)S(1)}, u32[]{:S(2)}, u32[]{:S(2)}) collective-permute-start(bf16[2,32,1024]{2,1,0:T(8,128)(2,1)S(1)} %get-tuple-element.38), channel_id=1, source_target_pairs={{8,0},{16,8},{24,16},{9,1},{17,9},{25,17},{10,2},{18,10},{26,18},{... | collective-permute-start | bytes 393224 | tf_op jit(solution)/shard_map/ppermute | solution.py:378
  34.7 0.0 collective-permute-done.6.refs_1_
  34.7 3.7 %collective-permute-done.7.refs_2_ = bf16[2,32,1024]{2,1,0:T(8,128)(2,1)S(1)} collective-permute-done((bf16[2,32,1024]{2,1,0:T(8,128)(2,1)S(1)}, bf16[2,32,1024]{2,1,0:T(8,128)(2,1)S(1)}, u32[]{:S(2)}, u32[]{:S(2)}) %collective-permute-start.7) | collective-permute-done | bytes 131104 | tf_op jit(solution)/shard_map/ppermute | solution.py:378
  38.4 2.8 %collective-permute-done.8.refs_3_ = bf16[2,32,1024]{2,1,0:T(8,128)(2,1)S(1)} collective-permute-done((bf16[2,32,1024]{2,1,0:T(8,128)(2,1)S(1)}, bf16[2,32,1024]{2,1,0:T(8,128)(2,1)S(1)}, u32[]{:S(2)}, u32[]{:S(2)}) %collective-permute-start.8) | collective-permute-done | bytes 131104 | tf_op jit(solution)/shard_map/ppermute | solution.py:378
  41.2 0.8 %shard_map.104 = bf16[1,3,2,32,1024]{4,3,2,1,0:T(8,128)(2,1)} custom-call(bf16[2,32,1024]{2,1,0:T(8,128)(2,1)S(1)} %get-tuple-element.35.refs_0_, bf16[2,32,1024]{2,1,0:T(8,128)(2,1)S(1)} %collective-permute-done.6.refs_1_, bf16[2,32,1024]{2,1,0:T(8,128)(2,1)S(1)} %collective-permute-done.7.refs_2_, bf16[2,32,1024]{2,1,0:T(8,128)(2,1)S(1)} %collective-permute-done.8.refs_3_), custom_call_target="tpu_custom_call" | custom-call | bytes 1000000 | tf_op jit(solution)/shard_map/pallas_call | solution.py:461
  (1 shorter events, 0.0 us)
Async XLA Ops:
  2.0 4.4 %copy-start = (bf16[2,32,1024]{2,1,0:T(8,128)(2,1)S(1)}, bf16[2,32,1024]{2,1,0:T(8,128)(2,1)}, u32[]{:S(2)}) copy-start(bf16[2,32,1024]{2,1,0:T(8,128)(2,1)} %get-tuple-element.23.incident) | copy-start | bytes 393220
  2.0 10.8 %all-to-all-start = ((bf16[4,32,1280]{2,1,0:T(8,128)(2,1)}), bf16[4,32,1280]{2,1,0:T(8,128)(2,1)S(1)}, u32[]{:S(2)}, u32[]{:S(2)}) async-start(bf16[4,32,1280]{2,1,0:T(8,128)(2,1)} %get-tuple-element.22), calls=%async_computation | async-start | bytes 655360 | tf_op jit(solution)/shard_map/all_to_all | solution.py:429
  6.4 16.4 %copy-start.1 = (bf16[256,256]{1,0:T(8,128)(2,1)S(1)}, bf16[256,256]{1,0:T(8,128)(2,1)}, u32[]{:S(2)}) copy-start(bf16[256,256]{1,0:T(8,128)(2,1)} %constant.6.clone.right_tab) | copy-start | bytes 393220
  6.4 16.4 %copy-start.2 = (bf16[256,256]{1,0:T(8,128)(2,1)S(1)}, bf16[256,256]{1,0:T(8,128)(2,1)}, u32[]{:S(2)}) copy-start(bf16[256,256]{1,0:T(8,128)(2,1)} %constant.7.clone.left_tab) | copy-start | bytes 393220
  6.4 6.4 %collective-permute-start = (bf16[64,1024]{1,0:T(8,128)(2,1)S(1)}, bf16[64,1024]{1,0:T(8,128)(2,1)S(1)}, u32[]{:S(2)}, u32[]{:S(2)}) collective-permute-start(bf16[64,1024]{1,0:T(8,128)(2,1)S(1)} %bitcast.1), channel_id=1, source_target_pairs={{1,2},{3,4},{5,6},{2,1},{4,3},{6,5},{9,10},{11,12},{13,14},{10,9},... | collective-permute-start | bytes 393224 | tf_op jit(solution)/shard_map/ppermute | solution.py:365
  12.9 9.9 %collective-permute-start.1 = (bf16[208,1152]{1,0:T(8,128)(2,1)S(1)}, bf16[208,1152]{1,0:T(8,128)(2,1)S(1)}, u32[]{:S(2)}, u32[]{:S(2)}) collective-permute-start(bf16[208,1152]{1,0:T(8,128)(2,1)S(1)} %get-tuple-element.24), channel_id=1, source_target_pairs={{0,1},{2,3},{4,5},{6,7},{1,0},{3,2},{5,4},{7,6},{8,9},{10,11},{12,... | collective-permute-start | bytes 1437704 | tf_op jit(solution)/shard_map/ppermute | solution.py:365
  13.1 9.7 %collective-permute-start.5 = (bf16[64,1024]{1,0:T(8,128)(2,1)S(1)}, bf16[64,1024]{1,0:T(8,128)(2,1)S(1)}, u32[]{:S(2)}, u32[]{:S(2)}) collective-permute-start(bf16[64,1024]{1,0:T(8,128)(2,1)S(1)} %bitcast.2), channel_id=1, source_target_pairs={{0,2},{2,4},{4,6},{3,1},{5,3},{7,5},{8,10},{10,12},{12,14},{11,9},... | collective-permute-start | bytes 393224 | tf_op jit(solution)/shard_map/ppermute | solution.py:372
  16.5 8.1 %collective-permute-start.2 = (bf16[80,1152]{1,0:T(8,128)(2,1)S(1)}, bf16[80,1152]{1,0:T(8,128)(2,1)S(1)}, u32[]{:S(2)}, u32[]{:S(2)}) collective-permute-start(bf16[80,1152]{1,0:T(8,128)(2,1)S(1)} %get-tuple-element.25), channel_id=1, source_target_pairs={{1,2},{3,4},{5,6},{2,1},{4,3},{6,5},{9,10},{11,12},{13,14},{10,9},... | collective-permute-start | bytes 552968 | tf_op jit(solution)/shard_map/ppermute | solution.py:365
  18.5 5.5 %collective-permute-start.3 = (bf16[16,1152]{1,0:T(8,128)(2,1)S(1)}, bf16[16,1152]{1,0:T(8,128)(2,1)S(1)}, u32[]{:S(2)}, u32[]{:S(2)}) collective-permute-start(bf16[16,1152]{1,0:T(8,128)(2,1)S(1)} %get-tuple-element.26), channel_id=1, source_target_pairs={{0,2},{1,3},{4,6},{5,7},{2,0},{3,1},{6,4},{7,5},{8,10},{9,11},{12,... | collective-permute-start | bytes 110600 | tf_op jit(solution)/shard_map/ppermute | solution.py:365
  18.6 6.1 %copy-start.3 = (bf16[192,192]{1,0:T(8,128)(2,1)S(1)}, bf16[192,192]{1,0:T(8,128)(2,1)}, u32[]{:S(2)}) copy-start(bf16[192,192]{1,0:T(8,128)(2,1)} %constant.8.clone.left_tab) | copy-start | bytes 221188
  18.6 6.1 %collective-permute-start.4 = (bf16[16,1152]{1,0:T(8,128)(2,1)S(1)}, bf16[16,1152]{1,0:T(8,128)(2,1)S(1)}, u32[]{:S(2)}, u32[]{:S(2)}) collective-permute-start(bf16[16,1152]{1,0:T(8,128)(2,1)S(1)} %get-tuple-element.27), channel_id=1, source_target_pairs={{2,4},{3,5},{4,2},{5,3},{10,12},{11,13},{12,10},{13,11},{18,20},{1... | collective-permute-start | bytes 110600 | tf_op jit(solution)/shard_map/ppermute | solution.py:365
  27.4 7.2 %collective-permute-start.6 = (bf16[2,32,1024]{2,1,0:T(8,128)(2,1)S(1)}, bf16[2,32,1024]{2,1,0:T(8,128)(2,1)S(1)}, u32[]{:S(2)}, u32[]{:S(2)}) collective-permute-start(bf16[2,32,1024]{2,1,0:T(8,128)(2,1)S(1)} %get-tuple-element.36), channel_id=1, source_target_pairs={{8,16},{16,24},{24,0},{9,17},{17,25},{25,1},{10,18},{18,26},{26,2}... | collective-permute-start | bytes 393224 | tf_op jit(solution)/shard_map/ppermute | solution.py:378
  30.8 7.5 %collective-permute-start.7 = (bf16[2,32,1024]{2,1,0:T(8,128)(2,1)S(1)}, bf16[2,32,1024]{2,1,0:T(8,128)(2,1)S(1)}, u32[]{:S(2)}, u32[]{:S(2)}) collective-permute-start(bf16[2,32,1024]{2,1,0:T(8,128)(2,1)S(1)} %get-tuple-element.37), channel_id=1, source_target_pairs={{8,24},{16,0},{24,8},{9,25},{17,1},{25,9},{10,26},{18,2},{26,10},{... | collective-permute-start | bytes 393224 | tf_op jit(solution)/shard_map/ppermute | solution.py:378
  32.8 8.4 %collective-permute-start.8 = (bf16[2,32,1024]{2,1,0:T(8,128)(2,1)S(1)}, bf16[2,32,1024]{2,1,0:T(8,128)(2,1)S(1)}, u32[]{:S(2)}, u32[]{:S(2)}) collective-permute-start(bf16[2,32,1024]{2,1,0:T(8,128)(2,1)S(1)} %get-tuple-element.38), channel_id=1, source_target_pairs={{8,0},{16,8},{24,16},{9,1},{17,9},{25,17},{10,2},{18,10},{26,18},{... | collective-permute-start | bytes 393224 | tf_op jit(solution)/shard_map/ppermute | solution.py:378

commit v5 on v4

--- a/solution.py
+++ b/solution.py
@@ -124,7 +124,7 @@
     picked.wait()
 
 
-def halo_kernel(own, incident, beyond, in_chip, cross, far_even, far_odd):
+def halo_kernel(own, incident, beyond, distant, in_chip, cross, far_even, far_odd):
     band = lax.axis_index("rows")
     core = band % 2
     odd = (band // 2) % 2
@@ -283,8 +283,7 @@
 def chain_kernel(
     in_chip, cross, far_even, far_odd, left_tab, right_tab, first, stereo, clear, col_mats, *rest
 ):
-    row_mats, outs, field = rest[: LAYERS - 1], rest[LAYERS - 1 : -1], rest[-1]
-    depth = lax.axis_index("depth")
+    row_mats, (out, field) = rest[: LAYERS - 1], rest[LAYERS - 1 :]
     low_near, high_near, low_far, high_far = ordered(in_chip, cross, far_even, far_odd)
     pieces = [
         low_far,
@@ -335,27 +334,8 @@
                 added = jnp.concatenate(pieces, axis=0)
                 value = passing[:, lanes] * columned[span, within] + added
                 field[part, :height, lanes] = value.astype(jnp.bfloat16)
-        for hop, out in enumerate(outs):
-
-            @pl.when((depth + hop) % LAYERS == layer)
-            def keep(out=out, side=side):
-                for part in range(2):
-                    out[part] = field[part, side : side + BAND]
-
-
-def home_kernel(*refs):
-    arrived, out, sems = refs[:LAYERS], refs[LAYERS], refs[LAYERS + 1]
-    depth = lax.axis_index("depth")
-    for colour in range(COLORS):
-        source = colour + LAYERS - COLORS
-        for hop in range(LAYERS):
-
-            @pl.when((source + hop) % LAYERS == depth)
-            def begin(hop=hop, colour=colour):
-                pltpu.make_async_copy(arrived[hop], out.at[0, colour], sems.at[colour]).start()
-
-    for colour in range(COLORS):
-        pltpu.make_async_copy(arrived[0], out.at[0, colour], sems.at[colour]).wait()
+        for part in range(2):
+            out[layer, part] = field[part, side : side + BAND]
 
 
 def exchanged(value, axis, by, phase):
@@ -370,12 +350,6 @@
     pairs = [(i, i + 2) for i in range(0, count - 2, 2)]
     pairs += [(i, i - 2) for i in range(3, count, 2)]
     return lax.ppermute(value, "rows", pairs)
-
-
-def sent_home(value, hop):
-    first = LAYERS - COLORS
-    pairs = [(i, (i + hop) % LAYERS) for i in range(first, LAYERS)]
-    return lax.ppermute(value, "depth", pairs)
 
 
 def neighbours(sent):
@@ -387,11 +361,8 @@
     return in_chip, cross, far_even, far_odd
 
 
-def call(
-    kernel, out_shape, in_specs, scratch=(), flops=0, moved=10**6, limit=VMEM_LIMIT,
-    out_space=pltpu.VMEM,
-):
-    vmem = pl.BlockSpec(memory_space=out_space)
+def call(kernel, out_shape, in_specs, scratch=(), flops=0, moved=10**6, limit=VMEM_LIMIT):
+    vmem = pl.BlockSpec(memory_space=pltpu.VMEM)
     many = isinstance(out_shape, (tuple, list))
     return pl.pallas_call(
         kernel,
@@ -432,7 +403,9 @@
     chip = shaped((NEAR + 4 * BAND, HALO_W), bf16)
     near = shaped((NEAR, HALO_W), bf16)
     far = shaped((FAR, HALO_W), bf16)
-    halos = neighbours(call(halo_kernel, (chip, near, far, far), [vmem] * 3)(own, mine, cross_in))
+    halos = neighbours(
+        call(halo_kernel, (chip, near, far, far), [vmem] * 4)(own, mine, cross_in, far_in)
+    )
     right_tab = jnp.asarray(right_table())
     made = call(
         prepare_kernel,
@@ -448,23 +421,16 @@
         moved=3 * 10**6,
     )(own, mine, halos[0], cross_in, far_in, jnp.asarray(left_table(LANES)), right_tab)
     halo_rows = NEAR + FAR
-    results = call(
+    result = call(
         chain_kernel,
-        [shaped((2, BAND, COLS), bf16)] * LAYERS,
+        shaped((LAYERS, 2, BAND, COLS), bf16),
         [vmem] * (6 + len(made)),
         [pltpu.VMEM((2, layer_height(0), COLS), bf16)],
         flops=2 * 10**9,
         moved=3 * 10**6,
     )(*halos, jnp.asarray(left_table(halo_rows)), right_tab, *made)
-    arrived = [results[0]] + [sent_home(results[hop], hop) for hop in (2, 1, 3)]
-    arrived = [arrived[0], arrived[2], arrived[1], arrived[3]]
-    return call(
-        home_kernel,
-        shaped((1, COLORS, 2, BAND, COLS), bf16),
-        [vmem] * LAYERS,
-        [pltpu.SemaphoreType.DMA((COLORS,))],
-        out_space=pltpu.HBM,
-    )(*arrived)
+    gathered = lax.all_to_all(result, "depth", 0, 0, tiled=True)
+    return gathered[None, LAYERS - COLORS :]
 
 
 def solution(mesh):

time: 42.3 us -> 40.9 us (0.967)
  the two profiles are of different devices: /device:TPU:10 before, /device:TPU:0 now
where the time goes in v5:
time: 40.9 us; the launch traced here: 40.6 us
  starting transfers between devices  17.9 us (44%)
  blocking collectives  12.1 us (30%)
  Pallas kernels  5.62 us (14%)
  waiting for transfers between devices  4.1 us (10%)
  local copies, waits for them, and re-layouts  0.79 us (2%)
    all_to_all x1, blocking collectives, body(): gathered = lax.all_to_all(result, 'depth', 0, 0, tiled=True)  12.1 us
    ppermute x5, starting transfers between devices, exchanged(): return lax.ppermute(value, axis, pairs)  8.97 us
    all_to_all x1, starting transfers between devices, body(): own = lax.all_to_all(payload, 'depth', 0, 0, tiled=True)  5.31 us
    ppermute x1, starting transfers between devices, far_incident(): return lax.ppermute(value, 'rows', pairs)  3.62 us
    pallas_call x1, Pallas kernels, body(): call(chain_kernel, shaped((LAYERS, 2, BAND, COLS), bf16), [vmem] * (6 + l...  2.47 us
    ppermute x5, waiting for transfers between devices, exchanged(): return lax.ppermute(value, axis, pairs)  2.27 us
    pallas_call x1, Pallas kernels, body(): call(pack_kernel, (shaped((LAYERS, BAND, FULL_W), bf16), shaped(incident....  1.97 us
    ppermute x1, waiting for transfers between devices, far_incident(): return lax.ppermute(value, 'rows', pairs)  1.82 us
  transfers between devices with their start and end apart: 7, of which 2 were waited for; matrix products, arithmetic and copies ran while one was open for 0% of the time, Pallas kernels for 3%

profile of v5, /device:TPU:0, one launch (start us, length us, event | category | flops | bytes accessed | tf_op | source)
XLA Modules:
  0.0 40.6 jit_solution(9670127193153451173)
XLA Ops:
  0.0 2.0 %shard_map.100 = (bf16[4,32,1280]{2,1,0:T(8,128)(2,1)}, bf16[2,32,1024]{2,1,0:T(8,128)(2,1)}) custom-call(f32[1,3,32,1024]{3,2,1,0:T(8,128)} %light.1, s32[1,32,64]{2,1,0:T(8,128)} %edges.1, s32[1,2]{1,0:T(1,128)} %counts.1, s32[1,2,64]{2,1,0:T(2,128)} %listed.1, bf16[1,3,2,33]{3,2,1,0:T(2,128)(2,1)} %row_taps.1, bf16[1,3,2,127]{3,2,1,0:T(2,128)(2,1)} %col_taps.1, ...), custom_call_target="tpu_custom_call" | custom-call | flops 10000000 | bytes 1000000 | tf_op jit(solution)/shard_map/pallas_call | solution.py:391
  2.0 0.0 copy-start
  2.0 5.3 %all-to-all-start = ((bf16[4,32,1280]{2,1,0:T(8,128)(2,1)}), bf16[4,32,1280]{2,1,0:T(8,128)(2,1)S(1)}, u32[]{:S(2)}, u32[]{:S(2)}) async-start(bf16[4,32,1280]{2,1,0:T(8,128)(2,1)} %get-tuple-element.18), calls=%async_computation | async-start | bytes 655360 | tf_op jit(solution)/shard_map/all_to_all | solution.py:400
  7.3 0.0 copy-done
  7.3 0.0 copy-start.1
  7.3 0.0 copy-start.2
  7.3 3.6 %collective-permute-start.1 = (bf16[64,1024]{1,0:T(8,128)(2,1)S(1)}, bf16[64,1024]{1,0:T(8,128)(2,1)S(1)}, u32[]{:S(2)}, u32[]{:S(2)}) collective-permute-start(bf16[64,1024]{1,0:T(8,128)(2,1)S(1)} %bitcast.3), channel_id=1, source_target_pairs={{0,2},{2,4},{4,6},{3,1},{5,3},{7,5},{8,10},{10,12},{12,14},{11,9},... | collective-permute-start | bytes 393224 | tf_op jit(solution)/shard_map/ppermute | solution.py:352
  10.9 0.7 %collective-permute-start = (bf16[64,1024]{1,0:T(8,128)(2,1)S(1)}, bf16[64,1024]{1,0:T(8,128)(2,1)S(1)}, u32[]{:S(2)}, u32[]{:S(2)}) collective-permute-start(bf16[64,1024]{1,0:T(8,128)(2,1)S(1)} %bitcast.4), channel_id=1, source_target_pairs={{1,2},{3,4},{5,6},{2,1},{4,3},{6,5},{9,10},{11,12},{13,14},{10,9},... | collective-permute-start | bytes 393224 | tf_op jit(solution)/shard_map/ppermute | solution.py:345
  11.6 1.8 %collective-permute-done.1.distant.far = bf16[64,1024]{1,0:T(8,128)(2,1)S(1)} collective-permute-done((bf16[64,1024]{1,0:T(8,128)(2,1)S(1)}, bf16[64,1024]{1,0:T(8,128)(2,1)S(1)}, u32[]{:S(2)}, u32[]{:S(2)}) %collective-permute-start.1) | collective-permute-done | bytes 131104 | tf_op jit(solution)/shard_map/ppermute | solution.py:352
  13.4 0.0 collective-permute-done.beyond.cross
  13.4 0.0 all-to-all-done.own
  13.5 3.8 %collective-permute-start.2 = (bf16[208,1152]{1,0:T(8,128)(2,1)S(1)}, bf16[208,1152]{1,0:T(8,128)(2,1)S(1)}, u32[]{:S(2)}, u32[]{:S(2)}) collective-permute-start(bf16[208,1152]{1,0:T(8,128)(2,1)S(1)} %get-tuple-element.20), channel_id=1, source_target_pairs={{0,1},{2,3},{4,5},{6,7},{1,0},{3,2},{5,4},{7,6},{8,9},{10,11},{12,... | collective-permute-start | bytes 1437704 | tf_op jit(solution)/shard_map/ppermute | solution.py:345
  17.3 0.7 %collective-permute-start.3 = (bf16[80,1152]{1,0:T(8,128)(2,1)S(1)}, bf16[80,1152]{1,0:T(8,128)(2,1)S(1)}, u32[]{:S(2)}, u32[]{:S(2)}) collective-permute-start(bf16[80,1152]{1,0:T(8,128)(2,1)S(1)} %get-tuple-element.21), channel_id=1, source_target_pairs={{1,2},{3,4},{5,6},{2,1},{4,3},{6,5},{9,10},{11,12},{13,14},{10,9},... | collective-permute-start | bytes 552968 | tf_op jit(solution)/shard_map/ppermute | solution.py:345
  18.0 3.0 %collective-permute-start.4 = (bf16[16,1152]{1,0:T(8,128)(2,1)S(1)}, bf16[16,1152]{1,0:T(8,128)(2,1)S(1)}, u32[]{:S(2)}, u32[]{:S(2)}) collective-permute-start(bf16[16,1152]{1,0:T(8,128)(2,1)S(1)} %get-tuple-element.22), channel_id=1, source_target_pairs={{0,2},{1,3},{4,6},{5,7},{2,0},{3,1},{6,4},{7,5},{8,10},{9,11},{12,... | collective-permute-start | bytes 110600 | tf_op jit(solution)/shard_map/ppermute | solution.py:345
  21.0 0.0 copy-start.3
  21.0 0.8 %collective-permute-start.5 = (bf16[16,1152]{1,0:T(8,128)(2,1)S(1)}, bf16[16,1152]{1,0:T(8,128)(2,1)S(1)}, u32[]{:S(2)}, u32[]{:S(2)}) collective-permute-start(bf16[16,1152]{1,0:T(8,128)(2,1)S(1)} %get-tuple-element.23), channel_id=1, source_target_pairs={{2,4},{3,5},{4,2},{5,3},{10,12},{11,13},{12,10},{13,11},{18,20},{1... | collective-permute-start | bytes 110600 | tf_op jit(solution)/shard_map/ppermute | solution.py:345
  21.8 0.0 collective-permute-done.2.in_chip
  21.8 0.0 copy-done.1
  21.8 0.0 copy-done.2
  21.8 1.1 %shard_map.102 = (f32[1024,256]{1,0:T(8,128)S(1)}, f32[2,128,1024]{2,1,0:T(8,128)S(1)}, f32[128,1024]{1,0:T(8,128)S(1)}, bf16[3,256,512]{2,1,0:T(8,128)(2,1)S(1)...) custom-call(bf16[4,32,1280]{2,1,0:T(8,128)(2,1)S(1)} %all-to-all-done.own, ...), custom_call_target="tpu_custom_call" | custom-call | flops 1000000000 | bytes 3000000 | tf_op jit(solution)/shard_map/pallas_call | solution.py:410
  23.0 2.3 %collective-permute-done.4.far_even = bf16[16,1152]{1,0:T(8,128)(2,1)S(1)} collective-permute-done((bf16[16,1152]{1,0:T(8,128)(2,1)S(1)}, bf16[16,1152]{1,0:T(8,128)(2,1)S(1)}, u32[]{:S(2)}, u32[]{:S(2)}) %collective-permute-start.4) | collective-permute-done | bytes 36896 | tf_op jit(solution)/shard_map/ppermute | solution.py:345
  25.2 0.0 collective-permute-done.5.far_odd
  25.2 0.0 collective-permute-done.3.cross
  25.2 0.0 copy-done.3
  25.2 2.5 %shard_map.103 = bf16[4,2,32,1024]{3,2,1,0:T(8,128)(2,1)S(1)} custom-call(bf16[208,1152]{1,0:T(8,128)(2,1)S(1)} %collective-permute-done.2.in_chip, bf16[80,1152]{1,0:T(8,128)(2,1)S(1)} %collective-permute-done.3.cross, bf16[16,1152]{1,0:T(8,128)(2,1)S(1)} %collective-permute-done.4.far_even, bf16[16,1152]{1,0:T(8,128)(2,1)S(1)} %collective-permute-done.5.far_odd, ...), custom_call_target="tpu_custom_call" | custom-call | flops 2000000000 | bytes 3000000 | tf_op jit(solution)/shard_map/pallas_call | solution.py:424
  27.7 12.1 %all_to_all.10 = bf16[4,2,32,1024]{3,2,1,0:T(8,128)(2,1)S(1)} all-to-all(bf16[4,2,32,1024]{3,2,1,0:T(8,128)(2,1)S(1)} %shard_map.103), channel_id=1, replica_groups=mesh['depth'=4,'rows'=8] {'depth'}, dimensions={0} | all-to-all | bytes 1048576 | tf_op jit(solution)/shard_map/all_to_all | solution.py:432
  39.8 0.8 %slice_bitcast_fusion = bf16[1,3,2,32,1024]{4,3,2,1,0:T(8,128)(2,1)} fusion(bf16[4,2,32,1024]{3,2,1,0:T(8,128)(2,1)S(1)} %all_to_all.10), kind=kLoop, calls=%fused_computation | loop fusion | bytes 786432 | tf_op jit(solution)/shard_map/broadcast_in_dim | solution.py:433
  (1 shorter events, 0.0 us)
Async XLA Ops:
  2.0 5.3 %copy-start = (bf16[2,32,1024]{2,1,0:T(8,128)(2,1)S(1)}, bf16[2,32,1024]{2,1,0:T(8,128)(2,1)}, u32[]{:S(2)}) copy-start(bf16[2,32,1024]{2,1,0:T(8,128)(2,1)} %get-tuple-element.19.incident) | copy-start | bytes 393220
  2.0 11.4 %all-to-all-start = ((bf16[4,32,1280]{2,1,0:T(8,128)(2,1)}), bf16[4,32,1280]{2,1,0:T(8,128)(2,1)S(1)}, u32[]{:S(2)}, u32[]{:S(2)}) async-start(bf16[4,32,1280]{2,1,0:T(8,128)(2,1)} %get-tuple-element.18), calls=%async_computation | async-start | bytes 655360 | tf_op jit(solution)/shard_map/all_to_all | solution.py:400
  7.3 14.5 %copy-start.1 = (bf16[256,256]{1,0:T(8,128)(2,1)S(1)}, bf16[256,256]{1,0:T(8,128)(2,1)}, u32[]{:S(2)}) copy-start(bf16[256,256]{1,0:T(8,128)(2,1)} %constant.6.clone.right_tab) | copy-start | bytes 393220
  7.3 14.5 %copy-start.2 = (bf16[256,256]{1,0:T(8,128)(2,1)S(1)}, bf16[256,256]{1,0:T(8,128)(2,1)}, u32[]{:S(2)}) copy-start(bf16[256,256]{1,0:T(8,128)(2,1)} %constant.7.clone.left_tab) | copy-start | bytes 393220
  7.3 6.1 %collective-permute-start.1 = (bf16[64,1024]{1,0:T(8,128)(2,1)S(1)}, bf16[64,1024]{1,0:T(8,128)(2,1)S(1)}, u32[]{:S(2)}, u32[]{:S(2)}) collective-permute-start(bf16[64,1024]{1,0:T(8,128)(2,1)S(1)} %bitcast.3), channel_id=1, source_target_pairs={{0,2},{2,4},{4,6},{3,1},{5,3},{7,5},{8,10},{10,12},{12,14},{11,9},... | collective-permute-start | bytes 393224 | tf_op jit(solution)/shard_map/ppermute | solution.py:352
  10.9 2.5 %collective-permute-start = (bf16[64,1024]{1,0:T(8,128)(2,1)S(1)}, bf16[64,1024]{1,0:T(8,128)(2,1)S(1)}, u32[]{:S(2)}, u32[]{:S(2)}) collective-permute-start(bf16[64,1024]{1,0:T(8,128)(2,1)S(1)} %bitcast.4), channel_id=1, source_target_pairs={{1,2},{3,4},{5,6},{2,1},{4,3},{6,5},{9,10},{11,12},{13,14},{10,9},... | collective-permute-start | bytes 393224 | tf_op jit(solution)/shard_map/ppermute | solution.py:345
  13.5 8.3 %collective-permute-start.2 = (bf16[208,1152]{1,0:T(8,128)(2,1)S(1)}, bf16[208,1152]{1,0:T(8,128)(2,1)S(1)}, u32[]{:S(2)}, u32[]{:S(2)}) collective-permute-start(bf16[208,1152]{1,0:T(8,128)(2,1)S(1)} %get-tuple-element.20), channel_id=1, source_target_pairs={{0,1},{2,3},{4,5},{6,7},{1,0},{3,2},{5,4},{7,6},{8,9},{10,11},{12,... | collective-permute-start | bytes 1437704 | tf_op jit(solution)/shard_map/ppermute | solution.py:345
  17.3 7.9 %collective-permute-start.3 = (bf16[80,1152]{1,0:T(8,128)(2,1)S(1)}, bf16[80,1152]{1,0:T(8,128)(2,1)S(1)}, u32[]{:S(2)}, u32[]{:S(2)}) collective-permute-start(bf16[80,1152]{1,0:T(8,128)(2,1)S(1)} %get-tuple-element.21), channel_id=1, source_target_pairs={{1,2},{3,4},{5,6},{2,1},{4,3},{6,5},{9,10},{11,12},{13,14},{10,9},... | collective-permute-start | bytes 552968 | tf_op jit(solution)/shard_map/ppermute | solution.py:345
  18.0 7.3 %collective-permute-start.4 = (bf16[16,1152]{1,0:T(8,128)(2,1)S(1)}, bf16[16,1152]{1,0:T(8,128)(2,1)S(1)}, u32[]{:S(2)}, u32[]{:S(2)}) collective-permute-start(bf16[16,1152]{1,0:T(8,128)(2,1)S(1)} %get-tuple-element.22), channel_id=1, source_target_pairs={{0,2},{1,3},{4,6},{5,7},{2,0},{3,1},{6,4},{7,5},{8,10},{9,11},{12,... | collective-permute-start | bytes 110600 | tf_op jit(solution)/shard_map/ppermute | solution.py:345
  21.0 4.2 %copy-start.3 = (bf16[192,192]{1,0:T(8,128)(2,1)S(1)}, bf16[192,192]{1,0:T(8,128)(2,1)}, u32[]{:S(2)}) copy-start(bf16[192,192]{1,0:T(8,128)(2,1)} %constant.8.clone.left_tab) | copy-start | bytes 221188
  21.0 4.2 %collective-permute-start.5 = (bf16[16,1152]{1,0:T(8,128)(2,1)S(1)}, bf16[16,1152]{1,0:T(8,128)(2,1)S(1)}, u32[]{:S(2)}, u32[]{:S(2)}) collective-permute-start(bf16[16,1152]{1,0:T(8,128)(2,1)S(1)} %get-tuple-element.23), channel_id=1, source_target_pairs={{2,4},{3,5},{4,2},{5,3},{10,12},{11,13},{12,10},{13,11},{18,20},{1... | collective-permute-start | bytes 110600 | tf_op jit(solution)/shard_map/ppermute | solution.py:345

commit v6 on v5

--- a/solution.py
+++ b/solution.py
@@ -124,7 +124,7 @@
     picked.wait()
 
 
-def halo_kernel(own, incident, beyond, distant, in_chip, cross, far_even, far_odd):
+def halo_kernel(own, incident, in_chip, cross, far_even, far_odd):
     band = lax.axis_index("rows")
     core = band % 2
     odd = (band // 2) % 2
@@ -134,8 +134,7 @@
         near[BAND : 2 * BAND] = own[1, :, :HALO_W]
         near[2 * BAND : NEAR] = own[2, pl.ds(pl.multiple_of(start, KR), KR), :HALO_W]
     in_chip[NEAR : NEAR + BAND, :COLS] = incident[0]
-    in_chip[NEAR + BAND : NEAR + 2 * BAND, :COLS] = incident[1]
-    in_chip[NEAR + 2 * BAND :, :COLS] = beyond[...]
+    in_chip[NEAR + BAND :, :COLS] = incident[1]
     for far, start in ((far_even, (1 - odd) * last), (far_odd, odd * last)):
         far[...] = own[0, pl.ds(pl.multiple_of(start, KR), KR), :HALO_W]
 
@@ -144,7 +143,7 @@
     band = lax.axis_index("rows")
     even_core = band % 2 == 0
     even_chip = (band // 2) % 2 == 0
-    in_chip, cross = in_chip[:NEAR], cross[...]
+    in_chip, cross = in_chip[...], cross[...]
     far_even, far_odd = far_even[...], far_odd[...]
     return (
         jnp.where(even_core, cross, in_chip),
@@ -243,22 +242,13 @@
 
 
 def prepare_kernel(
-    own, incident, in_chip, cross, far, left_tab, right_tab,
+    own, incident, in_chip, cross, far_even, far_odd, left_tab, right_tab,
     first, stereo, clear, col_mats, *row_mats
 ):
-    even_core = lax.axis_index("rows") % 2 == 0
-    cross, far = cross[...], far[...]
-    partner = in_chip[NEAR : NEAR + 2 * BAND, :COLS]
-    beyond = in_chip[NEAR + 2 * BAND :, :COLS]
-    sides = (
-        jnp.where(even_core, far, beyond),
-        jnp.where(even_core, cross, partner),
-        jnp.where(even_core, partner, cross),
-        jnp.where(even_core, beyond, far),
-    )
+    sides = ordered(in_chip[NEAR:, :COLS], cross, far_even, far_odd)
     extended = []
     for part in range(2):
-        low_far, low_near, high_near, high_far = (
+        low_near, high_near, low_far, high_far = (
             side[part * BAND : (part + 1) * BAND] for side in sides
         )
         pieces = [low_far, low_near, incident[part], high_near, high_far]
@@ -284,7 +274,7 @@
     in_chip, cross, far_even, far_odd, left_tab, right_tab, first, stereo, clear, col_mats, *rest
 ):
     row_mats, (out, field) = rest[: LAYERS - 1], rest[LAYERS - 1 :]
-    low_near, high_near, low_far, high_far = ordered(in_chip, cross, far_even, far_odd)
+    low_near, high_near, low_far, high_far = ordered(in_chip[:NEAR], cross, far_even, far_odd)
     pieces = [
         low_far,
         low_near[0:BAND],
@@ -345,13 +335,6 @@
     return lax.ppermute(value, axis, pairs)
 
 
-def far_incident(value):
-    count = lax.axis_size("rows")
-    pairs = [(i, i + 2) for i in range(0, count - 2, 2)]
-    pairs += [(i, i - 2) for i in range(3, count, 2)]
-    return lax.ppermute(value, "rows", pairs)
-
-
 def neighbours(sent):
     in_chip, cross, far_even, far_odd = sent
     in_chip = exchanged(in_chip, "rows", 1, 0)
@@ -399,13 +382,11 @@
     flat = mine.reshape(2 * BAND, COLS)
     own = lax.all_to_all(payload, "depth", 0, 0, tiled=True)
     cross_in = exchanged(flat, "rows", 1, 1)
-    far_in = far_incident(flat)
-    chip = shaped((NEAR + 4 * BAND, HALO_W), bf16)
+    far_in = [exchanged(flat, "rows", 2, phase) for phase in range(2)]
+    chip = shaped((NEAR + 2 * BAND, HALO_W), bf16)
     near = shaped((NEAR, HALO_W), bf16)
     far = shaped((FAR, HALO_W), bf16)
-    halos = neighbours(
-        call(halo_kernel, (chip, near, far, far), [vmem] * 4)(own, mine, cross_in, far_in)
-    )
+    halos = neighbours(call(halo_kernel, (chip, near, far, far), [vmem] * 2)(own, mine))
     right_tab = jnp.asarray(right_table())
     made = call(
         prepare_kernel,
@@ -416,10 +397,10 @@
             shaped((LAYERS - 1, 2 * LANES, 4 * LANES), bf16),
         ]
         + [shaped((2 * block_height(layer), 2 * LANES), bf16) for layer in range(1, LAYERS)],
-        [vmem] * 7,
+        [vmem] * 8,
         flops=10**9,
         moved=3 * 10**6,
-    )(own, mine, halos[0], cross_in, far_in, jnp.asarray(left_table(LANES)), right_tab)
+    )(own, mine, halos[0], cross_in, *far_in, jnp.asarray(left_table(LANES)), right_tab)
     halo_rows = NEAR + FAR
     result = call(
         chain_kernel,

time: 40.9 us -> 43.8 us (1.071)
  blocking collectives: 12.1 us -> 22.7 us
  starting transfers between devices: 17.9 us -> 11.6 us
  waiting for transfers between devices: 4.1 us -> 2.24 us
    all_to_all x0 -> x1, blocking collectives: none -> 11.9 us  [body(): own = lax.all_to_all(payload, 'depth', 0, 0, tiled=True)]
    all_to_all x1 -> x0, starting transfers between devices: 5.31 us -> none  [body(): own = lax.all_to_all(payload, 'depth', 0, 0, tiled=True)]
    ppermute x1 -> x0, starting transfers between devices: 3.62 us -> none  [far_incident(): return lax.ppermute(value, 'rows', pairs)]
    ppermute x5 -> x7, starting transfers between devices: 8.97 us -> 11.6 us  [exchanged(): return lax.ppermute(value, axis, pairs)]
    ppermute x1 -> x0, waiting for transfers between devices: 1.82 us -> none  [far_incident(): return lax.ppermute(value, 'rows', pairs)]
    all_to_all x1, blocking collectives: 12.1 us -> 10.8 us  [body(): gathered = lax.all_to_all(result, 'depth', 0, 0, tiled=True)]
    ppermute x5 -> x7, waiting for transfers between devices: 2.27 us -> 2.24 us  [exchanged(): return lax.ppermute(value, axis, pairs)]
  transfers between devices with their start and end apart: 7 -> 7, of which waited for: 2 -> 1; matrix products, arithmetic and copies ran while one was open for 0% -> 0% of each run, Pallas kernels for 3% -> 3%
where the time goes in v6:
time: 43.8 us; the launch traced here: 43.1 us
  blocking collectives  22.7 us (52%)
  starting transfers between devices  11.6 us (26%)
  Pallas kernels  5.66 us (13%)
  waiting for transfers between devices  2.24 us (5%)
  local copies, waits for them, and re-layouts  0.79 us (2%)
    all_to_all x1, blocking collectives, body(): own = lax.all_to_all(payload, 'depth', 0, 0, tiled=True)  11.9 us
    ppermute x7, starting transfers between devices, exchanged(): return lax.ppermute(value, axis, pairs)  11.6 us
    all_to_all x1, blocking collectives, body(): gathered = lax.all_to_all(result, 'depth', 0, 0, tiled=True)  10.8 us
    pallas_call x1, Pallas kernels, body(): call(chain_kernel, shaped((LAYERS, 2, BAND, COLS), bf16), [vmem] * (6 + l...  2.51 us
    ppermute x7, waiting for transfers between devices, exchanged(): return lax.ppermute(value, axis, pairs)  2.24 us
    pallas_call x1, Pallas kernels, body(): call(pack_kernel, (shaped((LAYERS, BAND, FULL_W), bf16), shaped(incident....  1.97 us
    pallas_call x1, Pallas kernels, body(): call(prepare_kernel, [shaped((TILES * layer_height(0), 2 * LANES), f32),...  1.14 us
  transfers between devices with their start and end apart: 7, of which 1 were waited for; matrix products, arithmetic and copies ran while one was open for 0% of the time, Pallas kernels for 3%

profile of v6, /device:TPU:0, one launch (start us, length us, event | category | flops | bytes accessed | tf_op | source)
XLA Modules:
  0.0 43.1 jit_solution(7611824800641127763)
XLA Ops:
  0.0 2.0 %shard_map.100 = (bf16[4,32,1280]{2,1,0:T(8,128)(2,1)}, bf16[2,32,1024]{2,1,0:T(8,128)(2,1)}) custom-call(f32[1,3,32,1024]{3,2,1,0:T(8,128)} %light.1, s32[1,32,64]{2,1,0:T(8,128)} %edges.1, s32[1,2]{1,0:T(1,128)} %counts.1, s32[1,2,64]{2,1,0:T(2,128)} %listed.1, bf16[1,3,2,33]{3,2,1,0:T(2,128)(2,1)} %row_taps.1, bf16[1,3,2,127]{3,2,1,0:T(2,128)(2,1)} %col_taps.1, ...), custom_call_target="tpu_custom_call" | custom-call | flops 10000000 | bytes 1000000 | tf_op jit(solution)/shard_map/pallas_call | solution.py:374
  2.0 0.0 copy-start
  2.0 11.9 %all_to_all.10.own = bf16[4,32,1280]{2,1,0:T(8,128)(2,1)S(1)} all-to-all(bf16[4,32,1280]{2,1,0:T(8,128)(2,1)} %get-tuple-element.18), channel_id=1, replica_groups=mesh['depth'=4,'rows'=8] {'depth'}, dimensions={0} | all-to-all | bytes 655360 | tf_op jit(solution)/shard_map/all_to_all | solution.py:383
  13.9 0.0 copy-done
  13.9 0.0 copy-start.1
  13.9 0.0 copy-start.2
  13.9 0.1 collective-permute-start
  14.0 0.7 %collective-permute-start.6 = (bf16[64,1024]{1,0:T(8,128)(2,1)S(1)}, bf16[64,1024]{1,0:T(8,128)(2,1)S(1)}, u32[]{:S(2)}, u32[]{:S(2)}) collective-permute-start(bf16[64,1024]{1,0:T(8,128)(2,1)S(1)} %bitcast.3), channel_id=1, source_target_pairs={{2,4},{3,5},{4,2},{5,3},{10,12},{11,13},{12,10},{13,11},{18,20},{1... | collective-permute-start | bytes 393224 | tf_op jit(solution)/shard_map/ppermute | solution.py:335
  14.7 4.5 %collective-permute-start.5 = (bf16[64,1024]{1,0:T(8,128)(2,1)S(1)}, bf16[64,1024]{1,0:T(8,128)(2,1)S(1)}, u32[]{:S(2)}, u32[]{:S(2)}) collective-permute-start(bf16[64,1024]{1,0:T(8,128)(2,1)S(1)} %bitcast.4), channel_id=1, source_target_pairs={{0,2},{1,3},{4,6},{5,7},{2,0},{3,1},{6,4},{7,5},{8,10},{9,11},{12,... | collective-permute-start | bytes 393224 | tf_op jit(solution)/shard_map/ppermute | solution.py:335
  19.2 0.7 %collective-permute-start.4 = (bf16[64,1024]{1,0:T(8,128)(2,1)S(1)}, bf16[64,1024]{1,0:T(8,128)(2,1)S(1)}, u32[]{:S(2)}, u32[]{:S(2)}) collective-permute-start(bf16[64,1024]{1,0:T(8,128)(2,1)S(1)} %bitcast.5), channel_id=1, source_target_pairs={{1,2},{3,4},{5,6},{2,1},{4,3},{6,5},{9,10},{11,12},{13,14},{10,9},... | collective-permute-start | bytes 393224 | tf_op jit(solution)/shard_map/ppermute | solution.py:335
  19.8 0.7 %collective-permute-start.1 = (bf16[80,1152]{1,0:T(8,128)(2,1)S(1)}, bf16[80,1152]{1,0:T(8,128)(2,1)S(1)}, u32[]{:S(2)}, u32[]{:S(2)}) collective-permute-start(bf16[80,1152]{1,0:T(8,128)(2,1)S(1)} %get-tuple-element.21), channel_id=1, source_target_pairs={{1,2},{3,4},{5,6},{2,1},{4,3},{6,5},{9,10},{11,12},{13,14},{10,9},... | collective-permute-start | bytes 552968 | tf_op jit(solution)/shard_map/ppermute | solution.py:335
  20.5 0.0 collective-permute-done.6.far_odd
  20.5 4.3 %collective-permute-start.2 = (bf16[16,1152]{1,0:T(8,128)(2,1)S(1)}, bf16[16,1152]{1,0:T(8,128)(2,1)S(1)}, u32[]{:S(2)}, u32[]{:S(2)}) collective-permute-start(bf16[16,1152]{1,0:T(8,128)(2,1)S(1)} %get-tuple-element.22), channel_id=1, source_target_pairs={{0,2},{1,3},{4,6},{5,7},{2,0},{3,1},{6,4},{7,5},{8,10},{9,11},{12,... | collective-permute-start | bytes 110600 | tf_op jit(solution)/shard_map/ppermute | solution.py:335
  24.8 0.0 collective-permute-done.5.far_even
  24.8 0.0 copy-start.3
  24.8 0.8 %collective-permute-start.3 = (bf16[16,1152]{1,0:T(8,128)(2,1)S(1)}, bf16[16,1152]{1,0:T(8,128)(2,1)S(1)}, u32[]{:S(2)}, u32[]{:S(2)}) collective-permute-start(bf16[16,1152]{1,0:T(8,128)(2,1)S(1)} %get-tuple-element.23), channel_id=1, source_target_pairs={{2,4},{3,5},{4,2},{5,3},{10,12},{11,13},{12,10},{13,11},{18,20},{1... | collective-permute-start | bytes 110600 | tf_op jit(solution)/shard_map/ppermute | solution.py:335
  25.6 0.0 collective-permute-done.4.cross
  25.6 0.0 collective-permute-done.in_chip
  25.6 0.0 copy-done.1
  25.7 0.0 copy-done.2
  25.7 1.1 %shard_map.102 = (f32[1024,256]{1,0:T(8,128)S(1)}, f32[2,128,1024]{2,1,0:T(8,128)S(1)}, f32[128,1024]{1,0:T(8,128)S(1)}, bf16[3,256,512]{2,1,0:T(8,128)(2,1)S(1)...) custom-call(bf16[4,32,1280]{2,1,0:T(8,128)(2,1)S(1)} %all_to_all.10.own, ...), custom_call_target="tpu_custom_call" | custom-call | flops 1000000000 | bytes 3000000 | tf_op jit(solution)/shard_map/pallas_call | solution.py:391
  26.8 2.2 %collective-permute-done.2.far_even = bf16[16,1152]{1,0:T(8,128)(2,1)S(1)} collective-permute-done((bf16[16,1152]{1,0:T(8,128)(2,1)S(1)}, bf16[16,1152]{1,0:T(8,128)(2,1)S(1)}, u32[]{:S(2)}, u32[]{:S(2)}) %collective-permute-start.2) | collective-permute-done | bytes 36896 | tf_op jit(solution)/shard_map/ppermute | solution.py:335
  29.0 0.0 collective-permute-done.3.far_odd
  29.0 0.0 collective-permute-done.1.cross
  29.0 0.0 copy-done.3
  29.0 2.5 %shard_map.103 = bf16[4,2,32,1024]{3,2,1,0:T(8,128)(2,1)S(1)} custom-call(bf16[144,1152]{1,0:T(8,128)(2,1)S(1)} %collective-permute-done.in_chip, bf16[80,1152]{1,0:T(8,128)(2,1)S(1)} %collective-permute-done.1.cross, bf16[16,1152]{1,0:T(8,128)(2,1)S(1)} %collective-permute-done.2.far_even, bf16[16,1152]{1,0:T(8,128)(2,1)S(1)} %collective-permute-done.3.far_odd, ...), custom_call_target="tpu_custom_call" | custom-call | flops 2000000000 | bytes 3000000 | tf_op jit(solution)/shard_map/pallas_call | solution.py:405
  31.6 10.8 %all_to_all.11 = bf16[4,2,32,1024]{3,2,1,0:T(8,128)(2,1)S(1)} all-to-all(bf16[4,2,32,1024]{3,2,1,0:T(8,128)(2,1)S(1)} %shard_map.103), channel_id=1, replica_groups=mesh['depth'=4,'rows'=8] {'depth'}, dimensions={0} | all-to-all | bytes 1048576 | tf_op jit(solution)/shard_map/all_to_all | solution.py:413
  42.3 0.8 %slice_bitcast_fusion = bf16[1,3,2,32,1024]{4,3,2,1,0:T(8,128)(2,1)} fusion(bf16[4,2,32,1024]{3,2,1,0:T(8,128)(2,1)S(1)} %all_to_all.11), kind=kLoop, calls=%fused_computation | loop fusion | bytes 786432 | tf_op jit(solution)/shard_map/broadcast_in_dim | solution.py:414
  (1 shorter events, 0.0 us)
Async XLA Ops:
  2.0 11.9 %copy-start = (bf16[2,32,1024]{2,1,0:T(8,128)(2,1)S(1)}, bf16[2,32,1024]{2,1,0:T(8,128)(2,1)}, u32[]{:S(2)}) copy-start(bf16[2,32,1024]{2,1,0:T(8,128)(2,1)} %get-tuple-element.19.incident) | copy-start | bytes 393220
  13.9 11.8 %copy-start.1 = (bf16[256,256]{1,0:T(8,128)(2,1)S(1)}, bf16[256,256]{1,0:T(8,128)(2,1)}, u32[]{:S(2)}) copy-start(bf16[256,256]{1,0:T(8,128)(2,1)} %constant.6.clone.right_tab) | copy-start | bytes 393220
  13.9 11.8 %copy-start.2 = (bf16[256,256]{1,0:T(8,128)(2,1)S(1)}, bf16[256,256]{1,0:T(8,128)(2,1)}, u32[]{:S(2)}) copy-start(bf16[256,256]{1,0:T(8,128)(2,1)} %constant.7.clone.left_tab) | copy-start | bytes 393220
  13.9 11.7 %collective-permute-start = (bf16[144,1152]{1,0:T(8,128)(2,1)S(1)}, bf16[144,1152]{1,0:T(8,128)(2,1)S(1)}, u32[]{:S(2)}, u32[]{:S(2)}) collective-permute-start(bf16[144,1152]{1,0:T(8,128)(2,1)S(1)} %get-tuple-element.20), channel_id=1, source_target_pairs={{0,1},{2,3},{4,5},{6,7},{1,0},{3,2},{5,4},{7,6},{8,9},{10,11},{12,... | collective-permute-start | bytes 995336 | tf_op jit(solution)/shard_map/ppermute | solution.py:335
  14.0 6.5 %collective-permute-start.6 = (bf16[64,1024]{1,0:T(8,128)(2,1)S(1)}, bf16[64,1024]{1,0:T(8,128)(2,1)S(1)}, u32[]{:S(2)}, u32[]{:S(2)}) collective-permute-start(bf16[64,1024]{1,0:T(8,128)(2,1)S(1)} %bitcast.3), channel_id=1, source_target_pairs={{2,4},{3,5},{4,2},{5,3},{10,12},{11,13},{12,10},{13,11},{18,20},{1... | collective-permute-start | bytes 393224 | tf_op jit(solution)/shard_map/ppermute | solution.py:335
  14.7 10.1 %collective-permute-start.5 = (bf16[64,1024]{1,0:T(8,128)(2,1)S(1)}, bf16[64,1024]{1,0:T(8,128)(2,1)S(1)}, u32[]{:S(2)}, u32[]{:S(2)}) collective-permute-start(bf16[64,1024]{1,0:T(8,128)(2,1)S(1)} %bitcast.4), channel_id=1, source_target_pairs={{0,2},{1,3},{4,6},{5,7},{2,0},{3,1},{6,4},{7,5},{8,10},{9,11},{12,... | collective-permute-start | bytes 393224 | tf_op jit(solution)/shard_map/ppermute | solution.py:335
  19.2 6.5 %collective-permute-start.4 = (bf16[64,1024]{1,0:T(8,128)(2,1)S(1)}, bf16[64,1024]{1,0:T(8,128)(2,1)S(1)}, u32[]{:S(2)}, u32[]{:S(2)}) collective-permute-start(bf16[64,1024]{1,0:T(8,128)(2,1)S(1)} %bitcast.5), channel_id=1, source_target_pairs={{1,2},{3,4},{5,6},{2,1},{4,3},{6,5},{9,10},{11,12},{13,14},{10,9},... | collective-permute-start | bytes 393224 | tf_op jit(solution)/shard_map/ppermute | solution.py:335
  19.8 9.2 %collective-permute-start.1 = (bf16[80,1152]{1,0:T(8,128)(2,1)S(1)}, bf16[80,1152]{1,0:T(8,128)(2,1)S(1)}, u32[]{:S(2)}, u32[]{:S(2)}) collective-permute-start(bf16[80,1152]{1,0:T(8,128)(2,1)S(1)} %get-tuple-element.21), channel_id=1, source_target_pairs={{1,2},{3,4},{5,6},{2,1},{4,3},{6,5},{9,10},{11,12},{13,14},{10,9},... | collective-permute-start | bytes 552968 | tf_op jit(solution)/shard_map/ppermute | solution.py:335
  20.5 8.5 %collective-permute-start.2 = (bf16[16,1152]{1,0:T(8,128)(2,1)S(1)}, bf16[16,1152]{1,0:T(8,128)(2,1)S(1)}, u32[]{:S(2)}, u32[]{:S(2)}) collective-permute-start(bf16[16,1152]{1,0:T(8,128)(2,1)S(1)} %get-tuple-element.22), channel_id=1, source_target_pairs={{0,2},{1,3},{4,6},{5,7},{2,0},{3,1},{6,4},{7,5},{8,10},{9,11},{12,... | collective-permute-start | bytes 110600 | tf_op jit(solution)/shard_map/ppermute | solution.py:335
  24.8 4.2 %copy-start.3 = (bf16[192,192]{1,0:T(8,128)(2,1)S(1)}, bf16[192,192]{1,0:T(8,128)(2,1)}, u32[]{:S(2)}) copy-start(bf16[192,192]{1,0:T(8,128)(2,1)} %constant.8.clone.left_tab) | copy-start | bytes 221188
  24.8 4.2 %collective-permute-start.3 = (bf16[16,1152]{1,0:T(8,128)(2,1)S(1)}, bf16[16,1152]{1,0:T(8,128)(2,1)S(1)}, u32[]{:S(2)}, u32[]{:S(2)}) collective-permute-start(bf16[16,1152]{1,0:T(8,128)(2,1)S(1)} %get-tuple-element.23), channel_id=1, source_target_pairs={{2,4},{3,5},{4,2},{5,3},{10,12},{11,13},{12,10},{13,11},{18,20},{1... | collective-permute-start | bytes 110600 | tf_op jit(solution)/shard_map/ppermute | solution.py:335

commit v7 on v6

--- a/solution.py
+++ b/solution.py
@@ -124,7 +124,8 @@
     picked.wait()
 
 
-def halo_kernel(own, incident, in_chip, cross, far_even, far_odd):
+def halo_kernel(own, incident, *rest):
+    in_chip, cross, far_even, far_odd = rest[-4:]
     band = lax.axis_index("rows")
     core = band % 2
     odd = (band // 2) % 2
@@ -386,7 +387,9 @@
     chip = shaped((NEAR + 2 * BAND, HALO_W), bf16)
     near = shaped((NEAR, HALO_W), bf16)
     far = shaped((FAR, HALO_W), bf16)
-    halos = neighbours(call(halo_kernel, (chip, near, far, far), [vmem] * 2)(own, mine))
+    halos = neighbours(
+        call(halo_kernel, (chip, near, far, far), [vmem] * 5)(own, mine, cross_in, *far_in)
+    )
     right_tab = jnp.asarray(right_table())
     made = call(
         prepare_kernel,

time: 43.8 us -> 41.2 us (0.941)
  blocking collectives: 22.7 us -> 11.8 us
  starting transfers between devices: 11.6 us -> 18 us
  waiting for transfers between devices: 2.24 us -> 4.58 us
    all_to_all x1 -> x0, blocking collectives: 11.9 us -> none  [body(): own = lax.all_to_all(payload, 'depth', 0, 0, tiled=True)]
    all_to_all x0 -> x1, starting transfers between devices: none -> 5.31 us  [body(): own = lax.all_to_all(payload, 'depth', 0, 0, tiled=True)]
    ppermute x7, waiting for transfers between devices: 2.24 us -> 4.58 us  [exchanged(): return lax.ppermute(value, axis, pairs)]
    ppermute x7, starting transfers between devices: 11.6 us -> 12.7 us  [exchanged(): return lax.ppermute(value, axis, pairs)]
    all_to_all x1, blocking collectives: 10.8 us -> 11.8 us  [body(): gathered = lax.all_to_all(result, 'depth', 0, 0, tiled=True)]
  transfers between devices with their start and end apart: 7 -> 8, of which waited for: 1 -> 2; matrix products, arithmetic and copies ran while one was open for 0% -> 0% of each run, Pallas kernels for 3% -> 3%
where the time goes in v7:
time: 41.2 us; the launch traced here: 40.9 us
  starting transfers between devices  18 us (44%)
  blocking collectives  11.8 us (29%)
  Pallas kernels  5.64 us (14%)
  waiting for transfers between devices  4.58 us (11%)
  local copies, waits for them, and re-layouts  0.79 us (2%)
    ppermute x7, starting transfers between devices, exchanged(): return lax.ppermute(value, axis, pairs)  12.7 us
    all_to_all x1, blocking collectives, body(): gathered = lax.all_to_all(result, 'depth', 0, 0, tiled=True)  11.8 us
    all_to_all x1, starting transfers between devices, body(): own = lax.all_to_all(payload, 'depth', 0, 0, tiled=True)  5.31 us
    ppermute x7, waiting for transfers between devices, exchanged(): return lax.ppermute(value, axis, pairs)  4.58 us
    pallas_call x1, Pallas kernels, body(): call(chain_kernel, shaped((LAYERS, 2, BAND, COLS), bf16), [vmem] * (6 + l...  2.48 us
    pallas_call x1, Pallas kernels, body(): call(pack_kernel, (shaped((LAYERS, BAND, FULL_W), bf16), shaped(incident....  1.98 us
    pallas_call x1, Pallas kernels, body(): call(prepare_kernel, [shaped((TILES * layer_height(0), 2 * LANES), f32),...  1.13 us
  transfers between devices with their start and end apart: 8, of which 2 were waited for; matrix products, arithmetic and copies ran while one was open for 0% of the time, Pallas kernels for 3%

profile of v7, /device:TPU:0, one launch (start us, length us, event | category | flops | bytes accessed | tf_op | source)
XLA Modules:
  0.0 40.9 jit_solution(9338580682878668734)
XLA Ops:
  0.0 2.0 %shard_map.100 = (bf16[4,32,1280]{2,1,0:T(8,128)(2,1)}, bf16[2,32,1024]{2,1,0:T(8,128)(2,1)}) custom-call(f32[1,3,32,1024]{3,2,1,0:T(8,128)} %light.1, s32[1,32,64]{2,1,0:T(8,128)} %edges.1, s32[1,2]{1,0:T(1,128)} %counts.1, s32[1,2,64]{2,1,0:T(2,128)} %listed.1, bf16[1,3,2,33]{3,2,1,0:T(2,128)(2,1)} %row_taps.1, bf16[1,3,2,127]{3,2,1,0:T(2,128)(2,1)} %col_taps.1, ...), custom_call_target="tpu_custom_call" | custom-call | flops 10000000 | bytes 1000000 | tf_op jit(solution)/shard_map/pallas_call | solution.py:375
  2.0 0.0 copy-start
  2.0 5.3 %all-to-all-start = ((bf16[4,32,1280]{2,1,0:T(8,128)(2,1)}), bf16[4,32,1280]{2,1,0:T(8,128)(2,1)S(1)}, u32[]{:S(2)}, u32[]{:S(2)}) async-start(bf16[4,32,1280]{2,1,0:T(8,128)(2,1)} %get-tuple-element.18), calls=%async_computation | async-start | bytes 655360 | tf_op jit(solution)/shard_map/all_to_all | solution.py:384
  7.3 0.0 copy-done
  7.3 0.0 copy-start.1
  7.3 0.0 copy-start.2
  7.3 0.8 %collective-permute-start.2 = (bf16[64,1024]{1,0:T(8,128)(2,1)S(1)}, bf16[64,1024]{1,0:T(8,128)(2,1)S(1)}, u32[]{:S(2)}, u32[]{:S(2)}) collective-permute-start(bf16[64,1024]{1,0:T(8,128)(2,1)S(1)} %bitcast.3), channel_id=1, source_target_pairs={{2,4},{3,5},{4,2},{5,3},{10,12},{11,13},{12,10},{13,11},{18,20},{1... | collective-permute-start | bytes 393224 | tf_op jit(solution)/shard_map/ppermute | solution.py:336
  8.1 4.5 %collective-permute-start.1 = (bf16[64,1024]{1,0:T(8,128)(2,1)S(1)}, bf16[64,1024]{1,0:T(8,128)(2,1)S(1)}, u32[]{:S(2)}, u32[]{:S(2)}) collective-permute-start(bf16[64,1024]{1,0:T(8,128)(2,1)S(1)} %bitcast.4), channel_id=1, source_target_pairs={{0,2},{1,3},{4,6},{5,7},{2,0},{3,1},{6,4},{7,5},{8,10},{9,11},{12,... | collective-permute-start | bytes 393224 | tf_op jit(solution)/shard_map/ppermute | solution.py:336
  12.6 0.7 %collective-permute-start = (bf16[64,1024]{1,0:T(8,128)(2,1)S(1)}, bf16[64,1024]{1,0:T(8,128)(2,1)S(1)}, u32[]{:S(2)}, u32[]{:S(2)}) collective-permute-start(bf16[64,1024]{1,0:T(8,128)(2,1)S(1)} %bitcast.5), channel_id=1, source_target_pairs={{1,2},{3,4},{5,6},{2,1},{4,3},{6,5},{9,10},{11,12},{13,14},{10,9},... | collective-permute-start | bytes 393224 | tf_op jit(solution)/shard_map/ppermute | solution.py:336
  13.3 0.0 collective-permute-done.2.rest_2_.far_odd
  13.3 2.3 %collective-permute-done.1.rest_1_.far_even = bf16[64,1024]{1,0:T(8,128)(2,1)S(1)} collective-permute-done((bf16[64,1024]{1,0:T(8,128)(2,1)S(1)}, bf16[64,1024]{1,0:T(8,128)(2,1)S(1)}, u32[]{:S(2)}, u32[]{:S(2)}) %collective-permute-start.1) | collective-permute-done | bytes 131104 | tf_op jit(solution)/shard_map/ppermute | solution.py:336
  15.6 0.0 collective-permute-done.rest_0_.cross
  15.6 0.0 all-to-all-done.own
  15.6 2.4 %collective-permute-start.3 = (bf16[144,1152]{1,0:T(8,128)(2,1)S(1)}, bf16[144,1152]{1,0:T(8,128)(2,1)S(1)}, u32[]{:S(2)}, u32[]{:S(2)}) collective-permute-start(bf16[144,1152]{1,0:T(8,128)(2,1)S(1)} %get-tuple-element.20), channel_id=1, source_target_pairs={{0,1},{2,3},{4,5},{6,7},{1,0},{3,2},{5,4},{7,6},{8,9},{10,11},{12,... | collective-permute-start | bytes 995336 | tf_op jit(solution)/shard_map/ppermute | solution.py:336
  18.0 0.7 %collective-permute-start.4 = (bf16[80,1152]{1,0:T(8,128)(2,1)S(1)}, bf16[80,1152]{1,0:T(8,128)(2,1)S(1)}, u32[]{:S(2)}, u32[]{:S(2)}) collective-permute-start(bf16[80,1152]{1,0:T(8,128)(2,1)S(1)} %get-tuple-element.21), channel_id=1, source_target_pairs={{1,2},{3,4},{5,6},{2,1},{4,3},{6,5},{9,10},{11,12},{13,14},{10,9},... | collective-permute-start | bytes 552968 | tf_op jit(solution)/shard_map/ppermute | solution.py:336
  18.7 3.0 %collective-permute-start.5 = (bf16[16,1152]{1,0:T(8,128)(2,1)S(1)}, bf16[16,1152]{1,0:T(8,128)(2,1)S(1)}, u32[]{:S(2)}, u32[]{:S(2)}) collective-permute-start(bf16[16,1152]{1,0:T(8,128)(2,1)S(1)} %get-tuple-element.22), channel_id=1, source_target_pairs={{0,2},{1,3},{4,6},{5,7},{2,0},{3,1},{6,4},{7,5},{8,10},{9,11},{12,... | collective-permute-start | bytes 110600 | tf_op jit(solution)/shard_map/ppermute | solution.py:336
  21.6 0.0 copy-start.3
  21.6 0.8 %collective-permute-start.6 = (bf16[16,1152]{1,0:T(8,128)(2,1)S(1)}, bf16[16,1152]{1,0:T(8,128)(2,1)S(1)}, u32[]{:S(2)}, u32[]{:S(2)}) collective-permute-start(bf16[16,1152]{1,0:T(8,128)(2,1)S(1)} %get-tuple-element.23), channel_id=1, source_target_pairs={{2,4},{3,5},{4,2},{5,3},{10,12},{11,13},{12,10},{13,11},{18,20},{1... | collective-permute-start | bytes 110600 | tf_op jit(solution)/shard_map/ppermute | solution.py:336
  22.4 0.0 collective-permute-done.3.in_chip
  22.4 0.0 copy-done.1
  22.5 0.0 copy-done.2
  22.5 1.1 %shard_map.102 = (f32[1024,256]{1,0:T(8,128)S(1)}, f32[2,128,1024]{2,1,0:T(8,128)S(1)}, f32[128,1024]{1,0:T(8,128)S(1)}, bf16[3,256,512]{2,1,0:T(8,128)(2,1)S(1)...) custom-call(bf16[4,32,1280]{2,1,0:T(8,128)(2,1)S(1)} %all-to-all-done.own, ...), custom_call_target="tpu_custom_call" | custom-call | flops 1000000000 | bytes 3000000 | tf_op jit(solution)/shard_map/pallas_call | solution.py:394
  23.6 2.3 %collective-permute-done.5.far_even = bf16[16,1152]{1,0:T(8,128)(2,1)S(1)} collective-permute-done((bf16[16,1152]{1,0:T(8,128)(2,1)S(1)}, bf16[16,1152]{1,0:T(8,128)(2,1)S(1)}, u32[]{:S(2)}, u32[]{:S(2)}) %collective-permute-start.5) | collective-permute-done | bytes 36896 | tf_op jit(solution)/shard_map/ppermute | solution.py:336
  25.9 0.0 collective-permute-done.6.far_odd
  25.9 0.0 collective-permute-done.4.cross
  25.9 0.0 copy-done.3
  25.9 2.5 %shard_map.103 = bf16[4,2,32,1024]{3,2,1,0:T(8,128)(2,1)S(1)} custom-call(bf16[144,1152]{1,0:T(8,128)(2,1)S(1)} %collective-permute-done.3.in_chip, bf16[80,1152]{1,0:T(8,128)(2,1)S(1)} %collective-permute-done.4.cross, bf16[16,1152]{1,0:T(8,128)(2,1)S(1)} %collective-permute-done.5.far_even, bf16[16,1152]{1,0:T(8,128)(2,1)S(1)} %collective-permute-done.6.far_odd, ...), custom_call_target="tpu_custom_call" | custom-call | flops 2000000000 | bytes 3000000 | tf_op jit(solution)/shard_map/pallas_call | solution.py:408
  28.4 11.8 %all_to_all.10 = bf16[4,2,32,1024]{3,2,1,0:T(8,128)(2,1)S(1)} all-to-all(bf16[4,2,32,1024]{3,2,1,0:T(8,128)(2,1)S(1)} %shard_map.103), channel_id=1, replica_groups=mesh['depth'=4,'rows'=8] {'depth'}, dimensions={0} | all-to-all | bytes 1048576 | tf_op jit(solution)/shard_map/all_to_all | solution.py:416
  40.1 0.8 %slice_bitcast_fusion = bf16[1,3,2,32,1024]{4,3,2,1,0:T(8,128)(2,1)} fusion(bf16[4,2,32,1024]{3,2,1,0:T(8,128)(2,1)S(1)} %all_to_all.10), kind=kLoop, calls=%fused_computation | loop fusion | bytes 786432 | tf_op jit(solution)/shard_map/broadcast_in_dim | solution.py:417
  (1 shorter events, 0.0 us)
Async XLA Ops:
  2.0 5.3 %copy-start = (bf16[2,32,1024]{2,1,0:T(8,128)(2,1)S(1)}, bf16[2,32,1024]{2,1,0:T(8,128)(2,1)}, u32[]{:S(2)}) copy-start(bf16[2,32,1024]{2,1,0:T(8,128)(2,1)} %get-tuple-element.19.incident) | copy-start | bytes 393220
  2.0 13.6 %all-to-all-start = ((bf16[4,32,1280]{2,1,0:T(8,128)(2,1)}), bf16[4,32,1280]{2,1,0:T(8,128)(2,1)S(1)}, u32[]{:S(2)}, u32[]{:S(2)}) async-start(bf16[4,32,1280]{2,1,0:T(8,128)(2,1)} %get-tuple-element.18), calls=%async_computation | async-start | bytes 655360 | tf_op jit(solution)/shard_map/all_to_all | solution.py:384
  7.3 15.1 %copy-start.1 = (bf16[256,256]{1,0:T(8,128)(2,1)S(1)}, bf16[256,256]{1,0:T(8,128)(2,1)}, u32[]{:S(2)}) copy-start(bf16[256,256]{1,0:T(8,128)(2,1)} %constant.6.clone.right_tab) | copy-start | bytes 393220
  7.3 15.1 %copy-start.2 = (bf16[256,256]{1,0:T(8,128)(2,1)S(1)}, bf16[256,256]{1,0:T(8,128)(2,1)}, u32[]{:S(2)}) copy-start(bf16[256,256]{1,0:T(8,128)(2,1)} %constant.7.clone.left_tab) | copy-start | bytes 393220
  7.3 5.9 %collective-permute-start.2 = (bf16[64,1024]{1,0:T(8,128)(2,1)S(1)}, bf16[64,1024]{1,0:T(8,128)(2,1)S(1)}, u32[]{:S(2)}, u32[]{:S(2)}) collective-permute-start(bf16[64,1024]{1,0:T(8,128)(2,1)S(1)} %bitcast.3), channel_id=1, source_target_pairs={{2,4},{3,5},{4,2},{5,3},{10,12},{11,13},{12,10},{13,11},{18,20},{1... | collective-permute-start | bytes 393224 | tf_op jit(solution)/shard_map/ppermute | solution.py:336
  8.1 7.4 %collective-permute-start.1 = (bf16[64,1024]{1,0:T(8,128)(2,1)S(1)}, bf16[64,1024]{1,0:T(8,128)(2,1)S(1)}, u32[]{:S(2)}, u32[]{:S(2)}) collective-permute-start(bf16[64,1024]{1,0:T(8,128)(2,1)S(1)} %bitcast.4), channel_id=1, source_target_pairs={{0,2},{1,3},{4,6},{5,7},{2,0},{3,1},{6,4},{7,5},{8,10},{9,11},{12,... | collective-permute-start | bytes 393224 | tf_op jit(solution)/shard_map/ppermute | solution.py:336
  12.6 3.0 %collective-permute-start = (bf16[64,1024]{1,0:T(8,128)(2,1)S(1)}, bf16[64,1024]{1,0:T(8,128)(2,1)S(1)}, u32[]{:S(2)}, u32[]{:S(2)}) collective-permute-start(bf16[64,1024]{1,0:T(8,128)(2,1)S(1)} %bitcast.5), channel_id=1, source_target_pairs={{1,2},{3,4},{5,6},{2,1},{4,3},{6,5},{9,10},{11,12},{13,14},{10,9},... | collective-permute-start | bytes 393224 | tf_op jit(solution)/shard_map/ppermute | solution.py:336
  15.6 6.8 %collective-permute-start.3 = (bf16[144,1152]{1,0:T(8,128)(2,1)S(1)}, bf16[144,1152]{1,0:T(8,128)(2,1)S(1)}, u32[]{:S(2)}, u32[]{:S(2)}) collective-permute-start(bf16[144,1152]{1,0:T(8,128)(2,1)S(1)} %get-tuple-element.20), channel_id=1, source_target_pairs={{0,1},{2,3},{4,5},{6,7},{1,0},{3,2},{5,4},{7,6},{8,9},{10,11},{12,... | collective-permute-start | bytes 995336 | tf_op jit(solution)/shard_map/ppermute | solution.py:336
  18.0 7.8 %collective-permute-start.4 = (bf16[80,1152]{1,0:T(8,128)(2,1)S(1)}, bf16[80,1152]{1,0:T(8,128)(2,1)S(1)}, u32[]{:S(2)}, u32[]{:S(2)}) collective-permute-start(bf16[80,1152]{1,0:T(8,128)(2,1)S(1)} %get-tuple-element.21), channel_id=1, source_target_pairs={{1,2},{3,4},{5,6},{2,1},{4,3},{6,5},{9,10},{11,12},{13,14},{10,9},... | collective-permute-start | bytes 552968 | tf_op jit(solution)/shard_map/ppermute | solution.py:336
  18.7 7.2 %collective-permute-start.5 = (bf16[16,1152]{1,0:T(8,128)(2,1)S(1)}, bf16[16,1152]{1,0:T(8,128)(2,1)S(1)}, u32[]{:S(2)}, u32[]{:S(2)}) collective-permute-start(bf16[16,1152]{1,0:T(8,128)(2,1)S(1)} %get-tuple-element.22), channel_id=1, source_target_pairs={{0,2},{1,3},{4,6},{5,7},{2,0},{3,1},{6,4},{7,5},{8,10},{9,11},{12,... | collective-permute-start | bytes 110600 | tf_op jit(solution)/shard_map/ppermute | solution.py:336
  21.6 4.2 %copy-start.3 = (bf16[192,192]{1,0:T(8,128)(2,1)S(1)}, bf16[192,192]{1,0:T(8,128)(2,1)}, u32[]{:S(2)}) copy-start(bf16[192,192]{1,0:T(8,128)(2,1)} %constant.8.clone.left_tab) | copy-start | bytes 221188
  21.6 4.2 %collective-permute-start.6 = (bf16[16,1152]{1,0:T(8,128)(2,1)S(1)}, bf16[16,1152]{1,0:T(8,128)(2,1)S(1)}, u32[]{:S(2)}, u32[]{:S(2)}) collective-permute-start(bf16[16,1152]{1,0:T(8,128)(2,1)S(1)} %get-tuple-element.23), channel_id=1, source_target_pairs={{2,4},{3,5},{4,2},{5,3},{10,12},{11,13},{12,10},{13,11},{18,20},{1... | collective-permute-start | bytes 110600 | tf_op jit(solution)/shard_map/ppermute | solution.py:336

commit v8 on v3

--- a/solution.py
+++ b/solution.py
@@ -75,8 +75,13 @@
     return jnp.where(column // HS == tile, 1.0, 0.0).astype(jnp.bfloat16)
 
 
-def pack_kernel(light, edges, counts, listed, row_taps, col_taps, out, *scratch):
+def own_colour():
+    return jnp.minimum(lax.axis_index("depth"), COLORS - 1)
+
+
+def pack_kernel(light, edges, counts, listed, row_taps, col_taps, incident, out, mine, *scratch):
     held, sems, taps = scratch[:6], scratch[6], scratch[7]
+    picked = pltpu.make_async_copy(incident.at[own_colour()], mine, sems.at[6])
     sources = (listed, counts, edges, row_taps, col_taps, light)
     copies = [
         pltpu.make_async_copy(source, target, sems.at[place])
@@ -84,6 +89,7 @@
     ]
     for copy in reversed(copies):
         copy.start()
+    picked.start()
     listed, counts, edges, row_taps, col_taps, light = held
     spread = spread_matrix()
     slot = lax.broadcasted_iota(jnp.int32, (NH, NH), 0)
@@ -113,6 +119,7 @@
     copies[5].wait()
     for colour in range(COLORS):
         out[colour, :, :COLS] = (light[0, colour] * live_pix).astype(jnp.bfloat16)
+    picked.wait()
 
 
 def halo_kernel(own, in_chip, cross, far_even, far_odd):
@@ -358,18 +365,15 @@
         pltpu.VMEM(col_taps.shape, bf16),
         pltpu.VMEM(hogel_light.shape, f32),
     ]
-    payload = call(
+    payload, mine = call(
         pack_kernel,
-        shaped((LAYERS, BAND, FULL_W), bf16),
-        [hbm] * 6,
-        held + [pltpu.SemaphoreType.DMA((6,)), pltpu.VMEM((BAND, LANES), f32)],
+        (shaped((LAYERS, BAND, FULL_W), bf16), shaped(incident.shape[1:], bf16)),
+        [hbm] * 7,
+        held + [pltpu.SemaphoreType.DMA((7,)), pltpu.VMEM((BAND, LANES), f32)],
         flops=10**7,
         limit=PACK_LIMIT,
-    )(hogel_light, silhouette, fill_counts, hogel_index, row_taps, col_taps)
-    colour = jnp.minimum(lax.axis_index("depth"), COLORS - 1)
-    mine = lax.dynamic_index_in_dim(incident, colour, 0, keepdims=False)
+    )(hogel_light, silhouette, fill_counts, hogel_index, row_taps, col_taps, incident)
     mine = mine.reshape(2 * BAND, COLS)
-    payload, mine = lax.optimization_barrier((payload, mine))
     own = lax.all_to_all(payload, "depth", 0, 0, tiled=True)
     arrived = neighbours((mine,) * 4)
     near = shaped((NEAR, HALO_W), bf16)

time: 39.4 us -> 38.6 us (0.980)
  local copies, waits for them, and re-layouts: 1.79 us -> 0.79 us
    unnamed x8, local copies, waits for them, and re-layouts: 1.01 us -> 0.02 us
where the time goes in v8:
time: 38.6 us; the launch traced here: 38.2 us
  starting transfers between devices  16.3 us (42%)
  blocking collectives  12.1 us (31%)
  Pallas kernels  5.6 us (15%)
  waiting for transfers between devices  3.3 us (9%)
  local copies, waits for them, and re-layouts  0.79 us (2%)
    all_to_all x1, blocking collectives, body(): gathered = lax.all_to_all(result, 'depth', 0, 0, tiled=True)  12.1 us
    ppermute x8, starting transfers between devices, exchanged(): return lax.ppermute(value, axis, pairs)  11 us
    all_to_all x1, starting transfers between devices, body(): own = lax.all_to_all(payload, 'depth', 0, 0, tiled=True)  5.31 us
    pallas_call x1, Pallas kernels, body(): call(chain_kernel, shaped((LAYERS, 2, BAND, COLS), bf16), [vmem] * (6 + l...  2.46 us
    ppermute x8, waiting for transfers between devices, exchanged(): return lax.ppermute(value, axis, pairs)  2.27 us
    pallas_call x1, Pallas kernels, body(): call(pack_kernel, (shaped((LAYERS, BAND, FULL_W), bf16), shaped(incident....  1.98 us
    pallas_call x1, Pallas kernels, body(): call(prepare_kernel, [shaped((TILES * layer_height(0), 2 * LANES), f32),...  1.13 us
    all_to_all x1, waiting for transfers between devices, body(): own = lax.all_to_all(payload, 'depth', 0, 0, tiled=True)  1.03 us
  transfers between devices with their start and end apart: 9, of which 2 were waited for; matrix products, arithmetic and copies ran while one was open for 0% of the time, Pallas kernels for 3%

profile of v8, /device:TPU:0, one launch (start us, length us, event | category | flops | bytes accessed | tf_op | source)
XLA Modules:
  0.0 38.2 jit_solution(3011505928858668406)
XLA Ops:
  0.0 2.0 %shard_map.100 = (bf16[4,32,1280]{2,1,0:T(8,128)(2,1)}, bf16[2,32,1024]{2,1,0:T(8,128)(2,1)}) custom-call(f32[1,3,32,1024]{3,2,1,0:T(8,128)} %light.1, s32[1,32,64]{2,1,0:T(8,128)} %edges.1, s32[1,2]{1,0:T(1,128)} %counts.1, s32[1,2,64]{2,1,0:T(2,128)} %listed.1, bf16[1,3,2,33]{3,2,1,0:T(2,128)(2,1)} %row_taps.1, bf16[1,3,2,127]{3,2,1,0:T(2,128)(2,1)} %col_taps.1, ...), custom_call_target="tpu_custom_call" | custom-call | flops 10000000 | bytes 1000000 | tf_op jit(solution)/shard_map/pallas_call | solution.py:368
  2.0 0.0 copy-start
  2.0 5.3 %all-to-all-start = ((bf16[4,32,1280]{2,1,0:T(8,128)(2,1)}), bf16[4,32,1280]{2,1,0:T(8,128)(2,1)S(1)}, u32[]{:S(2)}, u32[]{:S(2)}) async-start(bf16[4,32,1280]{2,1,0:T(8,128)(2,1)} %get-tuple-element.18), calls=%async_computation | async-start | bytes 655360 | tf_op jit(solution)/shard_map/all_to_all | solution.py:377
  7.3 0.0 copy-done
  7.3 0.0 copy-start.1
  7.3 0.0 copy-start.2
  7.3 0.1 collective-permute-start.4
  7.4 0.8 %collective-permute-start.5 = (bf16[64,1024]{1,0:T(8,128)(2,1)S(1)}, bf16[64,1024]{1,0:T(8,128)(2,1)S(1)}, u32[]{:S(2)}, u32[]{:S(2)}) collective-permute-start(bf16[64,1024]{1,0:T(8,128)(2,1)S(1)} %bitcast.4), channel_id=1, source_target_pairs={{1,2},{3,4},{5,6},{2,1},{4,3},{6,5},{9,10},{11,12},{13,14},{10,9},... | collective-permute-start | bytes 393224 | tf_op jit(solution)/shard_map/ppermute | solution.py:329
  8.2 3.3 %collective-permute-start.6 = (bf16[64,1024]{1,0:T(8,128)(2,1)S(1)}, bf16[64,1024]{1,0:T(8,128)(2,1)S(1)}, u32[]{:S(2)}, u32[]{:S(2)}) collective-permute-start(bf16[64,1024]{1,0:T(8,128)(2,1)S(1)} %bitcast.5), channel_id=1, source_target_pairs={{0,2},{1,3},{4,6},{5,7},{2,0},{3,1},{6,4},{7,5},{8,10},{9,11},{12,... | collective-permute-start | bytes 393224 | tf_op jit(solution)/shard_map/ppermute | solution.py:329
  11.5 0.7 %collective-permute-start.7 = (bf16[64,1024]{1,0:T(8,128)(2,1)S(1)}, bf16[64,1024]{1,0:T(8,128)(2,1)S(1)}, u32[]{:S(2)}, u32[]{:S(2)}) collective-permute-start(bf16[64,1024]{1,0:T(8,128)(2,1)S(1)} %bitcast.6), channel_id=1, source_target_pairs={{2,4},{3,5},{4,2},{5,3},{10,12},{11,13},{12,10},{13,11},{18,20},{1... | collective-permute-start | bytes 393224 | tf_op jit(solution)/shard_map/ppermute | solution.py:329
  12.2 1.0 %all-to-all-done.own = bf16[4,32,1280]{2,1,0:T(8,128)(2,1)S(1)} async-done(((bf16[4,32,1280]{2,1,0:T(8,128)(2,1)}), bf16[4,32,1280]{2,1,0:T(8,128)(2,1)S(1)}, u32[]{:S(2)}, u32[]{:S(2)}) %all-to-all-start) | async-done | bytes 327712 | tf_op jit(solution)/shard_map/all_to_all | solution.py:377
  13.2 0.1 collective-permute-start
  13.3 0.0 collective-permute-done.4.in_chip
  13.3 0.7 %collective-permute-start.1 = (bf16[80,1152]{1,0:T(8,128)(2,1)S(1)}, bf16[80,1152]{1,0:T(8,128)(2,1)S(1)}, u32[]{:S(2)}, u32[]{:S(2)}) collective-permute-start(bf16[80,1152]{1,0:T(8,128)(2,1)S(1)} %get-tuple-element.20), channel_id=1, source_target_pairs={{1,2},{3,4},{5,6},{2,1},{4,3},{6,5},{9,10},{11,12},{13,14},{10,9},... | collective-permute-start | bytes 552968 | tf_op jit(solution)/shard_map/ppermute | solution.py:329
  14.0 0.0 collective-permute-done.5.cross
  14.0 4.7 %collective-permute-start.2 = (bf16[16,1152]{1,0:T(8,128)(2,1)S(1)}, bf16[16,1152]{1,0:T(8,128)(2,1)S(1)}, u32[]{:S(2)}, u32[]{:S(2)}) collective-permute-start(bf16[16,1152]{1,0:T(8,128)(2,1)S(1)} %get-tuple-element.21), channel_id=1, source_target_pairs={{0,2},{1,3},{4,6},{5,7},{2,0},{3,1},{6,4},{7,5},{8,10},{9,11},{12,... | collective-permute-start | bytes 110600 | tf_op jit(solution)/shard_map/ppermute | solution.py:329
  18.7 0.0 collective-permute-done.6.far_even
  18.7 0.0 copy-start.3
  18.7 0.8 %collective-permute-start.3 = (bf16[16,1152]{1,0:T(8,128)(2,1)S(1)}, bf16[16,1152]{1,0:T(8,128)(2,1)S(1)}, u32[]{:S(2)}, u32[]{:S(2)}) collective-permute-start(bf16[16,1152]{1,0:T(8,128)(2,1)S(1)} %get-tuple-element.22), channel_id=1, source_target_pairs={{2,4},{3,5},{4,2},{5,3},{10,12},{11,13},{12,10},{13,11},{18,20},{1... | collective-permute-start | bytes 110600 | tf_op jit(solution)/shard_map/ppermute | solution.py:329
  19.5 0.0 collective-permute-done.7.far_odd
  19.5 0.0 copy-done.1
  19.5 0.0 copy-done.2
  19.5 1.1 %shard_map.102 = (f32[1024,256]{1,0:T(8,128)S(1)}, f32[2,128,1024]{2,1,0:T(8,128)S(1)}, f32[128,1024]{1,0:T(8,128)S(1)}, bf16[3,256,512]{2,1,0:T(8,128)(2,1)S(1)...) custom-call(bf16[4,32,1280]{2,1,0:T(8,128)(2,1)S(1)} %all-to-all-done.own, ...), custom_call_target="tpu_custom_call" | custom-call | flops 1000000000 | bytes 3000000 | tf_op jit(solution)/shard_map/pallas_call | solution.py:383
  20.7 2.2 %collective-permute-done.2.far_even = bf16[16,1152]{1,0:T(8,128)(2,1)S(1)} collective-permute-done((bf16[16,1152]{1,0:T(8,128)(2,1)S(1)}, bf16[16,1152]{1,0:T(8,128)(2,1)S(1)}, u32[]{:S(2)}, u32[]{:S(2)}) %collective-permute-start.2) | collective-permute-done | bytes 36896 | tf_op jit(solution)/shard_map/ppermute | solution.py:329
  22.9 0.0 collective-permute-done.3.far_odd
  22.9 0.0 collective-permute-done.in_chip
  22.9 0.0 collective-permute-done.1.cross
  22.9 0.0 copy-done.3
  22.9 2.5 %shard_map.103 = bf16[4,2,32,1024]{3,2,1,0:T(8,128)(2,1)S(1)} custom-call(bf16[80,1152]{1,0:T(8,128)(2,1)S(1)} %collective-permute-done.in_chip, bf16[80,1152]{1,0:T(8,128)(2,1)S(1)} %collective-permute-done.1.cross, bf16[16,1152]{1,0:T(8,128)(2,1)S(1)} %collective-permute-done.2.far_even, bf16[16,1152]{1,0:T(8,128)(2,1)S(1)} %collective-permute-done.3.far_odd, ...), custom_call_target="tpu_custom_call" | custom-call | flops 2000000000 | bytes 3000000 | tf_op jit(solution)/shard_map/pallas_call | solution.py:397
  25.4 12.1 %all_to_all.10 = bf16[4,2,32,1024]{3,2,1,0:T(8,128)(2,1)S(1)} all-to-all(bf16[4,2,32,1024]{3,2,1,0:T(8,128)(2,1)S(1)} %shard_map.103), channel_id=1, replica_groups=mesh['depth'=4,'rows'=8] {'depth'}, dimensions={0} | all-to-all | bytes 1048576 | tf_op jit(solution)/shard_map/all_to_all | solution.py:405
  37.5 0.8 %slice_bitcast_fusion = bf16[1,3,2,32,1024]{4,3,2,1,0:T(8,128)(2,1)} fusion(bf16[4,2,32,1024]{3,2,1,0:T(8,128)(2,1)S(1)} %all_to_all.10), kind=kLoop, calls=%fused_computation | loop fusion | bytes 786432 | tf_op jit(solution)/shard_map/broadcast_in_dim | solution.py:406
  (1 shorter events, 0.0 us)
Async XLA Ops:
  2.0 5.3 %copy-start = (bf16[2,32,1024]{2,1,0:T(8,128)(2,1)S(1)}, bf16[2,32,1024]{2,1,0:T(8,128)(2,1)}, u32[]{:S(2)}) copy-start(bf16[2,32,1024]{2,1,0:T(8,128)(2,1)} %get-tuple-element.23) | copy-start | bytes 393220
  2.0 11.2 %all-to-all-start = ((bf16[4,32,1280]{2,1,0:T(8,128)(2,1)}), bf16[4,32,1280]{2,1,0:T(8,128)(2,1)S(1)}, u32[]{:S(2)}, u32[]{:S(2)}) async-start(bf16[4,32,1280]{2,1,0:T(8,128)(2,1)} %get-tuple-element.18), calls=%async_computation | async-start | bytes 655360 | tf_op jit(solution)/shard_map/all_to_all | solution.py:377
  7.3 12.2 %copy-start.1 = (bf16[256,256]{1,0:T(8,128)(2,1)S(1)}, bf16[256,256]{1,0:T(8,128)(2,1)}, u32[]{:S(2)}) copy-start(bf16[256,256]{1,0:T(8,128)(2,1)} %constant.6.clone.right_tab) | copy-start | bytes 393220
  7.3 12.2 %copy-start.2 = (bf16[256,256]{1,0:T(8,128)(2,1)S(1)}, bf16[256,256]{1,0:T(8,128)(2,1)}, u32[]{:S(2)}) copy-start(bf16[256,256]{1,0:T(8,128)(2,1)} %constant.7.clone.left_tab) | copy-start | bytes 393220
  7.3 6.0 %collective-permute-start.4 = (bf16[64,1024]{1,0:T(8,128)(2,1)S(1)}, bf16[64,1024]{1,0:T(8,128)(2,1)S(1)}, u32[]{:S(2)}, u32[]{:S(2)}) collective-permute-start(bf16[64,1024]{1,0:T(8,128)(2,1)S(1)} %bitcast.3), channel_id=1, source_target_pairs={{0,1},{2,3},{4,5},{6,7},{1,0},{3,2},{5,4},{7,6},{8,9},{10,11},{12,... | collective-permute-start | bytes 393224 | tf_op jit(solution)/shard_map/ppermute | solution.py:329
  7.4 6.6 %collective-permute-start.5 = (bf16[64,1024]{1,0:T(8,128)(2,1)S(1)}, bf16[64,1024]{1,0:T(8,128)(2,1)S(1)}, u32[]{:S(2)}, u32[]{:S(2)}) collective-permute-start(bf16[64,1024]{1,0:T(8,128)(2,1)S(1)} %bitcast.4), channel_id=1, source_target_pairs={{1,2},{3,4},{5,6},{2,1},{4,3},{6,5},{9,10},{11,12},{13,14},{10,9},... | collective-permute-start | bytes 393224 | tf_op jit(solution)/shard_map/ppermute | solution.py:329
  8.2 10.5 %collective-permute-start.6 = (bf16[64,1024]{1,0:T(8,128)(2,1)S(1)}, bf16[64,1024]{1,0:T(8,128)(2,1)S(1)}, u32[]{:S(2)}, u32[]{:S(2)}) collective-permute-start(bf16[64,1024]{1,0:T(8,128)(2,1)S(1)} %bitcast.5), channel_id=1, source_target_pairs={{0,2},{1,3},{4,6},{5,7},{2,0},{3,1},{6,4},{7,5},{8,10},{9,11},{12,... | collective-permute-start | bytes 393224 | tf_op jit(solution)/shard_map/ppermute | solution.py:329
  11.5 8.0 %collective-permute-start.7 = (bf16[64,1024]{1,0:T(8,128)(2,1)S(1)}, bf16[64,1024]{1,0:T(8,128)(2,1)S(1)}, u32[]{:S(2)}, u32[]{:S(2)}) collective-permute-start(bf16[64,1024]{1,0:T(8,128)(2,1)S(1)} %bitcast.6), channel_id=1, source_target_pairs={{2,4},{3,5},{4,2},{5,3},{10,12},{11,13},{12,10},{13,11},{18,20},{1... | collective-permute-start | bytes 393224 | tf_op jit(solution)/shard_map/ppermute | solution.py:329
  13.2 9.7 %collective-permute-start = (bf16[80,1152]{1,0:T(8,128)(2,1)S(1)}, bf16[80,1152]{1,0:T(8,128)(2,1)S(1)}, u32[]{:S(2)}, u32[]{:S(2)}) collective-permute-start(bf16[80,1152]{1,0:T(8,128)(2,1)S(1)} %get-tuple-element.19), channel_id=1, source_target_pairs={{0,1},{2,3},{4,5},{6,7},{1,0},{3,2},{5,4},{7,6},{8,9},{10,11},{12,... | collective-permute-start | bytes 552968 | tf_op jit(solution)/shard_map/ppermute | solution.py:329
  13.3 9.6 %collective-permute-start.1 = (bf16[80,1152]{1,0:T(8,128)(2,1)S(1)}, bf16[80,1152]{1,0:T(8,128)(2,1)S(1)}, u32[]{:S(2)}, u32[]{:S(2)}) collective-permute-start(bf16[80,1152]{1,0:T(8,128)(2,1)S(1)} %get-tuple-element.20), channel_id=1, source_target_pairs={{1,2},{3,4},{5,6},{2,1},{4,3},{6,5},{9,10},{11,12},{13,14},{10,9},... | collective-permute-start | bytes 552968 | tf_op jit(solution)/shard_map/ppermute | solution.py:329
  14.0 8.9 %collective-permute-start.2 = (bf16[16,1152]{1,0:T(8,128)(2,1)S(1)}, bf16[16,1152]{1,0:T(8,128)(2,1)S(1)}, u32[]{:S(2)}, u32[]{:S(2)}) collective-permute-start(bf16[16,1152]{1,0:T(8,128)(2,1)S(1)} %get-tuple-element.21), channel_id=1, source_target_pairs={{0,2},{1,3},{4,6},{5,7},{2,0},{3,1},{6,4},{7,5},{8,10},{9,11},{12,... | collective-permute-start | bytes 110600 | tf_op jit(solution)/shard_map/ppermute | solution.py:329
  18.7 4.2 %copy-start.3 = (bf16[192,192]{1,0:T(8,128)(2,1)S(1)}, bf16[192,192]{1,0:T(8,128)(2,1)}, u32[]{:S(2)}) copy-start(bf16[192,192]{1,0:T(8,128)(2,1)} %constant.8.clone.left_tab) | copy-start | bytes 221188
  18.7 4.2 %collective-permute-start.3 = (bf16[16,1152]{1,0:T(8,128)(2,1)S(1)}, bf16[16,1152]{1,0:T(8,128)(2,1)S(1)}, u32[]{:S(2)}, u32[]{:S(2)}) collective-permute-start(bf16[16,1152]{1,0:T(8,128)(2,1)S(1)} %get-tuple-element.22), channel_id=1, source_target_pairs={{2,4},{3,5},{4,2},{5,3},{10,12},{11,13},{12,10},{13,11},{18,20},{1... | collective-permute-start | bytes 110600 | tf_op jit(solution)/shard_map/ppermute | solution.py:329

commit v9 on v8

--- a/solution.py
+++ b/solution.py
@@ -23,6 +23,7 @@
 FULL_W = COLS + 2 * LANES
 NEAR = 2 * BAND + KR
 FAR = KR
+REACH = 5
 VMEM_LIMIT = 48 * 1024 * 1024
 PACK_LIMIT = 63 * 1024 * 1024
 
@@ -238,17 +239,23 @@
 
 
 def prepare_kernel(
-    own, incident, in_chip, cross, far_even, far_odd, left_tab, right_tab,
-    first, stereo, clear, col_mats, *row_mats
+    own, bands, left_tab, right_tab, first, stereo, clear, col_mats, *rest
 ):
-    low_near, high_near, low_far, high_far = ordered(in_chip, cross, far_even, far_odd)
-    extended = []
-    for part in range(2):
-        pieces = [low_far, low_near, incident[...], high_near, high_far]
-        pieces = [piece[part * BAND : (part + 1) * BAND] for piece in pieces]
-        extended.append(jnp.concatenate(pieces, axis=0))
-    row_mat, col_mat = filters(own[0, 0:16, HALO_W:].astype(jnp.float32), 0)
-    first[...] = propagated(extended[0], extended[1], row_mat, col_mat, 0)
+    row_mats, (near, sems) = rest[:-2], rest[-2:]
+    here = lax.axis_index("rows")
+    count = lax.axis_size("rows")
+    for place in range(REACH):
+        band = here + place - REACH // 2
+        inside = (band >= 0) & (band < count)
+
+        @pl.when(inside)
+        def fetch(place=place, band=band):
+            pltpu.make_async_copy(bands.at[band], near.at[place], sems.at[place]).start()
+
+        @pl.when(jnp.logical_not(inside))
+        def blank(place=place):
+            near[place] = jnp.zeros((2 * BAND, COLS), jnp.bfloat16)
+
     for layer in range(1, LAYERS):
         row_mat, col_mat = filters(own[layer, 0:16, HALO_W:].astype(jnp.float32), layer)
         row_mats[layer - 1][...] = row_mat
@@ -262,6 +269,21 @@
                 tile * LANES : (tile + 1) * LANES, part * LANES : (part + 1) * LANES
             ]
             stereo[part, :, tile * LANES : (tile + 1) * LANES] = block
+    for place in range(REACH):
+        band = here + place - REACH // 2
+
+        @pl.when((band >= 0) & (band < count))
+        def arrive(place=place, band=band):
+            pltpu.make_async_copy(bands.at[band], near.at[place], sems.at[place]).wait()
+
+    extended = [
+        jnp.concatenate(
+            [near[place, part * BAND : (part + 1) * BAND] for place in range(REACH)], axis=0
+        )
+        for part in range(2)
+    ]
+    row_mat, col_mat = filters(own[0, 0:16, HALO_W:].astype(jnp.float32), 0)
+    first[...] = propagated(extended[0], extended[1], row_mat, col_mat, 0)
 
 
 def chain_kernel(
@@ -375,7 +397,7 @@
     )(hogel_light, silhouette, fill_counts, hogel_index, row_taps, col_taps, incident)
     mine = mine.reshape(2 * BAND, COLS)
     own = lax.all_to_all(payload, "depth", 0, 0, tiled=True)
-    arrived = neighbours((mine,) * 4)
+    bands = lax.all_gather(mine, "rows")
     near = shaped((NEAR, HALO_W), bf16)
     far = shaped((FAR, HALO_W), bf16)
     halos = neighbours(call(halo_kernel, (near, near, far, far), [vmem])(own))
@@ -389,10 +411,14 @@
             shaped((LAYERS - 1, 2 * LANES, 4 * LANES), bf16),
         ]
         + [shaped((2 * block_height(layer), 2 * LANES), bf16) for layer in range(1, LAYERS)],
-        [vmem] * 8,
+        [vmem, hbm, vmem, vmem],
+        [
+            pltpu.VMEM((REACH, 2 * BAND, COLS), bf16),
+            pltpu.SemaphoreType.DMA((REACH,)),
+        ],
         flops=10**9,
         moved=3 * 10**6,
-    )(own, mine, *arrived, jnp.asarray(left_table(LANES)), right_tab)
+    )(own, bands, jnp.asarray(left_table(LANES)), right_tab)
     halo_rows = NEAR + FAR
     result = call(
         chain_kernel,

time: 38.6 us -> 62.2 us (1.61)
  between operations: 0.14 us -> 13.5 us
  blocking collectives: 12.1 us -> 24.5 us
  starting transfers between devices: 16.3 us -> 4.81 us
  waiting for transfers between devices: 3.3 us -> 10.3 us
  local copies, waits for them, and re-layouts: 0.79 us -> 2.01 us
  Pallas kernels: 5.6 us -> 6.79 us
    all_to_all x0 -> x1, blocking collectives: none -> 11.8 us  [body(): own = lax.all_to_all(payload, 'depth', 0, 0, tiled=True)]
    all_gather x0 -> x1, waiting for transfers between devices: none -> 10.3 us  [body(): bands = lax.all_gather(mine, 'rows')]
    ppermute x8 -> x4, starting transfers between devices: 11 us -> 4.81 us  [exchanged(): return lax.ppermute(value, axis, pairs)]
    all_to_all x1 -> x0, starting transfers between devices: 5.31 us -> none  [body(): own = lax.all_to_all(payload, 'depth', 0, 0, tiled=True)]
    ppermute x8 -> x4, waiting for transfers between devices: 2.27 us -> 0.01 us  [exchanged(): return lax.ppermute(value, axis, pairs)]
    unnamed x8, local copies, waits for them, and re-layouts: 0.02 us -> 1.24 us
    pallas_call x1, Pallas kernels: 1.13 us -> 2.28 us  [body(): call(prepare_kernel, [shaped((TILES * layer_height(0), 2 * LANES), f32),...]
    all_to_all x1 -> x0, waiting for transfers between devices: 1.03 us -> none  [body(): own = lax.all_to_all(payload, 'depth', 0, 0, tiled=True)]
  transfers between devices with their start and end apart: 9 -> 5, of which waited for: 2 -> 1; matrix products, arithmetic and copies ran while one was open for 0% -> 0% of each run, Pallas kernels for 3% -> 4%
where the time goes in v9:
time: 62.2 us; the launch traced here: 61.9 us
  blocking collectives  24.5 us (39%)
  between operations  13.5 us (22%)
  waiting for transfers between devices  10.3 us (17%)
  Pallas kernels  6.79 us (11%)
  starting transfers between devices  4.81 us (8%)
  local copies, waits for them, and re-layouts  2.01 us (3%)
    all_to_all x1, blocking collectives, body(): gathered = lax.all_to_all(result, 'depth', 0, 0, tiled=True)  12.8 us
    all_to_all x1, blocking collectives, body(): own = lax.all_to_all(payload, 'depth', 0, 0, tiled=True)  11.8 us
    all_gather x1, waiting for transfers between devices, body(): bands = lax.all_gather(mine, 'rows')  10.3 us
    ppermute x4, starting transfers between devices, exchanged(): return lax.ppermute(value, axis, pairs)  4.81 us
    pallas_call x1, Pallas kernels, body(): call(chain_kernel, shaped((LAYERS, 2, BAND, COLS), bf16), [vmem] * (6 + l...  2.46 us
    pallas_call x1, Pallas kernels, body(): call(prepare_kernel, [shaped((TILES * layer_height(0), 2 * LANES), f32),...  2.28 us
    pallas_call x1, Pallas kernels, body(): call(pack_kernel, (shaped((LAYERS, BAND, FULL_W), bf16), shaped(incident....  2.02 us
  transfers between devices with their start and end apart: 5, of which 1 were waited for; matrix products, arithmetic and copies ran while one was open for 0% of the time, Pallas kernels for 4%

profile of v9, /device:TPU:0, one launch (start us, length us, event | category | flops | bytes accessed | tf_op | source)
XLA Modules:
  0.0 61.9 jit_solution(11877020170544087453)
XLA Ops:
  6.5 0.0 all-gather.2.cloned.1.call-start
  6.5 2.0 %shard_map.100 = (bf16[4,32,1280]{2,1,0:T(8,128)(2,1)}, bf16[2,32,1024]{2,1,0:T(8,128)(2,1)}) custom-call(f32[1,3,32,1024]{3,2,1,0:T(8,128)} %light.1, s32[1,32,64]{2,1,0:T(8,128)} %edges.1, s32[1,2]{1,0:T(1,128)} %counts.1, s32[1,2,64]{2,1,0:T(2,128)} %listed.1, bf16[1,3,2,33]{3,2,1,0:T(2,128)(2,1)} %row_taps.1, bf16[1,3,2,127]{3,2,1,0:T(2,128)(2,1)} %col_taps.1, ...), custom_call_target="tpu_custom_call" | custom-call | flops 10000000 | bytes 1000000 | tf_op jit(solution)/shard_map/pallas_call | solution.py:390
  8.6 0.0 all-gather.2.cloned.1.call-update
  8.6 11.8 %all_to_all.10.own = bf16[4,32,1280]{2,1,0:T(8,128)(2,1)S(1)} all-to-all(bf16[4,32,1280]{2,1,0:T(8,128)(2,1)} %get-tuple-element.18), channel_id=1, replica_groups=mesh['depth'=4,'rows'=8] {'depth'}, dimensions={0} | all-to-all | bytes 655360 | tf_op jit(solution)/shard_map/all_to_all | solution.py:399
  20.4 0.0 copy-start.1
  20.4 0.0 copy-start.2
  20.4 0.1 collective-permute-start
  20.5 0.7 %collective-permute-start.1 = (bf16[80,1152]{1,0:T(8,128)(2,1)S(1)}, bf16[80,1152]{1,0:T(8,128)(2,1)S(1)}, u32[]{:S(2)}, u32[]{:S(2)}) collective-permute-start(bf16[80,1152]{1,0:T(8,128)(2,1)S(1)} %get-tuple-element.20), channel_id=1, source_target_pairs={{1,2},{3,4},{5,6},{2,1},{4,3},{6,5},{9,10},{11,12},{13,14},{10,9},... | collective-permute-start | bytes 552968 | tf_op jit(solution)/shard_map/ppermute | solution.py:351
  21.2 3.4 %collective-permute-start.2 = (bf16[16,1152]{1,0:T(8,128)(2,1)S(1)}, bf16[16,1152]{1,0:T(8,128)(2,1)S(1)}, u32[]{:S(2)}, u32[]{:S(2)}) collective-permute-start(bf16[16,1152]{1,0:T(8,128)(2,1)S(1)} %get-tuple-element.21), channel_id=1, source_target_pairs={{0,2},{1,3},{4,6},{5,7},{2,0},{3,1},{6,4},{7,5},{8,10},{9,11},{12,... | collective-permute-start | bytes 110600 | tf_op jit(solution)/shard_map/ppermute | solution.py:351
  24.6 0.7 %collective-permute-start.3 = (bf16[16,1152]{1,0:T(8,128)(2,1)S(1)}, bf16[16,1152]{1,0:T(8,128)(2,1)S(1)}, u32[]{:S(2)}, u32[]{:S(2)}) collective-permute-start(bf16[16,1152]{1,0:T(8,128)(2,1)S(1)} %get-tuple-element.22), channel_id=1, source_target_pairs={{2,4},{3,5},{4,2},{5,3},{10,12},{11,13},{12,10},{13,11},{18,20},{1... | collective-permute-start | bytes 110600 | tf_op jit(solution)/shard_map/ppermute | solution.py:351
  25.2 10.3 %all-gather.2.cloned.1.call-done.bands = bf16[8,64,1024]{2,1,0:T(8,128)(2,1)} async-done(((bf16[1,64,1024]{2,1,0:T(8,128)(2,1)}), bf16[8,64,1024]{2,1,0:T(8,128)(2,1)}) %all-gather.2.cloned.1.call-update) | async-done | bytes 1048592 | tf_op jit(solution)/shard_map/all_gather | solution.py:400
  35.5 0.0 copy-done.1
  35.5 0.0 copy-done.2
  35.5 0.0 copy-start
  35.5 1.2 %copy-done = bf16[8,64,1024]{2,1,0:T(8,128)(2,1)S(1)} copy-done((bf16[8,64,1024]{2,1,0:T(8,128)(2,1)S(1)}, bf16[8,64,1024]{2,1,0:T(8,128)(2,1)}, u32[]{:S(2)}) %copy-start) | copy-done | bytes 1048600
  36.7 0.0 copy-start.3
  36.7 2.3 %shard_map.102 = (f32[1024,256]{1,0:T(8,128)S(1)}, f32[2,128,1024]{2,1,0:T(8,128)S(1)}, f32[128,1024]{1,0:T(8,128)S(1)}, bf16[3,256,512]{2,1,0:T(8,128)(2,1)S(1)...) custom-call(bf16[4,32,1280]{2,1,0:T(8,128)(2,1)S(1)} %all_to_all.10.own, ...), custom_call_target="tpu_custom_call" | custom-call | flops 1000000000 | bytes 3000000 | tf_op jit(solution)/shard_map/pallas_call | solution.py:405
  39.0 0.0 collective-permute-done.2.far_even
  39.0 0.0 collective-permute-done.3.far_odd
  39.0 0.0 collective-permute-done.in_chip
  39.0 0.0 collective-permute-done.1.cross
  39.0 0.0 copy-done.3
  39.1 2.5 %shard_map.103 = bf16[4,2,32,1024]{3,2,1,0:T(8,128)(2,1)S(1)} custom-call(bf16[80,1152]{1,0:T(8,128)(2,1)S(1)} %collective-permute-done.in_chip, bf16[80,1152]{1,0:T(8,128)(2,1)S(1)} %collective-permute-done.1.cross, bf16[16,1152]{1,0:T(8,128)(2,1)S(1)} %collective-permute-done.2.far_even, bf16[16,1152]{1,0:T(8,128)(2,1)S(1)} %collective-permute-done.3.far_odd, ...), custom_call_target="tpu_custom_call" | custom-call | flops 2000000000 | bytes 3000000 | tf_op jit(solution)/shard_map/pallas_call | solution.py:423
  41.5 12.8 %all_to_all.11 = bf16[4,2,32,1024]{3,2,1,0:T(8,128)(2,1)S(1)} all-to-all(bf16[4,2,32,1024]{3,2,1,0:T(8,128)(2,1)S(1)} %shard_map.103), channel_id=1, replica_groups=mesh['depth'=4,'rows'=8] {'depth'}, dimensions={0} | all-to-all | bytes 1048576 | tf_op jit(solution)/shard_map/all_to_all | solution.py:431
  54.3 0.8 %slice_bitcast_fusion = bf16[1,3,2,32,1024]{4,3,2,1,0:T(8,128)(2,1)} fusion(bf16[4,2,32,1024]{3,2,1,0:T(8,128)(2,1)S(1)} %all_to_all.11), kind=kLoop, calls=%fused_computation | loop fusion | bytes 786432 | tf_op jit(solution)/shard_map/broadcast_in_dim | solution.py:432
  (1 shorter events, 0.0 us)
Async XLA Ops:
  6.5 28.9 %all-gather.2.cloned.1.call-start = ((), (), s32[]{:S(2)}) async-start(), calls=%async_computation.2 | async-start | bytes 1179648 | tf_op jit(solution)/shard_map/all_gather | solution.py:400
  20.4 15.1 %copy-start.1 = (bf16[256,256]{1,0:T(8,128)(2,1)S(1)}, bf16[256,256]{1,0:T(8,128)(2,1)}, u32[]{:S(2)}) copy-start(bf16[256,256]{1,0:T(8,128)(2,1)} %constant.6.clone.right_tab) | copy-start | bytes 393220
  20.4 15.1 %copy-start.2 = (bf16[256,256]{1,0:T(8,128)(2,1)S(1)}, bf16[256,256]{1,0:T(8,128)(2,1)}, u32[]{:S(2)}) copy-start(bf16[256,256]{1,0:T(8,128)(2,1)} %constant.7.clone.left_tab) | copy-start | bytes 393220
  20.4 18.6 %collective-permute-start = (bf16[80,1152]{1,0:T(8,128)(2,1)S(1)}, bf16[80,1152]{1,0:T(8,128)(2,1)S(1)}, u32[]{:S(2)}, u32[]{:S(2)}) collective-permute-start(bf16[80,1152]{1,0:T(8,128)(2,1)S(1)} %get-tuple-element.19), channel_id=1, source_target_pairs={{0,1},{2,3},{4,5},{6,7},{1,0},{3,2},{5,4},{7,6},{8,9},{10,11},{12,... | collective-permute-start | bytes 552968 | tf_op jit(solution)/shard_map/ppermute | solution.py:351
  20.5 18.6 %collective-permute-start.1 = (bf16[80,1152]{1,0:T(8,128)(2,1)S(1)}, bf16[80,1152]{1,0:T(8,128)(2,1)S(1)}, u32[]{:S(2)}, u32[]{:S(2)}) collective-permute-start(bf16[80,1152]{1,0:T(8,128)(2,1)S(1)} %get-tuple-element.20), channel_id=1, source_target_pairs={{1,2},{3,4},{5,6},{2,1},{4,3},{6,5},{9,10},{11,12},{13,14},{10,9},... | collective-permute-start | bytes 552968 | tf_op jit(solution)/shard_map/ppermute | solution.py:351
  21.2 17.9 %collective-permute-start.2 = (bf16[16,1152]{1,0:T(8,128)(2,1)S(1)}, bf16[16,1152]{1,0:T(8,128)(2,1)S(1)}, u32[]{:S(2)}, u32[]{:S(2)}) collective-permute-start(bf16[16,1152]{1,0:T(8,128)(2,1)S(1)} %get-tuple-element.21), channel_id=1, source_target_pairs={{0,2},{1,3},{4,6},{5,7},{2,0},{3,1},{6,4},{7,5},{8,10},{9,11},{12,... | collective-permute-start | bytes 110600 | tf_op jit(solution)/shard_map/ppermute | solution.py:351
  24.6 14.4 %collective-permute-start.3 = (bf16[16,1152]{1,0:T(8,128)(2,1)S(1)}, bf16[16,1152]{1,0:T(8,128)(2,1)S(1)}, u32[]{:S(2)}, u32[]{:S(2)}) collective-permute-start(bf16[16,1152]{1,0:T(8,128)(2,1)S(1)} %get-tuple-element.22), channel_id=1, source_target_pairs={{2,4},{3,5},{4,2},{5,3},{10,12},{11,13},{12,10},{13,11},{18,20},{1... | collective-permute-start | bytes 110600 | tf_op jit(solution)/shard_map/ppermute | solution.py:351
  35.5 1.2 %copy-start = (bf16[8,64,1024]{2,1,0:T(8,128)(2,1)S(1)}, bf16[8,64,1024]{2,1,0:T(8,128)(2,1)}, u32[]{:S(2)}) copy-start(bf16[8,64,1024]{2,1,0:T(8,128)(2,1)} %all-gather.2.cloned.1.call-done.bands) | copy-start | bytes 3145732
  36.7 2.3 %copy-start.3 = (bf16[192,192]{1,0:T(8,128)(2,1)S(1)}, bf16[192,192]{1,0:T(8,128)(2,1)}, u32[]{:S(2)}) copy-start(bf16[192,192]{1,0:T(8,128)(2,1)} %constant.8.clone.left_tab) | copy-start | bytes 221188
Sparse Core Ops, SparseCore 0:
  9.0 26.4 all-gather.1

commit v10 on v8

--- a/solution.py
+++ b/solution.py
@@ -238,10 +238,16 @@
 
 
 def prepare_kernel(
-    own, incident, in_chip, cross, far_even, far_odd, left_tab, right_tab,
+    own, incident, partner, cross, relayed, left_tab, right_tab,
     first, stereo, clear, col_mats, *row_mats
 ):
-    low_near, high_near, low_far, high_far = ordered(in_chip, cross, far_even, far_odd)
+    even_core = lax.axis_index("rows") % 2 == 0
+    partner, beyond = partner[...], relayed[: 2 * BAND]
+    near, distant = cross[: 2 * BAND], cross[2 * BAND :]
+    low_far = jnp.where(even_core, distant, beyond)
+    low_near = jnp.where(even_core, near, partner)
+    high_near = jnp.where(even_core, partner, near)
+    high_far = jnp.where(even_core, beyond, distant)
     extended = []
     for part in range(2):
         pieces = [low_far, low_near, incident[...], high_near, high_far]
@@ -375,7 +381,9 @@
     )(hogel_light, silhouette, fill_counts, hogel_index, row_taps, col_taps, incident)
     mine = mine.reshape(2 * BAND, COLS)
     own = lax.all_to_all(payload, "depth", 0, 0, tiled=True)
-    arrived = neighbours((mine,) * 4)
+    partner = exchanged(mine, "rows", 1, 0)
+    cross = exchanged(jnp.concatenate([mine, partner], axis=0), "rows", 1, 1)
+    relayed = exchanged(cross, "rows", 1, 0)
     near = shaped((NEAR, HALO_W), bf16)
     far = shaped((FAR, HALO_W), bf16)
     halos = neighbours(call(halo_kernel, (near, near, far, far), [vmem])(own))
@@ -389,10 +397,10 @@
             shaped((LAYERS - 1, 2 * LANES, 4 * LANES), bf16),
         ]
         + [shaped((2 * block_height(layer), 2 * LANES), bf16) for layer in range(1, LAYERS)],
-        [vmem] * 8,
+        [vmem] * 7,
         flops=10**9,
         moved=3 * 10**6,
-    )(own, mine, *arrived, jnp.asarray(left_table(LANES)), right_tab)
+    )(own, mine, partner, cross, relayed, jnp.asarray(left_table(LANES)), right_tab)
     halo_rows = NEAR + FAR
     result = call(
         chain_kernel,

time: 38.6 us -> 41.4 us (1.073)
  waiting for transfers between devices: 3.3 us -> 5.92 us
  blocking collectives: 12.1 us -> 10.8 us
  other arithmetic: 0 us -> 0.92 us
  starting transfers between devices: 16.3 us -> 17 us
    all_to_all x1, waiting for transfers between devices: 1.03 us -> 2.46 us  [body(): own = lax.all_to_all(payload, 'depth', 0, 0, tiled=True)]
    all_to_all x1, blocking collectives: 12.1 us -> 10.8 us  [body(): gathered = lax.all_to_all(result, 'depth', 0, 0, tiled=True)]
    ppermute x8 -> x7, waiting for transfers between devices: 2.27 us -> 3.46 us  [exchanged(): return lax.ppermute(value, axis, pairs)]
    concatenate x0 -> x1, other arithmetic: none -> 0.92 us  [body(): cross = exchanged(jnp.concatenate([mine, partner], axis=0), 'rows', 1, 1)]
    ppermute x8 -> x7, starting transfers between devices: 11 us -> 11.8 us  [exchanged(): return lax.ppermute(value, axis, pairs)]
  transfers between devices with their start and end apart: 9 -> 8, of which waited for: 2 -> 3; matrix products, arithmetic and copies ran while one was open for 0% -> 0% of each run, Pallas kernels for 3% -> 3%
where the time goes in v10:
time: 41.4 us; the launch traced here: 41.1 us
  starting transfers between devices  17 us (41%)
  blocking collectives  10.8 us (26%)
  waiting for transfers between devices  5.92 us (14%)
  Pallas kernels  5.63 us (14%)
  other arithmetic  0.92 us (2%)
  local copies, waits for them, and re-layouts  0.79 us (2%)
    ppermute x7, starting transfers between devices, exchanged(): return lax.ppermute(value, axis, pairs)  11.8 us
    all_to_all x1, blocking collectives, body(): gathered = lax.all_to_all(result, 'depth', 0, 0, tiled=True)  10.8 us
    all_to_all x1, starting transfers between devices, body(): own = lax.all_to_all(payload, 'depth', 0, 0, tiled=True)  5.22 us
    ppermute x7, waiting for transfers between devices, exchanged(): return lax.ppermute(value, axis, pairs)  3.46 us
    pallas_call x1, Pallas kernels, body(): call(chain_kernel, shaped((LAYERS, 2, BAND, COLS), bf16), [vmem] * (6 + l...  2.48 us
    all_to_all x1, waiting for transfers between devices, body(): own = lax.all_to_all(payload, 'depth', 0, 0, tiled=True)  2.46 us
    pallas_call x1, Pallas kernels, body(): call(pack_kernel, (shaped((LAYERS, BAND, FULL_W), bf16), shaped(incident....  1.98 us
    pallas_call x1, Pallas kernels, body(): call(prepare_kernel, [shaped((TILES * layer_height(0), 2 * LANES), f32),...  1.13 us
  transfers between devices with their start and end apart: 8, of which 3 were waited for; matrix products, arithmetic and copies ran while one was open for 0% of the time, Pallas kernels for 3%

profile of v10, /device:TPU:0, one launch (start us, length us, event | category | flops | bytes accessed | tf_op | source)
XLA Modules:
  0.0 41.1 jit_solution(5879779662704718014)
XLA Ops:
  0.0 2.0 %shard_map.100 = (bf16[4,32,1280]{2,1,0:T(8,128)(2,1)}, bf16[2,32,1024]{2,1,0:T(8,128)(2,1)}) custom-call(f32[1,3,32,1024]{3,2,1,0:T(8,128)} %light.1, s32[1,32,64]{2,1,0:T(8,128)} %edges.1, s32[1,2]{1,0:T(1,128)} %counts.1, s32[1,2,64]{2,1,0:T(2,128)} %listed.1, bf16[1,3,2,33]{3,2,1,0:T(2,128)(2,1)} %row_taps.1, bf16[1,3,2,127]{3,2,1,0:T(2,128)(2,1)} %col_taps.1, ...), custom_call_target="tpu_custom_call" | custom-call | flops 10000000 | bytes 1000000 | tf_op jit(solution)/shard_map/pallas_call | solution.py:374
  2.0 0.5 %collective-permute-start.4 = (bf16[64,1024]{1,0:T(8,128)(2,1)}, bf16[64,1024]{1,0:T(8,128)(2,1)S(1)}, u32[]{:S(2)}, u32[]{:S(2)}) collective-permute-start(bf16[64,1024]{1,0:T(8,128)(2,1)} %bitcast.3), channel_id=1, source_target_pairs={{0,1},{2,3},{4,5},{6,7},{1,0},{3,2},{5,4},{7,6},{8,9},{10,11},{12,... | collective-permute-start | bytes 393224 | tf_op jit(solution)/shard_map/ppermute | solution.py:335
  2.5 1.2 %collective-permute-done.4.partner = bf16[64,1024]{1,0:T(8,128)(2,1)S(1)} collective-permute-done((bf16[64,1024]{1,0:T(8,128)(2,1)}, bf16[64,1024]{1,0:T(8,128)(2,1)S(1)}, u32[]{:S(2)}, u32[]{:S(2)}) %collective-permute-start.4) | collective-permute-done | bytes 131104 | tf_op jit(solution)/shard_map/ppermute | solution.py:335
  3.7 0.9 %pad_maximum_fusion = bf16[128,1024]{1,0:T(8,128)(2,1)S(1)} fusion(bf16[64,1024]{1,0:T(8,128)(2,1)S(1)} %collective-permute-done.4.partner, bf16[64,1024]{1,0:T(8,128)(2,1)} %bitcast.4), kind=kLoop, calls=%fused_computation.1 | loop fusion | flops 524288 | bytes 524288 | tf_op jit(solution)/shard_map/concatenate | solution.py:385
  4.6 0.7 %collective-permute-start.5 = (bf16[128,1024]{1,0:T(8,128)(2,1)S(1)}, bf16[128,1024]{1,0:T(8,128)(2,1)S(1)}, u32[]{:S(2)}, u32[]{:S(2)}) collective-permute-start(bf16[128,1024]{1,0:T(8,128)(2,1)S(1)} %pad_maximum_fusion), channel_id=1, source_target_pairs={{1,2},{3,4},{5,6},{2,1},{4,3},{6,5},{9,10},{11,12},{13,14},{10,9},... | collective-permute-start | bytes 786440 | tf_op jit(solution)/shard_map/ppermute | solution.py:335
  5.3 0.0 copy-start.2
  5.3 5.2 %all-to-all-start = ((bf16[4,32,1280]{2,1,0:T(8,128)(2,1)}), bf16[4,32,1280]{2,1,0:T(8,128)(2,1)S(1)}, u32[]{:S(2)}, u32[]{:S(2)}) async-start(bf16[4,32,1280]{2,1,0:T(8,128)(2,1)} %get-tuple-element.18), calls=%async_computation | async-start | bytes 655360 | tf_op jit(solution)/shard_map/all_to_all | solution.py:383
  10.5 0.0 copy-start
  10.5 0.0 copy-start.1
  10.5 0.0 collective-permute-done.5.cross
  10.6 3.1 %collective-permute-start.6 = (bf16[128,1024]{1,0:T(8,128)(2,1)S(1)}, bf16[128,1024]{1,0:T(8,128)(2,1)S(1)}, u32[]{:S(2)}, u32[]{:S(2)}) collective-permute-start(bf16[128,1024]{1,0:T(8,128)(2,1)S(1)} %collective-permute-done.5.cross), channel_id=1, source_target_pairs={{0,1},{2,3},{4,5},{6,7},{1,0},{3,2},{5,4},{7,6},{8,9},{10,11},{12,... | collective-permute-start | bytes 786440 | tf_op jit(solution)/shard_map/ppermute | solution.py:335
  13.6 2.5 %all-to-all-done.own = bf16[4,32,1280]{2,1,0:T(8,128)(2,1)S(1)} async-done(((bf16[4,32,1280]{2,1,0:T(8,128)(2,1)}), bf16[4,32,1280]{2,1,0:T(8,128)(2,1)S(1)}, u32[]{:S(2)}, u32[]{:S(2)}) %all-to-all-start) | async-done | bytes 327712 | tf_op jit(solution)/shard_map/all_to_all | solution.py:383
  16.1 1.6 %collective-permute-start = (bf16[80,1152]{1,0:T(8,128)(2,1)S(1)}, bf16[80,1152]{1,0:T(8,128)(2,1)S(1)}, u32[]{:S(2)}, u32[]{:S(2)}) collective-permute-start(bf16[80,1152]{1,0:T(8,128)(2,1)S(1)} %get-tuple-element.19), channel_id=1, source_target_pairs={{0,1},{2,3},{4,5},{6,7},{1,0},{3,2},{5,4},{7,6},{8,9},{10,11},{12,... | collective-permute-start | bytes 552968 | tf_op jit(solution)/shard_map/ppermute | solution.py:335
  17.8 0.7 %collective-permute-start.1 = (bf16[80,1152]{1,0:T(8,128)(2,1)S(1)}, bf16[80,1152]{1,0:T(8,128)(2,1)S(1)}, u32[]{:S(2)}, u32[]{:S(2)}) collective-permute-start(bf16[80,1152]{1,0:T(8,128)(2,1)S(1)} %get-tuple-element.20), channel_id=1, source_target_pairs={{1,2},{3,4},{5,6},{2,1},{4,3},{6,5},{9,10},{11,12},{13,14},{10,9},... | collective-permute-start | bytes 552968 | tf_op jit(solution)/shard_map/ppermute | solution.py:335
  18.4 4.4 %collective-permute-start.2 = (bf16[16,1152]{1,0:T(8,128)(2,1)S(1)}, bf16[16,1152]{1,0:T(8,128)(2,1)S(1)}, u32[]{:S(2)}, u32[]{:S(2)}) collective-permute-start(bf16[16,1152]{1,0:T(8,128)(2,1)S(1)} %get-tuple-element.21), channel_id=1, source_target_pairs={{0,2},{1,3},{4,6},{5,7},{2,0},{3,1},{6,4},{7,5},{8,10},{9,11},{12,... | collective-permute-start | bytes 110600 | tf_op jit(solution)/shard_map/ppermute | solution.py:335
  22.8 0.0 copy-start.3
  22.8 0.8 %collective-permute-start.3 = (bf16[16,1152]{1,0:T(8,128)(2,1)S(1)}, bf16[16,1152]{1,0:T(8,128)(2,1)S(1)}, u32[]{:S(2)}, u32[]{:S(2)}) collective-permute-start(bf16[16,1152]{1,0:T(8,128)(2,1)S(1)} %get-tuple-element.22), channel_id=1, source_target_pairs={{2,4},{3,5},{4,2},{5,3},{10,12},{11,13},{12,10},{13,11},{18,20},{1... | collective-permute-start | bytes 110600 | tf_op jit(solution)/shard_map/ppermute | solution.py:335
  23.6 0.0 collective-permute-done.6.relayed
  23.6 0.0 copy-done.2
  23.7 0.0 copy-done
  23.7 0.0 copy-done.1
  23.7 1.1 %shard_map.102 = (f32[1024,256]{1,0:T(8,128)S(1)}, f32[2,128,1024]{2,1,0:T(8,128)S(1)}, f32[128,1024]{1,0:T(8,128)S(1)}, bf16[3,256,512]{2,1,0:T(8,128)(2,1)S(1)...) custom-call(bf16[4,32,1280]{2,1,0:T(8,128)(2,1)S(1)} %all-to-all-done.own, ...), custom_call_target="tpu_custom_call" | custom-call | flops 1000000000 | bytes 3000000 | tf_op jit(solution)/shard_map/pallas_call | solution.py:391
  24.8 2.2 %collective-permute-done.2.far_even = bf16[16,1152]{1,0:T(8,128)(2,1)S(1)} collective-permute-done((bf16[16,1152]{1,0:T(8,128)(2,1)S(1)}, bf16[16,1152]{1,0:T(8,128)(2,1)S(1)}, u32[]{:S(2)}, u32[]{:S(2)}) %collective-permute-start.2) | collective-permute-done | bytes 36896 | tf_op jit(solution)/shard_map/ppermute | solution.py:335
  27.1 0.0 collective-permute-done.3.far_odd
  27.1 0.0 collective-permute-done.in_chip
  27.1 0.0 collective-permute-done.1.cross
  27.1 0.0 copy-done.3
  27.1 2.5 %shard_map.103 = bf16[4,2,32,1024]{3,2,1,0:T(8,128)(2,1)S(1)} custom-call(bf16[80,1152]{1,0:T(8,128)(2,1)S(1)} %collective-permute-done.in_chip, bf16[80,1152]{1,0:T(8,128)(2,1)S(1)} %collective-permute-done.1.cross, bf16[16,1152]{1,0:T(8,128)(2,1)S(1)} %collective-permute-done.2.far_even, bf16[16,1152]{1,0:T(8,128)(2,1)S(1)} %collective-permute-done.3.far_odd, ...), custom_call_target="tpu_custom_call" | custom-call | flops 2000000000 | bytes 3000000 | tf_op jit(solution)/shard_map/pallas_call | solution.py:405
  29.6 10.8 %all_to_all.10 = bf16[4,2,32,1024]{3,2,1,0:T(8,128)(2,1)S(1)} all-to-all(bf16[4,2,32,1024]{3,2,1,0:T(8,128)(2,1)S(1)} %shard_map.103), channel_id=1, replica_groups=mesh['depth'=4,'rows'=8] {'depth'}, dimensions={0} | all-to-all | bytes 1048576 | tf_op jit(solution)/shard_map/all_to_all | solution.py:413
  40.3 0.8 %slice_bitcast_fusion = bf16[1,3,2,32,1024]{4,3,2,1,0:T(8,128)(2,1)} fusion(bf16[4,2,32,1024]{3,2,1,0:T(8,128)(2,1)S(1)} %all_to_all.10), kind=kLoop, calls=%fused_computation | loop fusion | bytes 786432 | tf_op jit(solution)/shard_map/broadcast_in_dim | solution.py:414
  (1 shorter events, 0.0 us)
Async XLA Ops:
  2.0 1.7 %collective-permute-start.4 = (bf16[64,1024]{1,0:T(8,128)(2,1)}, bf16[64,1024]{1,0:T(8,128)(2,1)S(1)}, u32[]{:S(2)}, u32[]{:S(2)}) collective-permute-start(bf16[64,1024]{1,0:T(8,128)(2,1)} %bitcast.3), channel_id=1, source_target_pairs={{0,1},{2,3},{4,5},{6,7},{1,0},{3,2},{5,4},{7,6},{8,9},{10,11},{12,... | collective-permute-start | bytes 393224 | tf_op jit(solution)/shard_map/ppermute | solution.py:335
  4.6 5.9 %collective-permute-start.5 = (bf16[128,1024]{1,0:T(8,128)(2,1)S(1)}, bf16[128,1024]{1,0:T(8,128)(2,1)S(1)}, u32[]{:S(2)}, u32[]{:S(2)}) collective-permute-start(bf16[128,1024]{1,0:T(8,128)(2,1)S(1)} %pad_maximum_fusion), channel_id=1, source_target_pairs={{1,2},{3,4},{5,6},{2,1},{4,3},{6,5},{9,10},{11,12},{13,14},{10,9},... | collective-permute-start | bytes 786440 | tf_op jit(solution)/shard_map/ppermute | solution.py:335
  5.3 18.3 %copy-start.2 = (bf16[256,256]{1,0:T(8,128)(2,1)S(1)}, bf16[256,256]{1,0:T(8,128)(2,1)}, u32[]{:S(2)}) copy-start(bf16[256,256]{1,0:T(8,128)(2,1)} %constant.7.clone.left_tab) | copy-start | bytes 393220
  5.3 10.8 %all-to-all-start = ((bf16[4,32,1280]{2,1,0:T(8,128)(2,1)}), bf16[4,32,1280]{2,1,0:T(8,128)(2,1)S(1)}, u32[]{:S(2)}, u32[]{:S(2)}) async-start(bf16[4,32,1280]{2,1,0:T(8,128)(2,1)} %get-tuple-element.18), calls=%async_computation | async-start | bytes 655360 | tf_op jit(solution)/shard_map/all_to_all | solution.py:383
  10.5 13.1 %copy-start = (bf16[2,32,1024]{2,1,0:T(8,128)(2,1)S(1)}, bf16[2,32,1024]{2,1,0:T(8,128)(2,1)}, u32[]{:S(2)}) copy-start(bf16[2,32,1024]{2,1,0:T(8,128)(2,1)} %get-tuple-element.23) | copy-start | bytes 393220
  10.5 13.1 %copy-start.1 = (bf16[256,256]{1,0:T(8,128)(2,1)S(1)}, bf16[256,256]{1,0:T(8,128)(2,1)}, u32[]{:S(2)}) copy-start(bf16[256,256]{1,0:T(8,128)(2,1)} %constant.6.clone.right_tab) | copy-start | bytes 393220
  10.6 13.1 %collective-permute-start.6 = (bf16[128,1024]{1,0:T(8,128)(2,1)S(1)}, bf16[128,1024]{1,0:T(8,128)(2,1)S(1)}, u32[]{:S(2)}, u32[]{:S(2)}) collective-permute-start(bf16[128,1024]{1,0:T(8,128)(2,1)S(1)} %collective-permute-done.5.cross), channel_id=1, source_target_pairs={{0,1},{2,3},{4,5},{6,7},{1,0},{3,2},{5,4},{7,6},{8,9},{10,11},{12,... | collective-permute-start | bytes 786440 | tf_op jit(solution)/shard_map/ppermute | solution.py:335
  16.1 10.9 %collective-permute-start = (bf16[80,1152]{1,0:T(8,128)(2,1)S(1)}, bf16[80,1152]{1,0:T(8,128)(2,1)S(1)}, u32[]{:S(2)}, u32[]{:S(2)}) collective-permute-start(bf16[80,1152]{1,0:T(8,128)(2,1)S(1)} %get-tuple-element.19), channel_id=1, source_target_pairs={{0,1},{2,3},{4,5},{6,7},{1,0},{3,2},{5,4},{7,6},{8,9},{10,11},{12,... | collective-permute-start | bytes 552968 | tf_op jit(solution)/shard_map/ppermute | solution.py:335
  17.8 9.3 %collective-permute-start.1 = (bf16[80,1152]{1,0:T(8,128)(2,1)S(1)}, bf16[80,1152]{1,0:T(8,128)(2,1)S(1)}, u32[]{:S(2)}, u32[]{:S(2)}) collective-permute-start(bf16[80,1152]{1,0:T(8,128)(2,1)S(1)} %get-tuple-element.20), channel_id=1, source_target_pairs={{1,2},{3,4},{5,6},{2,1},{4,3},{6,5},{9,10},{11,12},{13,14},{10,9},... | collective-permute-start | bytes 552968 | tf_op jit(solution)/shard_map/ppermute | solution.py:335
  18.4 8.6 %collective-permute-start.2 = (bf16[16,1152]{1,0:T(8,128)(2,1)S(1)}, bf16[16,1152]{1,0:T(8,128)(2,1)S(1)}, u32[]{:S(2)}, u32[]{:S(2)}) collective-permute-start(bf16[16,1152]{1,0:T(8,128)(2,1)S(1)} %get-tuple-element.21), channel_id=1, source_target_pairs={{0,2},{1,3},{4,6},{5,7},{2,0},{3,1},{6,4},{7,5},{8,10},{9,11},{12,... | collective-permute-start | bytes 110600 | tf_op jit(solution)/shard_map/ppermute | solution.py:335
  22.8 4.2 %copy-start.3 = (bf16[192,192]{1,0:T(8,128)(2,1)S(1)}, bf16[192,192]{1,0:T(8,128)(2,1)}, u32[]{:S(2)}) copy-start(bf16[192,192]{1,0:T(8,128)(2,1)} %constant.8.clone.left_tab) | copy-start | bytes 221188
  22.8 4.2 %collective-permute-start.3 = (bf16[16,1152]{1,0:T(8,128)(2,1)S(1)}, bf16[16,1152]{1,0:T(8,128)(2,1)S(1)}, u32[]{:S(2)}, u32[]{:S(2)}) collective-permute-start(bf16[16,1152]{1,0:T(8,128)(2,1)S(1)} %get-tuple-element.22), channel_id=1, source_target_pairs={{2,4},{3,5},{4,2},{5,3},{10,12},{11,13},{12,10},{13,11},{18,20},{1... | collective-permute-start | bytes 110600 | tf_op jit(solution)/shard_map/ppermute | solution.py:335

commit v11 on v8

--- a/solution.py
+++ b/solution.py
@@ -238,7 +238,7 @@
 
 
 def prepare_kernel(
-    own, incident, in_chip, cross, far_even, far_odd, left_tab, right_tab,
+    own, incident, cross, far_even, far_odd, in_chip, left_tab, right_tab,
     first, stereo, clear, col_mats, *row_mats
 ):
     low_near, high_near, low_far, high_far = ordered(in_chip, cross, far_even, far_odd)
@@ -375,7 +375,7 @@
     )(hogel_light, silhouette, fill_counts, hogel_index, row_taps, col_taps, incident)
     mine = mine.reshape(2 * BAND, COLS)
     own = lax.all_to_all(payload, "depth", 0, 0, tiled=True)
-    arrived = neighbours((mine,) * 4)
+    in_chip, *arrived = neighbours((mine,) * 4)
     near = shaped((NEAR, HALO_W), bf16)
     far = shaped((FAR, HALO_W), bf16)
     halos = neighbours(call(halo_kernel, (near, near, far, far), [vmem])(own))
@@ -392,7 +392,7 @@
         [vmem] * 8,
         flops=10**9,
         moved=3 * 10**6,
-    )(own, mine, *arrived, jnp.asarray(left_table(LANES)), right_tab)
+    )(own, mine, *arrived, in_chip, jnp.asarray(left_table(LANES)), right_tab)
     halo_rows = NEAR + FAR
     result = call(
         chain_kernel,

time: 38.6 us -> 38.7 us (level)
  waiting for transfers between devices: 3.3 us -> 4.98 us
  starting transfers between devices: 16.3 us -> 14.7 us
    ppermute x8, waiting for transfers between devices: 2.27 us -> 4.94 us  [exchanged(): return lax.ppermute(value, axis, pairs)]
    ppermute x8, starting transfers between devices: 11 us -> 9.42 us  [exchanged(): return lax.ppermute(value, axis, pairs)]
    all_to_all x1, waiting for transfers between devices: 1.03 us -> 0.04 us  [body(): own = lax.all_to_all(payload, 'depth', 0, 0, tiled=True)]
where the time goes in v11:
time: 38.7 us; the launch traced here: 38.3 us
  starting transfers between devices  14.7 us (38%)
  blocking collectives  12.1 us (31%)
  Pallas kernels  5.6 us (14%)
  waiting for transfers between devices  4.98 us (13%)
  local copies, waits for them, and re-layouts  0.79 us (2%)
    all_to_all x1, blocking collectives, body(): gathered = lax.all_to_all(result, 'depth', 0, 0, tiled=True)  12.1 us
    ppermute x8, starting transfers between devices, exchanged(): return lax.ppermute(value, axis, pairs)  9.42 us
    all_to_all x1, starting transfers between devices, body(): own = lax.all_to_all(payload, 'depth', 0, 0, tiled=True)  5.31 us
    ppermute x8, waiting for transfers between devices, exchanged(): return lax.ppermute(value, axis, pairs)  4.94 us
    pallas_call x1, Pallas kernels, body(): call(chain_kernel, shaped((LAYERS, 2, BAND, COLS), bf16), [vmem] * (6 + l...  2.46 us
    pallas_call x1, Pallas kernels, body(): call(pack_kernel, (shaped((LAYERS, BAND, FULL_W), bf16), shaped(incident....  1.98 us
    pallas_call x1, Pallas kernels, body(): call(prepare_kernel, [shaped((TILES * layer_height(0), 2 * LANES), f32),...  1.13 us
  transfers between devices with their start and end apart: 9, of which 2 were waited for; matrix products, arithmetic and copies ran while one was open for 0% of the time, Pallas kernels for 3%

profile of v11, /device:TPU:0, one launch (start us, length us, event | category | flops | bytes accessed | tf_op | source)
XLA Modules:
  0.0 38.3 jit_solution(6952396163871537840)
XLA Ops:
  0.0 2.0 %shard_map.100 = (bf16[4,32,1280]{2,1,0:T(8,128)(2,1)}, bf16[2,32,1024]{2,1,0:T(8,128)(2,1)}) custom-call(f32[1,3,32,1024]{3,2,1,0:T(8,128)} %light.1, s32[1,32,64]{2,1,0:T(8,128)} %edges.1, s32[1,2]{1,0:T(1,128)} %counts.1, s32[1,2,64]{2,1,0:T(2,128)} %listed.1, bf16[1,3,2,33]{3,2,1,0:T(2,128)(2,1)} %row_taps.1, bf16[1,3,2,127]{3,2,1,0:T(2,128)(2,1)} %col_taps.1, ...), custom_call_target="tpu_custom_call" | custom-call | flops 10000000 | bytes 1000000 | tf_op jit(solution)/shard_map/pallas_call | solution.py:368
  2.0 0.0 copy-start
  2.0 5.3 %all-to-all-start = ((bf16[4,32,1280]{2,1,0:T(8,128)(2,1)}), bf16[4,32,1280]{2,1,0:T(8,128)(2,1)S(1)}, u32[]{:S(2)}, u32[]{:S(2)}) async-start(bf16[4,32,1280]{2,1,0:T(8,128)(2,1)} %get-tuple-element.18), calls=%async_computation | async-start | bytes 655360 | tf_op jit(solution)/shard_map/all_to_all | solution.py:377
  7.3 0.0 copy-done
  7.3 0.0 copy-start.1
  7.3 0.0 copy-start.2
  7.3 0.8 %collective-permute-start.4 = (bf16[64,1024]{1,0:T(8,128)(2,1)S(1)}, bf16[64,1024]{1,0:T(8,128)(2,1)S(1)}, u32[]{:S(2)}, u32[]{:S(2)}) collective-permute-start(bf16[64,1024]{1,0:T(8,128)(2,1)S(1)} %bitcast.3), channel_id=1, source_target_pairs={{1,2},{3,4},{5,6},{2,1},{4,3},{6,5},{9,10},{11,12},{13,14},{10,9},... | collective-permute-start | bytes 393224 | tf_op jit(solution)/shard_map/ppermute | solution.py:329
  8.1 2.9 %collective-permute-start.5 = (bf16[64,1024]{1,0:T(8,128)(2,1)S(1)}, bf16[64,1024]{1,0:T(8,128)(2,1)S(1)}, u32[]{:S(2)}, u32[]{:S(2)}) collective-permute-start(bf16[64,1024]{1,0:T(8,128)(2,1)S(1)} %bitcast.4), channel_id=1, source_target_pairs={{0,2},{1,3},{4,6},{5,7},{2,0},{3,1},{6,4},{7,5},{8,10},{9,11},{12,... | collective-permute-start | bytes 393224 | tf_op jit(solution)/shard_map/ppermute | solution.py:329
  11.0 0.7 %collective-permute-start.6 = (bf16[64,1024]{1,0:T(8,128)(2,1)S(1)}, bf16[64,1024]{1,0:T(8,128)(2,1)S(1)}, u32[]{:S(2)}, u32[]{:S(2)}) collective-permute-start(bf16[64,1024]{1,0:T(8,128)(2,1)S(1)} %bitcast.5), channel_id=1, source_target_pairs={{2,4},{3,5},{4,2},{5,3},{10,12},{11,13},{12,10},{13,11},{18,20},{1... | collective-permute-start | bytes 393224 | tf_op jit(solution)/shard_map/ppermute | solution.py:329
  11.7 1.5 %collective-permute-start.7 = (bf16[64,1024]{1,0:T(8,128)(2,1)S(1)}, bf16[64,1024]{1,0:T(8,128)(2,1)S(1)}, u32[]{:S(2)}, u32[]{:S(2)}) collective-permute-start(bf16[64,1024]{1,0:T(8,128)(2,1)S(1)} %bitcast.6), channel_id=1, source_target_pairs={{0,1},{2,3},{4,5},{6,7},{1,0},{3,2},{5,4},{7,6},{8,9},{10,11},{12,... | collective-permute-start | bytes 393224 | tf_op jit(solution)/shard_map/ppermute | solution.py:329
  13.2 0.0 all-to-all-done.own
  13.2 0.1 collective-permute-start
  13.3 0.0 collective-permute-done.4.cross
  13.3 0.7 %collective-permute-start.1 = (bf16[80,1152]{1,0:T(8,128)(2,1)S(1)}, bf16[80,1152]{1,0:T(8,128)(2,1)S(1)}, u32[]{:S(2)}, u32[]{:S(2)}) collective-permute-start(bf16[80,1152]{1,0:T(8,128)(2,1)S(1)} %get-tuple-element.20), channel_id=1, source_target_pairs={{1,2},{3,4},{5,6},{2,1},{4,3},{6,5},{9,10},{11,12},{13,14},{10,9},... | collective-permute-start | bytes 552968 | tf_op jit(solution)/shard_map/ppermute | solution.py:329
  14.0 2.7 %collective-permute-done.5.far_even = bf16[64,1024]{1,0:T(8,128)(2,1)S(1)} collective-permute-done((bf16[64,1024]{1,0:T(8,128)(2,1)S(1)}, bf16[64,1024]{1,0:T(8,128)(2,1)S(1)}, u32[]{:S(2)}, u32[]{:S(2)}) %collective-permute-start.5) | collective-permute-done | bytes 131104 | tf_op jit(solution)/shard_map/ppermute | solution.py:329
  16.7 2.1 %collective-permute-start.2 = (bf16[16,1152]{1,0:T(8,128)(2,1)S(1)}, bf16[16,1152]{1,0:T(8,128)(2,1)S(1)}, u32[]{:S(2)}, u32[]{:S(2)}) collective-permute-start(bf16[16,1152]{1,0:T(8,128)(2,1)S(1)} %get-tuple-element.21), channel_id=1, source_target_pairs={{0,2},{1,3},{4,6},{5,7},{2,0},{3,1},{6,4},{7,5},{8,10},{9,11},{12,... | collective-permute-start | bytes 110600 | tf_op jit(solution)/shard_map/ppermute | solution.py:329
  18.8 0.0 collective-permute-done.6.far_odd
  18.8 0.0 copy-start.3
  18.8 0.8 %collective-permute-start.3 = (bf16[16,1152]{1,0:T(8,128)(2,1)S(1)}, bf16[16,1152]{1,0:T(8,128)(2,1)S(1)}, u32[]{:S(2)}, u32[]{:S(2)}) collective-permute-start(bf16[16,1152]{1,0:T(8,128)(2,1)S(1)} %get-tuple-element.22), channel_id=1, source_target_pairs={{2,4},{3,5},{4,2},{5,3},{10,12},{11,13},{12,10},{13,11},{18,20},{1... | collective-permute-start | bytes 110600 | tf_op jit(solution)/shard_map/ppermute | solution.py:329
  19.6 0.0 collective-permute-done.7.in_chip
  19.6 0.0 copy-done.1
  19.6 0.0 copy-done.2
  19.6 1.1 %shard_map.102 = (f32[1024,256]{1,0:T(8,128)S(1)}, f32[2,128,1024]{2,1,0:T(8,128)S(1)}, f32[128,1024]{1,0:T(8,128)S(1)}, bf16[3,256,512]{2,1,0:T(8,128)(2,1)S(1)...) custom-call(bf16[4,32,1280]{2,1,0:T(8,128)(2,1)S(1)} %all-to-all-done.own, ...), custom_call_target="tpu_custom_call" | custom-call | flops 1000000000 | bytes 3000000 | tf_op jit(solution)/shard_map/pallas_call | solution.py:383
  20.7 2.2 %collective-permute-done.2.far_even = bf16[16,1152]{1,0:T(8,128)(2,1)S(1)} collective-permute-done((bf16[16,1152]{1,0:T(8,128)(2,1)S(1)}, bf16[16,1152]{1,0:T(8,128)(2,1)S(1)}, u32[]{:S(2)}, u32[]{:S(2)}) %collective-permute-start.2) | collective-permute-done | bytes 36896 | tf_op jit(solution)/shard_map/ppermute | solution.py:329
  23.0 0.0 collective-permute-done.3.far_odd
  23.0 0.0 collective-permute-done.in_chip
  23.0 0.0 collective-permute-done.1.cross
  23.0 0.0 copy-done.3
  23.0 2.5 %shard_map.103 = bf16[4,2,32,1024]{3,2,1,0:T(8,128)(2,1)S(1)} custom-call(bf16[80,1152]{1,0:T(8,128)(2,1)S(1)} %collective-permute-done.in_chip, bf16[80,1152]{1,0:T(8,128)(2,1)S(1)} %collective-permute-done.1.cross, bf16[16,1152]{1,0:T(8,128)(2,1)S(1)} %collective-permute-done.2.far_even, bf16[16,1152]{1,0:T(8,128)(2,1)S(1)} %collective-permute-done.3.far_odd, ...), custom_call_target="tpu_custom_call" | custom-call | flops 2000000000 | bytes 3000000 | tf_op jit(solution)/shard_map/pallas_call | solution.py:397
  25.4 12.1 %all_to_all.10 = bf16[4,2,32,1024]{3,2,1,0:T(8,128)(2,1)S(1)} all-to-all(bf16[4,2,32,1024]{3,2,1,0:T(8,128)(2,1)S(1)} %shard_map.103), channel_id=1, replica_groups=mesh['depth'=4,'rows'=8] {'depth'}, dimensions={0} | all-to-all | bytes 1048576 | tf_op jit(solution)/shard_map/all_to_all | solution.py:405
  37.5 0.8 %slice_bitcast_fusion = bf16[1,3,2,32,1024]{4,3,2,1,0:T(8,128)(2,1)} fusion(bf16[4,2,32,1024]{3,2,1,0:T(8,128)(2,1)S(1)} %all_to_all.10), kind=kLoop, calls=%fused_computation | loop fusion | bytes 786432 | tf_op jit(solution)/shard_map/broadcast_in_dim | solution.py:406
  (1 shorter events, 0.0 us)
Async XLA Ops:
  2.0 5.3 %copy-start = (bf16[2,32,1024]{2,1,0:T(8,128)(2,1)S(1)}, bf16[2,32,1024]{2,1,0:T(8,128)(2,1)}, u32[]{:S(2)}) copy-start(bf16[2,32,1024]{2,1,0:T(8,128)(2,1)} %get-tuple-element.23) | copy-start | bytes 393220
  2.0 11.2 %all-to-all-start = ((bf16[4,32,1280]{2,1,0:T(8,128)(2,1)}), bf16[4,32,1280]{2,1,0:T(8,128)(2,1)S(1)}, u32[]{:S(2)}, u32[]{:S(2)}) async-start(bf16[4,32,1280]{2,1,0:T(8,128)(2,1)} %get-tuple-element.18), calls=%async_computation | async-start | bytes 655360 | tf_op jit(solution)/shard_map/all_to_all | solution.py:377
  7.3 12.3 %copy-start.1 = (bf16[256,256]{1,0:T(8,128)(2,1)S(1)}, bf16[256,256]{1,0:T(8,128)(2,1)}, u32[]{:S(2)}) copy-start(bf16[256,256]{1,0:T(8,128)(2,1)} %constant.6.clone.right_tab) | copy-start | bytes 393220
  7.3 12.3 %copy-start.2 = (bf16[256,256]{1,0:T(8,128)(2,1)S(1)}, bf16[256,256]{1,0:T(8,128)(2,1)}, u32[]{:S(2)}) copy-start(bf16[256,256]{1,0:T(8,128)(2,1)} %constant.7.clone.left_tab) | copy-start | bytes 393220
  7.3 6.0 %collective-permute-start.4 = (bf16[64,1024]{1,0:T(8,128)(2,1)S(1)}, bf16[64,1024]{1,0:T(8,128)(2,1)S(1)}, u32[]{:S(2)}, u32[]{:S(2)}) collective-permute-start(bf16[64,1024]{1,0:T(8,128)(2,1)S(1)} %bitcast.3), channel_id=1, source_target_pairs={{1,2},{3,4},{5,6},{2,1},{4,3},{6,5},{9,10},{11,12},{13,14},{10,9},... | collective-permute-start | bytes 393224 | tf_op jit(solution)/shard_map/ppermute | solution.py:329
  8.1 8.6 %collective-permute-start.5 = (bf16[64,1024]{1,0:T(8,128)(2,1)S(1)}, bf16[64,1024]{1,0:T(8,128)(2,1)S(1)}, u32[]{:S(2)}, u32[]{:S(2)}) collective-permute-start(bf16[64,1024]{1,0:T(8,128)(2,1)S(1)} %bitcast.4), channel_id=1, source_target_pairs={{0,2},{1,3},{4,6},{5,7},{2,0},{3,1},{6,4},{7,5},{8,10},{9,11},{12,... | collective-permute-start | bytes 393224 | tf_op jit(solution)/shard_map/ppermute | solution.py:329
  11.0 7.7 %collective-permute-start.6 = (bf16[64,1024]{1,0:T(8,128)(2,1)S(1)}, bf16[64,1024]{1,0:T(8,128)(2,1)S(1)}, u32[]{:S(2)}, u32[]{:S(2)}) collective-permute-start(bf16[64,1024]{1,0:T(8,128)(2,1)S(1)} %bitcast.5), channel_id=1, source_target_pairs={{2,4},{3,5},{4,2},{5,3},{10,12},{11,13},{12,10},{13,11},{18,20},{1... | collective-permute-start | bytes 393224 | tf_op jit(solution)/shard_map/ppermute | solution.py:329
  11.7 7.9 %collective-permute-start.7 = (bf16[64,1024]{1,0:T(8,128)(2,1)S(1)}, bf16[64,1024]{1,0:T(8,128)(2,1)S(1)}, u32[]{:S(2)}, u32[]{:S(2)}) collective-permute-start(bf16[64,1024]{1,0:T(8,128)(2,1)S(1)} %bitcast.6), channel_id=1, source_target_pairs={{0,1},{2,3},{4,5},{6,7},{1,0},{3,2},{5,4},{7,6},{8,9},{10,11},{12,... | collective-permute-start | bytes 393224 | tf_op jit(solution)/shard_map/ppermute | solution.py:329
  13.2 9.7 %collective-permute-start = (bf16[80,1152]{1,0:T(8,128)(2,1)S(1)}, bf16[80,1152]{1,0:T(8,128)(2,1)S(1)}, u32[]{:S(2)}, u32[]{:S(2)}) collective-permute-start(bf16[80,1152]{1,0:T(8,128)(2,1)S(1)} %get-tuple-element.19), channel_id=1, source_target_pairs={{0,1},{2,3},{4,5},{6,7},{1,0},{3,2},{5,4},{7,6},{8,9},{10,11},{12,... | collective-permute-start | bytes 552968 | tf_op jit(solution)/shard_map/ppermute | solution.py:329
  13.3 9.6 %collective-permute-start.1 = (bf16[80,1152]{1,0:T(8,128)(2,1)S(1)}, bf16[80,1152]{1,0:T(8,128)(2,1)S(1)}, u32[]{:S(2)}, u32[]{:S(2)}) collective-permute-start(bf16[80,1152]{1,0:T(8,128)(2,1)S(1)} %get-tuple-element.20), channel_id=1, source_target_pairs={{1,2},{3,4},{5,6},{2,1},{4,3},{6,5},{9,10},{11,12},{13,14},{10,9},... | collective-permute-start | bytes 552968 | tf_op jit(solution)/shard_map/ppermute | solution.py:329
  16.7 6.3 %collective-permute-start.2 = (bf16[16,1152]{1,0:T(8,128)(2,1)S(1)}, bf16[16,1152]{1,0:T(8,128)(2,1)S(1)}, u32[]{:S(2)}, u32[]{:S(2)}) collective-permute-start(bf16[16,1152]{1,0:T(8,128)(2,1)S(1)} %get-tuple-element.21), channel_id=1, source_target_pairs={{0,2},{1,3},{4,6},{5,7},{2,0},{3,1},{6,4},{7,5},{8,10},{9,11},{12,... | collective-permute-start | bytes 110600 | tf_op jit(solution)/shard_map/ppermute | solution.py:329
  18.8 4.2 %copy-start.3 = (bf16[192,192]{1,0:T(8,128)(2,1)S(1)}, bf16[192,192]{1,0:T(8,128)(2,1)}, u32[]{:S(2)}) copy-start(bf16[192,192]{1,0:T(8,128)(2,1)} %constant.8.clone.left_tab) | copy-start | bytes 221188
  18.8 4.2 %collective-permute-start.3 = (bf16[16,1152]{1,0:T(8,128)(2,1)S(1)}, bf16[16,1152]{1,0:T(8,128)(2,1)S(1)}, u32[]{:S(2)}, u32[]{:S(2)}) collective-permute-start(bf16[16,1152]{1,0:T(8,128)(2,1)S(1)} %get-tuple-element.22), channel_id=1, source_target_pairs={{2,4},{3,5},{4,2},{5,3},{10,12},{11,13},{12,10},{13,11},{18,20},{1... | collective-permute-start | bytes 110600 | tf_op jit(solution)/shard_map/ppermute | solution.py:329

commit v12 on v8

--- a/solution.py
+++ b/solution.py
@@ -238,7 +238,7 @@
 
 
 def prepare_kernel(
-    own, incident, in_chip, cross, far_even, far_odd, left_tab, right_tab,
+    own, incident, far_odd, far_even, cross, in_chip, left_tab, right_tab,
     first, stereo, clear, col_mats, *row_mats
 ):
     low_near, high_near, low_far, high_far = ordered(in_chip, cross, far_even, far_odd)
@@ -331,9 +331,9 @@
 
 def neighbours(sent):
     in_chip, cross, far_even, far_odd = sent
+    far_odd = exchanged(far_odd, "rows", 2, 1)
+    far_even = exchanged(far_even, "rows", 2, 0)
     cross = exchanged(cross, "rows", 1, 1)
-    far_even = exchanged(far_even, "rows", 2, 0)
-    far_odd = exchanged(far_odd, "rows", 2, 1)
     in_chip = exchanged(in_chip, "rows", 1, 0)
     return in_chip, cross, far_even, far_odd
 
@@ -375,7 +375,7 @@
     )(hogel_light, silhouette, fill_counts, hogel_index, row_taps, col_taps, incident)
     mine = mine.reshape(2 * BAND, COLS)
     own = lax.all_to_all(payload, "depth", 0, 0, tiled=True)
-    arrived = neighbours((mine,) * 4)
+    arrived = neighbours((mine,) * 4)[::-1]
     near = shaped((NEAR, HALO_W), bf16)
     far = shaped((FAR, HALO_W), bf16)
     halos = neighbours(call(halo_kernel, (near, near, far, far), [vmem])(own))

time: 38.6 us -> 38.8 us (level)
  starting transfers between devices: 16.3 us -> 17.6 us
  waiting for transfers between devices: 3.3 us -> 2.33 us
    ppermute x8, starting transfers between devices: 11 us -> 12.3 us  [exchanged(): return lax.ppermute(value, axis, pairs)]
    all_to_all x1, waiting for transfers between devices: 1.03 us -> 0.01 us  [body(): own = lax.all_to_all(payload, 'depth', 0, 0, tiled=True)]
where the time goes in v12:
time: 38.8 us; the launch traced here: 38.5 us
  starting transfers between devices  17.6 us (45%)
  blocking collectives  12.1 us (31%)
  Pallas kernels  5.6 us (14%)
  waiting for transfers between devices  2.33 us (6%)
  local copies, waits for them, and re-layouts  0.79 us (2%)
    ppermute x8, starting transfers between devices, exchanged(): return lax.ppermute(value, axis, pairs)  12.3 us
    all_to_all x1, blocking collectives, body(): gathered = lax.all_to_all(result, 'depth', 0, 0, tiled=True)  12.1 us
    all_to_all x1, starting transfers between devices, body(): own = lax.all_to_all(payload, 'depth', 0, 0, tiled=True)  5.31 us
    pallas_call x1, Pallas kernels, body(): call(chain_kernel, shaped((LAYERS, 2, BAND, COLS), bf16), [vmem] * (6 + l...  2.46 us
    ppermute x8, waiting for transfers between devices, exchanged(): return lax.ppermute(value, axis, pairs)  2.33 us
    pallas_call x1, Pallas kernels, body(): call(pack_kernel, (shaped((LAYERS, BAND, FULL_W), bf16), shaped(incident....  1.98 us
    pallas_call x1, Pallas kernels, body(): call(prepare_kernel, [shaped((TILES * layer_height(0), 2 * LANES), f32),...  1.12 us
  transfers between devices with their start and end apart: 9, of which 2 were waited for; matrix products, arithmetic and copies ran while one was open for 0% of the time, Pallas kernels for 3%

profile of v12, /device:TPU:0, one launch (start us, length us, event | category | flops | bytes accessed | tf_op | source)
XLA Modules:
  0.0 38.5 jit_solution(6661377254515283209)
XLA Ops:
  0.0 2.0 %shard_map.100 = (bf16[4,32,1280]{2,1,0:T(8,128)(2,1)}, bf16[2,32,1024]{2,1,0:T(8,128)(2,1)}) custom-call(f32[1,3,32,1024]{3,2,1,0:T(8,128)} %light.1, s32[1,32,64]{2,1,0:T(8,128)} %edges.1, s32[1,2]{1,0:T(1,128)} %counts.1, s32[1,2,64]{2,1,0:T(2,128)} %listed.1, bf16[1,3,2,33]{3,2,1,0:T(2,128)(2,1)} %row_taps.1, bf16[1,3,2,127]{3,2,1,0:T(2,128)(2,1)} %col_taps.1, ...), custom_call_target="tpu_custom_call" | custom-call | flops 10000000 | bytes 1000000 | tf_op jit(solution)/shard_map/pallas_call | solution.py:368
  2.0 0.0 copy-start
  2.0 5.3 %all-to-all-start = ((bf16[4,32,1280]{2,1,0:T(8,128)(2,1)}), bf16[4,32,1280]{2,1,0:T(8,128)(2,1)S(1)}, u32[]{:S(2)}, u32[]{:S(2)}) async-start(bf16[4,32,1280]{2,1,0:T(8,128)(2,1)} %get-tuple-element.18), calls=%async_computation | async-start | bytes 655360 | tf_op jit(solution)/shard_map/all_to_all | solution.py:377
  7.3 0.0 copy-done
  7.3 0.0 copy-start.1
  7.3 0.0 copy-start.2
  7.3 0.8 %collective-permute-start.4 = (bf16[64,1024]{1,0:T(8,128)(2,1)S(1)}, bf16[64,1024]{1,0:T(8,128)(2,1)S(1)}, u32[]{:S(2)}, u32[]{:S(2)}) collective-permute-start(bf16[64,1024]{1,0:T(8,128)(2,1)S(1)} %bitcast.3), channel_id=1, source_target_pairs={{2,4},{3,5},{4,2},{5,3},{10,12},{11,13},{12,10},{13,11},{18,20},{1... | collective-permute-start | bytes 393224 | tf_op jit(solution)/shard_map/ppermute | solution.py:329
  8.1 4.5 %collective-permute-start.5 = (bf16[64,1024]{1,0:T(8,128)(2,1)S(1)}, bf16[64,1024]{1,0:T(8,128)(2,1)S(1)}, u32[]{:S(2)}, u32[]{:S(2)}) collective-permute-start(bf16[64,1024]{1,0:T(8,128)(2,1)S(1)} %bitcast.4), channel_id=1, source_target_pairs={{0,2},{1,3},{4,6},{5,7},{2,0},{3,1},{6,4},{7,5},{8,10},{9,11},{12,... | collective-permute-start | bytes 393224 | tf_op jit(solution)/shard_map/ppermute | solution.py:329
  12.6 0.7 %collective-permute-start.6 = (bf16[64,1024]{1,0:T(8,128)(2,1)S(1)}, bf16[64,1024]{1,0:T(8,128)(2,1)S(1)}, u32[]{:S(2)}, u32[]{:S(2)}) collective-permute-start(bf16[64,1024]{1,0:T(8,128)(2,1)S(1)} %bitcast.5), channel_id=1, source_target_pairs={{1,2},{3,4},{5,6},{2,1},{4,3},{6,5},{9,10},{11,12},{13,14},{10,9},... | collective-permute-start | bytes 393224 | tf_op jit(solution)/shard_map/ppermute | solution.py:329
  13.2 1.4 %collective-permute-start.7 = (bf16[64,1024]{1,0:T(8,128)(2,1)S(1)}, bf16[64,1024]{1,0:T(8,128)(2,1)S(1)}, u32[]{:S(2)}, u32[]{:S(2)}) collective-permute-start(bf16[64,1024]{1,0:T(8,128)(2,1)S(1)} %bitcast.6), channel_id=1, source_target_pairs={{0,1},{2,3},{4,5},{6,7},{1,0},{3,2},{5,4},{7,6},{8,9},{10,11},{12,... | collective-permute-start | bytes 393224 | tf_op jit(solution)/shard_map/ppermute | solution.py:329
  14.7 0.0 all-to-all-done.own
  14.7 0.1 collective-permute-start
  14.8 0.0 collective-permute-done.4.far_odd
  14.8 0.7 %collective-permute-start.1 = (bf16[80,1152]{1,0:T(8,128)(2,1)S(1)}, bf16[80,1152]{1,0:T(8,128)(2,1)S(1)}, u32[]{:S(2)}, u32[]{:S(2)}) collective-permute-start(bf16[80,1152]{1,0:T(8,128)(2,1)S(1)} %get-tuple-element.20), channel_id=1, source_target_pairs={{1,2},{3,4},{5,6},{2,1},{4,3},{6,5},{9,10},{11,12},{13,14},{10,9},... | collective-permute-start | bytes 552968 | tf_op jit(solution)/shard_map/ppermute | solution.py:329
  15.5 0.1 collective-permute-done.5.far_even
  15.6 3.4 %collective-permute-start.2 = (bf16[16,1152]{1,0:T(8,128)(2,1)S(1)}, bf16[16,1152]{1,0:T(8,128)(2,1)S(1)}, u32[]{:S(2)}, u32[]{:S(2)}) collective-permute-start(bf16[16,1152]{1,0:T(8,128)(2,1)S(1)} %get-tuple-element.21), channel_id=1, source_target_pairs={{0,2},{1,3},{4,6},{5,7},{2,0},{3,1},{6,4},{7,5},{8,10},{9,11},{12,... | collective-permute-start | bytes 110600 | tf_op jit(solution)/shard_map/ppermute | solution.py:329
  18.9 0.0 collective-permute-done.6.cross
  18.9 0.0 copy-start.3
  18.9 0.8 %collective-permute-start.3 = (bf16[16,1152]{1,0:T(8,128)(2,1)S(1)}, bf16[16,1152]{1,0:T(8,128)(2,1)S(1)}, u32[]{:S(2)}, u32[]{:S(2)}) collective-permute-start(bf16[16,1152]{1,0:T(8,128)(2,1)S(1)} %get-tuple-element.22), channel_id=1, source_target_pairs={{2,4},{3,5},{4,2},{5,3},{10,12},{11,13},{12,10},{13,11},{18,20},{1... | collective-permute-start | bytes 110600 | tf_op jit(solution)/shard_map/ppermute | solution.py:329
  19.7 0.0 collective-permute-done.7.in_chip
  19.7 0.0 copy-done.1
  19.7 0.0 copy-done.2
  19.8 1.1 %shard_map.102 = (f32[1024,256]{1,0:T(8,128)S(1)}, f32[2,128,1024]{2,1,0:T(8,128)S(1)}, f32[128,1024]{1,0:T(8,128)S(1)}, bf16[3,256,512]{2,1,0:T(8,128)(2,1)S(1)...) custom-call(bf16[4,32,1280]{2,1,0:T(8,128)(2,1)S(1)} %all-to-all-done.own, ...), custom_call_target="tpu_custom_call" | custom-call | flops 1000000000 | bytes 3000000 | tf_op jit(solution)/shard_map/pallas_call | solution.py:383
  20.9 2.2 %collective-permute-done.2.far_even = bf16[16,1152]{1,0:T(8,128)(2,1)S(1)} collective-permute-done((bf16[16,1152]{1,0:T(8,128)(2,1)S(1)}, bf16[16,1152]{1,0:T(8,128)(2,1)S(1)}, u32[]{:S(2)}, u32[]{:S(2)}) %collective-permute-start.2) | collective-permute-done | bytes 36896 | tf_op jit(solution)/shard_map/ppermute | solution.py:329
  23.1 0.0 collective-permute-done.3.far_odd
  23.1 0.0 collective-permute-done.in_chip
  23.1 0.0 collective-permute-done.1.cross
  23.1 0.0 copy-done.3
  23.2 2.5 %shard_map.103 = bf16[4,2,32,1024]{3,2,1,0:T(8,128)(2,1)S(1)} custom-call(bf16[80,1152]{1,0:T(8,128)(2,1)S(1)} %collective-permute-done.in_chip, bf16[80,1152]{1,0:T(8,128)(2,1)S(1)} %collective-permute-done.1.cross, bf16[16,1152]{1,0:T(8,128)(2,1)S(1)} %collective-permute-done.2.far_even, bf16[16,1152]{1,0:T(8,128)(2,1)S(1)} %collective-permute-done.3.far_odd, ...), custom_call_target="tpu_custom_call" | custom-call | flops 2000000000 | bytes 3000000 | tf_op jit(solution)/shard_map/pallas_call | solution.py:397
  25.6 12.1 %all_to_all.10 = bf16[4,2,32,1024]{3,2,1,0:T(8,128)(2,1)S(1)} all-to-all(bf16[4,2,32,1024]{3,2,1,0:T(8,128)(2,1)S(1)} %shard_map.103), channel_id=1, replica_groups=mesh['depth'=4,'rows'=8] {'depth'}, dimensions={0} | all-to-all | bytes 1048576 | tf_op jit(solution)/shard_map/all_to_all | solution.py:405
  37.7 0.8 %slice_bitcast_fusion = bf16[1,3,2,32,1024]{4,3,2,1,0:T(8,128)(2,1)} fusion(bf16[4,2,32,1024]{3,2,1,0:T(8,128)(2,1)S(1)} %all_to_all.10), kind=kLoop, calls=%fused_computation | loop fusion | bytes 786432 | tf_op jit(solution)/shard_map/broadcast_in_dim | solution.py:406
  (1 shorter events, 0.0 us)
Async XLA Ops:
  2.0 5.3 %copy-start = (bf16[2,32,1024]{2,1,0:T(8,128)(2,1)S(1)}, bf16[2,32,1024]{2,1,0:T(8,128)(2,1)}, u32[]{:S(2)}) copy-start(bf16[2,32,1024]{2,1,0:T(8,128)(2,1)} %get-tuple-element.23) | copy-start | bytes 393220
  2.0 12.7 %all-to-all-start = ((bf16[4,32,1280]{2,1,0:T(8,128)(2,1)}), bf16[4,32,1280]{2,1,0:T(8,128)(2,1)S(1)}, u32[]{:S(2)}, u32[]{:S(2)}) async-start(bf16[4,32,1280]{2,1,0:T(8,128)(2,1)} %get-tuple-element.18), calls=%async_computation | async-start | bytes 655360 | tf_op jit(solution)/shard_map/all_to_all | solution.py:377
  7.3 12.4 %copy-start.1 = (bf16[256,256]{1,0:T(8,128)(2,1)S(1)}, bf16[256,256]{1,0:T(8,128)(2,1)}, u32[]{:S(2)}) copy-start(bf16[256,256]{1,0:T(8,128)(2,1)} %constant.6.clone.right_tab) | copy-start | bytes 393220
  7.3 12.4 %copy-start.2 = (bf16[256,256]{1,0:T(8,128)(2,1)S(1)}, bf16[256,256]{1,0:T(8,128)(2,1)}, u32[]{:S(2)}) copy-start(bf16[256,256]{1,0:T(8,128)(2,1)} %constant.7.clone.left_tab) | copy-start | bytes 393220
  7.3 7.5 %collective-permute-start.4 = (bf16[64,1024]{1,0:T(8,128)(2,1)S(1)}, bf16[64,1024]{1,0:T(8,128)(2,1)S(1)}, u32[]{:S(2)}, u32[]{:S(2)}) collective-permute-start(bf16[64,1024]{1,0:T(8,128)(2,1)S(1)} %bitcast.3), channel_id=1, source_target_pairs={{2,4},{3,5},{4,2},{5,3},{10,12},{11,13},{12,10},{13,11},{18,20},{1... | collective-permute-start | bytes 393224 | tf_op jit(solution)/shard_map/ppermute | solution.py:329
  8.1 7.4 %collective-permute-start.5 = (bf16[64,1024]{1,0:T(8,128)(2,1)S(1)}, bf16[64,1024]{1,0:T(8,128)(2,1)S(1)}, u32[]{:S(2)}, u32[]{:S(2)}) collective-permute-start(bf16[64,1024]{1,0:T(8,128)(2,1)S(1)} %bitcast.4), channel_id=1, source_target_pairs={{0,2},{1,3},{4,6},{5,7},{2,0},{3,1},{6,4},{7,5},{8,10},{9,11},{12,... | collective-permute-start | bytes 393224 | tf_op jit(solution)/shard_map/ppermute | solution.py:329
  12.6 6.3 %collective-permute-start.6 = (bf16[64,1024]{1,0:T(8,128)(2,1)S(1)}, bf16[64,1024]{1,0:T(8,128)(2,1)S(1)}, u32[]{:S(2)}, u32[]{:S(2)}) collective-permute-start(bf16[64,1024]{1,0:T(8,128)(2,1)S(1)} %bitcast.5), channel_id=1, source_target_pairs={{1,2},{3,4},{5,6},{2,1},{4,3},{6,5},{9,10},{11,12},{13,14},{10,9},... | collective-permute-start | bytes 393224 | tf_op jit(solution)/shard_map/ppermute | solution.py:329
  13.2 6.5 %collective-permute-start.7 = (bf16[64,1024]{1,0:T(8,128)(2,1)S(1)}, bf16[64,1024]{1,0:T(8,128)(2,1)S(1)}, u32[]{:S(2)}, u32[]{:S(2)}) collective-permute-start(bf16[64,1024]{1,0:T(8,128)(2,1)S(1)} %bitcast.6), channel_id=1, source_target_pairs={{0,1},{2,3},{4,5},{6,7},{1,0},{3,2},{5,4},{7,6},{8,9},{10,11},{12,... | collective-permute-start | bytes 393224 | tf_op jit(solution)/shard_map/ppermute | solution.py:329
  14.7 8.4 %collective-permute-start = (bf16[80,1152]{1,0:T(8,128)(2,1)S(1)}, bf16[80,1152]{1,0:T(8,128)(2,1)S(1)}, u32[]{:S(2)}, u32[]{:S(2)}) collective-permute-start(bf16[80,1152]{1,0:T(8,128)(2,1)S(1)} %get-tuple-element.19), channel_id=1, source_target_pairs={{0,1},{2,3},{4,5},{6,7},{1,0},{3,2},{5,4},{7,6},{8,9},{10,11},{12,... | collective-permute-start | bytes 552968 | tf_op jit(solution)/shard_map/ppermute | solution.py:329
  14.8 8.3 %collective-permute-start.1 = (bf16[80,1152]{1,0:T(8,128)(2,1)S(1)}, bf16[80,1152]{1,0:T(8,128)(2,1)S(1)}, u32[]{:S(2)}, u32[]{:S(2)}) collective-permute-start(bf16[80,1152]{1,0:T(8,128)(2,1)S(1)} %get-tuple-element.20), channel_id=1, source_target_pairs={{1,2},{3,4},{5,6},{2,1},{4,3},{6,5},{9,10},{11,12},{13,14},{10,9},... | collective-permute-start | bytes 552968 | tf_op jit(solution)/shard_map/ppermute | solution.py:329
  15.6 7.6 %collective-permute-start.2 = (bf16[16,1152]{1,0:T(8,128)(2,1)S(1)}, bf16[16,1152]{1,0:T(8,128)(2,1)S(1)}, u32[]{:S(2)}, u32[]{:S(2)}) collective-permute-start(bf16[16,1152]{1,0:T(8,128)(2,1)S(1)} %get-tuple-element.21), channel_id=1, source_target_pairs={{0,2},{1,3},{4,6},{5,7},{2,0},{3,1},{6,4},{7,5},{8,10},{9,11},{12,... | collective-permute-start | bytes 110600 | tf_op jit(solution)/shard_map/ppermute | solution.py:329
  18.9 4.2 %copy-start.3 = (bf16[192,192]{1,0:T(8,128)(2,1)S(1)}, bf16[192,192]{1,0:T(8,128)(2,1)}, u32[]{:S(2)}) copy-start(bf16[192,192]{1,0:T(8,128)(2,1)} %constant.8.clone.left_tab) | copy-start | bytes 221188
  18.9 4.2 %collective-permute-start.3 = (bf16[16,1152]{1,0:T(8,128)(2,1)S(1)}, bf16[16,1152]{1,0:T(8,128)(2,1)S(1)}, u32[]{:S(2)}, u32[]{:S(2)}) collective-permute-start(bf16[16,1152]{1,0:T(8,128)(2,1)S(1)} %get-tuple-element.22), channel_id=1, source_target_pairs={{2,4},{3,5},{4,2},{5,3},{10,12},{11,13},{12,10},{13,11},{18,20},{1... | collective-permute-start | bytes 110600 | tf_op jit(solution)/shard_map/ppermute | solution.py:329

commit v13 on v8

--- a/solution.py
+++ b/solution.py
@@ -267,7 +267,8 @@
 def chain_kernel(
     in_chip, cross, far_even, far_odd, left_tab, right_tab, first, stereo, clear, col_mats, *rest
 ):
-    row_mats, (out, field) = rest[: LAYERS - 1], rest[LAYERS - 1 :]
+    row_mats, outs, field = rest[: LAYERS - 1], rest[LAYERS - 1 : -1], rest[-1]
+    depth = lax.axis_index("depth")
     low_near, high_near, low_far, high_far = ordered(in_chip, cross, far_even, far_odd)
     pieces = [
         low_far,
@@ -318,8 +319,30 @@
                 added = jnp.concatenate(pieces, axis=0)
                 value = passing[:, lanes] * columned[span, within] + added
                 field[part, :height, lanes] = value.astype(jnp.bfloat16)
-        for part in range(2):
-            out[layer, part] = field[part, side : side + BAND]
+        for hop, out in enumerate(outs):
+
+            @pl.when((depth ^ hop) == layer)
+            def keep(out=out, side=side):
+                for part in range(2):
+                    out[part] = field[part, side : side + BAND]
+
+
+def home_kernel(*refs):
+    arrived, out, sems = refs[:LAYERS], refs[LAYERS], refs[LAYERS + 1]
+    depth = lax.axis_index("depth")
+    for colour in range(COLORS):
+        for hop in range(LAYERS):
+
+            @pl.when((depth ^ hop) == colour)
+            def begin(hop=hop, colour=colour):
+                pltpu.make_async_copy(arrived[hop], out.at[0, colour], sems.at[colour]).start()
+
+    for colour in range(COLORS):
+        pltpu.make_async_copy(arrived[0], out.at[0, colour], sems.at[colour]).wait()
+
+
+def sent_home(value, hop):
+    return lax.ppermute(value, "depth", [(i, i ^ hop) for i in range(COLORS)])
 
 
 def exchanged(value, axis, by, phase):
@@ -338,8 +361,11 @@
     return in_chip, cross, far_even, far_odd
 
 
-def call(kernel, out_shape, in_specs, scratch=(), flops=0, moved=10**6, limit=VMEM_LIMIT):
-    vmem = pl.BlockSpec(memory_space=pltpu.VMEM)
+def call(
+    kernel, out_shape, in_specs, scratch=(), flops=0, moved=10**6, limit=VMEM_LIMIT,
+    out_space=pltpu.VMEM,
+):
+    vmem = pl.BlockSpec(memory_space=out_space)
     many = isinstance(out_shape, (tuple, list))
     return pl.pallas_call(
         kernel,
@@ -394,16 +420,24 @@
         moved=3 * 10**6,
     )(own, mine, *arrived, jnp.asarray(left_table(LANES)), right_tab)
     halo_rows = NEAR + FAR
-    result = call(
+    results = call(
         chain_kernel,
-        shaped((LAYERS, 2, BAND, COLS), bf16),
+        [shaped((2, BAND, COLS), bf16)] * LAYERS,
         [vmem] * (6 + len(made)),
         [pltpu.VMEM((2, layer_height(0), COLS), bf16)],
         flops=2 * 10**9,
         moved=3 * 10**6,
     )(*halos, jnp.asarray(left_table(halo_rows)), right_tab, *made)
-    gathered = lax.all_to_all(result, "depth", 0, 0, tiled=True)
-    return gathered[None, :COLORS]
+    diagonal = sent_home(results[3], 3)
+    along_x = sent_home(results[1], 1)
+    along_y = sent_home(results[2], 2)
+    return call(
+        home_kernel,
+        shaped((1, COLORS, 2, BAND, COLS), bf16),
+        [vmem] * LAYERS,
+        [pltpu.SemaphoreType.DMA((COLORS,))],
+        out_space=pltpu.HBM,
+    )(results[0], along_x, along_y, diagonal)
 
 
 def solution(mesh):

time: 38.6 us -> 41 us (1.062)
  blocking collectives: 12.1 us -> 0 us
  starting transfers between devices: 16.3 us -> 25.5 us
  waiting for transfers between devices: 3.3 us -> 8.23 us
  Pallas kernels: 5.6 us -> 6.63 us
  local copies, waits for them, and re-layouts: 0.79 us -> 0.02 us
    all_to_all x1 -> x0, blocking collectives: 12.1 us -> none  [body(): gathered = lax.all_to_all(result, 'depth', 0, 0, tiled=True)]
    ppermute x0 -> x3, starting transfers between devices: none -> 9.21 us  [sent_home(): return lax.ppermute(value, 'depth', [(i, i ^ hop) for i in range(COLORS)])]
    ppermute x0 -> x3, waiting for transfers between devices: none -> 4.92 us  [sent_home(): return lax.ppermute(value, 'depth', [(i, i ^ hop) for i in range(COLORS)])]
    pallas_call x1 -> x2, Pallas kernels: 2.46 us -> 3.5 us  [the longest x1 2.74 us: body(): call(chain_kernel, [shaped((2, BAND, COLS), bf16)] * LAYERS, [vmem] * (6...]
    broadcast_in_dim x1 -> x0, local copies, waits for them, and re-layouts: 0.77 us -> none  [body(): return gathered[None, :COLORS]]
  transfers between devices with their start and end apart: 9 -> 12, of which waited for: 2 -> 4; matrix products, arithmetic and copies ran while one was open for 0% -> 0% of each run, Pallas kernels for 3% -> 3%
where the time goes in v13:
time: 41 us; the launch traced here: 40.6 us
  starting transfers between devices  25.5 us (62%)
  waiting for transfers between devices  8.23 us (20%)
  Pallas kernels  6.63 us (16%)
    ppermute x8, starting transfers between devices, exchanged(): return lax.ppermute(value, axis, pairs)  11 us
    ppermute x3, starting transfers between devices, sent_home(): return lax.ppermute(value, 'depth', [(i, i ^ hop) for i in range(COLORS)])  9.21 us
    all_to_all x1, starting transfers between devices, body(): own = lax.all_to_all(payload, 'depth', 0, 0, tiled=True)  5.31 us
    ppermute x3, waiting for transfers between devices, sent_home(): return lax.ppermute(value, 'depth', [(i, i ^ hop) for i in range(COLORS)])  4.92 us
    pallas_call x1, Pallas kernels, body(): call(chain_kernel, [shaped((2, BAND, COLS), bf16)] * LAYERS, [vmem] * (6...  2.74 us
    ppermute x8, waiting for transfers between devices, exchanged(): return lax.ppermute(value, axis, pairs)  2.27 us
    pallas_call x1, Pallas kernels, body(): call(pack_kernel, (shaped((LAYERS, BAND, FULL_W), bf16), shaped(incident....  1.97 us
    pallas_call x1, Pallas kernels, body(): call(prepare_kernel, [shaped((TILES * layer_height(0), 2 * LANES), f32),...  1.13 us
  transfers between devices with their start and end apart: 12, of which 4 were waited for; matrix products, arithmetic and copies ran while one was open for 0% of the time, Pallas kernels for 3%

profile of v13, /device:TPU:0, one launch (start us, length us, event | category | flops | bytes accessed | tf_op | source)
XLA Modules:
  0.0 40.6 jit_solution(18339262306777471324)
XLA Ops:
  0.0 2.0 %shard_map.100 = (bf16[4,32,1280]{2,1,0:T(8,128)(2,1)}, bf16[2,32,1024]{2,1,0:T(8,128)(2,1)}) custom-call(f32[1,3,32,1024]{3,2,1,0:T(8,128)} %light.1, s32[1,32,64]{2,1,0:T(8,128)} %edges.1, s32[1,2]{1,0:T(1,128)} %counts.1, s32[1,2,64]{2,1,0:T(2,128)} %listed.1, bf16[1,3,2,33]{3,2,1,0:T(2,128)(2,1)} %row_taps.1, bf16[1,3,2,127]{3,2,1,0:T(2,128)(2,1)} %col_taps.1, ...), custom_call_target="tpu_custom_call" | custom-call | flops 10000000 | bytes 1000000 | tf_op jit(solution)/shard_map/pallas_call | solution.py:394
  2.0 0.0 copy-start
  2.0 5.3 %all-to-all-start = ((bf16[4,32,1280]{2,1,0:T(8,128)(2,1)}), bf16[4,32,1280]{2,1,0:T(8,128)(2,1)S(1)}, u32[]{:S(2)}, u32[]{:S(2)}) async-start(bf16[4,32,1280]{2,1,0:T(8,128)(2,1)} %get-tuple-element.22), calls=%async_computation | async-start | bytes 655360 | tf_op jit(solution)/shard_map/all_to_all | solution.py:403
  7.3 0.0 copy-done
  7.3 0.0 copy-start.1
  7.3 0.0 copy-start.2
  7.3 0.1 collective-permute-start.4
  7.4 0.8 %collective-permute-start.5 = (bf16[64,1024]{1,0:T(8,128)(2,1)S(1)}, bf16[64,1024]{1,0:T(8,128)(2,1)S(1)}, u32[]{:S(2)}, u32[]{:S(2)}) collective-permute-start(bf16[64,1024]{1,0:T(8,128)(2,1)S(1)} %bitcast.2), channel_id=1, source_target_pairs={{1,2},{3,4},{5,6},{2,1},{4,3},{6,5},{9,10},{11,12},{13,14},{10,9},... | collective-permute-start | bytes 393224 | tf_op jit(solution)/shard_map/ppermute | solution.py:352
  8.2 3.3 %collective-permute-start.6 = (bf16[64,1024]{1,0:T(8,128)(2,1)S(1)}, bf16[64,1024]{1,0:T(8,128)(2,1)S(1)}, u32[]{:S(2)}, u32[]{:S(2)}) collective-permute-start(bf16[64,1024]{1,0:T(8,128)(2,1)S(1)} %bitcast.3), channel_id=1, source_target_pairs={{0,2},{1,3},{4,6},{5,7},{2,0},{3,1},{6,4},{7,5},{8,10},{9,11},{12,... | collective-permute-start | bytes 393224 | tf_op jit(solution)/shard_map/ppermute | solution.py:352
  11.5 0.7 %collective-permute-start.7 = (bf16[64,1024]{1,0:T(8,128)(2,1)S(1)}, bf16[64,1024]{1,0:T(8,128)(2,1)S(1)}, u32[]{:S(2)}, u32[]{:S(2)}) collective-permute-start(bf16[64,1024]{1,0:T(8,128)(2,1)S(1)} %bitcast.4), channel_id=1, source_target_pairs={{2,4},{3,5},{4,2},{5,3},{10,12},{11,13},{12,10},{13,11},{18,20},{1... | collective-permute-start | bytes 393224 | tf_op jit(solution)/shard_map/ppermute | solution.py:352
  12.2 1.0 %all-to-all-done.own = bf16[4,32,1280]{2,1,0:T(8,128)(2,1)S(1)} async-done(((bf16[4,32,1280]{2,1,0:T(8,128)(2,1)}), bf16[4,32,1280]{2,1,0:T(8,128)(2,1)S(1)}, u32[]{:S(2)}, u32[]{:S(2)}) %all-to-all-start) | async-done | bytes 327712 | tf_op jit(solution)/shard_map/all_to_all | solution.py:403
  13.2 0.1 collective-permute-start
  13.3 0.0 collective-permute-done.4.in_chip
  13.3 0.7 %collective-permute-start.1 = (bf16[80,1152]{1,0:T(8,128)(2,1)S(1)}, bf16[80,1152]{1,0:T(8,128)(2,1)S(1)}, u32[]{:S(2)}, u32[]{:S(2)}) collective-permute-start(bf16[80,1152]{1,0:T(8,128)(2,1)S(1)} %get-tuple-element.24), channel_id=1, source_target_pairs={{1,2},{3,4},{5,6},{2,1},{4,3},{6,5},{9,10},{11,12},{13,14},{10,9},... | collective-permute-start | bytes 552968 | tf_op jit(solution)/shard_map/ppermute | solution.py:352
  14.0 0.0 collective-permute-done.5.cross
  14.0 4.7 %collective-permute-start.2 = (bf16[16,1152]{1,0:T(8,128)(2,1)S(1)}, bf16[16,1152]{1,0:T(8,128)(2,1)S(1)}, u32[]{:S(2)}, u32[]{:S(2)}) collective-permute-start(bf16[16,1152]{1,0:T(8,128)(2,1)S(1)} %get-tuple-element.25), channel_id=1, source_target_pairs={{0,2},{1,3},{4,6},{5,7},{2,0},{3,1},{6,4},{7,5},{8,10},{9,11},{12,... | collective-permute-start | bytes 110600 | tf_op jit(solution)/shard_map/ppermute | solution.py:352
  18.7 0.0 collective-permute-done.6.far_even
  18.7 0.0 copy-start.3
  18.7 0.8 %collective-permute-start.3 = (bf16[16,1152]{1,0:T(8,128)(2,1)S(1)}, bf16[16,1152]{1,0:T(8,128)(2,1)S(1)}, u32[]{:S(2)}, u32[]{:S(2)}) collective-permute-start(bf16[16,1152]{1,0:T(8,128)(2,1)S(1)} %get-tuple-element.26), channel_id=1, source_target_pairs={{2,4},{3,5},{4,2},{5,3},{10,12},{11,13},{12,10},{13,11},{18,20},{1... | collective-permute-start | bytes 110600 | tf_op jit(solution)/shard_map/ppermute | solution.py:352
  19.5 0.0 collective-permute-done.7.far_odd
  19.5 0.0 copy-done.1
  19.5 0.0 copy-done.2
  19.5 1.1 %shard_map.102 = (f32[1024,256]{1,0:T(8,128)S(1)}, f32[2,128,1024]{2,1,0:T(8,128)S(1)}, f32[128,1024]{1,0:T(8,128)S(1)}, bf16[3,256,512]{2,1,0:T(8,128)(2,1)S(1)...) custom-call(bf16[4,32,1280]{2,1,0:T(8,128)(2,1)S(1)} %all-to-all-done.own, ...), custom_call_target="tpu_custom_call" | custom-call | flops 1000000000 | bytes 3000000 | tf_op jit(solution)/shard_map/pallas_call | solution.py:409
  20.6 2.2 %collective-permute-done.2.far_even = bf16[16,1152]{1,0:T(8,128)(2,1)S(1)} collective-permute-done((bf16[16,1152]{1,0:T(8,128)(2,1)S(1)}, bf16[16,1152]{1,0:T(8,128)(2,1)S(1)}, u32[]{:S(2)}, u32[]{:S(2)}) %collective-permute-start.2) | collective-permute-done | bytes 36896 | tf_op jit(solution)/shard_map/ppermute | solution.py:352
  22.9 0.0 collective-permute-done.3.far_odd
  22.9 0.0 collective-permute-done.in_chip
  22.9 0.0 collective-permute-done.1.cross
  22.9 0.0 copy-done.3
  22.9 2.7 %shard_map.103 = (bf16[2,32,1024]{2,1,0:T(8,128)(2,1)S(1)}, bf16[2,32,1024]{2,1,0:T(8,128)(2,1)S(1)}, bf16[2,32,1024]{2,1,0:T(8,128)(2,1)S(1)}, bf16[2,32,1024]{2,1,0:T(8,128)(2,1)S(1)}) custom-call(bf16[80,1152]{1,0:T(8,128)(2,1)S(1)} %collective-permute-done.in_chip, bf16[80,1152]{1,0:T(8,128)(2,1)S(1)} %collective-permute-done.1.cross, ...), custom_call_target="tpu_custom_call" | custom-call | flops 2000000000 | bytes 3000000 | tf_op jit(solution)/shard_map/pallas_call | solution.py:423
  25.7 4.8 %collective-permute-start.10 = (bf16[2,32,1024]{2,1,0:T(8,128)(2,1)S(1)}, bf16[2,32,1024]{2,1,0:T(8,128)(2,1)S(1)}, u32[]{:S(2)}, u32[]{:S(2)}) collective-permute-start(bf16[2,32,1024]{2,1,0:T(8,128)(2,1)S(1)} %get-tuple-element.38), channel_id=1, source_target_pairs={{0,24},{8,16},{16,8},{1,25},{9,17},{17,9},{2,26},{10,18},{18,10},{... | collective-permute-start | bytes 393224 | tf_op jit(solution)/shard_map/ppermute | solution.py:345
  30.5 2.5 %collective-permute-start.8 = (bf16[2,32,1024]{2,1,0:T(8,128)(2,1)S(1)}, bf16[2,32,1024]{2,1,0:T(8,128)(2,1)S(1)}, u32[]{:S(2)}, u32[]{:S(2)}) collective-permute-start(bf16[2,32,1024]{2,1,0:T(8,128)(2,1)S(1)} %get-tuple-element.36), channel_id=1, source_target_pairs={{0,8},{8,0},{16,24},{1,9},{9,1},{17,25},{2,10},{10,2},{18,26},{3,1... | collective-permute-start | bytes 393224 | tf_op jit(solution)/shard_map/ppermute | solution.py:345
  33.0 1.9 %collective-permute-start.9 = (bf16[2,32,1024]{2,1,0:T(8,128)(2,1)S(1)}, bf16[2,32,1024]{2,1,0:T(8,128)(2,1)S(1)}, u32[]{:S(2)}, u32[]{:S(2)}) collective-permute-start(bf16[2,32,1024]{2,1,0:T(8,128)(2,1)S(1)} %get-tuple-element.37), channel_id=1, source_target_pairs={{0,16},{8,24},{16,0},{1,17},{9,25},{17,1},{2,18},{10,26},{18,2},{3... | collective-permute-start | bytes 393224 | tf_op jit(solution)/shard_map/ppermute | solution.py:345
  34.9 0.0 collective-permute-done.10.refs_3_
  34.9 2.5 %collective-permute-done.8.refs_1_ = bf16[2,32,1024]{2,1,0:T(8,128)(2,1)S(1)} collective-permute-done((bf16[2,32,1024]{2,1,0:T(8,128)(2,1)S(1)}, bf16[2,32,1024]{2,1,0:T(8,128)(2,1)S(1)}, u32[]{:S(2)}, u32[]{:S(2)}) %collective-permute-start.8) | collective-permute-done | bytes 131104 | tf_op jit(solution)/shard_map/ppermute | solution.py:345
  37.4 2.5 %collective-permute-done.9.refs_2_ = bf16[2,32,1024]{2,1,0:T(8,128)(2,1)S(1)} collective-permute-done((bf16[2,32,1024]{2,1,0:T(8,128)(2,1)S(1)}, bf16[2,32,1024]{2,1,0:T(8,128)(2,1)S(1)}, u32[]{:S(2)}, u32[]{:S(2)}) %collective-permute-start.9) | collective-permute-done | bytes 131104 | tf_op jit(solution)/shard_map/ppermute | solution.py:345
  39.8 0.8 %shard_map.104 = bf16[1,3,2,32,1024]{4,3,2,1,0:T(8,128)(2,1)} custom-call(bf16[2,32,1024]{2,1,0:T(8,128)(2,1)S(1)} %get-tuple-element.35.refs_0_, bf16[2,32,1024]{2,1,0:T(8,128)(2,1)S(1)} %collective-permute-done.8.refs_1_, bf16[2,32,1024]{2,1,0:T(8,128)(2,1)S(1)} %collective-permute-done.9.refs_2_, bf16[2,32,1024]{2,1,0:T(8,128)(2,1)S(1)} %collective-permute-done.10.refs_3_), custom_call_target="tpu_custom_call" | custom-call | bytes 1000000 | tf_op jit(solution)/shard_map/pallas_call | solution.py:434
  (1 shorter events, 0.0 us)
Async XLA Ops:
  2.0 5.3 %copy-start = (bf16[2,32,1024]{2,1,0:T(8,128)(2,1)S(1)}, bf16[2,32,1024]{2,1,0:T(8,128)(2,1)}, u32[]{:S(2)}) copy-start(bf16[2,32,1024]{2,1,0:T(8,128)(2,1)} %get-tuple-element.27) | copy-start | bytes 393220
  2.0 11.2 %all-to-all-start = ((bf16[4,32,1280]{2,1,0:T(8,128)(2,1)}), bf16[4,32,1280]{2,1,0:T(8,128)(2,1)S(1)}, u32[]{:S(2)}, u32[]{:S(2)}) async-start(bf16[4,32,1280]{2,1,0:T(8,128)(2,1)} %get-tuple-element.22), calls=%async_computation | async-start | bytes 655360 | tf_op jit(solution)/shard_map/all_to_all | solution.py:403
  7.3 12.2 %copy-start.1 = (bf16[256,256]{1,0:T(8,128)(2,1)S(1)}, bf16[256,256]{1,0:T(8,128)(2,1)}, u32[]{:S(2)}) copy-start(bf16[256,256]{1,0:T(8,128)(2,1)} %constant.6.clone.right_tab) | copy-start | bytes 393220
  7.3 12.2 %copy-start.2 = (bf16[256,256]{1,0:T(8,128)(2,1)S(1)}, bf16[256,256]{1,0:T(8,128)(2,1)}, u32[]{:S(2)}) copy-start(bf16[256,256]{1,0:T(8,128)(2,1)} %constant.7.clone.left_tab) | copy-start | bytes 393220
  7.3 6.0 %collective-permute-start.4 = (bf16[64,1024]{1,0:T(8,128)(2,1)S(1)}, bf16[64,1024]{1,0:T(8,128)(2,1)S(1)}, u32[]{:S(2)}, u32[]{:S(2)}) collective-permute-start(bf16[64,1024]{1,0:T(8,128)(2,1)S(1)} %bitcast.1), channel_id=1, source_target_pairs={{0,1},{2,3},{4,5},{6,7},{1,0},{3,2},{5,4},{7,6},{8,9},{10,11},{12,... | collective-permute-start | bytes 393224 | tf_op jit(solution)/shard_map/ppermute | solution.py:352
  7.4 6.6 %collective-permute-start.5 = (bf16[64,1024]{1,0:T(8,128)(2,1)S(1)}, bf16[64,1024]{1,0:T(8,128)(2,1)S(1)}, u32[]{:S(2)}, u32[]{:S(2)}) collective-permute-start(bf16[64,1024]{1,0:T(8,128)(2,1)S(1)} %bitcast.2), channel_id=1, source_target_pairs={{1,2},{3,4},{5,6},{2,1},{4,3},{6,5},{9,10},{11,12},{13,14},{10,9},... | collective-permute-start | bytes 393224 | tf_op jit(solution)/shard_map/ppermute | solution.py:352
  8.2 10.5 %collective-permute-start.6 = (bf16[64,1024]{1,0:T(8,128)(2,1)S(1)}, bf16[64,1024]{1,0:T(8,128)(2,1)S(1)}, u32[]{:S(2)}, u32[]{:S(2)}) collective-permute-start(bf16[64,1024]{1,0:T(8,128)(2,1)S(1)} %bitcast.3), channel_id=1, source_target_pairs={{0,2},{1,3},{4,6},{5,7},{2,0},{3,1},{6,4},{7,5},{8,10},{9,11},{12,... | collective-permute-start | bytes 393224 | tf_op jit(solution)/shard_map/ppermute | solution.py:352
  11.5 8.0 %collective-permute-start.7 = (bf16[64,1024]{1,0:T(8,128)(2,1)S(1)}, bf16[64,1024]{1,0:T(8,128)(2,1)S(1)}, u32[]{:S(2)}, u32[]{:S(2)}) collective-permute-start(bf16[64,1024]{1,0:T(8,128)(2,1)S(1)} %bitcast.4), channel_id=1, source_target_pairs={{2,4},{3,5},{4,2},{5,3},{10,12},{11,13},{12,10},{13,11},{18,20},{1... | collective-permute-start | bytes 393224 | tf_op jit(solution)/shard_map/ppermute | solution.py:352
  13.2 9.7 %collective-permute-start = (bf16[80,1152]{1,0:T(8,128)(2,1)S(1)}, bf16[80,1152]{1,0:T(8,128)(2,1)S(1)}, u32[]{:S(2)}, u32[]{:S(2)}) collective-permute-start(bf16[80,1152]{1,0:T(8,128)(2,1)S(1)} %get-tuple-element.23), channel_id=1, source_target_pairs={{0,1},{2,3},{4,5},{6,7},{1,0},{3,2},{5,4},{7,6},{8,9},{10,11},{12,... | collective-permute-start | bytes 552968 | tf_op jit(solution)/shard_map/ppermute | solution.py:352
  13.3 9.6 %collective-permute-start.1 = (bf16[80,1152]{1,0:T(8,128)(2,1)S(1)}, bf16[80,1152]{1,0:T(8,128)(2,1)S(1)}, u32[]{:S(2)}, u32[]{:S(2)}) collective-permute-start(bf16[80,1152]{1,0:T(8,128)(2,1)S(1)} %get-tuple-element.24), channel_id=1, source_target_pairs={{1,2},{3,4},{5,6},{2,1},{4,3},{6,5},{9,10},{11,12},{13,14},{10,9},... | collective-permute-start | bytes 552968 | tf_op jit(solution)/shard_map/ppermute | solution.py:352
  14.0 8.9 %collective-permute-start.2 = (bf16[16,1152]{1,0:T(8,128)(2,1)S(1)}, bf16[16,1152]{1,0:T(8,128)(2,1)S(1)}, u32[]{:S(2)}, u32[]{:S(2)}) collective-permute-start(bf16[16,1152]{1,0:T(8,128)(2,1)S(1)} %get-tuple-element.25), channel_id=1, source_target_pairs={{0,2},{1,3},{4,6},{5,7},{2,0},{3,1},{6,4},{7,5},{8,10},{9,11},{12,... | collective-permute-start | bytes 110600 | tf_op jit(solution)/shard_map/ppermute | solution.py:352
  18.7 4.2 %copy-start.3 = (bf16[192,192]{1,0:T(8,128)(2,1)S(1)}, bf16[192,192]{1,0:T(8,128)(2,1)}, u32[]{:S(2)}) copy-start(bf16[192,192]{1,0:T(8,128)(2,1)} %constant.8.clone.left_tab) | copy-start | bytes 221188
  18.7 4.2 %collective-permute-start.3 = (bf16[16,1152]{1,0:T(8,128)(2,1)S(1)}, bf16[16,1152]{1,0:T(8,128)(2,1)S(1)}, u32[]{:S(2)}, u32[]{:S(2)}) collective-permute-start(bf16[16,1152]{1,0:T(8,128)(2,1)S(1)} %get-tuple-element.26), channel_id=1, source_target_pairs={{2,4},{3,5},{4,2},{5,3},{10,12},{11,13},{12,10},{13,11},{18,20},{1... | collective-permute-start | bytes 110600 | tf_op jit(solution)/shard_map/ppermute | solution.py:352
  25.7 9.2 %collective-permute-start.10 = (bf16[2,32,1024]{2,1,0:T(8,128)(2,1)S(1)}, bf16[2,32,1024]{2,1,0:T(8,128)(2,1)S(1)}, u32[]{:S(2)}, u32[]{:S(2)}) collective-permute-start(bf16[2,32,1024]{2,1,0:T(8,128)(2,1)S(1)} %get-tuple-element.38), channel_id=1, source_target_pairs={{0,24},{8,16},{16,8},{1,25},{9,17},{17,9},{2,26},{10,18},{18,10},{... | collective-permute-start | bytes 393224 | tf_op jit(solution)/shard_map/ppermute | solution.py:345
  30.5 6.9 %collective-permute-start.8 = (bf16[2,32,1024]{2,1,0:T(8,128)(2,1)S(1)}, bf16[2,32,1024]{2,1,0:T(8,128)(2,1)S(1)}, u32[]{:S(2)}, u32[]{:S(2)}) collective-permute-start(bf16[2,32,1024]{2,1,0:T(8,128)(2,1)S(1)} %get-tuple-element.36), channel_id=1, source_target_pairs={{0,8},{8,0},{16,24},{1,9},{9,1},{17,25},{2,10},{10,2},{18,26},{3,1... | collective-permute-start | bytes 393224 | tf_op jit(solution)/shard_map/ppermute | solution.py:345
  33.0 6.9 %collective-permute-start.9 = (bf16[2,32,1024]{2,1,0:T(8,128)(2,1)S(1)}, bf16[2,32,1024]{2,1,0:T(8,128)(2,1)S(1)}, u32[]{:S(2)}, u32[]{:S(2)}) collective-permute-start(bf16[2,32,1024]{2,1,0:T(8,128)(2,1)S(1)} %get-tuple-element.37), channel_id=1, source_target_pairs={{0,16},{8,24},{16,0},{1,17},{9,25},{17,1},{2,18},{10,26},{18,2},{3... | collective-permute-start | bytes 393224 | tf_op jit(solution)/shard_map/ppermute | solution.py:345

commit v14 on v8

--- a/solution.py
+++ b/solution.py
@@ -135,18 +135,16 @@
         far[...] = own[0, pl.ds(pl.multiple_of(start, KR), KR), :HALO_W]
 
 
-def ordered(in_chip, cross, far_even, far_odd):
-    band = lax.axis_index("rows")
-    even_core = band % 2 == 0
-    even_chip = (band // 2) % 2 == 0
+def near_sides(in_chip, cross):
+    even_core = lax.axis_index("rows") % 2 == 0
     in_chip, cross = in_chip[...], cross[...]
+    return jnp.where(even_core, cross, in_chip), jnp.where(even_core, in_chip, cross)
+
+
+def far_sides(far_even, far_odd):
+    even_chip = (lax.axis_index("rows") // 2) % 2 == 0
     far_even, far_odd = far_even[...], far_odd[...]
-    return (
-        jnp.where(even_core, cross, in_chip),
-        jnp.where(even_core, in_chip, cross),
-        jnp.where(even_chip, far_odd, far_even),
-        jnp.where(even_chip, far_even, far_odd),
-    )
+    return jnp.where(even_chip, far_odd, far_even), jnp.where(even_chip, far_even, far_odd)
 
 
 def tiles_below(value, height):
@@ -238,10 +236,12 @@
 
 
 def prepare_kernel(
-    own, incident, in_chip, cross, far_even, far_odd, left_tab, right_tab,
-    first, stereo, clear, col_mats, *row_mats
+    own, incident, in_chip, cross, far_even, far_odd, light_in_chip, light_cross,
+    left_tab, near_tab, right_tab,
+    first, stereo, clear, near_tiles, near_clear, col_mats, *row_mats
 ):
-    low_near, high_near, low_far, high_far = ordered(in_chip, cross, far_even, far_odd)
+    low_near, high_near = near_sides(in_chip, cross)
+    low_far, high_far = far_sides(far_even, far_odd)
     extended = []
     for part in range(2):
         pieces = [low_far, low_near, incident[...], high_near, high_far]
@@ -262,35 +262,37 @@
                 tile * LANES : (tile + 1) * LANES, part * LANES : (part + 1) * LANES
             ]
             stereo[part, :, tile * LANES : (tile + 1) * LANES] = block
+    low, high = near_sides(light_in_chip, light_cross)
+    blocks = [
+        jnp.concatenate([low[0:BAND], high[0:BAND], low[2 * BAND :]], axis=0),
+        jnp.concatenate(
+            [low[BAND : 2 * BAND], high[BAND : 2 * BAND], high[2 * BAND :]], axis=0
+        ),
+    ]
+    near_tiles[...] = stereo_tiles([block[:, :COLS] for block in blocks], near_tab, right_tab)
+    edges = jnp.concatenate([block[:, COLS : COLS + NH] for block in blocks], axis=0)
+    near_clear[...] = clear_pixels(edges)
 
 
 def chain_kernel(
-    in_chip, cross, far_even, far_odd, left_tab, right_tab, first, stereo, clear, col_mats, *rest
+    far_even, far_odd, left_tab, right_tab,
+    first, stereo, clear, near_tiles, near_clear, col_mats, *rest
 ):
     row_mats, (out, field) = rest[: LAYERS - 1], rest[LAYERS - 1 :]
-    low_near, high_near, low_far, high_far = ordered(in_chip, cross, far_even, far_odd)
-    pieces = [
-        low_far,
-        low_near[0:BAND],
-        high_near[0:BAND],
-        high_far,
-        low_near[BAND : 2 * BAND],
-        high_near[BAND : 2 * BAND],
-        low_near[2 * BAND : NEAR],
-        high_near[2 * BAND : NEAR],
-    ]
-    halo = jnp.concatenate(pieces, axis=0)
-    half = halo.shape[0] // 2
-    halo_tiles = stereo_tiles(
-        [halo[:half, :COLS], halo[half:, :COLS]], left_tab, right_tab
-    )
-    halo_clear = clear_pixels(halo[:, COLS : COLS + NH])
-    begins = (0, half, half + 2 * BAND, 0)
-    sides = (BAND + FAR, BAND, KR, 0)
+    far = jnp.concatenate(far_sides(far_even, far_odd), axis=0)
+    far_tiles = stereo_tiles([far[:, :COLS]], left_tab, right_tab)
+    far_clear = clear_pixels(far[:, COLS : COLS + NH])
+
+    spots = (
+        ((0, BAND), (BAND, BAND)),
+        ((NEAR, BAND), (NEAR + BAND, BAND)),
+        ((2 * BAND, KR), (NEAR + 2 * BAND, KR)),
+        None,
+    )
     for layer in range(LAYERS):
         height = layer_height(layer)
         before = height + 2 * KR
-        low, side = begins[layer], sides[layer]
+        side = (height - BAND) // 2
         if layer == 0:
             columned = first
         else:
@@ -300,21 +302,33 @@
         band = slice(layer * BAND, (layer + 1) * BAND)
         pieces = [clear[band]]
         if side:
-            pieces = [halo_clear[low : low + side], clear[band], halo_clear[low + side : low + 2 * side]]
+            (low, count), (high, _) = spots[layer]
+            pieces = [near_clear[low : low + count], clear[band], near_clear[high : high + count]]
+        if layer == 0:
+            pieces = [far_clear[:FAR]] + pieces + [far_clear[FAR:]]
         passing = jnp.concatenate(pieces, axis=0)
         for tile in range(TILES):
             span = slice(tile * height, (tile + 1) * height)
             lanes = slice(tile * LANES, (tile + 1) * LANES)
-            row = (low // half * TILES + tile) * half + low % half
             for part in range(2):
                 within = slice(part * LANES, (part + 1) * LANES)
                 pieces = [stereo[part, band, lanes]]
                 if side:
+                    rows = [
+                        (start // NEAR * TILES + tile) * NEAR + start % NEAR for start in (low, high)
+                    ]
                     pieces = [
-                        halo_tiles[row : row + side, within],
+                        near_tiles[rows[0] : rows[0] + count, within],
                         stereo[part, band, lanes],
-                        halo_tiles[row + side : row + 2 * side, within],
+                        near_tiles[rows[1] : rows[1] + count, within],
                     ]
+                if layer == 0:
+                    row = tile * 2 * FAR
+                    pieces = (
+                        [far_tiles[row : row + FAR, within]]
+                        + pieces
+                        + [far_tiles[row + FAR : row + 2 * FAR, within]]
+                    )
                 added = jnp.concatenate(pieces, axis=0)
                 value = passing[:, lanes] * columned[span, within] + added
                 field[part, :height, lanes] = value.astype(jnp.bfloat16)
@@ -386,22 +400,31 @@
             shaped((TILES * layer_height(0), 2 * LANES), f32),
             shaped((2, LANES, COLS), f32),
             shaped((LANES, COLS), f32),
+            shaped((2 * NEAR * TILES, 2 * LANES), f32),
+            shaped((2 * NEAR, COLS), f32),
             shaped((LAYERS - 1, 2 * LANES, 4 * LANES), bf16),
         ]
         + [shaped((2 * block_height(layer), 2 * LANES), bf16) for layer in range(1, LAYERS)],
-        [vmem] * 8,
+        [vmem] * 11,
         flops=10**9,
         moved=3 * 10**6,
-    )(own, mine, *arrived, jnp.asarray(left_table(LANES)), right_tab)
-    halo_rows = NEAR + FAR
+    )(
+        own,
+        mine,
+        *arrived,
+        *halos[:2],
+        jnp.asarray(left_table(LANES)),
+        jnp.asarray(left_table(NEAR)),
+        right_tab,
+    )
     result = call(
         chain_kernel,
         shaped((LAYERS, 2, BAND, COLS), bf16),
-        [vmem] * (6 + len(made)),
+        [vmem] * (4 + len(made)),
         [pltpu.VMEM((2, layer_height(0), COLS), bf16)],
         flops=2 * 10**9,
         moved=3 * 10**6,
-    )(*halos, jnp.asarray(left_table(halo_rows)), right_tab, *made)
+    )(*halos[2:], jnp.asarray(left_table(2 * FAR)), right_tab, *made)
     gathered = lax.all_to_all(result, "depth", 0, 0, tiled=True)
     return gathered[None, :COLORS]
 

time: 38.6 us -> 46.1 us (1.19)
  the two profiles are of different devices: /device:TPU:0 before, /device:TPU:8 now
where the time goes in v14:
time: 46.1 us; the launch traced here: 45.7 us
  starting transfers between devices  19.8 us (43%)
  blocking collectives  11.9 us (26%)
  Pallas kernels  8.12 us (18%)
  waiting for transfers between devices  4.1 us (9%)
  local copies, waits for them, and re-layouts  1.68 us (4%)
    ppermute x8, starting transfers between devices, exchanged(): return lax.ppermute(value, axis, pairs)  16 us
    all_to_all x1, blocking collectives, body(): gathered = lax.all_to_all(result, 'depth', 0, 0, tiled=True)  11.9 us
    all_to_all x1, starting transfers between devices, body(): own = lax.all_to_all(payload, 'depth', 0, 0, tiled=True)  3.73 us
    pallas_call x1, Pallas kernels, body(): call(chain_kernel, shaped((LAYERS, 2, BAND, COLS), bf16), [vmem] * (4 + l...  3.41 us
    pallas_call x1, Pallas kernels, body(): call(prepare_kernel, [shaped((TILES * layer_height(0), 2 * LANES), f32),...  2.65 us
    all_to_all x1, waiting for transfers between devices, body(): own = lax.all_to_all(payload, 'depth', 0, 0, tiled=True)  2.41 us
    pallas_call x1, Pallas kernels, body(): call(pack_kernel, (shaped((LAYERS, BAND, FULL_W), bf16), shaped(incident....  2.02 us
    ppermute x8, waiting for transfers between devices, exchanged(): return lax.ppermute(value, axis, pairs)  1.69 us
  transfers between devices with their start and end apart: 9, of which 3 were waited for; matrix products, arithmetic and copies ran while one was open for 0% of the time, Pallas kernels for 6%

profile of v14, /device:TPU:8, one launch (start us, length us, event | category | flops | bytes accessed | tf_op | source)
XLA Modules:
  0.0 45.7 jit_solution(4353993660808797626)
XLA Ops:
  0.0 0.0 copy-start.1
  0.0 0.0 copy-start.3
  0.0 0.0 copy-start.2
  0.0 2.0 %shard_map.109 = (bf16[4,32,1280]{2,1,0:T(8,128)(2,1)}, bf16[2,32,1024]{2,1,0:T(8,128)(2,1)}) custom-call(f32[1,3,32,1024]{3,2,1,0:T(8,128)} %light.1, s32[1,32,64]{2,1,0:T(8,128)} %edges.1, s32[1,2]{1,0:T(1,128)} %counts.1, s32[1,2,64]{2,1,0:T(2,128)} %listed.1, bf16[1,3,2,33]{3,2,1,0:T(2,128)(2,1)} %row_taps.1, bf16[1,3,2,127]{3,2,1,0:T(2,128)(2,1)} %col_taps.1, ...), custom_call_target="tpu_custom_call" | custom-call | flops 10000000 | bytes 1000000 | tf_op jit(solution)/shard_map/pallas_call | solution.py:382
  2.0 3.7 %all-to-all-start = ((bf16[4,32,1280]{2,1,0:T(8,128)(2,1)}), bf16[4,32,1280]{2,1,0:T(8,128)(2,1)S(1)}, u32[]{:S(2)}, u32[]{:S(2)}) async-start(bf16[4,32,1280]{2,1,0:T(8,128)(2,1)} %get-tuple-element.20), calls=%async_computation | async-start | bytes 655360 | tf_op jit(solution)/shard_map/all_to_all | solution.py:391
  5.8 3.5 %collective-permute-start.5 = (bf16[64,1024]{1,0:T(8,128)(2,1)}, bf16[64,1024]{1,0:T(8,128)(2,1)S(1)}, u32[]{:S(2)}, u32[]{:S(2)}) collective-permute-start(bf16[64,1024]{1,0:T(8,128)(2,1)} %bitcast.3), channel_id=1, source_target_pairs={{2,4},{3,5},{4,2},{5,3},{10,12},{11,13},{12,10},{13,11},{18,20},{1... | collective-permute-start | bytes 393224 | tf_op jit(solution)/shard_map/ppermute | solution.py:343
  9.3 2.4 %all-to-all-done.own = bf16[4,32,1280]{2,1,0:T(8,128)(2,1)S(1)} async-done(((bf16[4,32,1280]{2,1,0:T(8,128)(2,1)}), bf16[4,32,1280]{2,1,0:T(8,128)(2,1)S(1)}, u32[]{:S(2)}, u32[]{:S(2)}) %all-to-all-start) | async-done | bytes 327712 | tf_op jit(solution)/shard_map/all_to_all | solution.py:391
  11.7 0.1 collective-permute-start.6
  11.8 2.4 %collective-permute-start.7 = (bf16[80,1152]{1,0:T(8,128)(2,1)S(1)}, bf16[80,1152]{1,0:T(8,128)(2,1)S(1)}, u32[]{:S(2)}, u32[]{:S(2)}) collective-permute-start(bf16[80,1152]{1,0:T(8,128)(2,1)S(1)} %get-tuple-element.25), channel_id=1, source_target_pairs={{1,2},{3,4},{5,6},{2,1},{4,3},{6,5},{9,10},{11,12},{13,14},{10,9},... | collective-permute-start | bytes 552968 | tf_op jit(solution)/shard_map/ppermute | solution.py:343
  14.2 0.1 collective-permute-start.4
  14.3 4.4 %collective-permute-start.3 = (bf16[64,1024]{1,0:T(8,128)(2,1)}, bf16[64,1024]{1,0:T(8,128)(2,1)S(1)}, u32[]{:S(2)}, u32[]{:S(2)}) collective-permute-start(bf16[64,1024]{1,0:T(8,128)(2,1)} %bitcast.5), channel_id=1, source_target_pairs={{1,2},{3,4},{5,6},{2,1},{4,3},{6,5},{9,10},{11,12},{13,14},{10,9},... | collective-permute-start | bytes 393224 | tf_op jit(solution)/shard_map/ppermute | solution.py:343
  18.7 0.0 collective-permute-done.5.far_odd
  18.7 0.8 %collective-permute-start.2 = (bf16[64,1024]{1,0:T(8,128)(2,1)}, bf16[64,1024]{1,0:T(8,128)(2,1)S(1)}, u32[]{:S(2)}, u32[]{:S(2)}) collective-permute-start(bf16[64,1024]{1,0:T(8,128)(2,1)} %bitcast.6), channel_id=1, source_target_pairs={{0,1},{2,3},{4,5},{6,7},{1,0},{3,2},{5,4},{7,6},{8,9},{10,11},{12,... | collective-permute-start | bytes 393224 | tf_op jit(solution)/shard_map/ppermute | solution.py:343
  19.5 1.4 %collective-permute-done.4.far_even = bf16[64,1024]{1,0:T(8,128)(2,1)S(1)} collective-permute-done((bf16[64,1024]{1,0:T(8,128)(2,1)}, bf16[64,1024]{1,0:T(8,128)(2,1)S(1)}, u32[]{:S(2)}, u32[]{:S(2)}) %collective-permute-start.4) | collective-permute-done | bytes 131104 | tf_op jit(solution)/shard_map/ppermute | solution.py:343
  20.9 1.6 %collective-permute-start = (bf16[16,1152]{1,0:T(8,128)(2,1)S(1)}, bf16[16,1152]{1,0:T(8,128)(2,1)S(1)}, u32[]{:S(2)}, u32[]{:S(2)}) collective-permute-start(bf16[16,1152]{1,0:T(8,128)(2,1)S(1)} %get-tuple-element.21), channel_id=1, source_target_pairs={{0,2},{1,3},{4,6},{5,7},{2,0},{3,1},{6,4},{7,5},{8,10},{9,11},{12,... | collective-permute-start | bytes 110600 | tf_op jit(solution)/shard_map/ppermute | solution.py:343
  22.6 0.3 collective-permute-done.3.cross
  22.8 3.1 %collective-permute-start.1 = (bf16[16,1152]{1,0:T(8,128)(2,1)S(1)}, bf16[16,1152]{1,0:T(8,128)(2,1)S(1)}, u32[]{:S(2)}, u32[]{:S(2)}) collective-permute-start(bf16[16,1152]{1,0:T(8,128)(2,1)S(1)} %get-tuple-element.22), channel_id=1, source_target_pairs={{2,4},{3,5},{4,2},{5,3},{10,12},{11,13},{12,10},{13,11},{18,20},{1... | collective-permute-start | bytes 110600 | tf_op jit(solution)/shard_map/ppermute | solution.py:343
  26.0 0.0 collective-permute-done.2.in_chip
  26.0 0.0 collective-permute-done.6.light_in_chip
  26.0 0.0 collective-permute-done.7.light_cross
  26.0 0.0 copy-done.1
  26.0 0.0 copy-done.3
  26.0 0.0 copy-done.2
  26.1 0.0 copy-start
  26.1 0.9 %copy-done = bf16[2,32,1024]{2,1,0:T(8,128)(2,1)S(1)} copy-done((bf16[2,32,1024]{2,1,0:T(8,128)(2,1)S(1)}, bf16[2,32,1024]{2,1,0:T(8,128)(2,1)}, u32[]{:S(2)}) %copy-start) | copy-done | bytes 131096
  27.0 0.0 copy-start.4
  27.0 2.7 %shard_map.111 = (f32[1024,256]{1,0:T(8,128)S(1)}, f32[2,128,1024]{2,1,0:T(8,128)S(1)}, f32[128,1024]{1,0:T(8,128)S(1)}, f32[1280,256]{1,0:T(8,128)}, f32[160,10...) custom-call(bf16[4,32,1280]{2,1,0:T(8,128)(2,1)S(1)} %all-to-all-don, ...), custom_call_target="tpu_custom_call" | custom-call | flops 1000000000 | bytes 3000000 | tf_op jit(solution)/shard_map/pallas_call | solution.py:397
  29.6 0.0 collective-permute-done.far_even
  29.6 0.0 collective-permute-done.1.far_odd
  29.6 0.0 copy-done.4
  29.6 3.4 %shard_map.112 = bf16[4,2,32,1024]{3,2,1,0:T(8,128)(2,1)S(1)} custom-call(bf16[16,1152]{1,0:T(8,128)(2,1)S(1)} %collective-permute-done.far_even, bf16[16,1152]{1,0:T(8,128)(2,1)S(1)} %collective-permute-done.1.far_odd, bf16[64,64]{1,0:T(8,128)(2,1)S(1)} %copy-done.4, bf16[256,256]{1,0:T(8,128)(2,1)S(1)} %copy-done.1, ...), custom_call_target="tpu_custom_call" | custom-call | flops 2000000000 | bytes 3000000 | tf_op jit(solution)/shard_map/pallas_call | solution.py:420
  33.0 11.9 %all_to_all.10 = bf16[4,2,32,1024]{3,2,1,0:T(8,128)(2,1)S(1)} all-to-all(bf16[4,2,32,1024]{3,2,1,0:T(8,128)(2,1)S(1)} %shard_map.112), channel_id=1, replica_groups=mesh['depth'=4,'rows'=8] {'depth'}, dimensions={0} | all-to-all | bytes 1048576 | tf_op jit(solution)/shard_map/all_to_all | solution.py:428
  45.0 0.8 %slice_bitcast_fusion = bf16[1,3,2,32,1024]{4,3,2,1,0:T(8,128)(2,1)} fusion(bf16[4,2,32,1024]{3,2,1,0:T(8,128)(2,1)S(1)} %all_to_all.10), kind=kLoop, calls=%fused_computation | loop fusion | bytes 786432 | tf_op jit(solution)/shard_map/broadcast_in_dim | solution.py:429
  (1 shorter events, 0.0 us)
Async XLA Ops:
  0.0 26.0 %copy-start.1 = (bf16[256,256]{1,0:T(8,128)(2,1)S(1)}, bf16[256,256]{1,0:T(8,128)(2,1)}, u32[]{:S(2)}) copy-start(bf16[256,256]{1,0:T(8,128)(2,1)} %constant.8.clone.right_tab) | copy-start | bytes 393220
  0.0 26.0 %copy-start.3 = (bf16[160,160]{1,0:T(8,128)(2,1)S(1)}, bf16[160,160]{1,0:T(8,128)(2,1)}, u32[]{:S(2)}) copy-start(bf16[160,160]{1,0:T(8,128)(2,1)} %constant.10.clone.near_tab) | copy-start | bytes 153604
  0.0 26.0 %copy-start.2 = (bf16[256,256]{1,0:T(8,128)(2,1)S(1)}, bf16[256,256]{1,0:T(8,128)(2,1)}, u32[]{:S(2)}) copy-start(bf16[256,256]{1,0:T(8,128)(2,1)} %constant.9.clone.left_tab) | copy-start | bytes 393220
  2.0 9.6 %all-to-all-start = ((bf16[4,32,1280]{2,1,0:T(8,128)(2,1)}), bf16[4,32,1280]{2,1,0:T(8,128)(2,1)S(1)}, u32[]{:S(2)}, u32[]{:S(2)}) async-start(bf16[4,32,1280]{2,1,0:T(8,128)(2,1)} %get-tuple-element.20), calls=%async_computation | async-start | bytes 655360 | tf_op jit(solution)/shard_map/all_to_all | solution.py:391
  5.8 12.9 %collective-permute-start.5 = (bf16[64,1024]{1,0:T(8,128)(2,1)}, bf16[64,1024]{1,0:T(8,128)(2,1)S(1)}, u32[]{:S(2)}, u32[]{:S(2)}) collective-permute-start(bf16[64,1024]{1,0:T(8,128)(2,1)} %bitcast.3), channel_id=1, source_target_pairs={{2,4},{3,5},{4,2},{5,3},{10,12},{11,13},{12,10},{13,11},{18,20},{1... | collective-permute-start | bytes 393224 | tf_op jit(solution)/shard_map/ppermute | solution.py:343
  11.7 14.3 %collective-permute-start.6 = (bf16[80,1152]{1,0:T(8,128)(2,1)S(1)}, bf16[80,1152]{1,0:T(8,128)(2,1)S(1)}, u32[]{:S(2)}, u32[]{:S(2)}) collective-permute-start(bf16[80,1152]{1,0:T(8,128)(2,1)S(1)} %get-tuple-element.24), channel_id=1, source_target_pairs={{0,1},{2,3},{4,5},{6,7},{1,0},{3,2},{5,4},{7,6},{8,9},{10,11},{12,... | collective-permute-start | bytes 552968 | tf_op jit(solution)/shard_map/ppermute | solution.py:343
  11.8 14.2 %collective-permute-start.7 = (bf16[80,1152]{1,0:T(8,128)(2,1)S(1)}, bf16[80,1152]{1,0:T(8,128)(2,1)S(1)}, u32[]{:S(2)}, u32[]{:S(2)}) collective-permute-start(bf16[80,1152]{1,0:T(8,128)(2,1)S(1)} %get-tuple-element.25), channel_id=1, source_target_pairs={{1,2},{3,4},{5,6},{2,1},{4,3},{6,5},{9,10},{11,12},{13,14},{10,9},... | collective-permute-start | bytes 552968 | tf_op jit(solution)/shard_map/ppermute | solution.py:343
  14.2 6.7 %collective-permute-start.4 = (bf16[64,1024]{1,0:T(8,128)(2,1)}, bf16[64,1024]{1,0:T(8,128)(2,1)S(1)}, u32[]{:S(2)}, u32[]{:S(2)}) collective-permute-start(bf16[64,1024]{1,0:T(8,128)(2,1)} %bitcast.4), channel_id=1, source_target_pairs={{0,2},{1,3},{4,6},{5,7},{2,0},{3,1},{6,4},{7,5},{8,10},{9,11},{12,... | collective-permute-start | bytes 393224 | tf_op jit(solution)/shard_map/ppermute | solution.py:343
  14.3 8.5 %collective-permute-start.3 = (bf16[64,1024]{1,0:T(8,128)(2,1)}, bf16[64,1024]{1,0:T(8,128)(2,1)S(1)}, u32[]{:S(2)}, u32[]{:S(2)}) collective-permute-start(bf16[64,1024]{1,0:T(8,128)(2,1)} %bitcast.5), channel_id=1, source_target_pairs={{1,2},{3,4},{5,6},{2,1},{4,3},{6,5},{9,10},{11,12},{13,14},{10,9},... | collective-permute-start | bytes 393224 | tf_op jit(solution)/shard_map/ppermute | solution.py:343
  18.7 7.3 %collective-permute-start.2 = (bf16[64,1024]{1,0:T(8,128)(2,1)}, bf16[64,1024]{1,0:T(8,128)(2,1)S(1)}, u32[]{:S(2)}, u32[]{:S(2)}) collective-permute-start(bf16[64,1024]{1,0:T(8,128)(2,1)} %bitcast.6), channel_id=1, source_target_pairs={{0,1},{2,3},{4,5},{6,7},{1,0},{3,2},{5,4},{7,6},{8,9},{10,11},{12,... | collective-permute-start | bytes 393224 | tf_op jit(solution)/shard_map/ppermute | solution.py:343
  20.9 8.7 %collective-permute-start = (bf16[16,1152]{1,0:T(8,128)(2,1)S(1)}, bf16[16,1152]{1,0:T(8,128)(2,1)S(1)}, u32[]{:S(2)}, u32[]{:S(2)}) collective-permute-start(bf16[16,1152]{1,0:T(8,128)(2,1)S(1)} %get-tuple-element.21), channel_id=1, source_target_pairs={{0,2},{1,3},{4,6},{5,7},{2,0},{3,1},{6,4},{7,5},{8,10},{9,11},{12,... | collective-permute-start | bytes 110600 | tf_op jit(solution)/shard_map/ppermute | solution.py:343
  22.8 6.8 %collective-permute-start.1 = (bf16[16,1152]{1,0:T(8,128)(2,1)S(1)}, bf16[16,1152]{1,0:T(8,128)(2,1)S(1)}, u32[]{:S(2)}, u32[]{:S(2)}) collective-permute-start(bf16[16,1152]{1,0:T(8,128)(2,1)S(1)} %get-tuple-element.22), channel_id=1, source_target_pairs={{2,4},{3,5},{4,2},{5,3},{10,12},{11,13},{12,10},{13,11},{18,20},{1... | collective-permute-start | bytes 110600 | tf_op jit(solution)/shard_map/ppermute | solution.py:343
  26.1 0.9 %copy-start = (bf16[2,32,1024]{2,1,0:T(8,128)(2,1)S(1)}, bf16[2,32,1024]{2,1,0:T(8,128)(2,1)}, u32[]{:S(2)}) copy-start(bf16[2,32,1024]{2,1,0:T(8,128)(2,1)} %get-tuple-element.23) | copy-start | bytes 393220
  27.0 2.7 %copy-start.4 = (bf16[64,64]{1,0:T(8,128)(2,1)S(1)}, bf16[64,64]{1,0:T(8,128)(2,1)}, u32[]{:S(2)}) copy-start(bf16[64,64]{1,0:T(8,128)(2,1)} %constant.11.clone.left_tab) | copy-start | bytes 24580

commit v15 on v8

--- a/solution.py
+++ b/solution.py
@@ -137,10 +137,18 @@
 
 def ordered(in_chip, cross, far_even, far_odd):
     band = lax.axis_index("rows")
+    count = lax.axis_size("rows")
     even_core = band % 2 == 0
     even_chip = (band // 2) % 2 == 0
-    in_chip, cross = in_chip[...], cross[...]
-    far_even, far_odd = far_even[...], far_odd[...]
+
+    def received(value, by, phase):
+        lower = (band // by) % 2 == phase
+        paired = jnp.where(lower, band + by < count, band >= by)
+        value = value[...]
+        return jnp.where(paired, value, jnp.zeros_like(value))
+
+    in_chip, cross = received(in_chip, 1, 0), received(cross, 1, 1)
+    far_even, far_odd = received(far_even, 2, 0), received(far_odd, 2, 1)
     return (
         jnp.where(even_core, cross, in_chip),
         jnp.where(even_core, in_chip, cross),
@@ -326,6 +334,8 @@
     count = lax.axis_size(axis)
     lower = [i for i in range(count - by) if (i // by) % 2 == phase]
     pairs = [(i, i + by) for i in lower] + [(i + by, i) for i in lower]
+    paired = {source for source, _ in pairs}
+    pairs += [(i, i) for i in range(count) if i not in paired]
     return lax.ppermute(value, axis, pairs)
 
 

time: 38.6 us -> 38.6 us (level)
  no operation moved by 1% of the time
where the time goes in v15:
time: 38.6 us; the launch traced here: 38.2 us
  starting transfers between devices  16.3 us (42%)
  blocking collectives  12 us (31%)
  Pallas kernels  5.63 us (15%)
  waiting for transfers between devices  3.29 us (9%)
  local copies, waits for them, and re-layouts  0.79 us (2%)
    all_to_all x1, blocking collectives, body(): gathered = lax.all_to_all(result, 'depth', 0, 0, tiled=True)  12 us
    ppermute x8, starting transfers between devices, exchanged(): return lax.ppermute(value, axis, pairs)  11 us
    all_to_all x1, starting transfers between devices, body(): own = lax.all_to_all(payload, 'depth', 0, 0, tiled=True)  5.31 us
    pallas_call x1, Pallas kernels, body(): call(chain_kernel, shaped((LAYERS, 2, BAND, COLS), bf16), [vmem] * (6 + l...  2.47 us
    ppermute x8, waiting for transfers between devices, exchanged(): return lax.ppermute(value, axis, pairs)  2.26 us
    pallas_call x1, Pallas kernels, body(): call(pack_kernel, (shaped((LAYERS, BAND, FULL_W), bf16), shaped(incident....  1.98 us
    pallas_call x1, Pallas kernels, body(): call(prepare_kernel, [shaped((TILES * layer_height(0), 2 * LANES), f32),...  1.14 us
    all_to_all x1, waiting for transfers between devices, body(): own = lax.all_to_all(payload, 'depth', 0, 0, tiled=True)  1.03 us
  transfers between devices with their start and end apart: 9, of which 2 were waited for; matrix products, arithmetic and copies ran while one was open for 0% of the time, Pallas kernels for 3%

profile of v15, /device:TPU:0, one launch (start us, length us, event | category | flops | bytes accessed | tf_op | source)
XLA Modules:
  0.0 38.2 jit_solution(2975995268737571124)
XLA Ops:
  0.0 2.0 %shard_map.100 = (bf16[4,32,1280]{2,1,0:T(8,128)(2,1)}, bf16[2,32,1024]{2,1,0:T(8,128)(2,1)}) custom-call(f32[1,3,32,1024]{3,2,1,0:T(8,128)} %light.1, s32[1,32,64]{2,1,0:T(8,128)} %edges.1, s32[1,2]{1,0:T(1,128)} %counts.1, s32[1,2,64]{2,1,0:T(2,128)} %listed.1, bf16[1,3,2,33]{3,2,1,0:T(2,128)(2,1)} %row_taps.1, bf16[1,3,2,127]{3,2,1,0:T(2,128)(2,1)} %col_taps.1, ...), custom_call_target="tpu_custom_call" | custom-call | flops 10000000 | bytes 1000000 | tf_op jit(solution)/shard_map/pallas_call | solution.py:378
  2.0 0.0 copy-start
  2.0 5.3 %all-to-all-start = ((bf16[4,32,1280]{2,1,0:T(8,128)(2,1)}), bf16[4,32,1280]{2,1,0:T(8,128)(2,1)S(1)}, u32[]{:S(2)}, u32[]{:S(2)}) async-start(bf16[4,32,1280]{2,1,0:T(8,128)(2,1)} %get-tuple-element.18), calls=%async_computation | async-start | bytes 655360 | tf_op jit(solution)/shard_map/all_to_all | solution.py:387
  7.3 0.0 copy-done
  7.3 0.0 copy-start.1
  7.3 0.0 copy-start.2
  7.3 0.1 collective-permute-start.4
  7.4 0.8 %collective-permute-start.5 = (bf16[64,1024]{1,0:T(8,128)(2,1)S(1)}, bf16[64,1024]{1,0:T(8,128)(2,1)S(1)}, u32[]{:S(2)}, u32[]{:S(2)}) collective-permute-start(bf16[64,1024]{1,0:T(8,128)(2,1)S(1)} %bitcast.4), channel_id=1, source_target_pairs={{1,2},{3,4},{5,6},{2,1},{4,3},{6,5},{0,0},{7,7},{9,10},{11,12},{13... | collective-permute-start | bytes 393224 | tf_op jit(solution)/shard_map/ppermute | solution.py:339
  8.2 3.3 %collective-permute-start.6 = (bf16[64,1024]{1,0:T(8,128)(2,1)S(1)}, bf16[64,1024]{1,0:T(8,128)(2,1)S(1)}, u32[]{:S(2)}, u32[]{:S(2)}) collective-permute-start(bf16[64,1024]{1,0:T(8,128)(2,1)S(1)} %bitcast.5), channel_id=1, source_target_pairs={{0,2},{1,3},{4,6},{5,7},{2,0},{3,1},{6,4},{7,5},{8,10},{9,11},{12,... | collective-permute-start | bytes 393224 | tf_op jit(solution)/shard_map/ppermute | solution.py:339
  11.5 0.7 %collective-permute-start.7 = (bf16[64,1024]{1,0:T(8,128)(2,1)S(1)}, bf16[64,1024]{1,0:T(8,128)(2,1)S(1)}, u32[]{:S(2)}, u32[]{:S(2)}) collective-permute-start(bf16[64,1024]{1,0:T(8,128)(2,1)S(1)} %bitcast.6), channel_id=1, source_target_pairs={{2,4},{3,5},{4,2},{5,3},{0,0},{1,1},{6,6},{7,7},{10,12},{11,13},{1... | collective-permute-start | bytes 393224 | tf_op jit(solution)/shard_map/ppermute | solution.py:339
  12.2 1.0 %all-to-all-done.own = bf16[4,32,1280]{2,1,0:T(8,128)(2,1)S(1)} async-done(((bf16[4,32,1280]{2,1,0:T(8,128)(2,1)}), bf16[4,32,1280]{2,1,0:T(8,128)(2,1)S(1)}, u32[]{:S(2)}, u32[]{:S(2)}) %all-to-all-start) | async-done | bytes 327712 | tf_op jit(solution)/shard_map/all_to_all | solution.py:387
  13.2 0.1 collective-permute-start
  13.3 0.0 collective-permute-done.4.in_chip
  13.3 0.7 %collective-permute-start.1 = (bf16[80,1152]{1,0:T(8,128)(2,1)S(1)}, bf16[80,1152]{1,0:T(8,128)(2,1)S(1)}, u32[]{:S(2)}, u32[]{:S(2)}) collective-permute-start(bf16[80,1152]{1,0:T(8,128)(2,1)S(1)} %get-tuple-element.20), channel_id=1, source_target_pairs={{1,2},{3,4},{5,6},{2,1},{4,3},{6,5},{0,0},{7,7},{9,10},{11,12},{13... | collective-permute-start | bytes 552968 | tf_op jit(solution)/shard_map/ppermute | solution.py:339
  14.0 0.0 collective-permute-done.5.cross
  14.0 4.7 %collective-permute-start.2 = (bf16[16,1152]{1,0:T(8,128)(2,1)S(1)}, bf16[16,1152]{1,0:T(8,128)(2,1)S(1)}, u32[]{:S(2)}, u32[]{:S(2)}) collective-permute-start(bf16[16,1152]{1,0:T(8,128)(2,1)S(1)} %get-tuple-element.21), channel_id=1, source_target_pairs={{0,2},{1,3},{4,6},{5,7},{2,0},{3,1},{6,4},{7,5},{8,10},{9,11},{12,... | collective-permute-start | bytes 110600 | tf_op jit(solution)/shard_map/ppermute | solution.py:339
  18.7 0.0 collective-permute-done.6.far_even
  18.7 0.0 copy-start.3
  18.7 0.8 %collective-permute-start.3 = (bf16[16,1152]{1,0:T(8,128)(2,1)S(1)}, bf16[16,1152]{1,0:T(8,128)(2,1)S(1)}, u32[]{:S(2)}, u32[]{:S(2)}) collective-permute-start(bf16[16,1152]{1,0:T(8,128)(2,1)S(1)} %get-tuple-element.22), channel_id=1, source_target_pairs={{2,4},{3,5},{4,2},{5,3},{0,0},{1,1},{6,6},{7,7},{10,12},{11,13},{1... | collective-permute-start | bytes 110600 | tf_op jit(solution)/shard_map/ppermute | solution.py:339
  19.5 0.0 collective-permute-done.7.far_odd
  19.5 0.0 copy-done.1
  19.5 0.0 copy-done.2
  19.5 1.1 %shard_map.102 = (f32[1024,256]{1,0:T(8,128)S(1)}, f32[2,128,1024]{2,1,0:T(8,128)S(1)}, f32[128,1024]{1,0:T(8,128)S(1)}, bf16[3,256,512]{2,1,0:T(8,128)(2,1)S(1)...) custom-call(bf16[4,32,1280]{2,1,0:T(8,128)(2,1)S(1)} %all-to-all-done.own, ...), custom_call_target="tpu_custom_call" | custom-call | flops 1000000000 | bytes 3000000 | tf_op jit(solution)/shard_map/pallas_call | solution.py:393
  20.7 2.2 %collective-permute-done.2.far_even = bf16[16,1152]{1,0:T(8,128)(2,1)S(1)} collective-permute-done((bf16[16,1152]{1,0:T(8,128)(2,1)S(1)}, bf16[16,1152]{1,0:T(8,128)(2,1)S(1)}, u32[]{:S(2)}, u32[]{:S(2)}) %collective-permute-start.2) | collective-permute-done | bytes 36896 | tf_op jit(solution)/shard_map/ppermute | solution.py:339
  22.9 0.0 collective-permute-done.3.far_odd
  22.9 0.0 collective-permute-done.in_chip
  22.9 0.0 collective-permute-done.1.cross
  22.9 0.0 copy-done.3
  22.9 2.5 %shard_map.103 = bf16[4,2,32,1024]{3,2,1,0:T(8,128)(2,1)S(1)} custom-call(bf16[80,1152]{1,0:T(8,128)(2,1)S(1)} %collective-permute-done.in_chip, bf16[80,1152]{1,0:T(8,128)(2,1)S(1)} %collective-permute-done.1.cross, bf16[16,1152]{1,0:T(8,128)(2,1)S(1)} %collective-permute-done.2.far_even, bf16[16,1152]{1,0:T(8,128)(2,1)S(1)} %collective-permute-done.3.far_odd, ...), custom_call_target="tpu_custom_call" | custom-call | flops 2000000000 | bytes 3000000 | tf_op jit(solution)/shard_map/pallas_call | solution.py:407
  25.4 12.0 %all_to_all.10 = bf16[4,2,32,1024]{3,2,1,0:T(8,128)(2,1)S(1)} all-to-all(bf16[4,2,32,1024]{3,2,1,0:T(8,128)(2,1)S(1)} %shard_map.103), channel_id=1, replica_groups=mesh['depth'=4,'rows'=8] {'depth'}, dimensions={0} | all-to-all | bytes 1048576 | tf_op jit(solution)/shard_map/all_to_all | solution.py:415
  37.5 0.8 %slice_bitcast_fusion = bf16[1,3,2,32,1024]{4,3,2,1,0:T(8,128)(2,1)} fusion(bf16[4,2,32,1024]{3,2,1,0:T(8,128)(2,1)S(1)} %all_to_all.10), kind=kLoop, calls=%fused_computation | loop fusion | bytes 786432 | tf_op jit(solution)/shard_map/broadcast_in_dim | solution.py:416
  (1 shorter events, 0.0 us)
Async XLA Ops:
  2.0 5.3 %copy-start = (bf16[2,32,1024]{2,1,0:T(8,128)(2,1)S(1)}, bf16[2,32,1024]{2,1,0:T(8,128)(2,1)}, u32[]{:S(2)}) copy-start(bf16[2,32,1024]{2,1,0:T(8,128)(2,1)} %get-tuple-element.23) | copy-start | bytes 393220
  2.0 11.2 %all-to-all-start = ((bf16[4,32,1280]{2,1,0:T(8,128)(2,1)}), bf16[4,32,1280]{2,1,0:T(8,128)(2,1)S(1)}, u32[]{:S(2)}, u32[]{:S(2)}) async-start(bf16[4,32,1280]{2,1,0:T(8,128)(2,1)} %get-tuple-element.18), calls=%async_computation | async-start | bytes 655360 | tf_op jit(solution)/shard_map/all_to_all | solution.py:387
  7.3 12.2 %copy-start.1 = (bf16[256,256]{1,0:T(8,128)(2,1)S(1)}, bf16[256,256]{1,0:T(8,128)(2,1)}, u32[]{:S(2)}) copy-start(bf16[256,256]{1,0:T(8,128)(2,1)} %constant.6.clone.right_tab) | copy-start | bytes 393220
  7.3 12.2 %copy-start.2 = (bf16[256,256]{1,0:T(8,128)(2,1)S(1)}, bf16[256,256]{1,0:T(8,128)(2,1)}, u32[]{:S(2)}) copy-start(bf16[256,256]{1,0:T(8,128)(2,1)} %constant.7.clone.left_tab) | copy-start | bytes 393220
  7.3 6.0 %collective-permute-start.4 = (bf16[64,1024]{1,0:T(8,128)(2,1)S(1)}, bf16[64,1024]{1,0:T(8,128)(2,1)S(1)}, u32[]{:S(2)}, u32[]{:S(2)}) collective-permute-start(bf16[64,1024]{1,0:T(8,128)(2,1)S(1)} %bitcast.3), channel_id=1, source_target_pairs={{0,1},{2,3},{4,5},{6,7},{1,0},{3,2},{5,4},{7,6},{8,9},{10,11},{12,... | collective-permute-start | bytes 393224 | tf_op jit(solution)/shard_map/ppermute | solution.py:339
  7.4 6.6 %collective-permute-start.5 = (bf16[64,1024]{1,0:T(8,128)(2,1)S(1)}, bf16[64,1024]{1,0:T(8,128)(2,1)S(1)}, u32[]{:S(2)}, u32[]{:S(2)}) collective-permute-start(bf16[64,1024]{1,0:T(8,128)(2,1)S(1)} %bitcast.4), channel_id=1, source_target_pairs={{1,2},{3,4},{5,6},{2,1},{4,3},{6,5},{0,0},{7,7},{9,10},{11,12},{13... | collective-permute-start | bytes 393224 | tf_op jit(solution)/shard_map/ppermute | solution.py:339
  8.2 10.5 %collective-permute-start.6 = (bf16[64,1024]{1,0:T(8,128)(2,1)S(1)}, bf16[64,1024]{1,0:T(8,128)(2,1)S(1)}, u32[]{:S(2)}, u32[]{:S(2)}) collective-permute-start(bf16[64,1024]{1,0:T(8,128)(2,1)S(1)} %bitcast.5), channel_id=1, source_target_pairs={{0,2},{1,3},{4,6},{5,7},{2,0},{3,1},{6,4},{7,5},{8,10},{9,11},{12,... | collective-permute-start | bytes 393224 | tf_op jit(solution)/shard_map/ppermute | solution.py:339
  11.5 8.0 %collective-permute-start.7 = (bf16[64,1024]{1,0:T(8,128)(2,1)S(1)}, bf16[64,1024]{1,0:T(8,128)(2,1)S(1)}, u32[]{:S(2)}, u32[]{:S(2)}) collective-permute-start(bf16[64,1024]{1,0:T(8,128)(2,1)S(1)} %bitcast.6), channel_id=1, source_target_pairs={{2,4},{3,5},{4,2},{5,3},{0,0},{1,1},{6,6},{7,7},{10,12},{11,13},{1... | collective-permute-start | bytes 393224 | tf_op jit(solution)/shard_map/ppermute | solution.py:339
  13.2 9.7 %collective-permute-start = (bf16[80,1152]{1,0:T(8,128)(2,1)S(1)}, bf16[80,1152]{1,0:T(8,128)(2,1)S(1)}, u32[]{:S(2)}, u32[]{:S(2)}) collective-permute-start(bf16[80,1152]{1,0:T(8,128)(2,1)S(1)} %get-tuple-element.19), channel_id=1, source_target_pairs={{0,1},{2,3},{4,5},{6,7},{1,0},{3,2},{5,4},{7,6},{8,9},{10,11},{12,... | collective-permute-start | bytes 552968 | tf_op jit(solution)/shard_map/ppermute | solution.py:339
  13.3 9.6 %collective-permute-start.1 = (bf16[80,1152]{1,0:T(8,128)(2,1)S(1)}, bf16[80,1152]{1,0:T(8,128)(2,1)S(1)}, u32[]{:S(2)}, u32[]{:S(2)}) collective-permute-start(bf16[80,1152]{1,0:T(8,128)(2,1)S(1)} %get-tuple-element.20), channel_id=1, source_target_pairs={{1,2},{3,4},{5,6},{2,1},{4,3},{6,5},{0,0},{7,7},{9,10},{11,12},{13... | collective-permute-start | bytes 552968 | tf_op jit(solution)/shard_map/ppermute | solution.py:339
  14.0 8.9 %collective-permute-start.2 = (bf16[16,1152]{1,0:T(8,128)(2,1)S(1)}, bf16[16,1152]{1,0:T(8,128)(2,1)S(1)}, u32[]{:S(2)}, u32[]{:S(2)}) collective-permute-start(bf16[16,1152]{1,0:T(8,128)(2,1)S(1)} %get-tuple-element.21), channel_id=1, source_target_pairs={{0,2},{1,3},{4,6},{5,7},{2,0},{3,1},{6,4},{7,5},{8,10},{9,11},{12,... | collective-permute-start | bytes 110600 | tf_op jit(solution)/shard_map/ppermute | solution.py:339
  18.7 4.2 %copy-start.3 = (bf16[192,192]{1,0:T(8,128)(2,1)S(1)}, bf16[192,192]{1,0:T(8,128)(2,1)}, u32[]{:S(2)}) copy-start(bf16[192,192]{1,0:T(8,128)(2,1)} %constant.8.clone.left_tab) | copy-start | bytes 221188
  18.7 4.2 %collective-permute-start.3 = (bf16[16,1152]{1,0:T(8,128)(2,1)S(1)}, bf16[16,1152]{1,0:T(8,128)(2,1)S(1)}, u32[]{:S(2)}, u32[]{:S(2)}) collective-permute-start(bf16[16,1152]{1,0:T(8,128)(2,1)S(1)} %get-tuple-element.22), channel_id=1, source_target_pairs={{2,4},{3,5},{4,2},{5,3},{0,0},{1,1},{6,6},{7,7},{10,12},{11,13},{1... | collective-permute-start | bytes 110600 | tf_op jit(solution)/shard_map/ppermute | solution.py:339

commit v16 on v14

--- a/solution.py
+++ b/solution.py
@@ -23,7 +23,7 @@
 FULL_W = COLS + 2 * LANES
 NEAR = 2 * BAND + KR
 FAR = KR
-VMEM_LIMIT = 48 * 1024 * 1024
+VMEM_LIMIT = 40 * 1024 * 1024
 PACK_LIMIT = 63 * 1024 * 1024
 
 
@@ -236,9 +236,8 @@
 
 
 def prepare_kernel(
-    own, incident, in_chip, cross, far_even, far_odd, light_in_chip, light_cross,
-    left_tab, near_tab, right_tab,
-    first, stereo, clear, near_tiles, near_clear, col_mats, *row_mats
+    own, incident, in_chip, cross, far_even, far_odd, left_tab, right_tab,
+    first, stereo, clear, col_mats, *row_mats
 ):
     low_near, high_near = near_sides(in_chip, cross)
     low_far, high_far = far_sides(far_even, far_odd)
@@ -262,6 +261,9 @@
                 tile * LANES : (tile + 1) * LANES, part * LANES : (part + 1) * LANES
             ]
             stereo[part, :, tile * LANES : (tile + 1) * LANES] = block
+
+
+def near_kernel(light_in_chip, light_cross, near_tab, right_tab, near_tiles, near_clear):
     low, high = near_sides(light_in_chip, light_cross)
     blocks = [
         jnp.concatenate([low[0:BAND], high[0:BAND], low[2 * BAND :]], axis=0),
@@ -276,7 +278,7 @@
 
 def chain_kernel(
     far_even, far_odd, left_tab, right_tab,
-    first, stereo, clear, near_tiles, near_clear, col_mats, *rest
+    near_tiles, near_clear, first, stereo, clear, col_mats, *rest
 ):
     row_mats, (out, field) = rest[: LAYERS - 1], rest[LAYERS - 1 :]
     far = jnp.concatenate(far_sides(far_even, far_odd), axis=0)
@@ -400,31 +402,28 @@
             shaped((TILES * layer_height(0), 2 * LANES), f32),
             shaped((2, LANES, COLS), f32),
             shaped((LANES, COLS), f32),
-            shaped((2 * NEAR * TILES, 2 * LANES), f32),
-            shaped((2 * NEAR, COLS), f32),
             shaped((LAYERS - 1, 2 * LANES, 4 * LANES), bf16),
         ]
         + [shaped((2 * block_height(layer), 2 * LANES), bf16) for layer in range(1, LAYERS)],
-        [vmem] * 11,
+        [vmem] * 8,
         flops=10**9,
         moved=3 * 10**6,
-    )(
-        own,
-        mine,
-        *arrived,
-        *halos[:2],
-        jnp.asarray(left_table(LANES)),
-        jnp.asarray(left_table(NEAR)),
-        right_tab,
-    )
+    )(own, mine, *arrived, jnp.asarray(left_table(LANES)), right_tab)
+    near_made = call(
+        near_kernel,
+        [shaped((2 * NEAR * TILES, 2 * LANES), f32), shaped((2 * NEAR, COLS), f32)],
+        [vmem] * 4,
+        flops=5 * 10**8,
+        moved=2 * 10**6,
+    )(*halos[:2], jnp.asarray(left_table(NEAR)), right_tab)
     result = call(
         chain_kernel,
         shaped((LAYERS, 2, BAND, COLS), bf16),
-        [vmem] * (4 + len(made)),
+        [vmem] * (6 + len(made)),
         [pltpu.VMEM((2, layer_height(0), COLS), bf16)],
         flops=2 * 10**9,
         moved=3 * 10**6,
-    )(*halos[2:], jnp.asarray(left_table(2 * FAR)), right_tab, *made)
+    )(*halos[2:], jnp.asarray(left_table(2 * FAR)), right_tab, *near_made, *made)
     gathered = lax.all_to_all(result, "depth", 0, 0, tiled=True)
     return gathered[None, :COLORS]
 

time: 46.1 us -> 38.8 us (0.84)
  the two profiles are of different devices: /device:TPU:8 before, /device:TPU:0 now
where the time goes in v16:
time: 38.8 us; the launch traced here: 38.5 us
  starting transfers between devices  15.9 us (41%)
  blocking collectives  12.8 us (33%)
  Pallas kernels  5.99 us (15%)
  waiting for transfers between devices  1.88 us (5%)
  local copies, waits for them, and re-layouts  1.69 us (4%)
    all_to_all x1, blocking collectives, body(): gathered = lax.all_to_all(result, 'depth', 0, 0, tiled=True)  12.8 us
    ppermute x8, starting transfers between devices, exchanged(): return lax.ppermute(value, axis, pairs)  10.8 us
    all_to_all x1, starting transfers between devices, body(): own = lax.all_to_all(payload, 'depth', 0, 0, tiled=True)  5.18 us
    pallas_call x1, Pallas kernels, body(): call(chain_kernel, shaped((LAYERS, 2, BAND, COLS), bf16), [vmem] * (6 + l...  2.11 us
    pallas_call x1, Pallas kernels, body(): call(pack_kernel, (shaped((LAYERS, BAND, FULL_W), bf16), shaped(incident....  2.04 us
    pallas_call x1, Pallas kernels, body(): call(prepare_kernel, [shaped((TILES * layer_height(0), 2 * LANES), f32),...  1.11 us
    all_to_all x1, waiting for transfers between devices, body(): own = lax.all_to_all(payload, 'depth', 0, 0, tiled=True)  1.11 us
    unnamed x10, local copies, waits for them, and re-layouts  0.92 us
  transfers between devices with their start and end apart: 9, of which 2 were waited for; matrix products, arithmetic and copies ran while one was open for 0% of the time, Pallas kernels for 5%

profile of v16, /device:TPU:0, one launch (start us, length us, event | category | flops | bytes accessed | tf_op | source)
XLA Modules:
  0.0 38.5 jit_solution(9894714286418574729)
XLA Ops:
  0.0 0.0 copy-start.1
  0.0 0.0 copy-start.2
  0.0 2.0 %shard_map.109 = (bf16[4,32,1280]{2,1,0:T(8,128)(2,1)}, bf16[2,32,1024]{2,1,0:T(8,128)(2,1)}) custom-call(f32[1,3,32,1024]{3,2,1,0:T(8,128)} %light.1, s32[1,32,64]{2,1,0:T(8,128)} %edges.1, s32[1,2]{1,0:T(1,128)} %counts.1, s32[1,2,64]{2,1,0:T(2,128)} %listed.1, bf16[1,3,2,33]{3,2,1,0:T(2,128)(2,1)} %row_taps.1, bf16[1,3,2,127]{3,2,1,0:T(2,128)(2,1)} %col_taps.1, ...), custom_call_target="tpu_custom_call" | custom-call | flops 10000000 | bytes 1000000 | tf_op jit(solution)/shard_map/pallas_call | solution.py:384
  2.0 5.2 %all-to-all-start = ((bf16[4,32,1280]{2,1,0:T(8,128)(2,1)}), bf16[4,32,1280]{2,1,0:T(8,128)(2,1)S(1)}, u32[]{:S(2)}, u32[]{:S(2)}) async-start(bf16[4,32,1280]{2,1,0:T(8,128)(2,1)} %get-tuple-element.20), calls=%async_computation | async-start | bytes 655360 | tf_op jit(solution)/shard_map/all_to_all | solution.py:393
  7.2 0.0 collective-permute-start.4
  7.2 0.7 %collective-permute-start.5 = (bf16[64,1024]{1,0:T(8,128)(2,1)}, bf16[64,1024]{1,0:T(8,128)(2,1)S(1)}, u32[]{:S(2)}, u32[]{:S(2)}) collective-permute-start(bf16[64,1024]{1,0:T(8,128)(2,1)} %bitcast.4), channel_id=1, source_target_pairs={{1,2},{3,4},{5,6},{2,1},{4,3},{6,5},{9,10},{11,12},{13,14},{10,9},... | collective-permute-start | bytes 393224 | tf_op jit(solution)/shard_map/ppermute | solution.py:345
  7.9 3.4 %collective-permute-start.6 = (bf16[64,1024]{1,0:T(8,128)(2,1)}, bf16[64,1024]{1,0:T(8,128)(2,1)S(1)}, u32[]{:S(2)}, u32[]{:S(2)}) collective-permute-start(bf16[64,1024]{1,0:T(8,128)(2,1)} %bitcast.5), channel_id=1, source_target_pairs={{0,2},{1,3},{4,6},{5,7},{2,0},{3,1},{6,4},{7,5},{8,10},{9,11},{12,... | collective-permute-start | bytes 393224 | tf_op jit(solution)/shard_map/ppermute | solution.py:345
  11.3 0.7 %collective-permute-start.7 = (bf16[64,1024]{1,0:T(8,128)(2,1)}, bf16[64,1024]{1,0:T(8,128)(2,1)S(1)}, u32[]{:S(2)}, u32[]{:S(2)}) collective-permute-start(bf16[64,1024]{1,0:T(8,128)(2,1)} %bitcast.6), channel_id=1, source_target_pairs={{2,4},{3,5},{4,2},{5,3},{10,12},{11,13},{12,10},{13,11},{18,20},{1... | collective-permute-start | bytes 393224 | tf_op jit(solution)/shard_map/ppermute | solution.py:345
  12.0 1.1 %all-to-all-done.own = bf16[4,32,1280]{2,1,0:T(8,128)(2,1)S(1)} async-done(((bf16[4,32,1280]{2,1,0:T(8,128)(2,1)}), bf16[4,32,1280]{2,1,0:T(8,128)(2,1)S(1)}, u32[]{:S(2)}, u32[]{:S(2)}) %all-to-all-start) | async-done | bytes 327712 | tf_op jit(solution)/shard_map/all_to_all | solution.py:393
  13.2 0.1 collective-permute-start.2
  13.2 0.0 collective-permute-done.4.in_chip
  13.2 0.7 %collective-permute-start.3 = (bf16[80,1152]{1,0:T(8,128)(2,1)S(1)}, bf16[80,1152]{1,0:T(8,128)(2,1)S(1)}, u32[]{:S(2)}, u32[]{:S(2)}) collective-permute-start(bf16[80,1152]{1,0:T(8,128)(2,1)S(1)} %get-tuple-element.24), channel_id=1, source_target_pairs={{1,2},{3,4},{5,6},{2,1},{4,3},{6,5},{9,10},{11,12},{13,14},{10,9},... | collective-permute-start | bytes 552968 | tf_op jit(solution)/shard_map/ppermute | solution.py:345
  13.9 0.0 collective-permute-done.5.cross
  13.9 4.6 %collective-permute-start = (bf16[16,1152]{1,0:T(8,128)(2,1)S(1)}, bf16[16,1152]{1,0:T(8,128)(2,1)S(1)}, u32[]{:S(2)}, u32[]{:S(2)}) collective-permute-start(bf16[16,1152]{1,0:T(8,128)(2,1)S(1)} %get-tuple-element.21), channel_id=1, source_target_pairs={{0,2},{1,3},{4,6},{5,7},{2,0},{3,1},{6,4},{7,5},{8,10},{9,11},{12,... | collective-permute-start | bytes 110600 | tf_op jit(solution)/shard_map/ppermute | solution.py:345
  18.5 0.0 collective-permute-done.6.far_even
  18.5 0.7 %collective-permute-start.1 = (bf16[16,1152]{1,0:T(8,128)(2,1)S(1)}, bf16[16,1152]{1,0:T(8,128)(2,1)S(1)}, u32[]{:S(2)}, u32[]{:S(2)}) collective-permute-start(bf16[16,1152]{1,0:T(8,128)(2,1)S(1)} %get-tuple-element.22), channel_id=1, source_target_pairs={{2,4},{3,5},{4,2},{5,3},{10,12},{11,13},{12,10},{13,11},{18,20},{1... | collective-permute-start | bytes 110600 | tf_op jit(solution)/shard_map/ppermute | solution.py:345
  19.2 0.0 collective-permute-done.7.far_odd
  19.2 0.0 copy-done.1
  19.2 0.0 copy-done.2
  19.2 0.0 copy-start
  19.2 0.9 %copy-done = bf16[2,32,1024]{2,1,0:T(8,128)(2,1)S(1)} copy-done((bf16[2,32,1024]{2,1,0:T(8,128)(2,1)S(1)}, bf16[2,32,1024]{2,1,0:T(8,128)(2,1)}, u32[]{:S(2)}) %copy-start) | copy-done | bytes 131096
  20.1 0.0 copy-start.3
  20.1 1.1 %shard_map.112 = (f32[1024,256]{1,0:T(8,128)S(1)}, f32[2,128,1024]{2,1,0:T(8,128)S(1)}, f32[128,1024]{1,0:T(8,128)S(1)}, bf16[3,256,512]{2,1,0:T(8,128)(2,1)S(1)...) custom-call(bf16[4,32,1280]{2,1,0:T(8,128)(2,1)S(1)} %all-to-all-done.own, ...), custom_call_target="tpu_custom_call" | custom-call | flops 1000000000 | bytes 3000000 | tf_op jit(solution)/shard_map/pallas_call | solution.py:399
  21.3 0.0 copy-start.4
  21.3 0.0 collective-permute-done.2.light_in_chip
  21.3 0.0 collective-permute-done.3.light_cross
  21.3 0.0 copy-done.3
  21.3 0.7 %shard_map.111 = (f32[1280,256]{1,0:T(8,128)S(1)}, f32[160,1024]{1,0:T(8,128)S(1)}) custom-call(bf16[80,1152]{1,0:T(8,128)(2,1)S(1)} %collective-permute-done.2.light_in_chip, bf16[80,1152]{1,0:T(8,128)(2,1)S(1)} %collective-permute-done.3.light_cross, bf16[160,160]{1,0:T(8,128)(2,1)S(1)} %copy-done.3, bf16[256,256]{1,0:T(8,128)(2,1)S(1)} %copy-done.1), custom_call_target="tpu_custom_call" | custom-call | flops 500000000 | bytes 2000000 | tf_op jit(solution)/shard_map/pallas_call | solution.py:412
  22.0 0.7 %collective-permute-done.far_even = bf16[16,1152]{1,0:T(8,128)(2,1)S(1)} collective-permute-done((bf16[16,1152]{1,0:T(8,128)(2,1)S(1)}, bf16[16,1152]{1,0:T(8,128)(2,1)S(1)}, u32[]{:S(2)}, u32[]{:S(2)}) %collective-permute-start) | collective-permute-done | bytes 36896 | tf_op jit(solution)/shard_map/ppermute | solution.py:345
  22.7 0.0 collective-permute-done.1.far_odd
  22.7 0.0 copy-done.4
  22.8 2.1 %shard_map.113 = bf16[4,2,32,1024]{3,2,1,0:T(8,128)(2,1)S(1)} custom-call(bf16[16,1152]{1,0:T(8,128)(2,1)S(1)} %collective-permute-done.far_even, bf16[16,1152]{1,0:T(8,128)(2,1)S(1)} %collective-permute-done.1.far_odd, bf16[64,64]{1,0:T(8,128)(2,1)S(1)} %copy-done.4, bf16[256,256]{1,0:T(8,128)(2,1)S(1)} %copy-done.1, ...), custom_call_target="tpu_custom_call" | custom-call | flops 2000000000 | bytes 3000000 | tf_op jit(solution)/shard_map/pallas_call | solution.py:419
  24.9 12.8 %all_to_all.10 = bf16[4,2,32,1024]{3,2,1,0:T(8,128)(2,1)S(1)} all-to-all(bf16[4,2,32,1024]{3,2,1,0:T(8,128)(2,1)S(1)} %shard_map.113), channel_id=1, replica_groups=mesh['depth'=4,'rows'=8] {'depth'}, dimensions={0} | all-to-all | bytes 1048576 | tf_op jit(solution)/shard_map/all_to_all | solution.py:427
  37.7 0.8 %slice_bitcast_fusion = bf16[1,3,2,32,1024]{4,3,2,1,0:T(8,128)(2,1)} fusion(bf16[4,2,32,1024]{3,2,1,0:T(8,128)(2,1)S(1)} %all_to_all.10), kind=kLoop, calls=%fused_computation | loop fusion | bytes 786432 | tf_op jit(solution)/shard_map/broadcast_in_dim | solution.py:428
  (1 shorter events, 0.0 us)
Async XLA Ops:
  0.0 19.2 %copy-start.1 = (bf16[256,256]{1,0:T(8,128)(2,1)S(1)}, bf16[256,256]{1,0:T(8,128)(2,1)}, u32[]{:S(2)}) copy-start(bf16[256,256]{1,0:T(8,128)(2,1)} %constant.8.clone.right_tab) | copy-start | bytes 393220
  0.0 19.2 %copy-start.2 = (bf16[256,256]{1,0:T(8,128)(2,1)S(1)}, bf16[256,256]{1,0:T(8,128)(2,1)}, u32[]{:S(2)}) copy-start(bf16[256,256]{1,0:T(8,128)(2,1)} %constant.9.clone.left_tab) | copy-start | bytes 393220
  2.0 11.1 %all-to-all-start = ((bf16[4,32,1280]{2,1,0:T(8,128)(2,1)}), bf16[4,32,1280]{2,1,0:T(8,128)(2,1)S(1)}, u32[]{:S(2)}, u32[]{:S(2)}) async-start(bf16[4,32,1280]{2,1,0:T(8,128)(2,1)} %get-tuple-element.20), calls=%async_computation | async-start | bytes 655360 | tf_op jit(solution)/shard_map/all_to_all | solution.py:393
  7.2 6.0 %collective-permute-start.4 = (bf16[64,1024]{1,0:T(8,128)(2,1)}, bf16[64,1024]{1,0:T(8,128)(2,1)S(1)}, u32[]{:S(2)}, u32[]{:S(2)}) collective-permute-start(bf16[64,1024]{1,0:T(8,128)(2,1)} %bitcast.3), channel_id=1, source_target_pairs={{0,1},{2,3},{4,5},{6,7},{1,0},{3,2},{5,4},{7,6},{8,9},{10,11},{12,... | collective-permute-start | bytes 393224 | tf_op jit(solution)/shard_map/ppermute | solution.py:345
  7.2 6.7 %collective-permute-start.5 = (bf16[64,1024]{1,0:T(8,128)(2,1)}, bf16[64,1024]{1,0:T(8,128)(2,1)S(1)}, u32[]{:S(2)}, u32[]{:S(2)}) collective-permute-start(bf16[64,1024]{1,0:T(8,128)(2,1)} %bitcast.4), channel_id=1, source_target_pairs={{1,2},{3,4},{5,6},{2,1},{4,3},{6,5},{9,10},{11,12},{13,14},{10,9},... | collective-permute-start | bytes 393224 | tf_op jit(solution)/shard_map/ppermute | solution.py:345
  7.9 10.6 %collective-permute-start.6 = (bf16[64,1024]{1,0:T(8,128)(2,1)}, bf16[64,1024]{1,0:T(8,128)(2,1)S(1)}, u32[]{:S(2)}, u32[]{:S(2)}) collective-permute-start(bf16[64,1024]{1,0:T(8,128)(2,1)} %bitcast.5), channel_id=1, source_target_pairs={{0,2},{1,3},{4,6},{5,7},{2,0},{3,1},{6,4},{7,5},{8,10},{9,11},{12,... | collective-permute-start | bytes 393224 | tf_op jit(solution)/shard_map/ppermute | solution.py:345
  11.3 7.9 %collective-permute-start.7 = (bf16[64,1024]{1,0:T(8,128)(2,1)}, bf16[64,1024]{1,0:T(8,128)(2,1)S(1)}, u32[]{:S(2)}, u32[]{:S(2)}) collective-permute-start(bf16[64,1024]{1,0:T(8,128)(2,1)} %bitcast.6), channel_id=1, source_target_pairs={{2,4},{3,5},{4,2},{5,3},{10,12},{11,13},{12,10},{13,11},{18,20},{1... | collective-permute-start | bytes 393224 | tf_op jit(solution)/shard_map/ppermute | solution.py:345
  13.2 8.1 %collective-permute-start.2 = (bf16[80,1152]{1,0:T(8,128)(2,1)S(1)}, bf16[80,1152]{1,0:T(8,128)(2,1)S(1)}, u32[]{:S(2)}, u32[]{:S(2)}) collective-permute-start(bf16[80,1152]{1,0:T(8,128)(2,1)S(1)} %get-tuple-element.23), channel_id=1, source_target_pairs={{0,1},{2,3},{4,5},{6,7},{1,0},{3,2},{5,4},{7,6},{8,9},{10,11},{12,... | collective-permute-start | bytes 552968 | tf_op jit(solution)/shard_map/ppermute | solution.py:345
  13.2 8.0 %collective-permute-start.3 = (bf16[80,1152]{1,0:T(8,128)(2,1)S(1)}, bf16[80,1152]{1,0:T(8,128)(2,1)S(1)}, u32[]{:S(2)}, u32[]{:S(2)}) collective-permute-start(bf16[80,1152]{1,0:T(8,128)(2,1)S(1)} %get-tuple-element.24), channel_id=1, source_target_pairs={{1,2},{3,4},{5,6},{2,1},{4,3},{6,5},{9,10},{11,12},{13,14},{10,9},... | collective-permute-start | bytes 552968 | tf_op jit(solution)/shard_map/ppermute | solution.py:345
  13.9 8.8 %collective-permute-start = (bf16[16,1152]{1,0:T(8,128)(2,1)S(1)}, bf16[16,1152]{1,0:T(8,128)(2,1)S(1)}, u32[]{:S(2)}, u32[]{:S(2)}) collective-permute-start(bf16[16,1152]{1,0:T(8,128)(2,1)S(1)} %get-tuple-element.21), channel_id=1, source_target_pairs={{0,2},{1,3},{4,6},{5,7},{2,0},{3,1},{6,4},{7,5},{8,10},{9,11},{12,... | collective-permute-start | bytes 110600 | tf_op jit(solution)/shard_map/ppermute | solution.py:345
  18.5 4.2 %collective-permute-start.1 = (bf16[16,1152]{1,0:T(8,128)(2,1)S(1)}, bf16[16,1152]{1,0:T(8,128)(2,1)S(1)}, u32[]{:S(2)}, u32[]{:S(2)}) collective-permute-start(bf16[16,1152]{1,0:T(8,128)(2,1)S(1)} %get-tuple-element.22), channel_id=1, source_target_pairs={{2,4},{3,5},{4,2},{5,3},{10,12},{11,13},{12,10},{13,11},{18,20},{1... | collective-permute-start | bytes 110600 | tf_op jit(solution)/shard_map/ppermute | solution.py:345
  19.2 0.9 %copy-start = (bf16[2,32,1024]{2,1,0:T(8,128)(2,1)S(1)}, bf16[2,32,1024]{2,1,0:T(8,128)(2,1)}, u32[]{:S(2)}) copy-start(bf16[2,32,1024]{2,1,0:T(8,128)(2,1)} %get-tuple-element.27) | copy-start | bytes 393220
  20.1 1.2 %copy-start.3 = (bf16[160,160]{1,0:T(8,128)(2,1)S(1)}, bf16[160,160]{1,0:T(8,128)(2,1)}, u32[]{:S(2)}) copy-start(bf16[160,160]{1,0:T(8,128)(2,1)} %constant.10.clone.near_tab) | copy-start | bytes 153604
  21.3 1.5 %copy-start.4 = (bf16[64,64]{1,0:T(8,128)(2,1)S(1)}, bf16[64,64]{1,0:T(8,128)(2,1)}, u32[]{:S(2)}) copy-start(bf16[64,64]{1,0:T(8,128)(2,1)} %constant.11.clone.left_tab) | copy-start | bytes 24580

commit v17 on v16

--- a/solution.py
+++ b/solution.py
@@ -241,10 +241,14 @@
 ):
     low_near, high_near = near_sides(in_chip, cross)
     low_far, high_far = far_sides(far_even, far_odd)
+    colour = own_colour()
     extended = []
     for part in range(2):
-        pieces = [low_far, low_near, incident[...], high_near, high_far]
-        pieces = [piece[part * BAND : (part + 1) * BAND] for piece in pieces]
+        low_rows, near_rows, high_rows, top_rows = (
+            side[part * BAND : (part + 1) * BAND]
+            for side in (low_far, low_near, high_near, high_far)
+        )
+        pieces = [low_rows, near_rows, incident[colour, part], high_rows, top_rows]
         extended.append(jnp.concatenate(pieces, axis=0))
     row_mat, col_mat = filters(own[0, 0:16, HALO_W:].astype(jnp.float32), 0)
     first[...] = propagated(extended[0], extended[1], row_mat, col_mat, 0)
@@ -408,7 +412,7 @@
         [vmem] * 8,
         flops=10**9,
         moved=3 * 10**6,
-    )(own, mine, *arrived, jnp.asarray(left_table(LANES)), right_tab)
+    )(own, incident, *arrived, jnp.asarray(left_table(LANES)), right_tab)
     near_made = call(
         near_kernel,
         [shaped((2 * NEAR * TILES, 2 * LANES), f32), shaped((2 * NEAR, COLS), f32)],

time: 38.8 us -> 38.8 us (level)
  local copies, waits for them, and re-layouts: 1.69 us -> 0.79 us
  waiting for transfers between devices: 1.88 us -> 2.63 us
    unnamed x10, local copies, waits for them, and re-layouts: 0.92 us -> 0.02 us
    ppermute x8, waiting for transfers between devices: 0.76 us -> 1.52 us  [exchanged(): return lax.ppermute(value, axis, pairs)]
where the time goes in v17:
time: 38.8 us; the launch traced here: 38.5 us
  starting transfers between devices  16.1 us (41%)
  blocking collectives  12.8 us (33%)
  Pallas kernels  6.01 us (15%)
  waiting for transfers between devices  2.63 us (7%)
  local copies, waits for them, and re-layouts  0.79 us (2%)
    all_to_all x1, blocking collectives, body(): gathered = lax.all_to_all(result, 'depth', 0, 0, tiled=True)  12.8 us
    ppermute x8, starting transfers between devices, exchanged(): return lax.ppermute(value, axis, pairs)  10.9 us
    all_to_all x1, starting transfers between devices, body(): own = lax.all_to_all(payload, 'depth', 0, 0, tiled=True)  5.18 us
    pallas_call x1, Pallas kernels, body(): call(chain_kernel, shaped((LAYERS, 2, BAND, COLS), bf16), [vmem] * (6 + l...  2.11 us
    pallas_call x1, Pallas kernels, body(): call(pack_kernel, (shaped((LAYERS, BAND, FULL_W), bf16), shaped(incident....  2.06 us
    ppermute x8, waiting for transfers between devices, exchanged(): return lax.ppermute(value, axis, pairs)  1.52 us
    pallas_call x1, Pallas kernels, body(): call(prepare_kernel, [shaped((TILES * layer_height(0), 2 * LANES), f32),...  1.12 us
    all_to_all x1, waiting for transfers between devices, body(): own = lax.all_to_all(payload, 'depth', 0, 0, tiled=True)  1.11 us
  transfers between devices with their start and end apart: 9, of which 2 were waited for; matrix products, arithmetic and copies ran while one was open for 0% of the time, Pallas kernels for 5%

profile of v17, /device:TPU:0, one launch (start us, length us, event | category | flops | bytes accessed | tf_op | source)
XLA Modules:
  0.0 38.5 jit_solution(16858082283779661166)
XLA Ops:
  0.0 0.0 copy-start.1
  0.0 0.0 copy-start.2
  0.0 0.0 copy-start
  0.0 2.1 %shard_map.109 = (bf16[4,32,1280]{2,1,0:T(8,128)(2,1)}, bf16[2,32,1024]{2,1,0:T(8,128)(2,1)}) custom-call(f32[1,3,32,1024]{3,2,1,0:T(8,128)} %light.1, s32[1,32,64]{2,1,0:T(8,128)} %edges.1, s32[1,2]{1,0:T(1,128)} %counts.1, s32[1,2,64]{2,1,0:T(2,128)} %listed.1, bf16[1,3,2,33]{3,2,1,0:T(2,128)(2,1)} %row_taps.1, bf16[1,3,2,127]{3,2,1,0:T(2,128)(2,1)} %col_taps.1, ...), custom_call_target="tpu_custom_call" | custom-call | flops 10000000 | bytes 1000000 | tf_op jit(solution)/shard_map/pallas_call | solution.py:388
  2.1 5.2 %all-to-all-start = ((bf16[4,32,1280]{2,1,0:T(8,128)(2,1)}), bf16[4,32,1280]{2,1,0:T(8,128)(2,1)S(1)}, u32[]{:S(2)}, u32[]{:S(2)}) async-start(bf16[4,32,1280]{2,1,0:T(8,128)(2,1)} %get-tuple-element.20), calls=%async_computation | async-start | bytes 655360 | tf_op jit(solution)/shard_map/all_to_all | solution.py:397
  7.3 0.0 collective-permute-start.4
  7.3 0.7 %collective-permute-start.5 = (bf16[64,1024]{1,0:T(8,128)(2,1)}, bf16[64,1024]{1,0:T(8,128)(2,1)S(1)}, u32[]{:S(2)}, u32[]{:S(2)}) collective-permute-start(bf16[64,1024]{1,0:T(8,128)(2,1)} %bitcast.4), channel_id=1, source_target_pairs={{1,2},{3,4},{5,6},{2,1},{4,3},{6,5},{9,10},{11,12},{13,14},{10,9},... | collective-permute-start | bytes 393224 | tf_op jit(solution)/shard_map/ppermute | solution.py:349
  7.9 3.4 %collective-permute-start.6 = (bf16[64,1024]{1,0:T(8,128)(2,1)}, bf16[64,1024]{1,0:T(8,128)(2,1)S(1)}, u32[]{:S(2)}, u32[]{:S(2)}) collective-permute-start(bf16[64,1024]{1,0:T(8,128)(2,1)} %bitcast.5), channel_id=1, source_target_pairs={{0,2},{1,3},{4,6},{5,7},{2,0},{3,1},{6,4},{7,5},{8,10},{9,11},{12,... | collective-permute-start | bytes 393224 | tf_op jit(solution)/shard_map/ppermute | solution.py:349
  11.4 0.7 %collective-permute-start.7 = (bf16[64,1024]{1,0:T(8,128)(2,1)}, bf16[64,1024]{1,0:T(8,128)(2,1)S(1)}, u32[]{:S(2)}, u32[]{:S(2)}) collective-permute-start(bf16[64,1024]{1,0:T(8,128)(2,1)} %bitcast.6), channel_id=1, source_target_pairs={{2,4},{3,5},{4,2},{5,3},{10,12},{11,13},{12,10},{13,11},{18,20},{1... | collective-permute-start | bytes 393224 | tf_op jit(solution)/shard_map/ppermute | solution.py:349
  12.0 1.1 %all-to-all-done.own = bf16[4,32,1280]{2,1,0:T(8,128)(2,1)S(1)} async-done(((bf16[4,32,1280]{2,1,0:T(8,128)(2,1)}), bf16[4,32,1280]{2,1,0:T(8,128)(2,1)S(1)}, u32[]{:S(2)}, u32[]{:S(2)}) %all-to-all-start) | async-done | bytes 327712 | tf_op jit(solution)/shard_map/all_to_all | solution.py:397
  13.2 0.1 collective-permute-start.2
  13.3 0.0 collective-permute-done.4.in_chip
  13.3 0.7 %collective-permute-start.3 = (bf16[80,1152]{1,0:T(8,128)(2,1)S(1)}, bf16[80,1152]{1,0:T(8,128)(2,1)S(1)}, u32[]{:S(2)}, u32[]{:S(2)}) collective-permute-start(bf16[80,1152]{1,0:T(8,128)(2,1)S(1)} %get-tuple-element.24), channel_id=1, source_target_pairs={{1,2},{3,4},{5,6},{2,1},{4,3},{6,5},{9,10},{11,12},{13,14},{10,9},... | collective-permute-start | bytes 552968 | tf_op jit(solution)/shard_map/ppermute | solution.py:349
  13.9 0.0 collective-permute-done.5.cross
  14.0 4.6 %collective-permute-start = (bf16[16,1152]{1,0:T(8,128)(2,1)S(1)}, bf16[16,1152]{1,0:T(8,128)(2,1)S(1)}, u32[]{:S(2)}, u32[]{:S(2)}) collective-permute-start(bf16[16,1152]{1,0:T(8,128)(2,1)S(1)} %get-tuple-element.21), channel_id=1, source_target_pairs={{0,2},{1,3},{4,6},{5,7},{2,0},{3,1},{6,4},{7,5},{8,10},{9,11},{12,... | collective-permute-start | bytes 110600 | tf_op jit(solution)/shard_map/ppermute | solution.py:349
  18.6 0.0 collective-permute-done.6.far_even
  18.6 0.0 copy-start.3
  18.6 0.8 %collective-permute-start.1 = (bf16[16,1152]{1,0:T(8,128)(2,1)S(1)}, bf16[16,1152]{1,0:T(8,128)(2,1)S(1)}, u32[]{:S(2)}, u32[]{:S(2)}) collective-permute-start(bf16[16,1152]{1,0:T(8,128)(2,1)S(1)} %get-tuple-element.22), channel_id=1, source_target_pairs={{2,4},{3,5},{4,2},{5,3},{10,12},{11,13},{12,10},{13,11},{18,20},{1... | collective-permute-start | bytes 110600 | tf_op jit(solution)/shard_map/ppermute | solution.py:349
  19.4 0.0 collective-permute-done.7.far_odd
  19.4 0.0 copy-done.1
  19.4 0.0 copy-done.2
  19.4 0.0 copy-done
  19.4 1.1 %shard_map.112 = (f32[1024,256]{1,0:T(8,128)S(1)}, f32[2,128,1024]{2,1,0:T(8,128)S(1)}, f32[128,1024]{1,0:T(8,128)S(1)}, bf16[3,256,512]{2,1,0:T(8,128)(2,1)S(1)...) custom-call(bf16[4,32,1280]{2,1,0:T(8,128)(2,1)S(1)} %all-to-all-done.own, ...), custom_call_target="tpu_custom_call" | custom-call | flops 1000000000 | bytes 3000000 | tf_op jit(solution)/shard_map/pallas_call | solution.py:403
  20.5 0.0 copy-start.4
  20.5 0.0 collective-permute-done.2.light_in_chip
  20.6 0.0 collective-permute-done.3.light_cross
  20.6 0.0 copy-done.3
  20.6 0.7 %shard_map.111 = (f32[1280,256]{1,0:T(8,128)S(1)}, f32[160,1024]{1,0:T(8,128)S(1)}) custom-call(bf16[80,1152]{1,0:T(8,128)(2,1)S(1)} %collective-permute-done.2.light_in_chip, bf16[80,1152]{1,0:T(8,128)(2,1)S(1)} %collective-permute-done.3.light_cross, bf16[160,160]{1,0:T(8,128)(2,1)S(1)} %copy-done.3, bf16[256,256]{1,0:T(8,128)(2,1)S(1)} %copy-done.1), custom_call_target="tpu_custom_call" | custom-call | flops 500000000 | bytes 2000000 | tf_op jit(solution)/shard_map/pallas_call | solution.py:416
  21.3 1.5 %collective-permute-done.far_even = bf16[16,1152]{1,0:T(8,128)(2,1)S(1)} collective-permute-done((bf16[16,1152]{1,0:T(8,128)(2,1)S(1)}, bf16[16,1152]{1,0:T(8,128)(2,1)S(1)}, u32[]{:S(2)}, u32[]{:S(2)}) %collective-permute-start) | collective-permute-done | bytes 36896 | tf_op jit(solution)/shard_map/ppermute | solution.py:349
  22.8 0.0 collective-permute-done.1.far_odd
  22.8 0.0 copy-done.4
  22.8 2.1 %shard_map.113 = bf16[4,2,32,1024]{3,2,1,0:T(8,128)(2,1)S(1)} custom-call(bf16[16,1152]{1,0:T(8,128)(2,1)S(1)} %collective-permute-done.far_even, bf16[16,1152]{1,0:T(8,128)(2,1)S(1)} %collective-permute-done.1.far_odd, bf16[64,64]{1,0:T(8,128)(2,1)S(1)} %copy-done.4, bf16[256,256]{1,0:T(8,128)(2,1)S(1)} %copy-done.1, ...), custom_call_target="tpu_custom_call" | custom-call | flops 2000000000 | bytes 3000000 | tf_op jit(solution)/shard_map/pallas_call | solution.py:423
  24.9 12.8 %all_to_all.10 = bf16[4,2,32,1024]{3,2,1,0:T(8,128)(2,1)S(1)} all-to-all(bf16[4,2,32,1024]{3,2,1,0:T(8,128)(2,1)S(1)} %shard_map.113), channel_id=1, replica_groups=mesh['depth'=4,'rows'=8] {'depth'}, dimensions={0} | all-to-all | bytes 1048576 | tf_op jit(solution)/shard_map/all_to_all | solution.py:431
  37.7 0.8 %slice_bitcast_fusion = bf16[1,3,2,32,1024]{4,3,2,1,0:T(8,128)(2,1)} fusion(bf16[4,2,32,1024]{3,2,1,0:T(8,128)(2,1)S(1)} %all_to_all.10), kind=kLoop, calls=%fused_computation | loop fusion | bytes 786432 | tf_op jit(solution)/shard_map/broadcast_in_dim | solution.py:432
  (1 shorter events, 0.0 us)
Async XLA Ops:
  0.0 19.4 %copy-start.1 = (bf16[256,256]{1,0:T(8,128)(2,1)S(1)}, bf16[256,256]{1,0:T(8,128)(2,1)}, u32[]{:S(2)}) copy-start(bf16[256,256]{1,0:T(8,128)(2,1)} %constant.8.clone.right_tab) | copy-start | bytes 393220
  0.0 19.4 %copy-start.2 = (bf16[256,256]{1,0:T(8,128)(2,1)S(1)}, bf16[256,256]{1,0:T(8,128)(2,1)}, u32[]{:S(2)}) copy-start(bf16[256,256]{1,0:T(8,128)(2,1)} %constant.9.clone.left_tab) | copy-start | bytes 393220
  0.0 19.4 %copy-start = (bf16[3,2,32,1024]{3,2,1,0:T(8,128)(2,1)S(1)}, bf16[3,2,32,1024]{3,2,1,0:T(8,128)(2,1)}, u32[]{:S(2)}) copy-start(bf16[3,2,32,1024]{3,2,1,0:T(8,128)(2,1)} %incident.3) | copy-start | bytes 1179652
  2.1 11.1 %all-to-all-start = ((bf16[4,32,1280]{2,1,0:T(8,128)(2,1)}), bf16[4,32,1280]{2,1,0:T(8,128)(2,1)S(1)}, u32[]{:S(2)}, u32[]{:S(2)}) async-start(bf16[4,32,1280]{2,1,0:T(8,128)(2,1)} %get-tuple-element.20), calls=%async_computation | async-start | bytes 655360 | tf_op jit(solution)/shard_map/all_to_all | solution.py:397
  7.3 6.0 %collective-permute-start.4 = (bf16[64,1024]{1,0:T(8,128)(2,1)}, bf16[64,1024]{1,0:T(8,128)(2,1)S(1)}, u32[]{:S(2)}, u32[]{:S(2)}) collective-permute-start(bf16[64,1024]{1,0:T(8,128)(2,1)} %bitcast.3), channel_id=1, source_target_pairs={{0,1},{2,3},{4,5},{6,7},{1,0},{3,2},{5,4},{7,6},{8,9},{10,11},{12,... | collective-permute-start | bytes 393224 | tf_op jit(solution)/shard_map/ppermute | solution.py:349
  7.3 6.7 %collective-permute-start.5 = (bf16[64,1024]{1,0:T(8,128)(2,1)}, bf16[64,1024]{1,0:T(8,128)(2,1)S(1)}, u32[]{:S(2)}, u32[]{:S(2)}) collective-permute-start(bf16[64,1024]{1,0:T(8,128)(2,1)} %bitcast.4), channel_id=1, source_target_pairs={{1,2},{3,4},{5,6},{2,1},{4,3},{6,5},{9,10},{11,12},{13,14},{10,9},... | collective-permute-start | bytes 393224 | tf_op jit(solution)/shard_map/ppermute | solution.py:349
  7.9 10.6 %collective-permute-start.6 = (bf16[64,1024]{1,0:T(8,128)(2,1)}, bf16[64,1024]{1,0:T(8,128)(2,1)S(1)}, u32[]{:S(2)}, u32[]{:S(2)}) collective-permute-start(bf16[64,1024]{1,0:T(8,128)(2,1)} %bitcast.5), channel_id=1, source_target_pairs={{0,2},{1,3},{4,6},{5,7},{2,0},{3,1},{6,4},{7,5},{8,10},{9,11},{12,... | collective-permute-start | bytes 393224 | tf_op jit(solution)/shard_map/ppermute | solution.py:349
  11.4 8.0 %collective-permute-start.7 = (bf16[64,1024]{1,0:T(8,128)(2,1)}, bf16[64,1024]{1,0:T(8,128)(2,1)S(1)}, u32[]{:S(2)}, u32[]{:S(2)}) collective-permute-start(bf16[64,1024]{1,0:T(8,128)(2,1)} %bitcast.6), channel_id=1, source_target_pairs={{2,4},{3,5},{4,2},{5,3},{10,12},{11,13},{12,10},{13,11},{18,20},{1... | collective-permute-start | bytes 393224 | tf_op jit(solution)/shard_map/ppermute | solution.py:349
  13.2 7.4 %collective-permute-start.2 = (bf16[80,1152]{1,0:T(8,128)(2,1)S(1)}, bf16[80,1152]{1,0:T(8,128)(2,1)S(1)}, u32[]{:S(2)}, u32[]{:S(2)}) collective-permute-start(bf16[80,1152]{1,0:T(8,128)(2,1)S(1)} %get-tuple-element.23), channel_id=1, source_target_pairs={{0,1},{2,3},{4,5},{6,7},{1,0},{3,2},{5,4},{7,6},{8,9},{10,11},{12,... | collective-permute-start | bytes 552968 | tf_op jit(solution)/shard_map/ppermute | solution.py:349
  13.3 7.3 %collective-permute-start.3 = (bf16[80,1152]{1,0:T(8,128)(2,1)S(1)}, bf16[80,1152]{1,0:T(8,128)(2,1)S(1)}, u32[]{:S(2)}, u32[]{:S(2)}) collective-permute-start(bf16[80,1152]{1,0:T(8,128)(2,1)S(1)} %get-tuple-element.24), channel_id=1, source_target_pairs={{1,2},{3,4},{5,6},{2,1},{4,3},{6,5},{9,10},{11,12},{13,14},{10,9},... | collective-permute-start | bytes 552968 | tf_op jit(solution)/shard_map/ppermute | solution.py:349
  14.0 8.8 %collective-permute-start = (bf16[16,1152]{1,0:T(8,128)(2,1)S(1)}, bf16[16,1152]{1,0:T(8,128)(2,1)S(1)}, u32[]{:S(2)}, u32[]{:S(2)}) collective-permute-start(bf16[16,1152]{1,0:T(8,128)(2,1)S(1)} %get-tuple-element.21), channel_id=1, source_target_pairs={{0,2},{1,3},{4,6},{5,7},{2,0},{3,1},{6,4},{7,5},{8,10},{9,11},{12,... | collective-permute-start | bytes 110600 | tf_op jit(solution)/shard_map/ppermute | solution.py:349
  18.6 2.0 %copy-start.3 = (bf16[160,160]{1,0:T(8,128)(2,1)S(1)}, bf16[160,160]{1,0:T(8,128)(2,1)}, u32[]{:S(2)}) copy-start(bf16[160,160]{1,0:T(8,128)(2,1)} %constant.10.clone.near_tab) | copy-start | bytes 153604
  18.6 4.2 %collective-permute-start.1 = (bf16[16,1152]{1,0:T(8,128)(2,1)S(1)}, bf16[16,1152]{1,0:T(8,128)(2,1)S(1)}, u32[]{:S(2)}, u32[]{:S(2)}) collective-permute-start(bf16[16,1152]{1,0:T(8,128)(2,1)S(1)} %get-tuple-element.22), channel_id=1, source_target_pairs={{2,4},{3,5},{4,2},{5,3},{10,12},{11,13},{12,10},{13,11},{18,20},{1... | collective-permute-start | bytes 110600 | tf_op jit(solution)/shard_map/ppermute | solution.py:349
  20.5 2.3 %copy-start.4 = (bf16[64,64]{1,0:T(8,128)(2,1)S(1)}, bf16[64,64]{1,0:T(8,128)(2,1)}, u32[]{:S(2)}) copy-start(bf16[64,64]{1,0:T(8,128)(2,1)} %constant.11.clone.left_tab) | copy-start | bytes 24580

commit v18 on v8

--- a/solution.py
+++ b/solution.py
@@ -20,7 +20,6 @@
 TILES = COLS // LANES
 HALO_W = COLS + LANES
 HALF = LANES // 2
-FULL_W = COLS + 2 * LANES
 NEAR = 2 * BAND + KR
 FAR = KR
 VMEM_LIMIT = 48 * 1024 * 1024
@@ -107,15 +106,19 @@
     live_pix = jnp.dot(live_rows, spread, preferred_element_type=jnp.float32)
     edge_tile = jnp.concatenate(
         [edges[0].astype(jnp.float32), jnp.zeros((BAND, LANES - NH), jnp.float32)], axis=1
-    ).astype(jnp.bfloat16)
+    )
+    left_half = lax.broadcasted_iota(jnp.int32, (BAND, LANES), 1) < HALF
     for colour in range(COLORS):
-        out[colour, :, COLS:HALO_W] = edge_tile
         taps[...] = jnp.zeros_like(taps)
-        taps[0:2, : 2 * KC + 1] = col_taps[0, colour].astype(jnp.float32)
-        taps[2:4, : 2 * KR + 1] = row_taps[0, colour].astype(jnp.float32)
-        out[colour, :, HALO_W:] = taps[...].astype(jnp.bfloat16)
+        taps[2:4, : 2 * KC + 1] = col_taps[0, colour].astype(jnp.float32)
+        taps[4:6, : 2 * KR + 1] = row_taps[0, colour].astype(jnp.float32)
+        turned = pltpu.roll(taps[0:8], HALF, 1)
+        taps[0:2] = turned[2:4]
+        taps[4:6] = turned[4:6]
+        tile = jnp.where(left_half, edge_tile, taps[...])
+        out[colour, :, COLS:] = tile.astype(jnp.bfloat16)
     for spare in range(COLORS, LAYERS):
-        out[spare] = jnp.zeros((BAND, FULL_W), jnp.bfloat16)
+        out[spare] = jnp.zeros((BAND, HALO_W), jnp.bfloat16)
     copies[5].wait()
     for colour in range(COLORS):
         out[colour, :, :COLS] = (light[0, colour] * live_pix).astype(jnp.bfloat16)
@@ -187,15 +190,19 @@
     return pltpu.roll(base, shift, 1, stride=1, stride_axis=0)
 
 
-def filters(taps, layer):
-    row_re, row_im = taps[2:3], taps[3:4]
+def filters(tile, layer):
+    turned = pltpu.roll(tile[0:8], HALF, 1)
+    left_half = lax.broadcasted_iota(jnp.int32, (2, LANES), 1) < HALF
+    col_taps = jnp.where(left_half, turned[0:2], tile[2:4])
+    row_taps = jnp.where(left_half, turned[4:6], 0.0)
+    row_re, row_im = row_taps[0:1], row_taps[1:2]
     height = block_height(layer)
     before = height + 2 * KR
     upper = banded(row_re, height, 0) - banded(row_im, height, before)
     lower = banded(row_im, height, 0) + banded(row_re, height, before)
     row_mat = jnp.concatenate([upper, lower], axis=0).astype(jnp.bfloat16)
-    col_re = banded(taps[0:1], LANES, 1)
-    col_im = banded(taps[1:2], LANES, 1)
+    col_re = banded(col_taps[0:1], LANES, 1)
+    col_im = banded(col_taps[1:2], LANES, 1)
     upper = jnp.concatenate([col_re, -col_im], axis=1)
     lower = jnp.concatenate([col_im, col_re], axis=1)
     col_mat = jnp.concatenate([upper, lower], axis=0).astype(jnp.bfloat16)
@@ -247,10 +254,10 @@
         pieces = [low_far, low_near, incident[...], high_near, high_far]
         pieces = [piece[part * BAND : (part + 1) * BAND] for piece in pieces]
         extended.append(jnp.concatenate(pieces, axis=0))
-    row_mat, col_mat = filters(own[0, 0:16, HALO_W:].astype(jnp.float32), 0)
+    row_mat, col_mat = filters(own[0, 0:16, COLS:].astype(jnp.float32), 0)
     first[...] = propagated(extended[0], extended[1], row_mat, col_mat, 0)
     for layer in range(1, LAYERS):
-        row_mat, col_mat = filters(own[layer, 0:16, HALO_W:].astype(jnp.float32), layer)
+        row_mat, col_mat = filters(own[layer, 0:16, COLS:].astype(jnp.float32), layer)
         row_mats[layer - 1][...] = row_mat
         col_mats[layer - 1] = col_mat
     packed = jnp.concatenate([own[layer, :, :HALO_W] for layer in range(LAYERS)], axis=0)
@@ -367,7 +374,7 @@
     ]
     payload, mine = call(
         pack_kernel,
-        (shaped((LAYERS, BAND, FULL_W), bf16), shaped(incident.shape[1:], bf16)),
+        (shaped((LAYERS, BAND, HALO_W), bf16), shaped(incident.shape[1:], bf16)),
         [hbm] * 7,
         held + [pltpu.SemaphoreType.DMA((7,)), pltpu.VMEM((BAND, LANES), f32)],
         flops=10**7,

time: 38.6 us -> 38.6 us (level)
  no operation moved by 1% of the time
where the time goes in v18:
time: 38.6 us; the launch traced here: 38.2 us
  starting transfers between devices  16.6 us (43%)
  blocking collectives  12.1 us (31%)
  Pallas kernels  5.68 us (15%)
  waiting for transfers between devices  2.97 us (8%)
  local copies, waits for them, and re-layouts  0.79 us (2%)
    all_to_all x1, blocking collectives, body(): gathered = lax.all_to_all(result, 'depth', 0, 0, tiled=True)  12.1 us
    ppermute x8, starting transfers between devices, exchanged(): return lax.ppermute(value, axis, pairs)  11.3 us
    all_to_all x1, starting transfers between devices, body(): own = lax.all_to_all(payload, 'depth', 0, 0, tiled=True)  5.31 us
    pallas_call x1, Pallas kernels, body(): call(chain_kernel, shaped((LAYERS, 2, BAND, COLS), bf16), [vmem] * (6 + l...  2.46 us
    ppermute x8, waiting for transfers between devices, exchanged(): return lax.ppermute(value, axis, pairs)  2.2 us
    pallas_call x1, Pallas kernels, body(): call(pack_kernel, (shaped((LAYERS, BAND, HALO_W), bf16), shaped(incident....  1.99 us
    pallas_call x1, Pallas kernels, body(): call(prepare_kernel, [shaped((TILES * layer_height(0), 2 * LANES), f32),...  1.19 us
    broadcast_in_dim x1, local copies, waits for them, and re-layouts, body(): return gathered[None, :COLORS]  0.77 us
  transfers between devices with their start and end apart: 9, of which 2 were waited for; matrix products, arithmetic and copies ran while one was open for 0% of the time, Pallas kernels for 3%

profile of v18, /device:TPU:0, one launch (start us, length us, event | category | flops | bytes accessed | tf_op | source)
XLA Modules:
  0.0 38.2 jit_solution(11011723446013781904)
XLA Ops:
  0.0 2.0 %shard_map.100 = (bf16[4,32,1152]{2,1,0:T(8,128)(2,1)}, bf16[2,32,1024]{2,1,0:T(8,128)(2,1)}) custom-call(f32[1,3,32,1024]{3,2,1,0:T(8,128)} %light.1, s32[1,32,64]{2,1,0:T(8,128)} %edges.1, s32[1,2]{1,0:T(1,128)} %counts.1, s32[1,2,64]{2,1,0:T(2,128)} %listed.1, bf16[1,3,2,33]{3,2,1,0:T(2,128)(2,1)} %row_taps.1, bf16[1,3,2,127]{3,2,1,0:T(2,128)(2,1)} %col_taps.1, ...), custom_call_target="tpu_custom_call" | custom-call | flops 10000000 | bytes 1000000 | tf_op jit(solution)/shard_map/pallas_call | solution.py:375
  2.0 0.0 copy-start
  2.0 5.3 %all-to-all-start = ((bf16[4,32,1152]{2,1,0:T(8,128)(2,1)}), bf16[4,32,1152]{2,1,0:T(8,128)(2,1)S(1)}, u32[]{:S(2)}, u32[]{:S(2)}) async-start(bf16[4,32,1152]{2,1,0:T(8,128)(2,1)} %get-tuple-element.18), calls=%async_computation | async-start | bytes 589824 | tf_op jit(solution)/shard_map/all_to_all | solution.py:384
  7.3 0.0 copy-done
  7.3 0.0 copy-start.1
  7.3 0.0 copy-start.2
  7.3 0.1 collective-permute-start.4
  7.4 0.8 %collective-permute-start.5 = (bf16[64,1024]{1,0:T(8,128)(2,1)S(1)}, bf16[64,1024]{1,0:T(8,128)(2,1)S(1)}, u32[]{:S(2)}, u32[]{:S(2)}) collective-permute-start(bf16[64,1024]{1,0:T(8,128)(2,1)S(1)} %bitcast.4), channel_id=1, source_target_pairs={{1,2},{3,4},{5,6},{2,1},{4,3},{6,5},{9,10},{11,12},{13,14},{10,9},... | collective-permute-start | bytes 393224 | tf_op jit(solution)/shard_map/ppermute | solution.py:336
  8.2 3.3 %collective-permute-start.6 = (bf16[64,1024]{1,0:T(8,128)(2,1)S(1)}, bf16[64,1024]{1,0:T(8,128)(2,1)S(1)}, u32[]{:S(2)}, u32[]{:S(2)}) collective-permute-start(bf16[64,1024]{1,0:T(8,128)(2,1)S(1)} %bitcast.5), channel_id=1, source_target_pairs={{0,2},{1,3},{4,6},{5,7},{2,0},{3,1},{6,4},{7,5},{8,10},{9,11},{12,... | collective-permute-start | bytes 393224 | tf_op jit(solution)/shard_map/ppermute | solution.py:336
  11.5 0.7 %collective-permute-start.7 = (bf16[64,1024]{1,0:T(8,128)(2,1)S(1)}, bf16[64,1024]{1,0:T(8,128)(2,1)S(1)}, u32[]{:S(2)}, u32[]{:S(2)}) collective-permute-start(bf16[64,1024]{1,0:T(8,128)(2,1)S(1)} %bitcast.6), channel_id=1, source_target_pairs={{2,4},{3,5},{4,2},{5,3},{10,12},{11,13},{12,10},{13,11},{18,20},{1... | collective-permute-start | bytes 393224 | tf_op jit(solution)/shard_map/ppermute | solution.py:336
  12.2 0.8 %all-to-all-done.own = bf16[4,32,1152]{2,1,0:T(8,128)(2,1)S(1)} async-done(((bf16[4,32,1152]{2,1,0:T(8,128)(2,1)}), bf16[4,32,1152]{2,1,0:T(8,128)(2,1)S(1)}, u32[]{:S(2)}, u32[]{:S(2)}) %all-to-all-start) | async-done | bytes 294944 | tf_op jit(solution)/shard_map/all_to_all | solution.py:384
  13.0 0.3 collective-permute-start
  13.3 0.0 collective-permute-done.4.in_chip
  13.3 0.7 %collective-permute-start.1 = (bf16[80,1152]{1,0:T(8,128)(2,1)S(1)}, bf16[80,1152]{1,0:T(8,128)(2,1)S(1)}, u32[]{:S(2)}, u32[]{:S(2)}) collective-permute-start(bf16[80,1152]{1,0:T(8,128)(2,1)S(1)} %get-tuple-element.20), channel_id=1, source_target_pairs={{1,2},{3,4},{5,6},{2,1},{4,3},{6,5},{9,10},{11,12},{13,14},{10,9},... | collective-permute-start | bytes 552968 | tf_op jit(solution)/shard_map/ppermute | solution.py:336
  14.0 0.0 collective-permute-done.5.cross
  14.0 4.7 %collective-permute-start.2 = (bf16[16,1152]{1,0:T(8,128)(2,1)S(1)}, bf16[16,1152]{1,0:T(8,128)(2,1)S(1)}, u32[]{:S(2)}, u32[]{:S(2)}) collective-permute-start(bf16[16,1152]{1,0:T(8,128)(2,1)S(1)} %get-tuple-element.21), channel_id=1, source_target_pairs={{0,2},{1,3},{4,6},{5,7},{2,0},{3,1},{6,4},{7,5},{8,10},{9,11},{12,... | collective-permute-start | bytes 110600 | tf_op jit(solution)/shard_map/ppermute | solution.py:336
  18.7 0.0 collective-permute-done.6.far_even
  18.7 0.0 copy-start.3
  18.7 0.8 %collective-permute-start.3 = (bf16[16,1152]{1,0:T(8,128)(2,1)S(1)}, bf16[16,1152]{1,0:T(8,128)(2,1)S(1)}, u32[]{:S(2)}, u32[]{:S(2)}) collective-permute-start(bf16[16,1152]{1,0:T(8,128)(2,1)S(1)} %get-tuple-element.22), channel_id=1, source_target_pairs={{2,4},{3,5},{4,2},{5,3},{10,12},{11,13},{12,10},{13,11},{18,20},{1... | collective-permute-start | bytes 110600 | tf_op jit(solution)/shard_map/ppermute | solution.py:336
  19.5 0.0 collective-permute-done.7.far_odd
  19.5 0.0 copy-done.1
  19.5 0.0 copy-done.2
  19.5 1.2 %shard_map.102 = (f32[1024,256]{1,0:T(8,128)S(1)}, f32[2,128,1024]{2,1,0:T(8,128)S(1)}, f32[128,1024]{1,0:T(8,128)S(1)}, bf16[3,256,512]{2,1,0:T(8,128)(2,1)S(1)...) custom-call(bf16[4,32,1152]{2,1,0:T(8,128)(2,1)S(1)} %all-to-all-done.own, ...), custom_call_target="tpu_custom_call" | custom-call | flops 1000000000 | bytes 3000000 | tf_op jit(solution)/shard_map/pallas_call | solution.py:390
  20.7 2.2 %collective-permute-done.2.far_even = bf16[16,1152]{1,0:T(8,128)(2,1)S(1)} collective-permute-done((bf16[16,1152]{1,0:T(8,128)(2,1)S(1)}, bf16[16,1152]{1,0:T(8,128)(2,1)S(1)}, u32[]{:S(2)}, u32[]{:S(2)}) %collective-permute-start.2) | collective-permute-done | bytes 36896 | tf_op jit(solution)/shard_map/ppermute | solution.py:336
  22.9 0.0 collective-permute-done.3.far_odd
  22.9 0.0 collective-permute-done.in_chip
  22.9 0.0 collective-permute-done.1.cross
  22.9 0.0 copy-done.3
  22.9 2.5 %shard_map.103 = bf16[4,2,32,1024]{3,2,1,0:T(8,128)(2,1)S(1)} custom-call(bf16[80,1152]{1,0:T(8,128)(2,1)S(1)} %collective-permute-done.in_chip, bf16[80,1152]{1,0:T(8,128)(2,1)S(1)} %collective-permute-done.1.cross, bf16[16,1152]{1,0:T(8,128)(2,1)S(1)} %collective-permute-done.2.far_even, bf16[16,1152]{1,0:T(8,128)(2,1)S(1)} %collective-permute-done.3.far_odd, ...), custom_call_target="tpu_custom_call" | custom-call | flops 2000000000 | bytes 3000000 | tf_op jit(solution)/shard_map/pallas_call | solution.py:404
  25.4 12.1 %all_to_all.10 = bf16[4,2,32,1024]{3,2,1,0:T(8,128)(2,1)S(1)} all-to-all(bf16[4,2,32,1024]{3,2,1,0:T(8,128)(2,1)S(1)} %shard_map.103), channel_id=1, replica_groups=mesh['depth'=4,'rows'=8] {'depth'}, dimensions={0} | all-to-all | bytes 1048576 | tf_op jit(solution)/shard_map/all_to_all | solution.py:412
  37.5 0.8 %slice_bitcast_fusion = bf16[1,3,2,32,1024]{4,3,2,1,0:T(8,128)(2,1)} fusion(bf16[4,2,32,1024]{3,2,1,0:T(8,128)(2,1)S(1)} %all_to_all.10), kind=kLoop, calls=%fused_computation | loop fusion | bytes 786432 | tf_op jit(solution)/shard_map/broadcast_in_dim | solution.py:413
  (1 shorter events, 0.0 us)
Async XLA Ops:
  2.0 5.3 %copy-start = (bf16[2,32,1024]{2,1,0:T(8,128)(2,1)S(1)}, bf16[2,32,1024]{2,1,0:T(8,128)(2,1)}, u32[]{:S(2)}) copy-start(bf16[2,32,1024]{2,1,0:T(8,128)(2,1)} %get-tuple-element.23) | copy-start | bytes 393220
  2.0 10.9 %all-to-all-start = ((bf16[4,32,1152]{2,1,0:T(8,128)(2,1)}), bf16[4,32,1152]{2,1,0:T(8,128)(2,1)S(1)}, u32[]{:S(2)}, u32[]{:S(2)}) async-start(bf16[4,32,1152]{2,1,0:T(8,128)(2,1)} %get-tuple-element.18), calls=%async_computation | async-start | bytes 589824 | tf_op jit(solution)/shard_map/all_to_all | solution.py:384
  7.3 12.2 %copy-start.1 = (bf16[256,256]{1,0:T(8,128)(2,1)S(1)}, bf16[256,256]{1,0:T(8,128)(2,1)}, u32[]{:S(2)}) copy-start(bf16[256,256]{1,0:T(8,128)(2,1)} %constant.6.clone.right_tab) | copy-start | bytes 393220
  7.3 12.2 %copy-start.2 = (bf16[256,256]{1,0:T(8,128)(2,1)S(1)}, bf16[256,256]{1,0:T(8,128)(2,1)}, u32[]{:S(2)}) copy-start(bf16[256,256]{1,0:T(8,128)(2,1)} %constant.7.clone.left_tab) | copy-start | bytes 393220
  7.3 6.0 %collective-permute-start.4 = (bf16[64,1024]{1,0:T(8,128)(2,1)S(1)}, bf16[64,1024]{1,0:T(8,128)(2,1)S(1)}, u32[]{:S(2)}, u32[]{:S(2)}) collective-permute-start(bf16[64,1024]{1,0:T(8,128)(2,1)S(1)} %bitcast.3), channel_id=1, source_target_pairs={{0,1},{2,3},{4,5},{6,7},{1,0},{3,2},{5,4},{7,6},{8,9},{10,11},{12,... | collective-permute-start | bytes 393224 | tf_op jit(solution)/shard_map/ppermute | solution.py:336
  7.4 6.6 %collective-permute-start.5 = (bf16[64,1024]{1,0:T(8,128)(2,1)S(1)}, bf16[64,1024]{1,0:T(8,128)(2,1)S(1)}, u32[]{:S(2)}, u32[]{:S(2)}) collective-permute-start(bf16[64,1024]{1,0:T(8,128)(2,1)S(1)} %bitcast.4), channel_id=1, source_target_pairs={{1,2},{3,4},{5,6},{2,1},{4,3},{6,5},{9,10},{11,12},{13,14},{10,9},... | collective-permute-start | bytes 393224 | tf_op jit(solution)/shard_map/ppermute | solution.py:336
  8.2 10.5 %collective-permute-start.6 = (bf16[64,1024]{1,0:T(8,128)(2,1)S(1)}, bf16[64,1024]{1,0:T(8,128)(2,1)S(1)}, u32[]{:S(2)}, u32[]{:S(2)}) collective-permute-start(bf16[64,1024]{1,0:T(8,128)(2,1)S(1)} %bitcast.5), channel_id=1, source_target_pairs={{0,2},{1,3},{4,6},{5,7},{2,0},{3,1},{6,4},{7,5},{8,10},{9,11},{12,... | collective-permute-start | bytes 393224 | tf_op jit(solution)/shard_map/ppermute | solution.py:336
  11.5 8.0 %collective-permute-start.7 = (bf16[64,1024]{1,0:T(8,128)(2,1)S(1)}, bf16[64,1024]{1,0:T(8,128)(2,1)S(1)}, u32[]{:S(2)}, u32[]{:S(2)}) collective-permute-start(bf16[64,1024]{1,0:T(8,128)(2,1)S(1)} %bitcast.6), channel_id=1, source_target_pairs={{2,4},{3,5},{4,2},{5,3},{10,12},{11,13},{12,10},{13,11},{18,20},{1... | collective-permute-start | bytes 393224 | tf_op jit(solution)/shard_map/ppermute | solution.py:336
  13.0 9.9 %collective-permute-start = (bf16[80,1152]{1,0:T(8,128)(2,1)S(1)}, bf16[80,1152]{1,0:T(8,128)(2,1)S(1)}, u32[]{:S(2)}, u32[]{:S(2)}) collective-permute-start(bf16[80,1152]{1,0:T(8,128)(2,1)S(1)} %get-tuple-element.19), channel_id=1, source_target_pairs={{0,1},{2,3},{4,5},{6,7},{1,0},{3,2},{5,4},{7,6},{8,9},{10,11},{12,... | collective-permute-start | bytes 552968 | tf_op jit(solution)/shard_map/ppermute | solution.py:336
  13.3 9.6 %collective-permute-start.1 = (bf16[80,1152]{1,0:T(8,128)(2,1)S(1)}, bf16[80,1152]{1,0:T(8,128)(2,1)S(1)}, u32[]{:S(2)}, u32[]{:S(2)}) collective-permute-start(bf16[80,1152]{1,0:T(8,128)(2,1)S(1)} %get-tuple-element.20), channel_id=1, source_target_pairs={{1,2},{3,4},{5,6},{2,1},{4,3},{6,5},{9,10},{11,12},{13,14},{10,9},... | collective-permute-start | bytes 552968 | tf_op jit(solution)/shard_map/ppermute | solution.py:336
  14.0 8.9 %collective-permute-start.2 = (bf16[16,1152]{1,0:T(8,128)(2,1)S(1)}, bf16[16,1152]{1,0:T(8,128)(2,1)S(1)}, u32[]{:S(2)}, u32[]{:S(2)}) collective-permute-start(bf16[16,1152]{1,0:T(8,128)(2,1)S(1)} %get-tuple-element.21), channel_id=1, source_target_pairs={{0,2},{1,3},{4,6},{5,7},{2,0},{3,1},{6,4},{7,5},{8,10},{9,11},{12,... | collective-permute-start | bytes 110600 | tf_op jit(solution)/shard_map/ppermute | solution.py:336
  18.7 4.2 %copy-start.3 = (bf16[192,192]{1,0:T(8,128)(2,1)S(1)}, bf16[192,192]{1,0:T(8,128)(2,1)}, u32[]{:S(2)}) copy-start(bf16[192,192]{1,0:T(8,128)(2,1)} %constant.8.clone.left_tab) | copy-start | bytes 221188
  18.7 4.2 %collective-permute-start.3 = (bf16[16,1152]{1,0:T(8,128)(2,1)S(1)}, bf16[16,1152]{1,0:T(8,128)(2,1)S(1)}, u32[]{:S(2)}, u32[]{:S(2)}) collective-permute-start(bf16[16,1152]{1,0:T(8,128)(2,1)S(1)} %get-tuple-element.22), channel_id=1, source_target_pairs={{2,4},{3,5},{4,2},{5,3},{10,12},{11,13},{12,10},{13,11},{18,20},{1... | collective-permute-start | bytes 110600 | tf_op jit(solution)/shard_map/ppermute | solution.py:336

commit v19 on v15

--- a/solution.py
+++ b/solution.py
@@ -330,21 +330,31 @@
             out[layer, part] = field[part, side : side + BAND]
 
 
-def exchanged(value, axis, by, phase):
-    count = lax.axis_size(axis)
-    lower = [i for i in range(count - by) if (i // by) % 2 == phase]
-    pairs = [(i, i + by) for i in lower] + [(i + by, i) for i in lower]
-    paired = {source for source, _ in pairs}
-    pairs += [(i, i) for i in range(count) if i not in paired]
-    return lax.ppermute(value, axis, pairs)
+def exchanged(value, by, phase):
+    count, depths = lax.axis_size("rows"), lax.axis_size("depth")
+    partner = {}
+    for low in range(count - by):
+        if (low // by) % 2 == phase:
+            partner[low], partner[low + by] = low + by, low
+    pairs = []
+    for depth in range(depths):
+        for band in range(count):
+            if band in partner:
+                to = (depth, partner[band])
+            elif by > 1:
+                to = (depth, band ^ 1)
+            else:
+                to = (depth ^ 1, band)
+            pairs.append((depth * count + band, to[0] * count + to[1]))
+    return lax.ppermute(value, ("depth", "rows"), pairs)
 
 
 def neighbours(sent):
     in_chip, cross, far_even, far_odd = sent
-    cross = exchanged(cross, "rows", 1, 1)
-    far_even = exchanged(far_even, "rows", 2, 0)
-    far_odd = exchanged(far_odd, "rows", 2, 1)
-    in_chip = exchanged(in_chip, "rows", 1, 0)
+    cross = exchanged(cross, 1, 1)
+    far_even = exchanged(far_even, 2, 0)
+    far_odd = exchanged(far_odd, 2, 1)
+    in_chip = exchanged(in_chip, 1, 0)
     return in_chip, cross, far_even, far_odd
 
 

time: 38.6 us -> 34.4 us (0.89)
  starting transfers between devices: 16.3 us -> 11.6 us
  waiting for transfers between devices: 3.29 us -> 4.97 us
  blocking collectives: 12 us -> 10.7 us
    ppermute x8, starting transfers between devices: 11 us -> 6.25 us  [exchanged(): return lax.ppermute(value, ('depth', 'rows'), pairs)]
    all_to_all x1, waiting for transfers between devices: 1.03 us -> 2.74 us  [body(): own = lax.all_to_all(payload, 'depth', 0, 0, tiled=True)]
    all_to_all x1, blocking collectives: 12 us -> 10.7 us  [body(): gathered = lax.all_to_all(result, 'depth', 0, 0, tiled=True)]
where the time goes in v19:
time: 34.4 us; the launch traced here: 33.8 us
  starting transfers between devices  11.6 us (34%)
  blocking collectives  10.7 us (31%)
  Pallas kernels  5.62 us (16%)
  waiting for transfers between devices  4.97 us (14%)
  local copies, waits for them, and re-layouts  0.79 us (2%)
    all_to_all x1, blocking collectives, body(): gathered = lax.all_to_all(result, 'depth', 0, 0, tiled=True)  10.7 us
    ppermute x8, starting transfers between devices, exchanged(): return lax.ppermute(value, ('depth', 'rows'), pairs)  6.25 us
    all_to_all x1, starting transfers between devices, body(): own = lax.all_to_all(payload, 'depth', 0, 0, tiled=True)  5.31 us
    all_to_all x1, waiting for transfers between devices, body(): own = lax.all_to_all(payload, 'depth', 0, 0, tiled=True)  2.74 us
    pallas_call x1, Pallas kernels, body(): call(chain_kernel, shaped((LAYERS, 2, BAND, COLS), bf16), [vmem] * (6 + l...  2.47 us
    ppermute x8, waiting for transfers between devices, exchanged(): return lax.ppermute(value, ('depth', 'rows'), pairs)  2.23 us
    pallas_call x1, Pallas kernels, body(): call(pack_kernel, (shaped((LAYERS, BAND, FULL_W), bf16), shaped(incident....  1.98 us
    pallas_call x1, Pallas kernels, body(): call(prepare_kernel, [shaped((TILES * layer_height(0), 2 * LANES), f32),...  1.14 us
  transfers between devices with their start and end apart: 9, of which 2 were waited for; matrix products, arithmetic and copies ran while one was open for 0% of the time, Pallas kernels for 3%

profile of v19, /device:TPU:0, one launch (start us, length us, event | category | flops | bytes accessed | tf_op | source)
XLA Modules:
  0.0 33.8 jit_solution(879796086992492729)
XLA Ops:
  0.0 2.0 %shard_map.100 = (bf16[4,32,1280]{2,1,0:T(8,128)(2,1)}, bf16[2,32,1024]{2,1,0:T(8,128)(2,1)}) custom-call(f32[1,3,32,1024]{3,2,1,0:T(8,128)} %light.1, s32[1,32,64]{2,1,0:T(8,128)} %edges.1, s32[1,2]{1,0:T(1,128)} %counts.1, s32[1,2,64]{2,1,0:T(2,128)} %listed.1, bf16[1,3,2,33]{3,2,1,0:T(2,128)(2,1)} %row_taps.1, bf16[1,3,2,127]{3,2,1,0:T(2,128)(2,1)} %col_taps.1, ...), custom_call_target="tpu_custom_call" | custom-call | flops 10000000 | bytes 1000000 | tf_op jit(solution)/shard_map/pallas_call | solution.py:388
  2.0 0.0 copy-start
  2.0 5.3 %all-to-all-start = ((bf16[4,32,1280]{2,1,0:T(8,128)(2,1)}), bf16[4,32,1280]{2,1,0:T(8,128)(2,1)S(1)}, u32[]{:S(2)}, u32[]{:S(2)}) async-start(bf16[4,32,1280]{2,1,0:T(8,128)(2,1)} %get-tuple-element.18), calls=%async_computation | async-start | bytes 655360 | tf_op jit(solution)/shard_map/all_to_all | solution.py:397
  7.3 0.0 copy-done
  7.3 0.0 copy-start.1
  7.3 0.0 copy-start.2
  7.3 0.1 collective-permute-start.4
  7.4 2.1 %collective-permute-start.5 = (bf16[64,1024]{1,0:T(8,128)(2,1)S(1)}, bf16[64,1024]{1,0:T(8,128)(2,1)S(1)}, u32[]{:S(2)}, u32[]{:S(2)}) collective-permute-start(bf16[64,1024]{1,0:T(8,128)(2,1)S(1)} %bitcast.4), channel_id=1, source_target_pairs={{0,8},{1,2},{2,1},{3,4},{4,3},{5,6},{6,5},{7,15},{8,0},{9,10},{10,... | collective-permute-start | bytes 393224 | tf_op jit(solution)/shard_map/ppermute | solution.py:349
  9.5 0.1 collective-permute-start.6
  9.5 0.9 %collective-permute-start.7 = (bf16[64,1024]{1,0:T(8,128)(2,1)S(1)}, bf16[64,1024]{1,0:T(8,128)(2,1)S(1)}, u32[]{:S(2)}, u32[]{:S(2)}) collective-permute-start(bf16[64,1024]{1,0:T(8,128)(2,1)S(1)} %bitcast.6), channel_id=1, source_target_pairs={{0,1},{1,0},{2,4},{3,5},{4,2},{5,3},{6,7},{7,6},{8,9},{9,8},{10,12... | collective-permute-start | bytes 393224 | tf_op jit(solution)/shard_map/ppermute | solution.py:349
  10.5 2.7 %all-to-all-done.own = bf16[4,32,1280]{2,1,0:T(8,128)(2,1)S(1)} async-done(((bf16[4,32,1280]{2,1,0:T(8,128)(2,1)}), bf16[4,32,1280]{2,1,0:T(8,128)(2,1)S(1)}, u32[]{:S(2)}, u32[]{:S(2)}) %all-to-all-start) | async-done | bytes 327712 | tf_op jit(solution)/shard_map/all_to_all | solution.py:397
  13.2 0.1 collective-permute-start
  13.3 0.0 collective-permute-done.4.in_chip
  13.3 1.5 %collective-permute-start.1 = (bf16[80,1152]{1,0:T(8,128)(2,1)S(1)}, bf16[80,1152]{1,0:T(8,128)(2,1)S(1)}, u32[]{:S(2)}, u32[]{:S(2)}) collective-permute-start(bf16[80,1152]{1,0:T(8,128)(2,1)S(1)} %get-tuple-element.20), channel_id=1, source_target_pairs={{0,8},{1,2},{2,1},{3,4},{4,3},{5,6},{6,5},{7,15},{8,0},{9,10},{10,... | collective-permute-start | bytes 552968 | tf_op jit(solution)/shard_map/ppermute | solution.py:349
  14.8 0.0 collective-permute-done.5.cross
  14.8 0.6 %collective-permute-start.2 = (bf16[16,1152]{1,0:T(8,128)(2,1)S(1)}, bf16[16,1152]{1,0:T(8,128)(2,1)S(1)}, u32[]{:S(2)}, u32[]{:S(2)}) collective-permute-start(bf16[16,1152]{1,0:T(8,128)(2,1)S(1)} %get-tuple-element.21), channel_id=1, source_target_pairs={{0,2},{1,3},{2,0},{3,1},{4,6},{5,7},{6,4},{7,5},{8,10},{9,11},{10,... | collective-permute-start | bytes 110600 | tf_op jit(solution)/shard_map/ppermute | solution.py:349
  15.4 0.0 collective-permute-done.6.far_even
  15.4 0.0 copy-start.3
  15.5 0.9 %collective-permute-start.3 = (bf16[16,1152]{1,0:T(8,128)(2,1)S(1)}, bf16[16,1152]{1,0:T(8,128)(2,1)S(1)}, u32[]{:S(2)}, u32[]{:S(2)}) collective-permute-start(bf16[16,1152]{1,0:T(8,128)(2,1)S(1)} %get-tuple-element.22), channel_id=1, source_target_pairs={{0,1},{1,0},{2,4},{3,5},{4,2},{5,3},{6,7},{7,6},{8,9},{9,8},{10,12... | collective-permute-start | bytes 110600 | tf_op jit(solution)/shard_map/ppermute | solution.py:349
  16.4 0.0 collective-permute-done.7.far_odd
  16.4 0.0 copy-done.1
  16.4 0.0 copy-done.2
  16.4 1.1 %shard_map.102 = (f32[1024,256]{1,0:T(8,128)S(1)}, f32[2,128,1024]{2,1,0:T(8,128)S(1)}, f32[128,1024]{1,0:T(8,128)S(1)}, bf16[3,256,512]{2,1,0:T(8,128)(2,1)S(1)...) custom-call(bf16[4,32,1280]{2,1,0:T(8,128)(2,1)S(1)} %all-to-all-done.own, ...), custom_call_target="tpu_custom_call" | custom-call | flops 1000000000 | bytes 3000000 | tf_op jit(solution)/shard_map/pallas_call | solution.py:403
  17.5 2.2 %collective-permute-done.2.far_even = bf16[16,1152]{1,0:T(8,128)(2,1)S(1)} collective-permute-done((bf16[16,1152]{1,0:T(8,128)(2,1)S(1)}, bf16[16,1152]{1,0:T(8,128)(2,1)S(1)}, u32[]{:S(2)}, u32[]{:S(2)}) %collective-permute-start.2) | collective-permute-done | bytes 36896 | tf_op jit(solution)/shard_map/ppermute | solution.py:349
  19.7 0.0 collective-permute-done.3.far_odd
  19.7 0.0 collective-permute-done.in_chip
  19.8 0.0 collective-permute-done.1.cross
  19.8 0.0 copy-done.3
  19.8 2.5 %shard_map.103 = bf16[4,2,32,1024]{3,2,1,0:T(8,128)(2,1)S(1)} custom-call(bf16[80,1152]{1,0:T(8,128)(2,1)S(1)} %collective-permute-done.in_chip, bf16[80,1152]{1,0:T(8,128)(2,1)S(1)} %collective-permute-done.1.cross, bf16[16,1152]{1,0:T(8,128)(2,1)S(1)} %collective-permute-done.2.far_even, bf16[16,1152]{1,0:T(8,128)(2,1)S(1)} %collective-permute-done.3.far_odd, ...), custom_call_target="tpu_custom_call" | custom-call | flops 2000000000 | bytes 3000000 | tf_op jit(solution)/shard_map/pallas_call | solution.py:417
  22.2 10.7 %all_to_all.10 = bf16[4,2,32,1024]{3,2,1,0:T(8,128)(2,1)S(1)} all-to-all(bf16[4,2,32,1024]{3,2,1,0:T(8,128)(2,1)S(1)} %shard_map.103), channel_id=1, replica_groups=mesh['depth'=4,'rows'=8] {'depth'}, dimensions={0} | all-to-all | bytes 1048576 | tf_op jit(solution)/shard_map/all_to_all | solution.py:425
  33.0 0.8 %slice_bitcast_fusion = bf16[1,3,2,32,1024]{4,3,2,1,0:T(8,128)(2,1)} fusion(bf16[4,2,32,1024]{3,2,1,0:T(8,128)(2,1)S(1)} %all_to_all.10), kind=kLoop, calls=%fused_computation | loop fusion | bytes 786432 | tf_op jit(solution)/shard_map/broadcast_in_dim | solution.py:426
  (1 shorter events, 0.0 us)
Async XLA Ops:
  2.0 5.3 %copy-start = (bf16[2,32,1024]{2,1,0:T(8,128)(2,1)S(1)}, bf16[2,32,1024]{2,1,0:T(8,128)(2,1)}, u32[]{:S(2)}) copy-start(bf16[2,32,1024]{2,1,0:T(8,128)(2,1)} %get-tuple-element.23) | copy-start | bytes 393220
  2.0 11.2 %all-to-all-start = ((bf16[4,32,1280]{2,1,0:T(8,128)(2,1)}), bf16[4,32,1280]{2,1,0:T(8,128)(2,1)S(1)}, u32[]{:S(2)}, u32[]{:S(2)}) async-start(bf16[4,32,1280]{2,1,0:T(8,128)(2,1)} %get-tuple-element.18), calls=%async_computation | async-start | bytes 655360 | tf_op jit(solution)/shard_map/all_to_all | solution.py:397
  7.3 9.1 %copy-start.1 = (bf16[256,256]{1,0:T(8,128)(2,1)S(1)}, bf16[256,256]{1,0:T(8,128)(2,1)}, u32[]{:S(2)}) copy-start(bf16[256,256]{1,0:T(8,128)(2,1)} %constant.6.clone.right_tab) | copy-start | bytes 393220
  7.3 9.1 %copy-start.2 = (bf16[256,256]{1,0:T(8,128)(2,1)S(1)}, bf16[256,256]{1,0:T(8,128)(2,1)}, u32[]{:S(2)}) copy-start(bf16[256,256]{1,0:T(8,128)(2,1)} %constant.7.clone.left_tab) | copy-start | bytes 393220
  7.3 6.0 %collective-permute-start.4 = (bf16[64,1024]{1,0:T(8,128)(2,1)S(1)}, bf16[64,1024]{1,0:T(8,128)(2,1)S(1)}, u32[]{:S(2)}, u32[]{:S(2)}) collective-permute-start(bf16[64,1024]{1,0:T(8,128)(2,1)S(1)} %bitcast.3), channel_id=1, source_target_pairs={{0,1},{1,0},{2,3},{3,2},{4,5},{5,4},{6,7},{7,6},{8,9},{9,8},{10,11... | collective-permute-start | bytes 393224 | tf_op jit(solution)/shard_map/ppermute | solution.py:349
  7.4 7.4 %collective-permute-start.5 = (bf16[64,1024]{1,0:T(8,128)(2,1)S(1)}, bf16[64,1024]{1,0:T(8,128)(2,1)S(1)}, u32[]{:S(2)}, u32[]{:S(2)}) collective-permute-start(bf16[64,1024]{1,0:T(8,128)(2,1)S(1)} %bitcast.4), channel_id=1, source_target_pairs={{0,8},{1,2},{2,1},{3,4},{4,3},{5,6},{6,5},{7,15},{8,0},{9,10},{10,... | collective-permute-start | bytes 393224 | tf_op jit(solution)/shard_map/ppermute | solution.py:349
  9.5 6.0 %collective-permute-start.6 = (bf16[64,1024]{1,0:T(8,128)(2,1)S(1)}, bf16[64,1024]{1,0:T(8,128)(2,1)S(1)}, u32[]{:S(2)}, u32[]{:S(2)}) collective-permute-start(bf16[64,1024]{1,0:T(8,128)(2,1)S(1)} %bitcast.5), channel_id=1, source_target_pairs={{0,2},{1,3},{2,0},{3,1},{4,6},{5,7},{6,4},{7,5},{8,10},{9,11},{10,... | collective-permute-start | bytes 393224 | tf_op jit(solution)/shard_map/ppermute | solution.py:349
  9.5 6.9 %collective-permute-start.7 = (bf16[64,1024]{1,0:T(8,128)(2,1)S(1)}, bf16[64,1024]{1,0:T(8,128)(2,1)S(1)}, u32[]{:S(2)}, u32[]{:S(2)}) collective-permute-start(bf16[64,1024]{1,0:T(8,128)(2,1)S(1)} %bitcast.6), channel_id=1, source_target_pairs={{0,1},{1,0},{2,4},{3,5},{4,2},{5,3},{6,7},{7,6},{8,9},{9,8},{10,12... | collective-permute-start | bytes 393224 | tf_op jit(solution)/shard_map/ppermute | solution.py:349
  13.2 6.5 %collective-permute-start = (bf16[80,1152]{1,0:T(8,128)(2,1)S(1)}, bf16[80,1152]{1,0:T(8,128)(2,1)S(1)}, u32[]{:S(2)}, u32[]{:S(2)}) collective-permute-start(bf16[80,1152]{1,0:T(8,128)(2,1)S(1)} %get-tuple-element.19), channel_id=1, source_target_pairs={{0,1},{1,0},{2,3},{3,2},{4,5},{5,4},{6,7},{7,6},{8,9},{9,8},{10,11... | collective-permute-start | bytes 552968 | tf_op jit(solution)/shard_map/ppermute | solution.py:349
  13.3 6.4 %collective-permute-start.1 = (bf16[80,1152]{1,0:T(8,128)(2,1)S(1)}, bf16[80,1152]{1,0:T(8,128)(2,1)S(1)}, u32[]{:S(2)}, u32[]{:S(2)}) collective-permute-start(bf16[80,1152]{1,0:T(8,128)(2,1)S(1)} %get-tuple-element.20), channel_id=1, source_target_pairs={{0,8},{1,2},{2,1},{3,4},{4,3},{5,6},{6,5},{7,15},{8,0},{9,10},{10,... | collective-permute-start | bytes 552968 | tf_op jit(solution)/shard_map/ppermute | solution.py:349
  14.8 4.9 %collective-permute-start.2 = (bf16[16,1152]{1,0:T(8,128)(2,1)S(1)}, bf16[16,1152]{1,0:T(8,128)(2,1)S(1)}, u32[]{:S(2)}, u32[]{:S(2)}) collective-permute-start(bf16[16,1152]{1,0:T(8,128)(2,1)S(1)} %get-tuple-element.21), channel_id=1, source_target_pairs={{0,2},{1,3},{2,0},{3,1},{4,6},{5,7},{6,4},{7,5},{8,10},{9,11},{10,... | collective-permute-start | bytes 110600 | tf_op jit(solution)/shard_map/ppermute | solution.py:349
  15.4 4.3 %copy-start.3 = (bf16[192,192]{1,0:T(8,128)(2,1)S(1)}, bf16[192,192]{1,0:T(8,128)(2,1)}, u32[]{:S(2)}) copy-start(bf16[192,192]{1,0:T(8,128)(2,1)} %constant.8.clone.left_tab) | copy-start | bytes 221188
  15.5 4.3 %collective-permute-start.3 = (bf16[16,1152]{1,0:T(8,128)(2,1)S(1)}, bf16[16,1152]{1,0:T(8,128)(2,1)S(1)}, u32[]{:S(2)}, u32[]{:S(2)}) collective-permute-start(bf16[16,1152]{1,0:T(8,128)(2,1)S(1)} %get-tuple-element.22), channel_id=1, source_target_pairs={{0,1},{1,0},{2,4},{3,5},{4,2},{5,3},{6,7},{7,6},{8,9},{9,8},{10,12... | collective-permute-start | bytes 110600 | tf_op jit(solution)/shard_map/ppermute | solution.py:349

commit v20 on v19

--- a/solution.py
+++ b/solution.py
@@ -20,7 +20,6 @@
 TILES = COLS // LANES
 HALO_W = COLS + LANES
 HALF = LANES // 2
-FULL_W = COLS + 2 * LANES
 NEAR = 2 * BAND + KR
 FAR = KR
 VMEM_LIMIT = 48 * 1024 * 1024
@@ -79,8 +78,9 @@
     return jnp.minimum(lax.axis_index("depth"), COLORS - 1)
 
 
-def pack_kernel(light, edges, counts, listed, row_taps, col_taps, incident, out, mine, *scratch):
-    held, sems, taps = scratch[:6], scratch[6], scratch[7]
+def pack_kernel(light, edges, counts, listed, row_taps, col_taps, incident, *rest):
+    outs, mine, held, sems, taps = rest[:LAYERS], rest[LAYERS], rest[5:11], rest[11], rest[12]
+    depth = lax.axis_index("depth")
     picked = pltpu.make_async_copy(incident.at[own_colour()], mine, sems.at[6])
     sources = (listed, counts, edges, row_taps, col_taps, light)
     copies = [
@@ -107,22 +107,29 @@
     live_pix = jnp.dot(live_rows, spread, preferred_element_type=jnp.float32)
     edge_tile = jnp.concatenate(
         [edges[0].astype(jnp.float32), jnp.zeros((BAND, LANES - NH), jnp.float32)], axis=1
-    ).astype(jnp.bfloat16)
-    for colour in range(COLORS):
-        out[colour, :, COLS:HALO_W] = edge_tile
+    )
+    left_half = lax.broadcasted_iota(jnp.int32, (BAND, LANES), 1) < HALF
+    colours = [jnp.minimum(depth ^ hop, COLORS - 1) for hop in range(LAYERS)]
+    for colour, out in zip(colours, outs):
         taps[...] = jnp.zeros_like(taps)
-        taps[0:2, : 2 * KC + 1] = col_taps[0, colour].astype(jnp.float32)
-        taps[2:4, : 2 * KR + 1] = row_taps[0, colour].astype(jnp.float32)
-        out[colour, :, HALO_W:] = taps[...].astype(jnp.bfloat16)
-    for spare in range(COLORS, LAYERS):
-        out[spare] = jnp.zeros((BAND, FULL_W), jnp.bfloat16)
+        taps[2:4, : 2 * KC + 1] = col_taps[0, colour].astype(jnp.float32)
+        taps[4:6, : 2 * KR + 1] = row_taps[0, colour].astype(jnp.float32)
+        turned = pltpu.roll(taps[0:8], HALF, 1)
+        taps[0:2] = turned[2:4]
+        taps[4:6] = turned[4:6]
+        tile = jnp.where(left_half, edge_tile, taps[...])
+        out[:, COLS:] = tile.astype(jnp.bfloat16)
     copies[5].wait()
-    for colour in range(COLORS):
-        out[colour, :, :COLS] = (light[0, colour] * live_pix).astype(jnp.bfloat16)
+    for colour, out in zip(colours, outs):
+        out[:, :COLS] = (light[0, colour] * live_pix).astype(jnp.bfloat16)
     picked.wait()
 
 
-def halo_kernel(own, in_chip, cross, far_even, far_odd):
+def halo_kernel(*refs):
+    arrived, (own, in_chip, cross, far_even, far_odd) = refs[:LAYERS], refs[LAYERS:]
+    depth = lax.axis_index("depth")
+    for hop in range(LAYERS):
+        own[depth ^ hop] = arrived[hop][...]
     band = lax.axis_index("rows")
     core = band % 2
     odd = (band // 2) % 2
@@ -195,15 +202,19 @@
     return pltpu.roll(base, shift, 1, stride=1, stride_axis=0)
 
 
-def filters(taps, layer):
-    row_re, row_im = taps[2:3], taps[3:4]
+def filters(tile, layer):
+    turned = pltpu.roll(tile[0:8], HALF, 1)
+    left_half = lax.broadcasted_iota(jnp.int32, (2, LANES), 1) < HALF
+    col_taps = jnp.where(left_half, turned[0:2], tile[2:4])
+    row_taps = jnp.where(left_half, turned[4:6], 0.0)
+    row_re, row_im = row_taps[0:1], row_taps[1:2]
     height = block_height(layer)
     before = height + 2 * KR
     upper = banded(row_re, height, 0) - banded(row_im, height, before)
     lower = banded(row_im, height, 0) + banded(row_re, height, before)
     row_mat = jnp.concatenate([upper, lower], axis=0).astype(jnp.bfloat16)
-    col_re = banded(taps[0:1], LANES, 1)
-    col_im = banded(taps[1:2], LANES, 1)
+    col_re = banded(col_taps[0:1], LANES, 1)
+    col_im = banded(col_taps[1:2], LANES, 1)
     upper = jnp.concatenate([col_re, -col_im], axis=1)
     lower = jnp.concatenate([col_im, col_re], axis=1)
     col_mat = jnp.concatenate([upper, lower], axis=0).astype(jnp.bfloat16)
@@ -255,10 +266,10 @@
         pieces = [low_far, low_near, incident[...], high_near, high_far]
         pieces = [piece[part * BAND : (part + 1) * BAND] for piece in pieces]
         extended.append(jnp.concatenate(pieces, axis=0))
-    row_mat, col_mat = filters(own[0, 0:16, HALO_W:].astype(jnp.float32), 0)
+    row_mat, col_mat = filters(own[0, 0:16, COLS:].astype(jnp.float32), 0)
     first[...] = propagated(extended[0], extended[1], row_mat, col_mat, 0)
     for layer in range(1, LAYERS):
-        row_mat, col_mat = filters(own[layer, 0:16, HALO_W:].astype(jnp.float32), layer)
+        row_mat, col_mat = filters(own[layer, 0:16, COLS:].astype(jnp.float32), layer)
         row_mats[layer - 1][...] = row_mat
         col_mats[layer - 1] = col_mat
     packed = jnp.concatenate([own[layer, :, :HALO_W] for layer in range(LAYERS)], axis=0)
@@ -275,7 +286,8 @@
 def chain_kernel(
     in_chip, cross, far_even, far_odd, left_tab, right_tab, first, stereo, clear, col_mats, *rest
 ):
-    row_mats, (out, field) = rest[: LAYERS - 1], rest[LAYERS - 1 :]
+    row_mats, outs, field = rest[: LAYERS - 1], rest[LAYERS - 1 : -1], rest[-1]
+    depth = lax.axis_index("depth")
     low_near, high_near, low_far, high_far = ordered(in_chip, cross, far_even, far_odd)
     pieces = [
         low_far,
@@ -326,8 +338,30 @@
                 added = jnp.concatenate(pieces, axis=0)
                 value = passing[:, lanes] * columned[span, within] + added
                 field[part, :height, lanes] = value.astype(jnp.bfloat16)
-        for part in range(2):
-            out[layer, part] = field[part, side : side + BAND]
+        for hop, out in enumerate(outs):
+
+            @pl.when((depth ^ hop) == layer)
+            def keep(out=out, side=side):
+                for part in range(2):
+                    out[part] = field[part, side : side + BAND]
+
+
+def home_kernel(*refs):
+    arrived, out, sems = refs[:LAYERS], refs[LAYERS], refs[LAYERS + 1]
+    depth = lax.axis_index("depth")
+    for colour in range(COLORS):
+        for hop in range(LAYERS):
+
+            @pl.when((depth ^ hop) == colour)
+            def begin(hop=hop, colour=colour):
+                pltpu.make_async_copy(arrived[hop], out.at[0, colour], sems.at[colour]).start()
+
+    for colour in range(COLORS):
+        pltpu.make_async_copy(arrived[0], out.at[0, colour], sems.at[colour]).wait()
+
+
+def over_depth(value, hop):
+    return lax.ppermute(value, "depth", [(i, i ^ hop) for i in range(LAYERS)])
 
 
 def exchanged(value, by, phase):
@@ -358,8 +392,11 @@
     return in_chip, cross, far_even, far_odd
 
 
-def call(kernel, out_shape, in_specs, scratch=(), flops=0, moved=10**6, limit=VMEM_LIMIT):
-    vmem = pl.BlockSpec(memory_space=pltpu.VMEM)
+def call(
+    kernel, out_shape, in_specs, scratch=(), flops=0, moved=10**6, limit=VMEM_LIMIT,
+    out_space=pltpu.VMEM,
+):
+    vmem = pl.BlockSpec(memory_space=out_space)
     many = isinstance(out_shape, (tuple, list))
     return pl.pallas_call(
         kernel,
@@ -385,20 +422,25 @@
         pltpu.VMEM(col_taps.shape, bf16),
         pltpu.VMEM(hogel_light.shape, f32),
     ]
-    payload, mine = call(
+    *messages, mine = call(
         pack_kernel,
-        (shaped((LAYERS, BAND, FULL_W), bf16), shaped(incident.shape[1:], bf16)),
+        (shaped((BAND, HALO_W), bf16),) * LAYERS + (shaped(incident.shape[1:], bf16),),
         [hbm] * 7,
         held + [pltpu.SemaphoreType.DMA((7,)), pltpu.VMEM((BAND, LANES), f32)],
         flops=10**7,
         limit=PACK_LIMIT,
     )(hogel_light, silhouette, fill_counts, hogel_index, row_taps, col_taps, incident)
     mine = mine.reshape(2 * BAND, COLS)
-    own = lax.all_to_all(payload, "depth", 0, 0, tiled=True)
+    layers_in = messages[:1] + [over_depth(messages[hop], hop) for hop in range(1, LAYERS)]
     arrived = neighbours((mine,) * 4)
     near = shaped((NEAR, HALO_W), bf16)
     far = shaped((FAR, HALO_W), bf16)
-    halos = neighbours(call(halo_kernel, (near, near, far, far), [vmem])(own))
+    own, *sent = call(
+        halo_kernel,
+        (shaped((LAYERS, BAND, HALO_W), bf16), near, near, far, far),
+        [vmem] * LAYERS,
+    )(*layers_in)
+    halos = neighbours(sent)
     right_tab = jnp.asarray(right_table())
     made = call(
         prepare_kernel,
@@ -414,16 +456,22 @@
         moved=3 * 10**6,
     )(own, mine, *arrived, jnp.asarray(left_table(LANES)), right_tab)
     halo_rows = NEAR + FAR
-    result = call(
+    results = call(
         chain_kernel,
-        shaped((LAYERS, 2, BAND, COLS), bf16),
+        [shaped((2, BAND, COLS), bf16)] * LAYERS,
         [vmem] * (6 + len(made)),
         [pltpu.VMEM((2, layer_height(0), COLS), bf16)],
         flops=2 * 10**9,
         moved=3 * 10**6,
     )(*halos, jnp.asarray(left_table(halo_rows)), right_tab, *made)
-    gathered = lax.all_to_all(result, "depth", 0, 0, tiled=True)
-    return gathered[None, :COLORS]
+    returned = [results[0]] + [over_depth(results[hop], hop) for hop in range(1, LAYERS)]
+    return call(
+        home_kernel,
+        shaped((1, COLORS, 2, BAND, COLS), bf16),
+        [vmem] * LAYERS,
+        [pltpu.SemaphoreType.DMA((COLORS,))],
+        out_space=pltpu.HBM,
+    )(*returned)
 
 
 def solution(mesh):

time: 34.4 us -> 32.8 us (0.953); the launches traced: 33.8 us -> 32.6 us
  blocking collectives: 10.7 us -> 0 us
  starting transfers between devices: 11.6 us -> 16.7 us
  waiting for transfers between devices: 4.97 us -> 8.04 us
  Pallas kernels: 5.62 us -> 6.91 us
    all_to_all x1 -> x0, blocking collectives: 10.7 us -> none  [body(): gathered = lax.all_to_all(result, 'depth', 0, 0, tiled=True)]
    ppermute x0 -> x6, starting transfers between devices: none -> 7.67 us  [over_depth(): return lax.ppermute(value, 'depth', [(i, i ^ hop) for i in range(LAYERS)])]
    all_to_all x1 -> x0, starting transfers between devices: 5.31 us -> none  [body(): own = lax.all_to_all(payload, 'depth', 0, 0, tiled=True)]
    ppermute x0 -> x6, waiting for transfers between devices: none -> 5.23 us  [over_depth(): return lax.ppermute(value, 'depth', [(i, i ^ hop) for i in range(LAYERS)])]
    ppermute x8, starting transfers between devices: 6.25 us -> 9.04 us  [exchanged(): return lax.ppermute(value, ('depth', 'rows'), pairs)]
    all_to_all x1 -> x0, waiting for transfers between devices: 2.74 us -> none  [body(): own = lax.all_to_all(payload, 'depth', 0, 0, tiled=True)]
    pallas_call x3 -> x4, Pallas kernels: 4.49 us -> 5.72 us  [the longest x1 2.77 us: body(): call(chain_kernel, [shaped((2, BAND, COLS), bf16)] * LAYERS, [vmem] * (6...]
    unnamed x8 -> x10, local copies, waits for them, and re-layouts: 0.02 us -> 0.9 us
  transfers between devices with their start and end apart: 9 -> 14, of which waited for: 2 -> 4; matrix products, arithmetic and copies ran while one was open for 0% -> 0% of each run, Pallas kernels for 3% -> 4%
where the time goes in v20:
time: 32.8 us; the launch traced here: 32.6 us
  starting transfers between devices  16.7 us (51%)
  waiting for transfers between devices  8.04 us (25%)
  Pallas kernels  6.91 us (21%)
  local copies, waits for them, and re-layouts  0.9 us (3%)
    ppermute x8, starting transfers between devices, exchanged(): return lax.ppermute(value, ('depth', 'rows'), pairs)  9.04 us
    ppermute x6, starting transfers between devices, over_depth(): return lax.ppermute(value, 'depth', [(i, i ^ hop) for i in range(LAYERS)])  7.67 us
    ppermute x6, waiting for transfers between devices, over_depth(): return lax.ppermute(value, 'depth', [(i, i ^ hop) for i in range(LAYERS)])  5.23 us
    ppermute x8, waiting for transfers between devices, exchanged(): return lax.ppermute(value, ('depth', 'rows'), pairs)  2.81 us
    pallas_call x1, Pallas kernels, body(): call(chain_kernel, [shaped((2, BAND, COLS), bf16)] * LAYERS, [vmem] * (6...  2.77 us
    pallas_call x1, Pallas kernels, body(): call(pack_kernel, (shaped((BAND, HALO_W), bf16),) * LAYERS + (shaped(inci...  2.12 us
    pallas_call x1, Pallas kernels, body(): call(prepare_kernel, [shaped((TILES * layer_height(0), 2 * LANES), f32),...  1.19 us
    unnamed x10, local copies, waits for them, and re-layouts  0.9 us
  transfers between devices with their start and end apart: 14, of which 4 were waited for; matrix products, arithmetic and copies ran while one was open for 0% of the time, Pallas kernels for 4%

profile of v20, /device:TPU:0, one launch (start us, length us, event | category | flops | bytes accessed | tf_op | source)
XLA Modules:
  0.0 32.6 jit_solution(15264560076668606331)
XLA Ops:
  0.0 0.0 copy-start.3
  0.0 2.1 %shard_map.100 = (bf16[32,1152]{1,0:T(8,128)(2,1)}, bf16[32,1152]{1,0:T(8,128)(2,1)}, bf16[32,1152]{1,0:T(8,128)(2,1)}, bf16[32,1152]{1,0:T(8,128)(2,1)}, bf16[2,32,1024]{2,1,0:T(8,128)(2,1)}) custom-call(f32[1,3,32,1024]{3,2,1,0:T(8,128)} %light.1, s32[1,32,64]{2,1,0:T(8,128)} %edges.1, s32[1,2]{1,0:T(1,128)} %counts.1, s32[1,2,64]{2,1,0:T(2,128)} %listed.1, ...), custom_call_target="tpu_custom_call" | custom-call | flops 10000000 | bytes 1000000 | tf_op jit(solution)/shard_map/pallas_call | solution.py:425
  2.1 0.5 %collective-permute-start.10 = (bf16[64,1024]{1,0:T(8,128)(2,1)}, bf16[64,1024]{1,0:T(8,128)(2,1)S(1)}, u32[]{:S(2)}, u32[]{:S(2)}) collective-permute-start(bf16[64,1024]{1,0:T(8,128)(2,1)} %bitcast.1), channel_id=1, source_target_pairs={{0,1},{1,0},{2,4},{3,5},{4,2},{5,3},{6,7},{7,6},{8,9},{9,8},{10,12... | collective-permute-start | bytes 393224 | tf_op jit(solution)/shard_map/ppermute | solution.py:383
  2.6 2.6 %collective-permute-start = (bf16[32,1152]{1,0:T(8,128)(2,1)}, bf16[32,1152]{1,0:T(8,128)(2,1)S(1)}, u32[]{:S(2)}, u32[]{:S(2)}) collective-permute-start(bf16[32,1152]{1,0:T(8,128)(2,1)} %get-tuple-element.27), channel_id=1, source_target_pairs={{0,8},{8,0},{16,24},{24,16},{1,9},{9,1},{17,25},{25,17},{2,10},{10... | collective-permute-start | bytes 221192 | tf_op jit(solution)/shard_map/ppermute | solution.py:364
  5.2 1.5 %collective-permute-start.1 = (bf16[32,1152]{1,0:T(8,128)(2,1)}, bf16[32,1152]{1,0:T(8,128)(2,1)S(1)}, u32[]{:S(2)}, u32[]{:S(2)}) collective-permute-start(bf16[32,1152]{1,0:T(8,128)(2,1)} %get-tuple-element.28), channel_id=1, source_target_pairs={{0,16},{8,24},{16,0},{24,8},{1,17},{9,25},{17,1},{25,9},{2,18},{10... | collective-permute-start | bytes 221192 | tf_op jit(solution)/shard_map/ppermute | solution.py:364
  6.7 0.0 collective-permute-start.2
  6.8 3.5 %collective-permute-start.9 = (bf16[64,1024]{1,0:T(8,128)(2,1)}, bf16[64,1024]{1,0:T(8,128)(2,1)S(1)}, u32[]{:S(2)}, u32[]{:S(2)}) collective-permute-start(bf16[64,1024]{1,0:T(8,128)(2,1)} %bitcast.2), channel_id=1, source_target_pairs={{0,2},{1,3},{2,0},{3,1},{4,6},{5,7},{6,4},{7,5},{8,10},{9,11},{10,... | collective-permute-start | bytes 393224 | tf_op jit(solution)/shard_map/ppermute | solution.py:383
  10.3 0.0 collective-permute-done.refs_1_
  10.3 1.5 %collective-permute-start.8 = (bf16[64,1024]{1,0:T(8,128)(2,1)}, bf16[64,1024]{1,0:T(8,128)(2,1)S(1)}, u32[]{:S(2)}, u32[]{:S(2)}) collective-permute-start(bf16[64,1024]{1,0:T(8,128)(2,1)} %bitcast.3), channel_id=1, source_target_pairs={{0,8},{1,2},{2,1},{3,4},{4,3},{5,6},{6,5},{7,15},{8,0},{9,10},{10,... | collective-permute-start | bytes 393224 | tf_op jit(solution)/shard_map/ppermute | solution.py:383
  11.8 0.0 collective-permute-done.1.refs_2_
  11.8 0.0 collective-permute-start.7
  11.8 0.4 %collective-permute-done.2.refs_3_ = bf16[32,1152]{1,0:T(8,128)(2,1)S(1)} collective-permute-done((bf16[32,1152]{1,0:T(8,128)(2,1)}, bf16[32,1152]{1,0:T(8,128)(2,1)S(1)}, u32[]{:S(2)}, u32[]{:S(2)}) %collective-permute-start.2) | collective-permute-done | bytes 73760 | tf_op jit(solution)/shard_map/ppermute | solution.py:364
  12.2 0.0 copy-start
  12.2 0.9 %copy-done = bf16[32,1152]{1,0:T(8,128)(2,1)S(1)} copy-done((bf16[32,1152]{1,0:T(8,128)(2,1)S(1)}, bf16[32,1152]{1,0:T(8,128)(2,1)}, u32[]{:S(2)}) %copy-start) | copy-done | bytes 73752
  13.1 0.0 copy-start.1
  13.1 0.0 copy-start.2
  13.1 0.1 shard_map.101
  13.2 0.2 collective-permute-start.3
  13.3 0.0 collective-permute-done.10.far_odd
  13.3 1.5 %collective-permute-start.4 = (bf16[80,1152]{1,0:T(8,128)(2,1)S(1)}, bf16[80,1152]{1,0:T(8,128)(2,1)S(1)}, u32[]{:S(2)}, u32[]{:S(2)}) collective-permute-start(bf16[80,1152]{1,0:T(8,128)(2,1)S(1)} %get-tuple-element.31), channel_id=1, source_target_pairs={{0,8},{1,2},{2,1},{3,4},{4,3},{5,6},{6,5},{7,15},{8,0},{9,10},{10,... | collective-permute-start | bytes 552968 | tf_op jit(solution)/shard_map/ppermute | solution.py:383
  14.9 0.0 collective-permute-done.9.far_even
  14.9 1.6 %collective-permute-start.5 = (bf16[16,1152]{1,0:T(8,128)(2,1)S(1)}, bf16[16,1152]{1,0:T(8,128)(2,1)S(1)}, u32[]{:S(2)}, u32[]{:S(2)}) collective-permute-start(bf16[16,1152]{1,0:T(8,128)(2,1)S(1)} %get-tuple-element.32), channel_id=1, source_target_pairs={{0,2},{1,3},{2,0},{3,1},{4,6},{5,7},{6,4},{7,5},{8,10},{9,11},{10,... | collective-permute-start | bytes 110600 | tf_op jit(solution)/shard_map/ppermute | solution.py:383
  16.5 0.0 collective-permute-done.8.cross
  16.5 0.2 collective-permute-start.6
  16.7 0.0 collective-permute-done.7.in_chip
  16.7 0.0 copy-done.3
  16.7 0.0 copy-done.1
  16.7 0.0 copy-done.2
  16.7 0.0 copy-start.4
  16.7 1.2 %shard_map.102 = (f32[1024,256]{1,0:T(8,128)S(1)}, f32[2,128,1024]{2,1,0:T(8,128)S(1)}, f32[128,1024]{1,0:T(8,128)S(1)}, bf16[3,256,512]{2,1,0:T(8,128)(2,1)S(1)...) custom-call(bf16[4,32,1152]{2,1,0:T(8,128)(2,1)S(1)} %get-tuple-element.34.own, ...), custom_call_target="tpu_custom_call" | custom-call | flops 1000000000 | bytes 3000000 | tf_op jit(solution)/shard_map/pallas_call | solution.py:445
  17.9 2.8 %collective-permute-done.5.far_even = bf16[16,1152]{1,0:T(8,128)(2,1)S(1)} collective-permute-done((bf16[16,1152]{1,0:T(8,128)(2,1)S(1)}, bf16[16,1152]{1,0:T(8,128)(2,1)S(1)}, u32[]{:S(2)}, u32[]{:S(2)}) %collective-permute-start.5) | collective-permute-done | bytes 36896 | tf_op jit(solution)/shard_map/ppermute | solution.py:383
  20.7 0.0 collective-permute-done.6.far_odd
  20.7 0.0 collective-permute-done.3.in_chip
  20.7 0.0 collective-permute-done.4.cross
  20.7 0.0 copy-done.4
  20.7 2.8 %shard_map.103 = (bf16[2,32,1024]{2,1,0:T(8,128)(2,1)S(1)}, bf16[2,32,1024]{2,1,0:T(8,128)(2,1)S(1)}, bf16[2,32,1024]{2,1,0:T(8,128)(2,1)S(1)}, bf16[2,32,1024]{2,1,0:T(8,128)(2,1)S(1)}) custom-call(bf16[80,1152]{1,0:T(8,128)(2,1)S(1)} %collective-permute-done.3.in_chip, bf16[80,1152]{1,0:T(8,128)(2,1)S(1)} %collective-permute-done.4.cross, ...), custom_call_target="tpu_custom_call" | custom-call | flops 2000000000 | bytes 3000000 | tf_op jit(solution)/shard_map/pallas_call | solution.py:459
  23.5 0.6 %collective-permute-start.11 = (bf16[2,32,1024]{2,1,0:T(8,128)(2,1)S(1)}, bf16[2,32,1024]{2,1,0:T(8,128)(2,1)S(1)}, u32[]{:S(2)}, u32[]{:S(2)}) collective-permute-start(bf16[2,32,1024]{2,1,0:T(8,128)(2,1)S(1)} %get-tuple-element.44), channel_id=1, source_target_pairs={{0,8},{8,0},{16,24},{24,16},{1,9},{9,1},{17,25},{25,17},{2,10},{10... | collective-permute-start | bytes 393224 | tf_op jit(solution)/shard_map/ppermute | solution.py:364
  24.1 1.5 %collective-permute-start.12 = (bf16[2,32,1024]{2,1,0:T(8,128)(2,1)S(1)}, bf16[2,32,1024]{2,1,0:T(8,128)(2,1)S(1)}, u32[]{:S(2)}, u32[]{:S(2)}) collective-permute-start(bf16[2,32,1024]{2,1,0:T(8,128)(2,1)S(1)} %get-tuple-element.45), channel_id=1, source_target_pairs={{0,16},{8,24},{16,0},{24,8},{1,17},{9,25},{17,1},{25,9},{2,18},{10... | collective-permute-start | bytes 393224 | tf_op jit(solution)/shard_map/ppermute | solution.py:364
  25.6 1.5 %collective-permute-start.13 = (bf16[2,32,1024]{2,1,0:T(8,128)(2,1)S(1)}, bf16[2,32,1024]{2,1,0:T(8,128)(2,1)S(1)}, u32[]{:S(2)}, u32[]{:S(2)}) collective-permute-start(bf16[2,32,1024]{2,1,0:T(8,128)(2,1)S(1)} %get-tuple-element.46), channel_id=1, source_target_pairs={{0,24},{8,16},{16,8},{24,0},{1,25},{9,17},{17,9},{25,1},{2,26},{10... | collective-permute-start | bytes 393224 | tf_op jit(solution)/shard_map/ppermute | solution.py:364
  27.1 2.7 %collective-permute-done.11.refs_1_ = bf16[2,32,1024]{2,1,0:T(8,128)(2,1)S(1)} collective-permute-done((bf16[2,32,1024]{2,1,0:T(8,128)(2,1)S(1)}, bf16[2,32,1024]{2,1,0:T(8,128)(2,1)S(1)}, u32[]{:S(2)}, u32[]{:S(2)}) %collective-permute-start.11) | collective-permute-done | bytes 131104 | tf_op jit(solution)/shard_map/ppermute | solution.py:364
  29.8 2.1 %collective-permute-done.12.refs_2_ = bf16[2,32,1024]{2,1,0:T(8,128)(2,1)S(1)} collective-permute-done((bf16[2,32,1024]{2,1,0:T(8,128)(2,1)S(1)}, bf16[2,32,1024]{2,1,0:T(8,128)(2,1)S(1)}, u32[]{:S(2)}, u32[]{:S(2)}) %collective-permute-start.12) | collective-permute-done | bytes 131104 | tf_op jit(solution)/shard_map/ppermute | solution.py:364
  31.9 0.0 collective-permute-done.13.refs_3_
  31.9 0.8 %shard_map.104 = bf16[1,3,2,32,1024]{4,3,2,1,0:T(8,128)(2,1)} custom-call(bf16[2,32,1024]{2,1,0:T(8,128)(2,1)S(1)} %get-tuple-element.43.refs_0_, bf16[2,32,1024]{2,1,0:T(8,128)(2,1)S(1)} %collective-permute-done.11.refs_1_, bf16[2,32,1024]{2,1,0:T(8,128)(2,1)S(1)} %collective-permute-done.12.refs_2_, bf16[2,32,1024]{2,1,0:T(8,128)(2,1)S(1)} %collective-permute-done.13.refs_3_), custom_call_target="tpu_custom_call" | custom-call | bytes 1000000 | tf_op jit(solution)/shard_map/pallas_call | solution.py:468
Async XLA Ops:
  0.0 16.7 %copy-start.3 = (bf16[256,256]{1,0:T(8,128)(2,1)S(1)}, bf16[256,256]{1,0:T(8,128)(2,1)}, u32[]{:S(2)}) copy-start(bf16[256,256]{1,0:T(8,128)(2,1)} %constant.7.clone.left_tab) | copy-start | bytes 393220
  2.1 11.2 %collective-permute-start.10 = (bf16[64,1024]{1,0:T(8,128)(2,1)}, bf16[64,1024]{1,0:T(8,128)(2,1)S(1)}, u32[]{:S(2)}, u32[]{:S(2)}) collective-permute-start(bf16[64,1024]{1,0:T(8,128)(2,1)} %bitcast.1), channel_id=1, source_target_pairs={{0,1},{1,0},{2,4},{3,5},{4,2},{5,3},{6,7},{7,6},{8,9},{9,8},{10,12... | collective-permute-start | bytes 393224 | tf_op jit(solution)/shard_map/ppermute | solution.py:383
  2.6 7.6 %collective-permute-start = (bf16[32,1152]{1,0:T(8,128)(2,1)}, bf16[32,1152]{1,0:T(8,128)(2,1)S(1)}, u32[]{:S(2)}, u32[]{:S(2)}) collective-permute-start(bf16[32,1152]{1,0:T(8,128)(2,1)} %get-tuple-element.27), channel_id=1, source_target_pairs={{0,8},{8,0},{16,24},{24,16},{1,9},{9,1},{17,25},{25,17},{2,10},{10... | collective-permute-start | bytes 221192 | tf_op jit(solution)/shard_map/ppermute | solution.py:364
  5.2 6.6 %collective-permute-start.1 = (bf16[32,1152]{1,0:T(8,128)(2,1)}, bf16[32,1152]{1,0:T(8,128)(2,1)S(1)}, u32[]{:S(2)}, u32[]{:S(2)}) collective-permute-start(bf16[32,1152]{1,0:T(8,128)(2,1)} %get-tuple-element.28), channel_id=1, source_target_pairs={{0,16},{8,24},{16,0},{24,8},{1,17},{9,25},{17,1},{25,9},{2,18},{10... | collective-permute-start | bytes 221192 | tf_op jit(solution)/shard_map/ppermute | solution.py:364
  6.7 5.5 %collective-permute-start.2 = (bf16[32,1152]{1,0:T(8,128)(2,1)}, bf16[32,1152]{1,0:T(8,128)(2,1)S(1)}, u32[]{:S(2)}, u32[]{:S(2)}) collective-permute-start(bf16[32,1152]{1,0:T(8,128)(2,1)} %get-tuple-element.29), channel_id=1, source_target_pairs={{0,24},{8,16},{16,8},{24,0},{1,25},{9,17},{17,9},{25,1},{2,26},{10... | collective-permute-start | bytes 221192 | tf_op jit(solution)/shard_map/ppermute | solution.py:364
  6.8 8.1 %collective-permute-start.9 = (bf16[64,1024]{1,0:T(8,128)(2,1)}, bf16[64,1024]{1,0:T(8,128)(2,1)S(1)}, u32[]{:S(2)}, u32[]{:S(2)}) collective-permute-start(bf16[64,1024]{1,0:T(8,128)(2,1)} %bitcast.2), channel_id=1, source_target_pairs={{0,2},{1,3},{2,0},{3,1},{4,6},{5,7},{6,4},{7,5},{8,10},{9,11},{10,... | collective-permute-start | bytes 393224 | tf_op jit(solution)/shard_map/ppermute | solution.py:383
  10.3 6.2 %collective-permute-start.8 = (bf16[64,1024]{1,0:T(8,128)(2,1)}, bf16[64,1024]{1,0:T(8,128)(2,1)S(1)}, u32[]{:S(2)}, u32[]{:S(2)}) collective-permute-start(bf16[64,1024]{1,0:T(8,128)(2,1)} %bitcast.3), channel_id=1, source_target_pairs={{0,8},{1,2},{2,1},{3,4},{4,3},{5,6},{6,5},{7,15},{8,0},{9,10},{10,... | collective-permute-start | bytes 393224 | tf_op jit(solution)/shard_map/ppermute | solution.py:383
  11.8 4.9 %collective-permute-start.7 = (bf16[64,1024]{1,0:T(8,128)(2,1)}, bf16[64,1024]{1,0:T(8,128)(2,1)S(1)}, u32[]{:S(2)}, u32[]{:S(2)}) collective-permute-start(bf16[64,1024]{1,0:T(8,128)(2,1)} %bitcast.4), channel_id=1, source_target_pairs={{0,1},{1,0},{2,3},{3,2},{4,5},{5,4},{6,7},{7,6},{8,9},{9,8},{10,11... | collective-permute-start | bytes 393224 | tf_op jit(solution)/shard_map/ppermute | solution.py:383
  12.2 0.9 %copy-start = (bf16[32,1152]{1,0:T(8,128)(2,1)S(1)}, bf16[32,1152]{1,0:T(8,128)(2,1)}, u32[]{:S(2)}) copy-start(bf16[32,1152]{1,0:T(8,128)(2,1)} %get-tuple-element.26.refs_0_) | copy-start | bytes 221188
  13.1 3.6 %copy-start.1 = (bf16[2,32,1024]{2,1,0:T(8,128)(2,1)S(1)}, bf16[2,32,1024]{2,1,0:T(8,128)(2,1)}, u32[]{:S(2)}) copy-start(bf16[2,32,1024]{2,1,0:T(8,128)(2,1)} %get-tuple-element.35) | copy-start | bytes 393220
  13.1 3.6 %copy-start.2 = (bf16[256,256]{1,0:T(8,128)(2,1)S(1)}, bf16[256,256]{1,0:T(8,128)(2,1)}, u32[]{:S(2)}) copy-start(bf16[256,256]{1,0:T(8,128)(2,1)} %constant.6.clone.right_tab) | copy-start | bytes 393220
  13.2 7.5 %collective-permute-start.3 = (bf16[80,1152]{1,0:T(8,128)(2,1)S(1)}, bf16[80,1152]{1,0:T(8,128)(2,1)S(1)}, u32[]{:S(2)}, u32[]{:S(2)}) collective-permute-start(bf16[80,1152]{1,0:T(8,128)(2,1)S(1)} %get-tuple-element.30), channel_id=1, source_target_pairs={{0,1},{1,0},{2,3},{3,2},{4,5},{5,4},{6,7},{7,6},{8,9},{9,8},{10,11... | collective-permute-start | bytes 552968 | tf_op jit(solution)/shard_map/ppermute | solution.py:383
  13.3 7.4 %collective-permute-start.4 = (bf16[80,1152]{1,0:T(8,128)(2,1)S(1)}, bf16[80,1152]{1,0:T(8,128)(2,1)S(1)}, u32[]{:S(2)}, u32[]{:S(2)}) collective-permute-start(bf16[80,1152]{1,0:T(8,128)(2,1)S(1)} %get-tuple-element.31), channel_id=1, source_target_pairs={{0,8},{1,2},{2,1},{3,4},{4,3},{5,6},{6,5},{7,15},{8,0},{9,10},{10,... | collective-permute-start | bytes 552968 | tf_op jit(solution)/shard_map/ppermute | solution.py:383
  14.9 5.8 %collective-permute-start.5 = (bf16[16,1152]{1,0:T(8,128)(2,1)S(1)}, bf16[16,1152]{1,0:T(8,128)(2,1)S(1)}, u32[]{:S(2)}, u32[]{:S(2)}) collective-permute-start(bf16[16,1152]{1,0:T(8,128)(2,1)S(1)} %get-tuple-element.32), channel_id=1, source_target_pairs={{0,2},{1,3},{2,0},{3,1},{4,6},{5,7},{6,4},{7,5},{8,10},{9,11},{10,... | collective-permute-start | bytes 110600 | tf_op jit(solution)/shard_map/ppermute | solution.py:383
  16.5 4.2 %collective-permute-start.6 = (bf16[16,1152]{1,0:T(8,128)(2,1)S(1)}, bf16[16,1152]{1,0:T(8,128)(2,1)S(1)}, u32[]{:S(2)}, u32[]{:S(2)}) collective-permute-start(bf16[16,1152]{1,0:T(8,128)(2,1)S(1)} %get-tuple-element.33), channel_id=1, source_target_pairs={{0,1},{1,0},{2,4},{3,5},{4,2},{5,3},{6,7},{7,6},{8,9},{9,8},{10,12... | collective-permute-start | bytes 110600 | tf_op jit(solution)/shard_map/ppermute | solution.py:383
  16.7 4.0 %copy-start.4 = (bf16[192,192]{1,0:T(8,128)(2,1)S(1)}, bf16[192,192]{1,0:T(8,128)(2,1)}, u32[]{:S(2)}) copy-start(bf16[192,192]{1,0:T(8,128)(2,1)} %constant.8.clone.left_tab) | copy-start | bytes 221188
  23.5 6.3 %collective-permute-start.11 = (bf16[2,32,1024]{2,1,0:T(8,128)(2,1)S(1)}, bf16[2,32,1024]{2,1,0:T(8,128)(2,1)S(1)}, u32[]{:S(2)}, u32[]{:S(2)}) collective-permute-start(bf16[2,32,1024]{2,1,0:T(8,128)(2,1)S(1)} %get-tuple-element.44), channel_id=1, source_target_pairs={{0,8},{8,0},{16,24},{24,16},{1,9},{9,1},{17,25},{25,17},{2,10},{10... | collective-permute-start | bytes 393224 | tf_op jit(solution)/shard_map/ppermute | solution.py:364
  24.1 7.8 %collective-permute-start.12 = (bf16[2,32,1024]{2,1,0:T(8,128)(2,1)S(1)}, bf16[2,32,1024]{2,1,0:T(8,128)(2,1)S(1)}, u32[]{:S(2)}, u32[]{:S(2)}) collective-permute-start(bf16[2,32,1024]{2,1,0:T(8,128)(2,1)S(1)} %get-tuple-element.45), channel_id=1, source_target_pairs={{0,16},{8,24},{16,0},{24,8},{1,17},{9,25},{17,1},{25,9},{2,18},{10... | collective-permute-start | bytes 393224 | tf_op jit(solution)/shard_map/ppermute | solution.py:364
  25.6 6.3 %collective-permute-start.13 = (bf16[2,32,1024]{2,1,0:T(8,128)(2,1)S(1)}, bf16[2,32,1024]{2,1,0:T(8,128)(2,1)S(1)}, u32[]{:S(2)}, u32[]{:S(2)}) collective-permute-start(bf16[2,32,1024]{2,1,0:T(8,128)(2,1)S(1)} %get-tuple-element.46), channel_id=1, source_target_pairs={{0,24},{8,16},{16,8},{24,0},{1,25},{9,17},{17,9},{25,1},{2,26},{10... | collective-permute-start | bytes 393224 | tf_op jit(solution)/shard_map/ppermute | solution.py:364

commit v21 on v20

--- a/solution.py
+++ b/solution.py
@@ -22,7 +22,7 @@
 HALF = LANES // 2
 NEAR = 2 * BAND + KR
 FAR = KR
-VMEM_LIMIT = 48 * 1024 * 1024
+VMEM_LIMIT = 40 * 1024 * 1024
 PACK_LIMIT = 63 * 1024 * 1024
 
 
@@ -142,26 +142,24 @@
         far[...] = own[0, pl.ds(pl.multiple_of(start, KR), KR), :HALO_W]
 
 
-def ordered(in_chip, cross, far_even, far_odd):
-    band = lax.axis_index("rows")
-    count = lax.axis_size("rows")
-    even_core = band % 2 == 0
-    even_chip = (band // 2) % 2 == 0
-
-    def received(value, by, phase):
-        lower = (band // by) % 2 == phase
-        paired = jnp.where(lower, band + by < count, band >= by)
-        value = value[...]
-        return jnp.where(paired, value, jnp.zeros_like(value))
-
+def received(value, by, phase):
+    band, count = lax.axis_index("rows"), lax.axis_size("rows")
+    lower = (band // by) % 2 == phase
+    paired = jnp.where(lower, band + by < count, band >= by)
+    value = value[...]
+    return jnp.where(paired, value, jnp.zeros_like(value))
+
+
+def near_sides(in_chip, cross):
+    even_core = lax.axis_index("rows") % 2 == 0
     in_chip, cross = received(in_chip, 1, 0), received(cross, 1, 1)
+    return jnp.where(even_core, cross, in_chip), jnp.where(even_core, in_chip, cross)
+
+
+def far_sides(far_even, far_odd):
+    even_chip = (lax.axis_index("rows") // 2) % 2 == 0
     far_even, far_odd = received(far_even, 2, 0), received(far_odd, 2, 1)
-    return (
-        jnp.where(even_core, cross, in_chip),
-        jnp.where(even_core, in_chip, cross),
-        jnp.where(even_chip, far_odd, far_even),
-        jnp.where(even_chip, far_even, far_odd),
-    )
+    return jnp.where(even_chip, far_odd, far_even), jnp.where(even_chip, far_even, far_odd)
 
 
 def tiles_below(value, height):
@@ -260,11 +258,16 @@
     own, incident, in_chip, cross, far_even, far_odd, left_tab, right_tab,
     first, stereo, clear, col_mats, *row_mats
 ):
-    low_near, high_near, low_far, high_far = ordered(in_chip, cross, far_even, far_odd)
+    low_near, high_near = near_sides(in_chip, cross)
+    low_far, high_far = far_sides(far_even, far_odd)
+    colour = own_colour()
     extended = []
     for part in range(2):
-        pieces = [low_far, low_near, incident[...], high_near, high_far]
-        pieces = [piece[part * BAND : (part + 1) * BAND] for piece in pieces]
+        low_rows, near_rows, high_rows, top_rows = (
+            side[part * BAND : (part + 1) * BAND]
+            for side in (low_far, low_near, high_near, high_far)
+        )
+        pieces = [low_rows, near_rows, incident[colour, part], high_rows, top_rows]
         extended.append(jnp.concatenate(pieces, axis=0))
     row_mat, col_mat = filters(own[0, 0:16, COLS:].astype(jnp.float32), 0)
     first[...] = propagated(extended[0], extended[1], row_mat, col_mat, 0)
@@ -283,34 +286,39 @@
             stereo[part, :, tile * LANES : (tile + 1) * LANES] = block
 
 
+def near_kernel(light_in_chip, light_cross, near_tab, right_tab, near_tiles, near_clear):
+    low, high = near_sides(light_in_chip, light_cross)
+    blocks = [
+        jnp.concatenate([low[0:BAND], high[0:BAND], low[2 * BAND :]], axis=0),
+        jnp.concatenate(
+            [low[BAND : 2 * BAND], high[BAND : 2 * BAND], high[2 * BAND :]], axis=0
+        ),
+    ]
+    near_tiles[...] = stereo_tiles([block[:, :COLS] for block in blocks], near_tab, right_tab)
+    edges = jnp.concatenate([block[:, COLS : COLS + NH] for block in blocks], axis=0)
+    near_clear[...] = clear_pixels(edges)
+
+
 def chain_kernel(
-    in_chip, cross, far_even, far_odd, left_tab, right_tab, first, stereo, clear, col_mats, *rest
+    far_even, far_odd, left_tab, right_tab,
+    near_tiles, near_clear, first, stereo, clear, col_mats, *rest
 ):
     row_mats, outs, field = rest[: LAYERS - 1], rest[LAYERS - 1 : -1], rest[-1]
     depth = lax.axis_index("depth")
-    low_near, high_near, low_far, high_far = ordered(in_chip, cross, far_even, far_odd)
-    pieces = [
-        low_far,
-        low_near[0:BAND],
-        high_near[0:BAND],
-        high_far,
-        low_near[BAND : 2 * BAND],
-        high_near[BAND : 2 * BAND],
-        low_near[2 * BAND : NEAR],
-        high_near[2 * BAND : NEAR],
-    ]
-    halo = jnp.concatenate(pieces, axis=0)
-    half = halo.shape[0] // 2
-    halo_tiles = stereo_tiles(
-        [halo[:half, :COLS], halo[half:, :COLS]], left_tab, right_tab
-    )
-    halo_clear = clear_pixels(halo[:, COLS : COLS + NH])
-    begins = (0, half, half + 2 * BAND, 0)
-    sides = (BAND + FAR, BAND, KR, 0)
+    far = jnp.concatenate(far_sides(far_even, far_odd), axis=0)
+    far_tiles = stereo_tiles([far[:, :COLS]], left_tab, right_tab)
+    far_clear = clear_pixels(far[:, COLS : COLS + NH])
+
+    spots = (
+        ((0, BAND), (BAND, BAND)),
+        ((NEAR, BAND), (NEAR + BAND, BAND)),
+        ((2 * BAND, KR), (NEAR + 2 * BAND, KR)),
+        None,
+    )
     for layer in range(LAYERS):
         height = layer_height(layer)
         before = height + 2 * KR
-        low, side = begins[layer], sides[layer]
+        side = (height - BAND) // 2
         if layer == 0:
             columned = first
         else:
@@ -320,21 +328,33 @@
         band = slice(layer * BAND, (layer + 1) * BAND)
         pieces = [clear[band]]
         if side:
-            pieces = [halo_clear[low : low + side], clear[band], halo_clear[low + side : low + 2 * side]]
+            (low, count), (high, _) = spots[layer]
+            pieces = [near_clear[low : low + count], clear[band], near_clear[high : high + count]]
+        if layer == 0:
+            pieces = [far_clear[:FAR]] + pieces + [far_clear[FAR:]]
         passing = jnp.concatenate(pieces, axis=0)
         for tile in range(TILES):
             span = slice(tile * height, (tile + 1) * height)
             lanes = slice(tile * LANES, (tile + 1) * LANES)
-            row = (low // half * TILES + tile) * half + low % half
             for part in range(2):
                 within = slice(part * LANES, (part + 1) * LANES)
                 pieces = [stereo[part, band, lanes]]
                 if side:
+                    rows = [
+                        (start // NEAR * TILES + tile) * NEAR + start % NEAR for start in (low, high)
+                    ]
                     pieces = [
-                        halo_tiles[row : row + side, within],
+                        near_tiles[rows[0] : rows[0] + count, within],
                         stereo[part, band, lanes],
-                        halo_tiles[row + side : row + 2 * side, within],
+                        near_tiles[rows[1] : rows[1] + count, within],
                     ]
+                if layer == 0:
+                    row = tile * 2 * FAR
+                    pieces = (
+                        [far_tiles[row : row + FAR, within]]
+                        + pieces
+                        + [far_tiles[row + FAR : row + 2 * FAR, within]]
+                    )
                 added = jnp.concatenate(pieces, axis=0)
                 value = passing[:, lanes] * columned[span, within] + added
                 field[part, :height, lanes] = value.astype(jnp.bfloat16)
@@ -360,8 +380,11 @@
         pltpu.make_async_copy(arrived[0], out.at[0, colour], sems.at[colour]).wait()
 
 
-def over_depth(value, hop):
-    return lax.ppermute(value, "depth", [(i, i ^ hop) for i in range(LAYERS)])
+def all_depths(values):
+    arrived = list(values)
+    for hop in (3, 1, 2):
+        arrived[hop] = lax.ppermute(values[hop], "depth", [(i, i ^ hop) for i in range(LAYERS)])
+    return arrived
 
 
 def exchanged(value, by, phase):
@@ -431,7 +454,7 @@
         limit=PACK_LIMIT,
     )(hogel_light, silhouette, fill_counts, hogel_index, row_taps, col_taps, incident)
     mine = mine.reshape(2 * BAND, COLS)
-    layers_in = messages[:1] + [over_depth(messages[hop], hop) for hop in range(1, LAYERS)]
+    layers_in = all_depths(messages)
     arrived = neighbours((mine,) * 4)
     near = shaped((NEAR, HALO_W), bf16)
     far = shaped((FAR, HALO_W), bf16)
@@ -454,8 +477,14 @@
         [vmem] * 8,
         flops=10**9,
         moved=3 * 10**6,
-    )(own, mine, *arrived, jnp.asarray(left_table(LANES)), right_tab)
-    halo_rows = NEAR + FAR
+    )(own, incident, *arrived, jnp.asarray(left_table(LANES)), right_tab)
+    side_made = call(
+        near_kernel,
+        [shaped((2 * NEAR * TILES, 2 * LANES), f32), shaped((2 * NEAR, COLS), f32)],
+        [vmem] * 4,
+        flops=5 * 10**8,
+        moved=2 * 10**6,
+    )(*halos[:2], jnp.asarray(left_table(NEAR)), right_tab)
     results = call(
         chain_kernel,
         [shaped((2, BAND, COLS), bf16)] * LAYERS,
@@ -463,8 +492,8 @@
         [pltpu.VMEM((2, layer_height(0), COLS), bf16)],
         flops=2 * 10**9,
         moved=3 * 10**6,
-    )(*halos, jnp.asarray(left_table(halo_rows)), right_tab, *made)
-    returned = [results[0]] + [over_depth(results[hop], hop) for hop in range(1, LAYERS)]
+    )(*halos[2:], jnp.asarray(left_table(2 * FAR)), right_tab, *side_made, *made)
+    returned = all_depths(results)
     return call(
         home_kernel,
         shaped((1, COLORS, 2, BAND, COLS), bf16),

time: 32.8 us -> 35.6 us (1.085)
  local copies, waits for them, and re-layouts: 0.9 us -> 3.7 us
  starting transfers between devices: 16.7 us -> 16.2 us
    unnamed x10 -> x14, local copies, waits for them, and re-layouts: 0.9 us -> 3.7 us
    ppermute x6, waiting for transfers between devices: 5.23 us -> 7.64 us  [all_depths(): lax.ppermute(values[hop], 'depth', [(i, i ^ hop) for i in range(LAYERS)])]
    ppermute x8, waiting for transfers between devices: 2.81 us -> 0.52 us  [exchanged(): return lax.ppermute(value, ('depth', 'rows'), pairs)]
    ppermute x8, starting transfers between devices: 9.04 us -> 8.07 us  [exchanged(): return lax.ppermute(value, ('depth', 'rows'), pairs)]
    pallas_call x0 -> x1, Pallas kernels: none -> 0.69 us  [body(): call(near_kernel, [shaped((2 * NEAR * TILES, 2 * LANES), f32), shaped((2...]
    ppermute x6, starting transfers between devices: 7.67 us -> 8.16 us  [all_depths(): lax.ppermute(values[hop], 'depth', [(i, i ^ hop) for i in range(LAYERS)])]
    pallas_call x1, Pallas kernels: 2.77 us -> 2.36 us  [body(): call(chain_kernel, [shaped((2, BAND, COLS), bf16)] * LAYERS, [vmem] * (6...]
  transfers between devices with their start and end apart: 14 -> 14, of which waited for: 4 -> 4; matrix products, arithmetic and copies ran while one was open for 0% -> 0% of each run, Pallas kernels for 4% -> 6%
where the time goes in v21:
time: 35.6 us; the launch traced here: 35.4 us
  starting transfers between devices  16.2 us (46%)
  waiting for transfers between devices  8.16 us (23%)
  Pallas kernels  7.16 us (20%)
  local copies, waits for them, and re-layouts  3.7 us (10%)
    ppermute x6, starting transfers between devices, all_depths(): lax.ppermute(values[hop], 'depth', [(i, i ^ hop) for i in range(LAYERS)])  8.16 us
    ppermute x8, starting transfers between devices, exchanged(): return lax.ppermute(value, ('depth', 'rows'), pairs)  8.07 us
    ppermute x6, waiting for transfers between devices, all_depths(): lax.ppermute(values[hop], 'depth', [(i, i ^ hop) for i in range(LAYERS)])  7.64 us
    unnamed x14, local copies, waits for them, and re-layouts  3.7 us
    pallas_call x1, Pallas kernels, body(): call(chain_kernel, [shaped((2, BAND, COLS), bf16)] * LAYERS, [vmem] * (6...  2.36 us
    pallas_call x1, Pallas kernels, body(): call(pack_kernel, (shaped((BAND, HALO_W), bf16),) * LAYERS + (shaped(inci...  2.08 us
    pallas_call x1, Pallas kernels, body(): call(prepare_kernel, [shaped((TILES * layer_height(0), 2 * LANES), f32),...  1.19 us
    pallas_call x1, Pallas kernels, body(): call(home_kernel, shaped((1, COLORS, 2, BAND, COLS), bf16), [vmem] * LAYE...  0.77 us
  transfers between devices with their start and end apart: 14, of which 4 were waited for; matrix products, arithmetic and copies ran while one was open for 0% of the time, Pallas kernels for 6%

profile of v21, /device:TPU:0, one launch (start us, length us, event | category | flops | bytes accessed | tf_op | source)
XLA Modules:
  0.0 35.4 jit_solution(3982650849205646052)
XLA Ops:
  0.0 2.1 %shard_map.109 = (bf16[32,1152]{1,0:T(8,128)(2,1)}, bf16[32,1152]{1,0:T(8,128)(2,1)}, bf16[32,1152]{1,0:T(8,128)(2,1)}, bf16[32,1152]{1,0:T(8,128)(2,1)}, bf16[2,32,1024]{2,1,0:T(8,128)(2,1)}) custom-call(f32[1,3,32,1024]{3,2,1,0:T(8,128)} %light.1, s32[1,32,64]{2,1,0:T(8,128)} %edges.1, s32[1,2]{1,0:T(1,128)} %counts.1, s32[1,2,64]{2,1,0:T(2,128)} %listed.1, ...), custom_call_target="tpu_custom_call" | custom-call | flops 10000000 | bytes 1000000 | tf_op jit(solution)/shard_map/pallas_call | solution.py:448
  2.1 0.5 %collective-permute-start.10 = (bf16[64,1024]{1,0:T(8,128)(2,1)}, bf16[64,1024]{1,0:T(8,128)(2,1)S(1)}, u32[]{:S(2)}, u32[]{:S(2)}) collective-permute-start(bf16[64,1024]{1,0:T(8,128)(2,1)} %bitcast.1), channel_id=1, source_target_pairs={{0,1},{1,0},{2,4},{3,5},{4,2},{5,3},{6,7},{7,6},{8,9},{9,8},{10,12... | collective-permute-start | bytes 393224 | tf_op jit(solution)/shard_map/ppermute | solution.py:406
  2.6 2.6 %collective-permute-start = (bf16[32,1152]{1,0:T(8,128)(2,1)}, bf16[32,1152]{1,0:T(8,128)(2,1)S(1)}, u32[]{:S(2)}, u32[]{:S(2)}) collective-permute-start(bf16[32,1152]{1,0:T(8,128)(2,1)} %get-tuple-element.29), channel_id=1, source_target_pairs={{0,8},{8,0},{16,24},{24,16},{1,9},{9,1},{17,25},{25,17},{2,10},{10... | collective-permute-start | bytes 221192 | tf_op jit(solution)/shard_map/ppermute | solution.py:386
  5.2 1.5 %collective-permute-start.1 = (bf16[32,1152]{1,0:T(8,128)(2,1)}, bf16[32,1152]{1,0:T(8,128)(2,1)S(1)}, u32[]{:S(2)}, u32[]{:S(2)}) collective-permute-start(bf16[32,1152]{1,0:T(8,128)(2,1)} %get-tuple-element.30), channel_id=1, source_target_pairs={{0,16},{8,24},{16,0},{24,8},{1,17},{9,25},{17,1},{25,9},{2,18},{10... | collective-permute-start | bytes 221192 | tf_op jit(solution)/shard_map/ppermute | solution.py:386
  6.7 0.0 collective-permute-start.2
  6.7 0.0 collective-permute-start.7
  6.7 1.5 %collective-permute-done.refs_1_ = bf16[32,1152]{1,0:T(8,128)(2,1)S(1)} collective-permute-done((bf16[32,1152]{1,0:T(8,128)(2,1)}, bf16[32,1152]{1,0:T(8,128)(2,1)S(1)}, u32[]{:S(2)}, u32[]{:S(2)}) %collective-permute-start) | collective-permute-done | bytes 73760 | tf_op jit(solution)/shard_map/ppermute | solution.py:386
  8.2 2.1 %collective-permute-start.8 = (bf16[64,1024]{1,0:T(8,128)(2,1)}, bf16[64,1024]{1,0:T(8,128)(2,1)S(1)}, u32[]{:S(2)}, u32[]{:S(2)}) collective-permute-start(bf16[64,1024]{1,0:T(8,128)(2,1)} %bitcast.3), channel_id=1, source_target_pairs={{0,8},{1,2},{2,1},{3,4},{4,3},{5,6},{6,5},{7,15},{8,0},{9,10},{10,... | collective-permute-start | bytes 393224 | tf_op jit(solution)/shard_map/ppermute | solution.py:406
  10.4 0.0 collective-permute-done.1.refs_2_
  10.4 3.2 %collective-permute-start.9 = (bf16[64,1024]{1,0:T(8,128)(2,1)}, bf16[64,1024]{1,0:T(8,128)(2,1)S(1)}, u32[]{:S(2)}, u32[]{:S(2)}) collective-permute-start(bf16[64,1024]{1,0:T(8,128)(2,1)} %bitcast.4), channel_id=1, source_target_pairs={{0,2},{1,3},{2,0},{3,1},{4,6},{5,7},{6,4},{7,5},{8,10},{9,11},{10,... | collective-permute-start | bytes 393224 | tf_op jit(solution)/shard_map/ppermute | solution.py:406
  13.6 0.0 collective-permute-done.2.refs_3_
  13.6 0.0 copy-start.1
  13.6 0.9 %copy-done.1 = bf16[32,1152]{1,0:T(8,128)(2,1)S(1)} copy-done((bf16[32,1152]{1,0:T(8,128)(2,1)S(1)}, bf16[32,1152]{1,0:T(8,128)(2,1)}, u32[]{:S(2)}) %copy-start.1) | copy-done | bytes 73752
  14.5 0.1 shard_map.110
  14.6 0.1 collective-permute-start.5
  14.6 0.0 collective-permute-done.10.far_odd
  14.7 0.2 collective-permute-start.6
  14.9 0.0 collective-permute-done.7.in_chip
  14.9 1.9 %collective-permute-start.3 = (bf16[16,1152]{1,0:T(8,128)(2,1)S(1)}, bf16[16,1152]{1,0:T(8,128)(2,1)S(1)}, u32[]{:S(2)}, u32[]{:S(2)}) collective-permute-start(bf16[16,1152]{1,0:T(8,128)(2,1)S(1)} %get-tuple-element.32), channel_id=1, source_target_pairs={{0,2},{1,3},{2,0},{3,1},{4,6},{5,7},{6,4},{7,5},{8,10},{9,11},{10,... | collective-permute-start | bytes 110600 | tf_op jit(solution)/shard_map/ppermute | solution.py:406
  16.8 0.0 collective-permute-done.8.cross
  16.8 0.0 collective-permute-start.4
  16.8 0.5 %collective-permute-done.9.far_even = bf16[64,1024]{1,0:T(8,128)(2,1)S(1)} collective-permute-done((bf16[64,1024]{1,0:T(8,128)(2,1)}, bf16[64,1024]{1,0:T(8,128)(2,1)S(1)}, u32[]{:S(2)}, u32[]{:S(2)}) %collective-permute-start.9) | collective-permute-done | bytes 131104 | tf_op jit(solution)/shard_map/ppermute | solution.py:406
  17.3 0.0 copy-start
  17.3 1.0 %copy-done = bf16[3,2,32,1024]{3,2,1,0:T(8,128)(2,1)S(1)} copy-done((bf16[3,2,32,1024]{3,2,1,0:T(8,128)(2,1)S(1)}, bf16[3,2,32,1024]{3,2,1,0:T(8,128)(2,1)}, u32[]{:S(2)}) %copy-start) | copy-done | bytes 393240
  18.3 0.0 copy-start.2
  18.3 0.9 %copy-done.2 = bf16[256,256]{1,0:T(8,128)(2,1)S(1)} copy-done((bf16[256,256]{1,0:T(8,128)(2,1)S(1)}, bf16[256,256]{1,0:T(8,128)(2,1)}, u32[]{:S(2)}) %copy-start.2) | copy-done | bytes 131096
  19.2 0.0 copy-start.4
  19.2 0.9 %copy-done.4 = bf16[256,256]{1,0:T(8,128)(2,1)S(1)} copy-done((bf16[256,256]{1,0:T(8,128)(2,1)S(1)}, bf16[256,256]{1,0:T(8,128)(2,1)}, u32[]{:S(2)}) %copy-start.4) | copy-done | bytes 131096
  20.1 0.0 copy-start.3
  20.1 0.0 copy-start.5
  20.1 1.2 %shard_map.112 = (f32[1024,256]{1,0:T(8,128)S(1)}, f32[2,128,1024]{2,1,0:T(8,128)S(1)}, f32[128,1024]{1,0:T(8,128)S(1)}, bf16[3,256,512]{2,1,0:T(8,128)(2,1)S(1)...) custom-call(bf16[4,32,1152]{2,1,0:T(8,128)(2,1)S(1)} %get-tuple-element.38.own, ...), custom_call_target="tpu_custom_call" | custom-call | flops 1000000000 | bytes 3000000 | tf_op jit(solution)/shard_map/pallas_call | solution.py:468
  21.3 0.0 copy-start.6
  21.3 0.0 collective-permute-done.5.light_in_chip
  21.3 0.0 collective-permute-done.6.light_cross
  21.3 0.0 copy-done.3
  21.3 0.0 copy-done.5
  21.3 0.7 %shard_map.111 = (f32[1280,256]{1,0:T(8,128)S(1)}, f32[160,1024]{1,0:T(8,128)S(1)}) custom-call(bf16[80,1152]{1,0:T(8,128)(2,1)S(1)} %collective-permute-done.5.light_in_chip, bf16[80,1152]{1,0:T(8,128)(2,1)S(1)} %collective-permute-done.6.light_cross, bf16[160,160]{1,0:T(8,128)(2,1)S(1)} %copy-done.5, bf16[256,256]{1,0:T(8,128)(2,1)S(1)} %copy-done.3), custom_call_target="tpu_custom_call" | custom-call | flops 500000000 | bytes 2000000 | tf_op jit(solution)/shard_map/pallas_call | solution.py:481
  22.0 0.0 collective-permute-done.3.far_even
  22.1 0.0 collective-permute-done.4.far_odd
  22.1 0.0 copy-done.6
  22.1 2.4 %shard_map.113 = (bf16[2,32,1024]{2,1,0:T(8,128)(2,1)S(1)}, bf16[2,32,1024]{2,1,0:T(8,128)(2,1)S(1)}, bf16[2,32,1024]{2,1,0:T(8,128)(2,1)S(1)}, bf16[2,32,1024]{2,1,0:T(8,128)(2,1)S(1)}) custom-call(bf16[16,1152]{1,0:T(8,128)(2,1)S(1)} %collective-permute-done.3.far_even, bf16[16,1152]{1,0:T(8,128)(2,1)S(1)} %collective-permute-done.4.far_odd, ...), custom_call_target="tpu_custom_call" | custom-call | flops 2000000000 | bytes 3000000 | tf_op jit(solution)/shard_map/pallas_call | solution.py:488
  24.4 2.3 %collective-permute-start.11 = (bf16[2,32,1024]{2,1,0:T(8,128)(2,1)S(1)}, bf16[2,32,1024]{2,1,0:T(8,128)(2,1)S(1)}, u32[]{:S(2)}, u32[]{:S(2)}) collective-permute-start(bf16[2,32,1024]{2,1,0:T(8,128)(2,1)S(1)} %get-tuple-element.48), channel_id=1, source_target_pairs={{0,8},{8,0},{16,24},{24,16},{1,9},{9,1},{17,25},{25,17},{2,10},{10... | collective-permute-start | bytes 393224 | tf_op jit(solution)/shard_map/ppermute | solution.py:386
  26.8 1.7 %collective-permute-start.12 = (bf16[2,32,1024]{2,1,0:T(8,128)(2,1)S(1)}, bf16[2,32,1024]{2,1,0:T(8,128)(2,1)S(1)}, u32[]{:S(2)}, u32[]{:S(2)}) collective-permute-start(bf16[2,32,1024]{2,1,0:T(8,128)(2,1)S(1)} %get-tuple-element.49), channel_id=1, source_target_pairs={{0,16},{8,24},{16,0},{24,8},{1,17},{9,25},{17,1},{25,9},{2,18},{10... | collective-permute-start | bytes 393224 | tf_op jit(solution)/shard_map/ppermute | solution.py:386
  28.5 0.0 collective-permute-start.13
  28.5 2.2 %collective-permute-done.11.refs_1_ = bf16[2,32,1024]{2,1,0:T(8,128)(2,1)S(1)} collective-permute-done((bf16[2,32,1024]{2,1,0:T(8,128)(2,1)S(1)}, bf16[2,32,1024]{2,1,0:T(8,128)(2,1)S(1)}, u32[]{:S(2)}, u32[]{:S(2)}) %collective-permute-start.11) | collective-permute-done | bytes 131104 | tf_op jit(solution)/shard_map/ppermute | solution.py:386
  30.7 4.0 %collective-permute-done.12.refs_2_ = bf16[2,32,1024]{2,1,0:T(8,128)(2,1)S(1)} collective-permute-done((bf16[2,32,1024]{2,1,0:T(8,128)(2,1)S(1)}, bf16[2,32,1024]{2,1,0:T(8,128)(2,1)S(1)}, u32[]{:S(2)}, u32[]{:S(2)}) %collective-permute-start.12) | collective-permute-done | bytes 131104 | tf_op jit(solution)/shard_map/ppermute | solution.py:386
  34.6 0.0 collective-permute-done.13.refs_3_
  34.6 0.8 %shard_map.114 = bf16[1,3,2,32,1024]{4,3,2,1,0:T(8,128)(2,1)} custom-call(bf16[2,32,1024]{2,1,0:T(8,128)(2,1)S(1)} %get-tuple-element.47.refs_0_, bf16[2,32,1024]{2,1,0:T(8,128)(2,1)S(1)} %collective-permute-done.11.refs_1_, bf16[2,32,1024]{2,1,0:T(8,128)(2,1)S(1)} %collective-permute-done.12.refs_2_, bf16[2,32,1024]{2,1,0:T(8,128)(2,1)S(1)} %collective-permute-done.13.refs_3_), custom_call_target="tpu_custom_call" | custom-call | bytes 1000000 | tf_op jit(solution)/shard_map/pallas_call | solution.py:497
Async XLA Ops:
  2.1 12.6 %collective-permute-start.10 = (bf16[64,1024]{1,0:T(8,128)(2,1)}, bf16[64,1024]{1,0:T(8,128)(2,1)S(1)}, u32[]{:S(2)}, u32[]{:S(2)}) collective-permute-start(bf16[64,1024]{1,0:T(8,128)(2,1)} %bitcast.1), channel_id=1, source_target_pairs={{0,1},{1,0},{2,4},{3,5},{4,2},{5,3},{6,7},{7,6},{8,9},{9,8},{10,12... | collective-permute-start | bytes 393224 | tf_op jit(solution)/shard_map/ppermute | solution.py:406
  2.6 5.6 %collective-permute-start = (bf16[32,1152]{1,0:T(8,128)(2,1)}, bf16[32,1152]{1,0:T(8,128)(2,1)S(1)}, u32[]{:S(2)}, u32[]{:S(2)}) collective-permute-start(bf16[32,1152]{1,0:T(8,128)(2,1)} %get-tuple-element.29), channel_id=1, source_target_pairs={{0,8},{8,0},{16,24},{24,16},{1,9},{9,1},{17,25},{25,17},{2,10},{10... | collective-permute-start | bytes 221192 | tf_op jit(solution)/shard_map/ppermute | solution.py:386
  5.2 5.2 %collective-permute-start.1 = (bf16[32,1152]{1,0:T(8,128)(2,1)}, bf16[32,1152]{1,0:T(8,128)(2,1)S(1)}, u32[]{:S(2)}, u32[]{:S(2)}) collective-permute-start(bf16[32,1152]{1,0:T(8,128)(2,1)} %get-tuple-element.30), channel_id=1, source_target_pairs={{0,16},{8,24},{16,0},{24,8},{1,17},{9,25},{17,1},{25,9},{2,18},{10... | collective-permute-start | bytes 221192 | tf_op jit(solution)/shard_map/ppermute | solution.py:386
  6.7 6.9 %collective-permute-start.2 = (bf16[32,1152]{1,0:T(8,128)(2,1)}, bf16[32,1152]{1,0:T(8,128)(2,1)S(1)}, u32[]{:S(2)}, u32[]{:S(2)}) collective-permute-start(bf16[32,1152]{1,0:T(8,128)(2,1)} %get-tuple-element.31), channel_id=1, source_target_pairs={{0,24},{8,16},{16,8},{24,0},{1,25},{9,17},{17,9},{25,1},{2,26},{10... | collective-permute-start | bytes 221192 | tf_op jit(solution)/shard_map/ppermute | solution.py:386
  6.7 8.2 %collective-permute-start.7 = (bf16[64,1024]{1,0:T(8,128)(2,1)}, bf16[64,1024]{1,0:T(8,128)(2,1)S(1)}, u32[]{:S(2)}, u32[]{:S(2)}) collective-permute-start(bf16[64,1024]{1,0:T(8,128)(2,1)} %bitcast.2), channel_id=1, source_target_pairs={{0,1},{1,0},{2,3},{3,2},{4,5},{5,4},{6,7},{7,6},{8,9},{9,8},{10,11... | collective-permute-start | bytes 393224 | tf_op jit(solution)/shard_map/ppermute | solution.py:406
  8.2 8.5 %collective-permute-start.8 = (bf16[64,1024]{1,0:T(8,128)(2,1)}, bf16[64,1024]{1,0:T(8,128)(2,1)S(1)}, u32[]{:S(2)}, u32[]{:S(2)}) collective-permute-start(bf16[64,1024]{1,0:T(8,128)(2,1)} %bitcast.3), channel_id=1, source_target_pairs={{0,8},{1,2},{2,1},{3,4},{4,3},{5,6},{6,5},{7,15},{8,0},{9,10},{10,... | collective-permute-start | bytes 393224 | tf_op jit(solution)/shard_map/ppermute | solution.py:406
  10.4 6.9 %collective-permute-start.9 = (bf16[64,1024]{1,0:T(8,128)(2,1)}, bf16[64,1024]{1,0:T(8,128)(2,1)S(1)}, u32[]{:S(2)}, u32[]{:S(2)}) collective-permute-start(bf16[64,1024]{1,0:T(8,128)(2,1)} %bitcast.4), channel_id=1, source_target_pairs={{0,2},{1,3},{2,0},{3,1},{4,6},{5,7},{6,4},{7,5},{8,10},{9,11},{10,... | collective-permute-start | bytes 393224 | tf_op jit(solution)/shard_map/ppermute | solution.py:406
  13.6 0.9 %copy-start.1 = (bf16[32,1152]{1,0:T(8,128)(2,1)S(1)}, bf16[32,1152]{1,0:T(8,128)(2,1)}, u32[]{:S(2)}) copy-start(bf16[32,1152]{1,0:T(8,128)(2,1)} %get-tuple-element.28.refs_0_) | copy-start | bytes 221188
  14.6 6.7 %collective-permute-start.5 = (bf16[80,1152]{1,0:T(8,128)(2,1)S(1)}, bf16[80,1152]{1,0:T(8,128)(2,1)S(1)}, u32[]{:S(2)}, u32[]{:S(2)}) collective-permute-start(bf16[80,1152]{1,0:T(8,128)(2,1)S(1)} %get-tuple-element.34), channel_id=1, source_target_pairs={{0,1},{1,0},{2,3},{3,2},{4,5},{5,4},{6,7},{7,6},{8,9},{9,8},{10,11... | collective-permute-start | bytes 552968 | tf_op jit(solution)/shard_map/ppermute | solution.py:406
  14.7 6.7 %collective-permute-start.6 = (bf16[80,1152]{1,0:T(8,128)(2,1)S(1)}, bf16[80,1152]{1,0:T(8,128)(2,1)S(1)}, u32[]{:S(2)}, u32[]{:S(2)}) collective-permute-start(bf16[80,1152]{1,0:T(8,128)(2,1)S(1)} %get-tuple-element.35), channel_id=1, source_target_pairs={{0,8},{1,2},{2,1},{3,4},{4,3},{5,6},{6,5},{7,15},{8,0},{9,10},{10,... | collective-permute-start | bytes 552968 | tf_op jit(solution)/shard_map/ppermute | solution.py:406
  14.9 7.1 %collective-permute-start.3 = (bf16[16,1152]{1,0:T(8,128)(2,1)S(1)}, bf16[16,1152]{1,0:T(8,128)(2,1)S(1)}, u32[]{:S(2)}, u32[]{:S(2)}) collective-permute-start(bf16[16,1152]{1,0:T(8,128)(2,1)S(1)} %get-tuple-element.32), channel_id=1, source_target_pairs={{0,2},{1,3},{2,0},{3,1},{4,6},{5,7},{6,4},{7,5},{8,10},{9,11},{10,... | collective-permute-start | bytes 110600 | tf_op jit(solution)/shard_map/ppermute | solution.py:406
  16.8 5.3 %collective-permute-start.4 = (bf16[16,1152]{1,0:T(8,128)(2,1)S(1)}, bf16[16,1152]{1,0:T(8,128)(2,1)S(1)}, u32[]{:S(2)}, u32[]{:S(2)}) collective-permute-start(bf16[16,1152]{1,0:T(8,128)(2,1)S(1)} %get-tuple-element.33), channel_id=1, source_target_pairs={{0,1},{1,0},{2,4},{3,5},{4,2},{5,3},{6,7},{7,6},{8,9},{9,8},{10,12... | collective-permute-start | bytes 110600 | tf_op jit(solution)/shard_map/ppermute | solution.py:406
  17.3 1.0 %copy-start = (bf16[3,2,32,1024]{3,2,1,0:T(8,128)(2,1)S(1)}, bf16[3,2,32,1024]{3,2,1,0:T(8,128)(2,1)}, u32[]{:S(2)}) copy-start(bf16[3,2,32,1024]{3,2,1,0:T(8,128)(2,1)} %incident.3) | copy-start | bytes 1179652
  18.3 0.9 %copy-start.2 = (bf16[256,256]{1,0:T(8,128)(2,1)S(1)}, bf16[256,256]{1,0:T(8,128)(2,1)}, u32[]{:S(2)}) copy-start(bf16[256,256]{1,0:T(8,128)(2,1)} %constant.8.clone.right_tab) | copy-start | bytes 393220
  19.2 0.9 %copy-start.4 = (bf16[256,256]{1,0:T(8,128)(2,1)S(1)}, bf16[256,256]{1,0:T(8,128)(2,1)}, u32[]{:S(2)}) copy-start(bf16[256,256]{1,0:T(8,128)(2,1)} %constant.9.clone.left_tab) | copy-start | bytes 393220
  20.1 1.2 %copy-start.3 = (bf16[256,256]{1,0:T(8,128)(2,1)S(1)}, bf16[256,256]{1,0:T(8,128)(2,1)}, u32[]{:S(2)}) copy-start(bf16[256,256]{1,0:T(8,128)(2,1)} %constant.8.clone.right_tab) | copy-start | bytes 393220
  20.1 1.2 %copy-start.5 = (bf16[160,160]{1,0:T(8,128)(2,1)S(1)}, bf16[160,160]{1,0:T(8,128)(2,1)}, u32[]{:S(2)}) copy-start(bf16[160,160]{1,0:T(8,128)(2,1)} %constant.10.clone.near_tab) | copy-start | bytes 153604
  21.3 0.8 %copy-start.6 = (bf16[64,64]{1,0:T(8,128)(2,1)S(1)}, bf16[64,64]{1,0:T(8,128)(2,1)}, u32[]{:S(2)}) copy-start(bf16[64,64]{1,0:T(8,128)(2,1)} %constant.11.clone.left_tab) | copy-start | bytes 24580
  24.4 6.2 %collective-permute-start.11 = (bf16[2,32,1024]{2,1,0:T(8,128)(2,1)S(1)}, bf16[2,32,1024]{2,1,0:T(8,128)(2,1)S(1)}, u32[]{:S(2)}, u32[]{:S(2)}) collective-permute-start(bf16[2,32,1024]{2,1,0:T(8,128)(2,1)S(1)} %get-tuple-element.48), channel_id=1, source_target_pairs={{0,8},{8,0},{16,24},{24,16},{1,9},{9,1},{17,25},{25,17},{2,10},{10... | collective-permute-start | bytes 393224 | tf_op jit(solution)/shard_map/ppermute | solution.py:386
  26.8 7.8 %collective-permute-start.12 = (bf16[2,32,1024]{2,1,0:T(8,128)(2,1)S(1)}, bf16[2,32,1024]{2,1,0:T(8,128)(2,1)S(1)}, u32[]{:S(2)}, u32[]{:S(2)}) collective-permute-start(bf16[2,32,1024]{2,1,0:T(8,128)(2,1)S(1)} %get-tuple-element.49), channel_id=1, source_target_pairs={{0,16},{8,24},{16,0},{24,8},{1,17},{9,25},{17,1},{25,9},{2,18},{10... | collective-permute-start | bytes 393224 | tf_op jit(solution)/shard_map/ppermute | solution.py:386
  28.5 6.1 %collective-permute-start.13 = (bf16[2,32,1024]{2,1,0:T(8,128)(2,1)S(1)}, bf16[2,32,1024]{2,1,0:T(8,128)(2,1)S(1)}, u32[]{:S(2)}, u32[]{:S(2)}) collective-permute-start(bf16[2,32,1024]{2,1,0:T(8,128)(2,1)S(1)} %get-tuple-element.50), channel_id=1, source_target_pairs={{0,24},{8,16},{16,8},{24,0},{1,25},{9,17},{17,9},{25,1},{2,26},{10... | collective-permute-start | bytes 393224 | tf_op jit(solution)/shard_map/ppermute | solution.py:386

commit v22 on v20

--- a/solution.py
+++ b/solution.py
@@ -257,7 +257,7 @@
 
 
 def prepare_kernel(
-    own, incident, in_chip, cross, far_even, far_odd, left_tab, right_tab,
+    own, incident, cross, far_even, far_odd, in_chip, left_tab, right_tab,
     first, stereo, clear, col_mats, *row_mats
 ):
     low_near, high_near, low_far, high_far = ordered(in_chip, cross, far_even, far_odd)
@@ -315,7 +315,11 @@
             columned = first
         else:
             columned = propagated(
-                field[0, :before], field[1, :before], row_mats[layer - 1], col_mats[layer - 1], layer
+                field[layer - 1, 0, :before],
+                field[layer - 1, 1, :before],
+                row_mats[layer - 1],
+                col_mats[layer - 1],
+                layer,
             )
         band = slice(layer * BAND, (layer + 1) * BAND)
         pieces = [clear[band]]
@@ -337,13 +341,12 @@
                     ]
                 added = jnp.concatenate(pieces, axis=0)
                 value = passing[:, lanes] * columned[span, within] + added
-                field[part, :height, lanes] = value.astype(jnp.bfloat16)
-        for hop, out in enumerate(outs):
-
-            @pl.when((depth ^ hop) == layer)
-            def keep(out=out, side=side):
-                for part in range(2):
-                    out[part] = field[part, side : side + BAND]
+                field[layer, part, :height, lanes] = value.astype(jnp.bfloat16)
+    for hop, out in enumerate(outs):
+        layer = depth ^ hop
+        start = pl.multiple_of((LAYERS - 1 - layer) * KR, KR)
+        for part in range(2):
+            out[part] = field[layer, part, pl.ds(start, BAND)]
 
 
 def home_kernel(*refs):
@@ -432,7 +435,7 @@
     )(hogel_light, silhouette, fill_counts, hogel_index, row_taps, col_taps, incident)
     mine = mine.reshape(2 * BAND, COLS)
     layers_in = messages[:1] + [over_depth(messages[hop], hop) for hop in range(1, LAYERS)]
-    arrived = neighbours((mine,) * 4)
+    in_chip, *arrived = neighbours((mine,) * 4)
     near = shaped((NEAR, HALO_W), bf16)
     far = shaped((FAR, HALO_W), bf16)
     own, *sent = call(
@@ -454,13 +457,13 @@
         [vmem] * 8,
         flops=10**9,
         moved=3 * 10**6,
-    )(own, mine, *arrived, jnp.asarray(left_table(LANES)), right_tab)
+    )(own, mine, *arrived, in_chip, jnp.asarray(left_table(LANES)), right_tab)
     halo_rows = NEAR + FAR
     results = call(
         chain_kernel,
         [shaped((2, BAND, COLS), bf16)] * LAYERS,
         [vmem] * (6 + len(made)),
-        [pltpu.VMEM((2, layer_height(0), COLS), bf16)],
+        [pltpu.VMEM((LAYERS, 2, layer_height(0), COLS), bf16)],
         flops=2 * 10**9,
         moved=3 * 10**6,
     )(*halos, jnp.asarray(left_table(halo_rows)), right_tab, *made)

time: 32.8 us -> 32.4 us (0.988)
  starting transfers between devices: 16.7 us -> 14.9 us
  waiting for transfers between devices: 8.04 us -> 9.68 us
    ppermute x6, waiting for transfers between devices: 5.23 us -> 7.54 us  [over_depth(): return lax.ppermute(value, 'depth', [(i, i ^ hop) for i in range(LAYERS)])]
    ppermute x8, starting transfers between devices: 9.04 us -> 7.22 us  [exchanged(): return lax.ppermute(value, ('depth', 'rows'), pairs)]
    ppermute x8, waiting for transfers between devices: 2.81 us -> 2.15 us  [exchanged(): return lax.ppermute(value, ('depth', 'rows'), pairs)]
  transfers between devices with their start and end apart: 14 -> 14, of which waited for: 4 -> 6; matrix products, arithmetic and copies ran while one was open for 0% -> 0% of each run, Pallas kernels for 4% -> 4%
where the time goes in v22:
time: 32.4 us; the launch traced here: 32.2 us
  starting transfers between devices  14.9 us (46%)
  waiting for transfers between devices  9.68 us (30%)
  Pallas kernels  6.67 us (21%)
  local copies, waits for them, and re-layouts  0.9 us (3%)
    ppermute x6, starting transfers between devices, over_depth(): return lax.ppermute(value, 'depth', [(i, i ^ hop) for i in range(LAYERS)])  7.67 us
    ppermute x6, waiting for transfers between devices, over_depth(): return lax.ppermute(value, 'depth', [(i, i ^ hop) for i in range(LAYERS)])  7.54 us
    ppermute x8, starting transfers between devices, exchanged(): return lax.ppermute(value, ('depth', 'rows'), pairs)  7.22 us
    pallas_call x1, Pallas kernels, body(): call(chain_kernel, [shaped((2, BAND, COLS), bf16)] * LAYERS, [vmem] * (6...  2.52 us
    ppermute x8, waiting for transfers between devices, exchanged(): return lax.ppermute(value, ('depth', 'rows'), pairs)  2.15 us
    pallas_call x1, Pallas kernels, body(): call(pack_kernel, (shaped((BAND, HALO_W), bf16),) * LAYERS + (shaped(inci...  2.12 us
    pallas_call x1, Pallas kernels, body(): call(prepare_kernel, [shaped((TILES * layer_height(0), 2 * LANES), f32),...  1.2 us
    unnamed x10, local copies, waits for them, and re-layouts  0.9 us
  transfers between devices with their start and end apart: 14, of which 6 were waited for; matrix products, arithmetic and copies ran while one was open for 0% of the time, Pallas kernels for 4%

profile of v22, /device:TPU:0, one launch (start us, length us, event | category | flops | bytes accessed | tf_op | source)
XLA Modules:
  0.0 32.2 jit_solution(15493931538440696173)
XLA Ops:
  0.0 0.0 copy-start.3
  0.0 2.1 %shard_map.100 = (bf16[32,1152]{1,0:T(8,128)(2,1)}, bf16[32,1152]{1,0:T(8,128)(2,1)}, bf16[32,1152]{1,0:T(8,128)(2,1)}, bf16[32,1152]{1,0:T(8,128)(2,1)}, bf16[2,32,1024]{2,1,0:T(8,128)(2,1)}) custom-call(f32[1,3,32,1024]{3,2,1,0:T(8,128)} %light.1, s32[1,32,64]{2,1,0:T(8,128)} %edges.1, s32[1,2]{1,0:T(1,128)} %counts.1, s32[1,2,64]{2,1,0:T(2,128)} %listed.1, ...), custom_call_target="tpu_custom_call" | custom-call | flops 10000000 | bytes 1000000 | tf_op jit(solution)/shard_map/pallas_call | solution.py:428
  2.1 0.5 %collective-permute-start.10 = (bf16[64,1024]{1,0:T(8,128)(2,1)}, bf16[64,1024]{1,0:T(8,128)(2,1)S(1)}, u32[]{:S(2)}, u32[]{:S(2)}) collective-permute-start(bf16[64,1024]{1,0:T(8,128)(2,1)} %bitcast.1), channel_id=1, source_target_pairs={{0,1},{1,0},{2,3},{3,2},{4,5},{5,4},{6,7},{7,6},{8,9},{9,8},{10,11... | collective-permute-start | bytes 393224 | tf_op jit(solution)/shard_map/ppermute | solution.py:386
  2.6 2.6 %collective-permute-start = (bf16[32,1152]{1,0:T(8,128)(2,1)}, bf16[32,1152]{1,0:T(8,128)(2,1)S(1)}, u32[]{:S(2)}, u32[]{:S(2)}) collective-permute-start(bf16[32,1152]{1,0:T(8,128)(2,1)} %get-tuple-element.27), channel_id=1, source_target_pairs={{0,8},{8,0},{16,24},{24,16},{1,9},{9,1},{17,25},{25,17},{2,10},{10... | collective-permute-start | bytes 221192 | tf_op jit(solution)/shard_map/ppermute | solution.py:367
  5.2 1.5 %collective-permute-start.1 = (bf16[32,1152]{1,0:T(8,128)(2,1)}, bf16[32,1152]{1,0:T(8,128)(2,1)S(1)}, u32[]{:S(2)}, u32[]{:S(2)}) collective-permute-start(bf16[32,1152]{1,0:T(8,128)(2,1)} %get-tuple-element.28), channel_id=1, source_target_pairs={{0,16},{8,24},{16,0},{24,8},{1,17},{9,25},{17,1},{25,9},{2,18},{10... | collective-permute-start | bytes 221192 | tf_op jit(solution)/shard_map/ppermute | solution.py:367
  6.7 0.0 collective-permute-start.2
  6.8 0.0 collective-permute-start.9
  6.8 1.5 %collective-permute-done.refs_1_ = bf16[32,1152]{1,0:T(8,128)(2,1)S(1)} collective-permute-done((bf16[32,1152]{1,0:T(8,128)(2,1)}, bf16[32,1152]{1,0:T(8,128)(2,1)S(1)}, u32[]{:S(2)}, u32[]{:S(2)}) %collective-permute-start) | collective-permute-done | bytes 73760 | tf_op jit(solution)/shard_map/ppermute | solution.py:367
  8.3 2.1 %collective-permute-start.8 = (bf16[64,1024]{1,0:T(8,128)(2,1)}, bf16[64,1024]{1,0:T(8,128)(2,1)S(1)}, u32[]{:S(2)}, u32[]{:S(2)}) collective-permute-start(bf16[64,1024]{1,0:T(8,128)(2,1)} %bitcast.3), channel_id=1, source_target_pairs={{0,2},{1,3},{2,0},{3,1},{4,6},{5,7},{6,4},{7,5},{8,10},{9,11},{10,... | collective-permute-start | bytes 393224 | tf_op jit(solution)/shard_map/ppermute | solution.py:386
  10.4 0.0 collective-permute-done.1.refs_2_
  10.4 1.5 %collective-permute-start.7 = (bf16[64,1024]{1,0:T(8,128)(2,1)}, bf16[64,1024]{1,0:T(8,128)(2,1)S(1)}, u32[]{:S(2)}, u32[]{:S(2)}) collective-permute-start(bf16[64,1024]{1,0:T(8,128)(2,1)} %bitcast.4), channel_id=1, source_target_pairs={{0,8},{1,2},{2,1},{3,4},{4,3},{5,6},{6,5},{7,15},{8,0},{9,10},{10,... | collective-permute-start | bytes 393224 | tf_op jit(solution)/shard_map/ppermute | solution.py:386
  11.9 0.3 %collective-permute-done.2.refs_3_ = bf16[32,1152]{1,0:T(8,128)(2,1)S(1)} collective-permute-done((bf16[32,1152]{1,0:T(8,128)(2,1)}, bf16[32,1152]{1,0:T(8,128)(2,1)S(1)}, u32[]{:S(2)}, u32[]{:S(2)}) %collective-permute-start.2) | collective-permute-done | bytes 73760 | tf_op jit(solution)/shard_map/ppermute | solution.py:367
  12.2 0.0 copy-start
  12.2 0.9 %copy-done = bf16[32,1152]{1,0:T(8,128)(2,1)S(1)} copy-done((bf16[32,1152]{1,0:T(8,128)(2,1)S(1)}, bf16[32,1152]{1,0:T(8,128)(2,1)}, u32[]{:S(2)}) %copy-start) | copy-done | bytes 73752
  13.1 0.0 copy-start.1
  13.1 0.0 copy-start.2
  13.1 0.1 shard_map.101
  13.2 0.1 collective-permute-start.3
  13.2 0.0 collective-permute-done.10.in_chip
  13.2 0.6 %collective-permute-start.4 = (bf16[80,1152]{1,0:T(8,128)(2,1)S(1)}, bf16[80,1152]{1,0:T(8,128)(2,1)S(1)}, u32[]{:S(2)}, u32[]{:S(2)}) collective-permute-start(bf16[80,1152]{1,0:T(8,128)(2,1)S(1)} %get-tuple-element.31), channel_id=1, source_target_pairs={{0,8},{1,2},{2,1},{3,4},{4,3},{5,6},{6,5},{7,15},{8,0},{9,10},{10,... | collective-permute-start | bytes 552968 | tf_op jit(solution)/shard_map/ppermute | solution.py:386
  13.8 0.0 collective-permute-done.9.far_odd
  13.8 1.5 %collective-permute-start.5 = (bf16[16,1152]{1,0:T(8,128)(2,1)S(1)}, bf16[16,1152]{1,0:T(8,128)(2,1)S(1)}, u32[]{:S(2)}, u32[]{:S(2)}) collective-permute-start(bf16[16,1152]{1,0:T(8,128)(2,1)S(1)} %get-tuple-element.32), channel_id=1, source_target_pairs={{0,2},{1,3},{2,0},{3,1},{4,6},{5,7},{6,4},{7,5},{8,10},{9,11},{10,... | collective-permute-start | bytes 110600 | tf_op jit(solution)/shard_map/ppermute | solution.py:386
  15.4 0.0 collective-permute-done.8.far_even
  15.4 0.9 %collective-permute-start.6 = (bf16[16,1152]{1,0:T(8,128)(2,1)S(1)}, bf16[16,1152]{1,0:T(8,128)(2,1)S(1)}, u32[]{:S(2)}, u32[]{:S(2)}) collective-permute-start(bf16[16,1152]{1,0:T(8,128)(2,1)S(1)} %get-tuple-element.33), channel_id=1, source_target_pairs={{0,1},{1,0},{2,4},{3,5},{4,2},{5,3},{6,7},{7,6},{8,9},{9,8},{10,12... | collective-permute-start | bytes 110600 | tf_op jit(solution)/shard_map/ppermute | solution.py:386
  16.3 0.0 collective-permute-done.7.cross
  16.3 0.0 copy-done.3
  16.3 0.0 copy-done.1
  16.3 0.0 copy-done.2
  16.3 0.0 copy-start.4
  16.3 1.2 %shard_map.102 = (f32[1024,256]{1,0:T(8,128)S(1)}, f32[2,128,1024]{2,1,0:T(8,128)S(1)}, f32[128,1024]{1,0:T(8,128)S(1)}, bf16[3,256,512]{2,1,0:T(8,128)(2,1)S(1)...) custom-call(bf16[4,32,1152]{2,1,0:T(8,128)(2,1)S(1)} %get-tuple-element.34.own, ...), custom_call_target="tpu_custom_call" | custom-call | flops 1000000000 | bytes 3000000 | tf_op jit(solution)/shard_map/pallas_call | solution.py:448
  17.5 2.1 %collective-permute-done.5.far_even = bf16[16,1152]{1,0:T(8,128)(2,1)S(1)} collective-permute-done((bf16[16,1152]{1,0:T(8,128)(2,1)S(1)}, bf16[16,1152]{1,0:T(8,128)(2,1)S(1)}, u32[]{:S(2)}, u32[]{:S(2)}) %collective-permute-start.5) | collective-permute-done | bytes 36896 | tf_op jit(solution)/shard_map/ppermute | solution.py:386
  19.7 0.0 collective-permute-done.6.far_odd
  19.7 0.0 collective-permute-done.3.in_chip
  19.7 0.0 collective-permute-done.4.cross
  19.7 0.0 copy-done.4
  19.7 2.5 %shard_map.103 = (bf16[2,32,1024]{2,1,0:T(8,128)(2,1)S(1)}, bf16[2,32,1024]{2,1,0:T(8,128)(2,1)S(1)}, bf16[2,32,1024]{2,1,0:T(8,128)(2,1)S(1)}, bf16[2,32,1024]{2,1,0:T(8,128)(2,1)S(1)}) custom-call(bf16[80,1152]{1,0:T(8,128)(2,1)S(1)} %collective-permute-done.3.in_chip, bf16[80,1152]{1,0:T(8,128)(2,1)S(1)} %collective-permute-done.4.cross, ...), custom_call_target="tpu_custom_call" | custom-call | flops 2000000000 | bytes 3000000 | tf_op jit(solution)/shard_map/pallas_call | solution.py:462
  22.2 0.8 %collective-permute-start.11 = (bf16[2,32,1024]{2,1,0:T(8,128)(2,1)S(1)}, bf16[2,32,1024]{2,1,0:T(8,128)(2,1)S(1)}, u32[]{:S(2)}, u32[]{:S(2)}) collective-permute-start(bf16[2,32,1024]{2,1,0:T(8,128)(2,1)S(1)} %get-tuple-element.44), channel_id=1, source_target_pairs={{0,8},{8,0},{16,24},{24,16},{1,9},{9,1},{17,25},{25,17},{2,10},{10... | collective-permute-start | bytes 393224 | tf_op jit(solution)/shard_map/ppermute | solution.py:367
  23.0 2.0 %collective-permute-start.12 = (bf16[2,32,1024]{2,1,0:T(8,128)(2,1)S(1)}, bf16[2,32,1024]{2,1,0:T(8,128)(2,1)S(1)}, u32[]{:S(2)}, u32[]{:S(2)}) collective-permute-start(bf16[2,32,1024]{2,1,0:T(8,128)(2,1)S(1)} %get-tuple-element.45), channel_id=1, source_target_pairs={{0,16},{8,24},{16,0},{24,8},{1,17},{9,25},{17,1},{25,9},{2,18},{10... | collective-permute-start | bytes 393224 | tf_op jit(solution)/shard_map/ppermute | solution.py:367
  25.0 0.8 %collective-permute-start.13 = (bf16[2,32,1024]{2,1,0:T(8,128)(2,1)S(1)}, bf16[2,32,1024]{2,1,0:T(8,128)(2,1)S(1)}, u32[]{:S(2)}, u32[]{:S(2)}) collective-permute-start(bf16[2,32,1024]{2,1,0:T(8,128)(2,1)S(1)} %get-tuple-element.46), channel_id=1, source_target_pairs={{0,24},{8,16},{16,8},{24,0},{1,25},{9,17},{17,9},{25,1},{2,26},{10... | collective-permute-start | bytes 393224 | tf_op jit(solution)/shard_map/ppermute | solution.py:367
  25.8 2.6 %collective-permute-done.11.refs_1_ = bf16[2,32,1024]{2,1,0:T(8,128)(2,1)S(1)} collective-permute-done((bf16[2,32,1024]{2,1,0:T(8,128)(2,1)S(1)}, bf16[2,32,1024]{2,1,0:T(8,128)(2,1)S(1)}, u32[]{:S(2)}, u32[]{:S(2)}) %collective-permute-start.11) | collective-permute-done | bytes 131104 | tf_op jit(solution)/shard_map/ppermute | solution.py:367
  28.4 1.4 %collective-permute-done.12.refs_2_ = bf16[2,32,1024]{2,1,0:T(8,128)(2,1)S(1)} collective-permute-done((bf16[2,32,1024]{2,1,0:T(8,128)(2,1)S(1)}, bf16[2,32,1024]{2,1,0:T(8,128)(2,1)S(1)}, u32[]{:S(2)}, u32[]{:S(2)}) %collective-permute-start.12) | collective-permute-done | bytes 131104 | tf_op jit(solution)/shard_map/ppermute | solution.py:367
  29.8 1.6 %collective-permute-done.13.refs_3_ = bf16[2,32,1024]{2,1,0:T(8,128)(2,1)S(1)} collective-permute-done((bf16[2,32,1024]{2,1,0:T(8,128)(2,1)S(1)}, bf16[2,32,1024]{2,1,0:T(8,128)(2,1)S(1)}, u32[]{:S(2)}, u32[]{:S(2)}) %collective-permute-start.13) | collective-permute-done | bytes 131104 | tf_op jit(solution)/shard_map/ppermute | solution.py:367
  31.5 0.8 %shard_map.104 = bf16[1,3,2,32,1024]{4,3,2,1,0:T(8,128)(2,1)} custom-call(bf16[2,32,1024]{2,1,0:T(8,128)(2,1)S(1)} %get-tuple-element.43.refs_0_, bf16[2,32,1024]{2,1,0:T(8,128)(2,1)S(1)} %collective-permute-done.11.refs_1_, bf16[2,32,1024]{2,1,0:T(8,128)(2,1)S(1)} %collective-permute-done.12.refs_2_, bf16[2,32,1024]{2,1,0:T(8,128)(2,1)S(1)} %collective-permute-done.13.refs_3_), custom_call_target="tpu_custom_call" | custom-call | bytes 1000000 | tf_op jit(solution)/shard_map/pallas_call | solution.py:471
Async XLA Ops:
  0.0 16.3 %copy-start.3 = (bf16[256,256]{1,0:T(8,128)(2,1)S(1)}, bf16[256,256]{1,0:T(8,128)(2,1)}, u32[]{:S(2)}) copy-start(bf16[256,256]{1,0:T(8,128)(2,1)} %constant.7.clone.left_tab) | copy-start | bytes 393220
  2.1 11.1 %collective-permute-start.10 = (bf16[64,1024]{1,0:T(8,128)(2,1)}, bf16[64,1024]{1,0:T(8,128)(2,1)S(1)}, u32[]{:S(2)}, u32[]{:S(2)}) collective-permute-start(bf16[64,1024]{1,0:T(8,128)(2,1)} %bitcast.1), channel_id=1, source_target_pairs={{0,1},{1,0},{2,3},{3,2},{4,5},{5,4},{6,7},{7,6},{8,9},{9,8},{10,11... | collective-permute-start | bytes 393224 | tf_op jit(solution)/shard_map/ppermute | solution.py:386
  2.6 5.6 %collective-permute-start = (bf16[32,1152]{1,0:T(8,128)(2,1)}, bf16[32,1152]{1,0:T(8,128)(2,1)S(1)}, u32[]{:S(2)}, u32[]{:S(2)}) collective-permute-start(bf16[32,1152]{1,0:T(8,128)(2,1)} %get-tuple-element.27), channel_id=1, source_target_pairs={{0,8},{8,0},{16,24},{24,16},{1,9},{9,1},{17,25},{25,17},{2,10},{10... | collective-permute-start | bytes 221192 | tf_op jit(solution)/shard_map/ppermute | solution.py:367
  5.2 5.2 %collective-permute-start.1 = (bf16[32,1152]{1,0:T(8,128)(2,1)}, bf16[32,1152]{1,0:T(8,128)(2,1)S(1)}, u32[]{:S(2)}, u32[]{:S(2)}) collective-permute-start(bf16[32,1152]{1,0:T(8,128)(2,1)} %get-tuple-element.28), channel_id=1, source_target_pairs={{0,16},{8,24},{16,0},{24,8},{1,17},{9,25},{17,1},{25,9},{2,18},{10... | collective-permute-start | bytes 221192 | tf_op jit(solution)/shard_map/ppermute | solution.py:367
  6.7 5.5 %collective-permute-start.2 = (bf16[32,1152]{1,0:T(8,128)(2,1)}, bf16[32,1152]{1,0:T(8,128)(2,1)S(1)}, u32[]{:S(2)}, u32[]{:S(2)}) collective-permute-start(bf16[32,1152]{1,0:T(8,128)(2,1)} %get-tuple-element.29), channel_id=1, source_target_pairs={{0,24},{8,16},{16,8},{24,0},{1,25},{9,17},{17,9},{25,1},{2,26},{10... | collective-permute-start | bytes 221192 | tf_op jit(solution)/shard_map/ppermute | solution.py:367
  6.8 7.1 %collective-permute-start.9 = (bf16[64,1024]{1,0:T(8,128)(2,1)}, bf16[64,1024]{1,0:T(8,128)(2,1)S(1)}, u32[]{:S(2)}, u32[]{:S(2)}) collective-permute-start(bf16[64,1024]{1,0:T(8,128)(2,1)} %bitcast.2), channel_id=1, source_target_pairs={{0,1},{1,0},{2,4},{3,5},{4,2},{5,3},{6,7},{7,6},{8,9},{9,8},{10,12... | collective-permute-start | bytes 393224 | tf_op jit(solution)/shard_map/ppermute | solution.py:386
  8.3 7.1 %collective-permute-start.8 = (bf16[64,1024]{1,0:T(8,128)(2,1)}, bf16[64,1024]{1,0:T(8,128)(2,1)S(1)}, u32[]{:S(2)}, u32[]{:S(2)}) collective-permute-start(bf16[64,1024]{1,0:T(8,128)(2,1)} %bitcast.3), channel_id=1, source_target_pairs={{0,2},{1,3},{2,0},{3,1},{4,6},{5,7},{6,4},{7,5},{8,10},{9,11},{10,... | collective-permute-start | bytes 393224 | tf_op jit(solution)/shard_map/ppermute | solution.py:386
  10.4 5.9 %collective-permute-start.7 = (bf16[64,1024]{1,0:T(8,128)(2,1)}, bf16[64,1024]{1,0:T(8,128)(2,1)S(1)}, u32[]{:S(2)}, u32[]{:S(2)}) collective-permute-start(bf16[64,1024]{1,0:T(8,128)(2,1)} %bitcast.4), channel_id=1, source_target_pairs={{0,8},{1,2},{2,1},{3,4},{4,3},{5,6},{6,5},{7,15},{8,0},{9,10},{10,... | collective-permute-start | bytes 393224 | tf_op jit(solution)/shard_map/ppermute | solution.py:386
  12.2 0.9 %copy-start = (bf16[32,1152]{1,0:T(8,128)(2,1)S(1)}, bf16[32,1152]{1,0:T(8,128)(2,1)}, u32[]{:S(2)}) copy-start(bf16[32,1152]{1,0:T(8,128)(2,1)} %get-tuple-element.26.refs_0_) | copy-start | bytes 221188
  13.1 3.2 %copy-start.1 = (bf16[2,32,1024]{2,1,0:T(8,128)(2,1)S(1)}, bf16[2,32,1024]{2,1,0:T(8,128)(2,1)}, u32[]{:S(2)}) copy-start(bf16[2,32,1024]{2,1,0:T(8,128)(2,1)} %get-tuple-element.35) | copy-start | bytes 393220
  13.1 3.2 %copy-start.2 = (bf16[256,256]{1,0:T(8,128)(2,1)S(1)}, bf16[256,256]{1,0:T(8,128)(2,1)}, u32[]{:S(2)}) copy-start(bf16[256,256]{1,0:T(8,128)(2,1)} %constant.6.clone.right_tab) | copy-start | bytes 393220
  13.2 6.5 %collective-permute-start.3 = (bf16[80,1152]{1,0:T(8,128)(2,1)S(1)}, bf16[80,1152]{1,0:T(8,128)(2,1)S(1)}, u32[]{:S(2)}, u32[]{:S(2)}) collective-permute-start(bf16[80,1152]{1,0:T(8,128)(2,1)S(1)} %get-tuple-element.30), channel_id=1, source_target_pairs={{0,1},{1,0},{2,3},{3,2},{4,5},{5,4},{6,7},{7,6},{8,9},{9,8},{10,11... | collective-permute-start | bytes 552968 | tf_op jit(solution)/shard_map/ppermute | solution.py:386
  13.2 6.4 %collective-permute-start.4 = (bf16[80,1152]{1,0:T(8,128)(2,1)S(1)}, bf16[80,1152]{1,0:T(8,128)(2,1)S(1)}, u32[]{:S(2)}, u32[]{:S(2)}) collective-permute-start(bf16[80,1152]{1,0:T(8,128)(2,1)S(1)} %get-tuple-element.31), channel_id=1, source_target_pairs={{0,8},{1,2},{2,1},{3,4},{4,3},{5,6},{6,5},{7,15},{8,0},{9,10},{10,... | collective-permute-start | bytes 552968 | tf_op jit(solution)/shard_map/ppermute | solution.py:386
  13.8 5.8 %collective-permute-start.5 = (bf16[16,1152]{1,0:T(8,128)(2,1)S(1)}, bf16[16,1152]{1,0:T(8,128)(2,1)S(1)}, u32[]{:S(2)}, u32[]{:S(2)}) collective-permute-start(bf16[16,1152]{1,0:T(8,128)(2,1)S(1)} %get-tuple-element.32), channel_id=1, source_target_pairs={{0,2},{1,3},{2,0},{3,1},{4,6},{5,7},{6,4},{7,5},{8,10},{9,11},{10,... | collective-permute-start | bytes 110600 | tf_op jit(solution)/shard_map/ppermute | solution.py:386
  15.4 4.3 %collective-permute-start.6 = (bf16[16,1152]{1,0:T(8,128)(2,1)S(1)}, bf16[16,1152]{1,0:T(8,128)(2,1)S(1)}, u32[]{:S(2)}, u32[]{:S(2)}) collective-permute-start(bf16[16,1152]{1,0:T(8,128)(2,1)S(1)} %get-tuple-element.33), channel_id=1, source_target_pairs={{0,1},{1,0},{2,4},{3,5},{4,2},{5,3},{6,7},{7,6},{8,9},{9,8},{10,12... | collective-permute-start | bytes 110600 | tf_op jit(solution)/shard_map/ppermute | solution.py:386
  16.3 3.4 %copy-start.4 = (bf16[192,192]{1,0:T(8,128)(2,1)S(1)}, bf16[192,192]{1,0:T(8,128)(2,1)}, u32[]{:S(2)}) copy-start(bf16[192,192]{1,0:T(8,128)(2,1)} %constant.8.clone.left_tab) | copy-start | bytes 221188
  22.2 6.2 %collective-permute-start.11 = (bf16[2,32,1024]{2,1,0:T(8,128)(2,1)S(1)}, bf16[2,32,1024]{2,1,0:T(8,128)(2,1)S(1)}, u32[]{:S(2)}, u32[]{:S(2)}) collective-permute-start(bf16[2,32,1024]{2,1,0:T(8,128)(2,1)S(1)} %get-tuple-element.44), channel_id=1, source_target_pairs={{0,8},{8,0},{16,24},{24,16},{1,9},{9,1},{17,25},{25,17},{2,10},{10... | collective-permute-start | bytes 393224 | tf_op jit(solution)/shard_map/ppermute | solution.py:367
  23.0 6.8 %collective-permute-start.12 = (bf16[2,32,1024]{2,1,0:T(8,128)(2,1)S(1)}, bf16[2,32,1024]{2,1,0:T(8,128)(2,1)S(1)}, u32[]{:S(2)}, u32[]{:S(2)}) collective-permute-start(bf16[2,32,1024]{2,1,0:T(8,128)(2,1)S(1)} %get-tuple-element.45), channel_id=1, source_target_pairs={{0,16},{8,24},{16,0},{24,8},{1,17},{9,25},{17,1},{25,9},{2,18},{10... | collective-permute-start | bytes 393224 | tf_op jit(solution)/shard_map/ppermute | solution.py:367
  25.0 6.5 %collective-permute-start.13 = (bf16[2,32,1024]{2,1,0:T(8,128)(2,1)S(1)}, bf16[2,32,1024]{2,1,0:T(8,128)(2,1)S(1)}, u32[]{:S(2)}, u32[]{:S(2)}) collective-permute-start(bf16[2,32,1024]{2,1,0:T(8,128)(2,1)S(1)} %get-tuple-element.46), channel_id=1, source_target_pairs={{0,24},{8,16},{16,8},{24,0},{1,25},{9,17},{17,9},{25,1},{2,26},{10... | collective-permute-start | bytes 393224 | tf_op jit(solution)/shard_map/ppermute | solution.py:367

commit v23 on v22

--- a/solution.py
+++ b/solution.py
@@ -257,7 +257,7 @@
 
 
 def prepare_kernel(
-    own, incident, cross, far_even, far_odd, in_chip, left_tab, right_tab,
+    own, incident, far_odd, far_even, cross, in_chip, left_tab, right_tab,
     first, stereo, clear, col_mats, *row_mats
 ):
     low_near, high_near, low_far, high_far = ordered(in_chip, cross, far_even, far_odd)
@@ -388,9 +388,9 @@
 
 def neighbours(sent):
     in_chip, cross, far_even, far_odd = sent
+    far_odd = exchanged(far_odd, 2, 1)
+    far_even = exchanged(far_even, 2, 0)
     cross = exchanged(cross, 1, 1)
-    far_even = exchanged(far_even, 2, 0)
-    far_odd = exchanged(far_odd, 2, 1)
     in_chip = exchanged(in_chip, 1, 0)
     return in_chip, cross, far_even, far_odd
 
@@ -435,7 +435,7 @@
     )(hogel_light, silhouette, fill_counts, hogel_index, row_taps, col_taps, incident)
     mine = mine.reshape(2 * BAND, COLS)
     layers_in = messages[:1] + [over_depth(messages[hop], hop) for hop in range(1, LAYERS)]
-    in_chip, *arrived = neighbours((mine,) * 4)
+    arrived = neighbours((mine,) * 4)[::-1]
     near = shaped((NEAR, HALO_W), bf16)
     far = shaped((FAR, HALO_W), bf16)
     own, *sent = call(
@@ -457,7 +457,7 @@
         [vmem] * 8,
         flops=10**9,
         moved=3 * 10**6,
-    )(own, mine, *arrived, in_chip, jnp.asarray(left_table(LANES)), right_tab)
+    )(own, mine, *arrived, jnp.asarray(left_table(LANES)), right_tab)
     halo_rows = NEAR + FAR
     results = call(
         chain_kernel,

time: 32.4 us -> 32.1 us (level)
  transfers between devices with their start and end apart: 14 -> 14, of which waited for: 6 -> 5; matrix products, arithmetic and copies ran while one was open for 0% -> 0% of each run, Pallas kernels for 4% -> 4%
where the time goes in v23:
time: 32.1 us; the launch traced here: 31.9 us
  starting transfers between devices  14.7 us (46%)
  waiting for transfers between devices  9.49 us (30%)
  Pallas kernels  6.67 us (21%)
  local copies, waits for them, and re-layouts  0.9 us (3%)
    ppermute x6, starting transfers between devices, over_depth(): return lax.ppermute(value, 'depth', [(i, i ^ hop) for i in range(LAYERS)])  7.67 us
    ppermute x6, waiting for transfers between devices, over_depth(): return lax.ppermute(value, 'depth', [(i, i ^ hop) for i in range(LAYERS)])  7.34 us
    ppermute x8, starting transfers between devices, exchanged(): return lax.ppermute(value, ('depth', 'rows'), pairs)  7.07 us
    pallas_call x1, Pallas kernels, body(): call(chain_kernel, [shaped((2, BAND, COLS), bf16)] * LAYERS, [vmem] * (6...  2.52 us
    ppermute x8, waiting for transfers between devices, exchanged(): return lax.ppermute(value, ('depth', 'rows'), pairs)  2.15 us
    pallas_call x1, Pallas kernels, body(): call(pack_kernel, (shaped((BAND, HALO_W), bf16),) * LAYERS + (shaped(inci...  2.12 us
    pallas_call x1, Pallas kernels, body(): call(prepare_kernel, [shaped((TILES * layer_height(0), 2 * LANES), f32),...  1.2 us
    unnamed x10, local copies, waits for them, and re-layouts  0.9 us
  transfers between devices with their start and end apart: 14, of which 5 were waited for; matrix products, arithmetic and copies ran while one was open for 0% of the time, Pallas kernels for 4%

profile of v23, /device:TPU:0, one launch (start us, length us, event | category | flops | bytes accessed | tf_op | source)
XLA Modules:
  0.0 31.9 jit_solution(3225847131379946014)
XLA Ops:
  0.0 0.0 copy-start.3
  0.0 2.1 %shard_map.100 = (bf16[32,1152]{1,0:T(8,128)(2,1)}, bf16[32,1152]{1,0:T(8,128)(2,1)}, bf16[32,1152]{1,0:T(8,128)(2,1)}, bf16[32,1152]{1,0:T(8,128)(2,1)}, bf16[2,32,1024]{2,1,0:T(8,128)(2,1)}) custom-call(f32[1,3,32,1024]{3,2,1,0:T(8,128)} %light.1, s32[1,32,64]{2,1,0:T(8,128)} %edges.1, s32[1,2]{1,0:T(1,128)} %counts.1, s32[1,2,64]{2,1,0:T(2,128)} %listed.1, ...), custom_call_target="tpu_custom_call" | custom-call | flops 10000000 | bytes 1000000 | tf_op jit(solution)/shard_map/pallas_call | solution.py:428
  2.1 0.5 %collective-permute-start.10 = (bf16[64,1024]{1,0:T(8,128)(2,1)}, bf16[64,1024]{1,0:T(8,128)(2,1)S(1)}, u32[]{:S(2)}, u32[]{:S(2)}) collective-permute-start(bf16[64,1024]{1,0:T(8,128)(2,1)} %bitcast.1), channel_id=1, source_target_pairs={{0,1},{1,0},{2,3},{3,2},{4,5},{5,4},{6,7},{7,6},{8,9},{9,8},{10,11... | collective-permute-start | bytes 393224 | tf_op jit(solution)/shard_map/ppermute | solution.py:386
  2.6 2.6 %collective-permute-start = (bf16[32,1152]{1,0:T(8,128)(2,1)}, bf16[32,1152]{1,0:T(8,128)(2,1)S(1)}, u32[]{:S(2)}, u32[]{:S(2)}) collective-permute-start(bf16[32,1152]{1,0:T(8,128)(2,1)} %get-tuple-element.27), channel_id=1, source_target_pairs={{0,8},{8,0},{16,24},{24,16},{1,9},{9,1},{17,25},{25,17},{2,10},{10... | collective-permute-start | bytes 221192 | tf_op jit(solution)/shard_map/ppermute | solution.py:367
  5.2 1.5 %collective-permute-start.1 = (bf16[32,1152]{1,0:T(8,128)(2,1)}, bf16[32,1152]{1,0:T(8,128)(2,1)S(1)}, u32[]{:S(2)}, u32[]{:S(2)}) collective-permute-start(bf16[32,1152]{1,0:T(8,128)(2,1)} %get-tuple-element.28), channel_id=1, source_target_pairs={{0,16},{8,24},{16,0},{24,8},{1,17},{9,25},{17,1},{25,9},{2,18},{10... | collective-permute-start | bytes 221192 | tf_op jit(solution)/shard_map/ppermute | solution.py:367
  6.7 0.0 collective-permute-start.2
  6.8 1.9 %collective-permute-start.9 = (bf16[64,1024]{1,0:T(8,128)(2,1)}, bf16[64,1024]{1,0:T(8,128)(2,1)S(1)}, u32[]{:S(2)}, u32[]{:S(2)}) collective-permute-start(bf16[64,1024]{1,0:T(8,128)(2,1)} %bitcast.2), channel_id=1, source_target_pairs={{0,8},{1,2},{2,1},{3,4},{4,3},{5,6},{6,5},{7,15},{8,0},{9,10},{10,... | collective-permute-start | bytes 393224 | tf_op jit(solution)/shard_map/ppermute | solution.py:386
  8.7 0.0 collective-permute-done.refs_1_
  8.7 1.4 %collective-permute-start.8 = (bf16[64,1024]{1,0:T(8,128)(2,1)}, bf16[64,1024]{1,0:T(8,128)(2,1)S(1)}, u32[]{:S(2)}, u32[]{:S(2)}) collective-permute-start(bf16[64,1024]{1,0:T(8,128)(2,1)} %bitcast.3), channel_id=1, source_target_pairs={{0,2},{1,3},{2,0},{3,1},{4,6},{5,7},{6,4},{7,5},{8,10},{9,11},{10,... | collective-permute-start | bytes 393224 | tf_op jit(solution)/shard_map/ppermute | solution.py:386
  10.1 0.0 collective-permute-done.1.refs_2_
  10.1 0.1 collective-permute-start.7
  10.2 2.0 %collective-permute-done.2.refs_3_ = bf16[32,1152]{1,0:T(8,128)(2,1)S(1)} collective-permute-done((bf16[32,1152]{1,0:T(8,128)(2,1)}, bf16[32,1152]{1,0:T(8,128)(2,1)S(1)}, u32[]{:S(2)}, u32[]{:S(2)}) %collective-permute-start.2) | collective-permute-done | bytes 73760 | tf_op jit(solution)/shard_map/ppermute | solution.py:367
  12.2 0.0 copy-start
  12.2 0.9 %copy-done = bf16[32,1152]{1,0:T(8,128)(2,1)S(1)} copy-done((bf16[32,1152]{1,0:T(8,128)(2,1)S(1)}, bf16[32,1152]{1,0:T(8,128)(2,1)}, u32[]{:S(2)}) %copy-start) | copy-done | bytes 73752
  13.1 0.0 copy-start.1
  13.1 0.0 copy-start.2
  13.1 0.1 shard_map.101
  13.2 0.1 collective-permute-start.3
  13.2 0.0 collective-permute-done.10.in_chip
  13.2 0.6 %collective-permute-start.4 = (bf16[80,1152]{1,0:T(8,128)(2,1)S(1)}, bf16[80,1152]{1,0:T(8,128)(2,1)S(1)}, u32[]{:S(2)}, u32[]{:S(2)}) collective-permute-start(bf16[80,1152]{1,0:T(8,128)(2,1)S(1)} %get-tuple-element.31), channel_id=1, source_target_pairs={{0,8},{1,2},{2,1},{3,4},{4,3},{5,6},{6,5},{7,15},{8,0},{9,10},{10,... | collective-permute-start | bytes 552968 | tf_op jit(solution)/shard_map/ppermute | solution.py:386
  13.8 0.0 collective-permute-done.9.cross
  13.8 1.5 %collective-permute-start.5 = (bf16[16,1152]{1,0:T(8,128)(2,1)S(1)}, bf16[16,1152]{1,0:T(8,128)(2,1)S(1)}, u32[]{:S(2)}, u32[]{:S(2)}) collective-permute-start(bf16[16,1152]{1,0:T(8,128)(2,1)S(1)} %get-tuple-element.32), channel_id=1, source_target_pairs={{0,2},{1,3},{2,0},{3,1},{4,6},{5,7},{6,4},{7,5},{8,10},{9,11},{10,... | collective-permute-start | bytes 110600 | tf_op jit(solution)/shard_map/ppermute | solution.py:386
  15.4 0.0 collective-permute-done.8.far_even
  15.4 0.9 %collective-permute-start.6 = (bf16[16,1152]{1,0:T(8,128)(2,1)S(1)}, bf16[16,1152]{1,0:T(8,128)(2,1)S(1)}, u32[]{:S(2)}, u32[]{:S(2)}) collective-permute-start(bf16[16,1152]{1,0:T(8,128)(2,1)S(1)} %get-tuple-element.33), channel_id=1, source_target_pairs={{0,1},{1,0},{2,4},{3,5},{4,2},{5,3},{6,7},{7,6},{8,9},{9,8},{10,12... | collective-permute-start | bytes 110600 | tf_op jit(solution)/shard_map/ppermute | solution.py:386
  16.3 0.0 collective-permute-done.7.far_odd
  16.3 0.0 copy-done.3
  16.3 0.0 copy-done.1
  16.3 0.0 copy-done.2
  16.3 0.0 copy-start.4
  16.3 1.2 %shard_map.102 = (f32[1024,256]{1,0:T(8,128)S(1)}, f32[2,128,1024]{2,1,0:T(8,128)S(1)}, f32[128,1024]{1,0:T(8,128)S(1)}, bf16[3,256,512]{2,1,0:T(8,128)(2,1)S(1)...) custom-call(bf16[4,32,1152]{2,1,0:T(8,128)(2,1)S(1)} %get-tuple-element.34.own, ...), custom_call_target="tpu_custom_call" | custom-call | flops 1000000000 | bytes 3000000 | tf_op jit(solution)/shard_map/pallas_call | solution.py:448
  17.5 2.1 %collective-permute-done.5.far_even = bf16[16,1152]{1,0:T(8,128)(2,1)S(1)} collective-permute-done((bf16[16,1152]{1,0:T(8,128)(2,1)S(1)}, bf16[16,1152]{1,0:T(8,128)(2,1)S(1)}, u32[]{:S(2)}, u32[]{:S(2)}) %collective-permute-start.5) | collective-permute-done | bytes 36896 | tf_op jit(solution)/shard_map/ppermute | solution.py:386
  19.7 0.0 collective-permute-done.6.far_odd
  19.7 0.0 collective-permute-done.3.in_chip
  19.7 0.0 collective-permute-done.4.cross
  19.7 0.0 copy-done.4
  19.7 2.5 %shard_map.103 = (bf16[2,32,1024]{2,1,0:T(8,128)(2,1)S(1)}, bf16[2,32,1024]{2,1,0:T(8,128)(2,1)S(1)}, bf16[2,32,1024]{2,1,0:T(8,128)(2,1)S(1)}, bf16[2,32,1024]{2,1,0:T(8,128)(2,1)S(1)}) custom-call(bf16[80,1152]{1,0:T(8,128)(2,1)S(1)} %collective-permute-done.3.in_chip, bf16[80,1152]{1,0:T(8,128)(2,1)S(1)} %collective-permute-done.4.cross, ...), custom_call_target="tpu_custom_call" | custom-call | flops 2000000000 | bytes 3000000 | tf_op jit(solution)/shard_map/pallas_call | solution.py:462
  22.2 0.8 %collective-permute-start.11 = (bf16[2,32,1024]{2,1,0:T(8,128)(2,1)S(1)}, bf16[2,32,1024]{2,1,0:T(8,128)(2,1)S(1)}, u32[]{:S(2)}, u32[]{:S(2)}) collective-permute-start(bf16[2,32,1024]{2,1,0:T(8,128)(2,1)S(1)} %get-tuple-element.44), channel_id=1, source_target_pairs={{0,8},{8,0},{16,24},{24,16},{1,9},{9,1},{17,25},{25,17},{2,10},{10... | collective-permute-start | bytes 393224 | tf_op jit(solution)/shard_map/ppermute | solution.py:367
  23.0 1.6 %collective-permute-start.12 = (bf16[2,32,1024]{2,1,0:T(8,128)(2,1)S(1)}, bf16[2,32,1024]{2,1,0:T(8,128)(2,1)S(1)}, u32[]{:S(2)}, u32[]{:S(2)}) collective-permute-start(bf16[2,32,1024]{2,1,0:T(8,128)(2,1)S(1)} %get-tuple-element.45), channel_id=1, source_target_pairs={{0,16},{8,24},{16,0},{24,8},{1,17},{9,25},{17,1},{25,9},{2,18},{10... | collective-permute-start | bytes 393224 | tf_op jit(solution)/shard_map/ppermute | solution.py:367
  24.6 1.2 %collective-permute-start.13 = (bf16[2,32,1024]{2,1,0:T(8,128)(2,1)S(1)}, bf16[2,32,1024]{2,1,0:T(8,128)(2,1)S(1)}, u32[]{:S(2)}, u32[]{:S(2)}) collective-permute-start(bf16[2,32,1024]{2,1,0:T(8,128)(2,1)S(1)} %get-tuple-element.46), channel_id=1, source_target_pairs={{0,24},{8,16},{16,8},{24,0},{1,25},{9,17},{17,9},{25,1},{2,26},{10... | collective-permute-start | bytes 393224 | tf_op jit(solution)/shard_map/ppermute | solution.py:367
  25.8 2.9 %collective-permute-done.11.refs_1_ = bf16[2,32,1024]{2,1,0:T(8,128)(2,1)S(1)} collective-permute-done((bf16[2,32,1024]{2,1,0:T(8,128)(2,1)S(1)}, bf16[2,32,1024]{2,1,0:T(8,128)(2,1)S(1)}, u32[]{:S(2)}, u32[]{:S(2)}) %collective-permute-start.11) | collective-permute-done | bytes 131104 | tf_op jit(solution)/shard_map/ppermute | solution.py:367
  28.6 0.8 %collective-permute-done.12.refs_2_ = bf16[2,32,1024]{2,1,0:T(8,128)(2,1)S(1)} collective-permute-done((bf16[2,32,1024]{2,1,0:T(8,128)(2,1)S(1)}, bf16[2,32,1024]{2,1,0:T(8,128)(2,1)S(1)}, u32[]{:S(2)}, u32[]{:S(2)}) %collective-permute-start.12) | collective-permute-done | bytes 131104 | tf_op jit(solution)/shard_map/ppermute | solution.py:367
  29.5 1.6 %collective-permute-done.13.refs_3_ = bf16[2,32,1024]{2,1,0:T(8,128)(2,1)S(1)} collective-permute-done((bf16[2,32,1024]{2,1,0:T(8,128)(2,1)S(1)}, bf16[2,32,1024]{2,1,0:T(8,128)(2,1)S(1)}, u32[]{:S(2)}, u32[]{:S(2)}) %collective-permute-start.13) | collective-permute-done | bytes 131104 | tf_op jit(solution)/shard_map/ppermute | solution.py:367
  31.1 0.8 %shard_map.104 = bf16[1,3,2,32,1024]{4,3,2,1,0:T(8,128)(2,1)} custom-call(bf16[2,32,1024]{2,1,0:T(8,128)(2,1)S(1)} %get-tuple-element.43.refs_0_, bf16[2,32,1024]{2,1,0:T(8,128)(2,1)S(1)} %collective-permute-done.11.refs_1_, bf16[2,32,1024]{2,1,0:T(8,128)(2,1)S(1)} %collective-permute-done.12.refs_2_, bf16[2,32,1024]{2,1,0:T(8,128)(2,1)S(1)} %collective-permute-done.13.refs_3_), custom_call_target="tpu_custom_call" | custom-call | bytes 1000000 | tf_op jit(solution)/shard_map/pallas_call | solution.py:471
Async XLA Ops:
  0.0 16.3 %copy-start.3 = (bf16[256,256]{1,0:T(8,128)(2,1)S(1)}, bf16[256,256]{1,0:T(8,128)(2,1)}, u32[]{:S(2)}) copy-start(bf16[256,256]{1,0:T(8,128)(2,1)} %constant.7.clone.left_tab) | copy-start | bytes 393220
  2.1 11.1 %collective-permute-start.10 = (bf16[64,1024]{1,0:T(8,128)(2,1)}, bf16[64,1024]{1,0:T(8,128)(2,1)S(1)}, u32[]{:S(2)}, u32[]{:S(2)}) collective-permute-start(bf16[64,1024]{1,0:T(8,128)(2,1)} %bitcast.1), channel_id=1, source_target_pairs={{0,1},{1,0},{2,3},{3,2},{4,5},{5,4},{6,7},{7,6},{8,9},{9,8},{10,11... | collective-permute-start | bytes 393224 | tf_op jit(solution)/shard_map/ppermute | solution.py:386
  2.6 6.1 %collective-permute-start = (bf16[32,1152]{1,0:T(8,128)(2,1)}, bf16[32,1152]{1,0:T(8,128)(2,1)S(1)}, u32[]{:S(2)}, u32[]{:S(2)}) collective-permute-start(bf16[32,1152]{1,0:T(8,128)(2,1)} %get-tuple-element.27), channel_id=1, source_target_pairs={{0,8},{8,0},{16,24},{24,16},{1,9},{9,1},{17,25},{25,17},{2,10},{10... | collective-permute-start | bytes 221192 | tf_op jit(solution)/shard_map/ppermute | solution.py:367
  5.2 4.9 %collective-permute-start.1 = (bf16[32,1152]{1,0:T(8,128)(2,1)}, bf16[32,1152]{1,0:T(8,128)(2,1)S(1)}, u32[]{:S(2)}, u32[]{:S(2)}) collective-permute-start(bf16[32,1152]{1,0:T(8,128)(2,1)} %get-tuple-element.28), channel_id=1, source_target_pairs={{0,16},{8,24},{16,0},{24,8},{1,17},{9,25},{17,1},{25,9},{2,18},{10... | collective-permute-start | bytes 221192 | tf_op jit(solution)/shard_map/ppermute | solution.py:367
  6.7 5.5 %collective-permute-start.2 = (bf16[32,1152]{1,0:T(8,128)(2,1)}, bf16[32,1152]{1,0:T(8,128)(2,1)S(1)}, u32[]{:S(2)}, u32[]{:S(2)}) collective-permute-start(bf16[32,1152]{1,0:T(8,128)(2,1)} %get-tuple-element.29), channel_id=1, source_target_pairs={{0,24},{8,16},{16,8},{24,0},{1,25},{9,17},{17,9},{25,1},{2,26},{10... | collective-permute-start | bytes 221192 | tf_op jit(solution)/shard_map/ppermute | solution.py:367
  6.8 7.1 %collective-permute-start.9 = (bf16[64,1024]{1,0:T(8,128)(2,1)}, bf16[64,1024]{1,0:T(8,128)(2,1)S(1)}, u32[]{:S(2)}, u32[]{:S(2)}) collective-permute-start(bf16[64,1024]{1,0:T(8,128)(2,1)} %bitcast.2), channel_id=1, source_target_pairs={{0,8},{1,2},{2,1},{3,4},{4,3},{5,6},{6,5},{7,15},{8,0},{9,10},{10,... | collective-permute-start | bytes 393224 | tf_op jit(solution)/shard_map/ppermute | solution.py:386
  8.7 6.7 %collective-permute-start.8 = (bf16[64,1024]{1,0:T(8,128)(2,1)}, bf16[64,1024]{1,0:T(8,128)(2,1)S(1)}, u32[]{:S(2)}, u32[]{:S(2)}) collective-permute-start(bf16[64,1024]{1,0:T(8,128)(2,1)} %bitcast.3), channel_id=1, source_target_pairs={{0,2},{1,3},{2,0},{3,1},{4,6},{5,7},{6,4},{7,5},{8,10},{9,11},{10,... | collective-permute-start | bytes 393224 | tf_op jit(solution)/shard_map/ppermute | solution.py:386
  10.1 6.2 %collective-permute-start.7 = (bf16[64,1024]{1,0:T(8,128)(2,1)}, bf16[64,1024]{1,0:T(8,128)(2,1)S(1)}, u32[]{:S(2)}, u32[]{:S(2)}) collective-permute-start(bf16[64,1024]{1,0:T(8,128)(2,1)} %bitcast.4), channel_id=1, source_target_pairs={{0,1},{1,0},{2,4},{3,5},{4,2},{5,3},{6,7},{7,6},{8,9},{9,8},{10,12... | collective-permute-start | bytes 393224 | tf_op jit(solution)/shard_map/ppermute | solution.py:386
  12.2 0.9 %copy-start = (bf16[32,1152]{1,0:T(8,128)(2,1)S(1)}, bf16[32,1152]{1,0:T(8,128)(2,1)}, u32[]{:S(2)}) copy-start(bf16[32,1152]{1,0:T(8,128)(2,1)} %get-tuple-element.26.refs_0_) | copy-start | bytes 221188
  13.1 3.2 %copy-start.1 = (bf16[2,32,1024]{2,1,0:T(8,128)(2,1)S(1)}, bf16[2,32,1024]{2,1,0:T(8,128)(2,1)}, u32[]{:S(2)}) copy-start(bf16[2,32,1024]{2,1,0:T(8,128)(2,1)} %get-tuple-element.35) | copy-start | bytes 393220
  13.1 3.2 %copy-start.2 = (bf16[256,256]{1,0:T(8,128)(2,1)S(1)}, bf16[256,256]{1,0:T(8,128)(2,1)}, u32[]{:S(2)}) copy-start(bf16[256,256]{1,0:T(8,128)(2,1)} %constant.6.clone.right_tab) | copy-start | bytes 393220
  13.2 6.5 %collective-permute-start.3 = (bf16[80,1152]{1,0:T(8,128)(2,1)S(1)}, bf16[80,1152]{1,0:T(8,128)(2,1)S(1)}, u32[]{:S(2)}, u32[]{:S(2)}) collective-permute-start(bf16[80,1152]{1,0:T(8,128)(2,1)S(1)} %get-tuple-element.30), channel_id=1, source_target_pairs={{0,1},{1,0},{2,3},{3,2},{4,5},{5,4},{6,7},{7,6},{8,9},{9,8},{10,11... | collective-permute-start | bytes 552968 | tf_op jit(solution)/shard_map/ppermute | solution.py:386
  13.2 6.4 %collective-permute-start.4 = (bf16[80,1152]{1,0:T(8,128)(2,1)S(1)}, bf16[80,1152]{1,0:T(8,128)(2,1)S(1)}, u32[]{:S(2)}, u32[]{:S(2)}) collective-permute-start(bf16[80,1152]{1,0:T(8,128)(2,1)S(1)} %get-tuple-element.31), channel_id=1, source_target_pairs={{0,8},{1,2},{2,1},{3,4},{4,3},{5,6},{6,5},{7,15},{8,0},{9,10},{10,... | collective-permute-start | bytes 552968 | tf_op jit(solution)/shard_map/ppermute | solution.py:386
  13.8 5.8 %collective-permute-start.5 = (bf16[16,1152]{1,0:T(8,128)(2,1)S(1)}, bf16[16,1152]{1,0:T(8,128)(2,1)S(1)}, u32[]{:S(2)}, u32[]{:S(2)}) collective-permute-start(bf16[16,1152]{1,0:T(8,128)(2,1)S(1)} %get-tuple-element.32), channel_id=1, source_target_pairs={{0,2},{1,3},{2,0},{3,1},{4,6},{5,7},{6,4},{7,5},{8,10},{9,11},{10,... | collective-permute-start | bytes 110600 | tf_op jit(solution)/shard_map/ppermute | solution.py:386
  15.4 4.3 %collective-permute-start.6 = (bf16[16,1152]{1,0:T(8,128)(2,1)S(1)}, bf16[16,1152]{1,0:T(8,128)(2,1)S(1)}, u32[]{:S(2)}, u32[]{:S(2)}) collective-permute-start(bf16[16,1152]{1,0:T(8,128)(2,1)S(1)} %get-tuple-element.33), channel_id=1, source_target_pairs={{0,1},{1,0},{2,4},{3,5},{4,2},{5,3},{6,7},{7,6},{8,9},{9,8},{10,12... | collective-permute-start | bytes 110600 | tf_op jit(solution)/shard_map/ppermute | solution.py:386
  16.3 3.4 %copy-start.4 = (bf16[192,192]{1,0:T(8,128)(2,1)S(1)}, bf16[192,192]{1,0:T(8,128)(2,1)}, u32[]{:S(2)}) copy-start(bf16[192,192]{1,0:T(8,128)(2,1)} %constant.8.clone.left_tab) | copy-start | bytes 221188
  22.2 6.4 %collective-permute-start.11 = (bf16[2,32,1024]{2,1,0:T(8,128)(2,1)S(1)}, bf16[2,32,1024]{2,1,0:T(8,128)(2,1)S(1)}, u32[]{:S(2)}, u32[]{:S(2)}) collective-permute-start(bf16[2,32,1024]{2,1,0:T(8,128)(2,1)S(1)} %get-tuple-element.44), channel_id=1, source_target_pairs={{0,8},{8,0},{16,24},{24,16},{1,9},{9,1},{17,25},{25,17},{2,10},{10... | collective-permute-start | bytes 393224 | tf_op jit(solution)/shard_map/ppermute | solution.py:367
  23.0 6.5 %collective-permute-start.12 = (bf16[2,32,1024]{2,1,0:T(8,128)(2,1)S(1)}, bf16[2,32,1024]{2,1,0:T(8,128)(2,1)S(1)}, u32[]{:S(2)}, u32[]{:S(2)}) collective-permute-start(bf16[2,32,1024]{2,1,0:T(8,128)(2,1)S(1)} %get-tuple-element.45), channel_id=1, source_target_pairs={{0,16},{8,24},{16,0},{24,8},{1,17},{9,25},{17,1},{25,9},{2,18},{10... | collective-permute-start | bytes 393224 | tf_op jit(solution)/shard_map/ppermute | solution.py:367
  24.6 6.5 %collective-permute-start.13 = (bf16[2,32,1024]{2,1,0:T(8,128)(2,1)S(1)}, bf16[2,32,1024]{2,1,0:T(8,128)(2,1)S(1)}, u32[]{:S(2)}, u32[]{:S(2)}) collective-permute-start(bf16[2,32,1024]{2,1,0:T(8,128)(2,1)S(1)} %get-tuple-element.46), channel_id=1, source_target_pairs={{0,24},{8,16},{16,8},{24,0},{1,25},{9,17},{17,9},{25,1},{2,26},{10... | collective-permute-start | bytes 393224 | tf_op jit(solution)/shard_map/ppermute | solution.py:367

commit v24 on v23

--- a/solution.py
+++ b/solution.py
@@ -123,6 +123,10 @@
     for colour, out in zip(colours, outs):
         out[:, :COLS] = (light[0, colour] * live_pix).astype(jnp.bfloat16)
     picked.wait()
+
+
+def stay_kernel(message, here):
+    here[...] = message[...]
 
 
 def halo_kernel(*refs):
@@ -434,7 +438,8 @@
         limit=PACK_LIMIT,
     )(hogel_light, silhouette, fill_counts, hogel_index, row_taps, col_taps, incident)
     mine = mine.reshape(2 * BAND, COLS)
-    layers_in = messages[:1] + [over_depth(messages[hop], hop) for hop in range(1, LAYERS)]
+    kept = call(stay_kernel, shaped((BAND, HALO_W), bf16), [vmem], moved=10**5)(messages[0])
+    layers_in = [kept] + [over_depth(messages[hop], hop) for hop in range(1, LAYERS)]
     arrived = neighbours((mine,) * 4)[::-1]
     near = shaped((NEAR, HALO_W), bf16)
     far = shaped((FAR, HALO_W), bf16)

time: 32.1 us -> 32.1 us (level)
  starting transfers between devices: 14.7 us -> 15.2 us
  waiting for transfers between devices: 9.49 us -> 9 us
    ppermute x6, starting transfers between devices: 7.67 us -> 8.38 us  [over_depth(): return lax.ppermute(value, 'depth', [(i, i ^ hop) for i in range(LAYERS)])]
    ppermute x6, waiting for transfers between devices: 7.34 us -> 6.66 us  [over_depth(): return lax.ppermute(value, 'depth', [(i, i ^ hop) for i in range(LAYERS)])]
  transfers between devices with their start and end apart: 14 -> 14, of which waited for: 5 -> 6; matrix products, arithmetic and copies ran while one was open for 0% -> 0% of each run, Pallas kernels for 4% -> 4%
where the time goes in v24:
time: 32.1 us; the launch traced here: 31.9 us
  starting transfers between devices  15.2 us (47%)
  waiting for transfers between devices  9 us (28%)
  Pallas kernels  6.65 us (21%)
  local copies, waits for them, and re-layouts  0.91 us (3%)
    ppermute x6, starting transfers between devices, over_depth(): return lax.ppermute(value, 'depth', [(i, i ^ hop) for i in range(LAYERS)])  8.38 us
    ppermute x8, starting transfers between devices, exchanged(): return lax.ppermute(value, ('depth', 'rows'), pairs)  6.87 us
    ppermute x6, waiting for transfers between devices, over_depth(): return lax.ppermute(value, 'depth', [(i, i ^ hop) for i in range(LAYERS)])  6.66 us
    pallas_call x1, Pallas kernels, body(): call(chain_kernel, [shaped((2, BAND, COLS), bf16)] * LAYERS, [vmem] * (6...  2.52 us
    ppermute x8, waiting for transfers between devices, exchanged(): return lax.ppermute(value, ('depth', 'rows'), pairs)  2.35 us
    pallas_call x1, Pallas kernels, body(): call(pack_kernel, (shaped((BAND, HALO_W), bf16),) * LAYERS + (shaped(inci...  2.08 us
    pallas_call x1, Pallas kernels, body(): call(prepare_kernel, [shaped((TILES * layer_height(0), 2 * LANES), f32),...  1.2 us
    unnamed x10, local copies, waits for them, and re-layouts  0.91 us
  transfers between devices with their start and end apart: 14, of which 6 were waited for; matrix products, arithmetic and copies ran while one was open for 0% of the time, Pallas kernels for 4%

profile of v24, /device:TPU:0, one launch (start us, length us, event | category | flops | bytes accessed | tf_op | source)
XLA Modules:
  0.0 31.9 jit_solution(10228792731963339882)
XLA Ops:
  0.0 2.1 %shard_map.100 = (bf16[32,1152]{1,0:T(8,128)(2,1)}, bf16[32,1152]{1,0:T(8,128)(2,1)}, bf16[32,1152]{1,0:T(8,128)(2,1)}, bf16[32,1152]{1,0:T(8,128)(2,1)}, bf16[2,32,1024]{2,1,0:T(8,128)(2,1)}) custom-call(f32[1,3,32,1024]{3,2,1,0:T(8,128)} %light.1, s32[1,32,64]{2,1,0:T(8,128)} %edges.1, s32[1,2]{1,0:T(1,128)} %counts.1, s32[1,2,64]{2,1,0:T(2,128)} %listed.1, ...), custom_call_target="tpu_custom_call" | custom-call | flops 10000000 | bytes 1000000 | tf_op jit(solution)/shard_map/pallas_call | solution.py:432
  2.1 0.5 %collective-permute-start.10 = (bf16[64,1024]{1,0:T(8,128)(2,1)}, bf16[64,1024]{1,0:T(8,128)(2,1)S(1)}, u32[]{:S(2)}, u32[]{:S(2)}) collective-permute-start(bf16[64,1024]{1,0:T(8,128)(2,1)} %bitcast.1), channel_id=1, source_target_pairs={{0,1},{1,0},{2,3},{3,2},{4,5},{5,4},{6,7},{7,6},{8,9},{9,8},{10,11... | collective-permute-start | bytes 393224 | tf_op jit(solution)/shard_map/ppermute | solution.py:390
  2.6 2.6 %collective-permute-start = (bf16[32,1152]{1,0:T(8,128)(2,1)}, bf16[32,1152]{1,0:T(8,128)(2,1)S(1)}, u32[]{:S(2)}, u32[]{:S(2)}) collective-permute-start(bf16[32,1152]{1,0:T(8,128)(2,1)} %get-tuple-element.27), channel_id=1, source_target_pairs={{0,8},{8,0},{16,24},{24,16},{1,9},{9,1},{17,25},{25,17},{2,10},{10... | collective-permute-start | bytes 221192 | tf_op jit(solution)/shard_map/ppermute | solution.py:371
  5.2 1.5 %collective-permute-start.1 = (bf16[32,1152]{1,0:T(8,128)(2,1)}, bf16[32,1152]{1,0:T(8,128)(2,1)S(1)}, u32[]{:S(2)}, u32[]{:S(2)}) collective-permute-start(bf16[32,1152]{1,0:T(8,128)(2,1)} %get-tuple-element.28), channel_id=1, source_target_pairs={{0,16},{8,24},{16,0},{24,8},{1,17},{9,25},{17,1},{25,9},{2,18},{10... | collective-permute-start | bytes 221192 | tf_op jit(solution)/shard_map/ppermute | solution.py:371
  6.7 0.0 collective-permute-start.2
  6.7 1.9 %collective-permute-start.9 = (bf16[64,1024]{1,0:T(8,128)(2,1)}, bf16[64,1024]{1,0:T(8,128)(2,1)S(1)}, u32[]{:S(2)}, u32[]{:S(2)}) collective-permute-start(bf16[64,1024]{1,0:T(8,128)(2,1)} %bitcast.2), channel_id=1, source_target_pairs={{0,8},{1,2},{2,1},{3,4},{4,3},{5,6},{6,5},{7,15},{8,0},{9,10},{10,... | collective-permute-start | bytes 393224 | tf_op jit(solution)/shard_map/ppermute | solution.py:390
  8.7 0.0 collective-permute-done.refs_1_
  8.7 1.4 %collective-permute-start.8 = (bf16[64,1024]{1,0:T(8,128)(2,1)}, bf16[64,1024]{1,0:T(8,128)(2,1)S(1)}, u32[]{:S(2)}, u32[]{:S(2)}) collective-permute-start(bf16[64,1024]{1,0:T(8,128)(2,1)} %bitcast.3), channel_id=1, source_target_pairs={{0,2},{1,3},{2,0},{3,1},{4,6},{5,7},{6,4},{7,5},{8,10},{9,11},{10,... | collective-permute-start | bytes 393224 | tf_op jit(solution)/shard_map/ppermute | solution.py:390
  10.1 0.0 collective-permute-done.1.refs_2_
  10.1 0.1 collective-permute-start.7
  10.2 0.0 copy-start
  10.2 0.9 %copy-done = bf16[32,1152]{1,0:T(8,128)(2,1)S(1)} copy-done((bf16[32,1152]{1,0:T(8,128)(2,1)S(1)}, bf16[32,1152]{1,0:T(8,128)(2,1)}, u32[]{:S(2)}) %copy-start) | copy-done | bytes 73752
  11.1 0.0 copy-start.3
  11.1 0.0 copy-start.1
  11.1 0.0 copy-start.2
  11.1 1.1 %collective-permute-done.2.refs_3_ = bf16[32,1152]{1,0:T(8,128)(2,1)S(1)} collective-permute-done((bf16[32,1152]{1,0:T(8,128)(2,1)}, bf16[32,1152]{1,0:T(8,128)(2,1)S(1)}, u32[]{:S(2)}, u32[]{:S(2)}) %collective-permute-start.2) | collective-permute-done | bytes 73760 | tf_op jit(solution)/shard_map/ppermute | solution.py:371
  12.2 0.1 shard_map.102
  12.2 0.1 collective-permute-start.3
  12.3 0.0 collective-permute-done.10.in_chip
  12.3 1.0 %collective-permute-start.4 = (bf16[80,1152]{1,0:T(8,128)(2,1)S(1)}, bf16[80,1152]{1,0:T(8,128)(2,1)S(1)}, u32[]{:S(2)}, u32[]{:S(2)}) collective-permute-start(bf16[80,1152]{1,0:T(8,128)(2,1)S(1)} %get-tuple-element.31), channel_id=1, source_target_pairs={{0,8},{1,2},{2,1},{3,4},{4,3},{5,6},{6,5},{7,15},{8,0},{9,10},{10,... | collective-permute-start | bytes 552968 | tf_op jit(solution)/shard_map/ppermute | solution.py:390
  13.3 0.0 collective-permute-done.9.cross
  13.3 1.2 %collective-permute-start.5 = (bf16[16,1152]{1,0:T(8,128)(2,1)S(1)}, bf16[16,1152]{1,0:T(8,128)(2,1)S(1)}, u32[]{:S(2)}, u32[]{:S(2)}) collective-permute-start(bf16[16,1152]{1,0:T(8,128)(2,1)S(1)} %get-tuple-element.32), channel_id=1, source_target_pairs={{0,2},{1,3},{2,0},{3,1},{4,6},{5,7},{6,4},{7,5},{8,10},{9,11},{10,... | collective-permute-start | bytes 110600 | tf_op jit(solution)/shard_map/ppermute | solution.py:390
  14.5 0.2 collective-permute-done.8.far_even
  14.7 0.7 %collective-permute-start.6 = (bf16[16,1152]{1,0:T(8,128)(2,1)S(1)}, bf16[16,1152]{1,0:T(8,128)(2,1)S(1)}, u32[]{:S(2)}, u32[]{:S(2)}) collective-permute-start(bf16[16,1152]{1,0:T(8,128)(2,1)S(1)} %get-tuple-element.33), channel_id=1, source_target_pairs={{0,1},{1,0},{2,4},{3,5},{4,2},{5,3},{6,7},{7,6},{8,9},{9,8},{10,12... | collective-permute-start | bytes 110600 | tf_op jit(solution)/shard_map/ppermute | solution.py:390
  15.4 0.0 collective-permute-done.7.far_odd
  15.4 0.0 copy-done.3
  15.4 0.0 copy-done.1
  15.4 0.0 copy-done.2
  15.4 0.0 copy-start.4
  15.4 1.2 %shard_map.103 = (f32[1024,256]{1,0:T(8,128)S(1)}, f32[2,128,1024]{2,1,0:T(8,128)S(1)}, f32[128,1024]{1,0:T(8,128)S(1)}, bf16[3,256,512]{2,1,0:T(8,128)(2,1)S(1)...) custom-call(bf16[4,32,1152]{2,1,0:T(8,128)(2,1)S(1)} %get-tuple-element.34.own, ...), custom_call_target="tpu_custom_call" | custom-call | flops 1000000000 | bytes 3000000 | tf_op jit(solution)/shard_map/pallas_call | solution.py:453
  16.6 2.1 %collective-permute-done.5.far_even = bf16[16,1152]{1,0:T(8,128)(2,1)S(1)} collective-permute-done((bf16[16,1152]{1,0:T(8,128)(2,1)S(1)}, bf16[16,1152]{1,0:T(8,128)(2,1)S(1)}, u32[]{:S(2)}, u32[]{:S(2)}) %collective-permute-start.5) | collective-permute-done | bytes 36896 | tf_op jit(solution)/shard_map/ppermute | solution.py:390
  18.7 0.0 collective-permute-done.6.far_odd
  18.7 0.0 collective-permute-done.3.in_chip
  18.8 0.0 collective-permute-done.4.cross
  18.8 0.0 copy-done.4
  18.8 2.5 %shard_map.104 = (bf16[2,32,1024]{2,1,0:T(8,128)(2,1)S(1)}, bf16[2,32,1024]{2,1,0:T(8,128)(2,1)S(1)}, bf16[2,32,1024]{2,1,0:T(8,128)(2,1)S(1)}, bf16[2,32,1024]{2,1,0:T(8,128)(2,1)S(1)}) custom-call(bf16[80,1152]{1,0:T(8,128)(2,1)S(1)} %collective-permute-done.3.in_chip, bf16[80,1152]{1,0:T(8,128)(2,1)S(1)} %collective-permute-done.4.cross, ...), custom_call_target="tpu_custom_call" | custom-call | flops 2000000000 | bytes 3000000 | tf_op jit(solution)/shard_map/pallas_call | solution.py:467
  21.3 1.7 %collective-permute-start.11 = (bf16[2,32,1024]{2,1,0:T(8,128)(2,1)S(1)}, bf16[2,32,1024]{2,1,0:T(8,128)(2,1)S(1)}, u32[]{:S(2)}, u32[]{:S(2)}) collective-permute-start(bf16[2,32,1024]{2,1,0:T(8,128)(2,1)S(1)} %get-tuple-element.44), channel_id=1, source_target_pairs={{0,8},{8,0},{16,24},{24,16},{1,9},{9,1},{17,25},{25,17},{2,10},{10... | collective-permute-start | bytes 393224 | tf_op jit(solution)/shard_map/ppermute | solution.py:371
  23.0 1.6 %collective-permute-start.12 = (bf16[2,32,1024]{2,1,0:T(8,128)(2,1)S(1)}, bf16[2,32,1024]{2,1,0:T(8,128)(2,1)S(1)}, u32[]{:S(2)}, u32[]{:S(2)}) collective-permute-start(bf16[2,32,1024]{2,1,0:T(8,128)(2,1)S(1)} %get-tuple-element.45), channel_id=1, source_target_pairs={{0,16},{8,24},{16,0},{24,8},{1,17},{9,25},{17,1},{25,9},{2,18},{10... | collective-permute-start | bytes 393224 | tf_op jit(solution)/shard_map/ppermute | solution.py:371
  24.6 0.9 %collective-permute-start.13 = (bf16[2,32,1024]{2,1,0:T(8,128)(2,1)S(1)}, bf16[2,32,1024]{2,1,0:T(8,128)(2,1)S(1)}, u32[]{:S(2)}, u32[]{:S(2)}) collective-permute-start(bf16[2,32,1024]{2,1,0:T(8,128)(2,1)S(1)} %get-tuple-element.46), channel_id=1, source_target_pairs={{0,24},{8,16},{16,8},{24,0},{1,25},{9,17},{17,9},{25,1},{2,26},{10... | collective-permute-start | bytes 393224 | tf_op jit(solution)/shard_map/ppermute | solution.py:371
  25.6 1.3 %collective-permute-done.11.refs_1_ = bf16[2,32,1024]{2,1,0:T(8,128)(2,1)S(1)} collective-permute-done((bf16[2,32,1024]{2,1,0:T(8,128)(2,1)S(1)}, bf16[2,32,1024]{2,1,0:T(8,128)(2,1)S(1)}, u32[]{:S(2)}, u32[]{:S(2)}) %collective-permute-start.11) | collective-permute-done | bytes 131104 | tf_op jit(solution)/shard_map/ppermute | solution.py:371
  26.8 2.7 %collective-permute-done.12.refs_2_ = bf16[2,32,1024]{2,1,0:T(8,128)(2,1)S(1)} collective-permute-done((bf16[2,32,1024]{2,1,0:T(8,128)(2,1)S(1)}, bf16[2,32,1024]{2,1,0:T(8,128)(2,1)S(1)}, u32[]{:S(2)}, u32[]{:S(2)}) %collective-permute-start.12) | collective-permute-done | bytes 131104 | tf_op jit(solution)/shard_map/ppermute | solution.py:371
  29.5 1.7 %collective-permute-done.13.refs_3_ = bf16[2,32,1024]{2,1,0:T(8,128)(2,1)S(1)} collective-permute-done((bf16[2,32,1024]{2,1,0:T(8,128)(2,1)S(1)}, bf16[2,32,1024]{2,1,0:T(8,128)(2,1)S(1)}, u32[]{:S(2)}, u32[]{:S(2)}) %collective-permute-start.13) | collective-permute-done | bytes 131104 | tf_op jit(solution)/shard_map/ppermute | solution.py:371
  31.1 0.8 %shard_map.105 = bf16[1,3,2,32,1024]{4,3,2,1,0:T(8,128)(2,1)} custom-call(bf16[2,32,1024]{2,1,0:T(8,128)(2,1)S(1)} %get-tuple-element.43.refs_0_, bf16[2,32,1024]{2,1,0:T(8,128)(2,1)S(1)} %collective-permute-done.11.refs_1_, bf16[2,32,1024]{2,1,0:T(8,128)(2,1)S(1)} %collective-permute-done.12.refs_2_, bf16[2,32,1024]{2,1,0:T(8,128)(2,1)S(1)} %collective-permute-done.13.refs_3_), custom_call_target="tpu_custom_call" | custom-call | bytes 1000000 | tf_op jit(solution)/shard_map/pallas_call | solution.py:476
  (1 shorter events, 0.0 us)
Async XLA Ops:
  2.1 10.2 %collective-permute-start.10 = (bf16[64,1024]{1,0:T(8,128)(2,1)}, bf16[64,1024]{1,0:T(8,128)(2,1)S(1)}, u32[]{:S(2)}, u32[]{:S(2)}) collective-permute-start(bf16[64,1024]{1,0:T(8,128)(2,1)} %bitcast.1), channel_id=1, source_target_pairs={{0,1},{1,0},{2,3},{3,2},{4,5},{5,4},{6,7},{7,6},{8,9},{9,8},{10,11... | collective-permute-start | bytes 393224 | tf_op jit(solution)/shard_map/ppermute | solution.py:390
  2.6 6.1 %collective-permute-start = (bf16[32,1152]{1,0:T(8,128)(2,1)}, bf16[32,1152]{1,0:T(8,128)(2,1)S(1)}, u32[]{:S(2)}, u32[]{:S(2)}) collective-permute-start(bf16[32,1152]{1,0:T(8,128)(2,1)} %get-tuple-element.27), channel_id=1, source_target_pairs={{0,8},{8,0},{16,24},{24,16},{1,9},{9,1},{17,25},{25,17},{2,10},{10... | collective-permute-start | bytes 221192 | tf_op jit(solution)/shard_map/ppermute | solution.py:371
  5.2 4.9 %collective-permute-start.1 = (bf16[32,1152]{1,0:T(8,128)(2,1)}, bf16[32,1152]{1,0:T(8,128)(2,1)S(1)}, u32[]{:S(2)}, u32[]{:S(2)}) collective-permute-start(bf16[32,1152]{1,0:T(8,128)(2,1)} %get-tuple-element.28), channel_id=1, source_target_pairs={{0,16},{8,24},{16,0},{24,8},{1,17},{9,25},{17,1},{25,9},{2,18},{10... | collective-permute-start | bytes 221192 | tf_op jit(solution)/shard_map/ppermute | solution.py:371
  6.7 5.5 %collective-permute-start.2 = (bf16[32,1152]{1,0:T(8,128)(2,1)}, bf16[32,1152]{1,0:T(8,128)(2,1)S(1)}, u32[]{:S(2)}, u32[]{:S(2)}) collective-permute-start(bf16[32,1152]{1,0:T(8,128)(2,1)} %get-tuple-element.29), channel_id=1, source_target_pairs={{0,24},{8,16},{16,8},{24,0},{1,25},{9,17},{17,9},{25,1},{2,26},{10... | collective-permute-start | bytes 221192 | tf_op jit(solution)/shard_map/ppermute | solution.py:371
  6.7 6.6 %collective-permute-start.9 = (bf16[64,1024]{1,0:T(8,128)(2,1)}, bf16[64,1024]{1,0:T(8,128)(2,1)S(1)}, u32[]{:S(2)}, u32[]{:S(2)}) collective-permute-start(bf16[64,1024]{1,0:T(8,128)(2,1)} %bitcast.2), channel_id=1, source_target_pairs={{0,8},{1,2},{2,1},{3,4},{4,3},{5,6},{6,5},{7,15},{8,0},{9,10},{10,... | collective-permute-start | bytes 393224 | tf_op jit(solution)/shard_map/ppermute | solution.py:390
  8.7 6.0 %collective-permute-start.8 = (bf16[64,1024]{1,0:T(8,128)(2,1)}, bf16[64,1024]{1,0:T(8,128)(2,1)S(1)}, u32[]{:S(2)}, u32[]{:S(2)}) collective-permute-start(bf16[64,1024]{1,0:T(8,128)(2,1)} %bitcast.3), channel_id=1, source_target_pairs={{0,2},{1,3},{2,0},{3,1},{4,6},{5,7},{6,4},{7,5},{8,10},{9,11},{10,... | collective-permute-start | bytes 393224 | tf_op jit(solution)/shard_map/ppermute | solution.py:390
  10.1 5.3 %collective-permute-start.7 = (bf16[64,1024]{1,0:T(8,128)(2,1)}, bf16[64,1024]{1,0:T(8,128)(2,1)S(1)}, u32[]{:S(2)}, u32[]{:S(2)}) collective-permute-start(bf16[64,1024]{1,0:T(8,128)(2,1)} %bitcast.4), channel_id=1, source_target_pairs={{0,1},{1,0},{2,4},{3,5},{4,2},{5,3},{6,7},{7,6},{8,9},{9,8},{10,12... | collective-permute-start | bytes 393224 | tf_op jit(solution)/shard_map/ppermute | solution.py:390
  10.2 0.9 %copy-start = (bf16[32,1152]{1,0:T(8,128)(2,1)S(1)}, bf16[32,1152]{1,0:T(8,128)(2,1)}, u32[]{:S(2)}) copy-start(bf16[32,1152]{1,0:T(8,128)(2,1)} %get-tuple-element.26.message) | copy-start | bytes 221188
  11.1 4.3 %copy-start.3 = (bf16[256,256]{1,0:T(8,128)(2,1)S(1)}, bf16[256,256]{1,0:T(8,128)(2,1)}, u32[]{:S(2)}) copy-start(bf16[256,256]{1,0:T(8,128)(2,1)} %constant.7.clone.left_tab) | copy-start | bytes 393220
  11.1 4.3 %copy-start.1 = (bf16[2,32,1024]{2,1,0:T(8,128)(2,1)S(1)}, bf16[2,32,1024]{2,1,0:T(8,128)(2,1)}, u32[]{:S(2)}) copy-start(bf16[2,32,1024]{2,1,0:T(8,128)(2,1)} %get-tuple-element.35) | copy-start | bytes 393220
  11.1 4.3 %copy-start.2 = (bf16[256,256]{1,0:T(8,128)(2,1)S(1)}, bf16[256,256]{1,0:T(8,128)(2,1)}, u32[]{:S(2)}) copy-start(bf16[256,256]{1,0:T(8,128)(2,1)} %constant.6.clone.right_tab) | copy-start | bytes 393220
  12.2 6.5 %collective-permute-start.3 = (bf16[80,1152]{1,0:T(8,128)(2,1)S(1)}, bf16[80,1152]{1,0:T(8,128)(2,1)S(1)}, u32[]{:S(2)}, u32[]{:S(2)}) collective-permute-start(bf16[80,1152]{1,0:T(8,128)(2,1)S(1)} %get-tuple-element.30), channel_id=1, source_target_pairs={{0,1},{1,0},{2,3},{3,2},{4,5},{5,4},{6,7},{7,6},{8,9},{9,8},{10,11... | collective-permute-start | bytes 552968 | tf_op jit(solution)/shard_map/ppermute | solution.py:390
  12.3 6.4 %collective-permute-start.4 = (bf16[80,1152]{1,0:T(8,128)(2,1)S(1)}, bf16[80,1152]{1,0:T(8,128)(2,1)S(1)}, u32[]{:S(2)}, u32[]{:S(2)}) collective-permute-start(bf16[80,1152]{1,0:T(8,128)(2,1)S(1)} %get-tuple-element.31), channel_id=1, source_target_pairs={{0,8},{1,2},{2,1},{3,4},{4,3},{5,6},{6,5},{7,15},{8,0},{9,10},{10,... | collective-permute-start | bytes 552968 | tf_op jit(solution)/shard_map/ppermute | solution.py:390
  13.3 5.4 %collective-permute-start.5 = (bf16[16,1152]{1,0:T(8,128)(2,1)S(1)}, bf16[16,1152]{1,0:T(8,128)(2,1)S(1)}, u32[]{:S(2)}, u32[]{:S(2)}) collective-permute-start(bf16[16,1152]{1,0:T(8,128)(2,1)S(1)} %get-tuple-element.32), channel_id=1, source_target_pairs={{0,2},{1,3},{2,0},{3,1},{4,6},{5,7},{6,4},{7,5},{8,10},{9,11},{10,... | collective-permute-start | bytes 110600 | tf_op jit(solution)/shard_map/ppermute | solution.py:390
  14.7 4.0 %collective-permute-start.6 = (bf16[16,1152]{1,0:T(8,128)(2,1)S(1)}, bf16[16,1152]{1,0:T(8,128)(2,1)S(1)}, u32[]{:S(2)}, u32[]{:S(2)}) collective-permute-start(bf16[16,1152]{1,0:T(8,128)(2,1)S(1)} %get-tuple-element.33), channel_id=1, source_target_pairs={{0,1},{1,0},{2,4},{3,5},{4,2},{5,3},{6,7},{7,6},{8,9},{9,8},{10,12... | collective-permute-start | bytes 110600 | tf_op jit(solution)/shard_map/ppermute | solution.py:390
  15.4 3.4 %copy-start.4 = (bf16[192,192]{1,0:T(8,128)(2,1)S(1)}, bf16[192,192]{1,0:T(8,128)(2,1)}, u32[]{:S(2)}) copy-start(bf16[192,192]{1,0:T(8,128)(2,1)} %constant.8.clone.left_tab) | copy-start | bytes 221188
  21.3 5.5 %collective-permute-start.11 = (bf16[2,32,1024]{2,1,0:T(8,128)(2,1)S(1)}, bf16[2,32,1024]{2,1,0:T(8,128)(2,1)S(1)}, u32[]{:S(2)}, u32[]{:S(2)}) collective-permute-start(bf16[2,32,1024]{2,1,0:T(8,128)(2,1)S(1)} %get-tuple-element.44), channel_id=1, source_target_pairs={{0,8},{8,0},{16,24},{24,16},{1,9},{9,1},{17,25},{25,17},{2,10},{10... | collective-permute-start | bytes 393224 | tf_op jit(solution)/shard_map/ppermute | solution.py:371
  23.0 6.5 %collective-permute-start.12 = (bf16[2,32,1024]{2,1,0:T(8,128)(2,1)S(1)}, bf16[2,32,1024]{2,1,0:T(8,128)(2,1)S(1)}, u32[]{:S(2)}, u32[]{:S(2)}) collective-permute-start(bf16[2,32,1024]{2,1,0:T(8,128)(2,1)S(1)} %get-tuple-element.45), channel_id=1, source_target_pairs={{0,16},{8,24},{16,0},{24,8},{1,17},{9,25},{17,1},{25,9},{2,18},{10... | collective-permute-start | bytes 393224 | tf_op jit(solution)/shard_map/ppermute | solution.py:371
  24.6 6.5 %collective-permute-start.13 = (bf16[2,32,1024]{2,1,0:T(8,128)(2,1)S(1)}, bf16[2,32,1024]{2,1,0:T(8,128)(2,1)S(1)}, u32[]{:S(2)}, u32[]{:S(2)}) collective-permute-start(bf16[2,32,1024]{2,1,0:T(8,128)(2,1)S(1)} %get-tuple-element.46), channel_id=1, source_target_pairs={{0,24},{8,16},{16,8},{24,0},{1,25},{9,17},{17,9},{25,1},{2,26},{10... | collective-permute-start | bytes 393224 | tf_op jit(solution)/shard_map/ppermute | solution.py:371

commit v25 on v24

--- a/solution.py
+++ b/solution.py
@@ -132,8 +132,8 @@
 def halo_kernel(*refs):
     arrived, (own, in_chip, cross, far_even, far_odd) = refs[:LAYERS], refs[LAYERS:]
     depth = lax.axis_index("depth")
-    for hop in range(LAYERS):
-        own[depth ^ hop] = arrived[hop][...]
+    for place, hop in enumerate((0, 3, 1, 2)):
+        own[depth ^ hop] = arrived[place][...]
     band = lax.axis_index("rows")
     core = band % 2
     odd = (band // 2) % 2
@@ -439,7 +439,8 @@
     )(hogel_light, silhouette, fill_counts, hogel_index, row_taps, col_taps, incident)
     mine = mine.reshape(2 * BAND, COLS)
     kept = call(stay_kernel, shaped((BAND, HALO_W), bf16), [vmem], moved=10**5)(messages[0])
-    layers_in = [kept] + [over_depth(messages[hop], hop) for hop in range(1, LAYERS)]
+    diagonal = over_depth(messages[3], 3)
+    layers_in = [kept, over_depth(messages[1], 1), over_depth(messages[2], 2), diagonal]
     arrived = neighbours((mine,) * 4)[::-1]
     near = shaped((NEAR, HALO_W), bf16)
     far = shaped((FAR, HALO_W), bf16)
@@ -447,7 +448,7 @@
         halo_kernel,
         (shaped((LAYERS, BAND, HALO_W), bf16), near, near, far, far),
         [vmem] * LAYERS,
-    )(*layers_in)
+    )(layers_in[0], layers_in[3], layers_in[1], layers_in[2])
     halos = neighbours(sent)
     right_tab = jnp.asarray(right_table())
     made = call(

time: 32.1 us -> 32.9 us (1.025)
  starting transfers between devices: 15.2 us -> 15.7 us
  waiting for transfers between devices: 9 us -> 9.34 us
    ppermute x8, starting transfers between devices: 6.87 us -> 8 us  [exchanged(): return lax.ppermute(value, ('depth', 'rows'), pairs)]
    ppermute x6, starting transfers between devices: 8.38 us -> 7.73 us  [over_depth(): return lax.ppermute(value, 'depth', [(i, i ^ hop) for i in range(LAYERS)])]
    ppermute x8, waiting for transfers between devices: 2.35 us -> 2.84 us  [exchanged(): return lax.ppermute(value, ('depth', 'rows'), pairs)]
  transfers between devices with their start and end apart: 14 -> 14, of which waited for: 6 -> 4; matrix products, arithmetic and copies ran while one was open for 0% -> 0% of each run, Pallas kernels for 4% -> 4%
where the time goes in v25:
time: 32.9 us; the launch traced here: 32.7 us
  starting transfers between devices  15.7 us (48%)
  waiting for transfers between devices  9.34 us (28%)
  Pallas kernels  6.65 us (20%)
  local copies, waits for them, and re-layouts  0.91 us (3%)
    ppermute x8, starting transfers between devices, exchanged(): return lax.ppermute(value, ('depth', 'rows'), pairs)  8 us
    ppermute x6, starting transfers between devices, over_depth(): return lax.ppermute(value, 'depth', [(i, i ^ hop) for i in range(LAYERS)])  7.73 us
    ppermute x6, waiting for transfers between devices, over_depth(): return lax.ppermute(value, 'depth', [(i, i ^ hop) for i in range(LAYERS)])  6.5 us
    ppermute x8, waiting for transfers between devices, exchanged(): return lax.ppermute(value, ('depth', 'rows'), pairs)  2.84 us
    pallas_call x1, Pallas kernels, body(): call(chain_kernel, [shaped((2, BAND, COLS), bf16)] * LAYERS, [vmem] * (6...  2.52 us
    pallas_call x1, Pallas kernels, body(): call(pack_kernel, (shaped((BAND, HALO_W), bf16),) * LAYERS + (shaped(inci...  2.08 us
    pallas_call x1, Pallas kernels, body(): call(prepare_kernel, [shaped((TILES * layer_height(0), 2 * LANES), f32),...  1.2 us
    unnamed x10, local copies, waits for them, and re-layouts  0.91 us
  transfers between devices with their start and end apart: 14, of which 4 were waited for; matrix products, arithmetic and copies ran while one was open for 0% of the time, Pallas kernels for 4%

profile of v25, /device:TPU:0, one launch (start us, length us, event | category | flops | bytes accessed | tf_op | source)
XLA Modules:
  0.0 32.7 jit_solution(1791634599406479661)
XLA Ops:
  0.0 2.1 %shard_map.100 = (bf16[32,1152]{1,0:T(8,128)(2,1)}, bf16[32,1152]{1,0:T(8,128)(2,1)}, bf16[32,1152]{1,0:T(8,128)(2,1)}, bf16[32,1152]{1,0:T(8,128)(2,1)}, bf16[2,32,1024]{2,1,0:T(8,128)(2,1)}) custom-call(f32[1,3,32,1024]{3,2,1,0:T(8,128)} %light.1, s32[1,32,64]{2,1,0:T(8,128)} %edges.1, s32[1,2]{1,0:T(1,128)} %counts.1, s32[1,2,64]{2,1,0:T(2,128)} %listed.1, ...), custom_call_target="tpu_custom_call" | custom-call | flops 10000000 | bytes 1000000 | tf_op jit(solution)/shard_map/pallas_call | solution.py:432
  2.1 0.5 %collective-permute-start.10 = (bf16[64,1024]{1,0:T(8,128)(2,1)}, bf16[64,1024]{1,0:T(8,128)(2,1)S(1)}, u32[]{:S(2)}, u32[]{:S(2)}) collective-permute-start(bf16[64,1024]{1,0:T(8,128)(2,1)} %bitcast.1), channel_id=1, source_target_pairs={{0,1},{1,0},{2,3},{3,2},{4,5},{5,4},{6,7},{7,6},{8,9},{9,8},{10,11... | collective-permute-start | bytes 393224 | tf_op jit(solution)/shard_map/ppermute | solution.py:390
  2.6 3.5 %collective-permute-start = (bf16[32,1152]{1,0:T(8,128)(2,1)}, bf16[32,1152]{1,0:T(8,128)(2,1)S(1)}, u32[]{:S(2)}, u32[]{:S(2)}) collective-permute-start(bf16[32,1152]{1,0:T(8,128)(2,1)} %get-tuple-element.27), channel_id=1, source_target_pairs={{0,24},{8,16},{16,8},{24,0},{1,25},{9,17},{17,9},{25,1},{2,26},{10... | collective-permute-start | bytes 221192 | tf_op jit(solution)/shard_map/ppermute | solution.py:371
  6.1 0.5 %collective-permute-start.1 = (bf16[32,1152]{1,0:T(8,128)(2,1)}, bf16[32,1152]{1,0:T(8,128)(2,1)S(1)}, u32[]{:S(2)}, u32[]{:S(2)}) collective-permute-start(bf16[32,1152]{1,0:T(8,128)(2,1)} %get-tuple-element.28), channel_id=1, source_target_pairs={{0,8},{8,0},{16,24},{24,16},{1,9},{9,1},{17,25},{25,17},{2,10},{10... | collective-permute-start | bytes 221192 | tf_op jit(solution)/shard_map/ppermute | solution.py:371
  6.7 0.1 collective-permute-start.2
  6.8 1.9 %collective-permute-start.9 = (bf16[64,1024]{1,0:T(8,128)(2,1)}, bf16[64,1024]{1,0:T(8,128)(2,1)S(1)}, u32[]{:S(2)}, u32[]{:S(2)}) collective-permute-start(bf16[64,1024]{1,0:T(8,128)(2,1)} %bitcast.2), channel_id=1, source_target_pairs={{0,8},{1,2},{2,1},{3,4},{4,3},{5,6},{6,5},{7,15},{8,0},{9,10},{10,... | collective-permute-start | bytes 393224 | tf_op jit(solution)/shard_map/ppermute | solution.py:390
  8.7 0.7 %collective-permute-done.refs_1_ = bf16[32,1152]{1,0:T(8,128)(2,1)S(1)} collective-permute-done((bf16[32,1152]{1,0:T(8,128)(2,1)}, bf16[32,1152]{1,0:T(8,128)(2,1)S(1)}, u32[]{:S(2)}, u32[]{:S(2)}) %collective-permute-start) | collective-permute-done | bytes 73760 | tf_op jit(solution)/shard_map/ppermute | solution.py:371
  9.3 2.1 %collective-permute-start.8 = (bf16[64,1024]{1,0:T(8,128)(2,1)}, bf16[64,1024]{1,0:T(8,128)(2,1)S(1)}, u32[]{:S(2)}, u32[]{:S(2)}) collective-permute-start(bf16[64,1024]{1,0:T(8,128)(2,1)} %bitcast.3), channel_id=1, source_target_pairs={{0,2},{1,3},{2,0},{3,1},{4,6},{5,7},{6,4},{7,5},{8,10},{9,11},{10,... | collective-permute-start | bytes 393224 | tf_op jit(solution)/shard_map/ppermute | solution.py:390
  11.4 0.0 collective-permute-done.1.refs_2_
  11.4 0.0 collective-permute-start.7
  11.4 0.0 copy-start
  11.4 0.9 %copy-done = bf16[32,1152]{1,0:T(8,128)(2,1)S(1)} copy-done((bf16[32,1152]{1,0:T(8,128)(2,1)S(1)}, bf16[32,1152]{1,0:T(8,128)(2,1)}, u32[]{:S(2)}) %copy-start) | copy-done | bytes 73752
  12.3 0.0 copy-start.3
  12.3 0.0 copy-start.1
  12.3 0.0 copy-start.2
  12.3 0.0 collective-permute-done.2.refs_3_
  12.3 0.1 shard_map.102
  12.4 0.6 %collective-permute-start.3 = (bf16[80,1152]{1,0:T(8,128)(2,1)S(1)}, bf16[80,1152]{1,0:T(8,128)(2,1)S(1)}, u32[]{:S(2)}, u32[]{:S(2)}) collective-permute-start(bf16[80,1152]{1,0:T(8,128)(2,1)S(1)} %get-tuple-element.30), channel_id=1, source_target_pairs={{0,1},{1,0},{2,3},{3,2},{4,5},{5,4},{6,7},{7,6},{8,9},{9,8},{10,11... | collective-permute-start | bytes 552968 | tf_op jit(solution)/shard_map/ppermute | solution.py:390
  13.0 0.0 collective-permute-done.10.in_chip
  13.0 1.5 %collective-permute-start.4 = (bf16[80,1152]{1,0:T(8,128)(2,1)S(1)}, bf16[80,1152]{1,0:T(8,128)(2,1)S(1)}, u32[]{:S(2)}, u32[]{:S(2)}) collective-permute-start(bf16[80,1152]{1,0:T(8,128)(2,1)S(1)} %get-tuple-element.31), channel_id=1, source_target_pairs={{0,8},{1,2},{2,1},{3,4},{4,3},{5,6},{6,5},{7,15},{8,0},{9,10},{10,... | collective-permute-start | bytes 552968 | tf_op jit(solution)/shard_map/ppermute | solution.py:390
  14.5 0.0 collective-permute-done.9.cross
  14.5 1.3 %collective-permute-start.5 = (bf16[16,1152]{1,0:T(8,128)(2,1)S(1)}, bf16[16,1152]{1,0:T(8,128)(2,1)S(1)}, u32[]{:S(2)}, u32[]{:S(2)}) collective-permute-start(bf16[16,1152]{1,0:T(8,128)(2,1)S(1)} %get-tuple-element.32), channel_id=1, source_target_pairs={{0,2},{1,3},{2,0},{3,1},{4,6},{5,7},{6,4},{7,5},{8,10},{9,11},{10,... | collective-permute-start | bytes 110600 | tf_op jit(solution)/shard_map/ppermute | solution.py:390
  15.8 0.0 collective-permute-done.8.far_even
  15.8 0.1 collective-permute-start.6
  16.0 0.0 collective-permute-done.7.far_odd
  16.0 0.0 copy-done.3
  16.0 0.0 copy-done.1
  16.0 0.0 copy-done.2
  16.0 0.0 copy-start.4
  16.0 1.2 %shard_map.103 = (f32[1024,256]{1,0:T(8,128)S(1)}, f32[2,128,1024]{2,1,0:T(8,128)S(1)}, f32[128,1024]{1,0:T(8,128)S(1)}, bf16[3,256,512]{2,1,0:T(8,128)(2,1)S(1)...) custom-call(bf16[4,32,1152]{2,1,0:T(8,128)(2,1)S(1)} %get-tuple-element.34.own, ...), custom_call_target="tpu_custom_call" | custom-call | flops 1000000000 | bytes 3000000 | tf_op jit(solution)/shard_map/pallas_call | solution.py:454
  17.2 2.8 %collective-permute-done.5.far_even = bf16[16,1152]{1,0:T(8,128)(2,1)S(1)} collective-permute-done((bf16[16,1152]{1,0:T(8,128)(2,1)S(1)}, bf16[16,1152]{1,0:T(8,128)(2,1)S(1)}, u32[]{:S(2)}, u32[]{:S(2)}) %collective-permute-start.5) | collective-permute-done | bytes 36896 | tf_op jit(solution)/shard_map/ppermute | solution.py:390
  20.0 0.0 collective-permute-done.6.far_odd
  20.0 0.0 collective-permute-done.3.in_chip
  20.0 0.0 collective-permute-done.4.cross
  20.0 0.0 copy-done.4
  20.1 2.5 %shard_map.104 = (bf16[2,32,1024]{2,1,0:T(8,128)(2,1)S(1)}, bf16[2,32,1024]{2,1,0:T(8,128)(2,1)S(1)}, bf16[2,32,1024]{2,1,0:T(8,128)(2,1)S(1)}, bf16[2,32,1024]{2,1,0:T(8,128)(2,1)S(1)}) custom-call(bf16[80,1152]{1,0:T(8,128)(2,1)S(1)} %collective-permute-done.3.in_chip, bf16[80,1152]{1,0:T(8,128)(2,1)S(1)} %collective-permute-done.4.cross, ...), custom_call_target="tpu_custom_call" | custom-call | flops 2000000000 | bytes 3000000 | tf_op jit(solution)/shard_map/pallas_call | solution.py:468
  22.6 1.6 %collective-permute-start.11 = (bf16[2,32,1024]{2,1,0:T(8,128)(2,1)S(1)}, bf16[2,32,1024]{2,1,0:T(8,128)(2,1)S(1)}, u32[]{:S(2)}, u32[]{:S(2)}) collective-permute-start(bf16[2,32,1024]{2,1,0:T(8,128)(2,1)S(1)} %get-tuple-element.44), channel_id=1, source_target_pairs={{0,8},{8,0},{16,24},{24,16},{1,9},{9,1},{17,25},{25,17},{2,10},{10... | collective-permute-start | bytes 393224 | tf_op jit(solution)/shard_map/ppermute | solution.py:371
  24.2 1.5 %collective-permute-start.12 = (bf16[2,32,1024]{2,1,0:T(8,128)(2,1)S(1)}, bf16[2,32,1024]{2,1,0:T(8,128)(2,1)S(1)}, u32[]{:S(2)}, u32[]{:S(2)}) collective-permute-start(bf16[2,32,1024]{2,1,0:T(8,128)(2,1)S(1)} %get-tuple-element.45), channel_id=1, source_target_pairs={{0,16},{8,24},{16,0},{24,8},{1,17},{9,25},{17,1},{25,9},{2,18},{10... | collective-permute-start | bytes 393224 | tf_op jit(solution)/shard_map/ppermute | solution.py:371
  25.7 0.4 %collective-permute-start.13 = (bf16[2,32,1024]{2,1,0:T(8,128)(2,1)S(1)}, bf16[2,32,1024]{2,1,0:T(8,128)(2,1)S(1)}, u32[]{:S(2)}, u32[]{:S(2)}) collective-permute-start(bf16[2,32,1024]{2,1,0:T(8,128)(2,1)S(1)} %get-tuple-element.46), channel_id=1, source_target_pairs={{0,24},{8,16},{16,8},{24,0},{1,25},{9,17},{17,9},{25,1},{2,26},{10... | collective-permute-start | bytes 393224 | tf_op jit(solution)/shard_map/ppermute | solution.py:371
  26.1 2.1 %collective-permute-done.11.refs_1_ = bf16[2,32,1024]{2,1,0:T(8,128)(2,1)S(1)} collective-permute-done((bf16[2,32,1024]{2,1,0:T(8,128)(2,1)S(1)}, bf16[2,32,1024]{2,1,0:T(8,128)(2,1)S(1)}, u32[]{:S(2)}, u32[]{:S(2)}) %collective-permute-start.11) | collective-permute-done | bytes 131104 | tf_op jit(solution)/shard_map/ppermute | solution.py:371
  28.2 3.7 %collective-permute-done.12.refs_2_ = bf16[2,32,1024]{2,1,0:T(8,128)(2,1)S(1)} collective-permute-done((bf16[2,32,1024]{2,1,0:T(8,128)(2,1)S(1)}, bf16[2,32,1024]{2,1,0:T(8,128)(2,1)S(1)}, u32[]{:S(2)}, u32[]{:S(2)}) %collective-permute-start.12) | collective-permute-done | bytes 131104 | tf_op jit(solution)/shard_map/ppermute | solution.py:371
  32.0 0.0 collective-permute-done.13.refs_3_
  32.0 0.8 %shard_map.105 = bf16[1,3,2,32,1024]{4,3,2,1,0:T(8,128)(2,1)} custom-call(bf16[2,32,1024]{2,1,0:T(8,128)(2,1)S(1)} %get-tuple-element.43.refs_0_, bf16[2,32,1024]{2,1,0:T(8,128)(2,1)S(1)} %collective-permute-done.11.refs_1_, bf16[2,32,1024]{2,1,0:T(8,128)(2,1)S(1)} %collective-permute-done.12.refs_2_, bf16[2,32,1024]{2,1,0:T(8,128)(2,1)S(1)} %collective-permute-done.13.refs_3_), custom_call_target="tpu_custom_call" | custom-call | bytes 1000000 | tf_op jit(solution)/shard_map/pallas_call | solution.py:477
  (1 shorter events, 0.0 us)
Async XLA Ops:
  2.1 10.9 %collective-permute-start.10 = (bf16[64,1024]{1,0:T(8,128)(2,1)}, bf16[64,1024]{1,0:T(8,128)(2,1)S(1)}, u32[]{:S(2)}, u32[]{:S(2)}) collective-permute-start(bf16[64,1024]{1,0:T(8,128)(2,1)} %bitcast.1), channel_id=1, source_target_pairs={{0,1},{1,0},{2,3},{3,2},{4,5},{5,4},{6,7},{7,6},{8,9},{9,8},{10,11... | collective-permute-start | bytes 393224 | tf_op jit(solution)/shard_map/ppermute | solution.py:390
  2.6 6.7 %collective-permute-start = (bf16[32,1152]{1,0:T(8,128)(2,1)}, bf16[32,1152]{1,0:T(8,128)(2,1)S(1)}, u32[]{:S(2)}, u32[]{:S(2)}) collective-permute-start(bf16[32,1152]{1,0:T(8,128)(2,1)} %get-tuple-element.27), channel_id=1, source_target_pairs={{0,24},{8,16},{16,8},{24,0},{1,25},{9,17},{17,9},{25,1},{2,26},{10... | collective-permute-start | bytes 221192 | tf_op jit(solution)/shard_map/ppermute | solution.py:371
  6.1 5.3 %collective-permute-start.1 = (bf16[32,1152]{1,0:T(8,128)(2,1)}, bf16[32,1152]{1,0:T(8,128)(2,1)S(1)}, u32[]{:S(2)}, u32[]{:S(2)}) collective-permute-start(bf16[32,1152]{1,0:T(8,128)(2,1)} %get-tuple-element.28), channel_id=1, source_target_pairs={{0,8},{8,0},{16,24},{24,16},{1,9},{9,1},{17,25},{25,17},{2,10},{10... | collective-permute-start | bytes 221192 | tf_op jit(solution)/shard_map/ppermute | solution.py:371
  6.7 5.7 %collective-permute-start.2 = (bf16[32,1152]{1,0:T(8,128)(2,1)}, bf16[32,1152]{1,0:T(8,128)(2,1)S(1)}, u32[]{:S(2)}, u32[]{:S(2)}) collective-permute-start(bf16[32,1152]{1,0:T(8,128)(2,1)} %get-tuple-element.29), channel_id=1, source_target_pairs={{0,16},{8,24},{16,0},{24,8},{1,17},{9,25},{17,1},{25,9},{2,18},{10... | collective-permute-start | bytes 221192 | tf_op jit(solution)/shard_map/ppermute | solution.py:371
  6.8 7.7 %collective-permute-start.9 = (bf16[64,1024]{1,0:T(8,128)(2,1)}, bf16[64,1024]{1,0:T(8,128)(2,1)S(1)}, u32[]{:S(2)}, u32[]{:S(2)}) collective-permute-start(bf16[64,1024]{1,0:T(8,128)(2,1)} %bitcast.2), channel_id=1, source_target_pairs={{0,8},{1,2},{2,1},{3,4},{4,3},{5,6},{6,5},{7,15},{8,0},{9,10},{10,... | collective-permute-start | bytes 393224 | tf_op jit(solution)/shard_map/ppermute | solution.py:390
  9.3 6.5 %collective-permute-start.8 = (bf16[64,1024]{1,0:T(8,128)(2,1)}, bf16[64,1024]{1,0:T(8,128)(2,1)S(1)}, u32[]{:S(2)}, u32[]{:S(2)}) collective-permute-start(bf16[64,1024]{1,0:T(8,128)(2,1)} %bitcast.3), channel_id=1, source_target_pairs={{0,2},{1,3},{2,0},{3,1},{4,6},{5,7},{6,4},{7,5},{8,10},{9,11},{10,... | collective-permute-start | bytes 393224 | tf_op jit(solution)/shard_map/ppermute | solution.py:390
  11.4 4.6 %collective-permute-start.7 = (bf16[64,1024]{1,0:T(8,128)(2,1)}, bf16[64,1024]{1,0:T(8,128)(2,1)S(1)}, u32[]{:S(2)}, u32[]{:S(2)}) collective-permute-start(bf16[64,1024]{1,0:T(8,128)(2,1)} %bitcast.4), channel_id=1, source_target_pairs={{0,1},{1,0},{2,4},{3,5},{4,2},{5,3},{6,7},{7,6},{8,9},{9,8},{10,12... | collective-permute-start | bytes 393224 | tf_op jit(solution)/shard_map/ppermute | solution.py:390
  11.4 0.9 %copy-start = (bf16[32,1152]{1,0:T(8,128)(2,1)S(1)}, bf16[32,1152]{1,0:T(8,128)(2,1)}, u32[]{:S(2)}) copy-start(bf16[32,1152]{1,0:T(8,128)(2,1)} %get-tuple-element.26.message) | copy-start | bytes 221188
  12.3 3.7 %copy-start.3 = (bf16[256,256]{1,0:T(8,128)(2,1)S(1)}, bf16[256,256]{1,0:T(8,128)(2,1)}, u32[]{:S(2)}) copy-start(bf16[256,256]{1,0:T(8,128)(2,1)} %constant.7.clone.left_tab) | copy-start | bytes 393220
  12.3 3.7 %copy-start.1 = (bf16[2,32,1024]{2,1,0:T(8,128)(2,1)S(1)}, bf16[2,32,1024]{2,1,0:T(8,128)(2,1)}, u32[]{:S(2)}) copy-start(bf16[2,32,1024]{2,1,0:T(8,128)(2,1)} %get-tuple-element.35) | copy-start | bytes 393220
  12.3 3.7 %copy-start.2 = (bf16[256,256]{1,0:T(8,128)(2,1)S(1)}, bf16[256,256]{1,0:T(8,128)(2,1)}, u32[]{:S(2)}) copy-start(bf16[256,256]{1,0:T(8,128)(2,1)} %constant.6.clone.right_tab) | copy-start | bytes 393220
  12.4 7.6 %collective-permute-start.3 = (bf16[80,1152]{1,0:T(8,128)(2,1)S(1)}, bf16[80,1152]{1,0:T(8,128)(2,1)S(1)}, u32[]{:S(2)}, u32[]{:S(2)}) collective-permute-start(bf16[80,1152]{1,0:T(8,128)(2,1)S(1)} %get-tuple-element.30), channel_id=1, source_target_pairs={{0,1},{1,0},{2,3},{3,2},{4,5},{5,4},{6,7},{7,6},{8,9},{9,8},{10,11... | collective-permute-start | bytes 552968 | tf_op jit(solution)/shard_map/ppermute | solution.py:390
  13.0 7.0 %collective-permute-start.4 = (bf16[80,1152]{1,0:T(8,128)(2,1)S(1)}, bf16[80,1152]{1,0:T(8,128)(2,1)S(1)}, u32[]{:S(2)}, u32[]{:S(2)}) collective-permute-start(bf16[80,1152]{1,0:T(8,128)(2,1)S(1)} %get-tuple-element.31), channel_id=1, source_target_pairs={{0,8},{1,2},{2,1},{3,4},{4,3},{5,6},{6,5},{7,15},{8,0},{9,10},{10,... | collective-permute-start | bytes 552968 | tf_op jit(solution)/shard_map/ppermute | solution.py:390
  14.5 5.5 %collective-permute-start.5 = (bf16[16,1152]{1,0:T(8,128)(2,1)S(1)}, bf16[16,1152]{1,0:T(8,128)(2,1)S(1)}, u32[]{:S(2)}, u32[]{:S(2)}) collective-permute-start(bf16[16,1152]{1,0:T(8,128)(2,1)S(1)} %get-tuple-element.32), channel_id=1, source_target_pairs={{0,2},{1,3},{2,0},{3,1},{4,6},{5,7},{6,4},{7,5},{8,10},{9,11},{10,... | collective-permute-start | bytes 110600 | tf_op jit(solution)/shard_map/ppermute | solution.py:390
  15.8 4.2 %collective-permute-start.6 = (bf16[16,1152]{1,0:T(8,128)(2,1)S(1)}, bf16[16,1152]{1,0:T(8,128)(2,1)S(1)}, u32[]{:S(2)}, u32[]{:S(2)}) collective-permute-start(bf16[16,1152]{1,0:T(8,128)(2,1)S(1)} %get-tuple-element.33), channel_id=1, source_target_pairs={{0,1},{1,0},{2,4},{3,5},{4,2},{5,3},{6,7},{7,6},{8,9},{9,8},{10,12... | collective-permute-start | bytes 110600 | tf_op jit(solution)/shard_map/ppermute | solution.py:390
  16.0 4.1 %copy-start.4 = (bf16[192,192]{1,0:T(8,128)(2,1)S(1)}, bf16[192,192]{1,0:T(8,128)(2,1)}, u32[]{:S(2)}) copy-start(bf16[192,192]{1,0:T(8,128)(2,1)} %constant.8.clone.left_tab) | copy-start | bytes 221188
  22.6 5.6 %collective-permute-start.11 = (bf16[2,32,1024]{2,1,0:T(8,128)(2,1)S(1)}, bf16[2,32,1024]{2,1,0:T(8,128)(2,1)S(1)}, u32[]{:S(2)}, u32[]{:S(2)}) collective-permute-start(bf16[2,32,1024]{2,1,0:T(8,128)(2,1)S(1)} %get-tuple-element.44), channel_id=1, source_target_pairs={{0,8},{8,0},{16,24},{24,16},{1,9},{9,1},{17,25},{25,17},{2,10},{10... | collective-permute-start | bytes 393224 | tf_op jit(solution)/shard_map/ppermute | solution.py:371
  24.2 7.8 %collective-permute-start.12 = (bf16[2,32,1024]{2,1,0:T(8,128)(2,1)S(1)}, bf16[2,32,1024]{2,1,0:T(8,128)(2,1)S(1)}, u32[]{:S(2)}, u32[]{:S(2)}) collective-permute-start(bf16[2,32,1024]{2,1,0:T(8,128)(2,1)S(1)} %get-tuple-element.45), channel_id=1, source_target_pairs={{0,16},{8,24},{16,0},{24,8},{1,17},{9,25},{17,1},{25,9},{2,18},{10... | collective-permute-start | bytes 393224 | tf_op jit(solution)/shard_map/ppermute | solution.py:371
  25.7 6.2 %collective-permute-start.13 = (bf16[2,32,1024]{2,1,0:T(8,128)(2,1)S(1)}, bf16[2,32,1024]{2,1,0:T(8,128)(2,1)S(1)}, u32[]{:S(2)}, u32[]{:S(2)}) collective-permute-start(bf16[2,32,1024]{2,1,0:T(8,128)(2,1)S(1)} %get-tuple-element.46), channel_id=1, source_target_pairs={{0,24},{8,16},{16,8},{24,0},{1,25},{9,17},{17,9},{25,1},{2,26},{10... | collective-permute-start | bytes 393224 | tf_op jit(solution)/shard_map/ppermute | solution.py:371

commit v26 on v24

--- a/solution.py
+++ b/solution.py
@@ -385,7 +385,7 @@
             elif by > 1:
                 to = (depth, band ^ 1)
             else:
-                to = (depth ^ 1, band)
+                to = (depth ^ 2, band)
             pairs.append((depth * count + band, to[0] * count + to[1]))
     return lax.ppermute(value, ("depth", "rows"), pairs)
 

time: 32.1 us -> 32.1 us (level)
  no operation moved by 1% of the time
where the time goes in v26:
time: 32.1 us; the launch traced here: 31.9 us
  starting transfers between devices  15.1 us (47%)
  waiting for transfers between devices  9.12 us (28%)
  Pallas kernels  6.66 us (21%)
  local copies, waits for them, and re-layouts  0.91 us (3%)
    ppermute x6, starting transfers between devices, over_depth(): return lax.ppermute(value, 'depth', [(i, i ^ hop) for i in range(LAYERS)])  8.31 us
    ppermute x8, starting transfers between devices, exchanged(): return lax.ppermute(value, ('depth', 'rows'), pairs)  6.81 us
    ppermute x6, waiting for transfers between devices, over_depth(): return lax.ppermute(value, 'depth', [(i, i ^ hop) for i in range(LAYERS)])  6.71 us
    pallas_call x1, Pallas kernels, body(): call(chain_kernel, [shaped((2, BAND, COLS), bf16)] * LAYERS, [vmem] * (6...  2.53 us
    ppermute x8, waiting for transfers between devices, exchanged(): return lax.ppermute(value, ('depth', 'rows'), pairs)  2.4 us
    pallas_call x1, Pallas kernels, body(): call(pack_kernel, (shaped((BAND, HALO_W), bf16),) * LAYERS + (shaped(inci...  2.08 us
    pallas_call x1, Pallas kernels, body(): call(prepare_kernel, [shaped((TILES * layer_height(0), 2 * LANES), f32),...  1.2 us
    unnamed x10, local copies, waits for them, and re-layouts  0.91 us
  transfers between devices with their start and end apart: 14, of which 6 were waited for; matrix products, arithmetic and copies ran while one was open for 0% of the time, Pallas kernels for 4%

profile of v26, /device:TPU:0, one launch (start us, length us, event | category | flops | bytes accessed | tf_op | source)
XLA Modules:
  0.0 31.9 jit_solution(2221777789950102442)
XLA Ops:
  0.0 2.1 %shard_map.100 = (bf16[32,1152]{1,0:T(8,128)(2,1)}, bf16[32,1152]{1,0:T(8,128)(2,1)}, bf16[32,1152]{1,0:T(8,128)(2,1)}, bf16[32,1152]{1,0:T(8,128)(2,1)}, bf16[2,32,1024]{2,1,0:T(8,128)(2,1)}) custom-call(f32[1,3,32,1024]{3,2,1,0:T(8,128)} %light.1, s32[1,32,64]{2,1,0:T(8,128)} %edges.1, s32[1,2]{1,0:T(1,128)} %counts.1, s32[1,2,64]{2,1,0:T(2,128)} %listed.1, ...), custom_call_target="tpu_custom_call" | custom-call | flops 10000000 | bytes 1000000 | tf_op jit(solution)/shard_map/pallas_call | solution.py:432
  2.1 0.5 %collective-permute-start.10 = (bf16[64,1024]{1,0:T(8,128)(2,1)}, bf16[64,1024]{1,0:T(8,128)(2,1)S(1)}, u32[]{:S(2)}, u32[]{:S(2)}) collective-permute-start(bf16[64,1024]{1,0:T(8,128)(2,1)} %bitcast.1), channel_id=1, source_target_pairs={{0,1},{1,0},{2,3},{3,2},{4,5},{5,4},{6,7},{7,6},{8,9},{9,8},{10,11... | collective-permute-start | bytes 393224 | tf_op jit(solution)/shard_map/ppermute | solution.py:390
  2.6 2.6 %collective-permute-start = (bf16[32,1152]{1,0:T(8,128)(2,1)}, bf16[32,1152]{1,0:T(8,128)(2,1)S(1)}, u32[]{:S(2)}, u32[]{:S(2)}) collective-permute-start(bf16[32,1152]{1,0:T(8,128)(2,1)} %get-tuple-element.27), channel_id=1, source_target_pairs={{0,8},{8,0},{16,24},{24,16},{1,9},{9,1},{17,25},{25,17},{2,10},{10... | collective-permute-start | bytes 221192 | tf_op jit(solution)/shard_map/ppermute | solution.py:371
  5.2 1.5 %collective-permute-start.1 = (bf16[32,1152]{1,0:T(8,128)(2,1)}, bf16[32,1152]{1,0:T(8,128)(2,1)S(1)}, u32[]{:S(2)}, u32[]{:S(2)}) collective-permute-start(bf16[32,1152]{1,0:T(8,128)(2,1)} %get-tuple-element.28), channel_id=1, source_target_pairs={{0,16},{8,24},{16,0},{24,8},{1,17},{9,25},{17,1},{25,9},{2,18},{10... | collective-permute-start | bytes 221192 | tf_op jit(solution)/shard_map/ppermute | solution.py:371
  6.7 0.0 collective-permute-start.2
  6.7 2.0 %collective-permute-start.9 = (bf16[64,1024]{1,0:T(8,128)(2,1)}, bf16[64,1024]{1,0:T(8,128)(2,1)S(1)}, u32[]{:S(2)}, u32[]{:S(2)}) collective-permute-start(bf16[64,1024]{1,0:T(8,128)(2,1)} %bitcast.2), channel_id=1, source_target_pairs={{0,16},{1,2},{2,1},{3,4},{4,3},{5,6},{6,5},{7,23},{8,24},{9,10},{1... | collective-permute-start | bytes 393224 | tf_op jit(solution)/shard_map/ppermute | solution.py:390
  8.7 0.0 collective-permute-done.refs_1_
  8.7 1.4 %collective-permute-start.8 = (bf16[64,1024]{1,0:T(8,128)(2,1)}, bf16[64,1024]{1,0:T(8,128)(2,1)S(1)}, u32[]{:S(2)}, u32[]{:S(2)}) collective-permute-start(bf16[64,1024]{1,0:T(8,128)(2,1)} %bitcast.3), channel_id=1, source_target_pairs={{0,2},{1,3},{2,0},{3,1},{4,6},{5,7},{6,4},{7,5},{8,10},{9,11},{10,... | collective-permute-start | bytes 393224 | tf_op jit(solution)/shard_map/ppermute | solution.py:390
  10.1 0.0 collective-permute-done.1.refs_2_
  10.1 0.1 collective-permute-start.7
  10.2 0.0 copy-start
  10.2 0.9 %copy-done = bf16[32,1152]{1,0:T(8,128)(2,1)S(1)} copy-done((bf16[32,1152]{1,0:T(8,128)(2,1)S(1)}, bf16[32,1152]{1,0:T(8,128)(2,1)}, u32[]{:S(2)}) %copy-start) | copy-done | bytes 73752
  11.1 0.0 copy-start.3
  11.1 0.0 copy-start.1
  11.1 0.0 copy-start.2
  11.1 1.1 %collective-permute-done.2.refs_3_ = bf16[32,1152]{1,0:T(8,128)(2,1)S(1)} collective-permute-done((bf16[32,1152]{1,0:T(8,128)(2,1)}, bf16[32,1152]{1,0:T(8,128)(2,1)S(1)}, u32[]{:S(2)}, u32[]{:S(2)}) %collective-permute-start.2) | collective-permute-done | bytes 73760 | tf_op jit(solution)/shard_map/ppermute | solution.py:371
  12.2 0.1 shard_map.102
  12.3 0.1 collective-permute-start.3
  12.4 0.0 collective-permute-done.10.in_chip
  12.4 2.0 %collective-permute-start.4 = (bf16[80,1152]{1,0:T(8,128)(2,1)S(1)}, bf16[80,1152]{1,0:T(8,128)(2,1)S(1)}, u32[]{:S(2)}, u32[]{:S(2)}) collective-permute-start(bf16[80,1152]{1,0:T(8,128)(2,1)S(1)} %get-tuple-element.31), channel_id=1, source_target_pairs={{0,16},{1,2},{2,1},{3,4},{4,3},{5,6},{6,5},{7,23},{8,24},{9,10},{1... | collective-permute-start | bytes 552968 | tf_op jit(solution)/shard_map/ppermute | solution.py:390
  14.4 0.0 collective-permute-done.9.cross
  14.4 0.1 collective-permute-start.5
  14.5 0.2 collective-permute-done.8.far_even
  14.7 0.7 %collective-permute-start.6 = (bf16[16,1152]{1,0:T(8,128)(2,1)S(1)}, bf16[16,1152]{1,0:T(8,128)(2,1)S(1)}, u32[]{:S(2)}, u32[]{:S(2)}) collective-permute-start(bf16[16,1152]{1,0:T(8,128)(2,1)S(1)} %get-tuple-element.33), channel_id=1, source_target_pairs={{0,1},{1,0},{2,4},{3,5},{4,2},{5,3},{6,7},{7,6},{8,9},{9,8},{10,12... | collective-permute-start | bytes 110600 | tf_op jit(solution)/shard_map/ppermute | solution.py:390
  15.4 0.0 collective-permute-done.7.far_odd
  15.4 0.0 copy-done.3
  15.4 0.0 copy-done.1
  15.4 0.0 copy-done.2
  15.4 0.0 copy-start.4
  15.4 1.2 %shard_map.103 = (f32[1024,256]{1,0:T(8,128)S(1)}, f32[2,128,1024]{2,1,0:T(8,128)S(1)}, f32[128,1024]{1,0:T(8,128)S(1)}, bf16[3,256,512]{2,1,0:T(8,128)(2,1)S(1)...) custom-call(bf16[4,32,1152]{2,1,0:T(8,128)(2,1)S(1)} %get-tuple-element.34.own, ...), custom_call_target="tpu_custom_call" | custom-call | flops 1000000000 | bytes 3000000 | tf_op jit(solution)/shard_map/pallas_call | solution.py:453
  16.6 2.2 %collective-permute-done.5.far_even = bf16[16,1152]{1,0:T(8,128)(2,1)S(1)} collective-permute-done((bf16[16,1152]{1,0:T(8,128)(2,1)S(1)}, bf16[16,1152]{1,0:T(8,128)(2,1)S(1)}, u32[]{:S(2)}, u32[]{:S(2)}) %collective-permute-start.5) | collective-permute-done | bytes 36896 | tf_op jit(solution)/shard_map/ppermute | solution.py:390
  18.8 0.0 collective-permute-done.6.far_odd
  18.8 0.0 collective-permute-done.3.in_chip
  18.8 0.0 collective-permute-done.4.cross
  18.8 0.0 copy-done.4
  18.8 2.5 %shard_map.104 = (bf16[2,32,1024]{2,1,0:T(8,128)(2,1)S(1)}, bf16[2,32,1024]{2,1,0:T(8,128)(2,1)S(1)}, bf16[2,32,1024]{2,1,0:T(8,128)(2,1)S(1)}, bf16[2,32,1024]{2,1,0:T(8,128)(2,1)S(1)}) custom-call(bf16[80,1152]{1,0:T(8,128)(2,1)S(1)} %collective-permute-done.3.in_chip, bf16[80,1152]{1,0:T(8,128)(2,1)S(1)} %collective-permute-done.4.cross, ...), custom_call_target="tpu_custom_call" | custom-call | flops 2000000000 | bytes 3000000 | tf_op jit(solution)/shard_map/pallas_call | solution.py:467
  21.4 1.6 %collective-permute-start.11 = (bf16[2,32,1024]{2,1,0:T(8,128)(2,1)S(1)}, bf16[2,32,1024]{2,1,0:T(8,128)(2,1)S(1)}, u32[]{:S(2)}, u32[]{:S(2)}) collective-permute-start(bf16[2,32,1024]{2,1,0:T(8,128)(2,1)S(1)} %get-tuple-element.44), channel_id=1, source_target_pairs={{0,8},{8,0},{16,24},{24,16},{1,9},{9,1},{17,25},{25,17},{2,10},{10... | collective-permute-start | bytes 393224 | tf_op jit(solution)/shard_map/ppermute | solution.py:371
  23.0 1.6 %collective-permute-start.12 = (bf16[2,32,1024]{2,1,0:T(8,128)(2,1)S(1)}, bf16[2,32,1024]{2,1,0:T(8,128)(2,1)S(1)}, u32[]{:S(2)}, u32[]{:S(2)}) collective-permute-start(bf16[2,32,1024]{2,1,0:T(8,128)(2,1)S(1)} %get-tuple-element.45), channel_id=1, source_target_pairs={{0,16},{8,24},{16,0},{24,8},{1,17},{9,25},{17,1},{25,9},{2,18},{10... | collective-permute-start | bytes 393224 | tf_op jit(solution)/shard_map/ppermute | solution.py:371
  24.6 0.9 %collective-permute-start.13 = (bf16[2,32,1024]{2,1,0:T(8,128)(2,1)S(1)}, bf16[2,32,1024]{2,1,0:T(8,128)(2,1)S(1)}, u32[]{:S(2)}, u32[]{:S(2)}) collective-permute-start(bf16[2,32,1024]{2,1,0:T(8,128)(2,1)S(1)} %get-tuple-element.46), channel_id=1, source_target_pairs={{0,24},{8,16},{16,8},{24,0},{1,25},{9,17},{17,9},{25,1},{2,26},{10... | collective-permute-start | bytes 393224 | tf_op jit(solution)/shard_map/ppermute | solution.py:371
  25.6 1.4 %collective-permute-done.11.refs_1_ = bf16[2,32,1024]{2,1,0:T(8,128)(2,1)S(1)} collective-permute-done((bf16[2,32,1024]{2,1,0:T(8,128)(2,1)S(1)}, bf16[2,32,1024]{2,1,0:T(8,128)(2,1)S(1)}, u32[]{:S(2)}, u32[]{:S(2)}) %collective-permute-start.11) | collective-permute-done | bytes 131104 | tf_op jit(solution)/shard_map/ppermute | solution.py:371
  27.0 2.5 %collective-permute-done.12.refs_2_ = bf16[2,32,1024]{2,1,0:T(8,128)(2,1)S(1)} collective-permute-done((bf16[2,32,1024]{2,1,0:T(8,128)(2,1)S(1)}, bf16[2,32,1024]{2,1,0:T(8,128)(2,1)S(1)}, u32[]{:S(2)}, u32[]{:S(2)}) %collective-permute-start.12) | collective-permute-done | bytes 131104 | tf_op jit(solution)/shard_map/ppermute | solution.py:371
  29.5 1.7 %collective-permute-done.13.refs_3_ = bf16[2,32,1024]{2,1,0:T(8,128)(2,1)S(1)} collective-permute-done((bf16[2,32,1024]{2,1,0:T(8,128)(2,1)S(1)}, bf16[2,32,1024]{2,1,0:T(8,128)(2,1)S(1)}, u32[]{:S(2)}, u32[]{:S(2)}) %collective-permute-start.13) | collective-permute-done | bytes 131104 | tf_op jit(solution)/shard_map/ppermute | solution.py:371
  31.1 0.8 %shard_map.105 = bf16[1,3,2,32,1024]{4,3,2,1,0:T(8,128)(2,1)} custom-call(bf16[2,32,1024]{2,1,0:T(8,128)(2,1)S(1)} %get-tuple-element.43.refs_0_, bf16[2,32,1024]{2,1,0:T(8,128)(2,1)S(1)} %collective-permute-done.11.refs_1_, bf16[2,32,1024]{2,1,0:T(8,128)(2,1)S(1)} %collective-permute-done.12.refs_2_, bf16[2,32,1024]{2,1,0:T(8,128)(2,1)S(1)} %collective-permute-done.13.refs_3_), custom_call_target="tpu_custom_call" | custom-call | bytes 1000000 | tf_op jit(solution)/shard_map/pallas_call | solution.py:476
  (1 shorter events, 0.0 us)
Async XLA Ops:
  2.1 10.3 %collective-permute-start.10 = (bf16[64,1024]{1,0:T(8,128)(2,1)}, bf16[64,1024]{1,0:T(8,128)(2,1)S(1)}, u32[]{:S(2)}, u32[]{:S(2)}) collective-permute-start(bf16[64,1024]{1,0:T(8,128)(2,1)} %bitcast.1), channel_id=1, source_target_pairs={{0,1},{1,0},{2,3},{3,2},{4,5},{5,4},{6,7},{7,6},{8,9},{9,8},{10,11... | collective-permute-start | bytes 393224 | tf_op jit(solution)/shard_map/ppermute | solution.py:390
  2.6 6.1 %collective-permute-start = (bf16[32,1152]{1,0:T(8,128)(2,1)}, bf16[32,1152]{1,0:T(8,128)(2,1)S(1)}, u32[]{:S(2)}, u32[]{:S(2)}) collective-permute-start(bf16[32,1152]{1,0:T(8,128)(2,1)} %get-tuple-element.27), channel_id=1, source_target_pairs={{0,8},{8,0},{16,24},{24,16},{1,9},{9,1},{17,25},{25,17},{2,10},{10... | collective-permute-start | bytes 221192 | tf_op jit(solution)/shard_map/ppermute | solution.py:371
  5.2 4.9 %collective-permute-start.1 = (bf16[32,1152]{1,0:T(8,128)(2,1)}, bf16[32,1152]{1,0:T(8,128)(2,1)S(1)}, u32[]{:S(2)}, u32[]{:S(2)}) collective-permute-start(bf16[32,1152]{1,0:T(8,128)(2,1)} %get-tuple-element.28), channel_id=1, source_target_pairs={{0,16},{8,24},{16,0},{24,8},{1,17},{9,25},{17,1},{25,9},{2,18},{10... | collective-permute-start | bytes 221192 | tf_op jit(solution)/shard_map/ppermute | solution.py:371
  6.7 5.5 %collective-permute-start.2 = (bf16[32,1152]{1,0:T(8,128)(2,1)}, bf16[32,1152]{1,0:T(8,128)(2,1)S(1)}, u32[]{:S(2)}, u32[]{:S(2)}) collective-permute-start(bf16[32,1152]{1,0:T(8,128)(2,1)} %get-tuple-element.29), channel_id=1, source_target_pairs={{0,24},{8,16},{16,8},{24,0},{1,25},{9,17},{17,9},{25,1},{2,26},{10... | collective-permute-start | bytes 221192 | tf_op jit(solution)/shard_map/ppermute | solution.py:371
  6.7 7.7 %collective-permute-start.9 = (bf16[64,1024]{1,0:T(8,128)(2,1)}, bf16[64,1024]{1,0:T(8,128)(2,1)S(1)}, u32[]{:S(2)}, u32[]{:S(2)}) collective-permute-start(bf16[64,1024]{1,0:T(8,128)(2,1)} %bitcast.2), channel_id=1, source_target_pairs={{0,16},{1,2},{2,1},{3,4},{4,3},{5,6},{6,5},{7,23},{8,24},{9,10},{1... | collective-permute-start | bytes 393224 | tf_op jit(solution)/shard_map/ppermute | solution.py:390
  8.7 6.0 %collective-permute-start.8 = (bf16[64,1024]{1,0:T(8,128)(2,1)}, bf16[64,1024]{1,0:T(8,128)(2,1)S(1)}, u32[]{:S(2)}, u32[]{:S(2)}) collective-permute-start(bf16[64,1024]{1,0:T(8,128)(2,1)} %bitcast.3), channel_id=1, source_target_pairs={{0,2},{1,3},{2,0},{3,1},{4,6},{5,7},{6,4},{7,5},{8,10},{9,11},{10,... | collective-permute-start | bytes 393224 | tf_op jit(solution)/shard_map/ppermute | solution.py:390
  10.1 5.3 %collective-permute-start.7 = (bf16[64,1024]{1,0:T(8,128)(2,1)}, bf16[64,1024]{1,0:T(8,128)(2,1)S(1)}, u32[]{:S(2)}, u32[]{:S(2)}) collective-permute-start(bf16[64,1024]{1,0:T(8,128)(2,1)} %bitcast.4), channel_id=1, source_target_pairs={{0,1},{1,0},{2,4},{3,5},{4,2},{5,3},{6,7},{7,6},{8,9},{9,8},{10,12... | collective-permute-start | bytes 393224 | tf_op jit(solution)/shard_map/ppermute | solution.py:390
  10.2 0.9 %copy-start = (bf16[32,1152]{1,0:T(8,128)(2,1)S(1)}, bf16[32,1152]{1,0:T(8,128)(2,1)}, u32[]{:S(2)}) copy-start(bf16[32,1152]{1,0:T(8,128)(2,1)} %get-tuple-element.26.message) | copy-start | bytes 221188
  11.1 4.3 %copy-start.3 = (bf16[256,256]{1,0:T(8,128)(2,1)S(1)}, bf16[256,256]{1,0:T(8,128)(2,1)}, u32[]{:S(2)}) copy-start(bf16[256,256]{1,0:T(8,128)(2,1)} %constant.7.clone.left_tab) | copy-start | bytes 393220
  11.1 4.3 %copy-start.1 = (bf16[2,32,1024]{2,1,0:T(8,128)(2,1)S(1)}, bf16[2,32,1024]{2,1,0:T(8,128)(2,1)}, u32[]{:S(2)}) copy-start(bf16[2,32,1024]{2,1,0:T(8,128)(2,1)} %get-tuple-element.35) | copy-start | bytes 393220
  11.1 4.3 %copy-start.2 = (bf16[256,256]{1,0:T(8,128)(2,1)S(1)}, bf16[256,256]{1,0:T(8,128)(2,1)}, u32[]{:S(2)}) copy-start(bf16[256,256]{1,0:T(8,128)(2,1)} %constant.6.clone.right_tab) | copy-start | bytes 393220
  12.3 6.5 %collective-permute-start.3 = (bf16[80,1152]{1,0:T(8,128)(2,1)S(1)}, bf16[80,1152]{1,0:T(8,128)(2,1)S(1)}, u32[]{:S(2)}, u32[]{:S(2)}) collective-permute-start(bf16[80,1152]{1,0:T(8,128)(2,1)S(1)} %get-tuple-element.30), channel_id=1, source_target_pairs={{0,1},{1,0},{2,3},{3,2},{4,5},{5,4},{6,7},{7,6},{8,9},{9,8},{10,11... | collective-permute-start | bytes 552968 | tf_op jit(solution)/shard_map/ppermute | solution.py:390
  12.4 6.4 %collective-permute-start.4 = (bf16[80,1152]{1,0:T(8,128)(2,1)S(1)}, bf16[80,1152]{1,0:T(8,128)(2,1)S(1)}, u32[]{:S(2)}, u32[]{:S(2)}) collective-permute-start(bf16[80,1152]{1,0:T(8,128)(2,1)S(1)} %get-tuple-element.31), channel_id=1, source_target_pairs={{0,16},{1,2},{2,1},{3,4},{4,3},{5,6},{6,5},{7,23},{8,24},{9,10},{1... | collective-permute-start | bytes 552968 | tf_op jit(solution)/shard_map/ppermute | solution.py:390
  14.4 4.4 %collective-permute-start.5 = (bf16[16,1152]{1,0:T(8,128)(2,1)S(1)}, bf16[16,1152]{1,0:T(8,128)(2,1)S(1)}, u32[]{:S(2)}, u32[]{:S(2)}) collective-permute-start(bf16[16,1152]{1,0:T(8,128)(2,1)S(1)} %get-tuple-element.32), channel_id=1, source_target_pairs={{0,2},{1,3},{2,0},{3,1},{4,6},{5,7},{6,4},{7,5},{8,10},{9,11},{10,... | collective-permute-start | bytes 110600 | tf_op jit(solution)/shard_map/ppermute | solution.py:390
  14.7 4.1 %collective-permute-start.6 = (bf16[16,1152]{1,0:T(8,128)(2,1)S(1)}, bf16[16,1152]{1,0:T(8,128)(2,1)S(1)}, u32[]{:S(2)}, u32[]{:S(2)}) collective-permute-start(bf16[16,1152]{1,0:T(8,128)(2,1)S(1)} %get-tuple-element.33), channel_id=1, source_target_pairs={{0,1},{1,0},{2,4},{3,5},{4,2},{5,3},{6,7},{7,6},{8,9},{9,8},{10,12... | collective-permute-start | bytes 110600 | tf_op jit(solution)/shard_map/ppermute | solution.py:390
  15.4 3.4 %copy-start.4 = (bf16[192,192]{1,0:T(8,128)(2,1)S(1)}, bf16[192,192]{1,0:T(8,128)(2,1)}, u32[]{:S(2)}) copy-start(bf16[192,192]{1,0:T(8,128)(2,1)} %constant.8.clone.left_tab) | copy-start | bytes 221188
  21.4 5.6 %collective-permute-start.11 = (bf16[2,32,1024]{2,1,0:T(8,128)(2,1)S(1)}, bf16[2,32,1024]{2,1,0:T(8,128)(2,1)S(1)}, u32[]{:S(2)}, u32[]{:S(2)}) collective-permute-start(bf16[2,32,1024]{2,1,0:T(8,128)(2,1)S(1)} %get-tuple-element.44), channel_id=1, source_target_pairs={{0,8},{8,0},{16,24},{24,16},{1,9},{9,1},{17,25},{25,17},{2,10},{10... | collective-permute-start | bytes 393224 | tf_op jit(solution)/shard_map/ppermute | solution.py:371
  23.0 6.5 %collective-permute-start.12 = (bf16[2,32,1024]{2,1,0:T(8,128)(2,1)S(1)}, bf16[2,32,1024]{2,1,0:T(8,128)(2,1)S(1)}, u32[]{:S(2)}, u32[]{:S(2)}) collective-permute-start(bf16[2,32,1024]{2,1,0:T(8,128)(2,1)S(1)} %get-tuple-element.45), channel_id=1, source_target_pairs={{0,16},{8,24},{16,0},{24,8},{1,17},{9,25},{17,1},{25,9},{2,18},{10... | collective-permute-start | bytes 393224 | tf_op jit(solution)/shard_map/ppermute | solution.py:371
  24.6 6.5 %collective-permute-start.13 = (bf16[2,32,1024]{2,1,0:T(8,128)(2,1)S(1)}, bf16[2,32,1024]{2,1,0:T(8,128)(2,1)S(1)}, u32[]{:S(2)}, u32[]{:S(2)}) collective-permute-start(bf16[2,32,1024]{2,1,0:T(8,128)(2,1)S(1)} %get-tuple-element.46), channel_id=1, source_target_pairs={{0,24},{8,16},{16,8},{24,0},{1,25},{9,17},{17,9},{25,1},{2,26},{10... | collective-permute-start | bytes 393224 | tf_op jit(solution)/shard_map/ppermute | solution.py:371

commit v27 on v24

--- a/solution.py
+++ b/solution.py
@@ -1,3 +1,4 @@
+import functools
 import math
 
 import jax
@@ -353,18 +354,21 @@
             out[part] = field[layer, part, pl.ds(start, BAND)]
 
 
-def home_kernel(*refs):
-    arrived, out, sems = refs[:LAYERS], refs[LAYERS], refs[LAYERS + 1]
+def home_kernel(hops, *refs):
+    arrived, out, sems = refs[: len(hops)], refs[-2], refs[-1]
     depth = lax.axis_index("depth")
-    for colour in range(COLORS):
-        for hop in range(LAYERS):
-
-            @pl.when((depth ^ hop) == colour)
-            def begin(hop=hop, colour=colour):
-                pltpu.make_async_copy(arrived[hop], out.at[0, colour], sems.at[colour]).start()
-
-    for colour in range(COLORS):
-        pltpu.make_async_copy(arrived[0], out.at[0, colour], sems.at[colour]).wait()
+    for finish in (False, True):
+        for place, hop in enumerate(hops):
+
+            @pl.when((depth ^ hop) < COLORS)
+            def write(place=place, hop=hop):
+                copy = pltpu.make_async_copy(
+                    arrived[place], out.at[0, depth ^ hop], sems.at[place]
+                )
+                if finish:
+                    copy.wait()
+                else:
+                    copy.start()
 
 
 def over_depth(value, hop):
@@ -401,7 +405,7 @@
 
 def call(
     kernel, out_shape, in_specs, scratch=(), flops=0, moved=10**6, limit=VMEM_LIMIT,
-    out_space=pltpu.VMEM,
+    out_space=pltpu.VMEM, aliases=None,
 ):
     vmem = pl.BlockSpec(memory_space=out_space)
     many = isinstance(out_shape, (tuple, list))
@@ -411,6 +415,7 @@
         in_specs=in_specs,
         out_specs=(vmem,) * len(out_shape) if many else vmem,
         scratch_shapes=scratch,
+        input_output_aliases=aliases or {},
         compiler_params=pltpu.CompilerParams(vmem_limit_bytes=limit),
         cost_estimate=pl.CostEstimate(flops=flops, bytes_accessed=moved, transcendentals=0),
     )
@@ -473,13 +478,23 @@
         moved=3 * 10**6,
     )(*halos, jnp.asarray(left_table(halo_rows)), right_tab, *made)
     returned = [results[0]] + [over_depth(results[hop], hop) for hop in range(1, LAYERS)]
+    home = shaped((1, COLORS, 2, BAND, COLS), bf16)
+    early = (0, 1, 2)
+    partly = call(
+        functools.partial(home_kernel, early),
+        home,
+        [vmem] * len(early),
+        [pltpu.SemaphoreType.DMA((len(early),))],
+        out_space=pltpu.HBM,
+    )(*(returned[hop] for hop in early))
     return call(
-        home_kernel,
-        shaped((1, COLORS, 2, BAND, COLS), bf16),
-        [vmem] * LAYERS,
-        [pltpu.SemaphoreType.DMA((COLORS,))],
+        functools.partial(home_kernel, (3,)),
+        home,
+        [vmem, hbm],
+        [pltpu.SemaphoreType.DMA((1,))],
         out_space=pltpu.HBM,
-    )(*returned)
+        aliases={1: 0},
+    )(returned[3], partly)
 
 
 def solution(mesh):

time: 32.1 us -> 31.3 us (0.975)
  waiting for transfers between devices: 9 us -> 8.23 us
    ppermute x6, waiting for transfers between devices: 6.66 us -> 5.88 us  [over_depth(): return lax.ppermute(value, 'depth', [(i, i ^ hop) for i in range(LAYERS)])]
    pallas_call x1 -> x2, Pallas kernels: 0.77 us -> 0.77 us  [the longest x1 0.77 us: body(): call(functools.partial(home_kernel, early), home, [vmem] * len(early), [p...]
  transfers between devices with their start and end apart: 14 -> 14, of which waited for: 6 -> 6; matrix products, arithmetic and copies ran while one was open for 0% -> 0% of each run, Pallas kernels for 4% -> 7%
where the time goes in v27:
time: 31.3 us; the launch traced here: 31.2 us
  starting transfers between devices  15.2 us (49%)
  waiting for transfers between devices  8.23 us (26%)
  Pallas kernels  6.65 us (21%)
  local copies, waits for them, and re-layouts  0.91 us (3%)
    ppermute x6, starting transfers between devices, over_depth(): return lax.ppermute(value, 'depth', [(i, i ^ hop) for i in range(LAYERS)])  8.38 us
    ppermute x8, starting transfers between devices, exchanged(): return lax.ppermute(value, ('depth', 'rows'), pairs)  6.87 us
    ppermute x6, waiting for transfers between devices, over_depth(): return lax.ppermute(value, 'depth', [(i, i ^ hop) for i in range(LAYERS)])  5.88 us
    pallas_call x1, Pallas kernels, body(): call(chain_kernel, [shaped((2, BAND, COLS), bf16)] * LAYERS, [vmem] * (6...  2.52 us
    ppermute x8, waiting for transfers between devices, exchanged(): return lax.ppermute(value, ('depth', 'rows'), pairs)  2.35 us
    pallas_call x1, Pallas kernels, body(): call(pack_kernel, (shaped((BAND, HALO_W), bf16),) * LAYERS + (shaped(inci...  2.08 us
    pallas_call x1, Pallas kernels, body(): call(prepare_kernel, [shaped((TILES * layer_height(0), 2 * LANES), f32),...  1.2 us
    unnamed x10, local copies, waits for them, and re-layouts  0.91 us
  transfers between devices with their start and end apart: 14, of which 6 were waited for; matrix products, arithmetic and copies ran while one was open for 0% of the time, Pallas kernels for 7%

profile of v27, /device:TPU:0, one launch (start us, length us, event | category | flops | bytes accessed | tf_op | source)
XLA Modules:
  0.0 31.2 jit_solution(980324141851638937)
XLA Ops:
  0.0 2.1 %shard_map.100 = (bf16[32,1152]{1,0:T(8,128)(2,1)}, bf16[32,1152]{1,0:T(8,128)(2,1)}, bf16[32,1152]{1,0:T(8,128)(2,1)}, bf16[32,1152]{1,0:T(8,128)(2,1)}, bf16[2,32,1024]{2,1,0:T(8,128)(2,1)}) custom-call(f32[1,3,32,1024]{3,2,1,0:T(8,128)} %light.1, s32[1,32,64]{2,1,0:T(8,128)} %edges.1, s32[1,2]{1,0:T(1,128)} %counts.1, s32[1,2,64]{2,1,0:T(2,128)} %listed.1, ...), custom_call_target="tpu_custom_call" | custom-call | flops 10000000 | bytes 1000000 | tf_op jit(solution)/shard_map/pallas_call | solution.py:437
  2.1 0.5 %collective-permute-start.10 = (bf16[64,1024]{1,0:T(8,128)(2,1)}, bf16[64,1024]{1,0:T(8,128)(2,1)S(1)}, u32[]{:S(2)}, u32[]{:S(2)}) collective-permute-start(bf16[64,1024]{1,0:T(8,128)(2,1)} %bitcast.1), channel_id=1, source_target_pairs={{0,1},{1,0},{2,3},{3,2},{4,5},{5,4},{6,7},{7,6},{8,9},{9,8},{10,11... | collective-permute-start | bytes 393224 | tf_op jit(solution)/shard_map/ppermute | solution.py:394
  2.6 2.6 %collective-permute-start = (bf16[32,1152]{1,0:T(8,128)(2,1)}, bf16[32,1152]{1,0:T(8,128)(2,1)S(1)}, u32[]{:S(2)}, u32[]{:S(2)}) collective-permute-start(bf16[32,1152]{1,0:T(8,128)(2,1)} %get-tuple-element.27), channel_id=1, source_target_pairs={{0,8},{8,0},{16,24},{24,16},{1,9},{9,1},{17,25},{25,17},{2,10},{10... | collective-permute-start | bytes 221192 | tf_op jit(solution)/shard_map/ppermute | solution.py:375
  5.2 1.5 %collective-permute-start.1 = (bf16[32,1152]{1,0:T(8,128)(2,1)}, bf16[32,1152]{1,0:T(8,128)(2,1)S(1)}, u32[]{:S(2)}, u32[]{:S(2)}) collective-permute-start(bf16[32,1152]{1,0:T(8,128)(2,1)} %get-tuple-element.28), channel_id=1, source_target_pairs={{0,16},{8,24},{16,0},{24,8},{1,17},{9,25},{17,1},{25,9},{2,18},{10... | collective-permute-start | bytes 221192 | tf_op jit(solution)/shard_map/ppermute | solution.py:375
  6.7 0.0 collective-permute-start.2
  6.7 1.9 %collective-permute-start.9 = (bf16[64,1024]{1,0:T(8,128)(2,1)}, bf16[64,1024]{1,0:T(8,128)(2,1)S(1)}, u32[]{:S(2)}, u32[]{:S(2)}) collective-permute-start(bf16[64,1024]{1,0:T(8,128)(2,1)} %bitcast.2), channel_id=1, source_target_pairs={{0,8},{1,2},{2,1},{3,4},{4,3},{5,6},{6,5},{7,15},{8,0},{9,10},{10,... | collective-permute-start | bytes 393224 | tf_op jit(solution)/shard_map/ppermute | solution.py:394
  8.7 0.0 collective-permute-done.refs_1_
  8.7 1.4 %collective-permute-start.8 = (bf16[64,1024]{1,0:T(8,128)(2,1)}, bf16[64,1024]{1,0:T(8,128)(2,1)S(1)}, u32[]{:S(2)}, u32[]{:S(2)}) collective-permute-start(bf16[64,1024]{1,0:T(8,128)(2,1)} %bitcast.3), channel_id=1, source_target_pairs={{0,2},{1,3},{2,0},{3,1},{4,6},{5,7},{6,4},{7,5},{8,10},{9,11},{10,... | collective-permute-start | bytes 393224 | tf_op jit(solution)/shard_map/ppermute | solution.py:394
  10.1 0.0 collective-permute-done.1.refs_2_
  10.1 0.1 collective-permute-start.7
  10.2 0.0 copy-start
  10.2 0.9 %copy-done = bf16[32,1152]{1,0:T(8,128)(2,1)S(1)} copy-done((bf16[32,1152]{1,0:T(8,128)(2,1)S(1)}, bf16[32,1152]{1,0:T(8,128)(2,1)}, u32[]{:S(2)}) %copy-start) | copy-done | bytes 73752
  11.1 0.0 copy-start.3
  11.1 0.0 copy-start.1
  11.1 0.0 copy-start.2
  11.1 1.1 %collective-permute-done.2.refs_3_ = bf16[32,1152]{1,0:T(8,128)(2,1)S(1)} collective-permute-done((bf16[32,1152]{1,0:T(8,128)(2,1)}, bf16[32,1152]{1,0:T(8,128)(2,1)S(1)}, u32[]{:S(2)}, u32[]{:S(2)}) %collective-permute-start.2) | collective-permute-done | bytes 73760 | tf_op jit(solution)/shard_map/ppermute | solution.py:375
  12.2 0.1 shard_map.102
  12.2 0.1 collective-permute-start.3
  12.3 0.0 collective-permute-done.10.in_chip
  12.3 1.0 %collective-permute-start.4 = (bf16[80,1152]{1,0:T(8,128)(2,1)S(1)}, bf16[80,1152]{1,0:T(8,128)(2,1)S(1)}, u32[]{:S(2)}, u32[]{:S(2)}) collective-permute-start(bf16[80,1152]{1,0:T(8,128)(2,1)S(1)} %get-tuple-element.31), channel_id=1, source_target_pairs={{0,8},{1,2},{2,1},{3,4},{4,3},{5,6},{6,5},{7,15},{8,0},{9,10},{10,... | collective-permute-start | bytes 552968 | tf_op jit(solution)/shard_map/ppermute | solution.py:394
  13.3 0.0 collective-permute-done.9.cross
  13.3 1.2 %collective-permute-start.5 = (bf16[16,1152]{1,0:T(8,128)(2,1)S(1)}, bf16[16,1152]{1,0:T(8,128)(2,1)S(1)}, u32[]{:S(2)}, u32[]{:S(2)}) collective-permute-start(bf16[16,1152]{1,0:T(8,128)(2,1)S(1)} %get-tuple-element.32), channel_id=1, source_target_pairs={{0,2},{1,3},{2,0},{3,1},{4,6},{5,7},{6,4},{7,5},{8,10},{9,11},{10,... | collective-permute-start | bytes 110600 | tf_op jit(solution)/shard_map/ppermute | solution.py:394
  14.5 0.2 collective-permute-done.8.far_even
  14.7 0.7 %collective-permute-start.6 = (bf16[16,1152]{1,0:T(8,128)(2,1)S(1)}, bf16[16,1152]{1,0:T(8,128)(2,1)S(1)}, u32[]{:S(2)}, u32[]{:S(2)}) collective-permute-start(bf16[16,1152]{1,0:T(8,128)(2,1)S(1)} %get-tuple-element.33), channel_id=1, source_target_pairs={{0,1},{1,0},{2,4},{3,5},{4,2},{5,3},{6,7},{7,6},{8,9},{9,8},{10,12... | collective-permute-start | bytes 110600 | tf_op jit(solution)/shard_map/ppermute | solution.py:394
  15.4 0.0 collective-permute-done.7.far_odd
  15.4 0.0 copy-done.3
  15.4 0.0 copy-done.1
  15.4 0.0 copy-done.2
  15.4 0.0 copy-start.4
  15.4 1.2 %shard_map.103 = (f32[1024,256]{1,0:T(8,128)S(1)}, f32[2,128,1024]{2,1,0:T(8,128)S(1)}, f32[128,1024]{1,0:T(8,128)S(1)}, bf16[3,256,512]{2,1,0:T(8,128)(2,1)S(1)...) custom-call(bf16[4,32,1152]{2,1,0:T(8,128)(2,1)S(1)} %get-tuple-element.34.own, ...), custom_call_target="tpu_custom_call" | custom-call | flops 1000000000 | bytes 3000000 | tf_op jit(solution)/shard_map/pallas_call | solution.py:458
  16.6 2.1 %collective-permute-done.5.far_even = bf16[16,1152]{1,0:T(8,128)(2,1)S(1)} collective-permute-done((bf16[16,1152]{1,0:T(8,128)(2,1)S(1)}, bf16[16,1152]{1,0:T(8,128)(2,1)S(1)}, u32[]{:S(2)}, u32[]{:S(2)}) %collective-permute-start.5) | collective-permute-done | bytes 36896 | tf_op jit(solution)/shard_map/ppermute | solution.py:394
  18.7 0.0 collective-permute-done.6.far_odd
  18.7 0.0 collective-permute-done.3.in_chip
  18.8 0.0 collective-permute-done.4.cross
  18.8 0.0 copy-done.4
  18.8 2.5 %shard_map.104 = (bf16[2,32,1024]{2,1,0:T(8,128)(2,1)S(1)}, bf16[2,32,1024]{2,1,0:T(8,128)(2,1)S(1)}, bf16[2,32,1024]{2,1,0:T(8,128)(2,1)S(1)}, bf16[2,32,1024]{2,1,0:T(8,128)(2,1)S(1)}) custom-call(bf16[80,1152]{1,0:T(8,128)(2,1)S(1)} %collective-permute-done.3.in_chip, bf16[80,1152]{1,0:T(8,128)(2,1)S(1)} %collective-permute-done.4.cross, ...), custom_call_target="tpu_custom_call" | custom-call | flops 2000000000 | bytes 3000000 | tf_op jit(solution)/shard_map/pallas_call | solution.py:472
  21.3 1.7 %collective-permute-start.12 = (bf16[2,32,1024]{2,1,0:T(8,128)(2,1)S(1)}, bf16[2,32,1024]{2,1,0:T(8,128)(2,1)S(1)}, u32[]{:S(2)}, u32[]{:S(2)}) collective-permute-start(bf16[2,32,1024]{2,1,0:T(8,128)(2,1)S(1)} %get-tuple-element.45), channel_id=1, source_target_pairs={{0,8},{8,0},{16,24},{24,16},{1,9},{9,1},{17,25},{25,17},{2,10},{10... | collective-permute-start | bytes 393224 | tf_op jit(solution)/shard_map/ppermute | solution.py:375
  23.0 1.6 %collective-permute-start.13 = (bf16[2,32,1024]{2,1,0:T(8,128)(2,1)S(1)}, bf16[2,32,1024]{2,1,0:T(8,128)(2,1)S(1)}, u32[]{:S(2)}, u32[]{:S(2)}) collective-permute-start(bf16[2,32,1024]{2,1,0:T(8,128)(2,1)S(1)} %get-tuple-element.46), channel_id=1, source_target_pairs={{0,16},{8,24},{16,0},{24,8},{1,17},{9,25},{17,1},{25,9},{2,18},{10... | collective-permute-start | bytes 393224 | tf_op jit(solution)/shard_map/ppermute | solution.py:375
  24.6 0.9 %collective-permute-start.11 = (bf16[2,32,1024]{2,1,0:T(8,128)(2,1)S(1)}, bf16[2,32,1024]{2,1,0:T(8,128)(2,1)S(1)}, u32[]{:S(2)}, u32[]{:S(2)}) collective-permute-start(bf16[2,32,1024]{2,1,0:T(8,128)(2,1)S(1)} %get-tuple-element.43), channel_id=1, source_target_pairs={{0,24},{8,16},{16,8},{24,0},{1,25},{9,17},{17,9},{25,1},{2,26},{10... | collective-permute-start | bytes 393224 | tf_op jit(solution)/shard_map/ppermute | solution.py:375
  25.6 1.3 %collective-permute-done.12.refs_1_ = bf16[2,32,1024]{2,1,0:T(8,128)(2,1)S(1)} collective-permute-done((bf16[2,32,1024]{2,1,0:T(8,128)(2,1)S(1)}, bf16[2,32,1024]{2,1,0:T(8,128)(2,1)S(1)}, u32[]{:S(2)}, u32[]{:S(2)}) %collective-permute-start.12) | collective-permute-done | bytes 131104 | tf_op jit(solution)/shard_map/ppermute | solution.py:375
  26.8 2.7 %collective-permute-done.13.refs_2_ = bf16[2,32,1024]{2,1,0:T(8,128)(2,1)S(1)} collective-permute-done((bf16[2,32,1024]{2,1,0:T(8,128)(2,1)S(1)}, bf16[2,32,1024]{2,1,0:T(8,128)(2,1)S(1)}, u32[]{:S(2)}, u32[]{:S(2)}) %collective-permute-start.13) | collective-permute-done | bytes 131104 | tf_op jit(solution)/shard_map/ppermute | solution.py:375
  29.5 0.8 %shard_map.105.refs_1_ = bf16[1,3,2,32,1024]{4,3,2,1,0:T(8,128)(2,1)} custom-call(bf16[2,32,1024]{2,1,0:T(8,128)(2,1)S(1)} %get-tuple-element.44.refs_0_, bf16[2,32,1024]{2,1,0:T(8,128)(2,1)S(1)} %collective-permute-done.12.refs_1_, bf16[2,32,1024]{2,1,0:T(8,128)(2,1)S(1)} %collective-permute-done.13.refs_2_), custom_call_target="tpu_custom_call" | custom-call | bytes 1000000 | tf_op jit(solution)/shard_map/pallas_call | solution.py:483
  30.2 0.9 %collective-permute-done.11.refs_0_ = bf16[2,32,1024]{2,1,0:T(8,128)(2,1)S(1)} collective-permute-done((bf16[2,32,1024]{2,1,0:T(8,128)(2,1)S(1)}, bf16[2,32,1024]{2,1,0:T(8,128)(2,1)S(1)}, u32[]{:S(2)}, u32[]{:S(2)}) %collective-permute-start.11) | collective-permute-done | bytes 131104 | tf_op jit(solution)/shard_map/ppermute | solution.py:375
  (2 shorter events, 0.0 us)
Async XLA Ops:
  2.1 10.2 %collective-permute-start.10 = (bf16[64,1024]{1,0:T(8,128)(2,1)}, bf16[64,1024]{1,0:T(8,128)(2,1)S(1)}, u32[]{:S(2)}, u32[]{:S(2)}) collective-permute-start(bf16[64,1024]{1,0:T(8,128)(2,1)} %bitcast.1), channel_id=1, source_target_pairs={{0,1},{1,0},{2,3},{3,2},{4,5},{5,4},{6,7},{7,6},{8,9},{9,8},{10,11... | collective-permute-start | bytes 393224 | tf_op jit(solution)/shard_map/ppermute | solution.py:394
  2.6 6.1 %collective-permute-start = (bf16[32,1152]{1,0:T(8,128)(2,1)}, bf16[32,1152]{1,0:T(8,128)(2,1)S(1)}, u32[]{:S(2)}, u32[]{:S(2)}) collective-permute-start(bf16[32,1152]{1,0:T(8,128)(2,1)} %get-tuple-element.27), channel_id=1, source_target_pairs={{0,8},{8,0},{16,24},{24,16},{1,9},{9,1},{17,25},{25,17},{2,10},{10... | collective-permute-start | bytes 221192 | tf_op jit(solution)/shard_map/ppermute | solution.py:375
  5.2 4.9 %collective-permute-start.1 = (bf16[32,1152]{1,0:T(8,128)(2,1)}, bf16[32,1152]{1,0:T(8,128)(2,1)S(1)}, u32[]{:S(2)}, u32[]{:S(2)}) collective-permute-start(bf16[32,1152]{1,0:T(8,128)(2,1)} %get-tuple-element.28), channel_id=1, source_target_pairs={{0,16},{8,24},{16,0},{24,8},{1,17},{9,25},{17,1},{25,9},{2,18},{10... | collective-permute-start | bytes 221192 | tf_op jit(solution)/shard_map/ppermute | solution.py:375
  6.7 5.5 %collective-permute-start.2 = (bf16[32,1152]{1,0:T(8,128)(2,1)}, bf16[32,1152]{1,0:T(8,128)(2,1)S(1)}, u32[]{:S(2)}, u32[]{:S(2)}) collective-permute-start(bf16[32,1152]{1,0:T(8,128)(2,1)} %get-tuple-element.29), channel_id=1, source_target_pairs={{0,24},{8,16},{16,8},{24,0},{1,25},{9,17},{17,9},{25,1},{2,26},{10... | collective-permute-start | bytes 221192 | tf_op jit(solution)/shard_map/ppermute | solution.py:375
  6.7 6.6 %collective-permute-start.9 = (bf16[64,1024]{1,0:T(8,128)(2,1)}, bf16[64,1024]{1,0:T(8,128)(2,1)S(1)}, u32[]{:S(2)}, u32[]{:S(2)}) collective-permute-start(bf16[64,1024]{1,0:T(8,128)(2,1)} %bitcast.2), channel_id=1, source_target_pairs={{0,8},{1,2},{2,1},{3,4},{4,3},{5,6},{6,5},{7,15},{8,0},{9,10},{10,... | collective-permute-start | bytes 393224 | tf_op jit(solution)/shard_map/ppermute | solution.py:394
  8.7 6.0 %collective-permute-start.8 = (bf16[64,1024]{1,0:T(8,128)(2,1)}, bf16[64,1024]{1,0:T(8,128)(2,1)S(1)}, u32[]{:S(2)}, u32[]{:S(2)}) collective-permute-start(bf16[64,1024]{1,0:T(8,128)(2,1)} %bitcast.3), channel_id=1, source_target_pairs={{0,2},{1,3},{2,0},{3,1},{4,6},{5,7},{6,4},{7,5},{8,10},{9,11},{10,... | collective-permute-start | bytes 393224 | tf_op jit(solution)/shard_map/ppermute | solution.py:394
  10.1 5.3 %collective-permute-start.7 = (bf16[64,1024]{1,0:T(8,128)(2,1)}, bf16[64,1024]{1,0:T(8,128)(2,1)S(1)}, u32[]{:S(2)}, u32[]{:S(2)}) collective-permute-start(bf16[64,1024]{1,0:T(8,128)(2,1)} %bitcast.4), channel_id=1, source_target_pairs={{0,1},{1,0},{2,4},{3,5},{4,2},{5,3},{6,7},{7,6},{8,9},{9,8},{10,12... | collective-permute-start | bytes 393224 | tf_op jit(solution)/shard_map/ppermute | solution.py:394
  10.2 0.9 %copy-start = (bf16[32,1152]{1,0:T(8,128)(2,1)S(1)}, bf16[32,1152]{1,0:T(8,128)(2,1)}, u32[]{:S(2)}) copy-start(bf16[32,1152]{1,0:T(8,128)(2,1)} %get-tuple-element.26.message) | copy-start | bytes 221188
  11.1 4.3 %copy-start.3 = (bf16[256,256]{1,0:T(8,128)(2,1)S(1)}, bf16[256,256]{1,0:T(8,128)(2,1)}, u32[]{:S(2)}) copy-start(bf16[256,256]{1,0:T(8,128)(2,1)} %constant.7.clone.left_tab) | copy-start | bytes 393220
  11.1 4.3 %copy-start.1 = (bf16[2,32,1024]{2,1,0:T(8,128)(2,1)S(1)}, bf16[2,32,1024]{2,1,0:T(8,128)(2,1)}, u32[]{:S(2)}) copy-start(bf16[2,32,1024]{2,1,0:T(8,128)(2,1)} %get-tuple-element.35) | copy-start | bytes 393220
  11.1 4.3 %copy-start.2 = (bf16[256,256]{1,0:T(8,128)(2,1)S(1)}, bf16[256,256]{1,0:T(8,128)(2,1)}, u32[]{:S(2)}) copy-start(bf16[256,256]{1,0:T(8,128)(2,1)} %constant.6.clone.right_tab) | copy-start | bytes 393220
  12.2 6.5 %collective-permute-start.3 = (bf16[80,1152]{1,0:T(8,128)(2,1)S(1)}, bf16[80,1152]{1,0:T(8,128)(2,1)S(1)}, u32[]{:S(2)}, u32[]{:S(2)}) collective-permute-start(bf16[80,1152]{1,0:T(8,128)(2,1)S(1)} %get-tuple-element.30), channel_id=1, source_target_pairs={{0,1},{1,0},{2,3},{3,2},{4,5},{5,4},{6,7},{7,6},{8,9},{9,8},{10,11... | collective-permute-start | bytes 552968 | tf_op jit(solution)/shard_map/ppermute | solution.py:394
  12.3 6.4 %collective-permute-start.4 = (bf16[80,1152]{1,0:T(8,128)(2,1)S(1)}, bf16[80,1152]{1,0:T(8,128)(2,1)S(1)}, u32[]{:S(2)}, u32[]{:S(2)}) collective-permute-start(bf16[80,1152]{1,0:T(8,128)(2,1)S(1)} %get-tuple-element.31), channel_id=1, source_target_pairs={{0,8},{1,2},{2,1},{3,4},{4,3},{5,6},{6,5},{7,15},{8,0},{9,10},{10,... | collective-permute-start | bytes 552968 | tf_op jit(solution)/shard_map/ppermute | solution.py:394
  13.3 5.4 %collective-permute-start.5 = (bf16[16,1152]{1,0:T(8,128)(2,1)S(1)}, bf16[16,1152]{1,0:T(8,128)(2,1)S(1)}, u32[]{:S(2)}, u32[]{:S(2)}) collective-permute-start(bf16[16,1152]{1,0:T(8,128)(2,1)S(1)} %get-tuple-element.32), channel_id=1, source_target_pairs={{0,2},{1,3},{2,0},{3,1},{4,6},{5,7},{6,4},{7,5},{8,10},{9,11},{10,... | collective-permute-start | bytes 110600 | tf_op jit(solution)/shard_map/ppermute | solution.py:394
  14.7 4.0 %collective-permute-start.6 = (bf16[16,1152]{1,0:T(8,128)(2,1)S(1)}, bf16[16,1152]{1,0:T(8,128)(2,1)S(1)}, u32[]{:S(2)}, u32[]{:S(2)}) collective-permute-start(bf16[16,1152]{1,0:T(8,128)(2,1)S(1)} %get-tuple-element.33), channel_id=1, source_target_pairs={{0,1},{1,0},{2,4},{3,5},{4,2},{5,3},{6,7},{7,6},{8,9},{9,8},{10,12... | collective-permute-start | bytes 110600 | tf_op jit(solution)/shard_map/ppermute | solution.py:394
  15.4 3.4 %copy-start.4 = (bf16[192,192]{1,0:T(8,128)(2,1)S(1)}, bf16[192,192]{1,0:T(8,128)(2,1)}, u32[]{:S(2)}) copy-start(bf16[192,192]{1,0:T(8,128)(2,1)} %constant.8.clone.left_tab) | copy-start | bytes 221188
  21.3 5.5 %collective-permute-start.12 = (bf16[2,32,1024]{2,1,0:T(8,128)(2,1)S(1)}, bf16[2,32,1024]{2,1,0:T(8,128)(2,1)S(1)}, u32[]{:S(2)}, u32[]{:S(2)}) collective-permute-start(bf16[2,32,1024]{2,1,0:T(8,128)(2,1)S(1)} %get-tuple-element.45), channel_id=1, source_target_pairs={{0,8},{8,0},{16,24},{24,16},{1,9},{9,1},{17,25},{25,17},{2,10},{10... | collective-permute-start | bytes 393224 | tf_op jit(solution)/shard_map/ppermute | solution.py:375
  23.0 6.5 %collective-permute-start.13 = (bf16[2,32,1024]{2,1,0:T(8,128)(2,1)S(1)}, bf16[2,32,1024]{2,1,0:T(8,128)(2,1)S(1)}, u32[]{:S(2)}, u32[]{:S(2)}) collective-permute-start(bf16[2,32,1024]{2,1,0:T(8,128)(2,1)S(1)} %get-tuple-element.46), channel_id=1, source_target_pairs={{0,16},{8,24},{16,0},{24,8},{1,17},{9,25},{17,1},{25,9},{2,18},{10... | collective-permute-start | bytes 393224 | tf_op jit(solution)/shard_map/ppermute | solution.py:375
  24.6 6.5 %collective-permute-start.11 = (bf16[2,32,1024]{2,1,0:T(8,128)(2,1)S(1)}, bf16[2,32,1024]{2,1,0:T(8,128)(2,1)S(1)}, u32[]{:S(2)}, u32[]{:S(2)}) collective-permute-start(bf16[2,32,1024]{2,1,0:T(8,128)(2,1)S(1)} %get-tuple-element.43), channel_id=1, source_target_pairs={{0,24},{8,16},{16,8},{24,0},{1,25},{9,17},{17,9},{25,1},{2,26},{10... | collective-permute-start | bytes 393224 | tf_op jit(solution)/shard_map/ppermute | solution.py:375

commit v28 on v27

--- a/solution.py
+++ b/solution.py
@@ -111,15 +111,18 @@
     )
     left_half = lax.broadcasted_iota(jnp.int32, (BAND, LANES), 1) < HALF
     colours = [jnp.minimum(depth ^ hop, COLORS - 1) for hop in range(LAYERS)]
-    for colour, out in zip(colours, outs):
-        taps[...] = jnp.zeros_like(taps)
-        taps[2:4, : 2 * KC + 1] = col_taps[0, colour].astype(jnp.float32)
-        taps[4:6, : 2 * KR + 1] = row_taps[0, colour].astype(jnp.float32)
-        turned = pltpu.roll(taps[0:8], HALF, 1)
-        taps[0:2] = turned[2:4]
-        taps[4:6] = turned[4:6]
-        tile = jnp.where(left_half, edge_tile, taps[...])
-        out[:, COLS:] = tile.astype(jnp.bfloat16)
+    taps[...] = jnp.zeros_like(taps)
+    for hop, colour in enumerate(colours):
+        col = col_taps[0, colour].astype(jnp.float32)
+        taps[8 * hop : 8 * hop + 2, : 2 * KC + 1] = col
+        taps[8 * hop + 2 : 8 * hop + 4, : 2 * KC + 1] = col
+        taps[8 * hop + 4 : 8 * hop + 6, : 2 * KR + 1] = row_taps[0, colour].astype(jnp.float32)
+    stays = lax.broadcasted_iota(jnp.int32, (BAND, LANES), 0) % 8 // 2 == 1
+    turned = jnp.where(stays, taps[...], pltpu.roll(taps[...], HALF, 1))
+    below = jnp.zeros((BAND - 8, LANES), jnp.float32)
+    for hop, out in enumerate(outs):
+        tile = jnp.concatenate([turned[8 * hop : 8 * hop + 8], below], axis=0)
+        out[:, COLS:] = jnp.where(left_half, edge_tile, tile).astype(jnp.bfloat16)
     copies[5].wait()
     for colour, out in zip(colours, outs):
         out[:, :COLS] = (light[0, colour] * live_pix).astype(jnp.bfloat16)

time: 31.3 us -> 31.2 us (level)
  no operation moved by 1% of the time
where the time goes in v28:
time: 31.2 us; the launch traced here: 31 us
  starting transfers between devices  15.2 us (49%)
  waiting for transfers between devices  8.24 us (26%)
  Pallas kernels  6.53 us (21%)
  local copies, waits for them, and re-layouts  0.91 us (3%)
    ppermute x6, starting transfers between devices, over_depth(): return lax.ppermute(value, 'depth', [(i, i ^ hop) for i in range(LAYERS)])  8.37 us
    ppermute x8, starting transfers between devices, exchanged(): return lax.ppermute(value, ('depth', 'rows'), pairs)  6.87 us
    ppermute x6, waiting for transfers between devices, over_depth(): return lax.ppermute(value, 'depth', [(i, i ^ hop) for i in range(LAYERS)])  5.89 us
    pallas_call x1, Pallas kernels, body(): call(chain_kernel, [shaped((2, BAND, COLS), bf16)] * LAYERS, [vmem] * (6...  2.52 us
    ppermute x8, waiting for transfers between devices, exchanged(): return lax.ppermute(value, ('depth', 'rows'), pairs)  2.35 us
    pallas_call x1, Pallas kernels, body(): call(pack_kernel, (shaped((BAND, HALO_W), bf16),) * LAYERS + (shaped(inci...  1.97 us
    pallas_call x1, Pallas kernels, body(): call(prepare_kernel, [shaped((TILES * layer_height(0), 2 * LANES), f32),...  1.2 us
    unnamed x10, local copies, waits for them, and re-layouts  0.91 us
  transfers between devices with their start and end apart: 14, of which 6 were waited for; matrix products, arithmetic and copies ran while one was open for 0% of the time, Pallas kernels for 7%

profile of v28, /device:TPU:0, one launch (start us, length us, event | category | flops | bytes accessed | tf_op | source)
XLA Modules:
  0.0 31.0 jit_solution(16983198457160421547)
XLA Ops:
  0.0 2.0 %shard_map.100 = (bf16[32,1152]{1,0:T(8,128)(2,1)}, bf16[32,1152]{1,0:T(8,128)(2,1)}, bf16[32,1152]{1,0:T(8,128)(2,1)}, bf16[32,1152]{1,0:T(8,128)(2,1)}, bf16[2,32,1024]{2,1,0:T(8,128)(2,1)}) custom-call(f32[1,3,32,1024]{3,2,1,0:T(8,128)} %light.1, s32[1,32,64]{2,1,0:T(8,128)} %edges.1, s32[1,2]{1,0:T(1,128)} %counts.1, s32[1,2,64]{2,1,0:T(2,128)} %listed.1, ...), custom_call_target="tpu_custom_call" | custom-call | flops 10000000 | bytes 1000000 | tf_op jit(solution)/shard_map/pallas_call | solution.py:440
  2.0 0.5 %collective-permute-start.10 = (bf16[64,1024]{1,0:T(8,128)(2,1)}, bf16[64,1024]{1,0:T(8,128)(2,1)S(1)}, u32[]{:S(2)}, u32[]{:S(2)}) collective-permute-start(bf16[64,1024]{1,0:T(8,128)(2,1)} %bitcast.1), channel_id=1, source_target_pairs={{0,1},{1,0},{2,3},{3,2},{4,5},{5,4},{6,7},{7,6},{8,9},{9,8},{10,11... | collective-permute-start | bytes 393224 | tf_op jit(solution)/shard_map/ppermute | solution.py:397
  2.5 2.6 %collective-permute-start = (bf16[32,1152]{1,0:T(8,128)(2,1)}, bf16[32,1152]{1,0:T(8,128)(2,1)S(1)}, u32[]{:S(2)}, u32[]{:S(2)}) collective-permute-start(bf16[32,1152]{1,0:T(8,128)(2,1)} %get-tuple-element.27), channel_id=1, source_target_pairs={{0,8},{8,0},{16,24},{24,16},{1,9},{9,1},{17,25},{25,17},{2,10},{10... | collective-permute-start | bytes 221192 | tf_op jit(solution)/shard_map/ppermute | solution.py:378
  5.1 1.5 %collective-permute-start.1 = (bf16[32,1152]{1,0:T(8,128)(2,1)}, bf16[32,1152]{1,0:T(8,128)(2,1)S(1)}, u32[]{:S(2)}, u32[]{:S(2)}) collective-permute-start(bf16[32,1152]{1,0:T(8,128)(2,1)} %get-tuple-element.28), channel_id=1, source_target_pairs={{0,16},{8,24},{16,0},{24,8},{1,17},{9,25},{17,1},{25,9},{2,18},{10... | collective-permute-start | bytes 221192 | tf_op jit(solution)/shard_map/ppermute | solution.py:378
  6.6 0.0 collective-permute-start.2
  6.6 1.9 %collective-permute-start.9 = (bf16[64,1024]{1,0:T(8,128)(2,1)}, bf16[64,1024]{1,0:T(8,128)(2,1)S(1)}, u32[]{:S(2)}, u32[]{:S(2)}) collective-permute-start(bf16[64,1024]{1,0:T(8,128)(2,1)} %bitcast.2), channel_id=1, source_target_pairs={{0,8},{1,2},{2,1},{3,4},{4,3},{5,6},{6,5},{7,15},{8,0},{9,10},{10,... | collective-permute-start | bytes 393224 | tf_op jit(solution)/shard_map/ppermute | solution.py:397
  8.5 0.0 collective-permute-done.refs_1_
  8.6 1.4 %collective-permute-start.8 = (bf16[64,1024]{1,0:T(8,128)(2,1)}, bf16[64,1024]{1,0:T(8,128)(2,1)S(1)}, u32[]{:S(2)}, u32[]{:S(2)}) collective-permute-start(bf16[64,1024]{1,0:T(8,128)(2,1)} %bitcast.3), channel_id=1, source_target_pairs={{0,2},{1,3},{2,0},{3,1},{4,6},{5,7},{6,4},{7,5},{8,10},{9,11},{10,... | collective-permute-start | bytes 393224 | tf_op jit(solution)/shard_map/ppermute | solution.py:397
  10.0 0.0 collective-permute-done.1.refs_2_
  10.0 0.1 collective-permute-start.7
  10.1 0.0 copy-start
  10.1 0.9 %copy-done = bf16[32,1152]{1,0:T(8,128)(2,1)S(1)} copy-done((bf16[32,1152]{1,0:T(8,128)(2,1)S(1)}, bf16[32,1152]{1,0:T(8,128)(2,1)}, u32[]{:S(2)}) %copy-start) | copy-done | bytes 73752
  10.9 0.0 copy-start.3
  10.9 0.0 copy-start.1
  11.0 0.0 copy-start.2
  11.0 1.1 %collective-permute-done.2.refs_3_ = bf16[32,1152]{1,0:T(8,128)(2,1)S(1)} collective-permute-done((bf16[32,1152]{1,0:T(8,128)(2,1)}, bf16[32,1152]{1,0:T(8,128)(2,1)S(1)}, u32[]{:S(2)}, u32[]{:S(2)}) %collective-permute-start.2) | collective-permute-done | bytes 73760 | tf_op jit(solution)/shard_map/ppermute | solution.py:378
  12.0 0.1 shard_map.102
  12.1 0.1 collective-permute-start.3
  12.2 0.0 collective-permute-done.10.in_chip
  12.2 1.0 %collective-permute-start.4 = (bf16[80,1152]{1,0:T(8,128)(2,1)S(1)}, bf16[80,1152]{1,0:T(8,128)(2,1)S(1)}, u32[]{:S(2)}, u32[]{:S(2)}) collective-permute-start(bf16[80,1152]{1,0:T(8,128)(2,1)S(1)} %get-tuple-element.31), channel_id=1, source_target_pairs={{0,8},{1,2},{2,1},{3,4},{4,3},{5,6},{6,5},{7,15},{8,0},{9,10},{10,... | collective-permute-start | bytes 552968 | tf_op jit(solution)/shard_map/ppermute | solution.py:397
  13.2 0.0 collective-permute-done.9.cross
  13.2 1.2 %collective-permute-start.5 = (bf16[16,1152]{1,0:T(8,128)(2,1)S(1)}, bf16[16,1152]{1,0:T(8,128)(2,1)S(1)}, u32[]{:S(2)}, u32[]{:S(2)}) collective-permute-start(bf16[16,1152]{1,0:T(8,128)(2,1)S(1)} %get-tuple-element.32), channel_id=1, source_target_pairs={{0,2},{1,3},{2,0},{3,1},{4,6},{5,7},{6,4},{7,5},{8,10},{9,11},{10,... | collective-permute-start | bytes 110600 | tf_op jit(solution)/shard_map/ppermute | solution.py:397
  14.4 0.2 collective-permute-done.8.far_even
  14.6 0.7 %collective-permute-start.6 = (bf16[16,1152]{1,0:T(8,128)(2,1)S(1)}, bf16[16,1152]{1,0:T(8,128)(2,1)S(1)}, u32[]{:S(2)}, u32[]{:S(2)}) collective-permute-start(bf16[16,1152]{1,0:T(8,128)(2,1)S(1)} %get-tuple-element.33), channel_id=1, source_target_pairs={{0,1},{1,0},{2,4},{3,5},{4,2},{5,3},{6,7},{7,6},{8,9},{9,8},{10,12... | collective-permute-start | bytes 110600 | tf_op jit(solution)/shard_map/ppermute | solution.py:397
  15.3 0.0 collective-permute-done.7.far_odd
  15.3 0.0 copy-done.3
  15.3 0.0 copy-done.1
  15.3 0.0 copy-done.2
  15.3 0.0 copy-start.4
  15.3 1.2 %shard_map.103 = (f32[1024,256]{1,0:T(8,128)S(1)}, f32[2,128,1024]{2,1,0:T(8,128)S(1)}, f32[128,1024]{1,0:T(8,128)S(1)}, bf16[3,256,512]{2,1,0:T(8,128)(2,1)S(1)...) custom-call(bf16[4,32,1152]{2,1,0:T(8,128)(2,1)S(1)} %get-tuple-element.34.own, ...), custom_call_target="tpu_custom_call" | custom-call | flops 1000000000 | bytes 3000000 | tf_op jit(solution)/shard_map/pallas_call | solution.py:461
  16.5 2.1 %collective-permute-done.5.far_even = bf16[16,1152]{1,0:T(8,128)(2,1)S(1)} collective-permute-done((bf16[16,1152]{1,0:T(8,128)(2,1)S(1)}, bf16[16,1152]{1,0:T(8,128)(2,1)S(1)}, u32[]{:S(2)}, u32[]{:S(2)}) %collective-permute-start.5) | collective-permute-done | bytes 36896 | tf_op jit(solution)/shard_map/ppermute | solution.py:397
  18.6 0.0 collective-permute-done.6.far_odd
  18.6 0.0 collective-permute-done.3.in_chip
  18.6 0.0 collective-permute-done.4.cross
  18.6 0.0 copy-done.4
  18.7 2.5 %shard_map.104 = (bf16[2,32,1024]{2,1,0:T(8,128)(2,1)S(1)}, bf16[2,32,1024]{2,1,0:T(8,128)(2,1)S(1)}, bf16[2,32,1024]{2,1,0:T(8,128)(2,1)S(1)}, bf16[2,32,1024]{2,1,0:T(8,128)(2,1)S(1)}) custom-call(bf16[80,1152]{1,0:T(8,128)(2,1)S(1)} %collective-permute-done.3.in_chip, bf16[80,1152]{1,0:T(8,128)(2,1)S(1)} %collective-permute-done.4.cross, ...), custom_call_target="tpu_custom_call" | custom-call | flops 2000000000 | bytes 3000000 | tf_op jit(solution)/shard_map/pallas_call | solution.py:475
  21.2 1.7 %collective-permute-start.12 = (bf16[2,32,1024]{2,1,0:T(8,128)(2,1)S(1)}, bf16[2,32,1024]{2,1,0:T(8,128)(2,1)S(1)}, u32[]{:S(2)}, u32[]{:S(2)}) collective-permute-start(bf16[2,32,1024]{2,1,0:T(8,128)(2,1)S(1)} %get-tuple-element.45), channel_id=1, source_target_pairs={{0,8},{8,0},{16,24},{24,16},{1,9},{9,1},{17,25},{25,17},{2,10},{10... | collective-permute-start | bytes 393224 | tf_op jit(solution)/shard_map/ppermute | solution.py:378
  22.9 1.6 %collective-permute-start.13 = (bf16[2,32,1024]{2,1,0:T(8,128)(2,1)S(1)}, bf16[2,32,1024]{2,1,0:T(8,128)(2,1)S(1)}, u32[]{:S(2)}, u32[]{:S(2)}) collective-permute-start(bf16[2,32,1024]{2,1,0:T(8,128)(2,1)S(1)} %get-tuple-element.46), channel_id=1, source_target_pairs={{0,16},{8,24},{16,0},{24,8},{1,17},{9,25},{17,1},{25,9},{2,18},{10... | collective-permute-start | bytes 393224 | tf_op jit(solution)/shard_map/ppermute | solution.py:378
  24.5 0.9 %collective-permute-start.11 = (bf16[2,32,1024]{2,1,0:T(8,128)(2,1)S(1)}, bf16[2,32,1024]{2,1,0:T(8,128)(2,1)S(1)}, u32[]{:S(2)}, u32[]{:S(2)}) collective-permute-start(bf16[2,32,1024]{2,1,0:T(8,128)(2,1)S(1)} %get-tuple-element.43), channel_id=1, source_target_pairs={{0,24},{8,16},{16,8},{24,0},{1,25},{9,17},{17,9},{25,1},{2,26},{10... | collective-permute-start | bytes 393224 | tf_op jit(solution)/shard_map/ppermute | solution.py:378
  25.4 1.2 %collective-permute-done.12.refs_1_ = bf16[2,32,1024]{2,1,0:T(8,128)(2,1)S(1)} collective-permute-done((bf16[2,32,1024]{2,1,0:T(8,128)(2,1)S(1)}, bf16[2,32,1024]{2,1,0:T(8,128)(2,1)S(1)}, u32[]{:S(2)}, u32[]{:S(2)}) %collective-permute-start.12) | collective-permute-done | bytes 131104 | tf_op jit(solution)/shard_map/ppermute | solution.py:378
  26.7 2.7 %collective-permute-done.13.refs_2_ = bf16[2,32,1024]{2,1,0:T(8,128)(2,1)S(1)} collective-permute-done((bf16[2,32,1024]{2,1,0:T(8,128)(2,1)S(1)}, bf16[2,32,1024]{2,1,0:T(8,128)(2,1)S(1)}, u32[]{:S(2)}, u32[]{:S(2)}) %collective-permute-start.13) | collective-permute-done | bytes 131104 | tf_op jit(solution)/shard_map/ppermute | solution.py:378
  29.4 0.8 %shard_map.105.refs_1_ = bf16[1,3,2,32,1024]{4,3,2,1,0:T(8,128)(2,1)} custom-call(bf16[2,32,1024]{2,1,0:T(8,128)(2,1)S(1)} %get-tuple-element.44.refs_0_, bf16[2,32,1024]{2,1,0:T(8,128)(2,1)S(1)} %collective-permute-done.12.refs_1_, bf16[2,32,1024]{2,1,0:T(8,128)(2,1)S(1)} %collective-permute-done.13.refs_2_), custom_call_target="tpu_custom_call" | custom-call | bytes 1000000 | tf_op jit(solution)/shard_map/pallas_call | solution.py:486
  30.1 0.9 %collective-permute-done.11.refs_0_ = bf16[2,32,1024]{2,1,0:T(8,128)(2,1)S(1)} collective-permute-done((bf16[2,32,1024]{2,1,0:T(8,128)(2,1)S(1)}, bf16[2,32,1024]{2,1,0:T(8,128)(2,1)S(1)}, u32[]{:S(2)}, u32[]{:S(2)}) %collective-permute-start.11) | collective-permute-done | bytes 131104 | tf_op jit(solution)/shard_map/ppermute | solution.py:378
  (2 shorter events, 0.0 us)
Async XLA Ops:
  2.0 10.2 %collective-permute-start.10 = (bf16[64,1024]{1,0:T(8,128)(2,1)}, bf16[64,1024]{1,0:T(8,128)(2,1)S(1)}, u32[]{:S(2)}, u32[]{:S(2)}) collective-permute-start(bf16[64,1024]{1,0:T(8,128)(2,1)} %bitcast.1), channel_id=1, source_target_pairs={{0,1},{1,0},{2,3},{3,2},{4,5},{5,4},{6,7},{7,6},{8,9},{9,8},{10,11... | collective-permute-start | bytes 393224 | tf_op jit(solution)/shard_map/ppermute | solution.py:397
  2.5 6.1 %collective-permute-start = (bf16[32,1152]{1,0:T(8,128)(2,1)}, bf16[32,1152]{1,0:T(8,128)(2,1)S(1)}, u32[]{:S(2)}, u32[]{:S(2)}) collective-permute-start(bf16[32,1152]{1,0:T(8,128)(2,1)} %get-tuple-element.27), channel_id=1, source_target_pairs={{0,8},{8,0},{16,24},{24,16},{1,9},{9,1},{17,25},{25,17},{2,10},{10... | collective-permute-start | bytes 221192 | tf_op jit(solution)/shard_map/ppermute | solution.py:378
  5.1 4.9 %collective-permute-start.1 = (bf16[32,1152]{1,0:T(8,128)(2,1)}, bf16[32,1152]{1,0:T(8,128)(2,1)S(1)}, u32[]{:S(2)}, u32[]{:S(2)}) collective-permute-start(bf16[32,1152]{1,0:T(8,128)(2,1)} %get-tuple-element.28), channel_id=1, source_target_pairs={{0,16},{8,24},{16,0},{24,8},{1,17},{9,25},{17,1},{25,9},{2,18},{10... | collective-permute-start | bytes 221192 | tf_op jit(solution)/shard_map/ppermute | solution.py:378
  6.6 5.5 %collective-permute-start.2 = (bf16[32,1152]{1,0:T(8,128)(2,1)}, bf16[32,1152]{1,0:T(8,128)(2,1)S(1)}, u32[]{:S(2)}, u32[]{:S(2)}) collective-permute-start(bf16[32,1152]{1,0:T(8,128)(2,1)} %get-tuple-element.29), channel_id=1, source_target_pairs={{0,24},{8,16},{16,8},{24,0},{1,25},{9,17},{17,9},{25,1},{2,26},{10... | collective-permute-start | bytes 221192 | tf_op jit(solution)/shard_map/ppermute | solution.py:378
  6.6 6.6 %collective-permute-start.9 = (bf16[64,1024]{1,0:T(8,128)(2,1)}, bf16[64,1024]{1,0:T(8,128)(2,1)S(1)}, u32[]{:S(2)}, u32[]{:S(2)}) collective-permute-start(bf16[64,1024]{1,0:T(8,128)(2,1)} %bitcast.2), channel_id=1, source_target_pairs={{0,8},{1,2},{2,1},{3,4},{4,3},{5,6},{6,5},{7,15},{8,0},{9,10},{10,... | collective-permute-start | bytes 393224 | tf_op jit(solution)/shard_map/ppermute | solution.py:397
  8.6 6.0 %collective-permute-start.8 = (bf16[64,1024]{1,0:T(8,128)(2,1)}, bf16[64,1024]{1,0:T(8,128)(2,1)S(1)}, u32[]{:S(2)}, u32[]{:S(2)}) collective-permute-start(bf16[64,1024]{1,0:T(8,128)(2,1)} %bitcast.3), channel_id=1, source_target_pairs={{0,2},{1,3},{2,0},{3,1},{4,6},{5,7},{6,4},{7,5},{8,10},{9,11},{10,... | collective-permute-start | bytes 393224 | tf_op jit(solution)/shard_map/ppermute | solution.py:397
  10.0 5.3 %collective-permute-start.7 = (bf16[64,1024]{1,0:T(8,128)(2,1)}, bf16[64,1024]{1,0:T(8,128)(2,1)S(1)}, u32[]{:S(2)}, u32[]{:S(2)}) collective-permute-start(bf16[64,1024]{1,0:T(8,128)(2,1)} %bitcast.4), channel_id=1, source_target_pairs={{0,1},{1,0},{2,4},{3,5},{4,2},{5,3},{6,7},{7,6},{8,9},{9,8},{10,12... | collective-permute-start | bytes 393224 | tf_op jit(solution)/shard_map/ppermute | solution.py:397
  10.1 0.9 %copy-start = (bf16[32,1152]{1,0:T(8,128)(2,1)S(1)}, bf16[32,1152]{1,0:T(8,128)(2,1)}, u32[]{:S(2)}) copy-start(bf16[32,1152]{1,0:T(8,128)(2,1)} %get-tuple-element.26.message) | copy-start | bytes 221188
  10.9 4.3 %copy-start.3 = (bf16[256,256]{1,0:T(8,128)(2,1)S(1)}, bf16[256,256]{1,0:T(8,128)(2,1)}, u32[]{:S(2)}) copy-start(bf16[256,256]{1,0:T(8,128)(2,1)} %constant.7.clone.left_tab) | copy-start | bytes 393220
  10.9 4.3 %copy-start.1 = (bf16[2,32,1024]{2,1,0:T(8,128)(2,1)S(1)}, bf16[2,32,1024]{2,1,0:T(8,128)(2,1)}, u32[]{:S(2)}) copy-start(bf16[2,32,1024]{2,1,0:T(8,128)(2,1)} %get-tuple-element.35) | copy-start | bytes 393220
  11.0 4.3 %copy-start.2 = (bf16[256,256]{1,0:T(8,128)(2,1)S(1)}, bf16[256,256]{1,0:T(8,128)(2,1)}, u32[]{:S(2)}) copy-start(bf16[256,256]{1,0:T(8,128)(2,1)} %constant.6.clone.right_tab) | copy-start | bytes 393220
  12.1 6.5 %collective-permute-start.3 = (bf16[80,1152]{1,0:T(8,128)(2,1)S(1)}, bf16[80,1152]{1,0:T(8,128)(2,1)S(1)}, u32[]{:S(2)}, u32[]{:S(2)}) collective-permute-start(bf16[80,1152]{1,0:T(8,128)(2,1)S(1)} %get-tuple-element.30), channel_id=1, source_target_pairs={{0,1},{1,0},{2,3},{3,2},{4,5},{5,4},{6,7},{7,6},{8,9},{9,8},{10,11... | collective-permute-start | bytes 552968 | tf_op jit(solution)/shard_map/ppermute | solution.py:397
  12.2 6.4 %collective-permute-start.4 = (bf16[80,1152]{1,0:T(8,128)(2,1)S(1)}, bf16[80,1152]{1,0:T(8,128)(2,1)S(1)}, u32[]{:S(2)}, u32[]{:S(2)}) collective-permute-start(bf16[80,1152]{1,0:T(8,128)(2,1)S(1)} %get-tuple-element.31), channel_id=1, source_target_pairs={{0,8},{1,2},{2,1},{3,4},{4,3},{5,6},{6,5},{7,15},{8,0},{9,10},{10,... | collective-permute-start | bytes 552968 | tf_op jit(solution)/shard_map/ppermute | solution.py:397
  13.2 5.4 %collective-permute-start.5 = (bf16[16,1152]{1,0:T(8,128)(2,1)S(1)}, bf16[16,1152]{1,0:T(8,128)(2,1)S(1)}, u32[]{:S(2)}, u32[]{:S(2)}) collective-permute-start(bf16[16,1152]{1,0:T(8,128)(2,1)S(1)} %get-tuple-element.32), channel_id=1, source_target_pairs={{0,2},{1,3},{2,0},{3,1},{4,6},{5,7},{6,4},{7,5},{8,10},{9,11},{10,... | collective-permute-start | bytes 110600 | tf_op jit(solution)/shard_map/ppermute | solution.py:397
  14.6 4.0 %collective-permute-start.6 = (bf16[16,1152]{1,0:T(8,128)(2,1)S(1)}, bf16[16,1152]{1,0:T(8,128)(2,1)S(1)}, u32[]{:S(2)}, u32[]{:S(2)}) collective-permute-start(bf16[16,1152]{1,0:T(8,128)(2,1)S(1)} %get-tuple-element.33), channel_id=1, source_target_pairs={{0,1},{1,0},{2,4},{3,5},{4,2},{5,3},{6,7},{7,6},{8,9},{9,8},{10,12... | collective-permute-start | bytes 110600 | tf_op jit(solution)/shard_map/ppermute | solution.py:397
  15.3 3.4 %copy-start.4 = (bf16[192,192]{1,0:T(8,128)(2,1)S(1)}, bf16[192,192]{1,0:T(8,128)(2,1)}, u32[]{:S(2)}) copy-start(bf16[192,192]{1,0:T(8,128)(2,1)} %constant.8.clone.left_tab) | copy-start | bytes 221188
  21.2 5.5 %collective-permute-start.12 = (bf16[2,32,1024]{2,1,0:T(8,128)(2,1)S(1)}, bf16[2,32,1024]{2,1,0:T(8,128)(2,1)S(1)}, u32[]{:S(2)}, u32[]{:S(2)}) collective-permute-start(bf16[2,32,1024]{2,1,0:T(8,128)(2,1)S(1)} %get-tuple-element.45), channel_id=1, source_target_pairs={{0,8},{8,0},{16,24},{24,16},{1,9},{9,1},{17,25},{25,17},{2,10},{10... | collective-permute-start | bytes 393224 | tf_op jit(solution)/shard_map/ppermute | solution.py:378
  22.9 6.5 %collective-permute-start.13 = (bf16[2,32,1024]{2,1,0:T(8,128)(2,1)S(1)}, bf16[2,32,1024]{2,1,0:T(8,128)(2,1)S(1)}, u32[]{:S(2)}, u32[]{:S(2)}) collective-permute-start(bf16[2,32,1024]{2,1,0:T(8,128)(2,1)S(1)} %get-tuple-element.46), channel_id=1, source_target_pairs={{0,16},{8,24},{16,0},{24,8},{1,17},{9,25},{17,1},{25,9},{2,18},{10... | collective-permute-start | bytes 393224 | tf_op jit(solution)/shard_map/ppermute | solution.py:378
  24.5 6.5 %collective-permute-start.11 = (bf16[2,32,1024]{2,1,0:T(8,128)(2,1)S(1)}, bf16[2,32,1024]{2,1,0:T(8,128)(2,1)S(1)}, u32[]{:S(2)}, u32[]{:S(2)}) collective-permute-start(bf16[2,32,1024]{2,1,0:T(8,128)(2,1)S(1)} %get-tuple-element.43), channel_id=1, source_target_pairs={{0,24},{8,16},{16,8},{24,0},{1,25},{9,17},{17,9},{25,1},{2,26},{10... | collective-permute-start | bytes 393224 | tf_op jit(solution)/shard_map/ppermute | solution.py:378

commit v29 on v28

--- a/solution.py
+++ b/solution.py
@@ -198,8 +198,8 @@
     return jnp.dot(arranged, right_tab[...], preferred_element_type=jnp.float32)
 
 
-def clear_pixels(edges):
-    edge_pix = jnp.dot(edges, spread_matrix(), preferred_element_type=jnp.float32)
+def clear_pixels(edges, spread):
+    edge_pix = jnp.dot(edges, spread, preferred_element_type=jnp.float32)
     within = (lax.broadcasted_iota(jnp.int32, (1, COLS), 1) % HS).astype(jnp.float32)
     return jnp.where(within < edge_pix, 1.0, 0.0)
 
@@ -266,7 +266,7 @@
 
 def prepare_kernel(
     own, incident, far_odd, far_even, cross, in_chip, left_tab, right_tab,
-    first, stereo, clear, col_mats, *row_mats
+    first, stereo, clear, col_mats, spread, *row_mats
 ):
     low_near, high_near, low_far, high_far = ordered(in_chip, cross, far_even, far_odd)
     extended = []
@@ -281,7 +281,8 @@
         row_mats[layer - 1][...] = row_mat
         col_mats[layer - 1] = col_mat
     packed = jnp.concatenate([own[layer, :, :HALO_W] for layer in range(LAYERS)], axis=0)
-    clear[...] = clear_pixels(packed[:, COLS : COLS + NH])
+    spread[...] = spread_matrix()
+    clear[...] = clear_pixels(packed[:, COLS : COLS + NH], spread[...])
     tiles = stereo_tiles([packed[:, :COLS]], left_tab, right_tab)
     for tile in range(TILES):
         for part in range(2):
@@ -292,7 +293,7 @@
 
 
 def chain_kernel(
-    in_chip, cross, far_even, far_odd, left_tab, right_tab, first, stereo, clear, col_mats, *rest
+    in_chip, cross, far_even, far_odd, left_tab, right_tab, first, stereo, clear, col_mats, spread, *rest
 ):
     row_mats, outs, field = rest[: LAYERS - 1], rest[LAYERS - 1 : -1], rest[-1]
     depth = lax.axis_index("depth")
@@ -312,7 +313,7 @@
     halo_tiles = stereo_tiles(
         [halo[:half, :COLS], halo[half:, :COLS]], left_tab, right_tab
     )
-    halo_clear = clear_pixels(halo[:, COLS : COLS + NH])
+    halo_clear = clear_pixels(halo[:, COLS : COLS + NH], spread[...])
     begins = (0, half, half + 2 * BAND, 0)
     sides = (BAND + FAR, BAND, KR, 0)
     for layer in range(LAYERS):
@@ -465,6 +466,7 @@
             shaped((2, LANES, COLS), f32),
             shaped((LANES, COLS), f32),
             shaped((LAYERS - 1, 2 * LANES, 4 * LANES), bf16),
+            shaped((NH, COLS), bf16),
         ]
         + [shaped((2 * block_height(layer), 2 * LANES), bf16) for layer in range(1, LAYERS)],
         [vmem] * 8,

time: 31.2 us -> 31.2 us (level)
  no operation moved by 1% of the time
where the time goes in v29:
time: 31.2 us; the launch traced here: 31 us
  starting transfers between devices  15.2 us (49%)
  waiting for transfers between devices  8.22 us (26%)
  Pallas kernels  6.54 us (21%)
  local copies, waits for them, and re-layouts  0.91 us (3%)
    ppermute x6, starting transfers between devices, over_depth(): return lax.ppermute(value, 'depth', [(i, i ^ hop) for i in range(LAYERS)])  8.37 us
    ppermute x8, starting transfers between devices, exchanged(): return lax.ppermute(value, ('depth', 'rows'), pairs)  6.87 us
    ppermute x6, waiting for transfers between devices, over_depth(): return lax.ppermute(value, 'depth', [(i, i ^ hop) for i in range(LAYERS)])  5.89 us
    pallas_call x1, Pallas kernels, body(): call(chain_kernel, [shaped((2, BAND, COLS), bf16)] * LAYERS, [vmem] * (6...  2.5 us
    ppermute x8, waiting for transfers between devices, exchanged(): return lax.ppermute(value, ('depth', 'rows'), pairs)  2.33 us
    pallas_call x1, Pallas kernels, body(): call(pack_kernel, (shaped((BAND, HALO_W), bf16),) * LAYERS + (shaped(inci...  1.97 us
    pallas_call x1, Pallas kernels, body(): call(prepare_kernel, [shaped((TILES * layer_height(0), 2 * LANES), f32),...  1.22 us
    unnamed x10, local copies, waits for them, and re-layouts  0.91 us
  transfers between devices with their start and end apart: 14, of which 6 were waited for; matrix products, arithmetic and copies ran while one was open for 0% of the time, Pallas kernels for 7%

profile of v29, /device:TPU:0, one launch (start us, length us, event | category | flops | bytes accessed | tf_op | source)
XLA Modules:
  0.0 31.0 jit_solution(2581962410608992324)
XLA Ops:
  0.0 2.0 %shard_map.100 = (bf16[32,1152]{1,0:T(8,128)(2,1)}, bf16[32,1152]{1,0:T(8,128)(2,1)}, bf16[32,1152]{1,0:T(8,128)(2,1)}, bf16[32,1152]{1,0:T(8,128)(2,1)}, bf16[2,32,1024]{2,1,0:T(8,128)(2,1)}) custom-call(f32[1,3,32,1024]{3,2,1,0:T(8,128)} %light.1, s32[1,32,64]{2,1,0:T(8,128)} %edges.1, s32[1,2]{1,0:T(1,128)} %counts.1, s32[1,2,64]{2,1,0:T(2,128)} %listed.1, ...), custom_call_target="tpu_custom_call" | custom-call | flops 10000000 | bytes 1000000 | tf_op jit(solution)/shard_map/pallas_call | solution.py:441
  2.0 0.5 %collective-permute-start.10 = (bf16[64,1024]{1,0:T(8,128)(2,1)}, bf16[64,1024]{1,0:T(8,128)(2,1)S(1)}, u32[]{:S(2)}, u32[]{:S(2)}) collective-permute-start(bf16[64,1024]{1,0:T(8,128)(2,1)} %bitcast.1), channel_id=1, source_target_pairs={{0,1},{1,0},{2,3},{3,2},{4,5},{5,4},{6,7},{7,6},{8,9},{9,8},{10,11... | collective-permute-start | bytes 393224 | tf_op jit(solution)/shard_map/ppermute | solution.py:398
  2.5 2.6 %collective-permute-start = (bf16[32,1152]{1,0:T(8,128)(2,1)}, bf16[32,1152]{1,0:T(8,128)(2,1)S(1)}, u32[]{:S(2)}, u32[]{:S(2)}) collective-permute-start(bf16[32,1152]{1,0:T(8,128)(2,1)} %get-tuple-element.28), channel_id=1, source_target_pairs={{0,8},{8,0},{16,24},{24,16},{1,9},{9,1},{17,25},{25,17},{2,10},{10... | collective-permute-start | bytes 221192 | tf_op jit(solution)/shard_map/ppermute | solution.py:379
  5.1 1.5 %collective-permute-start.1 = (bf16[32,1152]{1,0:T(8,128)(2,1)}, bf16[32,1152]{1,0:T(8,128)(2,1)S(1)}, u32[]{:S(2)}, u32[]{:S(2)}) collective-permute-start(bf16[32,1152]{1,0:T(8,128)(2,1)} %get-tuple-element.29), channel_id=1, source_target_pairs={{0,16},{8,24},{16,0},{24,8},{1,17},{9,25},{17,1},{25,9},{2,18},{10... | collective-permute-start | bytes 221192 | tf_op jit(solution)/shard_map/ppermute | solution.py:379
  6.6 0.0 collective-permute-start.2
  6.6 1.9 %collective-permute-start.9 = (bf16[64,1024]{1,0:T(8,128)(2,1)}, bf16[64,1024]{1,0:T(8,128)(2,1)S(1)}, u32[]{:S(2)}, u32[]{:S(2)}) collective-permute-start(bf16[64,1024]{1,0:T(8,128)(2,1)} %bitcast.2), channel_id=1, source_target_pairs={{0,8},{1,2},{2,1},{3,4},{4,3},{5,6},{6,5},{7,15},{8,0},{9,10},{10,... | collective-permute-start | bytes 393224 | tf_op jit(solution)/shard_map/ppermute | solution.py:398
  8.5 0.0 collective-permute-done.refs_1_
  8.6 1.4 %collective-permute-start.8 = (bf16[64,1024]{1,0:T(8,128)(2,1)}, bf16[64,1024]{1,0:T(8,128)(2,1)S(1)}, u32[]{:S(2)}, u32[]{:S(2)}) collective-permute-start(bf16[64,1024]{1,0:T(8,128)(2,1)} %bitcast.3), channel_id=1, source_target_pairs={{0,2},{1,3},{2,0},{3,1},{4,6},{5,7},{6,4},{7,5},{8,10},{9,11},{10,... | collective-permute-start | bytes 393224 | tf_op jit(solution)/shard_map/ppermute | solution.py:398
  10.0 0.0 collective-permute-done.1.refs_2_
  10.0 0.1 collective-permute-start.7
  10.1 0.0 copy-start
  10.1 0.9 %copy-done = bf16[32,1152]{1,0:T(8,128)(2,1)S(1)} copy-done((bf16[32,1152]{1,0:T(8,128)(2,1)S(1)}, bf16[32,1152]{1,0:T(8,128)(2,1)}, u32[]{:S(2)}) %copy-start) | copy-done | bytes 73752
  10.9 0.0 copy-start.3
  10.9 0.0 copy-start.1
  11.0 0.0 copy-start.2
  11.0 1.1 %collective-permute-done.2.refs_3_ = bf16[32,1152]{1,0:T(8,128)(2,1)S(1)} collective-permute-done((bf16[32,1152]{1,0:T(8,128)(2,1)}, bf16[32,1152]{1,0:T(8,128)(2,1)S(1)}, u32[]{:S(2)}, u32[]{:S(2)}) %collective-permute-start.2) | collective-permute-done | bytes 73760 | tf_op jit(solution)/shard_map/ppermute | solution.py:379
  12.0 0.1 shard_map.102
  12.1 0.1 collective-permute-start.3
  12.2 0.0 collective-permute-done.10.in_chip
  12.2 1.0 %collective-permute-start.4 = (bf16[80,1152]{1,0:T(8,128)(2,1)S(1)}, bf16[80,1152]{1,0:T(8,128)(2,1)S(1)}, u32[]{:S(2)}, u32[]{:S(2)}) collective-permute-start(bf16[80,1152]{1,0:T(8,128)(2,1)S(1)} %get-tuple-element.32), channel_id=1, source_target_pairs={{0,8},{1,2},{2,1},{3,4},{4,3},{5,6},{6,5},{7,15},{8,0},{9,10},{10,... | collective-permute-start | bytes 552968 | tf_op jit(solution)/shard_map/ppermute | solution.py:398
  13.2 0.0 collective-permute-done.9.cross
  13.2 1.2 %collective-permute-start.5 = (bf16[16,1152]{1,0:T(8,128)(2,1)S(1)}, bf16[16,1152]{1,0:T(8,128)(2,1)S(1)}, u32[]{:S(2)}, u32[]{:S(2)}) collective-permute-start(bf16[16,1152]{1,0:T(8,128)(2,1)S(1)} %get-tuple-element.33), channel_id=1, source_target_pairs={{0,2},{1,3},{2,0},{3,1},{4,6},{5,7},{6,4},{7,5},{8,10},{9,11},{10,... | collective-permute-start | bytes 110600 | tf_op jit(solution)/shard_map/ppermute | solution.py:398
  14.4 0.2 collective-permute-done.8.far_even
  14.6 0.7 %collective-permute-start.6 = (bf16[16,1152]{1,0:T(8,128)(2,1)S(1)}, bf16[16,1152]{1,0:T(8,128)(2,1)S(1)}, u32[]{:S(2)}, u32[]{:S(2)}) collective-permute-start(bf16[16,1152]{1,0:T(8,128)(2,1)S(1)} %get-tuple-element.34), channel_id=1, source_target_pairs={{0,1},{1,0},{2,4},{3,5},{4,2},{5,3},{6,7},{7,6},{8,9},{9,8},{10,12... | collective-permute-start | bytes 110600 | tf_op jit(solution)/shard_map/ppermute | solution.py:398
  15.3 0.0 collective-permute-done.7.far_odd
  15.3 0.0 copy-done.3
  15.3 0.0 copy-done.1
  15.3 0.0 copy-done.2
  15.3 0.0 copy-start.4
  15.3 1.2 %shard_map.103 = (f32[1024,256]{1,0:T(8,128)S(1)}, f32[2,128,1024]{2,1,0:T(8,128)S(1)}, f32[128,1024]{1,0:T(8,128)S(1)}, bf16[3,256,512]{2,1,0:T(8,128)(2,1)S(1)...) custom-call(bf16[4,32,1152]{2,1,0:T(8,128)(2,1)S(1)} %get-tuple-elem, ...), custom_call_target="tpu_custom_call" | custom-call | flops 1000000000 | bytes 3000000 | tf_op jit(solution)/shard_map/pallas_call | solution.py:462
  16.5 2.1 %collective-permute-done.5.far_even = bf16[16,1152]{1,0:T(8,128)(2,1)S(1)} collective-permute-done((bf16[16,1152]{1,0:T(8,128)(2,1)S(1)}, bf16[16,1152]{1,0:T(8,128)(2,1)S(1)}, u32[]{:S(2)}, u32[]{:S(2)}) %collective-permute-start.5) | collective-permute-done | bytes 36896 | tf_op jit(solution)/shard_map/ppermute | solution.py:398
  18.6 0.0 collective-permute-done.6.far_odd
  18.6 0.0 collective-permute-done.3.in_chip
  18.6 0.0 collective-permute-done.4.cross
  18.6 0.0 copy-done.4
  18.7 2.5 %shard_map.104 = (bf16[2,32,1024]{2,1,0:T(8,128)(2,1)S(1)}, bf16[2,32,1024]{2,1,0:T(8,128)(2,1)S(1)}, bf16[2,32,1024]{2,1,0:T(8,128)(2,1)S(1)}, bf16[2,32,1024]{2,1,0:T(8,128)(2,1)S(1)}) custom-call(bf16[80,1152]{1,0:T(8,128)(2,1)S(1)} %collective-permute-done.3.in_chip, bf16[80,1152]{1,0:T(8,128)(2,1)S(1)} %collective-permute-done.4.cross, ...), custom_call_target="tpu_custom_call" | custom-call | flops 2000000000 | bytes 3000000 | tf_op jit(solution)/shard_map/pallas_call | solution.py:477
  21.2 1.7 %collective-permute-start.12 = (bf16[2,32,1024]{2,1,0:T(8,128)(2,1)S(1)}, bf16[2,32,1024]{2,1,0:T(8,128)(2,1)S(1)}, u32[]{:S(2)}, u32[]{:S(2)}) collective-permute-start(bf16[2,32,1024]{2,1,0:T(8,128)(2,1)S(1)} %get-tuple-element.47), channel_id=1, source_target_pairs={{0,8},{8,0},{16,24},{24,16},{1,9},{9,1},{17,25},{25,17},{2,10},{10... | collective-permute-start | bytes 393224 | tf_op jit(solution)/shard_map/ppermute | solution.py:379
  22.9 1.6 %collective-permute-start.13 = (bf16[2,32,1024]{2,1,0:T(8,128)(2,1)S(1)}, bf16[2,32,1024]{2,1,0:T(8,128)(2,1)S(1)}, u32[]{:S(2)}, u32[]{:S(2)}) collective-permute-start(bf16[2,32,1024]{2,1,0:T(8,128)(2,1)S(1)} %get-tuple-element.48), channel_id=1, source_target_pairs={{0,16},{8,24},{16,0},{24,8},{1,17},{9,25},{17,1},{25,9},{2,18},{10... | collective-permute-start | bytes 393224 | tf_op jit(solution)/shard_map/ppermute | solution.py:379
  24.5 0.9 %collective-permute-start.11 = (bf16[2,32,1024]{2,1,0:T(8,128)(2,1)S(1)}, bf16[2,32,1024]{2,1,0:T(8,128)(2,1)S(1)}, u32[]{:S(2)}, u32[]{:S(2)}) collective-permute-start(bf16[2,32,1024]{2,1,0:T(8,128)(2,1)S(1)} %get-tuple-element.45), channel_id=1, source_target_pairs={{0,24},{8,16},{16,8},{24,0},{1,25},{9,17},{17,9},{25,1},{2,26},{10... | collective-permute-start | bytes 393224 | tf_op jit(solution)/shard_map/ppermute | solution.py:379
  25.4 1.3 %collective-permute-done.12.refs_1_ = bf16[2,32,1024]{2,1,0:T(8,128)(2,1)S(1)} collective-permute-done((bf16[2,32,1024]{2,1,0:T(8,128)(2,1)S(1)}, bf16[2,32,1024]{2,1,0:T(8,128)(2,1)S(1)}, u32[]{:S(2)}, u32[]{:S(2)}) %collective-permute-start.12) | collective-permute-done | bytes 131104 | tf_op jit(solution)/shard_map/ppermute | solution.py:379
  26.7 2.7 %collective-permute-done.13.refs_2_ = bf16[2,32,1024]{2,1,0:T(8,128)(2,1)S(1)} collective-permute-done((bf16[2,32,1024]{2,1,0:T(8,128)(2,1)S(1)}, bf16[2,32,1024]{2,1,0:T(8,128)(2,1)S(1)}, u32[]{:S(2)}, u32[]{:S(2)}) %collective-permute-start.13) | collective-permute-done | bytes 131104 | tf_op jit(solution)/shard_map/ppermute | solution.py:379
  29.4 0.8 %shard_map.105.refs_1_ = bf16[1,3,2,32,1024]{4,3,2,1,0:T(8,128)(2,1)} custom-call(bf16[2,32,1024]{2,1,0:T(8,128)(2,1)S(1)} %get-tuple-element.46.refs_0_, bf16[2,32,1024]{2,1,0:T(8,128)(2,1)S(1)} %collective-permute-done.12.refs_1_, bf16[2,32,1024]{2,1,0:T(8,128)(2,1)S(1)} %collective-permute-done.13.refs_2_), custom_call_target="tpu_custom_call" | custom-call | bytes 1000000 | tf_op jit(solution)/shard_map/pallas_call | solution.py:488
  30.1 0.9 %collective-permute-done.11.refs_0_ = bf16[2,32,1024]{2,1,0:T(8,128)(2,1)S(1)} collective-permute-done((bf16[2,32,1024]{2,1,0:T(8,128)(2,1)S(1)}, bf16[2,32,1024]{2,1,0:T(8,128)(2,1)S(1)}, u32[]{:S(2)}, u32[]{:S(2)}) %collective-permute-start.11) | collective-permute-done | bytes 131104 | tf_op jit(solution)/shard_map/ppermute | solution.py:379
  (2 shorter events, 0.0 us)
Async XLA Ops:
  2.0 10.2 %collective-permute-start.10 = (bf16[64,1024]{1,0:T(8,128)(2,1)}, bf16[64,1024]{1,0:T(8,128)(2,1)S(1)}, u32[]{:S(2)}, u32[]{:S(2)}) collective-permute-start(bf16[64,1024]{1,0:T(8,128)(2,1)} %bitcast.1), channel_id=1, source_target_pairs={{0,1},{1,0},{2,3},{3,2},{4,5},{5,4},{6,7},{7,6},{8,9},{9,8},{10,11... | collective-permute-start | bytes 393224 | tf_op jit(solution)/shard_map/ppermute | solution.py:398
  2.5 6.1 %collective-permute-start = (bf16[32,1152]{1,0:T(8,128)(2,1)}, bf16[32,1152]{1,0:T(8,128)(2,1)S(1)}, u32[]{:S(2)}, u32[]{:S(2)}) collective-permute-start(bf16[32,1152]{1,0:T(8,128)(2,1)} %get-tuple-element.28), channel_id=1, source_target_pairs={{0,8},{8,0},{16,24},{24,16},{1,9},{9,1},{17,25},{25,17},{2,10},{10... | collective-permute-start | bytes 221192 | tf_op jit(solution)/shard_map/ppermute | solution.py:379
  5.1 4.9 %collective-permute-start.1 = (bf16[32,1152]{1,0:T(8,128)(2,1)}, bf16[32,1152]{1,0:T(8,128)(2,1)S(1)}, u32[]{:S(2)}, u32[]{:S(2)}) collective-permute-start(bf16[32,1152]{1,0:T(8,128)(2,1)} %get-tuple-element.29), channel_id=1, source_target_pairs={{0,16},{8,24},{16,0},{24,8},{1,17},{9,25},{17,1},{25,9},{2,18},{10... | collective-permute-start | bytes 221192 | tf_op jit(solution)/shard_map/ppermute | solution.py:379
  6.6 5.5 %collective-permute-start.2 = (bf16[32,1152]{1,0:T(8,128)(2,1)}, bf16[32,1152]{1,0:T(8,128)(2,1)S(1)}, u32[]{:S(2)}, u32[]{:S(2)}) collective-permute-start(bf16[32,1152]{1,0:T(8,128)(2,1)} %get-tuple-element.30), channel_id=1, source_target_pairs={{0,24},{8,16},{16,8},{24,0},{1,25},{9,17},{17,9},{25,1},{2,26},{10... | collective-permute-start | bytes 221192 | tf_op jit(solution)/shard_map/ppermute | solution.py:379
  6.6 6.6 %collective-permute-start.9 = (bf16[64,1024]{1,0:T(8,128)(2,1)}, bf16[64,1024]{1,0:T(8,128)(2,1)S(1)}, u32[]{:S(2)}, u32[]{:S(2)}) collective-permute-start(bf16[64,1024]{1,0:T(8,128)(2,1)} %bitcast.2), channel_id=1, source_target_pairs={{0,8},{1,2},{2,1},{3,4},{4,3},{5,6},{6,5},{7,15},{8,0},{9,10},{10,... | collective-permute-start | bytes 393224 | tf_op jit(solution)/shard_map/ppermute | solution.py:398
  8.6 6.0 %collective-permute-start.8 = (bf16[64,1024]{1,0:T(8,128)(2,1)}, bf16[64,1024]{1,0:T(8,128)(2,1)S(1)}, u32[]{:S(2)}, u32[]{:S(2)}) collective-permute-start(bf16[64,1024]{1,0:T(8,128)(2,1)} %bitcast.3), channel_id=1, source_target_pairs={{0,2},{1,3},{2,0},{3,1},{4,6},{5,7},{6,4},{7,5},{8,10},{9,11},{10,... | collective-permute-start | bytes 393224 | tf_op jit(solution)/shard_map/ppermute | solution.py:398
  10.0 5.3 %collective-permute-start.7 = (bf16[64,1024]{1,0:T(8,128)(2,1)}, bf16[64,1024]{1,0:T(8,128)(2,1)S(1)}, u32[]{:S(2)}, u32[]{:S(2)}) collective-permute-start(bf16[64,1024]{1,0:T(8,128)(2,1)} %bitcast.4), channel_id=1, source_target_pairs={{0,1},{1,0},{2,4},{3,5},{4,2},{5,3},{6,7},{7,6},{8,9},{9,8},{10,12... | collective-permute-start | bytes 393224 | tf_op jit(solution)/shard_map/ppermute | solution.py:398
  10.1 0.9 %copy-start = (bf16[32,1152]{1,0:T(8,128)(2,1)S(1)}, bf16[32,1152]{1,0:T(8,128)(2,1)}, u32[]{:S(2)}) copy-start(bf16[32,1152]{1,0:T(8,128)(2,1)} %get-tuple-element.27.message) | copy-start | bytes 221188
  10.9 4.3 %copy-start.3 = (bf16[256,256]{1,0:T(8,128)(2,1)S(1)}, bf16[256,256]{1,0:T(8,128)(2,1)}, u32[]{:S(2)}) copy-start(bf16[256,256]{1,0:T(8,128)(2,1)} %constant.7.clone.left_tab) | copy-start | bytes 393220
  10.9 4.3 %copy-start.1 = (bf16[2,32,1024]{2,1,0:T(8,128)(2,1)S(1)}, bf16[2,32,1024]{2,1,0:T(8,128)(2,1)}, u32[]{:S(2)}) copy-start(bf16[2,32,1024]{2,1,0:T(8,128)(2,1)} %get-tuple-element.36) | copy-start | bytes 393220
  11.0 4.3 %copy-start.2 = (bf16[256,256]{1,0:T(8,128)(2,1)S(1)}, bf16[256,256]{1,0:T(8,128)(2,1)}, u32[]{:S(2)}) copy-start(bf16[256,256]{1,0:T(8,128)(2,1)} %constant.6.clone.right_tab) | copy-start | bytes 393220
  12.1 6.5 %collective-permute-start.3 = (bf16[80,1152]{1,0:T(8,128)(2,1)S(1)}, bf16[80,1152]{1,0:T(8,128)(2,1)S(1)}, u32[]{:S(2)}, u32[]{:S(2)}) collective-permute-start(bf16[80,1152]{1,0:T(8,128)(2,1)S(1)} %get-tuple-element.31), channel_id=1, source_target_pairs={{0,1},{1,0},{2,3},{3,2},{4,5},{5,4},{6,7},{7,6},{8,9},{9,8},{10,11... | collective-permute-start | bytes 552968 | tf_op jit(solution)/shard_map/ppermute | solution.py:398
  12.2 6.4 %collective-permute-start.4 = (bf16[80,1152]{1,0:T(8,128)(2,1)S(1)}, bf16[80,1152]{1,0:T(8,128)(2,1)S(1)}, u32[]{:S(2)}, u32[]{:S(2)}) collective-permute-start(bf16[80,1152]{1,0:T(8,128)(2,1)S(1)} %get-tuple-element.32), channel_id=1, source_target_pairs={{0,8},{1,2},{2,1},{3,4},{4,3},{5,6},{6,5},{7,15},{8,0},{9,10},{10,... | collective-permute-start | bytes 552968 | tf_op jit(solution)/shard_map/ppermute | solution.py:398
  13.2 5.4 %collective-permute-start.5 = (bf16[16,1152]{1,0:T(8,128)(2,1)S(1)}, bf16[16,1152]{1,0:T(8,128)(2,1)S(1)}, u32[]{:S(2)}, u32[]{:S(2)}) collective-permute-start(bf16[16,1152]{1,0:T(8,128)(2,1)S(1)} %get-tuple-element.33), channel_id=1, source_target_pairs={{0,2},{1,3},{2,0},{3,1},{4,6},{5,7},{6,4},{7,5},{8,10},{9,11},{10,... | collective-permute-start | bytes 110600 | tf_op jit(solution)/shard_map/ppermute | solution.py:398
  14.6 4.0 %collective-permute-start.6 = (bf16[16,1152]{1,0:T(8,128)(2,1)S(1)}, bf16[16,1152]{1,0:T(8,128)(2,1)S(1)}, u32[]{:S(2)}, u32[]{:S(2)}) collective-permute-start(bf16[16,1152]{1,0:T(8,128)(2,1)S(1)} %get-tuple-element.34), channel_id=1, source_target_pairs={{0,1},{1,0},{2,4},{3,5},{4,2},{5,3},{6,7},{7,6},{8,9},{9,8},{10,12... | collective-permute-start | bytes 110600 | tf_op jit(solution)/shard_map/ppermute | solution.py:398
  15.3 3.4 %copy-start.4 = (bf16[192,192]{1,0:T(8,128)(2,1)S(1)}, bf16[192,192]{1,0:T(8,128)(2,1)}, u32[]{:S(2)}) copy-start(bf16[192,192]{1,0:T(8,128)(2,1)} %constant.8.clone.left_tab) | copy-start | bytes 221188
  21.2 5.5 %collective-permute-start.12 = (bf16[2,32,1024]{2,1,0:T(8,128)(2,1)S(1)}, bf16[2,32,1024]{2,1,0:T(8,128)(2,1)S(1)}, u32[]{:S(2)}, u32[]{:S(2)}) collective-permute-start(bf16[2,32,1024]{2,1,0:T(8,128)(2,1)S(1)} %get-tuple-element.47), channel_id=1, source_target_pairs={{0,8},{8,0},{16,24},{24,16},{1,9},{9,1},{17,25},{25,17},{2,10},{10... | collective-permute-start | bytes 393224 | tf_op jit(solution)/shard_map/ppermute | solution.py:379
  22.9 6.5 %collective-permute-start.13 = (bf16[2,32,1024]{2,1,0:T(8,128)(2,1)S(1)}, bf16[2,32,1024]{2,1,0:T(8,128)(2,1)S(1)}, u32[]{:S(2)}, u32[]{:S(2)}) collective-permute-start(bf16[2,32,1024]{2,1,0:T(8,128)(2,1)S(1)} %get-tuple-element.48), channel_id=1, source_target_pairs={{0,16},{8,24},{16,0},{24,8},{1,17},{9,25},{17,1},{25,9},{2,18},{10... | collective-permute-start | bytes 393224 | tf_op jit(solution)/shard_map/ppermute | solution.py:379
  24.5 6.5 %collective-permute-start.11 = (bf16[2,32,1024]{2,1,0:T(8,128)(2,1)S(1)}, bf16[2,32,1024]{2,1,0:T(8,128)(2,1)S(1)}, u32[]{:S(2)}, u32[]{:S(2)}) collective-permute-start(bf16[2,32,1024]{2,1,0:T(8,128)(2,1)S(1)} %get-tuple-element.45), channel_id=1, source_target_pairs={{0,24},{8,16},{16,8},{24,0},{1,25},{9,17},{17,9},{25,1},{2,26},{10... | collective-permute-start | bytes 393224 | tf_op jit(solution)/shard_map/ppermute | solution.py:379

commit v30 on v29

--- a/solution.py
+++ b/solution.py
@@ -393,7 +393,7 @@
             elif by > 1:
                 to = (depth, band ^ 1)
             else:
-                to = (depth ^ 1, band)
+                to = (depth ^ 2, band)
             pairs.append((depth * count + band, to[0] * count + to[1]))
     return lax.ppermute(value, ("depth", "rows"), pairs)
 

time: 31.2 us -> 31.2 us (level)
  no operation moved by 1% of the time
where the time goes in v30:
time: 31.2 us; the launch traced here: 31 us
  starting transfers between devices  15.1 us (48%)
  waiting for transfers between devices  8.34 us (27%)
  Pallas kernels  6.54 us (21%)
  local copies, waits for them, and re-layouts  0.91 us (3%)
    ppermute x6, starting transfers between devices, over_depth(): return lax.ppermute(value, 'depth', [(i, i ^ hop) for i in range(LAYERS)])  8.31 us
    ppermute x8, starting transfers between devices, exchanged(): return lax.ppermute(value, ('depth', 'rows'), pairs)  6.81 us
    ppermute x6, waiting for transfers between devices, over_depth(): return lax.ppermute(value, 'depth', [(i, i ^ hop) for i in range(LAYERS)])  5.95 us
    pallas_call x1, Pallas kernels, body(): call(chain_kernel, [shaped((2, BAND, COLS), bf16)] * LAYERS, [vmem] * (6...  2.5 us
    ppermute x8, waiting for transfers between devices, exchanged(): return lax.ppermute(value, ('depth', 'rows'), pairs)  2.39 us
    pallas_call x1, Pallas kernels, body(): call(pack_kernel, (shaped((BAND, HALO_W), bf16),) * LAYERS + (shaped(inci...  1.97 us
    pallas_call x1, Pallas kernels, body(): call(prepare_kernel, [shaped((TILES * layer_height(0), 2 * LANES), f32),...  1.22 us
    unnamed x10, local copies, waits for them, and re-layouts  0.91 us
  transfers between devices with their start and end apart: 14, of which 6 were waited for; matrix products, arithmetic and copies ran while one was open for 0% of the time, Pallas kernels for 7%

profile of v30, /device:TPU:0, one launch (start us, length us, event | category | flops | bytes accessed | tf_op | source)
XLA Modules:
  0.0 31.0 jit_solution(3708170219141853629)
XLA Ops:
  0.0 2.0 %shard_map.100 = (bf16[32,1152]{1,0:T(8,128)(2,1)}, bf16[32,1152]{1,0:T(8,128)(2,1)}, bf16[32,1152]{1,0:T(8,128)(2,1)}, bf16[32,1152]{1,0:T(8,128)(2,1)}, bf16[2,32,1024]{2,1,0:T(8,128)(2,1)}) custom-call(f32[1,3,32,1024]{3,2,1,0:T(8,128)} %light.1, s32[1,32,64]{2,1,0:T(8,128)} %edges.1, s32[1,2]{1,0:T(1,128)} %counts.1, s32[1,2,64]{2,1,0:T(2,128)} %listed.1, ...), custom_call_target="tpu_custom_call" | custom-call | flops 10000000 | bytes 1000000 | tf_op jit(solution)/shard_map/pallas_call | solution.py:441
  2.0 0.5 %collective-permute-start.10 = (bf16[64,1024]{1,0:T(8,128)(2,1)}, bf16[64,1024]{1,0:T(8,128)(2,1)S(1)}, u32[]{:S(2)}, u32[]{:S(2)}) collective-permute-start(bf16[64,1024]{1,0:T(8,128)(2,1)} %bitcast.1), channel_id=1, source_target_pairs={{0,1},{1,0},{2,3},{3,2},{4,5},{5,4},{6,7},{7,6},{8,9},{9,8},{10,11... | collective-permute-start | bytes 393224 | tf_op jit(solution)/shard_map/ppermute | solution.py:398
  2.5 2.6 %collective-permute-start = (bf16[32,1152]{1,0:T(8,128)(2,1)}, bf16[32,1152]{1,0:T(8,128)(2,1)S(1)}, u32[]{:S(2)}, u32[]{:S(2)}) collective-permute-start(bf16[32,1152]{1,0:T(8,128)(2,1)} %get-tuple-element.28), channel_id=1, source_target_pairs={{0,8},{8,0},{16,24},{24,16},{1,9},{9,1},{17,25},{25,17},{2,10},{10... | collective-permute-start | bytes 221192 | tf_op jit(solution)/shard_map/ppermute | solution.py:379
  5.1 1.5 %collective-permute-start.1 = (bf16[32,1152]{1,0:T(8,128)(2,1)}, bf16[32,1152]{1,0:T(8,128)(2,1)S(1)}, u32[]{:S(2)}, u32[]{:S(2)}) collective-permute-start(bf16[32,1152]{1,0:T(8,128)(2,1)} %get-tuple-element.29), channel_id=1, source_target_pairs={{0,16},{8,24},{16,0},{24,8},{1,17},{9,25},{17,1},{25,9},{2,18},{10... | collective-permute-start | bytes 221192 | tf_op jit(solution)/shard_map/ppermute | solution.py:379
  6.6 0.0 collective-permute-start.2
  6.6 2.0 %collective-permute-start.9 = (bf16[64,1024]{1,0:T(8,128)(2,1)}, bf16[64,1024]{1,0:T(8,128)(2,1)S(1)}, u32[]{:S(2)}, u32[]{:S(2)}) collective-permute-start(bf16[64,1024]{1,0:T(8,128)(2,1)} %bitcast.2), channel_id=1, source_target_pairs={{0,16},{1,2},{2,1},{3,4},{4,3},{5,6},{6,5},{7,23},{8,24},{9,10},{1... | collective-permute-start | bytes 393224 | tf_op jit(solution)/shard_map/ppermute | solution.py:398
  8.6 0.0 collective-permute-done.refs_1_
  8.6 1.4 %collective-permute-start.8 = (bf16[64,1024]{1,0:T(8,128)(2,1)}, bf16[64,1024]{1,0:T(8,128)(2,1)S(1)}, u32[]{:S(2)}, u32[]{:S(2)}) collective-permute-start(bf16[64,1024]{1,0:T(8,128)(2,1)} %bitcast.3), channel_id=1, source_target_pairs={{0,2},{1,3},{2,0},{3,1},{4,6},{5,7},{6,4},{7,5},{8,10},{9,11},{10,... | collective-permute-start | bytes 393224 | tf_op jit(solution)/shard_map/ppermute | solution.py:398
  10.0 0.0 collective-permute-done.1.refs_2_
  10.0 0.1 collective-permute-start.7
  10.1 0.0 copy-start
  10.1 0.9 %copy-done = bf16[32,1152]{1,0:T(8,128)(2,1)S(1)} copy-done((bf16[32,1152]{1,0:T(8,128)(2,1)S(1)}, bf16[32,1152]{1,0:T(8,128)(2,1)}, u32[]{:S(2)}) %copy-start) | copy-done | bytes 73752
  10.9 0.0 copy-start.3
  10.9 0.0 copy-start.1
  11.0 0.0 copy-start.2
  11.0 1.1 %collective-permute-done.2.refs_3_ = bf16[32,1152]{1,0:T(8,128)(2,1)S(1)} collective-permute-done((bf16[32,1152]{1,0:T(8,128)(2,1)}, bf16[32,1152]{1,0:T(8,128)(2,1)S(1)}, u32[]{:S(2)}, u32[]{:S(2)}) %collective-permute-start.2) | collective-permute-done | bytes 73760 | tf_op jit(solution)/shard_map/ppermute | solution.py:379
  12.1 0.1 shard_map.102
  12.2 0.1 collective-permute-start.3
  12.3 0.0 collective-permute-done.10.in_chip
  12.3 2.0 %collective-permute-start.4 = (bf16[80,1152]{1,0:T(8,128)(2,1)S(1)}, bf16[80,1152]{1,0:T(8,128)(2,1)S(1)}, u32[]{:S(2)}, u32[]{:S(2)}) collective-permute-start(bf16[80,1152]{1,0:T(8,128)(2,1)S(1)} %get-tuple-element.32), channel_id=1, source_target_pairs={{0,16},{1,2},{2,1},{3,4},{4,3},{5,6},{6,5},{7,23},{8,24},{9,10},{1... | collective-permute-start | bytes 552968 | tf_op jit(solution)/shard_map/ppermute | solution.py:398
  14.3 0.0 collective-permute-done.9.cross
  14.3 0.1 collective-permute-start.5
  14.4 0.2 collective-permute-done.8.far_even
  14.6 0.7 %collective-permute-start.6 = (bf16[16,1152]{1,0:T(8,128)(2,1)S(1)}, bf16[16,1152]{1,0:T(8,128)(2,1)S(1)}, u32[]{:S(2)}, u32[]{:S(2)}) collective-permute-start(bf16[16,1152]{1,0:T(8,128)(2,1)S(1)} %get-tuple-element.34), channel_id=1, source_target_pairs={{0,1},{1,0},{2,4},{3,5},{4,2},{5,3},{6,7},{7,6},{8,9},{9,8},{10,12... | collective-permute-start | bytes 110600 | tf_op jit(solution)/shard_map/ppermute | solution.py:398
  15.3 0.0 collective-permute-done.7.far_odd
  15.3 0.0 copy-done.3
  15.3 0.0 copy-done.1
  15.3 0.0 copy-done.2
  15.3 0.0 copy-start.4
  15.3 1.2 %shard_map.103 = (f32[1024,256]{1,0:T(8,128)S(1)}, f32[2,128,1024]{2,1,0:T(8,128)S(1)}, f32[128,1024]{1,0:T(8,128)S(1)}, bf16[3,256,512]{2,1,0:T(8,128)(2,1)S(1)...) custom-call(bf16[4,32,1152]{2,1,0:T(8,128)(2,1)S(1)} %get-tuple-elem, ...), custom_call_target="tpu_custom_call" | custom-call | flops 1000000000 | bytes 3000000 | tf_op jit(solution)/shard_map/pallas_call | solution.py:462
  16.5 2.2 %collective-permute-done.5.far_even = bf16[16,1152]{1,0:T(8,128)(2,1)S(1)} collective-permute-done((bf16[16,1152]{1,0:T(8,128)(2,1)S(1)}, bf16[16,1152]{1,0:T(8,128)(2,1)S(1)}, u32[]{:S(2)}, u32[]{:S(2)}) %collective-permute-start.5) | collective-permute-done | bytes 36896 | tf_op jit(solution)/shard_map/ppermute | solution.py:398
  18.7 0.0 collective-permute-done.6.far_odd
  18.7 0.0 collective-permute-done.3.in_chip
  18.7 0.0 collective-permute-done.4.cross
  18.7 0.0 copy-done.4
  18.7 2.5 %shard_map.104 = (bf16[2,32,1024]{2,1,0:T(8,128)(2,1)S(1)}, bf16[2,32,1024]{2,1,0:T(8,128)(2,1)S(1)}, bf16[2,32,1024]{2,1,0:T(8,128)(2,1)S(1)}, bf16[2,32,1024]{2,1,0:T(8,128)(2,1)S(1)}) custom-call(bf16[80,1152]{1,0:T(8,128)(2,1)S(1)} %collective-permute-done.3.in_chip, bf16[80,1152]{1,0:T(8,128)(2,1)S(1)} %collective-permute-done.4.cross, ...), custom_call_target="tpu_custom_call" | custom-call | flops 2000000000 | bytes 3000000 | tf_op jit(solution)/shard_map/pallas_call | solution.py:477
  21.2 1.6 %collective-permute-start.12 = (bf16[2,32,1024]{2,1,0:T(8,128)(2,1)S(1)}, bf16[2,32,1024]{2,1,0:T(8,128)(2,1)S(1)}, u32[]{:S(2)}, u32[]{:S(2)}) collective-permute-start(bf16[2,32,1024]{2,1,0:T(8,128)(2,1)S(1)} %get-tuple-element.47), channel_id=1, source_target_pairs={{0,8},{8,0},{16,24},{24,16},{1,9},{9,1},{17,25},{25,17},{2,10},{10... | collective-permute-start | bytes 393224 | tf_op jit(solution)/shard_map/ppermute | solution.py:379
  22.9 1.6 %collective-permute-start.13 = (bf16[2,32,1024]{2,1,0:T(8,128)(2,1)S(1)}, bf16[2,32,1024]{2,1,0:T(8,128)(2,1)S(1)}, u32[]{:S(2)}, u32[]{:S(2)}) collective-permute-start(bf16[2,32,1024]{2,1,0:T(8,128)(2,1)S(1)} %get-tuple-element.48), channel_id=1, source_target_pairs={{0,16},{8,24},{16,0},{24,8},{1,17},{9,25},{17,1},{25,9},{2,18},{10... | collective-permute-start | bytes 393224 | tf_op jit(solution)/shard_map/ppermute | solution.py:379
  24.5 0.9 %collective-permute-start.11 = (bf16[2,32,1024]{2,1,0:T(8,128)(2,1)S(1)}, bf16[2,32,1024]{2,1,0:T(8,128)(2,1)S(1)}, u32[]{:S(2)}, u32[]{:S(2)}) collective-permute-start(bf16[2,32,1024]{2,1,0:T(8,128)(2,1)S(1)} %get-tuple-element.45), channel_id=1, source_target_pairs={{0,24},{8,16},{16,8},{24,0},{1,25},{9,17},{17,9},{25,1},{2,26},{10... | collective-permute-start | bytes 393224 | tf_op jit(solution)/shard_map/ppermute | solution.py:379
  25.4 1.4 %collective-permute-done.12.refs_1_ = bf16[2,32,1024]{2,1,0:T(8,128)(2,1)S(1)} collective-permute-done((bf16[2,32,1024]{2,1,0:T(8,128)(2,1)S(1)}, bf16[2,32,1024]{2,1,0:T(8,128)(2,1)S(1)}, u32[]{:S(2)}, u32[]{:S(2)}) %collective-permute-start.12) | collective-permute-done | bytes 131104 | tf_op jit(solution)/shard_map/ppermute | solution.py:379
  26.8 2.5 %collective-permute-done.13.refs_2_ = bf16[2,32,1024]{2,1,0:T(8,128)(2,1)S(1)} collective-permute-done((bf16[2,32,1024]{2,1,0:T(8,128)(2,1)S(1)}, bf16[2,32,1024]{2,1,0:T(8,128)(2,1)S(1)}, u32[]{:S(2)}, u32[]{:S(2)}) %collective-permute-start.13) | collective-permute-done | bytes 131104 | tf_op jit(solution)/shard_map/ppermute | solution.py:379
  29.3 0.8 %shard_map.105.refs_1_ = bf16[1,3,2,32,1024]{4,3,2,1,0:T(8,128)(2,1)} custom-call(bf16[2,32,1024]{2,1,0:T(8,128)(2,1)S(1)} %get-tuple-element.46.refs_0_, bf16[2,32,1024]{2,1,0:T(8,128)(2,1)S(1)} %collective-permute-done.12.refs_1_, bf16[2,32,1024]{2,1,0:T(8,128)(2,1)S(1)} %collective-permute-done.13.refs_2_), custom_call_target="tpu_custom_call" | custom-call | bytes 1000000 | tf_op jit(solution)/shard_map/pallas_call | solution.py:488
  30.1 0.9 %collective-permute-done.11.refs_0_ = bf16[2,32,1024]{2,1,0:T(8,128)(2,1)S(1)} collective-permute-done((bf16[2,32,1024]{2,1,0:T(8,128)(2,1)S(1)}, bf16[2,32,1024]{2,1,0:T(8,128)(2,1)S(1)}, u32[]{:S(2)}, u32[]{:S(2)}) %collective-permute-start.11) | collective-permute-done | bytes 131104 | tf_op jit(solution)/shard_map/ppermute | solution.py:379
  (2 shorter events, 0.0 us)
Async XLA Ops:
  2.0 10.3 %collective-permute-start.10 = (bf16[64,1024]{1,0:T(8,128)(2,1)}, bf16[64,1024]{1,0:T(8,128)(2,1)S(1)}, u32[]{:S(2)}, u32[]{:S(2)}) collective-permute-start(bf16[64,1024]{1,0:T(8,128)(2,1)} %bitcast.1), channel_id=1, source_target_pairs={{0,1},{1,0},{2,3},{3,2},{4,5},{5,4},{6,7},{7,6},{8,9},{9,8},{10,11... | collective-permute-start | bytes 393224 | tf_op jit(solution)/shard_map/ppermute | solution.py:398
  2.5 6.1 %collective-permute-start = (bf16[32,1152]{1,0:T(8,128)(2,1)}, bf16[32,1152]{1,0:T(8,128)(2,1)S(1)}, u32[]{:S(2)}, u32[]{:S(2)}) collective-permute-start(bf16[32,1152]{1,0:T(8,128)(2,1)} %get-tuple-element.28), channel_id=1, source_target_pairs={{0,8},{8,0},{16,24},{24,16},{1,9},{9,1},{17,25},{25,17},{2,10},{10... | collective-permute-start | bytes 221192 | tf_op jit(solution)/shard_map/ppermute | solution.py:379
  5.1 4.9 %collective-permute-start.1 = (bf16[32,1152]{1,0:T(8,128)(2,1)}, bf16[32,1152]{1,0:T(8,128)(2,1)S(1)}, u32[]{:S(2)}, u32[]{:S(2)}) collective-permute-start(bf16[32,1152]{1,0:T(8,128)(2,1)} %get-tuple-element.29), channel_id=1, source_target_pairs={{0,16},{8,24},{16,0},{24,8},{1,17},{9,25},{17,1},{25,9},{2,18},{10... | collective-permute-start | bytes 221192 | tf_op jit(solution)/shard_map/ppermute | solution.py:379
  6.6 5.5 %collective-permute-start.2 = (bf16[32,1152]{1,0:T(8,128)(2,1)}, bf16[32,1152]{1,0:T(8,128)(2,1)S(1)}, u32[]{:S(2)}, u32[]{:S(2)}) collective-permute-start(bf16[32,1152]{1,0:T(8,128)(2,1)} %get-tuple-element.30), channel_id=1, source_target_pairs={{0,24},{8,16},{16,8},{24,0},{1,25},{9,17},{17,9},{25,1},{2,26},{10... | collective-permute-start | bytes 221192 | tf_op jit(solution)/shard_map/ppermute | solution.py:379
  6.6 7.7 %collective-permute-start.9 = (bf16[64,1024]{1,0:T(8,128)(2,1)}, bf16[64,1024]{1,0:T(8,128)(2,1)S(1)}, u32[]{:S(2)}, u32[]{:S(2)}) collective-permute-start(bf16[64,1024]{1,0:T(8,128)(2,1)} %bitcast.2), channel_id=1, source_target_pairs={{0,16},{1,2},{2,1},{3,4},{4,3},{5,6},{6,5},{7,23},{8,24},{9,10},{1... | collective-permute-start | bytes 393224 | tf_op jit(solution)/shard_map/ppermute | solution.py:398
  8.6 6.0 %collective-permute-start.8 = (bf16[64,1024]{1,0:T(8,128)(2,1)}, bf16[64,1024]{1,0:T(8,128)(2,1)S(1)}, u32[]{:S(2)}, u32[]{:S(2)}) collective-permute-start(bf16[64,1024]{1,0:T(8,128)(2,1)} %bitcast.3), channel_id=1, source_target_pairs={{0,2},{1,3},{2,0},{3,1},{4,6},{5,7},{6,4},{7,5},{8,10},{9,11},{10,... | collective-permute-start | bytes 393224 | tf_op jit(solution)/shard_map/ppermute | solution.py:398
  10.0 5.3 %collective-permute-start.7 = (bf16[64,1024]{1,0:T(8,128)(2,1)}, bf16[64,1024]{1,0:T(8,128)(2,1)S(1)}, u32[]{:S(2)}, u32[]{:S(2)}) collective-permute-start(bf16[64,1024]{1,0:T(8,128)(2,1)} %bitcast.4), channel_id=1, source_target_pairs={{0,1},{1,0},{2,4},{3,5},{4,2},{5,3},{6,7},{7,6},{8,9},{9,8},{10,12... | collective-permute-start | bytes 393224 | tf_op jit(solution)/shard_map/ppermute | solution.py:398
  10.1 0.9 %copy-start = (bf16[32,1152]{1,0:T(8,128)(2,1)S(1)}, bf16[32,1152]{1,0:T(8,128)(2,1)}, u32[]{:S(2)}) copy-start(bf16[32,1152]{1,0:T(8,128)(2,1)} %get-tuple-element.27.message) | copy-start | bytes 221188
  10.9 4.3 %copy-start.3 = (bf16[256,256]{1,0:T(8,128)(2,1)S(1)}, bf16[256,256]{1,0:T(8,128)(2,1)}, u32[]{:S(2)}) copy-start(bf16[256,256]{1,0:T(8,128)(2,1)} %constant.7.clone.left_tab) | copy-start | bytes 393220
  10.9 4.3 %copy-start.1 = (bf16[2,32,1024]{2,1,0:T(8,128)(2,1)S(1)}, bf16[2,32,1024]{2,1,0:T(8,128)(2,1)}, u32[]{:S(2)}) copy-start(bf16[2,32,1024]{2,1,0:T(8,128)(2,1)} %get-tuple-element.36) | copy-start | bytes 393220
  11.0 4.3 %copy-start.2 = (bf16[256,256]{1,0:T(8,128)(2,1)S(1)}, bf16[256,256]{1,0:T(8,128)(2,1)}, u32[]{:S(2)}) copy-start(bf16[256,256]{1,0:T(8,128)(2,1)} %constant.6.clone.right_tab) | copy-start | bytes 393220
  12.2 6.5 %collective-permute-start.3 = (bf16[80,1152]{1,0:T(8,128)(2,1)S(1)}, bf16[80,1152]{1,0:T(8,128)(2,1)S(1)}, u32[]{:S(2)}, u32[]{:S(2)}) collective-permute-start(bf16[80,1152]{1,0:T(8,128)(2,1)S(1)} %get-tuple-element.31), channel_id=1, source_target_pairs={{0,1},{1,0},{2,3},{3,2},{4,5},{5,4},{6,7},{7,6},{8,9},{9,8},{10,11... | collective-permute-start | bytes 552968 | tf_op jit(solution)/shard_map/ppermute | solution.py:398
  12.3 6.4 %collective-permute-start.4 = (bf16[80,1152]{1,0:T(8,128)(2,1)S(1)}, bf16[80,1152]{1,0:T(8,128)(2,1)S(1)}, u32[]{:S(2)}, u32[]{:S(2)}) collective-permute-start(bf16[80,1152]{1,0:T(8,128)(2,1)S(1)} %get-tuple-element.32), channel_id=1, source_target_pairs={{0,16},{1,2},{2,1},{3,4},{4,3},{5,6},{6,5},{7,23},{8,24},{9,10},{1... | collective-permute-start | bytes 552968 | tf_op jit(solution)/shard_map/ppermute | solution.py:398
  14.3 4.4 %collective-permute-start.5 = (bf16[16,1152]{1,0:T(8,128)(2,1)S(1)}, bf16[16,1152]{1,0:T(8,128)(2,1)S(1)}, u32[]{:S(2)}, u32[]{:S(2)}) collective-permute-start(bf16[16,1152]{1,0:T(8,128)(2,1)S(1)} %get-tuple-element.33), channel_id=1, source_target_pairs={{0,2},{1,3},{2,0},{3,1},{4,6},{5,7},{6,4},{7,5},{8,10},{9,11},{10,... | collective-permute-start | bytes 110600 | tf_op jit(solution)/shard_map/ppermute | solution.py:398
  14.6 4.1 %collective-permute-start.6 = (bf16[16,1152]{1,0:T(8,128)(2,1)S(1)}, bf16[16,1152]{1,0:T(8,128)(2,1)S(1)}, u32[]{:S(2)}, u32[]{:S(2)}) collective-permute-start(bf16[16,1152]{1,0:T(8,128)(2,1)S(1)} %get-tuple-element.34), channel_id=1, source_target_pairs={{0,1},{1,0},{2,4},{3,5},{4,2},{5,3},{6,7},{7,6},{8,9},{9,8},{10,12... | collective-permute-start | bytes 110600 | tf_op jit(solution)/shard_map/ppermute | solution.py:398
  15.3 3.4 %copy-start.4 = (bf16[192,192]{1,0:T(8,128)(2,1)S(1)}, bf16[192,192]{1,0:T(8,128)(2,1)}, u32[]{:S(2)}) copy-start(bf16[192,192]{1,0:T(8,128)(2,1)} %constant.8.clone.left_tab) | copy-start | bytes 221188
  21.2 5.6 %collective-permute-start.12 = (bf16[2,32,1024]{2,1,0:T(8,128)(2,1)S(1)}, bf16[2,32,1024]{2,1,0:T(8,128)(2,1)S(1)}, u32[]{:S(2)}, u32[]{:S(2)}) collective-permute-start(bf16[2,32,1024]{2,1,0:T(8,128)(2,1)S(1)} %get-tuple-element.47), channel_id=1, source_target_pairs={{0,8},{8,0},{16,24},{24,16},{1,9},{9,1},{17,25},{25,17},{2,10},{10... | collective-permute-start | bytes 393224 | tf_op jit(solution)/shard_map/ppermute | solution.py:379
  22.9 6.5 %collective-permute-start.13 = (bf16[2,32,1024]{2,1,0:T(8,128)(2,1)S(1)}, bf16[2,32,1024]{2,1,0:T(8,128)(2,1)S(1)}, u32[]{:S(2)}, u32[]{:S(2)}) collective-permute-start(bf16[2,32,1024]{2,1,0:T(8,128)(2,1)S(1)} %get-tuple-element.48), channel_id=1, source_target_pairs={{0,16},{8,24},{16,0},{24,8},{1,17},{9,25},{17,1},{25,9},{2,18},{10... | collective-permute-start | bytes 393224 | tf_op jit(solution)/shard_map/ppermute | solution.py:379
  24.5 6.5 %collective-permute-start.11 = (bf16[2,32,1024]{2,1,0:T(8,128)(2,1)S(1)}, bf16[2,32,1024]{2,1,0:T(8,128)(2,1)S(1)}, u32[]{:S(2)}, u32[]{:S(2)}) collective-permute-start(bf16[2,32,1024]{2,1,0:T(8,128)(2,1)S(1)} %get-tuple-element.45), channel_id=1, source_target_pairs={{0,24},{8,16},{16,8},{24,0},{1,25},{9,17},{17,9},{25,1},{2,26},{10... | collective-permute-start | bytes 393224 | tf_op jit(solution)/shard_map/ppermute | solution.py:379
